TPU v7x, 32 devices: a whole 2x2x4 slice. The times are simulated.
32 devices in a mesh: dp: 2 (over x), context: 4 (over y, core), tensor: 4 (over z).
Axes of the slice: x: 2, y: 2, z: 4, core: 2. Of those that a mesh axis runs over, the one named last changes fastest.
Arguments:
- patches: bfloat16 [6144, 1280], P(('dp', 'context')), parts along dimension 0, may hold values from -6 to 6
- valid: int32 [6144], P(('dp', 'context')), parts along dimension 0, may hold values from 0 to 1, as said below
- place: int32 [1536], P(('dp', 'context')), parts along dimension 0, may hold values from -1 to 767, as said below
- gain_attn: float32 [1280], replicated, may hold values from 0.25 to 1.75
- w_qkv: bfloat16 [1280, 3, 1280], P('context', None, 'tensor'), may hold values from -1 to 1
- w_proj: bfloat16 [1280, 1280], P('tensor', 'context'), may hold values from -0.15625 to 0.15625
- gain_merge: float32 [1280], replicated, may hold values from 0.25 to 1.75
Outputs:
- placed: bfloat16 [1536, 5120], P(('dp', 'context'), 'tensor'), parts along dimension 0
There are 2 independent parts, one for each index of `dp`. A program takes and returns all parts, laid end to end along the dimension named above; an argument that names none is the same for every part. Nothing has to cross between parts.
Inputs may be any that keep to these rules, and one draw needn't show every extreme that they name: `valid`: slots of a window are ordered by 2 x 2 groups of 4 (group row-major over a 4 x 4 grid, then within the group row-major); the real patches of a window form its top-left h x w block with h and w even and at least 4. `place`: A merged row has a position exactly when its 4 slots are real; positions are distinct.
All inputs are finite; a program needn't handle non-finite values.
Results may differ from a plain program's by a relative error of at most 0.0073.
Values may be sent and summed in bfloat16 or wider, within the bound.
No kernel may reach another device: no remote copies, remote signals or barrier semaphores. Data moves between devices by JAX's collectives and lax.ppermute only.
A program may use at most 64 MiB of HBM per device.

v0:
```python
import jax
import jax.numpy as jnp
from jax import lax
from jax.sharding import PartitionSpec as P

HD = 80
WIN = 64


def normalize(tensor_in, gain):
    mean_sq = jnp.mean(tensor_in * tensor_in, axis=-1, keepdims=True)
    return tensor_in * lax.rsqrt(mean_sq + 1e-06) * gain


def local(patches, valid, place, gain_attn, w_qkv, w_proj, gain_merge):
    row_count = patches.shape[0]
    feat_width = patches.shape[1]
    local_width = w_qkv.shape[2]
    heads_here = local_width // HD
    windows = row_count // WIN
    groups = row_count // 4
    hidden = normalize(patches.astype(jnp.float32), gain_attn).astype(jnp.bfloat16)
    shard_piece = lax.all_gather(w_qkv, "context", axis=0, tiled=True)
    piece_rows = shard_piece.shape[0]
    flat_piece = shard_piece.reshape(piece_rows, 3 * local_width)
    projected = jnp.dot(hidden, flat_piece, preferred_element_type=jnp.float32)
    triple = projected.reshape(row_count, 3, heads_here, HD).astype(jnp.bfloat16)
    query_block = triple[:, 0].reshape(windows, WIN, heads_here, HD)
    key_block = triple[:, 1].reshape(windows, WIN, heads_here, HD)
    value_block = triple[:, 2].reshape(windows, WIN, heads_here, HD)
    scores = jnp.einsum(
        "wqhd,wkhd->whqk", query_block, key_block, preferred_element_type=jnp.float32
    ) * HD ** (-0.5)
    key_mask = valid.reshape(windows, 1, 1, WIN) > 0
    scores = jnp.where(key_mask, scores, jnp.float32(-1e30))
    peak = jnp.max(scores, axis=-1, keepdims=True)
    exp_terms = jnp.exp(scores - peak)
    weights = (exp_terms / jnp.sum(exp_terms, axis=-1, keepdims=True)).astype(jnp.bfloat16)
    mixed_heads = jnp.einsum(
        "whqk,wkhd->wqhd", weights, value_block, preferred_element_type=jnp.float32
    )
    mixed_heads = mixed_heads.reshape(row_count, local_width).astype(jnp.bfloat16)
    partial_value = jnp.dot(
        mixed_heads,
        lax.all_gather(w_proj, "context", axis=1, tiled=True),
        preferred_element_type=jnp.float32,
    )
    tensor_slot = lax.axis_index("tensor")
    head_total = lax.psum(partial_value, "tensor")
    residual = patches.astype(jnp.float32) + head_total
    normed = normalize(residual, gain_merge).astype(jnp.bfloat16).reshape(groups, 4, feat_width)
    own_rows = lax.dynamic_index_in_dim(normed, tensor_slot, 1, keepdims=False)
    first_spot = lax.axis_index("context") * groups
    spot_grid = jnp.arange(groups, dtype=jnp.int32)
    merged_rows = lax.all_gather(own_rows, "context", axis=0, tiled=True)
    spot_ids = lax.all_gather(place, "context", axis=0, tiled=True)
    local_spot = spot_ids - first_spot
    selector = (local_spot[None, :] == spot_grid[:, None]).astype(jnp.bfloat16)
    placed = jnp.dot(selector, merged_rows, preferred_element_type=jnp.float32)
    return placed.astype(jnp.bfloat16)


def solution(mesh):
    in_specs = (
        P(("dp", "context"), None),
        P(("dp", "context")),
        P(("dp", "context")),
        P(),
        P("context", None, "tensor"),
        P("tensor", "context"),
        P(),
    )
    out_specs = P(("dp", "context"), "tensor")
    return jax.shard_map(local, mesh=mesh, in_specs=in_specs, out_specs=out_specs, check_vma=False)
```

profile of v0, /device:TPU:0, one launch (start us, length us, event | category | flops | bytes accessed | tf_op | source)
XLA Modules:
  0.0 265.3 jit_solution(3645901701841421166)
XLA Ops:
  6.5 2.9 %copy.22 = bf16[320,3,320]{2,1,0:T(4,128)(2,1)} copy(bf16[320,3,320]{2,0,1:T(8,128)(2,1)} %param.11) | data formatting | bytes 1228800 | tf_op args[4]
  9.4 0.0 all-reduce.3.cloned.1.call-start
  9.5 0.1 gt.16
  9.6 0.2 copy.32
  9.8 0.5 fusion.1
  10.3 11.2 %all_gather.14 = bf16[320,1280]{0,1:T(8,128)(2,1)S(1)} all-gather(bf16[320,320]{0,1:T(8,128)(2,1)S(1)} %copy.32), channel_id=1, replica_groups=mesh['dp'=2,'context'=4,'tensor'=4] {'context'}, dimensions={1}, use_global_device_ids=true | all-gather | bytes 1024000 | tf_op jit(solution)/shard_map/all_gather | solution.py:45
  21.5 23.8 %all-gather.4.cloned.1.call-done = bf16[1280,3,320]{2,1,0:T(4,128)(2,1)} async-done(((bf16[320,3,320]{2,1,0:T(4,128)(2,1)}), bf16[1280,3,320]{2,1,0:T(4,128)(2,1)}) %all-gather.4.cloned.1.call-update) | async-done | bytes 2457616 | tf_op jit(solution)/shard_map/all_gather | solution.py:23
  45.3 7.4 %copy.23 = bf16[1280,3,320]{0,2,1:T(8,128)(2,1)} copy(bf16[1280,3,320]{2,1,0:T(4,128)(2,1)} %all-gather.4.cloned.1.call-done) | data formatting | bytes 4915200 | tf_op jit(solution)/shard_map/all_gather | solution.py:23
  52.7 3.9 %fusion.11 = bf16[768,3,4,80]{0,3,2,1:T(8,128)(2,1)S(1)} fusion(bf16[3,4,80,1280]{3,2,1,0:T(8,128)(2,1)} %bitcast.26, bf16[768,1280]{1,0:T(8,128)(2,1)S(1)} %copy-done, f32[1280]{0:T(1024)S(1)} %copy-done.6, f32[768]{0:T(1024)S(1)} %add_rsqrt_fusion.1), kind=kOutput, calls=%fused_computation.16 | convolution fusion | flops 1892106240 | bytes 5906432 | tf_op jit(solution)/shard_map/dot_general | solution.py:26
  56.6 1.1 fusion.22
  57.7 2.2 copy.25
  59.9 2.2 copy.26
  62.0 1.9 multiply_select_fusion
  64.0 1.1 copy-done.8
  65.1 0.4 fusion.23
  65.5 1.2 copy.24
  66.7 3.6 %fusion.15 = bf16[12,64,4,80]{3,1,2,0:T(8,128)(2,1)} fusion(bf16[12,64,4,80]{3,1,0,2:T(8,128)(2,1)} %bitcast.29, f32[12,4,64]{2,1,0:T(4,128)S(1)} %fusion.23, f32[12,4,64,64]{2,3,1,0:T(8,128)} %copy-done.8), kind=kOutput, calls=%fused_computation.21 | convolution fusion | flops 32296000 | bytes 1781760 | tf_op jit(solution)/shard_map/whqk,wkhd->wqhd/dot_general | solution.py:39
  70.3 2.6 copy.31
  72.9 1.8 convert_element_type.35
  74.7 3.1 %fusion.24 = f32[768,1280]{1,0:T(8,128)} fusion(bf16[768,320]{1,0:T(8,128)(2,1)S(1)} %convert_element_type.35, bf16[320,1280]{0,1:T(8,128)(2,1)S(1)} %all_gather.14), kind=kOutput, calls=%fused_computation.36 | convolution fusion | flops 629145600 | bytes 5242880 | tf_op jit(solution)/shard_map/dot_general | solution.py:43
  77.9 146.6 %all-reduce.3.cloned.1.call-done = f32[768,1280]{1,0:T(8,128)} async-done(((f32[768,1280]{1,0:T(8,128)}), f32[768,1280]{1,0:T(8,128)}) %all-reduce.3.cloned.1.call-update) | async-done | bytes 3932176 | tf_op jit(solution)/shard_map/psum | solution.py:49
  224.5 2.8 %multiply_reduce_fusion = f32[768]{0:T(1024)S(1)} fusion(f32[768,1280]{1,0:T(8,128)} %all-reduce.3.cloned.1.call-done, bf16[768,1280]{1,0:T(8,128)(2,1)S(1)} %copy-done), kind=kLoop, calls=%fused_computation.8 | loop fusion | flops 3931392 | bytes 5901312 | tf_op jit(solution)/shard_map/reduce_sum | solution.py:11
  227.4 0.4 copy-done.1
  227.8 1.9 multiply_convert_fusion
  229.8 3.2 %reshape.42 = bf16[192,4,1280]{2,1,0:T(4,128)(2,1)S(1)} reshape(bf16[768,1280]{1,0:T(8,128)(2,1)} %multiply_convert_fusion) | data formatting | bytes 3932160 | tf_op jit(solution)/shard_map/reshape | solution.py:51
  233.0 1.0 constant_dynamic-slice_fusion
  234.0 0.8 copy.36
  234.9 0.6 dynamic-slice
  236.2 0.2 dynamic-update-slice
  236.4 4.9 %all-reduce = s32[768]{0:T(1024)S(1)} all-reduce(s32[768]{0:T(1024)S(1)} %dynamic-update-slice), channel_id=1, replica_groups=mesh['dp'=2,'context'=4,'tensor'=4] {'context'}, use_global_device_ids=true, to_apply=%add | all-reduce | flops 768 | bytes 6144
  241.4 14.6 %all-gather.6.cloned.1.call-done = bf16[768,1,1280]{2,0,1:T(8,128)(2,1)} async-done(((bf16[192,1,1280]{2,0,1:T(8,128)(2,1)}), bf16[768,1,1280]{2,0,1:T(8,128)(2,1)}) %all-gather.6.cloned.1.call-update) | async-done | bytes 1966096 | tf_op jit(solution)/shard_map/all_gather | solution.py:55
  255.9 2.9 %convolution_convert_fusion = bf16[192,1280]{1,0:T(8,128)(2,1)} fusion(bf16[768,1,1280]{2,0,1:T(8,128)(2,1)} %all-gather.6.cloned.1.call-done, s32[768]{0:T(1024)S(1)} %broadcast_subtract_fusion), kind=kOutput, calls=%fused_computation.9 | convolution fusion | flops 377880576 | bytes 2460672 | tf_op jit(solution)/shard_map/dot_general | solution.py:59
  (26 shorter events, 0.2 us)
Async XLA Ops:
  6.5 2.9 %copy-start.4 = (s32[768]{0:T(1024)S(1)}, s32[768]{0:T(1024)}, u32[]{:S(2)}) copy-start(s32[768]{0:T(1024)} %param.8) | copy-start | bytes 9220
  6.5 3.1 %copy-start.2 = (bf16[320,320]{1,0:T(8,128)(2,1)S(1)}, bf16[320,320]{1,0:T(8,128)(2,1)}, u32[]{:S(2)}) copy-start(bf16[320,320]{1,0:T(8,128)(2,1)} %param.12) | copy-start | bytes 614404
  6.5 3.2 %copy-start = (bf16[768,1280]{1,0:T(8,128)(2,1)S(1)}, bf16[768,1280]{1,0:T(8,128)(2,1)}, u32[]{:S(2)}) copy-start(bf16[768,1280]{1,0:T(8,128)(2,1)} %param.7) | copy-start | bytes 5898244
  6.5 38.7 %all-gather.4.cloned.1.call-start = ((), (), s32[]{:S(2)}) async-start(), calls=%async_computation | async-start | bytes 4915200 | tf_op jit(solution)/shard_map/all_gather | solution.py:23
  9.4 215.1 %all-reduce.3.cloned.1.call-start = ((), (), s32[]{:S(2)}) async-start(), calls=%async_computation.1 | async-start | bytes 7864320 | tf_op jit(solution)/shard_map/psum | solution.py:49
  21.5 31.3 %copy-start.6 = (f32[1280]{0:T(1024)S(1)}, f32[1280]{0:T(1024)}, u32[]{:S(2)}) copy-start(f32[1280]{0:T(1024)} %param.10) | copy-start | bytes 15364
  64.0 1.2 copy-start.8
  77.9 178.1 %all-gather.6.cloned.1.call-start = ((), (), s32[]{:S(2)}) async-start(), calls=%async_computation.2 | async-start | bytes 2457600 | tf_op jit(solution)/shard_map/all_gather | solution.py:55
  77.9 149.5 %copy-start.3 = (f32[1280]{0:T(1024)S(1)}, f32[1280]{0:T(1024)}, u32[]{:S(2)}) copy-start(f32[1280]{0:T(1024)} %param.13) | copy-start | bytes 15364
  224.5 3.3 %copy-start.1 = (f32[768,1280]{1,0:T(8,128)S(1)}, f32[768,1280]{1,0:T(8,128)}, u32[]{:S(2)}) copy-start(f32[768,1280]{1,0:T(8,128)} %all-reduce.3.cloned.1.call-done) | copy-start | bytes 11796484
  233.0 1.9 copy-start.7
  233.0 3.2 %copy-start.5 = (s32[192]{0:T(256)S(1)}, s32[192]{0:T(256)}, u32[]{:S(2)}) copy-start(s32[192]{0:T(256)} %param.9) | copy-start | bytes 2308
Sparse Core Ops, SparseCore 0:
  9.5 35.6 all-gather.3
  78.0 146.4 all-reduce.2
  235.0 20.8 all-gather.5
where the time goes:
time: 266 us; the launch traced here: 265 us
  waiting for transfers between devices  185 us (70%)
  local copies, waits for them, and re-layouts  29.2 us (11%)
  blocking collectives  16.1 us (6%)
  matrix products  15.4 us (6%)
  between operations  13.9 us (5%)
  other arithmetic  5.67 us (2%)
    psum x1, waiting for transfers between devices, local(): head_total = lax.psum(partial_value, 'tensor')  147 us
    all_gather x1, waiting for transfers between devices, local(): shard_piece = lax.all_gather(w_qkv, 'context', axis=0, tiled=True)  23.8 us
    all_gather x1, waiting for transfers between devices, local(): merged_rows = lax.all_gather(own_rows, 'context', axis=0, tiled=True)  14.6 us
    all_gather x1, blocking collectives, local(): lax.all_gather(w_proj, 'context', axis=1, tiled=True)  11.2 us
    all_gather x1, local copies, waits for them, and re-layouts, local(): shard_piece = lax.all_gather(w_qkv, 'context', axis=0, tiled=True)  7.44 us
    unnamed x24, local copies, waits for them, and re-layouts  6.36 us
  transfers between devices with their start and end apart: 3, of which 3 were waited for; matrix products, arithmetic and copies ran while one was open for 1% of the time, Pallas kernels for 0%

commit v1 on v0

v1 whole, which is shorter than its diff:
```python
import functools

import jax
import jax.numpy as jnp
from jax import lax
from jax.experimental import pallas as pl
from jax.experimental.pallas import tpu as pltpu
from jax.sharding import PartitionSpec as P

HD = 80
WIN = 64
PAIR = 2 * WIN
CHUNKS = 1
F32 = jnp.float32
BF16 = jnp.bfloat16
VMEM = pl.BlockSpec(memory_space=pltpu.VMEM)
SMEM = pl.BlockSpec(memory_space=pltpu.SMEM)


def params(mib):
    return pltpu.CompilerParams(vmem_limit_bytes=mib * 1024 * 1024)


def swap(x, axis, size, bit):
    return lax.ppermute(x, axis, [(i, i ^ bit) for i in range(size)])


def gather_xor(x, axis, size):
    blocks = {0: x}
    bit = size // 2
    while bit:
        for key in list(blocks):
            blocks[key ^ bit] = swap(blocks[key], axis, size, bit)
        bit //= 2
    return blocks


def norm_kernel(slot_ref, patches_ref, gain_ref, hidden_ref, own_ref):
    rows = patches_ref.shape[0]
    x = patches_ref[...]
    xf = x.astype(F32)
    mean_sq = jnp.mean(xf * xf, axis=-1, keepdims=True)
    hidden_ref[...] = (xf * lax.rsqrt(mean_sq + 1e-06) * gain_ref[...]).astype(BF16)
    step = 256
    pick = step // 4
    row = lax.broadcasted_iota(jnp.int32, (pick, step), 0)
    col = lax.broadcasted_iota(jnp.int32, (pick, step), 1)
    chosen = (col == 4 * row + slot_ref[0]).astype(F32).astype(BF16)
    for i in range(rows // step):
        own_ref[i * pick : (i + 1) * pick, :] = jnp.dot(
            chosen, x[i * step : (i + 1) * step], preferred_element_type=F32
        ).astype(BF16)


def attention_kernel(n_ctx, row0, rows, *refs):
    ctx_ref, hidden_ref, valid_ref = refs[:3]
    shards = refs[3 : 3 + n_ctx]
    out_ref, w_ref, q_ref, k_ref, v_ref, mix_ref = refs[3 + n_ctx :]
    depth = shards[0].shape[1]
    width = shards[0].shape[2]
    heads = width // HD
    me = ctx_ref[0]
    for key in range(n_ctx):
        at = pl.multiple_of((me ^ key) * depth, depth)
        for j in range(3):
            w_ref[j, pl.ds(at, depth), :] = shards[key][j]
    hidden = hidden_ref[row0 : row0 + rows, :]
    q_ref[...] = jnp.dot(hidden, w_ref[0], preferred_element_type=F32).astype(BF16)
    k_ref[...] = jnp.dot(hidden, w_ref[1], preferred_element_type=F32).astype(BF16)
    v_ref[...] = jnp.dot(hidden, w_ref[2], preferred_element_type=F32).astype(BF16)
    lane = lax.broadcasted_iota(jnp.int32, (1, width), 1)
    head_masks = [
        ((lane >= h * HD) & (lane < (h + 1) * HD)).astype(F32).astype(BF16) for h in range(heads)
    ]
    q_win = lax.broadcasted_iota(jnp.int32, (PAIR, PAIR), 0) // WIN
    k_win = lax.broadcasted_iota(jnp.int32, (PAIR, PAIR), 1) // WIN
    same = q_win == k_win
    for p in range(rows // PAIR):
        at = p * PAIR
        q = q_ref[at : at + PAIR, :]
        k = k_ref[at : at + PAIR, :]
        v = v_ref[at : at + PAIR, :]
        k_all = jnp.concatenate([k * m for m in head_masks], axis=0)
        v_all = jnp.concatenate([v * m for m in head_masks], axis=0)
        scores = lax.dot_general(q, k_all, (((1,), (1,)), ((), ())), preferred_element_type=F32)
        live = valid_ref[row0 // PAIR + p : row0 // PAIR + p + 1, :] > 0
        floor = jnp.where(same, F32(-1e30), F32(-3e38))
        weights = []
        for h in range(heads):
            s = scores[:, h * PAIR : (h + 1) * PAIR] * F32(HD ** (-0.5))
            s = jnp.where(same & live, s, floor)
            e = jnp.exp(s - jnp.max(s, axis=-1, keepdims=True))
            weights.append((e / jnp.sum(e, axis=-1, keepdims=True)).astype(BF16))
        w_all = jnp.concatenate(weights, axis=1)
        mix_ref[at : at + PAIR, :] = jnp.dot(w_all, v_all, preferred_element_type=F32).astype(BF16)
    step = 128
    pick = step // 4
    src = lax.broadcasted_iota(jnp.int32, (step, step), 1)
    dst = lax.broadcasted_iota(jnp.int32, (step, step), 0)
    order = (src == 4 * (dst % pick) + dst // pick).astype(F32).astype(BF16)
    for i in range(rows // step):
        sorted_rows = jnp.dot(
            order, mix_ref[i * step : (i + 1) * step, :], preferred_element_type=F32
        ).astype(BF16)
        for t in range(4):
            out_ref[t, i * pick : (i + 1) * pick, :] = sorted_rows[t * pick : (t + 1) * pick]


def project_kernel(row0, mix0, mix1, mix2, mix3, w_ref, own_ref, gain_ref, out_ref):
    width = mix0.shape[1]
    rows = mix0.shape[0]
    total = own_ref[row0 : row0 + rows, :].astype(F32)
    for s, mix in enumerate((mix0, mix1, mix2, mix3)):
        total = total + jnp.dot(
            mix[...], w_ref[s * width : (s + 1) * width, :], preferred_element_type=F32
        )
    mean_sq = jnp.mean(total * total, axis=-1, keepdims=True)
    out_ref[...] = (total * lax.rsqrt(mean_sq + 1e-06) * gain_ref[...]).astype(BF16)


def place_kernel(n_ctx, ctx_ref, *refs):
    place_refs = refs[:n_ctx]
    row_refs = refs[n_ctx:-1]
    out_ref = refs[-1]
    spots = out_ref.shape[0]
    chunks = len(row_refs) // n_ctx
    total = None
    for key in range(n_ctx):
        target = place_refs[key][...] - ctx_ref[0] * spots
        grid = lax.broadcasted_iota(jnp.int32, (spots, target.shape[1]), 0)
        chosen = (grid == target).astype(F32).astype(BF16)
        for r in range(chunks):
            block = row_refs[key * chunks + r]
            count = block.shape[0]
            part = jnp.dot(
                chosen[:, r * count : (r + 1) * count], block[...], preferred_element_type=F32
            )
            total = part if total is None else total + part
    out_ref[...] = total.astype(BF16)


def local(n_ctx, n_ten, patches, valid, place, gain_attn, w_qkv, w_proj, gain_merge):
    rows, feat = patches.shape
    width = w_qkv.shape[2]
    depth = w_qkv.shape[0]
    groups = rows // 4
    ctx = lax.axis_index("context").astype(jnp.int32).reshape(1)
    ten = lax.axis_index("tensor").astype(jnp.int32).reshape(1)

    w_blocks = gather_xor(jnp.transpose(w_qkv, (1, 0, 2)), "context", n_ctx)
    proj = jnp.stack([w_proj] + [swap(w_proj, "tensor", n_ten, s) for s in range(1, n_ten)])
    places = gather_xor(place.reshape(1, groups), "context", n_ctx)

    hidden, own_patches = pl.pallas_call(
        norm_kernel,
        out_shape=(
            jax.ShapeDtypeStruct((rows, feat), BF16),
            jax.ShapeDtypeStruct((groups, feat), BF16),
        ),
        in_specs=[SMEM, VMEM, VMEM],
        out_specs=(VMEM, VMEM),
        compiler_params=params(32),
        name="norm",
    )(ten, patches, gain_attn.reshape(1, feat))

    proj_blocks = gather_xor(proj, "context", n_ctx)
    col = proj.shape[2]
    by_key = jnp.stack([proj_blocks[k] for k in range(n_ctx)])
    order = ctx[0] ^ jnp.arange(n_ctx, dtype=jnp.int32)
    w_full = jnp.transpose(by_key[order], (1, 2, 0, 3)).reshape(n_ten * width, n_ctx * col)

    valid_pairs = valid.reshape(rows // PAIR, PAIR)
    part = rows // CHUNKS
    gain2 = gain_merge.reshape(1, feat)
    finished = []
    for r in range(CHUNKS):
        mixed = pl.pallas_call(
            functools.partial(attention_kernel, n_ctx, r * part, part),
            out_shape=jax.ShapeDtypeStruct((n_ten, part // 4, width), BF16),
            in_specs=[SMEM, VMEM, VMEM] + [VMEM] * n_ctx,
            out_specs=VMEM,
            scratch_shapes=[
                pltpu.VMEM((3, feat, width), BF16),
                pltpu.VMEM((part, width), BF16),
                pltpu.VMEM((part, width), BF16),
                pltpu.VMEM((part, width), BF16),
                pltpu.VMEM((part, width), BF16),
            ],
            compiler_params=params(32),
            name="attention",
        )(ctx, hidden, valid_pairs, *[w_blocks[k] for k in range(n_ctx)])
        pieces = []
        for s in range(n_ten):
            piece = lax.dynamic_index_in_dim(mixed, ten[0] ^ s, 0, keepdims=False)
            pieces.append(piece if s == 0 else swap(piece, "tensor", n_ten, s))
        finished.append(
            pl.pallas_call(
                functools.partial(project_kernel, r * (part // 4)),
                out_shape=jax.ShapeDtypeStruct((part // 4, feat), BF16),
                in_specs=[VMEM] * 7,
                out_specs=VMEM,
                compiler_params=params(32),
                name="project",
            )(*pieces, w_full, own_patches, gain2)
        )
    gathered = [gather_xor(block, "context", n_ctx) for block in finished]
    return pl.pallas_call(
        functools.partial(place_kernel, n_ctx),
        out_shape=jax.ShapeDtypeStruct((groups, feat), BF16),
        in_specs=[SMEM] + [VMEM] * (n_ctx + n_ctx * CHUNKS),
        out_specs=VMEM,
        compiler_params=params(32),
        name="placement",
    )(
        ctx,
        *[places[k] for k in range(n_ctx)],
        *[gathered[r][k] for k in range(n_ctx) for r in range(CHUNKS)],
    )


def solution(mesh):
    in_specs = (
        P(("dp", "context"), None),
        P(("dp", "context")),
        P(("dp", "context")),
        P(),
        P("context", None, "tensor"),
        P("tensor", "context"),
        P(),
    )
    out_specs = P(("dp", "context"), "tensor")
    body = functools.partial(local, mesh.shape["context"], mesh.shape["tensor"])
    return jax.shard_map(body, mesh=mesh, in_specs=in_specs, out_specs=out_specs, check_vma=False)
```

time: 266 us -> 129 us (0.48)
  waiting for transfers between devices: 185 us -> 67 us
  starting transfers between devices: 0.09 us -> 19.8 us
  blocking collectives: 16.1 us -> 0 us
  matrix products: 15.4 us -> 0 us
  between operations: 13.9 us -> 0.16 us
  Pallas kernels: 0 us -> 13 us
  local copies, waits for them, and re-layouts: 29.2 us -> 21.7 us
    psum x1 -> x0, waiting for transfers between devices: 147 us -> none  [local(): head_total = lax.psum(partial_value, 'tensor')]
    ppermute x0 -> x18, waiting for transfers between devices: none -> 67 us  [swap(): return lax.ppermute(x, axis, [(i, i ^ bit) for i in range(size)])]
    all_gather x2 -> x0, waiting for transfers between devices: 38.4 us -> none  [the longest x1 23.8 us: local(): shard_piece = lax.all_gather(w_qkv, 'context', axis=0, tiled=True)]
    ppermute x0 -> x18, starting transfers between devices: none -> 19.8 us  [swap(): return lax.ppermute(x, axis, [(i, i ^ bit) for i in range(size)])]
    dot_general x5 -> x0, matrix products: 15.4 us -> none  [the longest x1 3.87 us: local(): projected = jnp.dot(hidden, flat_piece, preferred_element_type=jnp.float32)]
    pallas_call x0 -> x4, Pallas kernels: none -> 13 us  [the longest x1 8.22 us: local(): pl.pallas_call(functools.partial(attention_kernel, n_ctx, r * part, part)...]
    all_gather x1 -> x0, blocking collectives: 11.2 us -> none  [local(): lax.all_gather(w_proj, 'context', axis=1, tiled=True)]
    all_gather x1 -> x0, local copies, waits for them, and re-layouts: 7.44 us -> none  [local(): shard_piece = lax.all_gather(w_qkv, 'context', axis=0, tiled=True)]
  transfers between devices with their start and end apart: 3 -> 18, of which waited for: 3 -> 7; matrix products, arithmetic and copies ran while one was open for 1% -> 19% of each run, Pallas kernels for 0% -> 7%
where the time goes in v1:
time: 129 us; the launch traced here: 128 us
  waiting for transfers between devices  67 us (52%)
  local copies, waits for them, and re-layouts  21.7 us (17%)
  starting transfers between devices  19.8 us (15%)
  Pallas kernels  13 us (10%)
  other arithmetic  6.37 us (5%)
    ppermute x18, waiting for transfers between devices, swap(): return lax.ppermute(x, axis, [(i, i ^ bit) for i in range(size)])  67 us
    ppermute x18, starting transfers between devices, swap(): return lax.ppermute(x, axis, [(i, i ^ bit) for i in range(size)])  19.8 us
    pallas_call x1, Pallas kernels, local(): pl.pallas_call(functools.partial(attention_kernel, n_ctx, r * part, part)...  8.22 us
    transpose x1, local copies, waits for them, and re-layouts, local(): jnp.transpose(by_key[order], (1, 2, 0, 3))  7.03 us
    another operation x2, other arithmetic, local(): by_key = jnp.stack([proj_blocks[k] for k in range(n_ctx)])  6.35 us
    reshape x1, local copies, waits for them, and re-layouts, local(): jnp.transpose(by_key[order], (1, 2, 0, 3))  6.33 us
    gather x1, local copies, waits for them, and re-layouts, local(): by_key[order]  5.11 us
  transfers between devices with their start and end apart: 18, of which 7 were waited for; matrix products, arithmetic and copies ran while one was open for 19% of the time, Pallas kernels for 7%

profile of v1, /device:TPU:0, one launch (start us, length us, event | category | flops | bytes accessed | tf_op | source)
XLA Modules:
  0.0 128.0 jit_solution(2082794623511800774)
XLA Ops:
  0.0 3.1 %collective-permute-start.9 = (bf16[320,320]{1,0:T(8,128)(2,1)}, bf16[320,320]{1,0:T(8,128)(2,1)S(1)}, u32[]{:S(2)}, u32[]{:S(2)}) collective-permute-start(bf16[320,320]{1,0:T(8,128)(2,1)} %param.12), channel_id=1, source_target_pairs={{0,1},{1,0},{2,3},{3,2},{4,5},{5,4},{6,7},{7,6},{8,9},{9,8},{10,11... | collective-permute-start | bytes 614408 | tf_op jit(solution)/shard_map/ppermute | solution.py:25
  3.1 2.6 %collective-permute-start.10 = (bf16[320,320]{1,0:T(8,128)(2,1)}, bf16[320,320]{1,0:T(8,128)(2,1)S(1)}, u32[]{:S(2)}, u32[]{:S(2)}) collective-permute-start(bf16[320,320]{1,0:T(8,128)(2,1)} %param.12), channel_id=1, source_target_pairs={{0,2},{1,3},{2,0},{3,1},{4,6},{5,7},{6,4},{7,5},{8,10},{9,11},{10,... | collective-permute-start | bytes 614408 | tf_op jit(solution)/shard_map/ppermute | solution.py:25
  5.7 8.1 %collective-permute-done.9 = bf16[320,320]{1,0:T(8,128)(2,1)S(1)} collective-permute-done((bf16[320,320]{1,0:T(8,128)(2,1)}, bf16[320,320]{1,0:T(8,128)(2,1)S(1)}, u32[]{:S(2)}, u32[]{:S(2)}) %collective-permute-start.9) | collective-permute-done | bytes 204832 | tf_op jit(solution)/shard_map/ppermute | solution.py:25
  13.8 9.9 %collective-permute-done.10 = bf16[320,320]{1,0:T(8,128)(2,1)S(1)} collective-permute-done((bf16[320,320]{1,0:T(8,128)(2,1)}, bf16[320,320]{1,0:T(8,128)(2,1)S(1)}, u32[]{:S(2)}, u32[]{:S(2)}) %collective-permute-start.10) | collective-permute-done | bytes 204832 | tf_op jit(solution)/shard_map/ppermute | solution.py:25
  23.6 2.5 %fusion.1 = (bf16[1,4,320,320]{3,2,1,0:T(8,128)(2,1)}, bf16[4,320,320]{2,1,0:T(8,128)(2,1)}) fusion(bf16[1,320,320]{2,1,0:T(8,128)(2,1)S(1)} %bitcast.36, bf16[1,320,320]{2,1,0:T(8,128)(2,1)S(1)} %bitcast.35, bf16[1,320,320]{2,1,0:T(8,128)(2,1)S(1)} %bitcast.34, bf16[1,320,320]{2,1,0:T(8,128)(2,1)} %bitcast.33), kind=kLoop, calls=%fused_computation.10 | loop fusion | flops 1228800 | bytes 2457600 | tf_op jit(solution)/shard_map/stack | solution.py:168
  26.1 1.5 %collective-permute-start.13 = (bf16[4,320,320]{2,1,0:T(8,128)(2,1)}, bf16[4,320,320]{2,1,0:T(8,128)(2,1)}, u32[]{:S(2)}, u32[]{:S(2)}) collective-permute-start(bf16[4,320,320]{2,1,0:T(8,128)(2,1)} %get-tuple-element.10), channel_id=1, source_target_pairs={{0,8},{4,12},{8,0},{12,4},{1,9},{5,13},{9,1},{13,5},{2,10},{6,14},... | collective-permute-start | bytes 2457608 | tf_op jit(solution)/shard_map/ppermute | solution.py:25
  27.6 0.5 collective-permute-start.4
  28.2 23.0 %collective-permute-done.13 = bf16[4,320,320]{2,1,0:T(8,128)(2,1)} collective-permute-done((bf16[4,320,320]{2,1,0:T(8,128)(2,1)}, bf16[4,320,320]{2,1,0:T(8,128)(2,1)}, u32[]{:S(2)}, u32[]{:S(2)}) %collective-permute-start.13) | collective-permute-done | bytes 819232 | tf_op jit(solution)/shard_map/ppermute | solution.py:25
  51.1 0.5 collective-permute-start.3
  51.6 11.5 %collective-permute-done.4.refs_5_ = bf16[3,320,320]{2,1,0:T(8,128)(2,1)S(1)} collective-permute-done((bf16[3,320,320]{2,1,0:T(8,128)(2,1)}, bf16[3,320,320]{2,1,0:T(8,128)(2,1)S(1)}, u32[]{:S(2)}, u32[]{:S(2)}) %collective-permute-start.4) | collective-permute-done | bytes 614432 | tf_op jit(solution)/shard_map/ppermute | solution.py:25
  63.2 0.7 reshape.40.gain_ref
  63.9 0.7 reshape.43.gain_ref
  64.6 1.0 norm.1
  65.7 8.2 %attention.1 = bf16[4,192,320]{2,1,0:T(8,128)(2,1)S(1)} custom-call(s32[1]{0:T(128)} %bitcast.refs_0_.ctx_ref, bf16[768,1280]{1,0:T(8,128)(2,1)S(1)} %get-tuple-element.7.refs_1_, s32[6,128]{1,0:T(8,128)S(1)} %bitcast.28, bf16[3,320,320]{2,1,0:T(8,128)(2,1)S(1)} %bitcast.27, bf16[3,320,320]{2,1,0:T(8,128)(2,1)} %collective-permute-done.3.refs_4_, ...), custom_call_target="tpu_custom_call" | custom-call | tf_op jit(solution)/shard_map/attention/pallas_call | solution.py:177
  73.9 0.8 dynamic-slice_bitcast_fusion
  74.7 5.8 %collective-permute-start.6 = (bf16[192,320]{1,0:T(8,128)(2,1)}, bf16[192,320]{1,0:T(8,128)(2,1)}, u32[]{:S(2)}, u32[]{:S(2)}) collective-permute-start(bf16[192,320]{1,0:T(8,128)(2,1)} %get-tuple-element.13), channel_id=1, source_target_pairs={{0,1},{1,0},{2,3},{3,2},{4,5},{5,4},{6,7},{7,6},{8,9},{9,8},{10,11... | collective-permute-start | bytes 368648 | tf_op jit(solution)/shard_map/ppermute | solution.py:25
  80.5 1.0 collective-permute-start.7
  81.5 1.5 %collective-permute-start.8 = (bf16[192,320]{1,0:T(8,128)(2,1)}, bf16[192,320]{1,0:T(8,128)(2,1)}, u32[]{:S(2)}, u32[]{:S(2)}) collective-permute-start(bf16[192,320]{1,0:T(8,128)(2,1)} %get-tuple-element.11), channel_id=1, source_target_pairs={{0,3},{1,2},{2,1},{3,0},{4,7},{5,6},{6,5},{7,4},{8,11},{9,10},{10,... | collective-permute-start | bytes 368648 | tf_op jit(solution)/shard_map/ppermute | solution.py:25
  82.9 3.9 %pad_maximum_fusion = bf16[4,4,320,320]{3,2,1,0:T(8,128)(2,1)} fusion(bf16[1,4,320,320]{3,2,1,0:T(8,128)(2,1)} %bitcast.16, bf16[1,4,320,320]{3,2,1,0:T(8,128)(2,1)} %bitcast.15, bf16[1,4,320,320]{3,2,1,0:T(8,128)(2,1)} %bitcast.14, bf16[1,4,320,320]{3,2,1,0:T(8,128)(2,1)S(1)} %copy-done.6), kind=kLoop, calls=%fused_computation.1 | loop fusion | flops 4915200 | bytes 6553600 | tf_op jit(solution)/shard_map/stack | solution.py:168
  86.8 5.1 %gather_fusion = bf16[4,4,320,320]{3,2,1,0:T(8,128)(2,1)} fusion(bf16[4,4,320,320]{3,2,1,0:T(8,128)(2,1)} %pad_maximum_fusion, s32[1024]{0:T(1024)S(1)} %pad_clamp_fusion), kind=kCustom, calls=%fused_computation | custom fusion | bytes 6553616 | tf_op jit(solution)/shard_map/gather | solution.py:170
  91.9 7.0 %copy.8 = bf16[4,320,4,320]{3,2,1,0:T(4,128)(2,1)} copy(bf16[4,320,4,320]{3,1,0,2:T(8,128)(2,1)} %bitcast.32) | data formatting | bytes 6553600 | tf_op jit(solution)/shard_map/transpose | solution.py:170
  98.9 6.3 %reshape.42.w_ref = bf16[1280,1280]{1,0:T(8,128)(2,1)S(1)} reshape(bf16[4,320,4,320]{3,2,1,0:T(4,128)(2,1)} %copy.8) | data formatting | bytes 6553600 | tf_op jit(solution)/shard_map/reshape | solution.py:170
  105.3 0.0 copy-start.3
  105.3 1.0 copy-done.3
  106.3 2.3 %project.1.refs_4_ = bf16[192,1280]{1,0:T(8,128)(2,1)S(1)} custom-call(bf16[192,320]{1,0:T(8,128)(2,1)S(1)} %get-tuple-element.14.mix0, bf16[192,320]{1,0:T(8,128)(2,1)} %collective-permute-done.6.mix1, bf16[192,320]{1,0:T(8,128)(2,1)} %collective-permute-done.7.mix2, bf16[192,320]{1,0:T(8,128)(2,1)} %collective-permute-done.8.mix3, ...), custom_call_target="tpu_custom_call" | custom-call | tf_op jit(solution)/shard_map/project/pallas_call | solution.py:197
  108.7 1.6 %collective-permute-start.16 = (bf16[192,1280]{1,0:T(8,128)(2,1)S(1)}, bf16[192,1280]{1,0:T(8,128)(2,1)S(1)}, u32[]{:S(2)}, u32[]{:S(2)}) collective-permute-start(bf16[192,1280]{1,0:T(8,128)(2,1)S(1)} %project.1.refs_4_), channel_id=1, source_target_pairs={{0,8},{4,12},{8,0},{12,4},{1,9},{5,13},{9,1},{13,5},{2,10},{6,14},... | collective-permute-start | bytes 1474568 | tf_op jit(solution)/shard_map/ppermute | solution.py:25
  110.3 11.5 %collective-permute-done.16.refs_6_ = bf16[192,1280]{1,0:T(8,128)(2,1)S(1)} collective-permute-done((bf16[192,1280]{1,0:T(8,128)(2,1)S(1)}, bf16[192,1280]{1,0:T(8,128)(2,1)S(1)}, u32[]{:S(2)}, u32[]{:S(2)}) %collective-permute-start.16) | collective-permute-done | bytes 491552 | tf_op jit(solution)/shard_map/ppermute | solution.py:25
  121.8 1.5 %collective-permute-start.1 = (s32[1,192]{1,0:T(1,128)S(1)}, s32[1,192]{1,0:T(1,128)S(1)}, u32[]{:S(2)}, u32[]{:S(2)}) collective-permute-start(s32[1,192]{1,0:T(1,128)S(1)} %bitcast.29), channel_id=1, source_target_pairs={{0,8},{4,12},{8,0},{12,4},{1,9},{5,13},{9,1},{13,5},{2,10},{6,14},... | collective-permute-start | bytes 2312 | tf_op jit(solution)/shard_map/ppermute | solution.py:25
  123.4 0.2 collective-permute-start
  123.6 1.8 %collective-permute-done.1.refs_2_ = s32[1,192]{1,0:T(1,128)S(1)} collective-permute-done((s32[1,192]{1,0:T(1,128)S(1)}, s32[1,192]{1,0:T(1,128)S(1)}, u32[]{:S(2)}, u32[]{:S(2)}) %collective-permute-start.1) | collective-permute-done | bytes 800 | tf_op jit(solution)/shard_map/ppermute | solution.py:25
  125.4 1.1 collective-permute-done.2.refs_3_
  126.6 1.4 %placement.1 = bf16[192,1280]{1,0:T(8,128)(2,1)} custom-call(s32[1]{0:T(128)} %bitcast.refs_0_.ctx_ref, s32[1,192]{1,0:T(1,128)S(1)} %bitcast.31, s32[1,192]{1,0:T(1,128)S(1)} %collective-permute-done.refs_1_, s32[1,192]{1,0:T(1,128)S(1)} %collective-permute-done.1.refs_2_, s32[1,192]{1,0:T(1,128)S(1)} %collective-permute-done.2.refs_3_, ...), custom_call_target="tpu_custom_call" | custom-call | tf_op jit(solution)/shard_map/placement/pallas_call | solution.py:207
  (32 shorter events, 0.1 us)
Async XLA Ops:
  0.0 65.6 %copy-start.1 = (bf16[320,3,320]{2,0,1:T(8,128)(2,1)S(1)}, bf16[320,3,320]{2,0,1:T(8,128)(2,1)}, u32[]{:S(2)}) copy-start(bf16[320,3,320]{2,0,1:T(8,128)(2,1)} %param.11) | copy-start | bytes 1843204
  0.0 64.6 %copy-start = (bf16[768,1280]{1,0:T(8,128)(2,1)S(1)}, bf16[768,1280]{1,0:T(8,128)(2,1)}, u32[]{:S(2)}) copy-start(bf16[768,1280]{1,0:T(8,128)(2,1)} %patches_ref.1) | copy-start | bytes 5898244
  0.0 65.7 %copy-start.4 = (s32[768]{0:T(1024)S(1)}, s32[768]{0:T(1024)}, u32[]{:S(2)}) copy-start(s32[768]{0:T(1024)} %param.8) | copy-start | bytes 9220
  0.0 13.8 %collective-permute-start.9 = (bf16[320,320]{1,0:T(8,128)(2,1)}, bf16[320,320]{1,0:T(8,128)(2,1)S(1)}, u32[]{:S(2)}, u32[]{:S(2)}) collective-permute-start(bf16[320,320]{1,0:T(8,128)(2,1)} %param.12), channel_id=1, source_target_pairs={{0,1},{1,0},{2,3},{3,2},{4,5},{5,4},{6,7},{7,6},{8,9},{9,8},{10,11... | collective-permute-start | bytes 614408 | tf_op jit(solution)/shard_map/ppermute | solution.py:25
  3.1 20.5 %collective-permute-start.10 = (bf16[320,320]{1,0:T(8,128)(2,1)}, bf16[320,320]{1,0:T(8,128)(2,1)S(1)}, u32[]{:S(2)}, u32[]{:S(2)}) collective-permute-start(bf16[320,320]{1,0:T(8,128)(2,1)} %param.12), channel_id=1, source_target_pairs={{0,2},{1,3},{2,0},{3,1},{4,6},{5,7},{6,4},{7,5},{8,10},{9,11},{10,... | collective-permute-start | bytes 614408 | tf_op jit(solution)/shard_map/ppermute | solution.py:25
  5.7 17.9 %collective-permute-start.11 = (bf16[320,320]{1,0:T(8,128)(2,1)}, bf16[320,320]{1,0:T(8,128)(2,1)S(1)}, u32[]{:S(2)}, u32[]{:S(2)}) collective-permute-start(bf16[320,320]{1,0:T(8,128)(2,1)} %param.12), channel_id=1, source_target_pairs={{0,3},{1,2},{2,1},{3,0},{4,7},{5,6},{6,5},{7,4},{8,11},{9,10},{10,... | collective-permute-start | bytes 614408 | tf_op jit(solution)/shard_map/ppermute | solution.py:25
  26.1 25.0 %collective-permute-start.13 = (bf16[4,320,320]{2,1,0:T(8,128)(2,1)}, bf16[4,320,320]{2,1,0:T(8,128)(2,1)}, u32[]{:S(2)}, u32[]{:S(2)}) collective-permute-start(bf16[4,320,320]{2,1,0:T(8,128)(2,1)} %get-tuple-element.10), channel_id=1, source_target_pairs={{0,8},{4,12},{8,0},{12,4},{1,9},{5,13},{9,1},{13,5},{2,10},{6,14},... | collective-permute-start | bytes 2457608 | tf_op jit(solution)/shard_map/ppermute | solution.py:25
  27.6 35.5 %collective-permute-start.4 = (bf16[3,320,320]{2,1,0:T(8,128)(2,1)}, bf16[3,320,320]{2,1,0:T(8,128)(2,1)S(1)}, u32[]{:S(2)}, u32[]{:S(2)}) collective-permute-start(bf16[3,320,320]{2,1,0:T(8,128)(2,1)} %bitcast.25), channel_id=1, source_target_pairs={{0,8},{4,12},{8,0},{12,4},{1,9},{5,13},{9,1},{13,5},{2,10},{6,14},... | collective-permute-start | bytes 1843208 | tf_op jit(solution)/shard_map/ppermute | solution.py:25
  28.2 54.8 %collective-permute-start.12 = (bf16[4,320,320]{2,1,0:T(8,128)(2,1)}, bf16[4,320,320]{2,1,0:T(8,128)(2,1)}, u32[]{:S(2)}, u32[]{:S(2)}) collective-permute-start(bf16[4,320,320]{2,1,0:T(8,128)(2,1)} %get-tuple-element.10), channel_id=1, source_target_pairs={{0,4},{4,0},{8,12},{12,8},{1,5},{5,1},{9,13},{13,9},{2,6},{6,2},{1... | collective-permute-start | bytes 2457608 | tf_op jit(solution)/shard_map/ppermute | solution.py:25
  51.1 31.8 %collective-permute-start.14 = (bf16[4,320,320]{2,1,0:T(8,128)(2,1)}, bf16[4,320,320]{2,1,0:T(8,128)(2,1)}, u32[]{:S(2)}, u32[]{:S(2)}) collective-permute-start(bf16[4,320,320]{2,1,0:T(8,128)(2,1)} %collective-permute-done.13), channel_id=1, source_target_pairs={{0,4},{4,0},{8,12},{12,8},{1,5},{5,1},{9,13},{13,9},{2,6},{6,2},{1... | collective-permute-start | bytes 2457608 | tf_op jit(solution)/shard_map/ppermute | solution.py:25
  51.1 14.5 %collective-permute-start.3 = (bf16[3,320,320]{2,1,0:T(8,128)(2,1)}, bf16[3,320,320]{2,1,0:T(8,128)(2,1)}, u32[]{:S(2)}, u32[]{:S(2)}) collective-permute-start(bf16[3,320,320]{2,1,0:T(8,128)(2,1)} %bitcast.26), channel_id=1, source_target_pairs={{0,4},{4,0},{8,12},{12,8},{1,5},{5,1},{9,13},{13,9},{2,6},{6,2},{1... | collective-permute-start | bytes 1843208 | tf_op jit(solution)/shard_map/ppermute | solution.py:25
  63.2 2.5 %collective-permute-start.5 = (bf16[3,320,320]{2,1,0:T(8,128)(2,1)S(1)}, bf16[3,320,320]{2,1,0:T(8,128)(2,1)}, u32[]{:S(2)}, u32[]{:S(2)}) collective-permute-start(bf16[3,320,320]{2,1,0:T(8,128)(2,1)S(1)} %collective-permute-done.4.refs_5_), channel_id=1, source_target_pairs={{0,4},{4,0},{8,12},{12,8},{1,5},{5,1},{9,13},{13,9},{2,6},{6,2},{1... | collective-permute-start | bytes 1843208 | tf_op jit(solution)/shard_map/ppermute | solution.py:25
  64.6 18.4 %copy-start.6 = (bf16[1,4,320,320]{3,2,1,0:T(8,128)(2,1)S(1)}, bf16[1,4,320,320]{3,2,1,0:T(8,128)(2,1)}, u32[]{:S(2)}) copy-start(bf16[1,4,320,320]{3,2,1,0:T(8,128)(2,1)} %get-tuple-element.9) | copy-start | bytes 2457604
  65.6 9.1 %copy-start.2 = (bf16[192,1280]{1,0:T(8,128)(2,1)}, bf16[192,1280]{1,0:T(8,128)(2,1)S(1)}, u32[]{:S(2)}) copy-start(bf16[192,1280]{1,0:T(8,128)(2,1)S(1)} %get-tuple-element.8.own_ref) | copy-start | bytes 1474564
  74.7 30.6 %collective-permute-start.6 = (bf16[192,320]{1,0:T(8,128)(2,1)}, bf16[192,320]{1,0:T(8,128)(2,1)}, u32[]{:S(2)}, u32[]{:S(2)}) collective-permute-start(bf16[192,320]{1,0:T(8,128)(2,1)} %get-tuple-element.13), channel_id=1, source_target_pairs={{0,1},{1,0},{2,3},{3,2},{4,5},{5,4},{6,7},{7,6},{8,9},{9,8},{10,11... | collective-permute-start | bytes 368648 | tf_op jit(solution)/shard_map/ppermute | solution.py:25
  80.5 24.8 %collective-permute-start.7 = (bf16[192,320]{1,0:T(8,128)(2,1)}, bf16[192,320]{1,0:T(8,128)(2,1)}, u32[]{:S(2)}, u32[]{:S(2)}) collective-permute-start(bf16[192,320]{1,0:T(8,128)(2,1)} %get-tuple-element.12), channel_id=1, source_target_pairs={{0,2},{1,3},{2,0},{3,1},{4,6},{5,7},{6,4},{7,5},{8,10},{9,11},{10,... | collective-permute-start | bytes 368648 | tf_op jit(solution)/shard_map/ppermute | solution.py:25
  81.5 23.8 %collective-permute-start.8 = (bf16[192,320]{1,0:T(8,128)(2,1)}, bf16[192,320]{1,0:T(8,128)(2,1)}, u32[]{:S(2)}, u32[]{:S(2)}) collective-permute-start(bf16[192,320]{1,0:T(8,128)(2,1)} %get-tuple-element.11), channel_id=1, source_target_pairs={{0,3},{1,2},{2,1},{3,0},{4,7},{5,6},{6,5},{7,4},{8,11},{9,10},{10,... | collective-permute-start | bytes 368648 | tf_op jit(solution)/shard_map/ppermute | solution.py:25
  105.3 16.6 %copy-start.5 = (s32[192]{0:T(256)S(1)}, s32[192]{0:T(256)}, u32[]{:S(2)}) copy-start(s32[192]{0:T(256)} %param.9) | copy-start | bytes 2308
  105.3 1.0 copy-start.3
  108.7 13.1 %collective-permute-start.16 = (bf16[192,1280]{1,0:T(8,128)(2,1)S(1)}, bf16[192,1280]{1,0:T(8,128)(2,1)S(1)}, u32[]{:S(2)}, u32[]{:S(2)}) collective-permute-start(bf16[192,1280]{1,0:T(8,128)(2,1)S(1)} %project.1.refs_4_), channel_id=1, source_target_pairs={{0,8},{4,12},{8,0},{12,4},{1,9},{5,13},{9,1},{13,5},{2,10},{6,14},... | collective-permute-start | bytes 1474568 | tf_op jit(solution)/shard_map/ppermute | solution.py:25
  110.3 16.3 %collective-permute-start.15 = (bf16[192,1280]{1,0:T(8,128)(2,1)S(1)}, bf16[192,1280]{1,0:T(8,128)(2,1)S(1)}, u32[]{:S(2)}, u32[]{:S(2)}) collective-permute-start(bf16[192,1280]{1,0:T(8,128)(2,1)S(1)} %project.1.refs_4_), channel_id=1, source_target_pairs={{0,4},{4,0},{8,12},{12,8},{1,5},{5,1},{9,13},{13,9},{2,6},{6,2},{1... | collective-permute-start | bytes 1474568 | tf_op jit(solution)/shard_map/ppermute | solution.py:25
  121.8 4.7 %collective-permute-start.17 = (bf16[192,1280]{1,0:T(8,128)(2,1)S(1)}, bf16[192,1280]{1,0:T(8,128)(2,1)S(1)}, u32[]{:S(2)}, u32[]{:S(2)}) collective-permute-start(bf16[192,1280]{1,0:T(8,128)(2,1)S(1)} %collective-permute-done.16.refs_6_), channel_id=1, source_target_pairs={{0,4},{4,0},{8,12},{12,8},{1,5},{5,1},{9,13},{13,9},{2,6},{6,2},{1... | collective-permute-start | bytes 1474568 | tf_op jit(solution)/shard_map/ppermute | solution.py:25
  121.8 3.6 %collective-permute-start.1 = (s32[1,192]{1,0:T(1,128)S(1)}, s32[1,192]{1,0:T(1,128)S(1)}, u32[]{:S(2)}, u32[]{:S(2)}) collective-permute-start(s32[1,192]{1,0:T(1,128)S(1)} %bitcast.29), channel_id=1, source_target_pairs={{0,8},{4,12},{8,0},{12,4},{1,9},{5,13},{9,1},{13,5},{2,10},{6,14},... | collective-permute-start | bytes 2312 | tf_op jit(solution)/shard_map/ppermute | solution.py:25
  123.4 2.0 %collective-permute-start = (s32[1,192]{1,0:T(1,128)S(1)}, s32[1,192]{1,0:T(1,128)S(1)}, u32[]{:S(2)}, u32[]{:S(2)}) collective-permute-start(s32[1,192]{1,0:T(1,128)S(1)} %bitcast.30), channel_id=1, source_target_pairs={{0,4},{4,0},{8,12},{12,8},{1,5},{5,1},{9,13},{13,9},{2,6},{6,2},{1... | collective-permute-start | bytes 2312 | tf_op jit(solution)/shard_map/ppermute | solution.py:25
  125.4 1.1 collective-permute-start.2

commit v2 on v1

v2 whole, which is shorter than its diff:
```python
import functools

import jax
import jax.numpy as jnp
from jax import lax
from jax.experimental import pallas as pl
from jax.experimental.pallas import tpu as pltpu
from jax.sharding import PartitionSpec as P

HD = 80
WIN = 64
PAIR = 2 * WIN
CHUNKS = 2
F32 = jnp.float32
BF16 = jnp.bfloat16
VMEM = pl.BlockSpec(memory_space=pltpu.VMEM)
SMEM = pl.BlockSpec(memory_space=pltpu.SMEM)


def params(mib):
    return pltpu.CompilerParams(vmem_limit_bytes=mib * 1024 * 1024)


def swap(x, axis, size, bit):
    return lax.ppermute(x, axis, [(i, i ^ bit) for i in range(size)])


def cross_keys(size):
    return range(2, size, 2)


def gather_cross(x, size):
    blocks = {0: x}
    bit = size // 2
    while bit > 1:
        for key in list(blocks):
            blocks[key ^ bit] = swap(blocks[key], "context", size, bit)
        bit //= 2
    return blocks


def gather_xor(x, size):
    blocks = gather_cross(x, size)
    for key in list(blocks):
        blocks[key ^ 1] = swap(blocks[key], "context", size, 1)
    return blocks


def one_hot(mask):
    return mask.astype(F32).astype(BF16)


def norm_kernel(n_ctx, index_ref, *refs):
    place_refs = refs[:n_ctx]
    patches_ref, gain_ref, hidden_ref, own_ref, chosen_ref = refs[n_ctx:]
    rows = patches_ref.shape[0]
    x = patches_ref[...]
    xf = x.astype(F32)
    mean_sq = jnp.mean(xf * xf, axis=-1, keepdims=True)
    hidden_ref[...] = (xf * lax.rsqrt(mean_sq + 1e-06) * gain_ref[...]).astype(BF16)
    step = 256
    pick = step // 4
    row = lax.broadcasted_iota(jnp.int32, (pick, step), 0)
    col = lax.broadcasted_iota(jnp.int32, (pick, step), 1)
    chosen = one_hot(col == 4 * row + index_ref[1])
    for i in range(rows // step):
        own_ref[i * pick : (i + 1) * pick, :] = jnp.dot(
            chosen, x[i * step : (i + 1) * step], preferred_element_type=F32
        ).astype(BF16)
    spots = chosen_ref.shape[1]
    for key in range(n_ctx):
        target = place_refs[key][...] - index_ref[0] * spots
        grid = lax.broadcasted_iota(jnp.int32, (spots, target.shape[1]), 0)
        chosen_ref[key] = one_hot(grid == target)


def attend(row0, hidden_ref, valid_ref, w_ref, out_ref, q_ref, k_ref, v_ref, mix_ref):
    rows = q_ref.shape[0]
    width = q_ref.shape[1]
    heads = width // HD
    hidden = hidden_ref[row0 : row0 + rows, :]
    for j, ref in enumerate((q_ref, k_ref, v_ref)):
        ref[...] = jnp.dot(hidden, w_ref[j], preferred_element_type=F32).astype(BF16)
    lane = lax.broadcasted_iota(jnp.int32, (1, width), 1)
    head_masks = [one_hot((lane >= h * HD) & (lane < (h + 1) * HD)) for h in range(heads)]
    q_win = lax.broadcasted_iota(jnp.int32, (PAIR, PAIR), 0) // WIN
    k_win = lax.broadcasted_iota(jnp.int32, (PAIR, PAIR), 1) // WIN
    same = q_win == k_win
    floor = jnp.where(same, F32(-1e30), F32(-3e38))
    for p in range(rows // PAIR):
        at = p * PAIR
        q = q_ref[at : at + PAIR, :]
        k = k_ref[at : at + PAIR, :]
        v = v_ref[at : at + PAIR, :]
        k_all = jnp.concatenate([k * m for m in head_masks], axis=0)
        v_all = jnp.concatenate([v * m for m in head_masks], axis=0)
        scores = lax.dot_general(q, k_all, (((1,), (1,)), ((), ())), preferred_element_type=F32)
        live = valid_ref[row0 // PAIR + p : row0 // PAIR + p + 1, :] > 0
        weights = []
        for h in range(heads):
            s = scores[:, h * PAIR : (h + 1) * PAIR] * F32(HD ** (-0.5))
            s = jnp.where(same & live, s, floor)
            e = jnp.exp(s - jnp.max(s, axis=-1, keepdims=True))
            weights.append((e / jnp.sum(e, axis=-1, keepdims=True)).astype(BF16))
        w_all = jnp.concatenate(weights, axis=1)
        mix_ref[at : at + PAIR, :] = jnp.dot(w_all, v_all, preferred_element_type=F32).astype(BF16)
    pick = PAIR // 4
    src = lax.broadcasted_iota(jnp.int32, (PAIR, PAIR), 1)
    dst = lax.broadcasted_iota(jnp.int32, (PAIR, PAIR), 0)
    order = one_hot(src == 4 * (dst % pick) + dst // pick)
    for i in range(rows // PAIR):
        sorted_rows = jnp.dot(
            order, mix_ref[i * PAIR : (i + 1) * PAIR, :], preferred_element_type=F32
        ).astype(BF16)
        for t in range(4):
            out_ref[t, i * pick : (i + 1) * pick, :] = sorted_rows[t * pick : (t + 1) * pick]


def first_attention_kernel(n_ctx, index_ref, hidden_ref, valid_ref, *refs):
    shards = list(refs[: 2 + 3 * (n_ctx - 2)])
    out_ref, w_ref, *scratch = refs[len(shards) :]
    depth = shards[0].shape[1]
    me = index_ref[0]
    part = index_ref[2]
    for key in range(n_ctx):
        at = pl.multiple_of((me ^ key) * depth, depth)
        if key < 2:
            block = shards.pop(0)
            for j in range(3):
                w_ref[j, pl.ds(at, depth), :] = block[j]
        else:
            for j in (part, 1 - part, 2):
                w_ref[j, pl.ds(at, depth), :] = shards.pop(0)[...]
    attend(0, hidden_ref, valid_ref, w_ref, out_ref, *scratch)


def next_attention_kernel(row0, hidden_ref, valid_ref, w_ref, out_ref, *scratch):
    attend(row0, hidden_ref, valid_ref, w_ref, out_ref, *scratch)


def project_kernel(n_ctx, row0, index_ref, *refs):
    mixes = [m[...] for m in refs[:4]]
    blocks = list(refs[4 : 4 + 2 + 2 * (n_ctx - 2)])
    own_ref, gain_ref, out_ref, part_ref = refs[4 + len(blocks) :]
    rows = out_ref.shape[0]
    me = index_ref[0]
    flip = index_ref[2] > 0
    low = jnp.concatenate(mixes[:2], axis=1)
    high = jnp.concatenate(mixes[2:], axis=1)
    first = jnp.where(flip, high, low)
    second = jnp.where(flip, low, high)
    col = blocks[0].shape[2]

    def times(mix, ref, at):
        w = ref[at : at + 2].reshape(mix.shape[1], col)
        return jnp.dot(mix, w, preferred_element_type=F32)

    for key in range(n_ctx):
        if key < 2:
            block = blocks.pop(0)
            part_ref[me ^ key] = times(low, block, 0) + times(high, block, 2)
        else:
            part_ref[me ^ key] = times(first, blocks.pop(0), 0) + times(second, blocks.pop(0), 0)
    total = jnp.concatenate([part_ref[i] for i in range(n_ctx)], axis=1)
    total = total + own_ref[row0 : row0 + rows, :].astype(F32)
    mean_sq = jnp.mean(total * total, axis=-1, keepdims=True)
    out_ref[...] = (total * lax.rsqrt(mean_sq + 1e-06) * gain_ref[...]).astype(BF16)


def place_kernel(n_ctx, chosen_ref, *refs):
    row_refs = refs[:-1]
    out_ref = refs[-1]
    chunks = len(row_refs) // n_ctx
    total = None
    for key in range(n_ctx):
        for r in range(chunks):
            block = row_refs[key * chunks + r]
            count = block.shape[0]
            part = jnp.dot(
                chosen_ref[key, :, r * count : (r + 1) * count],
                block[...],
                preferred_element_type=F32,
            )
            total = part if total is None else total + part
    out_ref[...] = total.astype(BF16)


def local(n_dp, n_ctx, n_ten, patches, valid, place, gain_attn, w_qkv, w_proj, gain_merge):
    rows, feat = patches.shape
    width = w_qkv.shape[2]
    groups = rows // 4
    ten = lax.axis_index("tensor")
    half = lax.axis_index("dp") % 2
    index = jnp.stack([lax.axis_index("context"), ten, half]).astype(jnp.int32)

    w3 = jnp.transpose(w_qkv, (1, 0, 2))
    near = gather_cross(lax.dynamic_index_in_dim(w3, half, 0, keepdims=False), n_ctx)
    last = gather_cross(w3[2], n_ctx)
    shards = {0: [w3], 1: [swap(w3, "context", n_ctx, 1)]}
    for key in cross_keys(n_ctx):
        shards[key] = [near[key], swap(near[key], "dp", n_dp, 1), last[key]]
        shards[key ^ 1] = [swap(x, "context", n_ctx, 1) for x in shards[key]]

    pieces = [w_proj] + [swap(w_proj, "tensor", n_ten, s) for s in range(1, n_ten)]
    proj = jnp.stack(pieces)
    mine = gather_cross(lax.dynamic_slice_in_dim(proj, half * 2, 2, 0), n_ctx)
    blocks = {0: [proj], 1: [swap(proj, "context", n_ctx, 1)]}
    for key in cross_keys(n_ctx):
        blocks[key] = [mine[key], swap(mine[key], "dp", n_dp, 1)]
        blocks[key ^ 1] = [swap(x, "context", n_ctx, 1) for x in blocks[key]]

    places = gather_xor(place.reshape(1, groups), n_ctx)
    hidden, own_patches, chosen = pl.pallas_call(
        functools.partial(norm_kernel, n_ctx),
        out_shape=(
            jax.ShapeDtypeStruct((rows, feat), BF16),
            jax.ShapeDtypeStruct((groups, feat), BF16),
            jax.ShapeDtypeStruct((n_ctx, groups, groups), BF16),
        ),
        in_specs=[SMEM] + [VMEM] * (n_ctx + 2),
        out_specs=(VMEM, VMEM, VMEM),
        compiler_params=params(32),
        name="norm",
    )(index, *[places[k] for k in range(n_ctx)], patches, gain_attn.reshape(1, feat))

    valid_pairs = valid.reshape(rows // PAIR, PAIR)
    part = rows // CHUNKS
    gain2 = gain_merge.reshape(1, feat)
    mix_shape = jax.ShapeDtypeStruct((n_ten, part // 4, width), BF16)
    scratch = [pltpu.VMEM((part, width), BF16)] * 4
    shard_list = [x for k in range(n_ctx) for x in shards[k]]
    block_list = [x for k in range(n_ctx) for x in blocks[k]]
    w_full = None
    gathered = []
    for r in range(CHUNKS):
        if r == 0:
            mixed, w_full = pl.pallas_call(
                functools.partial(first_attention_kernel, n_ctx),
                out_shape=(mix_shape, jax.ShapeDtypeStruct((3, feat, width), BF16)),
                in_specs=[SMEM] + [VMEM] * (2 + len(shard_list)),
                out_specs=(VMEM, VMEM),
                scratch_shapes=scratch,
                compiler_params=params(32),
                name="attention0",
            )(index, hidden, valid_pairs, *shard_list)
        else:
            mixed = pl.pallas_call(
                functools.partial(next_attention_kernel, r * part),
                out_shape=mix_shape,
                in_specs=[VMEM] * 3,
                out_specs=VMEM,
                scratch_shapes=scratch,
                compiler_params=params(32),
                name="attention" + str(r),
            )(hidden, valid_pairs, w_full)
        mixes = []
        for s in range(n_ten):
            piece = lax.dynamic_index_in_dim(mixed, ten ^ s, 0, keepdims=False)
            mixes.append(piece if s == 0 else swap(piece, "tensor", n_ten, s))
        done = pl.pallas_call(
            functools.partial(project_kernel, n_ctx, r * (part // 4)),
            out_shape=jax.ShapeDtypeStruct((part // 4, feat), BF16),
            in_specs=[SMEM] + [VMEM] * (n_ten + len(block_list) + 2),
            out_specs=VMEM,
            scratch_shapes=[pltpu.VMEM((n_ctx, part // 4, w_proj.shape[1]), F32)],
            compiler_params=params(32),
            name="project" + str(r),
        )(index, *mixes, *block_list, own_patches, gain2)
        gathered.append(gather_xor(done, n_ctx))
    return pl.pallas_call(
        functools.partial(place_kernel, n_ctx),
        out_shape=jax.ShapeDtypeStruct((groups, feat), BF16),
        in_specs=[VMEM] * (1 + n_ctx * CHUNKS),
        out_specs=VMEM,
        compiler_params=params(32),
        name="placement",
    )(chosen, *[gathered[r][k] for k in range(n_ctx) for r in range(CHUNKS)])


def solution(mesh):
    in_specs = (
        P(("dp", "context"), None),
        P(("dp", "context")),
        P(("dp", "context")),
        P(),
        P("context", None, "tensor"),
        P("tensor", "context"),
        P(),
    )
    out_specs = P(("dp", "context"), "tensor")
    sizes = [mesh.shape[name] for name in ("dp", "context", "tensor")]
    body = functools.partial(local, *sizes)
    return jax.shard_map(body, mesh=mesh, in_specs=in_specs, out_specs=out_specs, check_vma=False)
```

time: 129 us -> 106 us (0.82)
  local copies, waits for them, and re-layouts: 21.7 us -> 2.45 us
  waiting for transfers between devices: 67 us -> 52.1 us
  starting transfers between devices: 19.8 us -> 32.8 us
  other arithmetic: 6.37 us -> 1.27 us
  Pallas kernels: 13 us -> 17.1 us
    ppermute x18 -> x30, waiting for transfers between devices: 67 us -> 52.1 us  [swap(): return lax.ppermute(x, axis, [(i, i ^ bit) for i in range(size)])]
    ppermute x18 -> x30, starting transfers between devices: 19.8 us -> 32.8 us  [swap(): return lax.ppermute(x, axis, [(i, i ^ bit) for i in range(size)])]
    transpose x1 -> x0, local copies, waits for them, and re-layouts: 7.03 us -> none  [local(): jnp.transpose(by_key[order], (1, 2, 0, 3))]
    reshape x1 -> x0, local copies, waits for them, and re-layouts: 6.33 us -> none  [local(): jnp.transpose(by_key[order], (1, 2, 0, 3))]
    gather x1 -> x0, local copies, waits for them, and re-layouts: 5.11 us -> none  [local(): by_key[order]]
    another operation x2, other arithmetic: 6.35 us -> 1.27 us  [the longest x1 1.2 us: local(): proj = jnp.stack(pieces)]
    pallas_call x3 -> x5, Pallas kernels: 11.6 us -> 15.1 us  [the longest x1 5.13 us: local(): pl.pallas_call(functools.partial(first_attention_kernel, n_ctx), out_shap...]
  transfers between devices with their start and end apart: 18 -> 30, of which waited for: 7 -> 14; matrix products, arithmetic and copies ran while one was open for 19% -> 0% of each run, Pallas kernels for 7% -> 14%
where the time goes in v2:
time: 106 us
  waiting for transfers between devices  52.1 us (49%)
  starting transfers between devices  32.8 us (31%)
  Pallas kernels  17.1 us (16%)
  local copies, waits for them, and re-layouts  2.45 us (2%)
  other arithmetic  1.27 us (1%)
    ppermute x30, waiting for transfers between devices, swap(): return lax.ppermute(x, axis, [(i, i ^ bit) for i in range(size)])  52.1 us
    ppermute x30, starting transfers between devices, swap(): return lax.ppermute(x, axis, [(i, i ^ bit) for i in range(size)])  32.8 us
    pallas_call x1, Pallas kernels, local(): pl.pallas_call(functools.partial(first_attention_kernel, n_ctx), out_shap...  5.13 us
    pallas_call x2, Pallas kernels, local(): pl.pallas_call(functools.partial(project_kernel, n_ctx, r * (part // 4)),...  4.96 us
    pallas_call x1, Pallas kernels, local(): pl.pallas_call(functools.partial(next_attention_kernel, r * part), out_sh...  3.36 us
    unnamed x16, local copies, waits for them, and re-layouts  2.26 us
  transfers between devices with their start and end apart: 30, of which 14 were waited for; matrix products, arithmetic and copies ran while one was open for 0% of the time, Pallas kernels for 14%

profile of v2, /device:TPU:0, one launch (start us, length us, event | category | flops | bytes accessed | tf_op | source)
XLA Modules:
  0.0 105.9 jit_solution(15563808875556742601)
XLA Ops:
  0.0 3.0 %collective-permute-start.13 = (bf16[320,320]{1,0:T(8,128)(2,1)}, bf16[320,320]{1,0:T(8,128)(2,1)S(1)}, u32[]{:S(2)}, u32[]{:S(2)}) collective-permute-start(bf16[320,320]{1,0:T(8,128)(2,1)} %param.12), channel_id=1, source_target_pairs={{0,1},{1,0},{2,3},{3,2},{4,5},{5,4},{6,7},{7,6},{8,9},{9,8},{10,11... | collective-permute-start | bytes 614408 | tf_op jit(solution)/shard_map/ppermute | solution.py:25
  3.0 2.6 %collective-permute-start.14 = (bf16[320,320]{1,0:T(8,128)(2,1)}, bf16[320,320]{1,0:T(8,128)(2,1)S(1)}, u32[]{:S(2)}, u32[]{:S(2)}) collective-permute-start(bf16[320,320]{1,0:T(8,128)(2,1)} %param.12), channel_id=1, source_target_pairs={{0,2},{1,3},{2,0},{3,1},{4,6},{5,7},{6,4},{7,5},{8,10},{9,11},{10,... | collective-permute-start | bytes 614408 | tf_op jit(solution)/shard_map/ppermute | solution.py:25
  5.6 8.1 %collective-permute-done.13 = bf16[320,320]{1,0:T(8,128)(2,1)S(1)} collective-permute-done((bf16[320,320]{1,0:T(8,128)(2,1)}, bf16[320,320]{1,0:T(8,128)(2,1)S(1)}, u32[]{:S(2)}, u32[]{:S(2)}) %collective-permute-start.13) | collective-permute-done | bytes 204832 | tf_op jit(solution)/shard_map/ppermute | solution.py:25
  13.7 9.9 %collective-permute-done.14 = bf16[320,320]{1,0:T(8,128)(2,1)S(1)} collective-permute-done((bf16[320,320]{1,0:T(8,128)(2,1)}, bf16[320,320]{1,0:T(8,128)(2,1)S(1)}, u32[]{:S(2)}, u32[]{:S(2)}) %collective-permute-start.14) | collective-permute-done | bytes 204832 | tf_op jit(solution)/shard_map/ppermute | solution.py:25
  23.6 1.2 %pad_maximum_fusion.refs_4_ = bf16[4,320,320]{2,1,0:T(8,128)(2,1)S(1)} fusion(bf16[1,320,320]{2,1,0:T(8,128)(2,1)S(1)} %bitcast.41, bf16[1,320,320]{2,1,0:T(8,128)(2,1)S(1)} %bitcast.40, bf16[1,320,320]{2,1,0:T(8,128)(2,1)S(1)} %bitcast.39, bf16[1,320,320]{2,1,0:T(8,128)(2,1)} %bitcast.38), kind=kLoop, calls=%fused_computation | loop fusion | flops 1228800 | bytes 1638400 | tf_op jit(solution)/shard_map/stack | solution.py:205
  24.8 1.6 %collective-permute-start.17 = (bf16[2,320,320]{2,1,0:T(8,128)(2,1)S(1)}, bf16[2,320,320]{2,1,0:T(8,128)(2,1)S(1)}, u32[]{:S(2)}, u32[]{:S(2)}) collective-permute-start(bf16[2,320,320]{2,1,0:T(8,128)(2,1)S(1)} %constant_dynamic-slice_fusion), channel_id=1, source_target_pairs={{0,8},{4,12},{8,0},{12,4},{1,9},{5,13},{9,1},{13,5},{2,10},{6,14},... | collective-permute-start | bytes 1228808 | tf_op jit(solution)/shard_map/ppermute | solution.py:25
  27.1 1.6 %collective-permute-start.6 = (bf16[320,320]{1,0:T(8,128)(2,1)S(1)}, bf16[320,320]{1,0:T(8,128)(2,1)}, u32[]{:S(2)}, u32[]{:S(2)}) collective-permute-start(bf16[320,320]{1,0:T(8,128)(2,1)S(1)} %slice_bitcast_fusion), channel_id=1, source_target_pairs={{0,8},{4,12},{8,0},{12,4},{1,9},{5,13},{9,1},{13,5},{2,10},{6,14},... | collective-permute-start | bytes 614408 | tf_op jit(solution)/shard_map/ppermute | solution.py:25
  28.6 14.7 %collective-permute-done.4.refs_2_ = bf16[320,320]{1,0:T(8,128)(2,1)S(1)} collective-permute-done((bf16[320,320]{1,0:T(8,128)(2,1)S(1)}, bf16[320,320]{1,0:T(8,128)(2,1)S(1)}, u32[]{:S(2)}, u32[]{:S(2)}) %collective-permute-start.4) | collective-permute-done | bytes 204832 | tf_op jit(solution)/shard_map/ppermute | solution.py:25
  43.3 1.5 %collective-permute-start.5 = (bf16[320,320]{1,0:T(8,128)(2,1)S(1)}, bf16[320,320]{1,0:T(8,128)(2,1)}, u32[]{:S(2)}, u32[]{:S(2)}) collective-permute-start(bf16[320,320]{1,0:T(8,128)(2,1)S(1)} %collective-permute-done.4.refs_2_), channel_id=1, source_target_pairs={{0,16},{16,0},{1,17},{17,1},{2,18},{18,2},{3,19},{19,3},{4,20},{20... | collective-permute-start | bytes 614408 | tf_op jit(solution)/shard_map/ppermute | solution.py:25
  45.3 1.5 %collective-permute-start.1 = (s32[1,192]{1,0:T(1,128)S(1)}, s32[1,192]{1,0:T(1,128)S(1)}, u32[]{:S(2)}, u32[]{:S(2)}) collective-permute-start(s32[1,192]{1,0:T(1,128)S(1)} %bitcast.35), channel_id=1, source_target_pairs={{0,8},{4,12},{8,0},{12,4},{1,9},{5,13},{9,1},{13,5},{2,10},{6,14},... | collective-permute-start | bytes 2312 | tf_op jit(solution)/shard_map/ppermute | solution.py:25
  46.9 2.0 %collective-permute-done.1.refs_2_ = s32[1,192]{1,0:T(1,128)S(1)} collective-permute-done((s32[1,192]{1,0:T(1,128)S(1)}, s32[1,192]{1,0:T(1,128)S(1)}, u32[]{:S(2)}, u32[]{:S(2)}) %collective-permute-start.1) | collective-permute-done | bytes 800 | tf_op jit(solution)/shard_map/ppermute | solution.py:25
  48.9 1.1 %collective-permute-done.refs_1_ = s32[1,192]{1,0:T(1,128)S(1)} collective-permute-done((s32[1,192]{1,0:T(1,128)S(1)}, s32[1,192]{1,0:T(1,128)S(1)}, u32[]{:S(2)}, u32[]{:S(2)}) %collective-permute-start) | collective-permute-done | bytes 800 | tf_op jit(solution)/shard_map/ppermute | solution.py:25
  51.9 2.6 %collective-permute-done.7.refs_5_ = bf16[320,320]{1,0:T(8,128)(2,1)S(1)} collective-permute-done((bf16[320,320]{1,0:T(8,128)(2,1)S(1)}, bf16[320,320]{1,0:T(8,128)(2,1)S(1)}, u32[]{:S(2)}, u32[]{:S(2)}) %collective-permute-start.7) | collective-permute-done | bytes 204832 | tf_op jit(solution)/shard_map/ppermute | solution.py:25
  56.0 1.5 %copy-done.1 = bf16[768,1280]{1,0:T(8,128)(2,1)S(1)} copy-done((bf16[768,1280]{1,0:T(8,128)(2,1)S(1)}, bf16[768,1280]{1,0:T(8,128)(2,1)}, u32[]{:S(2)}) %copy-start.1) | copy-done | bytes 1966104
  57.5 1.7 %norm.1 = (bf16[768,1280]{1,0:T(8,128)(2,1)S(1)}, bf16[192,1280]{1,0:T(8,128)(2,1)S(1)}, bf16[4,192,192]{2,1,0:T(8,128)(2,1)S(1)}) custom-call(s32[3]{0:T(128)S(1)} %pad_add_fusion.index_ref, s32[1,192]{1,0:T(1,128)S(1)} %bitcast.37, s32[1,192]{1,0:T(1,128)S(1)} %collective-permute-done.refs_1_, s32[1,192]{1,0:T(1,128)S(1)} %collective-permute-done.1.refs_2_, ...), custom_call_target="tpu_custom_call" | custom-call | tf_op jit(solution)/shard_map/norm/pallas_call | solution.py:213
  59.2 5.1 %attention0.1 = (bf16[4,96,320]{2,1,0:T(8,128)(2,1)S(1)}, bf16[3,1280,320]{2,1,0:T(8,128)(2,1)S(1)}) custom-call(s32[3]{0:T(128)S(1)} %pad_add_fusion.index_ref, bf16[768,1280]{1,0:T(8,128)(2,1)S(1)} %get-tuple-element.11.hidden_ref, s32[6,128]{1,0:T(8,128)S(1)} %bitcast.33, bf16[3,320,320]{2,1,0:T(8,128)(2,1)S(1)} %bitcast.32, ...), custom_call_target="tpu_custom_call" | custom-call | tf_op jit(solution)/shard_map/attention0/pallas_call | solution.py:237
  64.4 3.4 %attention1.1 = bf16[4,96,320]{2,1,0:T(8,128)(2,1)S(1)} custom-call(bf16[768,1280]{1,0:T(8,128)(2,1)S(1)} %get-tuple-element.11.hidden_ref, s32[6,128]{1,0:T(8,128)S(1)} %bitcast.34, bf16[3,1280,320]{2,1,0:T(8,128)(2,1)S(1)} %get-tuple-element.14.w_ref), custom_call_target="tpu_custom_call" | custom-call | tf_op jit(solution)/shard_map/attention1/pallas_call | solution.py:247
  67.8 6.9 %collective-permute-start.21 = (bf16[96,320]{1,0:T(8,128)(2,1)S(1)}, bf16[96,320]{1,0:T(8,128)(2,1)S(1)}, u32[]{:S(2)}, u32[]{:S(2)}) collective-permute-start(bf16[96,320]{1,0:T(8,128)(2,1)S(1)} %get-tuple-element.17), channel_id=1, source_target_pairs={{0,1},{1,0},{2,3},{3,2},{4,5},{5,4},{6,7},{7,6},{8,9},{9,8},{10,11... | collective-permute-start | bytes 184328 | tf_op jit(solution)/shard_map/ppermute | solution.py:25
  75.7 1.9 %collective-permute-done.21.refs_1_ = bf16[96,320]{1,0:T(8,128)(2,1)S(1)} collective-permute-done((bf16[96,320]{1,0:T(8,128)(2,1)S(1)}, bf16[96,320]{1,0:T(8,128)(2,1)S(1)}, u32[]{:S(2)}, u32[]{:S(2)}) %collective-permute-start.21) | collective-permute-done | bytes 61472 | tf_op jit(solution)/shard_map/ppermute | solution.py:25
  77.6 2.4 %collective-permute-start.23 = (bf16[96,320]{1,0:T(8,128)(2,1)S(1)}, bf16[96,320]{1,0:T(8,128)(2,1)S(1)}, u32[]{:S(2)}, u32[]{:S(2)}) collective-permute-start(bf16[96,320]{1,0:T(8,128)(2,1)S(1)} %get-tuple-element.15), channel_id=1, source_target_pairs={{0,3},{1,2},{2,1},{3,0},{4,7},{5,6},{6,5},{7,4},{8,11},{9,10},{10,... | collective-permute-start | bytes 184328 | tf_op jit(solution)/shard_map/ppermute | solution.py:25
  80.1 1.5 %collective-permute-done.22.refs_2_ = bf16[96,320]{1,0:T(8,128)(2,1)S(1)} collective-permute-done((bf16[96,320]{1,0:T(8,128)(2,1)S(1)}, bf16[96,320]{1,0:T(8,128)(2,1)S(1)}, u32[]{:S(2)}, u32[]{:S(2)}) %collective-permute-start.22) | collective-permute-done | bytes 61472 | tf_op jit(solution)/shard_map/ppermute | solution.py:25
  82.0 1.8 %collective-permute-done.23.refs_3_ = bf16[96,320]{1,0:T(8,128)(2,1)S(1)} collective-permute-done((bf16[96,320]{1,0:T(8,128)(2,1)S(1)}, bf16[96,320]{1,0:T(8,128)(2,1)S(1)}, u32[]{:S(2)}, u32[]{:S(2)}) %collective-permute-start.23) | collective-permute-done | bytes 61472 | tf_op jit(solution)/shard_map/ppermute | solution.py:25
  83.9 2.4 %collective-permute-start.11 = (bf16[96,320]{1,0:T(8,128)(2,1)S(1)}, bf16[96,320]{1,0:T(8,128)(2,1)S(1)}, u32[]{:S(2)}, u32[]{:S(2)}) collective-permute-start(bf16[96,320]{1,0:T(8,128)(2,1)S(1)} %get-tuple-element.20), channel_id=1, source_target_pairs={{0,2},{1,3},{2,0},{3,1},{4,6},{5,7},{6,4},{7,5},{8,10},{9,11},{10,... | collective-permute-start | bytes 184328 | tf_op jit(solution)/shard_map/ppermute | solution.py:25
  86.2 1.4 %collective-permute-start.12 = (bf16[96,320]{1,0:T(8,128)(2,1)S(1)}, bf16[96,320]{1,0:T(8,128)(2,1)S(1)}, u32[]{:S(2)}, u32[]{:S(2)}) collective-permute-start(bf16[96,320]{1,0:T(8,128)(2,1)S(1)} %get-tuple-element.19), channel_id=1, source_target_pairs={{0,3},{1,2},{2,1},{3,0},{4,7},{5,6},{6,5},{7,4},{8,11},{9,10},{10,... | collective-permute-start | bytes 184328 | tf_op jit(solution)/shard_map/ppermute | solution.py:25
  87.7 2.5 %project1.1.refs_1_ = bf16[96,1280]{1,0:T(8,128)(2,1)S(1)} custom-call(s32[3]{0:T(128)S(1)} %pad_add_fusion.index_ref, bf16[96,320]{1,0:T(8,128)(2,1)S(1)} %get-tuple-element.18.refs_0_, bf16[96,320]{1,0:T(8,128)(2,1)S(1)} %collective-permute-done.21.refs_1_, bf16[96,320]{1,0:T(8,128)(2,1)S(1)} %collective-permute-done.22.refs_2_, ...), custom_call_target="tpu_custom_call" | custom-call | tf_op jit(solution)/shard_map/project1/pallas_call | solution.py:260
  90.2 1.6 %collective-permute-start.27 = (bf16[96,1280]{1,0:T(8,128)(2,1)S(1)}, bf16[96,1280]{1,0:T(8,128)(2,1)S(1)}, u32[]{:S(2)}, u32[]{:S(2)}) collective-permute-start(bf16[96,1280]{1,0:T(8,128)(2,1)S(1)} %project1.1.refs_1_), channel_id=1, source_target_pairs={{0,8},{4,12},{8,0},{12,4},{1,9},{5,13},{9,1},{13,5},{2,10},{6,14},... | collective-permute-start | bytes 737288 | tf_op jit(solution)/shard_map/ppermute | solution.py:25
  92.5 2.5 %project0.1.refs_0_ = bf16[96,1280]{1,0:T(8,128)(2,1)S(1)} custom-call(s32[3]{0:T(128)S(1)} %pad_add_fusion.index_ref, bf16[96,320]{1,0:T(8,128)(2,1)S(1)} %get-tuple-element.22.refs_0_, bf16[96,320]{1,0:T(8,128)(2,1)S(1)} %collective-permute-done.10.refs_1_, bf16[96,320]{1,0:T(8,128)(2,1)S(1)} %collective-permute-done.11.refs_2_, ...), custom_call_target="tpu_custom_call" | custom-call | tf_op jit(solution)/shard_map/project0/pallas_call | solution.py:260
  95.0 1.6 %collective-permute-start.26 = (bf16[96,1280]{1,0:T(8,128)(2,1)S(1)}, bf16[96,1280]{1,0:T(8,128)(2,1)S(1)}, u32[]{:S(2)}, u32[]{:S(2)}) collective-permute-start(bf16[96,1280]{1,0:T(8,128)(2,1)S(1)} %project0.1.refs_0_), channel_id=1, source_target_pairs={{0,8},{4,12},{8,0},{12,4},{1,9},{5,13},{9,1},{13,5},{2,10},{6,14},... | collective-permute-start | bytes 737288 | tf_op jit(solution)/shard_map/ppermute | solution.py:25
  97.1 1.2 %collective-permute-done.27.refs_5_ = bf16[96,1280]{1,0:T(8,128)(2,1)S(1)} collective-permute-done((bf16[96,1280]{1,0:T(8,128)(2,1)S(1)}, bf16[96,1280]{1,0:T(8,128)(2,1)S(1)}, u32[]{:S(2)}, u32[]{:S(2)}) %collective-permute-start.27) | collective-permute-done | bytes 245792 | tf_op jit(solution)/shard_map/ppermute | solution.py:25
  98.3 4.1 %collective-permute-done.26.refs_4_ = bf16[96,1280]{1,0:T(8,128)(2,1)S(1)} collective-permute-done((bf16[96,1280]{1,0:T(8,128)(2,1)S(1)}, bf16[96,1280]{1,0:T(8,128)(2,1)S(1)}, u32[]{:S(2)}, u32[]{:S(2)}) %collective-permute-start.26) | collective-permute-done | bytes 245792 | tf_op jit(solution)/shard_map/ppermute | solution.py:25
  102.4 1.5 %collective-permute-done.28.refs_6_ = bf16[96,1280]{1,0:T(8,128)(2,1)S(1)} collective-permute-done((bf16[96,1280]{1,0:T(8,128)(2,1)S(1)}, bf16[96,1280]{1,0:T(8,128)(2,1)S(1)}, u32[]{:S(2)}, u32[]{:S(2)}) %collective-permute-start.28) | collective-permute-done | bytes 245792 | tf_op jit(solution)/shard_map/ppermute | solution.py:25
  103.9 2.0 %placement.1 = bf16[192,1280]{1,0:T(8,128)(2,1)} custom-call(bf16[4,192,192]{2,1,0:T(8,128)(2,1)S(1)} %get-tuple-element.10.chosen_ref, bf16[96,1280]{1,0:T(8,128)(2,1)S(1)} %project0.1.refs_0_, bf16[96,1280]{1,0:T(8,128)(2,1)S(1)} %project1.1.refs_1_, bf16[96,1280]{1,0:T(8,128)(2,1)S(1)} %collective-permute-done.24.refs_2_, ...), custom_call_target="tpu_custom_call" | custom-call | tf_op jit(solution)/shard_map/placement/pallas_call | solution.py:270
  (59 shorter events, 7.4 us)
Async XLA Ops:
  0.0 13.7 %collective-permute-start.13 = (bf16[320,320]{1,0:T(8,128)(2,1)}, bf16[320,320]{1,0:T(8,128)(2,1)S(1)}, u32[]{:S(2)}, u32[]{:S(2)}) collective-permute-start(bf16[320,320]{1,0:T(8,128)(2,1)} %param.12), channel_id=1, source_target_pairs={{0,1},{1,0},{2,3},{3,2},{4,5},{5,4},{6,7},{7,6},{8,9},{9,8},{10,11... | collective-permute-start | bytes 614408 | tf_op jit(solution)/shard_map/ppermute | solution.py:25
  3.0 20.5 %collective-permute-start.14 = (bf16[320,320]{1,0:T(8,128)(2,1)}, bf16[320,320]{1,0:T(8,128)(2,1)S(1)}, u32[]{:S(2)}, u32[]{:S(2)}) collective-permute-start(bf16[320,320]{1,0:T(8,128)(2,1)} %param.12), channel_id=1, source_target_pairs={{0,2},{1,3},{2,0},{3,1},{4,6},{5,7},{6,4},{7,5},{8,10},{9,11},{10,... | collective-permute-start | bytes 614408 | tf_op jit(solution)/shard_map/ppermute | solution.py:25
  5.6 17.9 %collective-permute-start.15 = (bf16[320,320]{1,0:T(8,128)(2,1)}, bf16[320,320]{1,0:T(8,128)(2,1)S(1)}, u32[]{:S(2)}, u32[]{:S(2)}) collective-permute-start(bf16[320,320]{1,0:T(8,128)(2,1)} %param.12), channel_id=1, source_target_pairs={{0,3},{1,2},{2,1},{3,0},{4,7},{5,6},{6,5},{7,4},{8,11},{9,10},{10,... | collective-permute-start | bytes 614408 | tf_op jit(solution)/shard_map/ppermute | solution.py:25
  23.6 32.4 %copy-start.6 = (f32[1280]{0:T(1024)S(1)}, f32[1280]{0:T(1024)}, u32[]{:S(2)}) copy-start(f32[1280]{0:T(1024)} %param.10) | copy-start | bytes 15364
  24.8 34.5 %copy-start.4 = (s32[768]{0:T(1024)S(1)}, s32[768]{0:T(1024)}, u32[]{:S(2)}) copy-start(s32[768]{0:T(1024)} %param.8) | copy-start | bytes 9220
  24.8 20.0 %collective-permute-start.17 = (bf16[2,320,320]{2,1,0:T(8,128)(2,1)S(1)}, bf16[2,320,320]{2,1,0:T(8,128)(2,1)S(1)}, u32[]{:S(2)}, u32[]{:S(2)}) collective-permute-start(bf16[2,320,320]{2,1,0:T(8,128)(2,1)S(1)} %constant_dynamic-slice_fusion), channel_id=1, source_target_pairs={{0,8},{4,12},{8,0},{12,4},{1,9},{5,13},{9,1},{13,5},{2,10},{6,14},... | collective-permute-start | bytes 1228808 | tf_op jit(solution)/shard_map/ppermute | solution.py:25
  26.5 16.9 %collective-permute-start.4 = (bf16[320,320]{1,0:T(8,128)(2,1)S(1)}, bf16[320,320]{1,0:T(8,128)(2,1)S(1)}, u32[]{:S(2)}, u32[]{:S(2)}) collective-permute-start(bf16[320,320]{1,0:T(8,128)(2,1)S(1)} %dynamic-slice_bitcast_fusion), channel_id=1, source_target_pairs={{0,8},{4,12},{8,0},{12,4},{1,9},{5,13},{9,1},{13,5},{2,10},{6,14},... | collective-permute-start | bytes 614408 | tf_op jit(solution)/shard_map/ppermute | solution.py:25
  27.1 24.3 %collective-permute-start.6 = (bf16[320,320]{1,0:T(8,128)(2,1)S(1)}, bf16[320,320]{1,0:T(8,128)(2,1)}, u32[]{:S(2)}, u32[]{:S(2)}) collective-permute-start(bf16[320,320]{1,0:T(8,128)(2,1)S(1)} %slice_bitcast_fusion), channel_id=1, source_target_pairs={{0,8},{4,12},{8,0},{12,4},{1,9},{5,13},{9,1},{13,5},{2,10},{6,14},... | collective-permute-start | bytes 614408 | tf_op jit(solution)/shard_map/ppermute | solution.py:25
  28.6 30.6 %collective-permute-start.3 = (bf16[3,320,320]{2,1,0:T(8,128)(2,1)S(1)}, bf16[3,320,320]{2,1,0:T(8,128)(2,1)}, u32[]{:S(2)}, u32[]{:S(2)}) collective-permute-start(bf16[3,320,320]{2,1,0:T(8,128)(2,1)S(1)} %bitcast.31), channel_id=1, source_target_pairs={{0,4},{4,0},{8,12},{12,8},{1,5},{5,1},{9,13},{13,9},{2,6},{6,2},{1... | collective-permute-start | bytes 1843208 | tf_op jit(solution)/shard_map/ppermute | solution.py:25
  43.3 8.4 %collective-permute-start.5 = (bf16[320,320]{1,0:T(8,128)(2,1)S(1)}, bf16[320,320]{1,0:T(8,128)(2,1)}, u32[]{:S(2)}, u32[]{:S(2)}) collective-permute-start(bf16[320,320]{1,0:T(8,128)(2,1)S(1)} %collective-permute-done.4.refs_2_), channel_id=1, source_target_pairs={{0,16},{16,0},{1,17},{17,1},{2,18},{18,2},{3,19},{19,3},{4,20},{20... | collective-permute-start | bytes 614408 | tf_op jit(solution)/shard_map/ppermute | solution.py:25
  44.8 10.9 %collective-permute-start.18 = (bf16[2,320,320]{2,1,0:T(8,128)(2,1)S(1)}, bf16[2,320,320]{2,1,0:T(8,128)(2,1)}, u32[]{:S(2)}, u32[]{:S(2)}) collective-permute-start(bf16[2,320,320]{2,1,0:T(8,128)(2,1)S(1)} %collective-permute-done.17.refs_6_), channel_id=1, source_target_pairs={{0,16},{16,0},{1,17},{17,1},{2,18},{18,2},{3,19},{19,3},{4,20},{20... | collective-permute-start | bytes 1228808 | tf_op jit(solution)/shard_map/ppermute | solution.py:25
  45.3 3.6 %collective-permute-start.1 = (s32[1,192]{1,0:T(1,128)S(1)}, s32[1,192]{1,0:T(1,128)S(1)}, u32[]{:S(2)}, u32[]{:S(2)}) collective-permute-start(s32[1,192]{1,0:T(1,128)S(1)} %bitcast.35), channel_id=1, source_target_pairs={{0,8},{4,12},{8,0},{12,4},{1,9},{5,13},{9,1},{13,5},{2,10},{6,14},... | collective-permute-start | bytes 2312 | tf_op jit(solution)/shard_map/ppermute | solution.py:25
  48.9 1.1 %collective-permute-start = (s32[1,192]{1,0:T(1,128)S(1)}, s32[1,192]{1,0:T(1,128)S(1)}, u32[]{:S(2)}, u32[]{:S(2)}) collective-permute-start(s32[1,192]{1,0:T(1,128)S(1)} %bitcast.36), channel_id=1, source_target_pairs={{0,4},{4,0},{8,12},{12,8},{1,5},{5,1},{9,13},{13,9},{2,6},{6,2},{1... | collective-permute-start | bytes 2312 | tf_op jit(solution)/shard_map/ppermute | solution.py:25
  50.1 1.1 %collective-permute-start.2 = (s32[1,192]{1,0:T(1,128)S(1)}, s32[1,192]{1,0:T(1,128)S(1)}, u32[]{:S(2)}, u32[]{:S(2)}) collective-permute-start(s32[1,192]{1,0:T(1,128)S(1)} %collective-permute-done.1.refs_2_), channel_id=1, source_target_pairs={{0,4},{4,0},{8,12},{12,8},{1,5},{5,1},{9,13},{13,9},{2,6},{6,2},{1... | collective-permute-start | bytes 2312 | tf_op jit(solution)/shard_map/ppermute | solution.py:25
  51.2 36.5 %collective-permute-start.16 = (bf16[4,320,320]{2,1,0:T(8,128)(2,1)S(1)}, bf16[4,320,320]{2,1,0:T(8,128)(2,1)S(1)}, u32[]{:S(2)}, u32[]{:S(2)}) collective-permute-start(bf16[4,320,320]{2,1,0:T(8,128)(2,1)S(1)} %pad_maximum_fusion.refs_4_), channel_id=1, source_target_pairs={{0,4},{4,0},{8,12},{12,8},{1,5},{5,1},{9,13},{13,9},{2,6},{6,2},{1... | collective-permute-start | bytes 2457608 | tf_op jit(solution)/shard_map/ppermute | solution.py:25
  51.4 3.1 %collective-permute-start.7 = (bf16[320,320]{1,0:T(8,128)(2,1)S(1)}, bf16[320,320]{1,0:T(8,128)(2,1)S(1)}, u32[]{:S(2)}, u32[]{:S(2)}) collective-permute-start(bf16[320,320]{1,0:T(8,128)(2,1)S(1)} %collective-permute-done.4.refs_2_), channel_id=1, source_target_pairs={{0,4},{4,0},{8,12},{12,8},{1,5},{5,1},{9,13},{13,9},{2,6},{6,2},{1... | collective-permute-start | bytes 614408 | tf_op jit(solution)/shard_map/ppermute | solution.py:25
  51.7 3.6 %collective-permute-start.9 = (bf16[320,320]{1,0:T(8,128)(2,1)}, bf16[320,320]{1,0:T(8,128)(2,1)}, u32[]{:S(2)}, u32[]{:S(2)}) collective-permute-start(bf16[320,320]{1,0:T(8,128)(2,1)} %collective-permute-done.6.refs_4_), channel_id=1, source_target_pairs={{0,4},{4,0},{8,12},{12,8},{1,5},{5,1},{9,13},{13,9},{2,6},{6,2},{1... | collective-permute-start | bytes 614408 | tf_op jit(solution)/shard_map/ppermute | solution.py:25
  55.2 4.0 %collective-permute-start.8 = (bf16[320,320]{1,0:T(8,128)(2,1)}, bf16[320,320]{1,0:T(8,128)(2,1)}, u32[]{:S(2)}, u32[]{:S(2)}) collective-permute-start(bf16[320,320]{1,0:T(8,128)(2,1)} %collective-permute-done.5.refs_3_), channel_id=1, source_target_pairs={{0,4},{4,0},{8,12},{12,8},{1,5},{5,1},{9,13},{13,9},{2,6},{6,2},{1... | collective-permute-start | bytes 614408 | tf_op jit(solution)/shard_map/ppermute | solution.py:25
  55.3 30.9 %collective-permute-start.19 = (bf16[2,320,320]{2,1,0:T(8,128)(2,1)S(1)}, bf16[2,320,320]{2,1,0:T(8,128)(2,1)}, u32[]{:S(2)}, u32[]{:S(2)}) collective-permute-start(bf16[2,320,320]{2,1,0:T(8,128)(2,1)S(1)} %collective-permute-done.17.refs_6_), channel_id=1, source_target_pairs={{0,4},{4,0},{8,12},{12,8},{1,5},{5,1},{9,13},{13,9},{2,6},{6,2},{1... | collective-permute-start | bytes 1228808 | tf_op jit(solution)/shard_map/ppermute | solution.py:25
  55.7 32.0 %collective-permute-start.20 = (bf16[2,320,320]{2,1,0:T(8,128)(2,1)}, bf16[2,320,320]{2,1,0:T(8,128)(2,1)}, u32[]{:S(2)}, u32[]{:S(2)}) collective-permute-start(bf16[2,320,320]{2,1,0:T(8,128)(2,1)} %collective-permute-done.18.refs_7_), channel_id=1, source_target_pairs={{0,4},{4,0},{8,12},{12,8},{1,5},{5,1},{9,13},{13,9},{2,6},{6,2},{1... | collective-permute-start | bytes 1228808 | tf_op jit(solution)/shard_map/ppermute | solution.py:25
  67.8 9.8 %collective-permute-start.21 = (bf16[96,320]{1,0:T(8,128)(2,1)S(1)}, bf16[96,320]{1,0:T(8,128)(2,1)S(1)}, u32[]{:S(2)}, u32[]{:S(2)}) collective-permute-start(bf16[96,320]{1,0:T(8,128)(2,1)S(1)} %get-tuple-element.17), channel_id=1, source_target_pairs={{0,1},{1,0},{2,3},{3,2},{4,5},{5,4},{6,7},{7,6},{8,9},{9,8},{10,11... | collective-permute-start | bytes 184328 | tf_op jit(solution)/shard_map/ppermute | solution.py:25
  74.7 6.9 %collective-permute-start.22 = (bf16[96,320]{1,0:T(8,128)(2,1)S(1)}, bf16[96,320]{1,0:T(8,128)(2,1)S(1)}, u32[]{:S(2)}, u32[]{:S(2)}) collective-permute-start(bf16[96,320]{1,0:T(8,128)(2,1)S(1)} %get-tuple-element.16), channel_id=1, source_target_pairs={{0,2},{1,3},{2,0},{3,1},{4,6},{5,7},{6,4},{7,5},{8,10},{9,11},{10,... | collective-permute-start | bytes 184328 | tf_op jit(solution)/shard_map/ppermute | solution.py:25
  77.6 6.2 %collective-permute-start.23 = (bf16[96,320]{1,0:T(8,128)(2,1)S(1)}, bf16[96,320]{1,0:T(8,128)(2,1)S(1)}, u32[]{:S(2)}, u32[]{:S(2)}) collective-permute-start(bf16[96,320]{1,0:T(8,128)(2,1)S(1)} %get-tuple-element.15), channel_id=1, source_target_pairs={{0,3},{1,2},{2,1},{3,0},{4,7},{5,6},{6,5},{7,4},{8,11},{9,10},{10,... | collective-permute-start | bytes 184328 | tf_op jit(solution)/shard_map/ppermute | solution.py:25
  81.6 10.1 %collective-permute-start.10 = (bf16[96,320]{1,0:T(8,128)(2,1)S(1)}, bf16[96,320]{1,0:T(8,128)(2,1)S(1)}, u32[]{:S(2)}, u32[]{:S(2)}) collective-permute-start(bf16[96,320]{1,0:T(8,128)(2,1)S(1)} %get-tuple-element.21), channel_id=1, source_target_pairs={{0,1},{1,0},{2,3},{3,2},{4,5},{5,4},{6,7},{7,6},{8,9},{9,8},{10,11... | collective-permute-start | bytes 184328 | tf_op jit(solution)/shard_map/ppermute | solution.py:25
  83.9 7.9 %collective-permute-start.11 = (bf16[96,320]{1,0:T(8,128)(2,1)S(1)}, bf16[96,320]{1,0:T(8,128)(2,1)S(1)}, u32[]{:S(2)}, u32[]{:S(2)}) collective-permute-start(bf16[96,320]{1,0:T(8,128)(2,1)S(1)} %get-tuple-element.20), channel_id=1, source_target_pairs={{0,2},{1,3},{2,0},{3,1},{4,6},{5,7},{6,4},{7,5},{8,10},{9,11},{10,... | collective-permute-start | bytes 184328 | tf_op jit(solution)/shard_map/ppermute | solution.py:25
  86.2 6.3 %collective-permute-start.12 = (bf16[96,320]{1,0:T(8,128)(2,1)S(1)}, bf16[96,320]{1,0:T(8,128)(2,1)S(1)}, u32[]{:S(2)}, u32[]{:S(2)}) collective-permute-start(bf16[96,320]{1,0:T(8,128)(2,1)S(1)} %get-tuple-element.19), channel_id=1, source_target_pairs={{0,3},{1,2},{2,1},{3,0},{4,7},{5,6},{6,5},{7,4},{8,11},{9,10},{10,... | collective-permute-start | bytes 184328 | tf_op jit(solution)/shard_map/ppermute | solution.py:25
  90.2 8.1 %collective-permute-start.27 = (bf16[96,1280]{1,0:T(8,128)(2,1)S(1)}, bf16[96,1280]{1,0:T(8,128)(2,1)S(1)}, u32[]{:S(2)}, u32[]{:S(2)}) collective-permute-start(bf16[96,1280]{1,0:T(8,128)(2,1)S(1)} %project1.1.refs_1_), channel_id=1, source_target_pairs={{0,8},{4,12},{8,0},{12,4},{1,9},{5,13},{9,1},{13,5},{2,10},{6,14},... | collective-permute-start | bytes 737288 | tf_op jit(solution)/shard_map/ppermute | solution.py:25
  95.0 7.4 %collective-permute-start.26 = (bf16[96,1280]{1,0:T(8,128)(2,1)S(1)}, bf16[96,1280]{1,0:T(8,128)(2,1)S(1)}, u32[]{:S(2)}, u32[]{:S(2)}) collective-permute-start(bf16[96,1280]{1,0:T(8,128)(2,1)S(1)} %project0.1.refs_0_), channel_id=1, source_target_pairs={{0,8},{4,12},{8,0},{12,4},{1,9},{5,13},{9,1},{13,5},{2,10},{6,14},... | collective-permute-start | bytes 737288 | tf_op jit(solution)/shard_map/ppermute | solution.py:25
  96.6 5.8 %collective-permute-start.25 = (bf16[96,1280]{1,0:T(8,128)(2,1)S(1)}, bf16[96,1280]{1,0:T(8,128)(2,1)S(1)}, u32[]{:S(2)}, u32[]{:S(2)}) collective-permute-start(bf16[96,1280]{1,0:T(8,128)(2,1)S(1)} %project1.1.refs_1_), channel_id=1, source_target_pairs={{0,4},{4,0},{8,12},{12,8},{1,5},{5,1},{9,13},{13,9},{2,6},{6,2},{1... | collective-permute-start | bytes 737288 | tf_op jit(solution)/shard_map/ppermute | solution.py:25
  96.6 5.8 %collective-permute-start.24 = (bf16[96,1280]{1,0:T(8,128)(2,1)S(1)}, bf16[96,1280]{1,0:T(8,128)(2,1)S(1)}, u32[]{:S(2)}, u32[]{:S(2)}) collective-permute-start(bf16[96,1280]{1,0:T(8,128)(2,1)S(1)} %project0.1.refs_0_), channel_id=1, source_target_pairs={{0,4},{4,0},{8,12},{12,8},{1,5},{5,1},{9,13},{13,9},{2,6},{6,2},{1... | collective-permute-start | bytes 737288 | tf_op jit(solution)/shard_map/ppermute | solution.py:25
  98.3 4.1 %collective-permute-start.29 = (bf16[96,1280]{1,0:T(8,128)(2,1)S(1)}, bf16[96,1280]{1,0:T(8,128)(2,1)S(1)}, u32[]{:S(2)}, u32[]{:S(2)}) collective-permute-start(bf16[96,1280]{1,0:T(8,128)(2,1)S(1)} %collective-permute-done.27.refs_5_), channel_id=1, source_target_pairs={{0,4},{4,0},{8,12},{12,8},{1,5},{5,1},{9,13},{13,9},{2,6},{6,2},{1... | collective-permute-start | bytes 737288 | tf_op jit(solution)/shard_map/ppermute | solution.py:25
  102.4 1.5 %collective-permute-start.28 = (bf16[96,1280]{1,0:T(8,128)(2,1)S(1)}, bf16[96,1280]{1,0:T(8,128)(2,1)S(1)}, u32[]{:S(2)}, u32[]{:S(2)}) collective-permute-start(bf16[96,1280]{1,0:T(8,128)(2,1)S(1)} %collective-permute-done.26.refs_4_), channel_id=1, source_target_pairs={{0,4},{4,0},{8,12},{12,8},{1,5},{5,1},{9,13},{13,9},{2,6},{6,2},{1... | collective-permute-start | bytes 737288 | tf_op jit(solution)/shard_map/ppermute | solution.py:25
  (6 other events, 75.5 us)

commit v3 on v2

--- a/solution.py
+++ b/solution.py
@@ -50,9 +50,7 @@
     return mask.astype(F32).astype(BF16)
 
 
-def norm_kernel(n_ctx, index_ref, *refs):
-    place_refs = refs[:n_ctx]
-    patches_ref, gain_ref, hidden_ref, own_ref, chosen_ref = refs[n_ctx:]
+def norm_kernel(index_ref, patches_ref, gain_ref, hidden_ref, own_ref):
     rows = patches_ref.shape[0]
     x = patches_ref[...]
     xf = x.astype(F32)
@@ -67,11 +65,6 @@
         own_ref[i * pick : (i + 1) * pick, :] = jnp.dot(
             chosen, x[i * step : (i + 1) * step], preferred_element_type=F32
         ).astype(BF16)
-    spots = chosen_ref.shape[1]
-    for key in range(n_ctx):
-        target = place_refs[key][...] - index_ref[0] * spots
-        grid = lax.broadcasted_iota(jnp.int32, (spots, target.shape[1]), 0)
-        chosen_ref[key] = one_hot(grid == target)
 
 
 def attend(row0, hidden_ref, valid_ref, w_ref, out_ref, q_ref, k_ref, v_ref, mix_ref):
@@ -139,50 +132,48 @@
 
 
 def project_kernel(n_ctx, row0, index_ref, *refs):
-    mixes = [m[...] for m in refs[:4]]
-    blocks = list(refs[4 : 4 + 2 + 2 * (n_ctx - 2)])
-    own_ref, gain_ref, out_ref, part_ref = refs[4 + len(blocks) :]
+    mixed = jnp.concatenate([m[...] for m in refs[:4]], axis=1)
+    *blocks, own_ref, gain_ref, out_ref, part_ref = refs[4:]
     rows = out_ref.shape[0]
     me = index_ref[0]
-    flip = index_ref[2] > 0
-    low = jnp.concatenate(mixes[:2], axis=1)
-    high = jnp.concatenate(mixes[2:], axis=1)
-    first = jnp.where(flip, high, low)
-    second = jnp.where(flip, low, high)
-    col = blocks[0].shape[2]
-
-    def times(mix, ref, at):
-        w = ref[at : at + 2].reshape(mix.shape[1], col)
-        return jnp.dot(mix, w, preferred_element_type=F32)
-
     for key in range(n_ctx):
-        if key < 2:
-            block = blocks.pop(0)
-            part_ref[me ^ key] = times(low, block, 0) + times(high, block, 2)
-        else:
-            part_ref[me ^ key] = times(first, blocks.pop(0), 0) + times(second, blocks.pop(0), 0)
+        count = (4, 1)[key] if key < 2 else 2
+        pieces = []
+        for ref in [blocks.pop(0) for _ in range(count)]:
+            block = ref[...]
+            pieces.append(block.reshape(-1, block.shape[-1]))
+        part_ref[me ^ key] = jnp.dot(
+            mixed, jnp.concatenate(pieces, axis=0), preferred_element_type=F32
+        )
     total = jnp.concatenate([part_ref[i] for i in range(n_ctx)], axis=1)
     total = total + own_ref[row0 : row0 + rows, :].astype(F32)
     mean_sq = jnp.mean(total * total, axis=-1, keepdims=True)
     out_ref[...] = (total * lax.rsqrt(mean_sq + 1e-06) * gain_ref[...]).astype(BF16)
 
 
-def place_kernel(n_ctx, chosen_ref, *refs):
-    row_refs = refs[:-1]
+def place_kernel(n_ctx, index_ref, *refs):
+    place_refs = refs[:n_ctx]
+    row_refs = refs[n_ctx:-1]
     out_ref = refs[-1]
+    spots = out_ref.shape[0]
     chunks = len(row_refs) // n_ctx
     total = None
     for key in range(n_ctx):
+        target = place_refs[key][...] - index_ref[0] * spots
+        grid = lax.broadcasted_iota(jnp.int32, (spots, target.shape[1]), 0)
+        chosen = one_hot(grid == target)
         for r in range(chunks):
             block = row_refs[key * chunks + r]
             count = block.shape[0]
             part = jnp.dot(
-                chosen_ref[key, :, r * count : (r + 1) * count],
-                block[...],
-                preferred_element_type=F32,
+                chosen[:, r * count : (r + 1) * count], block[...], preferred_element_type=F32
             )
             total = part if total is None else total + part
     out_ref[...] = total.astype(BF16)
+
+
+def together(*values):
+    return lax.optimization_barrier(values)
 
 
 def local(n_dp, n_ctx, n_ten, patches, valid, place, gain_attn, w_qkv, w_proj, gain_merge):
@@ -192,89 +183,118 @@
     ten = lax.axis_index("tensor")
     half = lax.axis_index("dp") % 2
     index = jnp.stack([lax.axis_index("context"), ten, half]).astype(jnp.int32)
+    cross = list(cross_keys(n_ctx))
+
+    def over_dp(x):
+        return swap(x, "dp", n_dp, 1)
+
+    def over_core(x):
+        return swap(x, "context", n_ctx, 1)
 
     w3 = jnp.transpose(w_qkv, (1, 0, 2))
-    near = gather_cross(lax.dynamic_index_in_dim(w3, half, 0, keepdims=False), n_ctx)
-    last = gather_cross(w3[2], n_ctx)
-    shards = {0: [w3], 1: [swap(w3, "context", n_ctx, 1)]}
-    for key in cross_keys(n_ctx):
-        shards[key] = [near[key], swap(near[key], "dp", n_dp, 1), last[key]]
-        shards[key ^ 1] = [swap(x, "context", n_ctx, 1) for x in shards[key]]
-
-    pieces = [w_proj] + [swap(w_proj, "tensor", n_ten, s) for s in range(1, n_ten)]
-    proj = jnp.stack(pieces)
-    mine = gather_cross(lax.dynamic_slice_in_dim(proj, half * 2, 2, 0), n_ctx)
-    blocks = {0: [proj], 1: [swap(proj, "context", n_ctx, 1)]}
-    for key in cross_keys(n_ctx):
-        blocks[key] = [mine[key], swap(mine[key], "dp", n_dp, 1)]
-        blocks[key ^ 1] = [swap(x, "context", n_ctx, 1) for x in blocks[key]]
-
-    places = gather_xor(place.reshape(1, groups), n_ctx)
-    hidden, own_patches, chosen = pl.pallas_call(
-        functools.partial(norm_kernel, n_ctx),
+    first = gather_cross(lax.dynamic_index_in_dim(w3, half, 0, keepdims=False), n_ctx)
+    value = gather_cross(w3[2], n_ctx)
+    twin = over_core(w3)
+    by_one = swap(w_proj, "tensor", n_ten, 1)
+    by_two = swap(w_proj, "tensor", n_ten, 2)
+    hidden, own_patches = pl.pallas_call(
+        norm_kernel,
         out_shape=(
             jax.ShapeDtypeStruct((rows, feat), BF16),
             jax.ShapeDtypeStruct((groups, feat), BF16),
-            jax.ShapeDtypeStruct((n_ctx, groups, groups), BF16),
         ),
-        in_specs=[SMEM] + [VMEM] * (n_ctx + 2),
-        out_specs=(VMEM, VMEM, VMEM),
+        in_specs=[SMEM, VMEM, VMEM],
+        out_specs=(VMEM, VMEM),
         compiler_params=params(32),
         name="norm",
-    )(index, *[places[k] for k in range(n_ctx)], patches, gain_attn.reshape(1, feat))
+    )(index, patches, gain_attn.reshape(1, feat))
+    first, by_one, twin, hidden = together(first, by_one, twin, hidden)
+
+    second = {k: over_dp(first[k]) for k in cross}
+    first_twin = {k: over_core(first[k]) for k in cross}
+    low = gather_cross(jnp.stack([w_proj, by_one]), n_ctx)
+    second, value, first_twin, by_two, w_proj = together(second, value, first_twin, by_two, w_proj)
+
+    second_twin = {k: over_core(second[k]) for k in cross}
+    value_twin = {k: over_core(value[k]) for k in cross}
+    by_three = swap(w_proj, "tensor", n_ten, 3)
+    places = gather_cross(place.reshape(1, groups), n_ctx)
+
+    shard_list = [w3, twin]
+    for k in cross:
+        shard_list += [first[k], second[k], value[k], first_twin[k], second_twin[k], value_twin[k]]
 
     valid_pairs = valid.reshape(rows // PAIR, PAIR)
     part = rows // CHUNKS
     gain2 = gain_merge.reshape(1, feat)
     mix_shape = jax.ShapeDtypeStruct((n_ten, part // 4, width), BF16)
     scratch = [pltpu.VMEM((part, width), BF16)] * 4
-    shard_list = [x for k in range(n_ctx) for x in shards[k]]
-    block_list = [x for k in range(n_ctx) for x in blocks[k]]
-    w_full = None
+    mixed, w_full = pl.pallas_call(
+        functools.partial(first_attention_kernel, n_ctx),
+        out_shape=(mix_shape, jax.ShapeDtypeStruct((3, feat, width), BF16)),
+        in_specs=[SMEM] + [VMEM] * (2 + len(shard_list)),
+        out_specs=(VMEM, VMEM),
+        scratch_shapes=scratch,
+        compiler_params=params(32),
+        name="attention0",
+    )(index, hidden, valid_pairs, *shard_list)
+    def by_tensor(mixed):
+        return [lax.dynamic_index_in_dim(mixed, ten ^ s, 0, keepdims=False) for s in range(n_ten)]
+
+    def exchange(pieces):
+        return [pieces[0]] + [swap(pieces[s], "tensor", n_ten, s) for s in range(1, n_ten)]
+
+    pieces = by_tensor(mixed)
+    pieces, by_three, low, places, w_proj = together(pieces, by_three, low, places, w_proj)
+    received = [exchange(pieces)]
+    high = gather_cross(jnp.stack([by_two, by_three]), n_ctx)
+    own_twin = over_core(jnp.stack([w_proj, by_one, by_two, by_three]))
+    for r in range(1, CHUNKS):
+        received[r - 1][1], hidden = together(received[r - 1][1], hidden)
+        mixed = pl.pallas_call(
+            functools.partial(next_attention_kernel, r * part),
+            out_shape=mix_shape,
+            in_specs=[VMEM] * 3,
+            out_specs=VMEM,
+            scratch_shapes=scratch,
+            compiler_params=params(32),
+            name="attention" + str(r),
+        )(hidden, valid_pairs, w_full)
+        pieces, received[r - 1], own_twin, low = together(
+            by_tensor(mixed), received[r - 1], own_twin, low
+        )
+        received.append(exchange(pieces))
+    high, received[-1][1] = together(high, received[-1][1])
+
+    blocks = [w_proj, by_one, by_two, by_three, own_twin]
+    for k in cross:
+        blocks += [low[k], high[k], over_core(low[k]), over_core(high[k])]
     gathered = []
     for r in range(CHUNKS):
-        if r == 0:
-            mixed, w_full = pl.pallas_call(
-                functools.partial(first_attention_kernel, n_ctx),
-                out_shape=(mix_shape, jax.ShapeDtypeStruct((3, feat, width), BF16)),
-                in_specs=[SMEM] + [VMEM] * (2 + len(shard_list)),
-                out_specs=(VMEM, VMEM),
-                scratch_shapes=scratch,
-                compiler_params=params(32),
-                name="attention0",
-            )(index, hidden, valid_pairs, *shard_list)
-        else:
-            mixed = pl.pallas_call(
-                functools.partial(next_attention_kernel, r * part),
-                out_shape=mix_shape,
-                in_specs=[VMEM] * 3,
-                out_specs=VMEM,
-                scratch_shapes=scratch,
-                compiler_params=params(32),
-                name="attention" + str(r),
-            )(hidden, valid_pairs, w_full)
-        mixes = []
-        for s in range(n_ten):
-            piece = lax.dynamic_index_in_dim(mixed, ten ^ s, 0, keepdims=False)
-            mixes.append(piece if s == 0 else swap(piece, "tensor", n_ten, s))
+        if r > 0:
+            received[r], done = together(received[r], done)
         done = pl.pallas_call(
             functools.partial(project_kernel, n_ctx, r * (part // 4)),
             out_shape=jax.ShapeDtypeStruct((part // 4, feat), BF16),
-            in_specs=[SMEM] + [VMEM] * (n_ten + len(block_list) + 2),
+            in_specs=[SMEM] + [VMEM] * (n_ten + len(blocks) + 2),
             out_specs=VMEM,
             scratch_shapes=[pltpu.VMEM((n_ctx, part // 4, w_proj.shape[1]), F32)],
             compiler_params=params(32),
             name="project" + str(r),
-        )(index, *mixes, *block_list, own_patches, gain2)
+        )(index, *received[r], *blocks, own_patches, gain2)
         gathered.append(gather_xor(done, n_ctx))
+    place_twin = over_core(jnp.stack([places[k] for k in (0, *cross)]))
+    place_list = []
+    for i, k in enumerate((0, *cross)):
+        place_list += [places[k], place_twin[i]]
     return pl.pallas_call(
         functools.partial(place_kernel, n_ctx),
         out_shape=jax.ShapeDtypeStruct((groups, feat), BF16),
-        in_specs=[VMEM] * (1 + n_ctx * CHUNKS),
+        in_specs=[SMEM] + [VMEM] * (n_ctx + n_ctx * CHUNKS),
         out_specs=VMEM,
         compiler_params=params(32),
         name="placement",
-    )(chosen, *[gathered[r][k] for k in range(n_ctx) for r in range(CHUNKS)])
+    )(index, *place_list, *[gathered[r][k] for k in range(n_ctx) for r in range(CHUNKS)])
 
 
 def solution(mesh):

time: 106 us -> 76.5 us (0.72)
  waiting for transfers between devices: 52.1 us -> 19.7 us
  local copies, waits for them, and re-layouts: 2.45 us -> 9.4 us
  starting transfers between devices: 32.8 us -> 28.6 us
    ppermute x30 -> x29, waiting for transfers between devices: 52.1 us -> 19.7 us  [swap(): return lax.ppermute(x, axis, [(i, i ^ bit) for i in range(size)])]
    ppermute x30 -> x29, starting transfers between devices: 32.8 us -> 28.6 us  [swap(): return lax.ppermute(x, axis, [(i, i ^ bit) for i in range(size)])]
    unnamed x16 -> x20, local copies, waits for them, and re-layouts: 2.26 us -> 5.26 us
    squeeze x1, local copies, waits for them, and re-layouts: 0.03 us -> 1.69 us  [local(): lax.dynamic_index_in_dim(w3, half, 0, keepdims=False)]
    squeeze x3 -> x4, local copies, waits for them, and re-layouts: 0.1 us -> 1.74 us  [the longest x1 1.65 us: local(): value = gather_cross(w3[2], n_ctx)]
  transfers between devices with their start and end apart: 30 -> 29, of which waited for: 14 -> 11; matrix products, arithmetic and copies ran while one was open for 0% -> 7% of each run, Pallas kernels for 14% -> 19%
where the time goes in v3:
time: 76.5 us; the launch traced here: 76 us
  starting transfers between devices  28.6 us (37%)
  waiting for transfers between devices  19.7 us (26%)
  Pallas kernels  16.9 us (22%)
  local copies, waits for them, and re-layouts  9.4 us (12%)
  other arithmetic  1.28 us (2%)
    ppermute x29, starting transfers between devices, swap(): return lax.ppermute(x, axis, [(i, i ^ bit) for i in range(size)])  28.6 us
    ppermute x29, waiting for transfers between devices, swap(): return lax.ppermute(x, axis, [(i, i ^ bit) for i in range(size)])  19.7 us
    unnamed x20, local copies, waits for them, and re-layouts  5.26 us
    pallas_call x1, Pallas kernels, local(): pl.pallas_call(functools.partial(first_attention_kernel, n_ctx), out_shap...  5.12 us
    pallas_call x2, Pallas kernels, local(): pl.pallas_call(functools.partial(project_kernel, n_ctx, r * (part // 4)),...  4.33 us
    pallas_call x1, Pallas kernels, local(): pl.pallas_call(functools.partial(next_attention_kernel, r * part), out_sh...  3.37 us
    pallas_call x1, Pallas kernels, local(): pl.pallas_call(functools.partial(place_kernel, n_ctx), out_shape=jax.Shap...  2.53 us
    squeeze x1, local copies, waits for them, and re-layouts, local(): lax.dynamic_index_in_dim(w3, half, 0, keepdims=False)  1.69 us
  transfers between devices with their start and end apart: 29, of which 11 were waited for; matrix products, arithmetic and copies ran while one was open for 7% of the time, Pallas kernels for 19%

profile of v3, /device:TPU:0, one launch (start us, length us, event | category | flops | bytes accessed | tf_op | source)
XLA Modules:
  0.0 76.0 jit_solution(17566265877059658356)
XLA Ops:
  0.5 2.6 %collective-permute-start.1 = (bf16[320,320]{1,0:T(8,128)(2,1)}, bf16[320,320]{1,0:T(8,128)(2,1)S(1)}, u32[]{:S(2)}, u32[]{:S(2)}) collective-permute-start(bf16[320,320]{1,0:T(8,128)(2,1)} %refs_4_.1), channel_id=1, source_target_pairs={{0,1},{1,0},{2,3},{3,2},{4,5},{5,4},{6,7},{7,6},{8,9},{9,8},{10,11... | collective-permute-start | bytes 614408 | tf_op jit(solution)/shard_map/ppermute | solution.py:25
  3.1 2.6 %collective-permute-start.6 = (bf16[320,320]{1,0:T(8,128)(2,1)}, bf16[320,320]{1,0:T(8,128)(2,1)S(1)}, u32[]{:S(2)}, u32[]{:S(2)}) collective-permute-start(bf16[320,320]{1,0:T(8,128)(2,1)} %refs_4_.1), channel_id=1, source_target_pairs={{0,2},{1,3},{2,0},{3,1},{4,6},{5,7},{6,4},{7,5},{8,10},{9,11},{10,... | collective-permute-start | bytes 614408 | tf_op jit(solution)/shard_map/ppermute | solution.py:25
  5.7 1.7 %dynamic-slice_bitcast_fusion = bf16[320,320]{1,0:T(8,128)(2,1)} fusion(bf16[320,3,320]{2,0,1:T(8,128)(2,1)} %param.11, s32[]{:T(128)S(6)} %select_n.29), kind=kLoop, calls=%fused_computation.4 | loop fusion | bytes 409604 | tf_op jit(solution)/shard_map/jit(dynamic_index_in_dim)/squeeze | solution.py:195
  7.4 1.5 %collective-permute-start = (bf16[320,320]{1,0:T(8,128)(2,1)}, bf16[320,320]{1,0:T(8,128)(2,1)S(1)}, u32[]{:S(2)}, u32[]{:S(2)}) collective-permute-start(bf16[320,320]{1,0:T(8,128)(2,1)} %dynamic-slice_bitcast_fusion), channel_id=1, source_target_pairs={{0,8},{4,12},{8,0},{12,4},{1,9},{5,13},{9,1},{13,5},{2,10},{6,14},... | collective-permute-start | bytes 614408 | tf_op jit(solution)/shard_map/ppermute | solution.py:25
  8.9 1.7 %slice_bitcast_fusion = bf16[320,320]{1,0:T(8,128)(2,1)} fusion(bf16[3,320,320]{2,1,0:T(8,128)(2,1)} %bitcast.46), kind=kLoop, calls=%fused_computation.3 | loop fusion | bytes 409600 | tf_op jit(solution)/shard_map/squeeze | solution.py:196
  11.8 1.5 %copy-done.2 = bf16[768,1280]{1,0:T(8,128)(2,1)S(1)} copy-done((bf16[768,1280]{1,0:T(8,128)(2,1)S(1)}, bf16[768,1280]{1,0:T(8,128)(2,1)}, u32[]{:S(2)}) %copy-start.2) | copy-done | bytes 1966104
  13.4 1.6 %norm.1 = (bf16[768,1280]{1,0:T(8,128)(2,1)S(1)}, bf16[192,1280]{1,0:T(8,128)(2,1)S(1)}) custom-call(s32[3]{0:T(128)S(1)} %pad_add_fusion.1.index_ref, bf16[768,1280]{1,0:T(8,128)(2,1)S(1)} %copy-done.2, f32[1,1280]{1,0:T(1,128)S(1)} %reshape.14.gain_ref), custom_call_target="tpu_custom_call" | custom-call | tf_op jit(solution)/shard_map/norm/pallas_call | solution.py:200
  14.9 1.5 %collective-permute-done.refs_2_ = bf16[320,320]{1,0:T(8,128)(2,1)S(1)} collective-permute-done((bf16[320,320]{1,0:T(8,128)(2,1)}, bf16[320,320]{1,0:T(8,128)(2,1)S(1)}, u32[]{:S(2)}, u32[]{:S(2)}) %collective-permute-start) | collective-permute-done | bytes 204832 | tf_op jit(solution)/shard_map/ppermute | solution.py:25
  16.4 1.6 %collective-permute-start.3 = (bf16[320,320]{1,0:T(8,128)(2,1)S(1)}, bf16[320,320]{1,0:T(8,128)(2,1)}, u32[]{:S(2)}, u32[]{:S(2)}) collective-permute-start(bf16[320,320]{1,0:T(8,128)(2,1)S(1)} %collective-permute-done.refs_2_), channel_id=1, source_target_pairs={{0,16},{16,0},{1,17},{17,1},{2,18},{18,2},{3,19},{19,3},{4,20},{20... | collective-permute-start | bytes 614408 | tf_op jit(solution)/shard_map/ppermute | solution.py:25
  18.9 1.5 %collective-permute-start.10 = (bf16[2,320,320]{2,1,0:T(8,128)(2,1)}, bf16[2,320,320]{2,1,0:T(8,128)(2,1)}, u32[]{:S(2)}, u32[]{:S(2)}) collective-permute-start(bf16[2,320,320]{2,1,0:T(8,128)(2,1)} %pad_maximum_fusion.1), channel_id=1, source_target_pairs={{0,8},{4,12},{8,0},{12,4},{1,9},{5,13},{9,1},{13,5},{2,10},{6,14},... | collective-permute-start | bytes 1228808 | tf_op jit(solution)/shard_map/ppermute | solution.py:25
  20.7 2.1 %collective-permute-done.3.refs_3_ = bf16[320,320]{1,0:T(8,128)(2,1)} collective-permute-done((bf16[320,320]{1,0:T(8,128)(2,1)S(1)}, bf16[320,320]{1,0:T(8,128)(2,1)}, u32[]{:S(2)}, u32[]{:S(2)}) %collective-permute-start.3) | collective-permute-done | bytes 204832 | tf_op jit(solution)/shard_map/ppermute | solution.py:25
  24.1 2.6 %collective-permute-start.9 = (bf16[320,320]{1,0:T(8,128)(2,1)S(1)}, bf16[320,320]{1,0:T(8,128)(2,1)S(1)}, u32[]{:S(2)}, u32[]{:S(2)}) collective-permute-start(bf16[320,320]{1,0:T(8,128)(2,1)S(1)} %copy-done), channel_id=1, source_target_pairs={{0,3},{1,2},{2,1},{3,0},{4,7},{5,6},{6,5},{7,4},{8,11},{9,10},{10,... | collective-permute-start | bytes 614408 | tf_op jit(solution)/shard_map/ppermute | solution.py:25
  26.6 1.5 %collective-permute-start.11 = (s32[1,192]{1,0:T(1,128)S(1)}, s32[1,192]{1,0:T(1,128)S(1)}, u32[]{:S(2)}, u32[]{:S(2)}) collective-permute-start(s32[1,192]{1,0:T(1,128)S(1)} %bitcast.50), channel_id=1, source_target_pairs={{0,8},{4,12},{8,0},{12,4},{1,9},{5,13},{9,1},{13,5},{2,10},{6,14},... | collective-permute-start | bytes 2312 | tf_op jit(solution)/shard_map/ppermute | solution.py:25
  28.2 1.1 %copy-done.1 = bf16[320,3,320]{2,0,1:T(8,128)(2,1)S(1)} copy-done((bf16[320,3,320]{2,0,1:T(8,128)(2,1)S(1)}, bf16[320,3,320]{2,0,1:T(8,128)(2,1)}, u32[]{:S(2)}) %copy-start.1) | copy-done | bytes 614424
  29.3 0.9 %copy-done.4 = bf16[320,320]{1,0:T(8,128)(2,1)S(1)} copy-done((bf16[320,320]{1,0:T(8,128)(2,1)S(1)}, bf16[320,320]{1,0:T(8,128)(2,1)}, u32[]{:S(2)}) %copy-start.4) | copy-done | bytes 204824
  30.2 0.9 %copy-done.6 = bf16[320,320]{1,0:T(8,128)(2,1)S(1)} copy-done((bf16[320,320]{1,0:T(8,128)(2,1)S(1)}, bf16[320,320]{1,0:T(8,128)(2,1)}, u32[]{:S(2)}) %copy-start.6) | copy-done | bytes 204824
  31.2 5.1 %attention0.1 = (bf16[4,96,320]{2,1,0:T(8,128)(2,1)S(1)}, bf16[3,1280,320]{2,1,0:T(8,128)(2,1)S(1)}) custom-call(s32[3]{0:T(128)S(1)} %pad_add_fusion.1.index_ref, bf16[768,1280]{1,0:T(8,128)(2,1)S(1)} %get-tuple-element.58.hidden_ref, s32[6,128]{1,0:T(8,128)S(1)} %bitcast.48, bf16[3,320,320]{2,1,0:T(8,128)(2,1)S(1)} %bitcast.47, ...), custom_call_target="tpu_custom_call" | custom-call | tf_op jit(solution)/shard_map/attention0/pallas_call | solution.py:232
  37.3 2.3 %collective-permute-start.13 = (bf16[96,320]{1,0:T(8,128)(2,1)S(1)}, bf16[96,320]{1,0:T(8,128)(2,1)S(1)}, u32[]{:S(2)}, u32[]{:S(2)}) collective-permute-start(bf16[96,320]{1,0:T(8,128)(2,1)S(1)} %get-tuple-element.57), channel_id=1, source_target_pairs={{0,1},{1,0},{2,3},{3,2},{4,5},{5,4},{6,7},{7,6},{8,9},{9,8},{10,11... | collective-permute-start | bytes 184328 | tf_op jit(solution)/shard_map/ppermute | solution.py:25
  39.8 2.1 %collective-permute-start.15 = (bf16[96,320]{1,0:T(8,128)(2,1)S(1)}, bf16[96,320]{1,0:T(8,128)(2,1)S(1)}, u32[]{:S(2)}, u32[]{:S(2)}) collective-permute-start(bf16[96,320]{1,0:T(8,128)(2,1)S(1)} %get-tuple-element.63), channel_id=1, source_target_pairs={{0,3},{1,2},{2,1},{3,0},{4,7},{5,6},{6,5},{7,4},{8,11},{9,10},{10,... | collective-permute-start | bytes 184328 | tf_op jit(solution)/shard_map/ppermute | solution.py:25
  42.2 3.4 %attention1.1 = bf16[4,96,320]{2,1,0:T(8,128)(2,1)S(1)} custom-call(bf16[768,1280]{1,0:T(8,128)(2,1)S(1)} %get-tuple-element.58.hidden_ref, s32[6,128]{1,0:T(8,128)S(1)} %bitcast.49, bf16[3,1280,320]{2,1,0:T(8,128)(2,1)S(1)} %get-tuple-element.59.w_ref), custom_call_target="tpu_custom_call" | custom-call | tf_op jit(solution)/shard_map/attention1/pallas_call | solution.py:254
  45.7 2.6 %collective-permute-done.14.refs_2_ = bf16[96,320]{1,0:T(8,128)(2,1)S(1)} collective-permute-done((bf16[96,320]{1,0:T(8,128)(2,1)S(1)}, bf16[96,320]{1,0:T(8,128)(2,1)S(1)}, u32[]{:S(2)}, u32[]{:S(2)}) %collective-permute-start.14) | collective-permute-done | bytes 61472 | tf_op jit(solution)/shard_map/ppermute | solution.py:25
  48.2 1.6 %collective-permute-start.18 = (bf16[96,320]{1,0:T(8,128)(2,1)S(1)}, bf16[96,320]{1,0:T(8,128)(2,1)S(1)}, u32[]{:S(2)}, u32[]{:S(2)}) collective-permute-start(bf16[96,320]{1,0:T(8,128)(2,1)S(1)} %get-tuple-element.74), channel_id=1, source_target_pairs={{0,1},{1,0},{2,3},{3,2},{4,5},{5,4},{6,7},{7,6},{8,9},{9,8},{10,11... | collective-permute-start | bytes 184328 | tf_op jit(solution)/shard_map/ppermute | solution.py:25
  50.5 2.1 %collective-permute-done.18.refs_1_ = bf16[96,320]{1,0:T(8,128)(2,1)S(1)} collective-permute-done((bf16[96,320]{1,0:T(8,128)(2,1)S(1)}, bf16[96,320]{1,0:T(8,128)(2,1)S(1)}, u32[]{:S(2)}, u32[]{:S(2)}) %collective-permute-start.18) | collective-permute-done | bytes 61472 | tf_op jit(solution)/shard_map/ppermute | solution.py:25
  52.6 1.9 %collective-permute-start.21 = (bf16[96,320]{1,0:T(8,128)(2,1)S(1)}, bf16[96,320]{1,0:T(8,128)(2,1)S(1)}, u32[]{:S(2)}, u32[]{:S(2)}) collective-permute-start(bf16[96,320]{1,0:T(8,128)(2,1)S(1)} %get-tuple-element.79), channel_id=1, source_target_pairs={{0,2},{1,3},{2,0},{3,1},{4,6},{5,7},{6,4},{7,5},{8,10},{9,11},{10,... | collective-permute-start | bytes 184328 | tf_op jit(solution)/shard_map/ppermute | solution.py:25
  54.5 2.1 %collective-permute-start.22 = (bf16[96,320]{1,0:T(8,128)(2,1)S(1)}, bf16[96,320]{1,0:T(8,128)(2,1)S(1)}, u32[]{:S(2)}, u32[]{:S(2)}) collective-permute-start(bf16[96,320]{1,0:T(8,128)(2,1)S(1)} %get-tuple-element.80), channel_id=1, source_target_pairs={{0,3},{1,2},{2,1},{3,0},{4,7},{5,6},{6,5},{7,4},{8,11},{9,10},{10,... | collective-permute-start | bytes 184328 | tf_op jit(solution)/shard_map/ppermute | solution.py:25
  56.6 2.2 %project0.1.refs_4_ = bf16[96,1280]{1,0:T(8,128)(2,1)S(1)} custom-call(s32[3]{0:T(128)S(1)} %pad_add_fusion.1.index_ref, bf16[96,320]{1,0:T(8,128)(2,1)S(1)} %get-tuple-element.68.refs_0_, bf16[96,320]{1,0:T(8,128)(2,1)S(1)} %collective-permute-done.13.refs_1_, bf16[96,320]{1,0:T(8,128)(2,1)S(1)} %collective-permute-done.14.refs_2_, ...), custom_call_target="tpu_custom_call" | custom-call | tf_op jit(solution)/shard_map/project0/pallas_call | solution.py:276
  59.4 2.3 %collective-permute-done.21.refs_2_ = bf16[96,320]{1,0:T(8,128)(2,1)S(1)} collective-permute-done((bf16[96,320]{1,0:T(8,128)(2,1)S(1)}, bf16[96,320]{1,0:T(8,128)(2,1)S(1)}, u32[]{:S(2)}, u32[]{:S(2)}) %collective-permute-start.21) | collective-permute-done | bytes 61472 | tf_op jit(solution)/shard_map/ppermute | solution.py:25
  61.7 2.2 %project1.1.refs_5_ = bf16[96,1280]{1,0:T(8,128)(2,1)S(1)} custom-call(s32[3]{0:T(128)S(1)} %pad_add_fusion.1.index_ref, bf16[96,320]{1,0:T(8,128)(2,1)S(1)} %get-tuple-element.81.refs_0_, bf16[96,320]{1,0:T(8,128)(2,1)S(1)} %collective-permute-done.18.refs_1_, bf16[96,320]{1,0:T(8,128)(2,1)S(1)} %collective-permute-done.21.refs_2_, ...), custom_call_target="tpu_custom_call" | custom-call | tf_op jit(solution)/shard_map/project1/pallas_call | solution.py:276
  65.1 2.2 %collective-permute-done.25.refs_8_ = bf16[96,1280]{1,0:T(8,128)(2,1)S(1)} collective-permute-done((bf16[96,1280]{1,0:T(8,128)(2,1)S(1)}, bf16[96,1280]{1,0:T(8,128)(2,1)S(1)}, u32[]{:S(2)}, u32[]{:S(2)}) %collective-permute-start.25) | collective-permute-done | bytes 245792 | tf_op jit(solution)/shard_map/ppermute | solution.py:25
  67.3 4.6 %collective-permute-done.26.refs_9_ = bf16[96,1280]{1,0:T(8,128)(2,1)S(1)} collective-permute-done((bf16[96,1280]{1,0:T(8,128)(2,1)S(1)}, bf16[96,1280]{1,0:T(8,128)(2,1)S(1)}, u32[]{:S(2)}, u32[]{:S(2)}) %collective-permute-start.26) | collective-permute-done | bytes 245792 | tf_op jit(solution)/shard_map/ppermute | solution.py:25
  72.4 1.0 %collective-permute-done.12 = s32[2,1,192]{2,1,0:T(1,128)S(1)} collective-permute-done((s32[2,1,192]{2,1,0:T(1,128)S(1)}, s32[2,1,192]{2,1,0:T(1,128)S(1)}, u32[]{:S(2)}, u32[]{:S(2)}) %collective-permute-start.12) | collective-permute-done | bytes 1568 | tf_op jit(solution)/shard_map/ppermute | solution.py:25
  73.5 2.5 %placement.1 = bf16[192,1280]{1,0:T(8,128)(2,1)} custom-call(s32[3]{0:T(128)S(1)} %pad_add_fusion.1.index_ref, s32[1,192]{1,0:T(1,128)S(1)} %bitcast.52, s32[1,192]{1,0:T(1,128)S(1)} %get-tuple-element.94.refs_1_, s32[1,192]{1,0:T(1,128)S(1)} %collective-permute-done.11.refs_2_, s32[1,192]{1,0:T(1,128)S(1)} %get-tuple-element.93.refs_3_, ...), custom_call_target="tpu_custom_call" | custom-call | tf_op jit(solution)/shard_map/placement/pallas_call | solution.py:290
  (64 shorter events, 8.7 us)
Async XLA Ops:
  0.0 18.0 %copy-start = (bf16[320,320]{1,0:T(8,128)(2,1)S(1)}, bf16[320,320]{1,0:T(8,128)(2,1)}, u32[]{:S(2)}) copy-start(bf16[320,320]{1,0:T(8,128)(2,1)} %refs_4_.1) | copy-start | bytes 614404
  0.0 16.4 %collective-permute-start.2 = (bf16[3,320,320]{2,1,0:T(8,128)(2,1)}, bf16[3,320,320]{2,1,0:T(8,128)(2,1)}, u32[]{:S(2)}, u32[]{:S(2)}) collective-permute-start(bf16[3,320,320]{2,1,0:T(8,128)(2,1)} %bitcast.45), channel_id=1, source_target_pairs={{0,4},{4,0},{8,12},{12,8},{1,5},{5,1},{9,13},{13,9},{2,6},{6,2},{1... | collective-permute-start | bytes 1843208 | tf_op jit(solution)/shard_map/ppermute | solution.py:25
  0.5 16.0 %collective-permute-start.1 = (bf16[320,320]{1,0:T(8,128)(2,1)}, bf16[320,320]{1,0:T(8,128)(2,1)S(1)}, u32[]{:S(2)}, u32[]{:S(2)}) collective-permute-start(bf16[320,320]{1,0:T(8,128)(2,1)} %refs_4_.1), channel_id=1, source_target_pairs={{0,1},{1,0},{2,3},{3,2},{4,5},{5,4},{6,7},{7,6},{8,9},{9,8},{10,11... | collective-permute-start | bytes 614408 | tf_op jit(solution)/shard_map/ppermute | solution.py:25
  3.1 17.6 %collective-permute-start.6 = (bf16[320,320]{1,0:T(8,128)(2,1)}, bf16[320,320]{1,0:T(8,128)(2,1)S(1)}, u32[]{:S(2)}, u32[]{:S(2)}) collective-permute-start(bf16[320,320]{1,0:T(8,128)(2,1)} %refs_4_.1), channel_id=1, source_target_pairs={{0,2},{1,3},{2,0},{3,1},{4,6},{5,7},{6,4},{7,5},{8,10},{9,11},{10,... | collective-permute-start | bytes 614408 | tf_op jit(solution)/shard_map/ppermute | solution.py:25
  5.7 20.9 %copy-start.8 = (s32[192]{0:T(256)S(1)}, s32[192]{0:T(256)}, u32[]{:S(2)}) copy-start(s32[192]{0:T(256)} %param.9) | copy-start | bytes 2308
  5.7 22.5 %copy-start.7 = (s32[768]{0:T(1024)S(1)}, s32[768]{0:T(1024)}, u32[]{:S(2)}) copy-start(s32[768]{0:T(1024)} %param.8) | copy-start | bytes 9220
  7.4 9.0 %collective-permute-start = (bf16[320,320]{1,0:T(8,128)(2,1)}, bf16[320,320]{1,0:T(8,128)(2,1)S(1)}, u32[]{:S(2)}, u32[]{:S(2)}) collective-permute-start(bf16[320,320]{1,0:T(8,128)(2,1)} %dynamic-slice_bitcast_fusion), channel_id=1, source_target_pairs={{0,8},{4,12},{8,0},{12,4},{1,9},{5,13},{9,1},{13,5},{2,10},{6,14},... | collective-permute-start | bytes 614408 | tf_op jit(solution)/shard_map/ppermute | solution.py:25
  10.5 10.2 %collective-permute-start.4 = (bf16[320,320]{1,0:T(8,128)(2,1)}, bf16[320,320]{1,0:T(8,128)(2,1)}, u32[]{:S(2)}, u32[]{:S(2)}) collective-permute-start(bf16[320,320]{1,0:T(8,128)(2,1)} %slice_bitcast_fusion), channel_id=1, source_target_pairs={{0,8},{4,12},{8,0},{12,4},{1,9},{5,13},{9,1},{13,5},{2,10},{6,14},... | collective-permute-start | bytes 614408 | tf_op jit(solution)/shard_map/ppermute | solution.py:25
  16.4 6.4 %collective-permute-start.3 = (bf16[320,320]{1,0:T(8,128)(2,1)S(1)}, bf16[320,320]{1,0:T(8,128)(2,1)}, u32[]{:S(2)}, u32[]{:S(2)}) collective-permute-start(bf16[320,320]{1,0:T(8,128)(2,1)S(1)} %collective-permute-done.refs_2_), channel_id=1, source_target_pairs={{0,16},{16,0},{1,17},{17,1},{2,18},{18,2},{3,19},{19,3},{4,20},{20... | collective-permute-start | bytes 614408 | tf_op jit(solution)/shard_map/ppermute | solution.py:25
  18.0 4.8 %collective-permute-start.5 = (bf16[320,320]{1,0:T(8,128)(2,1)S(1)}, bf16[320,320]{1,0:T(8,128)(2,1)S(1)}, u32[]{:S(2)}, u32[]{:S(2)}) collective-permute-start(bf16[320,320]{1,0:T(8,128)(2,1)S(1)} %collective-permute-done.refs_2_), channel_id=1, source_target_pairs={{0,4},{4,0},{8,12},{12,8},{1,5},{5,1},{9,13},{13,9},{2,6},{6,2},{1... | collective-permute-start | bytes 614408 | tf_op jit(solution)/shard_map/ppermute | solution.py:25
  18.9 17.5 %collective-permute-start.10 = (bf16[2,320,320]{2,1,0:T(8,128)(2,1)}, bf16[2,320,320]{2,1,0:T(8,128)(2,1)}, u32[]{:S(2)}, u32[]{:S(2)}) collective-permute-start(bf16[2,320,320]{2,1,0:T(8,128)(2,1)} %pad_maximum_fusion.1), channel_id=1, source_target_pairs={{0,8},{4,12},{8,0},{12,4},{1,9},{5,13},{9,1},{13,5},{2,10},{6,14},... | collective-permute-start | bytes 1228808 | tf_op jit(solution)/shard_map/ppermute | solution.py:25
  23.5 4.6 %collective-permute-start.7 = (bf16[320,320]{1,0:T(8,128)(2,1)}, bf16[320,320]{1,0:T(8,128)(2,1)}, u32[]{:S(2)}, u32[]{:S(2)}) collective-permute-start(bf16[320,320]{1,0:T(8,128)(2,1)} %collective-permute-done.3.refs_3_), channel_id=1, source_target_pairs={{0,4},{4,0},{8,12},{12,8},{1,5},{5,1},{9,13},{13,9},{2,6},{6,2},{1... | collective-permute-start | bytes 614408 | tf_op jit(solution)/shard_map/ppermute | solution.py:25
  23.5 4.6 %collective-permute-start.8 = (bf16[320,320]{1,0:T(8,128)(2,1)}, bf16[320,320]{1,0:T(8,128)(2,1)}, u32[]{:S(2)}, u32[]{:S(2)}) collective-permute-start(bf16[320,320]{1,0:T(8,128)(2,1)} %collective-permute-done.4.refs_4_), channel_id=1, source_target_pairs={{0,4},{4,0},{8,12},{12,8},{1,5},{5,1},{9,13},{13,9},{2,6},{6,2},{1... | collective-permute-start | bytes 614408 | tf_op jit(solution)/shard_map/ppermute | solution.py:25
  24.1 12.3 %collective-permute-start.9 = (bf16[320,320]{1,0:T(8,128)(2,1)S(1)}, bf16[320,320]{1,0:T(8,128)(2,1)S(1)}, u32[]{:S(2)}, u32[]{:S(2)}) collective-permute-start(bf16[320,320]{1,0:T(8,128)(2,1)S(1)} %copy-done), channel_id=1, source_target_pairs={{0,3},{1,2},{2,1},{3,0},{4,7},{5,6},{6,5},{7,4},{8,11},{9,10},{10,... | collective-permute-start | bytes 614408 | tf_op jit(solution)/shard_map/ppermute | solution.py:25
  26.6 9.7 %collective-permute-start.11 = (s32[1,192]{1,0:T(1,128)S(1)}, s32[1,192]{1,0:T(1,128)S(1)}, u32[]{:S(2)}, u32[]{:S(2)}) collective-permute-start(s32[1,192]{1,0:T(1,128)S(1)} %bitcast.50), channel_id=1, source_target_pairs={{0,8},{4,12},{8,0},{12,4},{1,9},{5,13},{9,1},{13,5},{2,10},{6,14},... | collective-permute-start | bytes 2312 | tf_op jit(solution)/shard_map/ppermute | solution.py:25
  36.6 11.6 %collective-permute-start.16 = (bf16[4,320,320]{2,1,0:T(8,128)(2,1)S(1)}, bf16[4,320,320]{2,1,0:T(8,128)(2,1)S(1)}, u32[]{:S(2)}, u32[]{:S(2)}) collective-permute-start(bf16[4,320,320]{2,1,0:T(8,128)(2,1)S(1)} %pad_maximum_fusion), channel_id=1, source_target_pairs={{0,4},{4,0},{8,12},{12,8},{1,5},{5,1},{9,13},{13,9},{2,6},{6,2},{1... | collective-permute-start | bytes 2457608 | tf_op jit(solution)/shard_map/ppermute | solution.py:25
  36.8 13.7 %collective-permute-start.17 = (bf16[2,320,320]{2,1,0:T(8,128)(2,1)S(1)}, bf16[2,320,320]{2,1,0:T(8,128)(2,1)S(1)}, u32[]{:S(2)}, u32[]{:S(2)}) collective-permute-start(bf16[2,320,320]{2,1,0:T(8,128)(2,1)S(1)} %pad_maximum_fusion.2), channel_id=1, source_target_pairs={{0,8},{4,12},{8,0},{12,4},{1,9},{5,13},{9,1},{13,5},{2,10},{6,14},... | collective-permute-start | bytes 1228808 | tf_op jit(solution)/shard_map/ppermute | solution.py:25
  37.3 4.9 %collective-permute-start.13 = (bf16[96,320]{1,0:T(8,128)(2,1)S(1)}, bf16[96,320]{1,0:T(8,128)(2,1)S(1)}, u32[]{:S(2)}, u32[]{:S(2)}) collective-permute-start(bf16[96,320]{1,0:T(8,128)(2,1)S(1)} %get-tuple-element.57), channel_id=1, source_target_pairs={{0,1},{1,0},{2,3},{3,2},{4,5},{5,4},{6,7},{7,6},{8,9},{9,8},{10,11... | collective-permute-start | bytes 184328 | tf_op jit(solution)/shard_map/ppermute | solution.py:25
  39.6 8.6 %collective-permute-start.14 = (bf16[96,320]{1,0:T(8,128)(2,1)S(1)}, bf16[96,320]{1,0:T(8,128)(2,1)S(1)}, u32[]{:S(2)}, u32[]{:S(2)}) collective-permute-start(bf16[96,320]{1,0:T(8,128)(2,1)S(1)} %get-tuple-element.62), channel_id=1, source_target_pairs={{0,2},{1,3},{2,0},{3,1},{4,6},{5,7},{6,4},{7,5},{8,10},{9,11},{10,... | collective-permute-start | bytes 184328 | tf_op jit(solution)/shard_map/ppermute | solution.py:25
  39.8 8.4 %collective-permute-start.15 = (bf16[96,320]{1,0:T(8,128)(2,1)S(1)}, bf16[96,320]{1,0:T(8,128)(2,1)S(1)}, u32[]{:S(2)}, u32[]{:S(2)}) collective-permute-start(bf16[96,320]{1,0:T(8,128)(2,1)S(1)} %get-tuple-element.63), channel_id=1, source_target_pairs={{0,3},{1,2},{2,1},{3,0},{4,7},{5,6},{6,5},{7,4},{8,11},{9,10},{10,... | collective-permute-start | bytes 184328 | tf_op jit(solution)/shard_map/ppermute | solution.py:25
  48.2 4.4 %collective-permute-start.18 = (bf16[96,320]{1,0:T(8,128)(2,1)S(1)}, bf16[96,320]{1,0:T(8,128)(2,1)S(1)}, u32[]{:S(2)}, u32[]{:S(2)}) collective-permute-start(bf16[96,320]{1,0:T(8,128)(2,1)S(1)} %get-tuple-element.74), channel_id=1, source_target_pairs={{0,1},{1,0},{2,3},{3,2},{4,5},{5,4},{6,7},{7,6},{8,9},{9,8},{10,11... | collective-permute-start | bytes 184328 | tf_op jit(solution)/shard_map/ppermute | solution.py:25
  49.9 6.7 %collective-permute-start.19 = (bf16[2,320,320]{2,1,0:T(8,128)(2,1)}, bf16[2,320,320]{2,1,0:T(8,128)(2,1)S(1)}, u32[]{:S(2)}, u32[]{:S(2)}) collective-permute-start(bf16[2,320,320]{2,1,0:T(8,128)(2,1)} %collective-permute-done.10.refs_9_), channel_id=1, source_target_pairs={{0,4},{4,0},{8,12},{12,8},{1,5},{5,1},{9,13},{13,9},{2,6},{6,2},{1... | collective-permute-start | bytes 1228808 | tf_op jit(solution)/shard_map/ppermute | solution.py:25
  52.6 4.0 %collective-permute-start.20 = (bf16[2,320,320]{2,1,0:T(8,128)(2,1)S(1)}, bf16[2,320,320]{2,1,0:T(8,128)(2,1)S(1)}, u32[]{:S(2)}, u32[]{:S(2)}) collective-permute-start(bf16[2,320,320]{2,1,0:T(8,128)(2,1)S(1)} %collective-permute-done.17.refs_10_), channel_id=1, source_target_pairs={{0,4},{4,0},{8,12},{12,8},{1,5},{5,1},{9,13},{13,9},{2,6},{6,2},{1... | collective-permute-start | bytes 1228808 | tf_op jit(solution)/shard_map/ppermute | solution.py:25
  52.6 9.1 %collective-permute-start.21 = (bf16[96,320]{1,0:T(8,128)(2,1)S(1)}, bf16[96,320]{1,0:T(8,128)(2,1)S(1)}, u32[]{:S(2)}, u32[]{:S(2)}) collective-permute-start(bf16[96,320]{1,0:T(8,128)(2,1)S(1)} %get-tuple-element.79), channel_id=1, source_target_pairs={{0,2},{1,3},{2,0},{3,1},{4,6},{5,7},{6,4},{7,5},{8,10},{9,11},{10,... | collective-permute-start | bytes 184328 | tf_op jit(solution)/shard_map/ppermute | solution.py:25
  54.5 7.2 %collective-permute-start.22 = (bf16[96,320]{1,0:T(8,128)(2,1)S(1)}, bf16[96,320]{1,0:T(8,128)(2,1)S(1)}, u32[]{:S(2)}, u32[]{:S(2)}) collective-permute-start(bf16[96,320]{1,0:T(8,128)(2,1)S(1)} %get-tuple-element.80), channel_id=1, source_target_pairs={{0,3},{1,2},{2,1},{3,0},{4,7},{5,6},{6,5},{7,4},{8,11},{9,10},{10,... | collective-permute-start | bytes 184328 | tf_op jit(solution)/shard_map/ppermute | solution.py:25
  58.8 8.6 %collective-permute-start.25 = (bf16[96,1280]{1,0:T(8,128)(2,1)S(1)}, bf16[96,1280]{1,0:T(8,128)(2,1)S(1)}, u32[]{:S(2)}, u32[]{:S(2)}) collective-permute-start(bf16[96,1280]{1,0:T(8,128)(2,1)S(1)} %project0.1.refs_4_), channel_id=1, source_target_pairs={{0,8},{4,12},{8,0},{12,4},{1,9},{5,13},{9,1},{13,5},{2,10},{6,14},... | collective-permute-start | bytes 737288 | tf_op jit(solution)/shard_map/ppermute | solution.py:25
  63.9 8.0 %collective-permute-start.26 = (bf16[96,1280]{1,0:T(8,128)(2,1)S(1)}, bf16[96,1280]{1,0:T(8,128)(2,1)S(1)}, u32[]{:S(2)}, u32[]{:S(2)}) collective-permute-start(bf16[96,1280]{1,0:T(8,128)(2,1)S(1)} %project1.1.refs_5_), channel_id=1, source_target_pairs={{0,8},{4,12},{8,0},{12,4},{1,9},{5,13},{9,1},{13,5},{2,10},{6,14},... | collective-permute-start | bytes 737288 | tf_op jit(solution)/shard_map/ppermute | solution.py:25
  64.6 8.8 %collective-permute-start.23 = (bf16[96,1280]{1,0:T(8,128)(2,1)S(1)}, bf16[96,1280]{1,0:T(8,128)(2,1)S(1)}, u32[]{:S(2)}, u32[]{:S(2)}) collective-permute-start(bf16[96,1280]{1,0:T(8,128)(2,1)S(1)} %project0.1.refs_4_), channel_id=1, source_target_pairs={{0,4},{4,0},{8,12},{12,8},{1,5},{5,1},{9,13},{13,9},{2,6},{6,2},{1... | collective-permute-start | bytes 737288 | tf_op jit(solution)/shard_map/ppermute | solution.py:25
  64.6 8.8 %collective-permute-start.24 = (bf16[96,1280]{1,0:T(8,128)(2,1)S(1)}, bf16[96,1280]{1,0:T(8,128)(2,1)S(1)}, u32[]{:S(2)}, u32[]{:S(2)}) collective-permute-start(bf16[96,1280]{1,0:T(8,128)(2,1)S(1)} %project1.1.refs_5_), channel_id=1, source_target_pairs={{0,4},{4,0},{8,12},{12,8},{1,5},{5,1},{9,13},{13,9},{2,6},{6,2},{1... | collective-permute-start | bytes 737288 | tf_op jit(solution)/shard_map/ppermute | solution.py:25
  67.3 6.1 %collective-permute-start.27 = (bf16[96,1280]{1,0:T(8,128)(2,1)S(1)}, bf16[96,1280]{1,0:T(8,128)(2,1)S(1)}, u32[]{:S(2)}, u32[]{:S(2)}) collective-permute-start(bf16[96,1280]{1,0:T(8,128)(2,1)S(1)} %collective-permute-done.25.refs_8_), channel_id=1, source_target_pairs={{0,4},{4,0},{8,12},{12,8},{1,5},{5,1},{9,13},{13,9},{2,6},{6,2},{1... | collective-permute-start | bytes 737288 | tf_op jit(solution)/shard_map/ppermute | solution.py:25
  71.9 1.5 %collective-permute-start.28 = (bf16[96,1280]{1,0:T(8,128)(2,1)S(1)}, bf16[96,1280]{1,0:T(8,128)(2,1)S(1)}, u32[]{:S(2)}, u32[]{:S(2)}) collective-permute-start(bf16[96,1280]{1,0:T(8,128)(2,1)S(1)} %collective-permute-done.26.refs_9_), channel_id=1, source_target_pairs={{0,4},{4,0},{8,12},{12,8},{1,5},{5,1},{9,13},{13,9},{2,6},{6,2},{1... | collective-permute-start | bytes 737288 | tf_op jit(solution)/shard_map/ppermute | solution.py:25
  71.9 1.5 %collective-permute-start.12 = (s32[2,1,192]{2,1,0:T(1,128)S(1)}, s32[2,1,192]{2,1,0:T(1,128)S(1)}, u32[]{:S(2)}, u32[]{:S(2)}) collective-permute-start(s32[2,1,192]{2,1,0:T(1,128)S(1)} %pad_add_fusion), channel_id=1, source_target_pairs={{0,4},{4,0},{8,12},{12,8},{1,5},{5,1},{9,13},{13,9},{2,6},{6,2},{1... | collective-permute-start | bytes 4616 | tf_op jit(solution)/shard_map/ppermute | solution.py:25
  (7 other events, 26.7 us)

commit v4 on v3

--- a/solution.py
+++ b/solution.py
@@ -13,6 +13,7 @@
 CHUNKS = 2
 F32 = jnp.float32
 BF16 = jnp.bfloat16
+ANY = pl.BlockSpec(memory_space=pl.ANY)
 VMEM = pl.BlockSpec(memory_space=pltpu.VMEM)
 SMEM = pl.BlockSpec(memory_space=pltpu.SMEM)
 
@@ -111,8 +112,14 @@
 
 def first_attention_kernel(n_ctx, index_ref, hidden_ref, valid_ref, *refs):
     shards = list(refs[: 2 + 3 * (n_ctx - 2)])
-    out_ref, w_ref, *scratch = refs[len(shards) :]
+    out_ref, w_ref, *scratch, sem = refs[len(shards) :]
     depth = shards[0].shape[1]
+    copies = []
+
+    def bring(src, dst):
+        copies.append(pltpu.make_async_copy(src, dst, sem.at[len(copies)]))
+        copies[-1].start()
+
     me = index_ref[0]
     part = index_ref[2]
     for key in range(n_ctx):
@@ -120,10 +127,12 @@
         if key < 2:
             block = shards.pop(0)
             for j in range(3):
-                w_ref[j, pl.ds(at, depth), :] = block[j]
+                bring(block.at[j], w_ref.at[j, pl.ds(at, depth), :])
         else:
             for j in (part, 1 - part, 2):
-                w_ref[j, pl.ds(at, depth), :] = shards.pop(0)[...]
+                bring(shards.pop(0), w_ref.at[j, pl.ds(at, depth), :])
+    for copy in copies:
+        copy.wait()
     attend(0, hidden_ref, valid_ref, w_ref, out_ref, *scratch)
 
 
@@ -132,8 +141,8 @@
 
 
 def project_kernel(n_ctx, row0, index_ref, *refs):
-    mixed = jnp.concatenate([m[...] for m in refs[:4]], axis=1)
-    *blocks, own_ref, gain_ref, out_ref, part_ref = refs[4:]
+    mix_ref, *blocks, own_ref, gain_ref, out_ref, part_ref = refs
+    mixed = jnp.concatenate([mix_ref[index_ref[1] ^ s] for s in range(4)], axis=1)
     rows = out_ref.shape[0]
     me = index_ref[0]
     for key in range(n_ctx):
@@ -192,8 +201,10 @@
         return swap(x, "context", n_ctx, 1)
 
     w3 = jnp.transpose(w_qkv, (1, 0, 2))
-    first = gather_cross(lax.dynamic_index_in_dim(w3, half, 0, keepdims=False), n_ctx)
-    value = gather_cross(w3[2], n_ctx)
+    third = lax.dynamic_index_in_dim(w3, half, 0, keepdims=False)
+    third, last, w_proj = together(third, w3[2], w_proj)
+    first = gather_cross(third, n_ctx)
+    value = gather_cross(last, n_ctx)
     twin = over_core(w3)
     by_one = swap(w_proj, "tensor", n_ten, 1)
     by_two = swap(w_proj, "tensor", n_ten, 2)
@@ -232,25 +243,20 @@
     mixed, w_full = pl.pallas_call(
         functools.partial(first_attention_kernel, n_ctx),
         out_shape=(mix_shape, jax.ShapeDtypeStruct((3, feat, width), BF16)),
-        in_specs=[SMEM] + [VMEM] * (2 + len(shard_list)),
+        in_specs=[SMEM, VMEM, VMEM] + [ANY] * len(shard_list),
         out_specs=(VMEM, VMEM),
-        scratch_shapes=scratch,
+        scratch_shapes=scratch + [pltpu.SemaphoreType.DMA((3 * n_ctx,))],
         compiler_params=params(32),
         name="attention0",
     )(index, hidden, valid_pairs, *shard_list)
-    def by_tensor(mixed):
-        return [lax.dynamic_index_in_dim(mixed, ten ^ s, 0, keepdims=False) for s in range(n_ten)]
-
-    def exchange(pieces):
-        return [pieces[0]] + [swap(pieces[s], "tensor", n_ten, s) for s in range(1, n_ten)]
-
-    pieces = by_tensor(mixed)
-    pieces, by_three, low, places, w_proj = together(pieces, by_three, low, places, w_proj)
-    received = [exchange(pieces)]
+    def exchange(mixed):
+        return lax.all_to_all(mixed, "tensor", 0, 0, tiled=True)
+
+    mixed, by_three, low, places, w_proj = together(mixed, by_three, low, places, w_proj)
+    received = [exchange(mixed)]
     high = gather_cross(jnp.stack([by_two, by_three]), n_ctx)
     own_twin = over_core(jnp.stack([w_proj, by_one, by_two, by_three]))
     for r in range(1, CHUNKS):
-        received[r - 1][1], hidden = together(received[r - 1][1], hidden)
         mixed = pl.pallas_call(
             functools.partial(next_attention_kernel, r * part),
             out_shape=mix_shape,
@@ -260,12 +266,11 @@
             compiler_params=params(32),
             name="attention" + str(r),
         )(hidden, valid_pairs, w_full)
-        pieces, received[r - 1], own_twin, low = together(
-            by_tensor(mixed), received[r - 1], own_twin, low
-        )
-        received.append(exchange(pieces))
-    high, received[-1][1] = together(high, received[-1][1])
-
+        mixed, own_twin, low = together(mixed, own_twin, low)
+        received.append(exchange(mixed))
+
+    place_twin = over_core(jnp.stack([places[k] for k in (0, *cross)]))
+    received[0], place_twin = together(received[0], place_twin)
     blocks = [w_proj, by_one, by_two, by_three, own_twin]
     for k in cross:
         blocks += [low[k], high[k], over_core(low[k]), over_core(high[k])]
@@ -276,14 +281,13 @@
         done = pl.pallas_call(
             functools.partial(project_kernel, n_ctx, r * (part // 4)),
             out_shape=jax.ShapeDtypeStruct((part // 4, feat), BF16),
-            in_specs=[SMEM] + [VMEM] * (n_ten + len(blocks) + 2),
+            in_specs=[SMEM] + [VMEM] * (1 + len(blocks) + 2),
             out_specs=VMEM,
             scratch_shapes=[pltpu.VMEM((n_ctx, part // 4, w_proj.shape[1]), F32)],
             compiler_params=params(32),
             name="project" + str(r),
-        )(index, *received[r], *blocks, own_patches, gain2)
+        )(index, received[r], *blocks, own_patches, gain2)
         gathered.append(gather_xor(done, n_ctx))
-    place_twin = over_core(jnp.stack([places[k] for k in (0, *cross)]))
     place_list = []
     for i, k in enumerate((0, *cross)):
         place_list += [places[k], place_twin[i]]

time: 76.5 us -> 88.1 us (1.15)
  waiting for transfers between devices: 19.7 us -> 25.8 us
  Pallas kernels: 16.9 us -> 19.9 us
  local copies, waits for them, and re-layouts: 9.4 us -> 12 us
  starting transfers between devices: 28.6 us -> 26.3 us
  other arithmetic: 1.28 us -> 3.18 us
    ppermute x29 -> x23, starting transfers between devices: 28.6 us -> 18.1 us  [swap(): return lax.ppermute(x, axis, [(i, i ^ bit) for i in range(size)])]
    all_to_all x0 -> x2, starting transfers between devices: none -> 8.19 us  [exchange(): return lax.all_to_all(mixed, 'tensor', 0, 0, tiled=True)]
    ppermute x29 -> x23, waiting for transfers between devices: 19.7 us -> 23.5 us  [swap(): return lax.ppermute(x, axis, [(i, i ^ bit) for i in range(size)])]
    unnamed x20 -> x38, local copies, waits for them, and re-layouts: 5.26 us -> 7.9 us
    all_to_all x0 -> x2, waiting for transfers between devices: none -> 2.32 us  [exchange(): return lax.all_to_all(mixed, 'tensor', 0, 0, tiled=True)]
    another operation x1, other arithmetic: 0.09 us -> 1.82 us  [local(): high = gather_cross(jnp.stack([by_two, by_three]), n_ctx)]
    pallas_call x1, Pallas kernels: 5.12 us -> 6.44 us  [local(): pl.pallas_call(functools.partial(first_attention_kernel, n_ctx), out_shap...]
    pallas_call x2, Pallas kernels: 4.33 us -> 5.52 us  [local(): pl.pallas_call(functools.partial(project_kernel, n_ctx, r * (part // 4)),...]
  transfers between devices with their start and end apart: 29 -> 25, of which waited for: 11 -> 10; matrix products, arithmetic and copies ran while one was open for 7% -> 7% of each run, Pallas kernels for 19% -> 19%
where the time goes in v4:
time: 88.1 us; the launch traced here: 87.4 us
  starting transfers between devices  26.3 us (30%)
  waiting for transfers between devices  25.8 us (29%)
  Pallas kernels  19.9 us (23%)
  local copies, waits for them, and re-layouts  12 us (14%)
  other arithmetic  3.18 us (4%)
    ppermute x23, waiting for transfers between devices, swap(): return lax.ppermute(x, axis, [(i, i ^ bit) for i in range(size)])  23.5 us
    ppermute x23, starting transfers between devices, swap(): return lax.ppermute(x, axis, [(i, i ^ bit) for i in range(size)])  18.1 us
    all_to_all x2, starting transfers between devices, exchange(): return lax.all_to_all(mixed, 'tensor', 0, 0, tiled=True)  8.19 us
    unnamed x38, local copies, waits for them, and re-layouts  7.9 us
    pallas_call x1, Pallas kernels, local(): pl.pallas_call(functools.partial(first_attention_kernel, n_ctx), out_shap...  6.44 us
    pallas_call x2, Pallas kernels, local(): pl.pallas_call(functools.partial(project_kernel, n_ctx, r * (part // 4)),...  5.52 us
    pallas_call x1, Pallas kernels, local(): pl.pallas_call(functools.partial(next_attention_kernel, r * part), out_sh...  3.36 us
    pallas_call x1, Pallas kernels, local(): pl.pallas_call(functools.partial(place_kernel, n_ctx), out_shape=jax.Shap...  3.06 us
  transfers between devices with their start and end apart: 25, of which 10 were waited for; matrix products, arithmetic and copies ran while one was open for 7% of the time, Pallas kernels for 19%

profile of v4, /device:TPU:0, one launch (start us, length us, event | category | flops | bytes accessed | tf_op | source)
XLA Modules:
  0.0 87.4 jit_solution(15819275281837776714)
XLA Ops:
  0.5 1.7 %dynamic-slice_bitcast_fusion = bf16[320,320]{1,0:T(8,128)(2,1)} fusion(bf16[320,3,320]{2,0,1:T(8,128)(2,1)} %param.11, s32[]{:T(128)S(6)} %select_n.12), kind=kLoop, calls=%fused_computation.4 | loop fusion | bytes 409604 | tf_op jit(solution)/shard_map/jit(dynamic_index_in_dim)/squeeze | solution.py:204
  2.2 1.7 %slice_bitcast_fusion = bf16[320,320]{1,0:T(8,128)(2,1)} fusion(bf16[3,320,320]{2,1,0:T(8,128)(2,1)} %bitcast.30), kind=kLoop, calls=%fused_computation.3 | loop fusion | bytes 409600 | tf_op jit(solution)/shard_map/squeeze | solution.py:205
  3.9 2.6 %collective-permute-start = (bf16[320,320]{1,0:T(8,128)(2,1)}, bf16[320,320]{1,0:T(8,128)(2,1)}, u32[]{:S(2)}, u32[]{:S(2)}) collective-permute-start(bf16[320,320]{1,0:T(8,128)(2,1)} %dynamic-slice_bitcast_fusion), channel_id=1, source_target_pairs={{0,8},{4,12},{8,0},{12,4},{1,9},{5,13},{9,1},{13,5},{2,10},{6,14},... | collective-permute-start | bytes 614408 | tf_op jit(solution)/shard_map/ppermute | solution.py:26
  6.4 1.6 %collective-permute-start.1 = (bf16[320,320]{1,0:T(8,128)(2,1)}, bf16[320,320]{1,0:T(8,128)(2,1)S(1)}, u32[]{:S(2)}, u32[]{:S(2)}) collective-permute-start(bf16[320,320]{1,0:T(8,128)(2,1)} %refs_1_.1), channel_id=1, source_target_pairs={{0,1},{1,0},{2,3},{3,2},{4,5},{5,4},{6,7},{7,6},{8,9},{9,8},{10,11... | collective-permute-start | bytes 614408 | tf_op jit(solution)/shard_map/ppermute | solution.py:26
  8.0 2.6 %collective-permute-start.6 = (bf16[320,320]{1,0:T(8,128)(2,1)}, bf16[320,320]{1,0:T(8,128)(2,1)S(1)}, u32[]{:S(2)}, u32[]{:S(2)}) collective-permute-start(bf16[320,320]{1,0:T(8,128)(2,1)} %refs_1_.1), channel_id=1, source_target_pairs={{0,2},{1,3},{2,0},{3,1},{4,6},{5,7},{6,4},{7,5},{8,10},{9,11},{10,... | collective-permute-start | bytes 614408 | tf_op jit(solution)/shard_map/ppermute | solution.py:26
  11.9 1.5 %copy-done.10 = bf16[768,1280]{1,0:T(8,128)(2,1)S(1)} copy-done((bf16[768,1280]{1,0:T(8,128)(2,1)S(1)}, bf16[768,1280]{1,0:T(8,128)(2,1)}, u32[]{:S(2)}) %copy-start.10) | copy-done | bytes 1966104
  13.4 1.5 %norm.1 = (bf16[768,1280]{1,0:T(8,128)(2,1)S(1)}, bf16[192,1280]{1,0:T(8,128)(2,1)S(1)}) custom-call(s32[3]{0:T(128)S(1)} %pad_add_fusion.1.index_ref, bf16[768,1280]{1,0:T(8,128)(2,1)S(1)} %copy-done.10, f32[1,1280]{1,0:T(1,128)S(1)} %reshape.14.gain_ref), custom_call_target="tpu_custom_call" | custom-call | tf_op jit(solution)/shard_map/norm/pallas_call | solution.py:211
  15.0 4.8 %collective-permute-done.1.refs_2_ = bf16[320,320]{1,0:T(8,128)(2,1)S(1)} collective-permute-done((bf16[320,320]{1,0:T(8,128)(2,1)}, bf16[320,320]{1,0:T(8,128)(2,1)S(1)}, u32[]{:S(2)}, u32[]{:S(2)}) %collective-permute-start.1) | collective-permute-done | bytes 204832 | tf_op jit(solution)/shard_map/ppermute | solution.py:26
  19.8 1.5 %collective-permute-start.3 = (bf16[320,320]{1,0:T(8,128)(2,1)}, bf16[320,320]{1,0:T(8,128)(2,1)S(1)}, u32[]{:S(2)}, u32[]{:S(2)}) collective-permute-start(bf16[320,320]{1,0:T(8,128)(2,1)} %collective-permute-done.refs_2_), channel_id=1, source_target_pairs={{0,16},{16,0},{1,17},{17,1},{2,18},{18,2},{3,19},{19,3},{4,20},{20... | collective-permute-start | bytes 614408 | tf_op jit(solution)/shard_map/ppermute | solution.py:26
  22.2 5.1 %collective-permute-done.3.refs_3_ = bf16[320,320]{1,0:T(8,128)(2,1)S(1)} collective-permute-done((bf16[320,320]{1,0:T(8,128)(2,1)}, bf16[320,320]{1,0:T(8,128)(2,1)S(1)}, u32[]{:S(2)}, u32[]{:S(2)}) %collective-permute-start.3) | collective-permute-done | bytes 204832 | tf_op jit(solution)/shard_map/ppermute | solution.py:26
  27.8 2.6 %collective-permute-start.9 = (bf16[320,320]{1,0:T(8,128)(2,1)S(1)}, bf16[320,320]{1,0:T(8,128)(2,1)S(1)}, u32[]{:S(2)}, u32[]{:S(2)}) collective-permute-start(bf16[320,320]{1,0:T(8,128)(2,1)S(1)} %copy-done), channel_id=1, source_target_pairs={{0,3},{1,2},{2,1},{3,0},{4,7},{5,6},{6,5},{7,4},{8,11},{9,10},{10,... | collective-permute-start | bytes 614408 | tf_op jit(solution)/shard_map/ppermute | solution.py:26
  30.9 6.4 %attention0.1 = (bf16[4,96,320]{2,1,0:T(8,128)(2,1)S(1)}, bf16[3,1280,320]{2,1,0:T(8,128)(2,1)S(1)}) custom-call(s32[3]{0:T(128)S(1)} %pad_add_fusion.1.index_ref, bf16[768,1280]{1,0:T(8,128)(2,1)S(1)} %get-tuple-element.36.hidden_ref, s32[6,128]{1,0:T(8,128)S(1)} %bitcast.32, bf16[3,320,320]{2,1,0:T(8,128)(2,1)S(1)} %bitcast.31, ...), custom_call_target="tpu_custom_call" | custom-call | tf_op jit(solution)/shard_map/attention0/pallas_call | solution.py:243
  37.4 1.6 %copy-done.7 = bf16[3,1280,320]{2,1,0:T(8,128)(2,1)} copy-done((bf16[3,1280,320]{2,1,0:T(8,128)(2,1)}, bf16[3,1280,320]{2,1,0:T(8,128)(2,1)S(1)}, u32[]{:S(2)}) %copy-start.7) | copy-done | bytes 2457624
  39.0 1.2 %pad_maximum_fusion = bf16[4,320,320]{2,1,0:T(8,128)(2,1)} fusion(bf16[1,320,320]{2,1,0:T(8,128)(2,1)S(1)} %bitcast.27, bf16[1,320,320]{2,1,0:T(8,128)(2,1)S(1)} %bitcast.25, bf16[1,320,320]{2,1,0:T(8,128)(2,1)S(1)} %bitcast.24, bf16[1,320,320]{2,1,0:T(8,128)(2,1)S(1)} %bitcast.22), kind=kLoop, calls=%fused_computation | loop fusion | flops 1228800 | bytes 1638400 | tf_op jit(solution)/shard_map/stack | solution.py:258
  40.2 1.8 %pad_maximum_fusion.2 = bf16[2,320,320]{2,1,0:T(8,128)(2,1)} fusion(bf16[1,320,320]{2,1,0:T(8,128)(2,1)S(1)} %bitcast.28, bf16[1,320,320]{2,1,0:T(8,128)(2,1)} %bitcast.26), kind=kLoop, calls=%fused_computation.2 | loop fusion | flops 204800 | bytes 819200 | tf_op jit(solution)/shard_map/stack | solution.py:257
  42.0 1.5 %collective-permute-start.14 = (bf16[2,320,320]{2,1,0:T(8,128)(2,1)}, bf16[2,320,320]{2,1,0:T(8,128)(2,1)}, u32[]{:S(2)}, u32[]{:S(2)}) collective-permute-start(bf16[2,320,320]{2,1,0:T(8,128)(2,1)} %pad_maximum_fusion.2), channel_id=1, source_target_pairs={{0,8},{4,12},{8,0},{12,4},{1,9},{5,13},{9,1},{13,5},{2,10},{6,14},... | collective-permute-start | bytes 1228808 | tf_op jit(solution)/shard_map/ppermute | solution.py:26
  43.5 4.1 %all-to-all-start = ((bf16[4,96,320]{2,1,0:T(8,128)(2,1)}), bf16[4,96,320]{2,1,0:T(8,128)(2,1)}, u32[]{:S(2)}, u32[]{:S(2)}) async-start(bf16[4,96,320]{2,1,0:T(8,128)(2,1)} %copy-done.15), calls=%async_computation | async-start | bytes 589824 | tf_op jit(solution)/shard_map/all_to_all | solution.py:253
  47.6 1.8 %copy-done.8 = bf16[3,1280,320]{2,1,0:T(8,128)(2,1)S(1)} copy-done((bf16[3,1280,320]{2,1,0:T(8,128)(2,1)S(1)}, bf16[3,1280,320]{2,1,0:T(8,128)(2,1)}, u32[]{:S(2)}) %copy-start.8) | copy-done | bytes 2457624
  49.4 3.4 %attention1.1 = bf16[4,96,320]{2,1,0:T(8,128)(2,1)S(1)} custom-call(bf16[768,1280]{1,0:T(8,128)(2,1)S(1)} %get-tuple-element.36.hidden_ref, s32[6,128]{1,0:T(8,128)S(1)} %bitcast.33, bf16[3,1280,320]{2,1,0:T(8,128)(2,1)S(1)} %copy-done.8), custom_call_target="tpu_custom_call" | custom-call | tf_op jit(solution)/shard_map/attention1/pallas_call | solution.py:260
  52.8 3.1 %collective-permute-done.14.refs_7_ = bf16[2,320,320]{2,1,0:T(8,128)(2,1)} collective-permute-done((bf16[2,320,320]{2,1,0:T(8,128)(2,1)}, bf16[2,320,320]{2,1,0:T(8,128)(2,1)}, u32[]{:S(2)}, u32[]{:S(2)}) %collective-permute-start.14) | collective-permute-done | bytes 409632 | tf_op jit(solution)/shard_map/ppermute | solution.py:26
  56.5 1.5 %all-to-all-done.refs_0_ = bf16[4,96,320]{2,1,0:T(8,128)(2,1)} async-done(((bf16[4,96,320]{2,1,0:T(8,128)(2,1)}), bf16[4,96,320]{2,1,0:T(8,128)(2,1)}, u32[]{:S(2)}, u32[]{:S(2)}) %all-to-all-start) | async-done | bytes 245792 | tf_op jit(solution)/shard_map/all_to_all | solution.py:253
  57.9 4.1 %all-to-all-start.1 = ((bf16[4,96,320]{2,1,0:T(8,128)(2,1)}), bf16[4,96,320]{2,1,0:T(8,128)(2,1)}, u32[]{:S(2)}, u32[]{:S(2)}) async-start(bf16[4,96,320]{2,1,0:T(8,128)(2,1)} %copy-done.14), calls=%async_computation.1 | async-start | bytes 589824 | tf_op jit(solution)/shard_map/all_to_all | solution.py:253
  62.1 1.1 %collective-permute-done.12 = s32[2,1,192]{2,1,0:T(1,128)S(1)} collective-permute-done((s32[2,1,192]{2,1,0:T(1,128)S(1)}, s32[2,1,192]{2,1,0:T(1,128)S(1)}, u32[]{:S(2)}, u32[]{:S(2)}) %collective-permute-start.12) | collective-permute-done | bytes 1568 | tf_op jit(solution)/shard_map/ppermute | solution.py:26
  63.3 0.9 %copy-done.2 = bf16[320,320]{1,0:T(8,128)(2,1)S(1)} copy-done((bf16[320,320]{1,0:T(8,128)(2,1)S(1)}, bf16[320,320]{1,0:T(8,128)(2,1)}, u32[]{:S(2)}) %copy-start.2) | copy-done | bytes 204824
  65.2 1.0 %copy-done.12 = bf16[192,1280]{1,0:T(8,128)(2,1)S(1)} copy-done((bf16[192,1280]{1,0:T(8,128)(2,1)S(1)}, bf16[192,1280]{1,0:T(8,128)(2,1)}, u32[]{:S(2)}) %copy-start.12) | copy-done | bytes 491544
  66.2 3.2 %project0.1.refs_4_ = bf16[96,1280]{1,0:T(8,128)(2,1)} custom-call(s32[3]{0:T(128)S(1)} %pad_add_fusion.1.index_ref, bf16[4,96,320]{2,1,0:T(8,128)(2,1)} %all-to-all-done.refs_0_, bf16[320,320]{1,0:T(8,128)(2,1)S(1)} %copy-done, bf16[320,320]{1,0:T(8,128)(2,1)S(1)} %collective-permute-done.1.refs_2_, bf16[320,320]{1,0:T(8,128)(2,1)S(1)} %copy-done.2, ...), custom_call_target="tpu_custom_call" | custom-call | tf_op jit(solution)/shard_map/project0/pallas_call | solution.py:281
  70.7 2.4 %project1.1.refs_5_ = bf16[96,1280]{1,0:T(8,128)(2,1)S(1)} custom-call(s32[3]{0:T(128)S(1)} %pad_add_fusion.1.index_ref, bf16[4,96,320]{2,1,0:T(8,128)(2,1)} %all-to-all-done.1.refs_0_, bf16[320,320]{1,0:T(8,128)(2,1)S(1)} %copy-done, bf16[320,320]{1,0:T(8,128)(2,1)S(1)} %collective-permute-done.1.refs_2_, bf16[320,320]{1,0:T(8,128)(2,1)S(1)} %copy-done.3, ...), custom_call_target="tpu_custom_call" | custom-call | tf_op jit(solution)/shard_map/project1/pallas_call | solution.py:281
  73.1 1.6 %collective-permute-start.20 = (bf16[96,1280]{1,0:T(8,128)(2,1)S(1)}, bf16[96,1280]{1,0:T(8,128)(2,1)S(1)}, u32[]{:S(2)}, u32[]{:S(2)}) collective-permute-start(bf16[96,1280]{1,0:T(8,128)(2,1)S(1)} %project1.1.refs_5_), channel_id=1, source_target_pairs={{0,8},{4,12},{8,0},{12,4},{1,9},{5,13},{9,1},{13,5},{2,10},{6,14},... | collective-permute-start | bytes 737288 | tf_op jit(solution)/shard_map/ppermute | solution.py:26
  75.2 3.2 %collective-permute-done.19.refs_8_ = bf16[96,1280]{1,0:T(8,128)(2,1)} collective-permute-done((bf16[96,1280]{1,0:T(8,128)(2,1)}, bf16[96,1280]{1,0:T(8,128)(2,1)}, u32[]{:S(2)}, u32[]{:S(2)}) %collective-permute-start.19) | collective-permute-done | bytes 245792 | tf_op jit(solution)/shard_map/ppermute | solution.py:26
  78.5 4.4 %collective-permute-done.20.refs_9_ = bf16[96,1280]{1,0:T(8,128)(2,1)S(1)} collective-permute-done((bf16[96,1280]{1,0:T(8,128)(2,1)S(1)}, bf16[96,1280]{1,0:T(8,128)(2,1)S(1)}, u32[]{:S(2)}, u32[]{:S(2)}) %collective-permute-start.20) | collective-permute-done | bytes 245792 | tf_op jit(solution)/shard_map/ppermute | solution.py:26
  82.9 1.5 %collective-permute-done.22.refs_11_ = bf16[96,1280]{1,0:T(8,128)(2,1)S(1)} collective-permute-done((bf16[96,1280]{1,0:T(8,128)(2,1)S(1)}, bf16[96,1280]{1,0:T(8,128)(2,1)S(1)}, u32[]{:S(2)}, u32[]{:S(2)}) %collective-permute-start.22) | collective-permute-done | bytes 245792 | tf_op jit(solution)/shard_map/ppermute | solution.py:26
  84.4 3.1 %placement.1 = bf16[192,1280]{1,0:T(8,128)(2,1)} custom-call(s32[3]{0:T(128)S(1)} %pad_add_fusion.1.index_ref, s32[1,192]{1,0:T(1,128)S(1)} %bitcast.36, s32[1,192]{1,0:T(1,128)S(1)} %get-tuple-element.62.refs_1_, s32[1,192]{1,0:T(1,128)S(1)} %collective-permute-done.11.refs_2_, s32[1,192]{1,0:T(1,128)S(1)} %get-tuple-element.61.refs_3_, ...), custom_call_target="tpu_custom_call" | custom-call | tf_op jit(solution)/shard_map/placement/pallas_call | solution.py:294
  (72 shorter events, 7.2 us)
Async XLA Ops:
  0.0 21.3 %copy-start = (bf16[320,320]{1,0:T(8,128)(2,1)S(1)}, bf16[320,320]{1,0:T(8,128)(2,1)}, u32[]{:S(2)}) copy-start(bf16[320,320]{1,0:T(8,128)(2,1)} %refs_1_.1) | copy-start | bytes 614404
  0.0 19.8 %collective-permute-start.2 = (bf16[3,320,320]{2,1,0:T(8,128)(2,1)}, bf16[3,320,320]{2,1,0:T(8,128)(2,1)}, u32[]{:S(2)}, u32[]{:S(2)}) collective-permute-start(bf16[3,320,320]{2,1,0:T(8,128)(2,1)} %bitcast.29), channel_id=1, source_target_pairs={{0,4},{4,0},{8,12},{12,8},{1,5},{5,1},{9,13},{13,9},{2,6},{6,2},{1... | collective-permute-start | bytes 1843208 | tf_op jit(solution)/shard_map/ppermute | solution.py:26
  0.5 29.9 %copy-start.17 = (s32[192]{0:T(256)S(1)}, s32[192]{0:T(256)}, u32[]{:S(2)}) copy-start(s32[192]{0:T(256)} %param.9) | copy-start | bytes 2308
  0.5 30.4 %copy-start.9 = (bf16[320,3,320]{2,0,1:T(8,128)(2,1)S(1)}, bf16[320,3,320]{2,0,1:T(8,128)(2,1)}, u32[]{:S(2)}) copy-start(bf16[320,3,320]{2,0,1:T(8,128)(2,1)} %param.11) | copy-start | bytes 1843204
  0.5 30.4 %copy-start.16 = (s32[768]{0:T(1024)S(1)}, s32[768]{0:T(1024)}, u32[]{:S(2)}) copy-start(s32[768]{0:T(1024)} %param.8) | copy-start | bytes 9220
  3.9 11.1 %collective-permute-start = (bf16[320,320]{1,0:T(8,128)(2,1)}, bf16[320,320]{1,0:T(8,128)(2,1)}, u32[]{:S(2)}, u32[]{:S(2)}) collective-permute-start(bf16[320,320]{1,0:T(8,128)(2,1)} %dynamic-slice_bitcast_fusion), channel_id=1, source_target_pairs={{0,8},{4,12},{8,0},{12,4},{1,9},{5,13},{9,1},{13,5},{2,10},{6,14},... | collective-permute-start | bytes 614408 | tf_op jit(solution)/shard_map/ppermute | solution.py:26
  6.4 13.4 %collective-permute-start.1 = (bf16[320,320]{1,0:T(8,128)(2,1)}, bf16[320,320]{1,0:T(8,128)(2,1)S(1)}, u32[]{:S(2)}, u32[]{:S(2)}) collective-permute-start(bf16[320,320]{1,0:T(8,128)(2,1)} %refs_1_.1), channel_id=1, source_target_pairs={{0,1},{1,0},{2,3},{3,2},{4,5},{5,4},{6,7},{7,6},{8,9},{9,8},{10,11... | collective-permute-start | bytes 614408 | tf_op jit(solution)/shard_map/ppermute | solution.py:26
  8.0 14.2 %collective-permute-start.6 = (bf16[320,320]{1,0:T(8,128)(2,1)}, bf16[320,320]{1,0:T(8,128)(2,1)S(1)}, u32[]{:S(2)}, u32[]{:S(2)}) collective-permute-start(bf16[320,320]{1,0:T(8,128)(2,1)} %refs_1_.1), channel_id=1, source_target_pairs={{0,2},{1,3},{2,0},{3,1},{4,6},{5,7},{6,4},{7,5},{8,10},{9,11},{10,... | collective-permute-start | bytes 614408 | tf_op jit(solution)/shard_map/ppermute | solution.py:26
  10.6 11.4 %collective-permute-start.4 = (bf16[320,320]{1,0:T(8,128)(2,1)}, bf16[320,320]{1,0:T(8,128)(2,1)}, u32[]{:S(2)}, u32[]{:S(2)}) collective-permute-start(bf16[320,320]{1,0:T(8,128)(2,1)} %slice_bitcast_fusion), channel_id=1, source_target_pairs={{0,8},{4,12},{8,0},{12,4},{1,9},{5,13},{9,1},{13,5},{2,10},{6,14},... | collective-permute-start | bytes 614408 | tf_op jit(solution)/shard_map/ppermute | solution.py:26
  14.9 15.9 %copy-start.11 = (bf16[192,1280]{1,0:T(8,128)(2,1)}, bf16[192,1280]{1,0:T(8,128)(2,1)S(1)}, u32[]{:S(2)}) copy-start(bf16[192,1280]{1,0:T(8,128)(2,1)S(1)} %get-tuple-element.58.refs_10_) | copy-start | bytes 1474564
  19.8 7.4 %collective-permute-start.3 = (bf16[320,320]{1,0:T(8,128)(2,1)}, bf16[320,320]{1,0:T(8,128)(2,1)S(1)}, u32[]{:S(2)}, u32[]{:S(2)}) collective-permute-start(bf16[320,320]{1,0:T(8,128)(2,1)} %collective-permute-done.refs_2_), channel_id=1, source_target_pairs={{0,16},{16,0},{1,17},{17,1},{2,18},{18,2},{3,19},{19,3},{4,20},{20... | collective-permute-start | bytes 614408 | tf_op jit(solution)/shard_map/ppermute | solution.py:26
  21.3 6.0 %collective-permute-start.5 = (bf16[320,320]{1,0:T(8,128)(2,1)}, bf16[320,320]{1,0:T(8,128)(2,1)S(1)}, u32[]{:S(2)}, u32[]{:S(2)}) collective-permute-start(bf16[320,320]{1,0:T(8,128)(2,1)} %collective-permute-done.refs_2_), channel_id=1, source_target_pairs={{0,4},{4,0},{8,12},{12,8},{1,5},{5,1},{9,13},{13,9},{2,6},{6,2},{1... | collective-permute-start | bytes 614408 | tf_op jit(solution)/shard_map/ppermute | solution.py:26
  21.4 17.5 %collective-permute-start.10 = (bf16[2,320,320]{2,1,0:T(8,128)(2,1)S(1)}, bf16[2,320,320]{2,1,0:T(8,128)(2,1)}, u32[]{:S(2)}, u32[]{:S(2)}) collective-permute-start(bf16[2,320,320]{2,1,0:T(8,128)(2,1)S(1)} %pad_maximum_fusion.1), channel_id=1, source_target_pairs={{0,8},{4,12},{8,0},{12,4},{1,9},{5,13},{9,1},{13,5},{2,10},{6,14},... | collective-permute-start | bytes 1228808 | tf_op jit(solution)/shard_map/ppermute | solution.py:26
  22.2 16.8 %copy-start.1 = (bf16[320,320]{1,0:T(8,128)(2,1)}, bf16[320,320]{1,0:T(8,128)(2,1)S(1)}, u32[]{:S(2)}) copy-start(bf16[320,320]{1,0:T(8,128)(2,1)S(1)} %collective-permute-done.6.refs_3_) | copy-start | bytes 614404
  27.3 3.6 %collective-permute-start.7 = (bf16[320,320]{1,0:T(8,128)(2,1)S(1)}, bf16[320,320]{1,0:T(8,128)(2,1)S(1)}, u32[]{:S(2)}, u32[]{:S(2)}) collective-permute-start(bf16[320,320]{1,0:T(8,128)(2,1)S(1)} %collective-permute-done.3.refs_3_), channel_id=1, source_target_pairs={{0,4},{4,0},{8,12},{12,8},{1,5},{5,1},{9,13},{13,9},{2,6},{6,2},{1... | collective-permute-start | bytes 614408 | tf_op jit(solution)/shard_map/ppermute | solution.py:26
  27.3 3.6 %collective-permute-start.8 = (bf16[320,320]{1,0:T(8,128)(2,1)}, bf16[320,320]{1,0:T(8,128)(2,1)S(1)}, u32[]{:S(2)}, u32[]{:S(2)}) collective-permute-start(bf16[320,320]{1,0:T(8,128)(2,1)} %collective-permute-done.4.refs_4_), channel_id=1, source_target_pairs={{0,4},{4,0},{8,12},{12,8},{1,5},{5,1},{9,13},{13,9},{2,6},{6,2},{1... | collective-permute-start | bytes 614408 | tf_op jit(solution)/shard_map/ppermute | solution.py:26
  27.8 11.2 %collective-permute-start.9 = (bf16[320,320]{1,0:T(8,128)(2,1)S(1)}, bf16[320,320]{1,0:T(8,128)(2,1)S(1)}, u32[]{:S(2)}, u32[]{:S(2)}) collective-permute-start(bf16[320,320]{1,0:T(8,128)(2,1)S(1)} %copy-done), channel_id=1, source_target_pairs={{0,3},{1,2},{2,1},{3,0},{4,7},{5,6},{6,5},{7,4},{8,11},{9,10},{10,... | collective-permute-start | bytes 614408 | tf_op jit(solution)/shard_map/ppermute | solution.py:26
  30.4 8.6 %collective-permute-start.11 = (s32[1,192]{1,0:T(1,128)S(1)}, s32[1,192]{1,0:T(1,128)S(1)}, u32[]{:S(2)}, u32[]{:S(2)}) collective-permute-start(s32[1,192]{1,0:T(1,128)S(1)} %bitcast.34), channel_id=1, source_target_pairs={{0,8},{4,12},{8,0},{12,4},{1,9},{5,13},{9,1},{13,5},{2,10},{6,14},... | collective-permute-start | bytes 2312 | tf_op jit(solution)/shard_map/ppermute | solution.py:26
  40.2 15.8 %collective-permute-start.13 = (bf16[4,320,320]{2,1,0:T(8,128)(2,1)}, bf16[4,320,320]{2,1,0:T(8,128)(2,1)S(1)}, u32[]{:S(2)}, u32[]{:S(2)}) collective-permute-start(bf16[4,320,320]{2,1,0:T(8,128)(2,1)} %pad_maximum_fusion), channel_id=1, source_target_pairs={{0,4},{4,0},{8,12},{12,8},{1,5},{5,1},{9,13},{13,9},{2,6},{6,2},{1... | collective-permute-start | bytes 2457608 | tf_op jit(solution)/shard_map/ppermute | solution.py:26
  42.0 13.9 %collective-permute-start.14 = (bf16[2,320,320]{2,1,0:T(8,128)(2,1)}, bf16[2,320,320]{2,1,0:T(8,128)(2,1)}, u32[]{:S(2)}, u32[]{:S(2)}) collective-permute-start(bf16[2,320,320]{2,1,0:T(8,128)(2,1)} %pad_maximum_fusion.2), channel_id=1, source_target_pairs={{0,8},{4,12},{8,0},{12,4},{1,9},{5,13},{9,1},{13,5},{2,10},{6,14},... | collective-permute-start | bytes 1228808 | tf_op jit(solution)/shard_map/ppermute | solution.py:26
  43.5 14.4 %all-to-all-start = ((bf16[4,96,320]{2,1,0:T(8,128)(2,1)}), bf16[4,96,320]{2,1,0:T(8,128)(2,1)}, u32[]{:S(2)}, u32[]{:S(2)}) async-start(bf16[4,96,320]{2,1,0:T(8,128)(2,1)} %copy-done.15), calls=%async_computation | async-start | bytes 589824 | tf_op jit(solution)/shard_map/all_to_all | solution.py:253
  49.4 12.7 %copy-start.18 = (f32[1280]{0:T(1024)S(1)}, f32[1280]{0:T(1024)}, u32[]{:S(2)}) copy-start(f32[1280]{0:T(1024)} %param.13) | copy-start | bytes 15364
  55.9 7.3 %collective-permute-start.16 = (bf16[2,320,320]{2,1,0:T(8,128)(2,1)}, bf16[2,320,320]{2,1,0:T(8,128)(2,1)S(1)}, u32[]{:S(2)}, u32[]{:S(2)}) collective-permute-start(bf16[2,320,320]{2,1,0:T(8,128)(2,1)} %collective-permute-done.14.refs_7_), channel_id=1, source_target_pairs={{0,4},{4,0},{8,12},{12,8},{1,5},{5,1},{9,13},{13,9},{2,6},{6,2},{1... | collective-permute-start | bytes 1228808 | tf_op jit(solution)/shard_map/ppermute | solution.py:26
  55.9 7.3 %collective-permute-start.15 = (bf16[2,320,320]{2,1,0:T(8,128)(2,1)}, bf16[2,320,320]{2,1,0:T(8,128)(2,1)S(1)}, u32[]{:S(2)}, u32[]{:S(2)}) collective-permute-start(bf16[2,320,320]{2,1,0:T(8,128)(2,1)} %collective-permute-done.10.refs_6_), channel_id=1, source_target_pairs={{0,4},{4,0},{8,12},{12,8},{1,5},{5,1},{9,13},{13,9},{2,6},{6,2},{1... | collective-permute-start | bytes 1228808 | tf_op jit(solution)/shard_map/ppermute | solution.py:26
  57.9 12.8 %all-to-all-start.1 = ((bf16[4,96,320]{2,1,0:T(8,128)(2,1)}), bf16[4,96,320]{2,1,0:T(8,128)(2,1)}, u32[]{:S(2)}, u32[]{:S(2)}) async-start(bf16[4,96,320]{2,1,0:T(8,128)(2,1)} %copy-done.14), calls=%async_computation.1 | async-start | bytes 589824 | tf_op jit(solution)/shard_map/all_to_all | solution.py:253
  62.0 1.2 %collective-permute-start.12 = (s32[2,1,192]{2,1,0:T(1,128)S(1)}, s32[2,1,192]{2,1,0:T(1,128)S(1)}, u32[]{:S(2)}, u32[]{:S(2)}) collective-permute-start(s32[2,1,192]{2,1,0:T(1,128)S(1)} %pad_add_fusion), channel_id=1, source_target_pairs={{0,4},{4,0},{8,12},{12,8},{1,5},{5,1},{9,13},{13,9},{2,6},{6,2},{1... | collective-permute-start | bytes 4616 | tf_op jit(solution)/shard_map/ppermute | solution.py:26
  69.3 9.1 %collective-permute-start.19 = (bf16[96,1280]{1,0:T(8,128)(2,1)}, bf16[96,1280]{1,0:T(8,128)(2,1)}, u32[]{:S(2)}, u32[]{:S(2)}) collective-permute-start(bf16[96,1280]{1,0:T(8,128)(2,1)} %project0.1.refs_4_), channel_id=1, source_target_pairs={{0,8},{4,12},{8,0},{12,4},{1,9},{5,13},{9,1},{13,5},{2,10},{6,14},... | collective-permute-start | bytes 737288 | tf_op jit(solution)/shard_map/ppermute | solution.py:26
  73.1 9.8 %collective-permute-start.20 = (bf16[96,1280]{1,0:T(8,128)(2,1)S(1)}, bf16[96,1280]{1,0:T(8,128)(2,1)S(1)}, u32[]{:S(2)}, u32[]{:S(2)}) collective-permute-start(bf16[96,1280]{1,0:T(8,128)(2,1)S(1)} %project1.1.refs_5_), channel_id=1, source_target_pairs={{0,8},{4,12},{8,0},{12,4},{1,9},{5,13},{9,1},{13,5},{2,10},{6,14},... | collective-permute-start | bytes 737288 | tf_op jit(solution)/shard_map/ppermute | solution.py:26
  74.7 8.1 %collective-permute-start.17 = (bf16[96,1280]{1,0:T(8,128)(2,1)}, bf16[96,1280]{1,0:T(8,128)(2,1)S(1)}, u32[]{:S(2)}, u32[]{:S(2)}) collective-permute-start(bf16[96,1280]{1,0:T(8,128)(2,1)} %project0.1.refs_4_), channel_id=1, source_target_pairs={{0,4},{4,0},{8,12},{12,8},{1,5},{5,1},{9,13},{13,9},{2,6},{6,2},{1... | collective-permute-start | bytes 737288 | tf_op jit(solution)/shard_map/ppermute | solution.py:26
  74.7 8.1 %collective-permute-start.18 = (bf16[96,1280]{1,0:T(8,128)(2,1)S(1)}, bf16[96,1280]{1,0:T(8,128)(2,1)S(1)}, u32[]{:S(2)}, u32[]{:S(2)}) collective-permute-start(bf16[96,1280]{1,0:T(8,128)(2,1)S(1)} %project1.1.refs_5_), channel_id=1, source_target_pairs={{0,4},{4,0},{8,12},{12,8},{1,5},{5,1},{9,13},{13,9},{2,6},{6,2},{1... | collective-permute-start | bytes 737288 | tf_op jit(solution)/shard_map/ppermute | solution.py:26
  78.5 4.4 %collective-permute-start.21 = (bf16[96,1280]{1,0:T(8,128)(2,1)}, bf16[96,1280]{1,0:T(8,128)(2,1)S(1)}, u32[]{:S(2)}, u32[]{:S(2)}) collective-permute-start(bf16[96,1280]{1,0:T(8,128)(2,1)} %collective-permute-done.19.refs_8_), channel_id=1, source_target_pairs={{0,4},{4,0},{8,12},{12,8},{1,5},{5,1},{9,13},{13,9},{2,6},{6,2},{1... | collective-permute-start | bytes 737288 | tf_op jit(solution)/shard_map/ppermute | solution.py:26
  82.8 1.5 %collective-permute-start.22 = (bf16[96,1280]{1,0:T(8,128)(2,1)S(1)}, bf16[96,1280]{1,0:T(8,128)(2,1)S(1)}, u32[]{:S(2)}, u32[]{:S(2)}) collective-permute-start(bf16[96,1280]{1,0:T(8,128)(2,1)S(1)} %collective-permute-done.20.refs_9_), channel_id=1, source_target_pairs={{0,4},{4,0},{8,12},{12,8},{1,5},{5,1},{9,13},{13,9},{2,6},{6,2},{1... | collective-permute-start | bytes 737288 | tf_op jit(solution)/shard_map/ppermute | solution.py:26
  (12 other events, 28.9 us)

commit v5 on v3

v5 whole, which is shorter than its diff:
```python
import functools

import jax
import jax.numpy as jnp
from jax import lax
from jax.experimental import pallas as pl
from jax.experimental.pallas import tpu as pltpu
from jax.sharding import PartitionSpec as P

HD = 80
WIN = 64
PAIR = 2 * WIN
LANES = 128
CHUNKS = 2
F32 = jnp.float32
BF16 = jnp.bfloat16
VMEM = pl.BlockSpec(memory_space=pltpu.VMEM)
SMEM = pl.BlockSpec(memory_space=pltpu.SMEM)


def params(mib):
    return pltpu.CompilerParams(vmem_limit_bytes=mib * 1024 * 1024)


def swap(x, axis, size, bit):
    return lax.ppermute(x, axis, [(i, i ^ bit) for i in range(size)])


def cross_keys(size):
    return range(2, size, 2)


def gather_cross(x, size):
    blocks = {0: x}
    bit = size // 2
    while bit > 1:
        for key in list(blocks):
            blocks[key ^ bit] = swap(blocks[key], "context", size, bit)
        bit //= 2
    return blocks


def gather_xor(x, size):
    blocks = gather_cross(x, size)
    for key in list(blocks):
        blocks[key ^ 1] = swap(blocks[key], "context", size, 1)
    return blocks


def together(*values):
    return lax.optimization_barrier(values)


def one_hot(mask):
    return mask.astype(F32).astype(BF16)


def shape(*dims):
    return jax.ShapeDtypeStruct(dims, BF16)


def packs(rows, cols):
    return rows % 32 == 0 and cols == 2 * LANES + LANES // 2


def packed_shape(rows, cols):
    return (rows * 5 // 2, LANES) if packs(rows, cols) else (rows, cols)


def pack(x):
    rows, cols = x.shape
    if not packs(rows, cols):
        return x
    rest = x[:, 2 * LANES :]
    tail = jnp.concatenate([rest[: rows // 2], rest[rows // 2 :]], axis=1)
    return jnp.concatenate([x[:, :LANES], x[:, LANES : 2 * LANES], tail], axis=0)


def unpack(p, rows, cols):
    if not packs(rows, cols):
        return p[:, : 2 * LANES], p[:, 2 * LANES :]
    tail = p[2 * rows :]
    rest = jnp.concatenate([tail[:, : LANES // 2], tail[:, LANES // 2 :]], axis=0)
    return jnp.concatenate([p[:rows], p[rows : 2 * rows]], axis=1), rest


def pack_kernel(index_ref, qkv_ref, proj_ref, first_ref, value_ref, all_ref, proj_out_ref):
    for j in range(3):
        all_ref[j] = pack(qkv_ref[j])
    first_ref[...] = all_ref[index_ref[2]]
    value_ref[...] = all_ref[2]
    proj_out_ref[...] = pack(proj_ref[...])


def norm_kernel(index_ref, patches_ref, gain_ref, hidden_ref, own_ref):
    rows = patches_ref.shape[0]
    x = patches_ref[...]
    xf = x.astype(F32)
    mean_sq = jnp.mean(xf * xf, axis=-1, keepdims=True)
    hidden_ref[...] = (xf * lax.rsqrt(mean_sq + 1e-06) * gain_ref[...]).astype(BF16)
    step = 256
    pick = step // 4
    row = lax.broadcasted_iota(jnp.int32, (pick, step), 0)
    col = lax.broadcasted_iota(jnp.int32, (pick, step), 1)
    chosen = one_hot(col == 4 * row + index_ref[1])
    for i in range(rows // step):
        own_ref[i * pick : (i + 1) * pick, :] = jnp.dot(
            chosen, x[i * step : (i + 1) * step], preferred_element_type=F32
        ).astype(BF16)


def attend(row0, index_ref, hidden_ref, valid_ref, w_ref, out_refs, q_ref, k_ref, v_ref, mix_ref):
    rows, width = q_ref.shape
    heads = width // HD
    main = 2 * LANES
    rest = width - main
    qkv = jnp.dot(hidden_ref[row0 : row0 + rows, :], w_ref[...], preferred_element_type=F32)
    for j, ref in enumerate((q_ref, k_ref, v_ref)):
        ref[:, :main] = qkv[:, j * main : (j + 1) * main].astype(BF16)
        at = 3 * main + j * rest
        ref[:, main:] = qkv[:, at : at + rest].astype(BF16)
    lane = lax.broadcasted_iota(jnp.int32, (1, width), 1)
    head_masks = [one_hot((lane >= h * HD) & (lane < (h + 1) * HD)) for h in range(heads)]
    q_win = lax.broadcasted_iota(jnp.int32, (PAIR, PAIR), 0) // WIN
    k_win = lax.broadcasted_iota(jnp.int32, (PAIR, PAIR), 1) // WIN
    same = q_win == k_win
    floor = jnp.where(same, F32(-1e30), F32(-3e38))
    pick = PAIR // 4
    src = lax.broadcasted_iota(jnp.int32, (PAIR, PAIR), 1)
    dst = lax.broadcasted_iota(jnp.int32, (PAIR, PAIR), 0)
    order = one_hot(src == 4 * (dst % pick) + dst // pick)
    for p in range(rows // PAIR):
        at = p * PAIR
        q = q_ref[at : at + PAIR, :]
        k = k_ref[at : at + PAIR, :]
        v = v_ref[at : at + PAIR, :]
        k_all = jnp.concatenate([k * m for m in head_masks], axis=0)
        v_all = jnp.concatenate([v * m for m in head_masks], axis=0)
        scores = lax.dot_general(q, k_all, (((1,), (1,)), ((), ())), preferred_element_type=F32)
        live = valid_ref[row0 // PAIR + p : row0 // PAIR + p + 1, :] > 0
        weights = []
        for h in range(heads):
            s = scores[:, h * PAIR : (h + 1) * PAIR] * F32(HD ** (-0.5))
            s = jnp.where(same & live, s, floor)
            e = jnp.exp(s - jnp.max(s, axis=-1, keepdims=True))
            weights.append((e / jnp.sum(e, axis=-1, keepdims=True)).astype(BF16))
        w_all = jnp.concatenate(weights, axis=1)
        mixed = jnp.dot(w_all, v_all, preferred_element_type=F32).astype(BF16)
        mixed = jnp.dot(order, mixed, preferred_element_type=F32).astype(BF16)
        for t in range(4):
            mix_ref[t, p * pick : (p + 1) * pick, :] = mixed[t * pick : (t + 1) * pick]
    for s, out_ref in enumerate(out_refs):
        out_ref[...] = pack(mix_ref[index_ref[1] ^ s])


def first_attention_kernel(n_ctx, width, index_ref, hidden_ref, valid_ref, *refs):
    shards = list(refs[: 2 + 3 * (n_ctx - 2)])
    *out_refs, w_ref, q_ref, k_ref, v_ref, mix_ref = refs[len(shards) :]
    depth = w_ref.shape[0] // n_ctx
    me = index_ref[0]
    flip = index_ref[2] > 0
    main = 2 * LANES
    for key in range(n_ctx):
        rows = pl.ds(pl.multiple_of((me ^ key) * depth, depth), depth)
        if key < 2:
            block = shards.pop(0)
            thirds = [block[j] for j in range(3)]
        else:
            first, second, value = [shards.pop(0)[...] for _ in range(3)]
            thirds = [jnp.where(flip, second, first), jnp.where(flip, first, second), value]
        tails = []
        for j, third in enumerate(thirds):
            w_ref[rows, j * main : (j + 1) * main], tail = unpack(third, depth, width)
            tails.append(tail)
        w_ref[rows, 3 * main :] = jnp.concatenate(tails, axis=1)
    attend(0, index_ref, hidden_ref, valid_ref, w_ref, out_refs, q_ref, k_ref, v_ref, mix_ref)


def next_attention_kernel(row0, index_ref, hidden_ref, valid_ref, w_ref, *refs):
    *out_refs, q_ref, k_ref, v_ref, mix_ref = refs
    attend(row0, index_ref, hidden_ref, valid_ref, w_ref, out_refs, q_ref, k_ref, v_ref, mix_ref)


def project_kernel(n_ctx, row0, width, col, index_ref, *refs):
    mixes = [unpack(m[...], refs[-2].shape[0], width) for m in refs[:4]]
    *blocks, own_ref, gain_ref, out_ref, part_ref = refs[4:]
    rows = out_ref.shape[0]
    me = index_ref[0]
    main = 2 * LANES
    mixed = jnp.concatenate([m for m, _ in mixes] + [r for _, r in mixes], axis=1)
    mains = []
    rests = []
    for key in range(n_ctx):
        pieces = []
        for ref in [blocks.pop(0) for _ in range((4, 1)[key] if key < 2 else 2)]:
            pieces += [ref[...]] if len(ref.shape) == 2 else [ref[i] for i in range(ref.shape[0])]
        halves = [unpack(p, width, col) for p in pieces]
        both = []
        for half in ([h[0] for h in halves], [h[1] for h in halves]):
            both.append(jnp.concatenate([h[:main] for h in half] + [h[main:] for h in half], axis=0))
        mains.append(jnp.dot(mixed, both[0], preferred_element_type=F32))
        rests.append(both[1])
    if rests[0].shape[1]:
        rest = jnp.dot(mixed, jnp.concatenate(rests, axis=1), preferred_element_type=F32)
        count = rests[0].shape[1]
        mains = [
            jnp.concatenate([m, rest[:, key * count : (key + 1) * count]], axis=1)
            for key, m in enumerate(mains)
        ]
    for key in range(n_ctx):
        part_ref[me ^ key] = mains[key]
    total = jnp.concatenate([part_ref[i] for i in range(n_ctx)], axis=1)
    total = total + own_ref[row0 : row0 + rows, :].astype(F32)
    mean_sq = jnp.mean(total * total, axis=-1, keepdims=True)
    out_ref[...] = (total * lax.rsqrt(mean_sq + 1e-06) * gain_ref[...]).astype(BF16)


def place_kernel(n_ctx, index_ref, *refs):
    place_refs = refs[:n_ctx]
    row_refs = refs[n_ctx:-1]
    out_ref = refs[-1]
    spots = out_ref.shape[0]
    chosen = []
    for place_ref in place_refs:
        target = place_ref[...] - index_ref[0] * spots
        grid = lax.broadcasted_iota(jnp.int32, (spots, target.shape[1]), 0)
        chosen.append(one_hot(grid == target))
    out_ref[...] = jnp.dot(
        jnp.concatenate(chosen, axis=1),
        jnp.concatenate([ref[...] for ref in row_refs], axis=0),
        preferred_element_type=F32,
    ).astype(BF16)


def local(n_dp, n_ctx, n_ten, patches, valid, place, gain_attn, w_qkv, w_proj, gain_merge):
    rows, feat = patches.shape
    depth, _, width = w_qkv.shape
    col = w_proj.shape[1]
    groups = rows // 4
    ten = lax.axis_index("tensor")
    half = lax.axis_index("dp") % 2
    index = jnp.stack([lax.axis_index("context"), ten, half]).astype(jnp.int32)
    cross = list(cross_keys(n_ctx))

    def over_dp(x):
        return swap(x, "dp", n_dp, 1)

    def over_core(x):
        return swap(x, "context", n_ctx, 1)

    third = packed_shape(depth, width)
    piece = packed_shape(width, col)
    first, value, own, w_proj = pl.pallas_call(
        pack_kernel,
        out_shape=(shape(*third), shape(*third), shape(3, *third), shape(*piece)),
        in_specs=[SMEM, VMEM, VMEM],
        out_specs=(VMEM,) * 4,
        compiler_params=params(8),
        name="pack",
    )(index, jnp.transpose(w_qkv, (1, 0, 2)), w_proj)
    first = gather_cross(first, n_ctx)
    value = gather_cross(value, n_ctx)
    twin = over_core(own)
    by_one = swap(w_proj, "tensor", n_ten, 1)
    by_two = swap(w_proj, "tensor", n_ten, 2)
    hidden, own_patches = pl.pallas_call(
        norm_kernel,
        out_shape=(shape(rows, feat), shape(groups, feat)),
        in_specs=[SMEM, VMEM, VMEM],
        out_specs=(VMEM, VMEM),
        compiler_params=params(16),
        name="norm",
    )(index, patches, gain_attn.reshape(1, feat))
    first, twin, hidden = together(first, twin, hidden)

    second = {k: over_dp(first[k]) for k in cross}
    first_twin = {k: over_core(first[k]) for k in cross}
    by_one, first = together(by_one, first)
    low = gather_cross(jnp.stack([w_proj, by_one]), n_ctx)
    second, value, first_twin = together(second, value, first_twin)

    second_twin = {k: over_core(second[k]) for k in cross}
    value_twin = {k: over_core(value[k]) for k in cross}
    by_two, w_proj, place = together(by_two, w_proj, place, second, value)[:3]
    by_three = swap(w_proj, "tensor", n_ten, 3)
    places = gather_cross(place.reshape(1, groups), n_ctx)

    shard_list = [own, twin]
    for k in cross:
        shard_list += [first[k], second[k], value[k], first_twin[k], second_twin[k], value_twin[k]]

    valid_pairs = valid.reshape(rows // PAIR, PAIR)
    part = rows // CHUNKS
    gain2 = gain_merge.reshape(1, feat)
    mix_shapes = (shape(*packed_shape(part // 4, width)),) * n_ten
    scratch = [pltpu.VMEM((part, width), BF16)] * 3 + [pltpu.VMEM((4, part // 4, width), BF16)]
    *mixed, w_full = pl.pallas_call(
        functools.partial(first_attention_kernel, n_ctx, width),
        out_shape=mix_shapes + (shape(feat, 3 * width),),
        in_specs=[SMEM] + [VMEM] * (2 + len(shard_list)),
        out_specs=(VMEM,) * (n_ten + 1),
        scratch_shapes=scratch,
        compiler_params=params(16),
        name="attention0",
    )(index, hidden, valid_pairs, *shard_list)

    def exchange(pieces):
        return [pieces[0]] + [swap(pieces[s], "tensor", n_ten, s) for s in range(1, n_ten)]

    mixed, by_three, low, places = together(mixed, by_three, low, places)
    received = [exchange(mixed)]
    high = gather_cross(jnp.stack([by_two, by_three]), n_ctx)
    own_twin = over_core(jnp.stack([w_proj, by_one, by_two, by_three]))
    place_twin = over_core(jnp.stack([places[k] for k in (0, *cross)]))
    for r in range(1, CHUNKS):
        received[r - 1][1], hidden = together(received[r - 1][1], hidden)
        mixed = pl.pallas_call(
            functools.partial(next_attention_kernel, r * part),
            out_shape=mix_shapes,
            in_specs=[SMEM, VMEM, VMEM, VMEM],
            out_specs=(VMEM,) * n_ten,
            scratch_shapes=scratch,
            compiler_params=params(12),
            name="attention" + str(r),
        )(index, hidden, valid_pairs, w_full)
        mixed, received[r - 1], own_twin, low = together(mixed, received[r - 1], own_twin, low)
        received.append(exchange(mixed))
    high, received[-1][1], place_twin = together(high, received[-1][1], place_twin)

    blocks = [w_proj, by_one, by_two, by_three, own_twin]
    for k in cross:
        blocks += [low[k], high[k], over_core(low[k]), over_core(high[k])]
    gathered = []
    for r in range(CHUNKS):
        if r > 0:
            received[r], done = together(received[r], done)
        done = pl.pallas_call(
            functools.partial(project_kernel, n_ctx, r * (part // 4), width, col),
            out_shape=shape(part // 4, feat),
            in_specs=[SMEM] + [VMEM] * (n_ten + len(blocks) + 2),
            out_specs=VMEM,
            scratch_shapes=[pltpu.VMEM((n_ctx, part // 4, col), F32)],
            compiler_params=params(20),
            name="project" + str(r),
        )(index, *received[r], *blocks, own_patches, gain2)
        gathered.append(gather_xor(done, n_ctx))
    place_list = []
    for i, k in enumerate((0, *cross)):
        place_list += [places[k], place_twin[i]]
    return pl.pallas_call(
        functools.partial(place_kernel, n_ctx),
        out_shape=shape(groups, feat),
        in_specs=[SMEM] + [VMEM] * (n_ctx + n_ctx * CHUNKS),
        out_specs=VMEM,
        compiler_params=params(28),
        name="placement",
    )(index, *place_list, *[gathered[r][k] for k in range(n_ctx) for r in range(CHUNKS)])


def solution(mesh):
    in_specs = (
        P(("dp", "context"), None),
        P(("dp", "context")),
        P(("dp", "context")),
        P(),
        P("context", None, "tensor"),
        P("tensor", "context"),
        P(),
    )
    out_specs = P(("dp", "context"), "tensor")
    sizes = [mesh.shape[name] for name in ("dp", "context", "tensor")]
    body = functools.partial(local, *sizes)
    return jax.shard_map(body, mesh=mesh, in_specs=in_specs, out_specs=out_specs, check_vma=False)
```

time: 76.5 us -> 69.2 us (0.905)
  local copies, waits for them, and re-layouts: 9.4 us -> 4.32 us
  other arithmetic: 1.28 us -> 0.27 us
  starting transfers between devices: 28.6 us -> 27.6 us
  waiting for transfers between devices: 19.7 us -> 20.7 us
  Pallas kernels: 16.9 us -> 15.9 us
    squeeze x4 -> x0, local copies, waits for them, and re-layouts: 3.43 us -> none  [the longest x1 1.69 us: local(): lax.dynamic_index_in_dim(w3, half, 0, keepdims=False)]
    unnamed x20 -> x12, local copies, waits for them, and re-layouts: 5.26 us -> 3.62 us
    pallas_call x5 -> x6, Pallas kernels: 13.6 us -> 12 us  [the longest x1 4.51 us: local(): pl.pallas_call(functools.partial(first_attention_kernel, n_ctx, width), o...]
    ppermute x29, waiting for transfers between devices: 19.7 us -> 20.7 us  [swap(): return lax.ppermute(x, axis, [(i, i ^ bit) for i in range(size)])]
    ppermute x29, starting transfers between devices: 28.6 us -> 27.6 us  [swap(): return lax.ppermute(x, axis, [(i, i ^ bit) for i in range(size)])]
    another operation x1, other arithmetic: 0.87 us -> 0.04 us  [local(): low = gather_cross(jnp.stack([w_proj, by_one]), n_ctx)]
  transfers between devices with their start and end apart: 29 -> 29, of which waited for: 11 -> 10; matrix products, arithmetic and copies ran while one was open for 7% -> 1% of each run, Pallas kernels for 19% -> 19%
where the time goes in v5:
time: 69.2 us; the launch traced here: 69 us
  starting transfers between devices  27.6 us (40%)
  waiting for transfers between devices  20.7 us (30%)
  Pallas kernels  15.9 us (23%)
  local copies, waits for them, and re-layouts  4.32 us (6%)
    ppermute x29, starting transfers between devices, swap(): return lax.ppermute(x, axis, [(i, i ^ bit) for i in range(size)])  27.6 us
    ppermute x29, waiting for transfers between devices, swap(): return lax.ppermute(x, axis, [(i, i ^ bit) for i in range(size)])  20.7 us
    pallas_call x1, Pallas kernels, local(): pl.pallas_call(functools.partial(first_attention_kernel, n_ctx, width), o...  4.51 us
    pallas_call x1, Pallas kernels, local(): pl.pallas_call(functools.partial(next_attention_kernel, r * part), out_sh...  3.97 us
    unnamed x12, local copies, waits for them, and re-layouts  3.62 us
    pallas_call x2, Pallas kernels, local(): pl.pallas_call(functools.partial(project_kernel, n_ctx, r * (part // 4),...  3.27 us
    pallas_call x1, Pallas kernels, local(): pl.pallas_call(functools.partial(place_kernel, n_ctx), out_shape=shape(gr...  1.92 us
    pallas_call x1, Pallas kernels, local(): pl.pallas_call(norm_kernel, out_shape=(shape(rows, feat), shape(groups, f...  1.57 us
  transfers between devices with their start and end apart: 29, of which 10 were waited for; matrix products, arithmetic and copies ran while one was open for 1% of the time, Pallas kernels for 19%

profile of v5, /device:TPU:0, one launch (start us, length us, event | category | flops | bytes accessed | tf_op | source)
XLA Modules:
  0.0 69.0 jit_solution(8653650937033547469)
XLA Ops:
  0.1 1.1 %copy-done.1 = bf16[320,3,320]{2,0,1:T(8,128)(2,1)S(1)} copy-done((bf16[320,3,320]{2,0,1:T(8,128)(2,1)S(1)}, bf16[320,3,320]{2,0,1:T(8,128)(2,1)}, u32[]{:S(2)}) %copy-start.1) | copy-done | bytes 614424
  1.2 0.9 %copy-done.2 = bf16[320,320]{1,0:T(8,128)(2,1)S(1)} copy-done((bf16[320,320]{1,0:T(8,128)(2,1)S(1)}, bf16[320,320]{1,0:T(8,128)(2,1)}, u32[]{:S(2)}) %copy-start.2) | copy-done | bytes 204824
  2.1 0.7 %pack.1 = (bf16[800,128]{1,0:T(8,128)(2,1)S(1)}, bf16[800,128]{1,0:T(8,128)(2,1)S(1)}, bf16[3,800,128]{2,1,0:T(8,128)(2,1)S(1)}, bf16[800,128]{1,0:T(8,128)(2,1)S(1)}) custom-call(s32[3]{0:T(128)S(1)} %pad_add_fusion.1.index_ref, bf16[3,320,320]{2,1,0:T(8,128)(2,1)S(1)} %bitcast.25, bf16[320,320]{1,0:T(8,128)(2,1)S(1)} %copy-done.2), custom_call_target="tpu_custom_call" | custom-call | tf_op jit(solution)/shard_map/pack/pallas_call | solution.py:253
  3.4 2.6 %collective-permute-start = (bf16[800,128]{1,0:T(8,128)(2,1)S(1)}, bf16[800,128]{1,0:T(8,128)(2,1)S(1)}, u32[]{:S(2)}, u32[]{:S(2)}) collective-permute-start(bf16[800,128]{1,0:T(8,128)(2,1)S(1)} %get-tuple-element.58), channel_id=1, source_target_pairs={{0,8},{4,12},{8,0},{12,4},{1,9},{5,13},{9,1},{13,5},{2,10},{6,14},... | collective-permute-start | bytes 614408 | tf_op jit(solution)/shard_map/ppermute | solution.py:26
  6.0 1.6 %collective-permute-start.2 = (bf16[800,128]{1,0:T(8,128)(2,1)S(1)}, bf16[800,128]{1,0:T(8,128)(2,1)S(1)}, u32[]{:S(2)}, u32[]{:S(2)}) collective-permute-start(bf16[800,128]{1,0:T(8,128)(2,1)S(1)} %get-tuple-element.74.refs_4_), channel_id=1, source_target_pairs={{0,1},{1,0},{2,3},{3,2},{4,5},{5,4},{6,7},{7,6},{8,9},{9,8},{10,11... | collective-permute-start | bytes 614408 | tf_op jit(solution)/shard_map/ppermute | solution.py:26
  7.5 2.6 %collective-permute-start.8 = (bf16[800,128]{1,0:T(8,128)(2,1)S(1)}, bf16[800,128]{1,0:T(8,128)(2,1)S(1)}, u32[]{:S(2)}, u32[]{:S(2)}) collective-permute-start(bf16[800,128]{1,0:T(8,128)(2,1)S(1)} %get-tuple-element.74.refs_4_), channel_id=1, source_target_pairs={{0,2},{1,3},{2,0},{3,1},{4,6},{5,7},{6,4},{7,5},{8,10},{9,11},{10,... | collective-permute-start | bytes 614408 | tf_op jit(solution)/shard_map/ppermute | solution.py:26
  10.6 0.7 %reshape.12.gain_ref = f32[1,1280]{1,0:T(1,128)S(1)} reshape(f32[1280]{0:T(1024)} %param.10) | data formatting | bytes 10240 | tf_op jit(solution)/shard_map/reshape | solution.py:273
  11.3 1.5 %copy-done = bf16[768,1280]{1,0:T(8,128)(2,1)S(1)} copy-done((bf16[768,1280]{1,0:T(8,128)(2,1)S(1)}, bf16[768,1280]{1,0:T(8,128)(2,1)}, u32[]{:S(2)}) %copy-start) | copy-done | bytes 1966104
  12.9 1.6 %norm.1 = (bf16[768,1280]{1,0:T(8,128)(2,1)S(1)}, bf16[192,1280]{1,0:T(8,128)(2,1)S(1)}) custom-call(s32[3]{0:T(128)S(1)} %pad_add_fusion.1.index_ref, bf16[768,1280]{1,0:T(8,128)(2,1)S(1)} %copy-done, f32[1,1280]{1,0:T(1,128)S(1)} %reshape.12.gain_ref), custom_call_target="tpu_custom_call" | custom-call | tf_op jit(solution)/shard_map/norm/pallas_call | solution.py:266
  14.5 1.6 %collective-permute-start.3 = (bf16[800,128]{1,0:T(8,128)(2,1)S(1)}, bf16[800,128]{1,0:T(8,128)(2,1)S(1)}, u32[]{:S(2)}, u32[]{:S(2)}) collective-permute-start(bf16[800,128]{1,0:T(8,128)(2,1)S(1)} %collective-permute-done.refs_2_), channel_id=1, source_target_pairs={{0,16},{16,0},{1,17},{17,1},{2,18},{18,2},{3,19},{19,3},{4,20},{20... | collective-permute-start | bytes 614408 | tf_op jit(solution)/shard_map/ppermute | solution.py:26
  16.0 1.3 %collective-permute-done.2.refs_5_ = bf16[800,128]{1,0:T(8,128)(2,1)S(1)} collective-permute-done((bf16[800,128]{1,0:T(8,128)(2,1)S(1)}, bf16[800,128]{1,0:T(8,128)(2,1)S(1)}, u32[]{:S(2)}, u32[]{:S(2)}) %collective-permute-start.2) | collective-permute-done | bytes 204832 | tf_op jit(solution)/shard_map/ppermute | solution.py:26
  17.8 3.0 %collective-permute-done.3.refs_3_ = bf16[800,128]{1,0:T(8,128)(2,1)S(1)} collective-permute-done((bf16[800,128]{1,0:T(8,128)(2,1)S(1)}, bf16[800,128]{1,0:T(8,128)(2,1)S(1)}, u32[]{:S(2)}, u32[]{:S(2)}) %collective-permute-start.3) | collective-permute-done | bytes 204832 | tf_op jit(solution)/shard_map/ppermute | solution.py:26
  21.4 1.3 %collective-permute-start.9 = (bf16[800,128]{1,0:T(8,128)(2,1)S(1)}, bf16[800,128]{1,0:T(8,128)(2,1)S(1)}, u32[]{:S(2)}, u32[]{:S(2)}) collective-permute-start(bf16[800,128]{1,0:T(8,128)(2,1)S(1)} %get-tuple-element.74.refs_4_), channel_id=1, source_target_pairs={{0,3},{1,2},{2,1},{3,0},{4,7},{5,6},{6,5},{7,4},{8,11},{9,10},{10,... | collective-permute-start | bytes 614408 | tf_op jit(solution)/shard_map/ppermute | solution.py:26
  22.6 1.5 %collective-permute-start.11 = (s32[1,192]{1,0:T(1,128)S(1)}, s32[1,192]{1,0:T(1,128)S(1)}, u32[]{:S(2)}, u32[]{:S(2)}) collective-permute-start(s32[1,192]{1,0:T(1,128)S(1)} %bitcast.28), channel_id=1, source_target_pairs={{0,8},{4,12},{8,0},{12,4},{1,9},{5,13},{9,1},{13,5},{2,10},{6,14},... | collective-permute-start | bytes 2312 | tf_op jit(solution)/shard_map/ppermute | solution.py:26
  24.2 4.5 %attention0.1 = (bf16[240,128]{1,0:T(8,128)(2,1)S(1)}, bf16[240,128]{1,0:T(8,128)(2,1)S(1)}, bf16[240,128]{1,0:T(8,128)(2,1)S(1)}, bf16[240,128]{1,0:T(8,128)(2,1)S(1)}, bf16[1280,960]{1,0:T(8,128)(2,1)S(1)}) custom-call(s32[3]{0:T(128)S(1)} %pad_add_fusion.1.index_ref, bf16[768,1280]{1,0:T(8,128)(2,1)S(1)} %get-tuple-element.81.hidden_ref, ...), custom_call_target="tpu_custom_call" | custom-call | tf_op jit(solution)/shard_map/attention0/pallas_call | solution.py:297
  28.7 1.6 %collective-permute-done.9.refs_7_ = bf16[800,128]{1,0:T(8,128)(2,1)S(1)} collective-permute-done((bf16[800,128]{1,0:T(8,128)(2,1)S(1)}, bf16[800,128]{1,0:T(8,128)(2,1)S(1)}, u32[]{:S(2)}, u32[]{:S(2)}) %collective-permute-start.9) | collective-permute-done | bytes 204832 | tf_op jit(solution)/shard_map/ppermute | solution.py:26
  30.5 1.6 %collective-permute-start.12 = (bf16[2,800,128]{2,1,0:T(8,128)(2,1)S(1)}, bf16[2,800,128]{2,1,0:T(8,128)(2,1)S(1)}, u32[]{:S(2)}, u32[]{:S(2)}) collective-permute-start(bf16[2,800,128]{2,1,0:T(8,128)(2,1)S(1)} %pad_maximum_fusion.2), channel_id=1, source_target_pairs={{0,8},{4,12},{8,0},{12,4},{1,9},{5,13},{9,1},{13,5},{2,10},{6,14},... | collective-permute-start | bytes 1228808 | tf_op jit(solution)/shard_map/ppermute | solution.py:26
  32.1 2.9 %collective-permute-start.13 = (bf16[240,128]{1,0:T(8,128)(2,1)S(1)}, bf16[240,128]{1,0:T(8,128)(2,1)S(1)}, u32[]{:S(2)}, u32[]{:S(2)}) collective-permute-start(bf16[240,128]{1,0:T(8,128)(2,1)S(1)} %get-tuple-element.80), channel_id=1, source_target_pairs={{0,1},{1,0},{2,3},{3,2},{4,5},{5,4},{6,7},{7,6},{8,9},{9,8},{10,11... | collective-permute-start | bytes 184328 | tf_op jit(solution)/shard_map/ppermute | solution.py:26
  35.0 2.4 %collective-permute-start.15 = (bf16[240,128]{1,0:T(8,128)(2,1)S(1)}, bf16[240,128]{1,0:T(8,128)(2,1)S(1)}, u32[]{:S(2)}, u32[]{:S(2)}) collective-permute-start(bf16[240,128]{1,0:T(8,128)(2,1)S(1)} %get-tuple-element.90), channel_id=1, source_target_pairs={{0,3},{1,2},{2,1},{3,0},{4,7},{5,6},{6,5},{7,4},{8,11},{9,10},{10,... | collective-permute-start | bytes 184328 | tf_op jit(solution)/shard_map/ppermute | solution.py:26
  37.4 4.0 %attention1.1 = (bf16[240,128]{1,0:T(8,128)(2,1)S(1)}, bf16[240,128]{1,0:T(8,128)(2,1)S(1)}, bf16[240,128]{1,0:T(8,128)(2,1)S(1)}, bf16[240,128]{1,0:T(8,128)(2,1)S(1)}) custom-call(s32[3]{0:T(128)S(1)} %pad_add_fusion.1.index_ref, bf16[768,1280]{1,0:T(8,128)(2,1)S(1)} %get-tuple-element.81.hidden_ref, s32[6,128]{1,0:T(8,128)S(1)} %bitcast.27, ...), custom_call_target="tpu_custom_call" | custom-call | tf_op jit(solution)/shard_map/attention1/pallas_call | solution.py:317
  41.4 1.2 %collective-permute-done.14.refs_2_ = bf16[240,128]{1,0:T(8,128)(2,1)S(1)} collective-permute-done((bf16[240,128]{1,0:T(8,128)(2,1)S(1)}, bf16[240,128]{1,0:T(8,128)(2,1)S(1)}, u32[]{:S(2)}, u32[]{:S(2)}) %collective-permute-start.14) | collective-permute-done | bytes 61472 | tf_op jit(solution)/shard_map/ppermute | solution.py:26
  42.6 1.5 %collective-permute-start.17 = (bf16[240,128]{1,0:T(8,128)(2,1)S(1)}, bf16[240,128]{1,0:T(8,128)(2,1)S(1)}, u32[]{:S(2)}, u32[]{:S(2)}) collective-permute-start(bf16[240,128]{1,0:T(8,128)(2,1)S(1)} %get-tuple-element.92), channel_id=1, source_target_pairs={{0,1},{1,0},{2,3},{3,2},{4,5},{5,4},{6,7},{7,6},{8,9},{9,8},{10,11... | collective-permute-start | bytes 184328 | tf_op jit(solution)/shard_map/ppermute | solution.py:26
  45.3 1.5 %collective-permute-done.17.refs_1_ = bf16[240,128]{1,0:T(8,128)(2,1)S(1)} collective-permute-done((bf16[240,128]{1,0:T(8,128)(2,1)S(1)}, bf16[240,128]{1,0:T(8,128)(2,1)S(1)}, u32[]{:S(2)}, u32[]{:S(2)}) %collective-permute-start.17) | collective-permute-done | bytes 61472 | tf_op jit(solution)/shard_map/ppermute | solution.py:26
  46.8 1.6 %collective-permute-start.21 = (bf16[240,128]{1,0:T(8,128)(2,1)S(1)}, bf16[240,128]{1,0:T(8,128)(2,1)S(1)}, u32[]{:S(2)}, u32[]{:S(2)}) collective-permute-start(bf16[240,128]{1,0:T(8,128)(2,1)S(1)} %get-tuple-element.105), channel_id=1, source_target_pairs={{0,2},{1,3},{2,0},{3,1},{4,6},{5,7},{6,4},{7,5},{8,10},{9,11},{10,... | collective-permute-start | bytes 184328 | tf_op jit(solution)/shard_map/ppermute | solution.py:26
  48.5 2.3 %collective-permute-start.22 = (bf16[240,128]{1,0:T(8,128)(2,1)S(1)}, bf16[240,128]{1,0:T(8,128)(2,1)S(1)}, u32[]{:S(2)}, u32[]{:S(2)}) collective-permute-start(bf16[240,128]{1,0:T(8,128)(2,1)S(1)} %get-tuple-element.106), channel_id=1, source_target_pairs={{0,3},{1,2},{2,1},{3,0},{4,7},{5,6},{6,5},{7,4},{8,11},{9,10},{10,... | collective-permute-start | bytes 184328 | tf_op jit(solution)/shard_map/ppermute | solution.py:26
  50.7 1.6 %project0.1.refs_4_ = bf16[96,1280]{1,0:T(8,128)(2,1)S(1)} custom-call(s32[3]{0:T(128)S(1)} %pad_add_fusion.1.index_ref, bf16[240,128]{1,0:T(8,128)(2,1)S(1)} %get-tuple-element.95.refs_0_, bf16[240,128]{1,0:T(8,128)(2,1)S(1)} %collective-permute-done.13.refs_1_, bf16[240,128]{1,0:T(8,128)(2,1)S(1)} %collective-permute-done.14.refs_2_, ...), custom_call_target="tpu_custom_call" | custom-call | tf_op jit(solution)/shard_map/project0/pallas_call | solution.py:337
  53.0 2.2 %collective-permute-done.21.refs_2_ = bf16[240,128]{1,0:T(8,128)(2,1)S(1)} collective-permute-done((bf16[240,128]{1,0:T(8,128)(2,1)S(1)}, bf16[240,128]{1,0:T(8,128)(2,1)S(1)}, u32[]{:S(2)}, u32[]{:S(2)}) %collective-permute-start.21) | collective-permute-done | bytes 61472 | tf_op jit(solution)/shard_map/ppermute | solution.py:26
  55.2 1.6 %project1.1.refs_5_ = bf16[96,1280]{1,0:T(8,128)(2,1)S(1)} custom-call(s32[3]{0:T(128)S(1)} %pad_add_fusion.1.index_ref, bf16[240,128]{1,0:T(8,128)(2,1)S(1)} %get-tuple-element.107.refs_0_, bf16[240,128]{1,0:T(8,128)(2,1)S(1)} %collective-permute-done.17.refs_1_, bf16[240,128]{1,0:T(8,128)(2,1)S(1)} %collective-permute-done.21.refs_2_, ...), custom_call_target="tpu_custom_call" | custom-call | tf_op jit(solution)/shard_map/project1/pallas_call | solution.py:337
  57.9 3.4 %collective-permute-done.25.refs_8_ = bf16[96,1280]{1,0:T(8,128)(2,1)S(1)} collective-permute-done((bf16[96,1280]{1,0:T(8,128)(2,1)S(1)}, bf16[96,1280]{1,0:T(8,128)(2,1)S(1)}, u32[]{:S(2)}, u32[]{:S(2)}) %collective-permute-start.25) | collective-permute-done | bytes 245792 | tf_op jit(solution)/shard_map/ppermute | solution.py:26
  61.3 4.2 %collective-permute-done.26.refs_9_ = bf16[96,1280]{1,0:T(8,128)(2,1)S(1)} collective-permute-done((bf16[96,1280]{1,0:T(8,128)(2,1)S(1)}, bf16[96,1280]{1,0:T(8,128)(2,1)S(1)}, u32[]{:S(2)}, u32[]{:S(2)}) %collective-permute-start.26) | collective-permute-done | bytes 245792 | tf_op jit(solution)/shard_map/ppermute | solution.py:26
  65.6 1.5 %collective-permute-done.28.refs_11_ = bf16[96,1280]{1,0:T(8,128)(2,1)S(1)} collective-permute-done((bf16[96,1280]{1,0:T(8,128)(2,1)S(1)}, bf16[96,1280]{1,0:T(8,128)(2,1)S(1)}, u32[]{:S(2)}, u32[]{:S(2)}) %collective-permute-start.28) | collective-permute-done | bytes 245792 | tf_op jit(solution)/shard_map/ppermute | solution.py:26
  67.0 1.9 %placement.1 = bf16[192,1280]{1,0:T(8,128)(2,1)} custom-call(s32[3]{0:T(128)S(1)} %pad_add_fusion.1.index_ref, s32[1,192]{1,0:T(1,128)S(1)} %bitcast.30, s32[1,192]{1,0:T(1,128)S(1)} %get-tuple-element.112.refs_1_, s32[1,192]{1,0:T(1,128)S(1)} %collective-permute-done.11.refs_2_, s32[1,192]{1,0:T(1,128)S(1)} %get-tuple-element.111.refs_3_, ...), custom_call_target="tpu_custom_call" | custom-call | tf_op jit(solution)/shard_map/placement/pallas_call | solution.py:350
  (53 shorter events, 5.2 us)
Async XLA Ops:
  0.0 22.6 %copy-start.4 = (s32[192]{0:T(256)S(1)}, s32[192]{0:T(256)}, u32[]{:S(2)}) copy-start(s32[192]{0:T(256)} %param.9) | copy-start | bytes 2308
  0.0 24.2 %copy-start.3 = (s32[768]{0:T(1024)S(1)}, s32[768]{0:T(1024)}, u32[]{:S(2)}) copy-start(s32[768]{0:T(1024)} %param.8) | copy-start | bytes 9220
  2.8 11.6 %collective-permute-start.1 = (bf16[3,800,128]{2,1,0:T(8,128)(2,1)S(1)}, bf16[3,800,128]{2,1,0:T(8,128)(2,1)S(1)}, u32[]{:S(2)}, u32[]{:S(2)}) collective-permute-start(bf16[3,800,128]{2,1,0:T(8,128)(2,1)S(1)} %get-tuple-element.59.refs_0_), channel_id=1, source_target_pairs={{0,4},{4,0},{8,12},{12,8},{1,5},{5,1},{9,13},{13,9},{2,6},{6,2},{1... | collective-permute-start | bytes 1843208 | tf_op jit(solution)/shard_map/ppermute | solution.py:26
  3.4 11.1 %collective-permute-start = (bf16[800,128]{1,0:T(8,128)(2,1)S(1)}, bf16[800,128]{1,0:T(8,128)(2,1)S(1)}, u32[]{:S(2)}, u32[]{:S(2)}) collective-permute-start(bf16[800,128]{1,0:T(8,128)(2,1)S(1)} %get-tuple-element.58), channel_id=1, source_target_pairs={{0,8},{4,12},{8,0},{12,4},{1,9},{5,13},{9,1},{13,5},{2,10},{6,14},... | collective-permute-start | bytes 614408 | tf_op jit(solution)/shard_map/ppermute | solution.py:26
  6.0 11.4 %collective-permute-start.2 = (bf16[800,128]{1,0:T(8,128)(2,1)S(1)}, bf16[800,128]{1,0:T(8,128)(2,1)S(1)}, u32[]{:S(2)}, u32[]{:S(2)}) collective-permute-start(bf16[800,128]{1,0:T(8,128)(2,1)S(1)} %get-tuple-element.74.refs_4_), channel_id=1, source_target_pairs={{0,1},{1,0},{2,3},{3,2},{4,5},{5,4},{6,7},{7,6},{8,9},{9,8},{10,11... | collective-permute-start | bytes 614408 | tf_op jit(solution)/shard_map/ppermute | solution.py:26
  7.5 13.8 %collective-permute-start.8 = (bf16[800,128]{1,0:T(8,128)(2,1)S(1)}, bf16[800,128]{1,0:T(8,128)(2,1)S(1)}, u32[]{:S(2)}, u32[]{:S(2)}) collective-permute-start(bf16[800,128]{1,0:T(8,128)(2,1)S(1)} %get-tuple-element.74.refs_4_), channel_id=1, source_target_pairs={{0,2},{1,3},{2,0},{3,1},{4,6},{5,7},{6,4},{7,5},{8,10},{9,11},{10,... | collective-permute-start | bytes 614408 | tf_op jit(solution)/shard_map/ppermute | solution.py:26
  10.1 7.7 %collective-permute-start.4 = (bf16[800,128]{1,0:T(8,128)(2,1)S(1)}, bf16[800,128]{1,0:T(8,128)(2,1)S(1)}, u32[]{:S(2)}, u32[]{:S(2)}) collective-permute-start(bf16[800,128]{1,0:T(8,128)(2,1)S(1)} %get-tuple-element.66), channel_id=1, source_target_pairs={{0,8},{4,12},{8,0},{12,4},{1,9},{5,13},{9,1},{13,5},{2,10},{6,14},... | collective-permute-start | bytes 614408 | tf_op jit(solution)/shard_map/ppermute | solution.py:26
  14.5 6.4 %collective-permute-start.3 = (bf16[800,128]{1,0:T(8,128)(2,1)S(1)}, bf16[800,128]{1,0:T(8,128)(2,1)S(1)}, u32[]{:S(2)}, u32[]{:S(2)}) collective-permute-start(bf16[800,128]{1,0:T(8,128)(2,1)S(1)} %collective-permute-done.refs_2_), channel_id=1, source_target_pairs={{0,16},{16,0},{1,17},{17,1},{2,18},{18,2},{3,19},{19,3},{4,20},{20... | collective-permute-start | bytes 614408 | tf_op jit(solution)/shard_map/ppermute | solution.py:26
  16.0 4.8 %collective-permute-start.5 = (bf16[800,128]{1,0:T(8,128)(2,1)S(1)}, bf16[800,128]{1,0:T(8,128)(2,1)S(1)}, u32[]{:S(2)}, u32[]{:S(2)}) collective-permute-start(bf16[800,128]{1,0:T(8,128)(2,1)S(1)} %collective-permute-done.refs_2_), channel_id=1, source_target_pairs={{0,4},{4,0},{8,12},{12,8},{1,5},{5,1},{9,13},{13,9},{2,6},{6,2},{1... | collective-permute-start | bytes 614408 | tf_op jit(solution)/shard_map/ppermute | solution.py:26
  17.4 12.8 %collective-permute-start.10 = (bf16[2,800,128]{2,1,0:T(8,128)(2,1)S(1)}, bf16[2,800,128]{2,1,0:T(8,128)(2,1)S(1)}, u32[]{:S(2)}, u32[]{:S(2)}) collective-permute-start(bf16[2,800,128]{2,1,0:T(8,128)(2,1)S(1)} %pad_maximum_fusion.1), channel_id=1, source_target_pairs={{0,8},{4,12},{8,0},{12,4},{1,9},{5,13},{9,1},{13,5},{2,10},{6,14},... | collective-permute-start | bytes 1228808 | tf_op jit(solution)/shard_map/ppermute | solution.py:26
  20.8 3.3 %collective-permute-start.6 = (bf16[800,128]{1,0:T(8,128)(2,1)S(1)}, bf16[800,128]{1,0:T(8,128)(2,1)S(1)}, u32[]{:S(2)}, u32[]{:S(2)}) collective-permute-start(bf16[800,128]{1,0:T(8,128)(2,1)S(1)} %collective-permute-done.3.refs_3_), channel_id=1, source_target_pairs={{0,4},{4,0},{8,12},{12,8},{1,5},{5,1},{9,13},{13,9},{2,6},{6,2},{1... | collective-permute-start | bytes 614408 | tf_op jit(solution)/shard_map/ppermute | solution.py:26
  20.8 3.3 %collective-permute-start.7 = (bf16[800,128]{1,0:T(8,128)(2,1)S(1)}, bf16[800,128]{1,0:T(8,128)(2,1)S(1)}, u32[]{:S(2)}, u32[]{:S(2)}) collective-permute-start(bf16[800,128]{1,0:T(8,128)(2,1)S(1)} %collective-permute-done.4.refs_4_), channel_id=1, source_target_pairs={{0,4},{4,0},{8,12},{12,8},{1,5},{5,1},{9,13},{13,9},{2,6},{6,2},{1... | collective-permute-start | bytes 614408 | tf_op jit(solution)/shard_map/ppermute | solution.py:26
  21.4 8.9 %collective-permute-start.9 = (bf16[800,128]{1,0:T(8,128)(2,1)S(1)}, bf16[800,128]{1,0:T(8,128)(2,1)S(1)}, u32[]{:S(2)}, u32[]{:S(2)}) collective-permute-start(bf16[800,128]{1,0:T(8,128)(2,1)S(1)} %get-tuple-element.74.refs_4_), channel_id=1, source_target_pairs={{0,3},{1,2},{2,1},{3,0},{4,7},{5,6},{6,5},{7,4},{8,11},{9,10},{10,... | collective-permute-start | bytes 614408 | tf_op jit(solution)/shard_map/ppermute | solution.py:26
  22.6 6.0 %collective-permute-start.11 = (s32[1,192]{1,0:T(1,128)S(1)}, s32[1,192]{1,0:T(1,128)S(1)}, u32[]{:S(2)}, u32[]{:S(2)}) collective-permute-start(s32[1,192]{1,0:T(1,128)S(1)} %bitcast.28), channel_id=1, source_target_pairs={{0,8},{4,12},{8,0},{12,4},{1,9},{5,13},{9,1},{13,5},{2,10},{6,14},... | collective-permute-start | bytes 2312 | tf_op jit(solution)/shard_map/ppermute | solution.py:26
  30.4 12.2 %collective-permute-start.16 = (bf16[4,800,128]{2,1,0:T(8,128)(2,1)S(1)}, bf16[4,800,128]{2,1,0:T(8,128)(2,1)S(1)}, u32[]{:S(2)}, u32[]{:S(2)}) collective-permute-start(bf16[4,800,128]{2,1,0:T(8,128)(2,1)S(1)} %pad_maximum_fusion), channel_id=1, source_target_pairs={{0,4},{4,0},{8,12},{12,8},{1,5},{5,1},{9,13},{13,9},{2,6},{6,2},{1... | collective-permute-start | bytes 2457608 | tf_op jit(solution)/shard_map/ppermute | solution.py:26
  30.5 14.8 %collective-permute-start.12 = (bf16[2,800,128]{2,1,0:T(8,128)(2,1)S(1)}, bf16[2,800,128]{2,1,0:T(8,128)(2,1)S(1)}, u32[]{:S(2)}, u32[]{:S(2)}) collective-permute-start(bf16[2,800,128]{2,1,0:T(8,128)(2,1)S(1)} %pad_maximum_fusion.2), channel_id=1, source_target_pairs={{0,8},{4,12},{8,0},{12,4},{1,9},{5,13},{9,1},{13,5},{2,10},{6,14},... | collective-permute-start | bytes 1228808 | tf_op jit(solution)/shard_map/ppermute | solution.py:26
  32.1 5.3 %collective-permute-start.13 = (bf16[240,128]{1,0:T(8,128)(2,1)S(1)}, bf16[240,128]{1,0:T(8,128)(2,1)S(1)}, u32[]{:S(2)}, u32[]{:S(2)}) collective-permute-start(bf16[240,128]{1,0:T(8,128)(2,1)S(1)} %get-tuple-element.80), channel_id=1, source_target_pairs={{0,1},{1,0},{2,3},{3,2},{4,5},{5,4},{6,7},{7,6},{8,9},{9,8},{10,11... | collective-permute-start | bytes 184328 | tf_op jit(solution)/shard_map/ppermute | solution.py:26
  35.0 7.6 %collective-permute-start.14 = (bf16[240,128]{1,0:T(8,128)(2,1)S(1)}, bf16[240,128]{1,0:T(8,128)(2,1)S(1)}, u32[]{:S(2)}, u32[]{:S(2)}) collective-permute-start(bf16[240,128]{1,0:T(8,128)(2,1)S(1)} %get-tuple-element.89), channel_id=1, source_target_pairs={{0,2},{1,3},{2,0},{3,1},{4,6},{5,7},{6,4},{7,5},{8,10},{9,11},{10,... | collective-permute-start | bytes 184328 | tf_op jit(solution)/shard_map/ppermute | solution.py:26
  35.0 7.6 %collective-permute-start.15 = (bf16[240,128]{1,0:T(8,128)(2,1)S(1)}, bf16[240,128]{1,0:T(8,128)(2,1)S(1)}, u32[]{:S(2)}, u32[]{:S(2)}) collective-permute-start(bf16[240,128]{1,0:T(8,128)(2,1)S(1)} %get-tuple-element.90), channel_id=1, source_target_pairs={{0,3},{1,2},{2,1},{3,0},{4,7},{5,6},{6,5},{7,4},{8,11},{9,10},{10,... | collective-permute-start | bytes 184328 | tf_op jit(solution)/shard_map/ppermute | solution.py:26
  37.4 13.3 %copy-start.5 = (f32[1280]{0:T(1024)S(1)}, f32[1280]{0:T(1024)}, u32[]{:S(2)}) copy-start(f32[1280]{0:T(1024)} %param.13) | copy-start | bytes 15364
  42.6 4.2 %collective-permute-start.17 = (bf16[240,128]{1,0:T(8,128)(2,1)S(1)}, bf16[240,128]{1,0:T(8,128)(2,1)S(1)}, u32[]{:S(2)}, u32[]{:S(2)}) collective-permute-start(bf16[240,128]{1,0:T(8,128)(2,1)S(1)} %get-tuple-element.92), channel_id=1, source_target_pairs={{0,1},{1,0},{2,3},{3,2},{4,5},{5,4},{6,7},{7,6},{8,9},{9,8},{10,11... | collective-permute-start | bytes 184328 | tf_op jit(solution)/shard_map/ppermute | solution.py:26
  44.1 1.2 %collective-permute-start.18 = (s32[2,1,192]{2,1,0:T(1,128)S(1)}, s32[2,1,192]{2,1,0:T(1,128)S(1)}, u32[]{:S(2)}, u32[]{:S(2)}) collective-permute-start(s32[2,1,192]{2,1,0:T(1,128)S(1)} %pad_add_fusion), channel_id=1, source_target_pairs={{0,4},{4,0},{8,12},{12,8},{1,5},{5,1},{9,13},{13,9},{2,6},{6,2},{1... | collective-permute-start | bytes 4616 | tf_op jit(solution)/shard_map/ppermute | solution.py:26
  44.1 6.6 %collective-permute-start.19 = (bf16[2,800,128]{2,1,0:T(8,128)(2,1)S(1)}, bf16[2,800,128]{2,1,0:T(8,128)(2,1)S(1)}, u32[]{:S(2)}, u32[]{:S(2)}) collective-permute-start(bf16[2,800,128]{2,1,0:T(8,128)(2,1)S(1)} %collective-permute-done.10.refs_9_), channel_id=1, source_target_pairs={{0,4},{4,0},{8,12},{12,8},{1,5},{5,1},{9,13},{13,9},{2,6},{6,2},{1... | collective-permute-start | bytes 1228808 | tf_op jit(solution)/shard_map/ppermute | solution.py:26
  46.8 3.9 %collective-permute-start.20 = (bf16[2,800,128]{2,1,0:T(8,128)(2,1)S(1)}, bf16[2,800,128]{2,1,0:T(8,128)(2,1)S(1)}, u32[]{:S(2)}, u32[]{:S(2)}) collective-permute-start(bf16[2,800,128]{2,1,0:T(8,128)(2,1)S(1)} %collective-permute-done.12.refs_10_), channel_id=1, source_target_pairs={{0,4},{4,0},{8,12},{12,8},{1,5},{5,1},{9,13},{13,9},{2,6},{6,2},{1... | collective-permute-start | bytes 1228808 | tf_op jit(solution)/shard_map/ppermute | solution.py:26
  46.8 8.3 %collective-permute-start.21 = (bf16[240,128]{1,0:T(8,128)(2,1)S(1)}, bf16[240,128]{1,0:T(8,128)(2,1)S(1)}, u32[]{:S(2)}, u32[]{:S(2)}) collective-permute-start(bf16[240,128]{1,0:T(8,128)(2,1)S(1)} %get-tuple-element.105), channel_id=1, source_target_pairs={{0,2},{1,3},{2,0},{3,1},{4,6},{5,7},{6,4},{7,5},{8,10},{9,11},{10,... | collective-permute-start | bytes 184328 | tf_op jit(solution)/shard_map/ppermute | solution.py:26
  48.5 6.7 %collective-permute-start.22 = (bf16[240,128]{1,0:T(8,128)(2,1)S(1)}, bf16[240,128]{1,0:T(8,128)(2,1)S(1)}, u32[]{:S(2)}, u32[]{:S(2)}) collective-permute-start(bf16[240,128]{1,0:T(8,128)(2,1)S(1)} %get-tuple-element.106), channel_id=1, source_target_pairs={{0,3},{1,2},{2,1},{3,0},{4,7},{5,6},{6,5},{7,4},{8,11},{9,10},{10,... | collective-permute-start | bytes 184328 | tf_op jit(solution)/shard_map/ppermute | solution.py:26
  52.4 8.9 %collective-permute-start.25 = (bf16[96,1280]{1,0:T(8,128)(2,1)S(1)}, bf16[96,1280]{1,0:T(8,128)(2,1)S(1)}, u32[]{:S(2)}, u32[]{:S(2)}) collective-permute-start(bf16[96,1280]{1,0:T(8,128)(2,1)S(1)} %project0.1.refs_4_), channel_id=1, source_target_pairs={{0,8},{4,12},{8,0},{12,4},{1,9},{5,13},{9,1},{13,5},{2,10},{6,14},... | collective-permute-start | bytes 737288 | tf_op jit(solution)/shard_map/ppermute | solution.py:26
  56.8 8.7 %collective-permute-start.26 = (bf16[96,1280]{1,0:T(8,128)(2,1)S(1)}, bf16[96,1280]{1,0:T(8,128)(2,1)S(1)}, u32[]{:S(2)}, u32[]{:S(2)}) collective-permute-start(bf16[96,1280]{1,0:T(8,128)(2,1)S(1)} %project1.1.refs_5_), channel_id=1, source_target_pairs={{0,8},{4,12},{8,0},{12,4},{1,9},{5,13},{9,1},{13,5},{2,10},{6,14},... | collective-permute-start | bytes 737288 | tf_op jit(solution)/shard_map/ppermute | solution.py:26
  57.4 8.1 %collective-permute-start.23 = (bf16[96,1280]{1,0:T(8,128)(2,1)S(1)}, bf16[96,1280]{1,0:T(8,128)(2,1)S(1)}, u32[]{:S(2)}, u32[]{:S(2)}) collective-permute-start(bf16[96,1280]{1,0:T(8,128)(2,1)S(1)} %project0.1.refs_4_), channel_id=1, source_target_pairs={{0,4},{4,0},{8,12},{12,8},{1,5},{5,1},{9,13},{13,9},{2,6},{6,2},{1... | collective-permute-start | bytes 737288 | tf_op jit(solution)/shard_map/ppermute | solution.py:26
  57.4 8.1 %collective-permute-start.24 = (bf16[96,1280]{1,0:T(8,128)(2,1)S(1)}, bf16[96,1280]{1,0:T(8,128)(2,1)S(1)}, u32[]{:S(2)}, u32[]{:S(2)}) collective-permute-start(bf16[96,1280]{1,0:T(8,128)(2,1)S(1)} %project1.1.refs_5_), channel_id=1, source_target_pairs={{0,4},{4,0},{8,12},{12,8},{1,5},{5,1},{9,13},{13,9},{2,6},{6,2},{1... | collective-permute-start | bytes 737288 | tf_op jit(solution)/shard_map/ppermute | solution.py:26
  61.3 4.3 %collective-permute-start.27 = (bf16[96,1280]{1,0:T(8,128)(2,1)S(1)}, bf16[96,1280]{1,0:T(8,128)(2,1)S(1)}, u32[]{:S(2)}, u32[]{:S(2)}) collective-permute-start(bf16[96,1280]{1,0:T(8,128)(2,1)S(1)} %collective-permute-done.25.refs_8_), channel_id=1, source_target_pairs={{0,4},{4,0},{8,12},{12,8},{1,5},{5,1},{9,13},{13,9},{2,6},{6,2},{1... | collective-permute-start | bytes 737288 | tf_op jit(solution)/shard_map/ppermute | solution.py:26
  65.5 1.5 %collective-permute-start.28 = (bf16[96,1280]{1,0:T(8,128)(2,1)S(1)}, bf16[96,1280]{1,0:T(8,128)(2,1)S(1)}, u32[]{:S(2)}, u32[]{:S(2)}) collective-permute-start(bf16[96,1280]{1,0:T(8,128)(2,1)S(1)} %collective-permute-done.26.refs_9_), channel_id=1, source_target_pairs={{0,4},{4,0},{8,12},{12,8},{1,5},{5,1},{9,13},{13,9},{2,6},{6,2},{1... | collective-permute-start | bytes 737288 | tf_op jit(solution)/shard_map/ppermute | solution.py:26
  (3 other events, 3.6 us)

commit v6 on v5

--- a/solution.py
+++ b/solution.py
@@ -14,12 +14,17 @@
 CHUNKS = 2
 F32 = jnp.float32
 BF16 = jnp.bfloat16
+ANY = pl.BlockSpec(memory_space=pl.ANY)
 VMEM = pl.BlockSpec(memory_space=pltpu.VMEM)
 SMEM = pl.BlockSpec(memory_space=pltpu.SMEM)
 
 
 def params(mib):
     return pltpu.CompilerParams(vmem_limit_bytes=mib * 1024 * 1024)
+
+
+def cost(us):
+    return pl.CostEstimate(flops=int(us * 1e9), bytes_accessed=int(us * 3.3e6), transcendentals=0)
 
 
 def swap(x, axis, size, bit):
@@ -84,28 +89,45 @@
     return jnp.concatenate([p[:rows], p[rows : 2 * rows]], axis=1), rest
 
 
-def pack_kernel(index_ref, qkv_ref, proj_ref, first_ref, value_ref, all_ref, proj_out_ref):
+def pack_kernel(
+    index_ref, qkv_any, proj_any, first_ref, value_ref, all_ref, proj_out_ref, qkv_ref, proj_ref, sem
+):
+    copies = [pltpu.make_async_copy(qkv_any.at[j], qkv_ref.at[j], sem.at[j]) for j in range(3)]
+    copies.append(pltpu.make_async_copy(proj_any, proj_ref, sem.at[3]))
+    for copy in copies:
+        copy.start()
     for j in range(3):
+        copies[j].wait()
         all_ref[j] = pack(qkv_ref[j])
     first_ref[...] = all_ref[index_ref[2]]
     value_ref[...] = all_ref[2]
+    copies[3].wait()
     proj_out_ref[...] = pack(proj_ref[...])
 
 
-def norm_kernel(index_ref, patches_ref, gain_ref, hidden_ref, own_ref):
-    rows = patches_ref.shape[0]
-    x = patches_ref[...]
-    xf = x.astype(F32)
-    mean_sq = jnp.mean(xf * xf, axis=-1, keepdims=True)
-    hidden_ref[...] = (xf * lax.rsqrt(mean_sq + 1e-06) * gain_ref[...]).astype(BF16)
+def norm_kernel(index_ref, patches_any, gain_ref, hidden_ref, own_ref, x_ref, sem):
     step = 256
+    count = x_ref.shape[0] // step
+    copies = []
+    for i in range(count):
+        rows = pl.ds(i * step, step)
+        copies.append(pltpu.make_async_copy(patches_any.at[rows], x_ref.at[rows], sem.at[i]))
+        copies[i].start()
+    gain = gain_ref[...].reshape(1, -1)
     pick = step // 4
     row = lax.broadcasted_iota(jnp.int32, (pick, step), 0)
     col = lax.broadcasted_iota(jnp.int32, (pick, step), 1)
     chosen = one_hot(col == 4 * row + index_ref[1])
-    for i in range(rows // step):
+    for i in range(count):
+        copies[i].wait()
+        x = x_ref[i * step : (i + 1) * step, :]
+        xf = x.astype(F32)
+        mean_sq = jnp.mean(xf * xf, axis=-1, keepdims=True)
+        hidden_ref[i * step : (i + 1) * step, :] = (
+            xf * lax.rsqrt(mean_sq + 1e-06) * gain
+        ).astype(BF16)
         own_ref[i * pick : (i + 1) * pick, :] = jnp.dot(
-            chosen, x[i * step : (i + 1) * step], preferred_element_type=F32
+            chosen, x, preferred_element_type=F32
         ).astype(BF16)
 
 
@@ -183,6 +205,11 @@
 
 def project_kernel(n_ctx, row0, width, col, index_ref, *refs):
     mixes = [unpack(m[...], refs[-2].shape[0], width) for m in refs[:4]]
+    flip = index_ref[2] > 0
+    mixes[2:] = [
+        [jnp.where(flip, b, a) for a, b in zip(mixes[2], mixes[3])],
+        [jnp.where(flip, a, b) for a, b in zip(mixes[2], mixes[3])],
+    ]
     *blocks, own_ref, gain_ref, out_ref, part_ref = refs[4:]
     rows = out_ref.shape[0]
     me = index_ref[0]
@@ -212,7 +239,7 @@
     total = jnp.concatenate([part_ref[i] for i in range(n_ctx)], axis=1)
     total = total + own_ref[row0 : row0 + rows, :].astype(F32)
     mean_sq = jnp.mean(total * total, axis=-1, keepdims=True)
-    out_ref[...] = (total * lax.rsqrt(mean_sq + 1e-06) * gain_ref[...]).astype(BF16)
+    out_ref[...] = (total * lax.rsqrt(mean_sq + 1e-06) * gain_ref[...].reshape(1, -1)).astype(BF16)
 
 
 def place_kernel(n_ctx, index_ref, *refs):
@@ -253,37 +280,50 @@
     first, value, own, w_proj = pl.pallas_call(
         pack_kernel,
         out_shape=(shape(*third), shape(*third), shape(3, *third), shape(*piece)),
-        in_specs=[SMEM, VMEM, VMEM],
+        in_specs=[SMEM, ANY, ANY],
         out_specs=(VMEM,) * 4,
+        scratch_shapes=[
+            pltpu.VMEM((3, depth, width), BF16),
+            pltpu.VMEM((width, col), BF16),
+            pltpu.SemaphoreType.DMA((4,)),
+        ],
         compiler_params=params(8),
+        cost_estimate=cost(1),
         name="pack",
     )(index, jnp.transpose(w_qkv, (1, 0, 2)), w_proj)
     first = gather_cross(first, n_ctx)
     value = gather_cross(value, n_ctx)
     twin = over_core(own)
+    far = lax.ppermute(
+        w_proj,
+        ("dp", "tensor"),
+        [
+            (d * n_ten + t, d * n_ten + (t ^ (2 + d % 2)))
+            for d in range(n_dp)
+            for t in range(n_ten)
+        ],
+    )
     by_one = swap(w_proj, "tensor", n_ten, 1)
-    by_two = swap(w_proj, "tensor", n_ten, 2)
+    first, twin, patches = together(first, twin, patches)
+
+    second = {k: over_dp(first[k]) for k in cross}
+    first_twin = {k: over_core(first[k]) for k in cross}
     hidden, own_patches = pl.pallas_call(
         norm_kernel,
         out_shape=(shape(rows, feat), shape(groups, feat)),
-        in_specs=[SMEM, VMEM, VMEM],
+        in_specs=[SMEM, ANY, VMEM],
         out_specs=(VMEM, VMEM),
+        scratch_shapes=[pltpu.VMEM((rows, feat), BF16), pltpu.SemaphoreType.DMA((rows // 256,))],
         compiler_params=params(16),
+        cost_estimate=cost(2),
         name="norm",
-    )(index, patches, gain_attn.reshape(1, feat))
-    first, twin, hidden = together(first, twin, hidden)
-
-    second = {k: over_dp(first[k]) for k in cross}
-    first_twin = {k: over_core(first[k]) for k in cross}
-    by_one, first = together(by_one, first)
+    )(index, patches, gain_attn)
     low = gather_cross(jnp.stack([w_proj, by_one]), n_ctx)
     second, value, first_twin = together(second, value, first_twin)
 
     second_twin = {k: over_core(second[k]) for k in cross}
     value_twin = {k: over_core(value[k]) for k in cross}
-    by_two, w_proj, place = together(by_two, w_proj, place, second, value)[:3]
-    by_three = swap(w_proj, "tensor", n_ten, 3)
-    places = gather_cross(place.reshape(1, groups), n_ctx)
+    far2 = over_dp(far)
 
     shard_list = [own, twin]
     for k in cross:
@@ -291,7 +331,6 @@
 
     valid_pairs = valid.reshape(rows // PAIR, PAIR)
     part = rows // CHUNKS
-    gain2 = gain_merge.reshape(1, feat)
     mix_shapes = (shape(*packed_shape(part // 4, width)),) * n_ten
     scratch = [pltpu.VMEM((part, width), BF16)] * 3 + [pltpu.VMEM((4, part // 4, width), BF16)]
     *mixed, w_full = pl.pallas_call(
@@ -301,17 +340,17 @@
         out_specs=(VMEM,) * (n_ten + 1),
         scratch_shapes=scratch,
         compiler_params=params(16),
+        cost_estimate=cost(5),
         name="attention0",
     )(index, hidden, valid_pairs, *shard_list)
 
     def exchange(pieces):
         return [pieces[0]] + [swap(pieces[s], "tensor", n_ten, s) for s in range(1, n_ten)]
 
-    mixed, by_three, low, places = together(mixed, by_three, low, places)
+    mixed, far, far2, low = together(mixed, far, far2, low)
     received = [exchange(mixed)]
-    high = gather_cross(jnp.stack([by_two, by_three]), n_ctx)
-    own_twin = over_core(jnp.stack([w_proj, by_one, by_two, by_three]))
-    place_twin = over_core(jnp.stack([places[k] for k in (0, *cross)]))
+    high = gather_cross(jnp.stack([far, far2]), n_ctx)
+    own_twin = None
     for r in range(1, CHUNKS):
         received[r - 1][1], hidden = together(received[r - 1][1], hidden)
         mixed = pl.pallas_call(
@@ -321,19 +360,21 @@
             out_specs=(VMEM,) * n_ten,
             scratch_shapes=scratch,
             compiler_params=params(12),
-            name="attention" + str(r),
+            cost_estimate=cost(4),
+        name="attention" + str(r),
         )(index, hidden, valid_pairs, w_full)
-        mixed, received[r - 1], own_twin, low = together(mixed, received[r - 1], own_twin, low)
+        mixed, received[r - 1], low, w_proj = together(mixed, received[r - 1], low, w_proj)
         received.append(exchange(mixed))
-    high, received[-1][1], place_twin = together(high, received[-1][1], place_twin)
-
-    blocks = [w_proj, by_one, by_two, by_three, own_twin]
+        if own_twin is None:
+            own_twin = over_core(jnp.stack([w_proj, by_one, far, far2]))
+
+    blocks = [w_proj, by_one, far, far2, own_twin]
     for k in cross:
         blocks += [low[k], high[k], over_core(low[k]), over_core(high[k])]
     gathered = []
     for r in range(CHUNKS):
         if r > 0:
-            received[r], done = together(received[r], done)
+            received[r], gathered[0][1], place = together(received[r], gathered[0][1], place)
         done = pl.pallas_call(
             functools.partial(project_kernel, n_ctx, r * (part // 4), width, col),
             out_shape=shape(part // 4, feat),
@@ -341,9 +382,12 @@
             out_specs=VMEM,
             scratch_shapes=[pltpu.VMEM((n_ctx, part // 4, col), F32)],
             compiler_params=params(20),
-            name="project" + str(r),
-        )(index, *received[r], *blocks, own_patches, gain2)
+            cost_estimate=cost(2),
+        name="project" + str(r),
+        )(index, *received[r], *blocks, own_patches, gain_merge)
         gathered.append(gather_xor(done, n_ctx))
+    places = gather_cross(place.reshape(1, groups), n_ctx)
+    place_twin = over_core(jnp.stack([places[k] for k in (0, *cross)]))
     place_list = []
     for i, k in enumerate((0, *cross)):
         place_list += [places[k], place_twin[i]]
@@ -353,6 +397,7 @@
         in_specs=[SMEM] + [VMEM] * (n_ctx + n_ctx * CHUNKS),
         out_specs=VMEM,
         compiler_params=params(28),
+        cost_estimate=cost(2),
         name="placement",
     )(index, *place_list, *[gathered[r][k] for k in range(n_ctx) for r in range(CHUNKS)])
 

time: 69.2 us -> 75.3 us (1.088)
  waiting for transfers between devices: 20.7 us -> 27.7 us
  Pallas kernels: 15.9 us -> 18.2 us
  local copies, waits for them, and re-layouts: 4.32 us -> 2.09 us
  starting transfers between devices: 27.6 us -> 26.7 us
    ppermute x29 -> x28, waiting for transfers between devices: 20.7 us -> 27 us  [swap(): return lax.ppermute(x, axis, [(i, i ^ bit) for i in range(size)])]
    ppermute x29 -> x28, starting transfers between devices: 27.6 us -> 24.1 us  [swap(): return lax.ppermute(x, axis, [(i, i ^ bit) for i in range(size)])]
    ppermute x0 -> x1, starting transfers between devices: none -> 2.59 us  [local(): lax.ppermute(w_proj, ('dp', 'tensor'), [(d * n_ten + t, d * n_ten + (t ^...]
    pallas_call x1, Pallas kernels: 0.69 us -> 2.23 us  [local(): pl.pallas_call(pack_kernel, out_shape=(shape(*third), shape(*third), shap...]
    unnamed x12 -> x14, local copies, waits for them, and re-layouts: 3.62 us -> 2.08 us
  transfers between devices with their start and end apart: 29 -> 29, of which waited for: 10 -> 13; matrix products, arithmetic and copies ran while one was open for 1% -> 0% of each run, Pallas kernels for 19% -> 17%
where the time goes in v6:
time: 75.3 us; the launch traced here: 75.1 us
  waiting for transfers between devices  27.7 us (37%)
  starting transfers between devices  26.7 us (35%)
  Pallas kernels  18.2 us (24%)
  local copies, waits for them, and re-layouts  2.09 us (3%)
    ppermute x28, waiting for transfers between devices, swap(): return lax.ppermute(x, axis, [(i, i ^ bit) for i in range(size)])  27 us
    ppermute x28, starting transfers between devices, swap(): return lax.ppermute(x, axis, [(i, i ^ bit) for i in range(size)])  24.1 us
    pallas_call x1, Pallas kernels, local(): pl.pallas_call(functools.partial(first_attention_kernel, n_ctx, width), o...  4.55 us
    pallas_call x1, Pallas kernels, local(): pl.pallas_call(functools.partial(next_attention_kernel, r * part), out_sh...  3.99 us
    pallas_call x2, Pallas kernels, local(): pl.pallas_call(functools.partial(project_kernel, n_ctx, r * (part // 4),...  3.3 us
    ppermute x1, starting transfers between devices, local(): lax.ppermute(w_proj, ('dp', 'tensor'), [(d * n_ten + t, d * n_ten + (t ^...  2.59 us
    pallas_call x1, Pallas kernels, local(): pl.pallas_call(pack_kernel, out_shape=(shape(*third), shape(*third), shap...  2.23 us
    pallas_call x1, Pallas kernels, local(): pl.pallas_call(norm_kernel, out_shape=(shape(rows, feat), shape(groups, f...  2.21 us
  transfers between devices with their start and end apart: 29, of which 13 were waited for; matrix products, arithmetic and copies ran while one was open for 0% of the time, Pallas kernels for 17%

profile of v6, /device:TPU:0, one launch (start us, length us, event | category | flops | bytes accessed | tf_op | source)
XLA Modules:
  0.0 75.1 jit_solution(5167753634038081482)
XLA Ops:
  0.1 1.1 %copy-done.2 = bf16[320,3,320]{2,0,1:T(8,128)(2,1)S(1)} copy-done((bf16[320,3,320]{2,0,1:T(8,128)(2,1)S(1)}, bf16[320,3,320]{2,0,1:T(8,128)(2,1)}, u32[]{:S(2)}) %copy-start.2) | copy-done | bytes 614424
  1.2 0.9 %copy-done.3 = bf16[320,320]{1,0:T(8,128)(2,1)S(1)} copy-done((bf16[320,320]{1,0:T(8,128)(2,1)S(1)}, bf16[320,320]{1,0:T(8,128)(2,1)}, u32[]{:S(2)}) %copy-start.3) | copy-done | bytes 204824
  2.1 2.2 %pack.1 = (bf16[800,128]{1,0:T(8,128)(2,1)S(1)}, bf16[800,128]{1,0:T(8,128)(2,1)S(1)}, bf16[3,800,128]{2,1,0:T(8,128)(2,1)S(1)}, bf16[800,128]{1,0:T(8,128)(2,1)S(1)}) custom-call(s32[3]{0:T(128)S(1)} %pad_add_fusion.1.index_ref, bf16[3,320,320]{2,1,0:T(8,128)(2,1)S(1)} %bitcast.29, bf16[320,320]{1,0:T(8,128)(2,1)S(1)} %copy-done.3), custom_call_target="tpu_custom_call" | custom-call | flops 1000000000 | bytes 3300000 | tf_op jit(solution)/shard_map/pack/pallas_call | solution.py:280
  4.9 2.6 %collective-permute-start = (bf16[800,128]{1,0:T(8,128)(2,1)S(1)}, bf16[800,128]{1,0:T(8,128)(2,1)S(1)}, u32[]{:S(2)}, u32[]{:S(2)}) collective-permute-start(bf16[800,128]{1,0:T(8,128)(2,1)S(1)} %get-tuple-element.51), channel_id=1, source_target_pairs={{0,8},{4,12},{8,0},{12,4},{1,9},{5,13},{9,1},{13,5},{2,10},{6,14},... | collective-permute-start | bytes 614408 | tf_op jit(solution)/shard_map/ppermute | solution.py:31
  7.6 5.8 %collective-permute-done.refs_2_ = bf16[800,128]{1,0:T(8,128)(2,1)S(1)} collective-permute-done((bf16[800,128]{1,0:T(8,128)(2,1)S(1)}, bf16[800,128]{1,0:T(8,128)(2,1)S(1)}, u32[]{:S(2)}, u32[]{:S(2)}) %collective-permute-start) | collective-permute-done | bytes 204832 | tf_op jit(solution)/shard_map/ppermute | solution.py:31
  13.4 1.9 %collective-permute-start.2 = (bf16[800,128]{1,0:T(8,128)(2,1)S(1)}, bf16[800,128]{1,0:T(8,128)(2,1)S(1)}, u32[]{:S(2)}, u32[]{:S(2)}) collective-permute-start(bf16[800,128]{1,0:T(8,128)(2,1)S(1)} %collective-permute-done.refs_2_), channel_id=1, source_target_pairs={{0,16},{16,0},{1,17},{17,1},{2,18},{18,2},{3,19},{19,3},{4,20},{20... | collective-permute-start | bytes 614408 | tf_op jit(solution)/shard_map/ppermute | solution.py:31
  15.4 1.6 %collective-permute-start.9 = (bf16[800,128]{1,0:T(8,128)(2,1)S(1)}, bf16[800,128]{1,0:T(8,128)(2,1)S(1)}, u32[]{:S(2)}, u32[]{:S(2)}) collective-permute-start(bf16[800,128]{1,0:T(8,128)(2,1)S(1)} %get-tuple-element.86.refs_4_), channel_id=1, source_target_pairs={{0,1},{1,0},{2,3},{3,2},{4,5},{5,4},{6,7},{7,6},{8,9},{9,8},{10,11... | collective-permute-start | bytes 614408 | tf_op jit(solution)/shard_map/ppermute | solution.py:31
  16.9 2.6 %collective-permute-start.7 = (bf16[800,128]{1,0:T(8,128)(2,1)S(1)}, bf16[800,128]{1,0:T(8,128)(2,1)S(1)}, u32[]{:S(2)}, u32[]{:S(2)}) collective-permute-start(bf16[800,128]{1,0:T(8,128)(2,1)S(1)} %get-tuple-element.86.refs_4_), channel_id=1, source_target_pairs={{0,2},{1,3},{2,0},{3,1},{16,19},{17,18},{18,17},{19,16},{4,6},{5,7... | collective-permute-start | bytes 614408 | tf_op jit(solution)/shard_map/ppermute | solution.py:297
  20.5 6.6 %collective-permute-done.9.refs_5_ = bf16[800,128]{1,0:T(8,128)(2,1)S(1)} collective-permute-done((bf16[800,128]{1,0:T(8,128)(2,1)S(1)}, bf16[800,128]{1,0:T(8,128)(2,1)S(1)}, u32[]{:S(2)}, u32[]{:S(2)}) %collective-permute-start.9) | collective-permute-done | bytes 204832 | tf_op jit(solution)/shard_map/ppermute | solution.py:31
  27.2 1.6 %collective-permute-start.10 = (bf16[2,800,128]{2,1,0:T(8,128)(2,1)S(1)}, bf16[2,800,128]{2,1,0:T(8,128)(2,1)S(1)}, u32[]{:S(2)}, u32[]{:S(2)}) collective-permute-start(bf16[2,800,128]{2,1,0:T(8,128)(2,1)S(1)} %pad_maximum_fusion.1), channel_id=1, source_target_pairs={{0,8},{4,12},{8,0},{12,4},{1,9},{5,13},{9,1},{13,5},{2,10},{6,14},... | collective-permute-start | bytes 1228808 | tf_op jit(solution)/shard_map/ppermute | solution.py:31
  28.8 0.7 collective-permute-done.7.refs_6_
  29.9 2.2 %norm.1 = (bf16[768,1280]{1,0:T(8,128)(2,1)S(1)}, bf16[192,1280]{1,0:T(8,128)(2,1)S(1)}) custom-call(s32[3]{0:T(128)S(1)} %pad_add_fusion.1.index_ref, bf16[768,1280]{1,0:T(8,128)(2,1)S(1)} %copy-done.1, f32[1280]{0:T(1024)S(1)} %copy-done.4), custom_call_target="tpu_custom_call" | custom-call | flops 2000000000 | bytes 6600000 | tf_op jit(solution)/shard_map/norm/pallas_call | solution.py:311
  32.2 4.5 %attention0.1 = (bf16[240,128]{1,0:T(8,128)(2,1)S(1)}, bf16[240,128]{1,0:T(8,128)(2,1)S(1)}, bf16[240,128]{1,0:T(8,128)(2,1)S(1)}, bf16[240,128]{1,0:T(8,128)(2,1)S(1)}, bf16[1280,960]{1,0:T(8,128)(2,1)S(1)}) custom-call(s32[3]{0:T(128)S(1)} %pad_add_fusion.1.index_ref, bf16[768,1280]{1,0:T(8,128)(2,1)S(1)} %get-tuple-element.67.hidden_ref, ...), custom_call_target="tpu_custom_call" | custom-call | flops 5000000000 | bytes 16500000 | tf_op jit(solution)/shard_map/attention0/pallas_call | solution.py:336
  36.7 1.6 %collective-permute-done.10.refs_9_ = bf16[2,800,128]{2,1,0:T(8,128)(2,1)S(1)} collective-permute-done((bf16[2,800,128]{2,1,0:T(8,128)(2,1)S(1)}, bf16[2,800,128]{2,1,0:T(8,128)(2,1)S(1)}, u32[]{:S(2)}, u32[]{:S(2)}) %collective-permute-start.10) | collective-permute-done | bytes 409632 | tf_op jit(solution)/shard_map/ppermute | solution.py:31
  38.4 1.6 %collective-permute-start.18 = (bf16[2,800,128]{2,1,0:T(8,128)(2,1)S(1)}, bf16[2,800,128]{2,1,0:T(8,128)(2,1)S(1)}, u32[]{:S(2)}, u32[]{:S(2)}) collective-permute-start(bf16[2,800,128]{2,1,0:T(8,128)(2,1)S(1)} %pad_maximum_fusion.2), channel_id=1, source_target_pairs={{0,8},{4,12},{8,0},{12,4},{1,9},{5,13},{9,1},{13,5},{2,10},{6,14},... | collective-permute-start | bytes 1228808 | tf_op jit(solution)/shard_map/ppermute | solution.py:31
  40.0 3.0 %collective-permute-start.12 = (bf16[240,128]{1,0:T(8,128)(2,1)S(1)}, bf16[240,128]{1,0:T(8,128)(2,1)S(1)}, u32[]{:S(2)}, u32[]{:S(2)}) collective-permute-start(bf16[240,128]{1,0:T(8,128)(2,1)S(1)} %get-tuple-element.75), channel_id=1, source_target_pairs={{0,2},{1,3},{2,0},{3,1},{4,6},{5,7},{6,4},{7,5},{8,10},{9,11},{10,... | collective-permute-start | bytes 184328 | tf_op jit(solution)/shard_map/ppermute | solution.py:31
  43.0 1.3 %collective-permute-start.13 = (bf16[240,128]{1,0:T(8,128)(2,1)S(1)}, bf16[240,128]{1,0:T(8,128)(2,1)S(1)}, u32[]{:S(2)}, u32[]{:S(2)}) collective-permute-start(bf16[240,128]{1,0:T(8,128)(2,1)S(1)} %get-tuple-element.76), channel_id=1, source_target_pairs={{0,3},{1,2},{2,1},{3,0},{4,7},{5,6},{6,5},{7,4},{8,11},{9,10},{10,... | collective-permute-start | bytes 184328 | tf_op jit(solution)/shard_map/ppermute | solution.py:31
  44.4 4.0 %attention1.1 = (bf16[240,128]{1,0:T(8,128)(2,1)S(1)}, bf16[240,128]{1,0:T(8,128)(2,1)S(1)}, bf16[240,128]{1,0:T(8,128)(2,1)S(1)}, bf16[240,128]{1,0:T(8,128)(2,1)S(1)}) custom-call(s32[3]{0:T(128)S(1)} %pad_add_fusion.1.index_ref, bf16[768,1280]{1,0:T(8,128)(2,1)S(1)} %get-tuple-element.67.hidden_ref, s32[6,128]{1,0:T(8,128)S(1)} %bitcast.31, ...), custom_call_target="tpu_custom_call" | custom-call | flops 4000000000 | bytes 13200000 | tf_op jit(solution)/shard_map/attention1/pallas_call | solution.py:356
  48.4 0.7 collective-permute-done.13.refs_3_
  49.8 2.3 %collective-permute-done.19.refs_11_ = bf16[2,800,128]{2,1,0:T(8,128)(2,1)S(1)} collective-permute-done((bf16[2,800,128]{2,1,0:T(8,128)(2,1)S(1)}, bf16[2,800,128]{2,1,0:T(8,128)(2,1)S(1)}, u32[]{:S(2)}, u32[]{:S(2)}) %collective-permute-start.19) | collective-permute-done | bytes 409632 | tf_op jit(solution)/shard_map/ppermute | solution.py:31
  52.1 0.6 collective-permute-done.20.refs_12_
  52.7 1.7 %project0.1.refs_4_ = bf16[96,1280]{1,0:T(8,128)(2,1)S(1)} custom-call(s32[3]{0:T(128)S(1)} %pad_add_fusion.1.index_ref, bf16[240,128]{1,0:T(8,128)(2,1)S(1)} %get-tuple-element.82.refs_0_, bf16[240,128]{1,0:T(8,128)(2,1)S(1)} %collective-permute-done.11.refs_1_, bf16[240,128]{1,0:T(8,128)(2,1)S(1)} %collective-permute-done.12.refs_2_, ...), custom_call_target="tpu_custom_call" | custom-call | flops 2000000000 | bytes 6600000 | tf_op jit(solution)/shard_map/project0/pallas_call | solution.py:378
  54.6 2.4 %collective-permute-start.15 = (bf16[240,128]{1,0:T(8,128)(2,1)S(1)}, bf16[240,128]{1,0:T(8,128)(2,1)S(1)}, u32[]{:S(2)}, u32[]{:S(2)}) collective-permute-start(bf16[240,128]{1,0:T(8,128)(2,1)S(1)} %get-tuple-element.80), channel_id=1, source_target_pairs={{0,2},{1,3},{2,0},{3,1},{4,6},{5,7},{6,4},{7,5},{8,10},{9,11},{10,... | collective-permute-start | bytes 184328 | tf_op jit(solution)/shard_map/ppermute | solution.py:31
  57.0 2.0 %collective-permute-start.16 = (bf16[240,128]{1,0:T(8,128)(2,1)S(1)}, bf16[240,128]{1,0:T(8,128)(2,1)S(1)}, u32[]{:S(2)}, u32[]{:S(2)}) collective-permute-start(bf16[240,128]{1,0:T(8,128)(2,1)S(1)} %get-tuple-element.81), channel_id=1, source_target_pairs={{0,3},{1,2},{2,1},{3,0},{4,7},{5,6},{6,5},{7,4},{8,11},{9,10},{10,... | collective-permute-start | bytes 184328 | tf_op jit(solution)/shard_map/ppermute | solution.py:31
  59.9 2.4 %collective-permute-done.15.refs_2_ = bf16[240,128]{1,0:T(8,128)(2,1)S(1)} collective-permute-done((bf16[240,128]{1,0:T(8,128)(2,1)S(1)}, bf16[240,128]{1,0:T(8,128)(2,1)S(1)}, u32[]{:S(2)}, u32[]{:S(2)}) %collective-permute-start.15) | collective-permute-done | bytes 61472 | tf_op jit(solution)/shard_map/ppermute | solution.py:31
  62.3 0.8 %collective-permute-done.16.refs_3_ = bf16[240,128]{1,0:T(8,128)(2,1)S(1)} collective-permute-done((bf16[240,128]{1,0:T(8,128)(2,1)S(1)}, bf16[240,128]{1,0:T(8,128)(2,1)S(1)}, u32[]{:S(2)}, u32[]{:S(2)}) %collective-permute-start.16) | collective-permute-done | bytes 61472 | tf_op jit(solution)/shard_map/ppermute | solution.py:31
  63.1 1.6 %project1.1.refs_5_ = bf16[96,1280]{1,0:T(8,128)(2,1)S(1)} custom-call(s32[3]{0:T(128)S(1)} %pad_add_fusion.1.index_ref, bf16[240,128]{1,0:T(8,128)(2,1)S(1)} %get-tuple-element.92.refs_0_, bf16[240,128]{1,0:T(8,128)(2,1)S(1)} %collective-permute-done.14.refs_1_, bf16[240,128]{1,0:T(8,128)(2,1)S(1)} %collective-permute-done.15.refs_2_, ...), custom_call_target="tpu_custom_call" | custom-call | flops 2000000000 | bytes 6600000 | tf_op jit(solution)/shard_map/project1/pallas_call | solution.py:378
  64.8 0.7 collective-permute-start.26
  65.5 1.4 %collective-permute-start.22 = (s32[1,192]{1,0:T(1,128)S(1)}, s32[1,192]{1,0:T(1,128)S(1)}, u32[]{:S(2)}, u32[]{:S(2)}) collective-permute-start(s32[1,192]{1,0:T(1,128)S(1)} %bitcast.25), channel_id=1, source_target_pairs={{0,8},{4,12},{8,0},{12,4},{1,9},{5,13},{9,1},{13,5},{2,10},{6,14},... | collective-permute-start | bytes 2312 | tf_op jit(solution)/shard_map/ppermute | solution.py:31
  67.4 4.2 %collective-permute-done.26.refs_9_ = bf16[96,1280]{1,0:T(8,128)(2,1)S(1)} collective-permute-done((bf16[96,1280]{1,0:T(8,128)(2,1)S(1)}, bf16[96,1280]{1,0:T(8,128)(2,1)S(1)}, u32[]{:S(2)}, u32[]{:S(2)}) %collective-permute-start.26) | collective-permute-done | bytes 245792 | tf_op jit(solution)/shard_map/ppermute | solution.py:31
  72.2 0.9 %collective-permute-done.23 = s32[2,1,192]{2,1,0:T(1,128)S(1)} collective-permute-done((s32[2,1,192]{2,1,0:T(1,128)S(1)}, s32[2,1,192]{2,1,0:T(1,128)S(1)}, u32[]{:S(2)}, u32[]{:S(2)}) %collective-permute-start.23) | collective-permute-done | bytes 1568 | tf_op jit(solution)/shard_map/ppermute | solution.py:31
  73.2 1.9 %placement.1 = bf16[192,1280]{1,0:T(8,128)(2,1)} custom-call(s32[3]{0:T(128)S(1)} %pad_add_fusion.1.index_ref, s32[1,192]{1,0:T(1,128)S(1)} %bitcast.27, s32[1,192]{1,0:T(1,128)S(1)} %get-tuple-element.98.refs_1_, s32[1,192]{1,0:T(1,128)S(1)} %collective-permute-done.22.refs_2_, s32[1,192]{1,0:T(1,128)S(1)} %get-tuple-element.97.refs_3_, ...), custom_call_target="tpu_custom_call" | custom-call | flops 2000000000 | bytes 6600000 | tf_op jit(solution)/shard_map/placement/pallas_call | solution.py:394
  (53 shorter events, 5.2 us)
Async XLA Ops:
  2.1 27.8 %copy-start.1 = (bf16[768,1280]{1,0:T(8,128)(2,1)S(1)}, bf16[768,1280]{1,0:T(8,128)(2,1)}, u32[]{:S(2)}) copy-start(bf16[768,1280]{1,0:T(8,128)(2,1)} %patches_any) | copy-start | bytes 5898244
  2.1 27.8 %copy-start.4 = (f32[1280]{0:T(1024)S(1)}, f32[1280]{0:T(1024)}, u32[]{:S(2)}) copy-start(f32[1280]{0:T(1024)} %gain_ref.1) | copy-start | bytes 15364
  4.4 9.0 %collective-permute-start.1 = (bf16[3,800,128]{2,1,0:T(8,128)(2,1)S(1)}, bf16[3,800,128]{2,1,0:T(8,128)(2,1)S(1)}, u32[]{:S(2)}, u32[]{:S(2)}) collective-permute-start(bf16[3,800,128]{2,1,0:T(8,128)(2,1)S(1)} %get-tuple-element.52.refs_0_), channel_id=1, source_target_pairs={{0,4},{4,0},{8,12},{12,8},{1,5},{5,1},{9,13},{13,9},{2,6},{6,2},{1... | collective-permute-start | bytes 1843208 | tf_op jit(solution)/shard_map/ppermute | solution.py:31
  4.9 8.5 %collective-permute-start = (bf16[800,128]{1,0:T(8,128)(2,1)S(1)}, bf16[800,128]{1,0:T(8,128)(2,1)S(1)}, u32[]{:S(2)}, u32[]{:S(2)}) collective-permute-start(bf16[800,128]{1,0:T(8,128)(2,1)S(1)} %get-tuple-element.51), channel_id=1, source_target_pairs={{0,8},{4,12},{8,0},{12,4},{1,9},{5,13},{9,1},{13,5},{2,10},{6,14},... | collective-permute-start | bytes 614408 | tf_op jit(solution)/shard_map/ppermute | solution.py:31
  7.5 12.0 %collective-permute-start.3 = (bf16[800,128]{1,0:T(8,128)(2,1)S(1)}, bf16[800,128]{1,0:T(8,128)(2,1)S(1)}, u32[]{:S(2)}, u32[]{:S(2)}) collective-permute-start(bf16[800,128]{1,0:T(8,128)(2,1)S(1)} %get-tuple-element.57), channel_id=1, source_target_pairs={{0,8},{4,12},{8,0},{12,4},{1,9},{5,13},{9,1},{13,5},{2,10},{6,14},... | collective-permute-start | bytes 614408 | tf_op jit(solution)/shard_map/ppermute | solution.py:31
  13.4 6.6 %collective-permute-start.2 = (bf16[800,128]{1,0:T(8,128)(2,1)S(1)}, bf16[800,128]{1,0:T(8,128)(2,1)S(1)}, u32[]{:S(2)}, u32[]{:S(2)}) collective-permute-start(bf16[800,128]{1,0:T(8,128)(2,1)S(1)} %collective-permute-done.refs_2_), channel_id=1, source_target_pairs={{0,16},{16,0},{1,17},{17,1},{2,18},{18,2},{3,19},{19,3},{4,20},{20... | collective-permute-start | bytes 614408 | tf_op jit(solution)/shard_map/ppermute | solution.py:31
  15.4 4.7 %collective-permute-start.4 = (bf16[800,128]{1,0:T(8,128)(2,1)S(1)}, bf16[800,128]{1,0:T(8,128)(2,1)S(1)}, u32[]{:S(2)}, u32[]{:S(2)}) collective-permute-start(bf16[800,128]{1,0:T(8,128)(2,1)S(1)} %collective-permute-done.refs_2_), channel_id=1, source_target_pairs={{0,4},{4,0},{8,12},{12,8},{1,5},{5,1},{9,13},{13,9},{2,6},{6,2},{1... | collective-permute-start | bytes 614408 | tf_op jit(solution)/shard_map/ppermute | solution.py:31
  15.4 11.8 %collective-permute-start.9 = (bf16[800,128]{1,0:T(8,128)(2,1)S(1)}, bf16[800,128]{1,0:T(8,128)(2,1)S(1)}, u32[]{:S(2)}, u32[]{:S(2)}) collective-permute-start(bf16[800,128]{1,0:T(8,128)(2,1)S(1)} %get-tuple-element.86.refs_4_), channel_id=1, source_target_pairs={{0,1},{1,0},{2,3},{3,2},{4,5},{5,4},{6,7},{7,6},{8,9},{9,8},{10,11... | collective-permute-start | bytes 614408 | tf_op jit(solution)/shard_map/ppermute | solution.py:31
  16.9 12.5 %collective-permute-start.7 = (bf16[800,128]{1,0:T(8,128)(2,1)S(1)}, bf16[800,128]{1,0:T(8,128)(2,1)S(1)}, u32[]{:S(2)}, u32[]{:S(2)}) collective-permute-start(bf16[800,128]{1,0:T(8,128)(2,1)S(1)} %get-tuple-element.86.refs_4_), channel_id=1, source_target_pairs={{0,2},{1,3},{2,0},{3,1},{16,19},{17,18},{18,17},{19,16},{4,6},{5,7... | collective-permute-start | bytes 614408 | tf_op jit(solution)/shard_map/ppermute | solution.py:297
  20.0 12.1 %collective-permute-start.5 = (bf16[800,128]{1,0:T(8,128)(2,1)S(1)}, bf16[800,128]{1,0:T(8,128)(2,1)S(1)}, u32[]{:S(2)}, u32[]{:S(2)}) collective-permute-start(bf16[800,128]{1,0:T(8,128)(2,1)S(1)} %collective-permute-done.2.refs_3_), channel_id=1, source_target_pairs={{0,4},{4,0},{8,12},{12,8},{1,5},{5,1},{9,13},{13,9},{2,6},{6,2},{1... | collective-permute-start | bytes 614408 | tf_op jit(solution)/shard_map/ppermute | solution.py:31
  20.0 12.1 %collective-permute-start.6 = (bf16[800,128]{1,0:T(8,128)(2,1)S(1)}, bf16[800,128]{1,0:T(8,128)(2,1)S(1)}, u32[]{:S(2)}, u32[]{:S(2)}) collective-permute-start(bf16[800,128]{1,0:T(8,128)(2,1)S(1)} %collective-permute-done.3.refs_4_), channel_id=1, source_target_pairs={{0,4},{4,0},{8,12},{12,8},{1,5},{5,1},{9,13},{13,9},{2,6},{6,2},{1... | collective-permute-start | bytes 614408 | tf_op jit(solution)/shard_map/ppermute | solution.py:31
  27.2 11.2 %collective-permute-start.10 = (bf16[2,800,128]{2,1,0:T(8,128)(2,1)S(1)}, bf16[2,800,128]{2,1,0:T(8,128)(2,1)S(1)}, u32[]{:S(2)}, u32[]{:S(2)}) collective-permute-start(bf16[2,800,128]{2,1,0:T(8,128)(2,1)S(1)} %pad_maximum_fusion.1), channel_id=1, source_target_pairs={{0,8},{4,12},{8,0},{12,4},{1,9},{5,13},{9,1},{13,5},{2,10},{6,14},... | collective-permute-start | bytes 1228808 | tf_op jit(solution)/shard_map/ppermute | solution.py:31
  29.5 7.2 %collective-permute-start.8 = (bf16[800,128]{1,0:T(8,128)(2,1)S(1)}, bf16[800,128]{1,0:T(8,128)(2,1)S(1)}, u32[]{:S(2)}, u32[]{:S(2)}) collective-permute-start(bf16[800,128]{1,0:T(8,128)(2,1)S(1)} %collective-permute-done.7.refs_6_), channel_id=1, source_target_pairs={{0,16},{16,0},{1,17},{17,1},{2,18},{18,2},{3,19},{19,3},{4,20},{20... | collective-permute-start | bytes 614408 | tf_op jit(solution)/shard_map/ppermute | solution.py:31
  38.3 6.0 %collective-permute-start.11 = (bf16[240,128]{1,0:T(8,128)(2,1)S(1)}, bf16[240,128]{1,0:T(8,128)(2,1)S(1)}, u32[]{:S(2)}, u32[]{:S(2)}) collective-permute-start(bf16[240,128]{1,0:T(8,128)(2,1)S(1)} %get-tuple-element.66), channel_id=1, source_target_pairs={{0,1},{1,0},{2,3},{3,2},{4,5},{5,4},{6,7},{7,6},{8,9},{9,8},{10,11... | collective-permute-start | bytes 184328 | tf_op jit(solution)/shard_map/ppermute | solution.py:31
  38.4 11.3 %collective-permute-start.18 = (bf16[2,800,128]{2,1,0:T(8,128)(2,1)S(1)}, bf16[2,800,128]{2,1,0:T(8,128)(2,1)S(1)}, u32[]{:S(2)}, u32[]{:S(2)}) collective-permute-start(bf16[2,800,128]{2,1,0:T(8,128)(2,1)S(1)} %pad_maximum_fusion.2), channel_id=1, source_target_pairs={{0,8},{4,12},{8,0},{12,4},{1,9},{5,13},{9,1},{13,5},{2,10},{6,14},... | collective-permute-start | bytes 1228808 | tf_op jit(solution)/shard_map/ppermute | solution.py:31
  40.0 8.4 %collective-permute-start.12 = (bf16[240,128]{1,0:T(8,128)(2,1)S(1)}, bf16[240,128]{1,0:T(8,128)(2,1)S(1)}, u32[]{:S(2)}, u32[]{:S(2)}) collective-permute-start(bf16[240,128]{1,0:T(8,128)(2,1)S(1)} %get-tuple-element.75), channel_id=1, source_target_pairs={{0,2},{1,3},{2,0},{3,1},{4,6},{5,7},{6,4},{7,5},{8,10},{9,11},{10,... | collective-permute-start | bytes 184328 | tf_op jit(solution)/shard_map/ppermute | solution.py:31
  43.0 6.0 %collective-permute-start.13 = (bf16[240,128]{1,0:T(8,128)(2,1)S(1)}, bf16[240,128]{1,0:T(8,128)(2,1)S(1)}, u32[]{:S(2)}, u32[]{:S(2)}) collective-permute-start(bf16[240,128]{1,0:T(8,128)(2,1)S(1)} %get-tuple-element.76), channel_id=1, source_target_pairs={{0,3},{1,2},{2,1},{3,0},{4,7},{5,6},{6,5},{7,4},{8,11},{9,10},{10,... | collective-permute-start | bytes 184328 | tf_op jit(solution)/shard_map/ppermute | solution.py:31
  49.1 3.6 %collective-permute-start.17 = (bf16[4,800,128]{2,1,0:T(8,128)(2,1)S(1)}, bf16[4,800,128]{2,1,0:T(8,128)(2,1)S(1)}, u32[]{:S(2)}, u32[]{:S(2)}) collective-permute-start(bf16[4,800,128]{2,1,0:T(8,128)(2,1)S(1)} %pad_maximum_fusion), channel_id=1, source_target_pairs={{0,4},{4,0},{8,12},{12,8},{1,5},{5,1},{9,13},{13,9},{2,6},{6,2},{1... | collective-permute-start | bytes 2457608 | tf_op jit(solution)/shard_map/ppermute | solution.py:31
  49.2 2.9 %collective-permute-start.19 = (bf16[2,800,128]{2,1,0:T(8,128)(2,1)S(1)}, bf16[2,800,128]{2,1,0:T(8,128)(2,1)S(1)}, u32[]{:S(2)}, u32[]{:S(2)}) collective-permute-start(bf16[2,800,128]{2,1,0:T(8,128)(2,1)S(1)} %collective-permute-done.10.refs_9_), channel_id=1, source_target_pairs={{0,4},{4,0},{8,12},{12,8},{1,5},{5,1},{9,13},{13,9},{2,6},{6,2},{1... | collective-permute-start | bytes 1228808 | tf_op jit(solution)/shard_map/ppermute | solution.py:31
  49.7 3.0 %collective-permute-start.20 = (bf16[2,800,128]{2,1,0:T(8,128)(2,1)S(1)}, bf16[2,800,128]{2,1,0:T(8,128)(2,1)S(1)}, u32[]{:S(2)}, u32[]{:S(2)}) collective-permute-start(bf16[2,800,128]{2,1,0:T(8,128)(2,1)S(1)} %collective-permute-done.18.refs_10_), channel_id=1, source_target_pairs={{0,4},{4,0},{8,12},{12,8},{1,5},{5,1},{9,13},{13,9},{2,6},{6,2},{1... | collective-permute-start | bytes 1228808 | tf_op jit(solution)/shard_map/ppermute | solution.py:31
  54.4 11.1 %copy-start = (s32[192]{0:T(256)S(1)}, s32[192]{0:T(256)}, u32[]{:S(2)}) copy-start(s32[192]{0:T(256)} %param.9) | copy-start | bytes 2308
  54.4 8.8 %collective-permute-start.21 = (bf16[96,1280]{1,0:T(8,128)(2,1)S(1)}, bf16[96,1280]{1,0:T(8,128)(2,1)S(1)}, u32[]{:S(2)}, u32[]{:S(2)}) collective-permute-start(bf16[96,1280]{1,0:T(8,128)(2,1)S(1)} %project0.1.refs_4_), channel_id=1, source_target_pairs={{0,4},{4,0},{8,12},{12,8},{1,5},{5,1},{9,13},{13,9},{2,6},{6,2},{1... | collective-permute-start | bytes 737288 | tf_op jit(solution)/shard_map/ppermute | solution.py:31
  54.6 5.3 %collective-permute-start.14 = (bf16[240,128]{1,0:T(8,128)(2,1)S(1)}, bf16[240,128]{1,0:T(8,128)(2,1)S(1)}, u32[]{:S(2)}, u32[]{:S(2)}) collective-permute-start(bf16[240,128]{1,0:T(8,128)(2,1)S(1)} %get-tuple-element.79), channel_id=1, source_target_pairs={{0,1},{1,0},{2,3},{3,2},{4,5},{5,4},{6,7},{7,6},{8,9},{9,8},{10,11... | collective-permute-start | bytes 184328 | tf_op jit(solution)/shard_map/ppermute | solution.py:31
  54.6 7.7 %collective-permute-start.15 = (bf16[240,128]{1,0:T(8,128)(2,1)S(1)}, bf16[240,128]{1,0:T(8,128)(2,1)S(1)}, u32[]{:S(2)}, u32[]{:S(2)}) collective-permute-start(bf16[240,128]{1,0:T(8,128)(2,1)S(1)} %get-tuple-element.80), channel_id=1, source_target_pairs={{0,2},{1,3},{2,0},{3,1},{4,6},{5,7},{6,4},{7,5},{8,10},{9,11},{10,... | collective-permute-start | bytes 184328 | tf_op jit(solution)/shard_map/ppermute | solution.py:31
  57.0 6.1 %collective-permute-start.16 = (bf16[240,128]{1,0:T(8,128)(2,1)S(1)}, bf16[240,128]{1,0:T(8,128)(2,1)S(1)}, u32[]{:S(2)}, u32[]{:S(2)}) collective-permute-start(bf16[240,128]{1,0:T(8,128)(2,1)S(1)} %get-tuple-element.81), channel_id=1, source_target_pairs={{0,3},{1,2},{2,1},{3,0},{4,7},{5,6},{6,5},{7,4},{8,11},{9,10},{10,... | collective-permute-start | bytes 184328 | tf_op jit(solution)/shard_map/ppermute | solution.py:31
  59.0 7.9 %collective-permute-start.25 = (bf16[96,1280]{1,0:T(8,128)(2,1)S(1)}, bf16[96,1280]{1,0:T(8,128)(2,1)S(1)}, u32[]{:S(2)}, u32[]{:S(2)}) collective-permute-start(bf16[96,1280]{1,0:T(8,128)(2,1)S(1)} %project0.1.refs_4_), channel_id=1, source_target_pairs={{0,8},{4,12},{8,0},{12,4},{1,9},{5,13},{9,1},{13,5},{2,10},{6,14},... | collective-permute-start | bytes 737288 | tf_op jit(solution)/shard_map/ppermute | solution.py:31
  64.8 6.8 %collective-permute-start.26 = (bf16[96,1280]{1,0:T(8,128)(2,1)S(1)}, bf16[96,1280]{1,0:T(8,128)(2,1)S(1)}, u32[]{:S(2)}, u32[]{:S(2)}) collective-permute-start(bf16[96,1280]{1,0:T(8,128)(2,1)S(1)} %project1.1.refs_5_), channel_id=1, source_target_pairs={{0,8},{4,12},{8,0},{12,4},{1,9},{5,13},{9,1},{13,5},{2,10},{6,14},... | collective-permute-start | bytes 737288 | tf_op jit(solution)/shard_map/ppermute | solution.py:31
  65.5 6.2 %collective-permute-start.22 = (s32[1,192]{1,0:T(1,128)S(1)}, s32[1,192]{1,0:T(1,128)S(1)}, u32[]{:S(2)}, u32[]{:S(2)}) collective-permute-start(s32[1,192]{1,0:T(1,128)S(1)} %bitcast.25), channel_id=1, source_target_pairs={{0,8},{4,12},{8,0},{12,4},{1,9},{5,13},{9,1},{13,5},{2,10},{6,14},... | collective-permute-start | bytes 2312 | tf_op jit(solution)/shard_map/ppermute | solution.py:31
  66.9 6.3 %collective-permute-start.24 = (bf16[96,1280]{1,0:T(8,128)(2,1)S(1)}, bf16[96,1280]{1,0:T(8,128)(2,1)S(1)}, u32[]{:S(2)}, u32[]{:S(2)}) collective-permute-start(bf16[96,1280]{1,0:T(8,128)(2,1)S(1)} %project1.1.refs_5_), channel_id=1, source_target_pairs={{0,4},{4,0},{8,12},{12,8},{1,5},{5,1},{9,13},{13,9},{2,6},{6,2},{1... | collective-permute-start | bytes 737288 | tf_op jit(solution)/shard_map/ppermute | solution.py:31
  66.9 6.3 %collective-permute-start.27 = (bf16[96,1280]{1,0:T(8,128)(2,1)S(1)}, bf16[96,1280]{1,0:T(8,128)(2,1)S(1)}, u32[]{:S(2)}, u32[]{:S(2)}) collective-permute-start(bf16[96,1280]{1,0:T(8,128)(2,1)S(1)} %collective-permute-done.25.refs_8_), channel_id=1, source_target_pairs={{0,4},{4,0},{8,12},{12,8},{1,5},{5,1},{9,13},{13,9},{2,6},{6,2},{1... | collective-permute-start | bytes 737288 | tf_op jit(solution)/shard_map/ppermute | solution.py:31
  71.6 1.5 %collective-permute-start.28 = (bf16[96,1280]{1,0:T(8,128)(2,1)S(1)}, bf16[96,1280]{1,0:T(8,128)(2,1)S(1)}, u32[]{:S(2)}, u32[]{:S(2)}) collective-permute-start(bf16[96,1280]{1,0:T(8,128)(2,1)S(1)} %collective-permute-done.26.refs_9_), channel_id=1, source_target_pairs={{0,4},{4,0},{8,12},{12,8},{1,5},{5,1},{9,13},{13,9},{2,6},{6,2},{1... | collective-permute-start | bytes 737288 | tf_op jit(solution)/shard_map/ppermute | solution.py:31
  71.7 1.5 %collective-permute-start.23 = (s32[2,1,192]{2,1,0:T(1,128)S(1)}, s32[2,1,192]{2,1,0:T(1,128)S(1)}, u32[]{:S(2)}, u32[]{:S(2)}) collective-permute-start(s32[2,1,192]{2,1,0:T(1,128)S(1)} %pad_add_fusion), channel_id=1, source_target_pairs={{0,4},{4,0},{8,12},{12,8},{1,5},{5,1},{9,13},{13,9},{2,6},{6,2},{1... | collective-permute-start | bytes 4616 | tf_op jit(solution)/shard_map/ppermute | solution.py:31
  (4 other events, 15.4 us)

commit v7 on v5

--- a/solution.py
+++ b/solution.py
@@ -84,12 +84,15 @@
     return jnp.concatenate([p[:rows], p[rows : 2 * rows]], axis=1), rest
 
 
-def pack_kernel(index_ref, qkv_ref, proj_ref, first_ref, value_ref, all_ref, proj_out_ref):
+def pack_kernel(index_ref, qkv_ref, first_ref, value_ref, all_ref):
     for j in range(3):
         all_ref[j] = pack(qkv_ref[j])
     first_ref[...] = all_ref[index_ref[2]]
     value_ref[...] = all_ref[2]
-    proj_out_ref[...] = pack(proj_ref[...])
+
+
+def pack_proj_kernel(proj_ref, out_ref):
+    out_ref[...] = pack(proj_ref[...])
 
 
 def norm_kernel(index_ref, patches_ref, gain_ref, hidden_ref, own_ref):
@@ -97,7 +100,8 @@
     x = patches_ref[...]
     xf = x.astype(F32)
     mean_sq = jnp.mean(xf * xf, axis=-1, keepdims=True)
-    hidden_ref[...] = (xf * lax.rsqrt(mean_sq + 1e-06) * gain_ref[...]).astype(BF16)
+    gain = gain_ref[...].reshape(1, -1)
+    hidden_ref[...] = (xf * lax.rsqrt(mean_sq + 1e-06) * gain).astype(BF16)
     step = 256
     pick = step // 4
     row = lax.broadcasted_iota(jnp.int32, (pick, step), 0)
@@ -183,6 +187,11 @@
 
 def project_kernel(n_ctx, row0, width, col, index_ref, *refs):
     mixes = [unpack(m[...], refs[-2].shape[0], width) for m in refs[:4]]
+    flip = index_ref[2] > 0
+    mixes[2:] = [
+        [jnp.where(flip, b, a) for a, b in zip(mixes[2], mixes[3])],
+        [jnp.where(flip, a, b) for a, b in zip(mixes[2], mixes[3])],
+    ]
     *blocks, own_ref, gain_ref, out_ref, part_ref = refs[4:]
     rows = out_ref.shape[0]
     me = index_ref[0]
@@ -212,7 +221,7 @@
     total = jnp.concatenate([part_ref[i] for i in range(n_ctx)], axis=1)
     total = total + own_ref[row0 : row0 + rows, :].astype(F32)
     mean_sq = jnp.mean(total * total, axis=-1, keepdims=True)
-    out_ref[...] = (total * lax.rsqrt(mean_sq + 1e-06) * gain_ref[...]).astype(BF16)
+    out_ref[...] = (total * lax.rsqrt(mean_sq + 1e-06) * gain_ref[...].reshape(1, -1)).astype(BF16)
 
 
 def place_kernel(n_ctx, index_ref, *refs):
@@ -250,19 +259,39 @@
 
     third = packed_shape(depth, width)
     piece = packed_shape(width, col)
-    first, value, own, w_proj = pl.pallas_call(
+    first, value, own = pl.pallas_call(
         pack_kernel,
-        out_shape=(shape(*third), shape(*third), shape(3, *third), shape(*piece)),
-        in_specs=[SMEM, VMEM, VMEM],
-        out_specs=(VMEM,) * 4,
+        out_shape=(shape(*third), shape(*third), shape(3, *third)),
+        in_specs=[SMEM, VMEM],
+        out_specs=(VMEM,) * 3,
         compiler_params=params(8),
         name="pack",
-    )(index, jnp.transpose(w_qkv, (1, 0, 2)), w_proj)
+    )(index, jnp.transpose(w_qkv, (1, 0, 2)))
+    w_proj = pl.pallas_call(
+        pack_proj_kernel,
+        out_shape=shape(*piece),
+        in_specs=[VMEM],
+        out_specs=VMEM,
+        compiler_params=params(8),
+        name="pack_proj",
+    )(w_proj)
     first = gather_cross(first, n_ctx)
     value = gather_cross(value, n_ctx)
     twin = over_core(own)
+    far = lax.ppermute(
+        w_proj,
+        ("dp", "tensor"),
+        [
+            (d * n_ten + t, d * n_ten + (t ^ (2 + d % 2)))
+            for d in range(n_dp)
+            for t in range(n_ten)
+        ],
+    )
     by_one = swap(w_proj, "tensor", n_ten, 1)
-    by_two = swap(w_proj, "tensor", n_ten, 2)
+    first, twin, patches = together(first, twin, patches)
+
+    second = {k: over_dp(first[k]) for k in cross}
+    first_twin = {k: over_core(first[k]) for k in cross}
     hidden, own_patches = pl.pallas_call(
         norm_kernel,
         out_shape=(shape(rows, feat), shape(groups, feat)),
@@ -270,20 +299,13 @@
         out_specs=(VMEM, VMEM),
         compiler_params=params(16),
         name="norm",
-    )(index, patches, gain_attn.reshape(1, feat))
-    first, twin, hidden = together(first, twin, hidden)
-
-    second = {k: over_dp(first[k]) for k in cross}
-    first_twin = {k: over_core(first[k]) for k in cross}
-    by_one, first = together(by_one, first)
+    )(index, patches, gain_attn)
     low = gather_cross(jnp.stack([w_proj, by_one]), n_ctx)
-    second, value, first_twin = together(second, value, first_twin)
+    second, value, first_twin, hidden = together(second, value, first_twin, hidden)
 
     second_twin = {k: over_core(second[k]) for k in cross}
     value_twin = {k: over_core(value[k]) for k in cross}
-    by_two, w_proj, place = together(by_two, w_proj, place, second, value)[:3]
-    by_three = swap(w_proj, "tensor", n_ten, 3)
-    places = gather_cross(place.reshape(1, groups), n_ctx)
+    far2 = over_dp(far)
 
     shard_list = [own, twin]
     for k in cross:
@@ -291,7 +313,6 @@
 
     valid_pairs = valid.reshape(rows // PAIR, PAIR)
     part = rows // CHUNKS
-    gain2 = gain_merge.reshape(1, feat)
     mix_shapes = (shape(*packed_shape(part // 4, width)),) * n_ten
     scratch = [pltpu.VMEM((part, width), BF16)] * 3 + [pltpu.VMEM((4, part // 4, width), BF16)]
     *mixed, w_full = pl.pallas_call(
@@ -307,11 +328,10 @@
     def exchange(pieces):
         return [pieces[0]] + [swap(pieces[s], "tensor", n_ten, s) for s in range(1, n_ten)]
 
-    mixed, by_three, low, places = together(mixed, by_three, low, places)
+    mixed, far, far2, low = together(mixed, far, far2, low)
     received = [exchange(mixed)]
-    high = gather_cross(jnp.stack([by_two, by_three]), n_ctx)
-    own_twin = over_core(jnp.stack([w_proj, by_one, by_two, by_three]))
-    place_twin = over_core(jnp.stack([places[k] for k in (0, *cross)]))
+    high = gather_cross(jnp.stack([far, far2]), n_ctx)
+    own_twin = None
     for r in range(1, CHUNKS):
         received[r - 1][1], hidden = together(received[r - 1][1], hidden)
         mixed = pl.pallas_call(
@@ -323,11 +343,14 @@
             compiler_params=params(12),
             name="attention" + str(r),
         )(index, hidden, valid_pairs, w_full)
-        mixed, received[r - 1], own_twin, low = together(mixed, received[r - 1], own_twin, low)
+        mixed, received[r - 1], low, w_proj = together(mixed, received[r - 1], low, w_proj)
         received.append(exchange(mixed))
-    high, received[-1][1], place_twin = together(high, received[-1][1], place_twin)
-
-    blocks = [w_proj, by_one, by_two, by_three, own_twin]
+        if own_twin is None:
+            own_twin = over_core(jnp.stack([w_proj, by_one, far, far2]))
+
+    high, received[-1][1] = together(high, received[-1][1])
+
+    blocks = [w_proj, by_one, far, far2, own_twin]
     for k in cross:
         blocks += [low[k], high[k], over_core(low[k]), over_core(high[k])]
     gathered = []
@@ -342,8 +365,16 @@
             scratch_shapes=[pltpu.VMEM((n_ctx, part // 4, col), F32)],
             compiler_params=params(20),
             name="project" + str(r),
-        )(index, *received[r], *blocks, own_patches, gain2)
-        gathered.append(gather_xor(done, n_ctx))
+        )(index, *received[r], *blocks, own_patches, gain_merge)
+        crossed = gather_cross(done, n_ctx)
+        if r > 0:
+            for k in cross:
+                crossed[k], gathered[r - 1][k ^ 1] = together(crossed[k], gathered[r - 1][k ^ 1])
+        for k in list(crossed):
+            crossed[k ^ 1] = over_core(crossed[k])
+        gathered.append(crossed)
+    places = gather_cross(place.reshape(1, groups), n_ctx)
+    place_twin = over_core(jnp.stack([places[k] for k in (0, *cross)]))
     place_list = []
     for i, k in enumerate((0, *cross)):
         place_list += [places[k], place_twin[i]]

time: 69.2 us -> 67.7 us (0.978)
  starting transfers between devices: 27.6 us -> 25.3 us
  waiting for transfers between devices: 20.7 us -> 22.4 us
  local copies, waits for them, and re-layouts: 4.32 us -> 2.9 us
    ppermute x29 -> x28, starting transfers between devices: 27.6 us -> 22.8 us  [swap(): return lax.ppermute(x, axis, [(i, i ^ bit) for i in range(size)])]
    ppermute x0 -> x1, starting transfers between devices: none -> 2.59 us  [local(): lax.ppermute(w_proj, ('dp', 'tensor'), [(d * n_ten + t, d * n_ten + (t ^...]
    ppermute x29 -> x28, waiting for transfers between devices: 20.7 us -> 22.4 us  [swap(): return lax.ppermute(x, axis, [(i, i ^ bit) for i in range(size)])]
    unnamed x12 -> x14, local copies, waits for them, and re-layouts: 3.62 us -> 2.9 us
    reshape x2 -> x0, local copies, waits for them, and re-layouts: 0.7 us -> none  [the longest x1 0.7 us: local(): gain_attn.reshape(1, feat)]
  transfers between devices with their start and end apart: 29 -> 29, of which waited for: 10 -> 10; matrix products, arithmetic and copies ran while one was open for 1% -> 0% of each run, Pallas kernels for 19% -> 17%
where the time goes in v7:
time: 67.7 us; the launch traced here: 67.1 us
  starting transfers between devices  25.3 us (37%)
  waiting for transfers between devices  22.4 us (33%)
  Pallas kernels  16 us (24%)
  local copies, waits for them, and re-layouts  2.9 us (4%)
    ppermute x28, starting transfers between devices, swap(): return lax.ppermute(x, axis, [(i, i ^ bit) for i in range(size)])  22.8 us
    ppermute x28, waiting for transfers between devices, swap(): return lax.ppermute(x, axis, [(i, i ^ bit) for i in range(size)])  22.4 us
    pallas_call x1, Pallas kernels, local(): pl.pallas_call(functools.partial(first_attention_kernel, n_ctx, width), o...  4.51 us
    pallas_call x1, Pallas kernels, local(): pl.pallas_call(functools.partial(next_attention_kernel, r * part), out_sh...  3.97 us
    pallas_call x2, Pallas kernels, local(): pl.pallas_call(functools.partial(project_kernel, n_ctx, r * (part // 4),...  3.31 us
    unnamed x14, local copies, waits for them, and re-layouts  2.9 us
    ppermute x1, starting transfers between devices, local(): lax.ppermute(w_proj, ('dp', 'tensor'), [(d * n_ten + t, d * n_ten + (t ^...  2.59 us
    pallas_call x1, Pallas kernels, local(): pl.pallas_call(functools.partial(place_kernel, n_ctx), out_shape=shape(gr...  1.92 us
  transfers between devices with their start and end apart: 29, of which 10 were waited for; matrix products, arithmetic and copies ran while one was open for 0% of the time, Pallas kernels for 17%

profile of v7, /device:TPU:0, one launch (start us, length us, event | category | flops | bytes accessed | tf_op | source)
XLA Modules:
  0.0 67.1 jit_solution(17594048979010516602)
XLA Ops:
  0.1 1.2 %copy-done.1 = bf16[320,3,320]{2,0,1:T(8,128)(2,1)S(1)} copy-done((bf16[320,3,320]{2,0,1:T(8,128)(2,1)S(1)}, bf16[320,3,320]{2,0,1:T(8,128)(2,1)}, u32[]{:S(2)}) %copy-start.1) | copy-done | bytes 614424
  1.3 0.7 %pack.1 = (bf16[800,128]{1,0:T(8,128)(2,1)S(1)}, bf16[800,128]{1,0:T(8,128)(2,1)S(1)}, bf16[3,800,128]{2,1,0:T(8,128)(2,1)S(1)}) custom-call(s32[3]{0:T(128)S(1)} %pad_add_fusion.1.index_ref, bf16[3,320,320]{2,1,0:T(8,128)(2,1)S(1)} %bitcast.25), custom_call_target="tpu_custom_call" | custom-call | tf_op jit(solution)/shard_map/pack/pallas_call | solution.py:262
  2.0 0.5 collective-permute-start.3
  2.5 2.6 %collective-permute-start.2 = (bf16[800,128]{1,0:T(8,128)(2,1)S(1)}, bf16[800,128]{1,0:T(8,128)(2,1)S(1)}, u32[]{:S(2)}, u32[]{:S(2)}) collective-permute-start(bf16[800,128]{1,0:T(8,128)(2,1)S(1)} %get-tuple-element.53), channel_id=1, source_target_pairs={{0,8},{4,12},{8,0},{12,4},{1,9},{5,13},{9,1},{13,5},{2,10},{6,14},... | collective-permute-start | bytes 614408 | tf_op jit(solution)/shard_map/ppermute | solution.py:26
  5.1 0.9 %copy-done.2 = bf16[320,320]{1,0:T(8,128)(2,1)S(1)} copy-done((bf16[320,320]{1,0:T(8,128)(2,1)S(1)}, bf16[320,320]{1,0:T(8,128)(2,1)}, u32[]{:S(2)}) %copy-start.2) | copy-done | bytes 204824
  6.1 1.6 %collective-permute-start.11 = (bf16[800,128]{1,0:T(8,128)(2,1)S(1)}, bf16[800,128]{1,0:T(8,128)(2,1)S(1)}, u32[]{:S(2)}, u32[]{:S(2)}) collective-permute-start(bf16[800,128]{1,0:T(8,128)(2,1)S(1)} %pack_proj.1.refs_4_), channel_id=1, source_target_pairs={{0,1},{1,0},{2,3},{3,2},{4,5},{5,4},{6,7},{7,6},{8,9},{9,8},{10,11... | collective-permute-start | bytes 614408 | tf_op jit(solution)/shard_map/ppermute | solution.py:26
  7.8 2.6 %collective-permute-start.9 = (bf16[800,128]{1,0:T(8,128)(2,1)S(1)}, bf16[800,128]{1,0:T(8,128)(2,1)S(1)}, u32[]{:S(2)}, u32[]{:S(2)}) collective-permute-start(bf16[800,128]{1,0:T(8,128)(2,1)S(1)} %pack_proj.1.refs_4_), channel_id=1, source_target_pairs={{0,2},{1,3},{2,0},{3,1},{16,19},{17,18},{18,17},{19,16},{4,6},{5,7... | collective-permute-start | bytes 614408 | tf_op jit(solution)/shard_map/ppermute | solution.py:281
  10.4 0.5 collective-permute-start.5
  10.9 1.6 %collective-permute-start.4 = (bf16[800,128]{1,0:T(8,128)(2,1)S(1)}, bf16[800,128]{1,0:T(8,128)(2,1)S(1)}, u32[]{:S(2)}, u32[]{:S(2)}) collective-permute-start(bf16[800,128]{1,0:T(8,128)(2,1)S(1)} %collective-permute-done.2.refs_2_), channel_id=1, source_target_pairs={{0,16},{16,0},{1,17},{17,1},{2,18},{18,2},{3,19},{19,3},{4,20},{20... | collective-permute-start | bytes 614408 | tf_op jit(solution)/shard_map/ppermute | solution.py:26
  12.5 5.1 %collective-permute-done.11.refs_5_ = bf16[800,128]{1,0:T(8,128)(2,1)S(1)} collective-permute-done((bf16[800,128]{1,0:T(8,128)(2,1)S(1)}, bf16[800,128]{1,0:T(8,128)(2,1)S(1)}, u32[]{:S(2)}, u32[]{:S(2)}) %collective-permute-start.11) | collective-permute-done | bytes 204832 | tf_op jit(solution)/shard_map/ppermute | solution.py:26
  18.1 0.7 %copy-done.5 = f32[1280]{0:T(1024)S(1)} copy-done((f32[1280]{0:T(1024)S(1)}, f32[1280]{0:T(1024)}, u32[]{:S(2)}) %copy-start.5) | copy-done | bytes 5144
  18.8 1.5 %norm.1 = (bf16[768,1280]{1,0:T(8,128)(2,1)S(1)}, bf16[192,1280]{1,0:T(8,128)(2,1)S(1)}) custom-call(s32[3]{0:T(128)S(1)} %pad_add_fusion.1.index_ref, bf16[768,1280]{1,0:T(8,128)(2,1)S(1)} %copy-done, f32[1280]{0:T(1024)S(1)} %copy-done.5), custom_call_target="tpu_custom_call" | custom-call | tf_op jit(solution)/shard_map/norm/pallas_call | solution.py:295
  22.2 4.5 %attention0.1 = (bf16[240,128]{1,0:T(8,128)(2,1)S(1)}, bf16[240,128]{1,0:T(8,128)(2,1)S(1)}, bf16[240,128]{1,0:T(8,128)(2,1)S(1)}, bf16[240,128]{1,0:T(8,128)(2,1)S(1)}, bf16[1280,960]{1,0:T(8,128)(2,1)S(1)}) custom-call(s32[3]{0:T(128)S(1)} %pad_add_fusion.1.index_ref, bf16[768,1280]{1,0:T(8,128)(2,1)S(1)} %get-tuple-element.69.hidden_ref, ...), custom_call_target="tpu_custom_call" | custom-call | tf_op jit(solution)/shard_map/attention0/pallas_call | solution.py:318
  26.7 1.3 %collective-permute-done.10.refs_7_ = bf16[800,128]{1,0:T(8,128)(2,1)S(1)} collective-permute-done((bf16[800,128]{1,0:T(8,128)(2,1)S(1)}, bf16[800,128]{1,0:T(8,128)(2,1)S(1)}, u32[]{:S(2)}, u32[]{:S(2)}) %collective-permute-start.10) | collective-permute-done | bytes 204832 | tf_op jit(solution)/shard_map/ppermute | solution.py:26
  28.4 3.7 %collective-permute-start.14 = (bf16[240,128]{1,0:T(8,128)(2,1)S(1)}, bf16[240,128]{1,0:T(8,128)(2,1)S(1)}, u32[]{:S(2)}, u32[]{:S(2)}) collective-permute-start(bf16[240,128]{1,0:T(8,128)(2,1)S(1)} %get-tuple-element.77), channel_id=1, source_target_pairs={{0,2},{1,3},{2,0},{3,1},{4,6},{5,7},{6,4},{7,5},{8,10},{9,11},{10,... | collective-permute-start | bytes 184328 | tf_op jit(solution)/shard_map/ppermute | solution.py:26
  32.2 0.6 collective-permute-start.15
  32.9 1.3 %collective-permute-start.17 = (bf16[2,800,128]{2,1,0:T(8,128)(2,1)S(1)}, bf16[2,800,128]{2,1,0:T(8,128)(2,1)S(1)}, u32[]{:S(2)}, u32[]{:S(2)}) collective-permute-start(bf16[2,800,128]{2,1,0:T(8,128)(2,1)S(1)} %pad_maximum_fusion.2), channel_id=1, source_target_pairs={{0,8},{4,12},{8,0},{12,4},{1,9},{5,13},{9,1},{13,5},{2,10},{6,14},... | collective-permute-start | bytes 1228808 | tf_op jit(solution)/shard_map/ppermute | solution.py:26
  34.2 4.0 %attention1.1 = (bf16[240,128]{1,0:T(8,128)(2,1)S(1)}, bf16[240,128]{1,0:T(8,128)(2,1)S(1)}, bf16[240,128]{1,0:T(8,128)(2,1)S(1)}, bf16[240,128]{1,0:T(8,128)(2,1)S(1)}) custom-call(s32[3]{0:T(128)S(1)} %pad_add_fusion.1.index_ref, bf16[768,1280]{1,0:T(8,128)(2,1)S(1)} %get-tuple-element.69.hidden_ref, s32[6,128]{1,0:T(8,128)S(1)} %bitcast.27, ...), custom_call_target="tpu_custom_call" | custom-call | tf_op jit(solution)/shard_map/attention1/pallas_call | solution.py:337
  38.9 3.9 %collective-permute-done.18.refs_1_ = bf16[240,128]{1,0:T(8,128)(2,1)S(1)} collective-permute-done((bf16[240,128]{1,0:T(8,128)(2,1)S(1)}, bf16[240,128]{1,0:T(8,128)(2,1)S(1)}, u32[]{:S(2)}, u32[]{:S(2)}) %collective-permute-start.18) | collective-permute-done | bytes 61472 | tf_op jit(solution)/shard_map/ppermute | solution.py:26
  42.8 1.7 %collective-permute-done.20.refs_12_ = bf16[2,800,128]{2,1,0:T(8,128)(2,1)S(1)} collective-permute-done((bf16[2,800,128]{2,1,0:T(8,128)(2,1)S(1)}, bf16[2,800,128]{2,1,0:T(8,128)(2,1)S(1)}, u32[]{:S(2)}, u32[]{:S(2)}) %collective-permute-start.20) | collective-permute-done | bytes 409632 | tf_op jit(solution)/shard_map/ppermute | solution.py:26
  44.6 1.7 %project0.1.refs_4_ = bf16[96,1280]{1,0:T(8,128)(2,1)S(1)} custom-call(s32[3]{0:T(128)S(1)} %pad_add_fusion.1.index_ref, bf16[240,128]{1,0:T(8,128)(2,1)S(1)} %get-tuple-element.80.refs_0_, bf16[240,128]{1,0:T(8,128)(2,1)S(1)} %collective-permute-done.13.refs_1_, bf16[240,128]{1,0:T(8,128)(2,1)S(1)} %collective-permute-done.14.refs_2_, ...), custom_call_target="tpu_custom_call" | custom-call | tf_op jit(solution)/shard_map/project0/pallas_call | solution.py:360
  46.2 1.6 %collective-permute-start.25 = (bf16[96,1280]{1,0:T(8,128)(2,1)S(1)}, bf16[96,1280]{1,0:T(8,128)(2,1)S(1)}, u32[]{:S(2)}, u32[]{:S(2)}) collective-permute-start(bf16[96,1280]{1,0:T(8,128)(2,1)S(1)} %project0.1.refs_4_), channel_id=1, source_target_pairs={{0,8},{4,12},{8,0},{12,4},{1,9},{5,13},{9,1},{13,5},{2,10},{6,14},... | collective-permute-start | bytes 737288 | tf_op jit(solution)/shard_map/ppermute | solution.py:26
  47.8 1.3 %collective-permute-start.21 = (bf16[240,128]{1,0:T(8,128)(2,1)S(1)}, bf16[240,128]{1,0:T(8,128)(2,1)S(1)}, u32[]{:S(2)}, u32[]{:S(2)}) collective-permute-start(bf16[240,128]{1,0:T(8,128)(2,1)S(1)} %get-tuple-element.93), channel_id=1, source_target_pairs={{0,2},{1,3},{2,0},{3,1},{4,6},{5,7},{6,4},{7,5},{8,10},{9,11},{10,... | collective-permute-start | bytes 184328 | tf_op jit(solution)/shard_map/ppermute | solution.py:26
  49.1 2.1 %collective-permute-start.22 = (bf16[240,128]{1,0:T(8,128)(2,1)S(1)}, bf16[240,128]{1,0:T(8,128)(2,1)S(1)}, u32[]{:S(2)}, u32[]{:S(2)}) collective-permute-start(bf16[240,128]{1,0:T(8,128)(2,1)S(1)} %get-tuple-element.94), channel_id=1, source_target_pairs={{0,3},{1,2},{2,1},{3,0},{4,7},{5,6},{6,5},{7,4},{8,11},{9,10},{10,... | collective-permute-start | bytes 184328 | tf_op jit(solution)/shard_map/ppermute | solution.py:26
  51.2 4.5 %collective-permute-done.21.refs_2_ = bf16[240,128]{1,0:T(8,128)(2,1)S(1)} collective-permute-done((bf16[240,128]{1,0:T(8,128)(2,1)S(1)}, bf16[240,128]{1,0:T(8,128)(2,1)S(1)}, u32[]{:S(2)}, u32[]{:S(2)}) %collective-permute-start.21) | collective-permute-done | bytes 61472 | tf_op jit(solution)/shard_map/ppermute | solution.py:26
  55.7 1.7 %project1.1.refs_5_ = bf16[96,1280]{1,0:T(8,128)(2,1)S(1)} custom-call(s32[3]{0:T(128)S(1)} %pad_add_fusion.1.index_ref, bf16[240,128]{1,0:T(8,128)(2,1)S(1)} %get-tuple-element.95.refs_0_, bf16[240,128]{1,0:T(8,128)(2,1)S(1)} %collective-permute-done.18.refs_1_, bf16[240,128]{1,0:T(8,128)(2,1)S(1)} %collective-permute-done.21.refs_2_, ...), custom_call_target="tpu_custom_call" | custom-call | tf_op jit(solution)/shard_map/project1/pallas_call | solution.py:360
  57.3 1.1 %collective-permute-start.26 = (bf16[96,1280]{1,0:T(8,128)(2,1)S(1)}, bf16[96,1280]{1,0:T(8,128)(2,1)S(1)}, u32[]{:S(2)}, u32[]{:S(2)}) collective-permute-start(bf16[96,1280]{1,0:T(8,128)(2,1)S(1)} %project1.1.refs_5_), channel_id=1, source_target_pairs={{0,8},{4,12},{8,0},{12,4},{1,9},{5,13},{9,1},{13,5},{2,10},{6,14},... | collective-permute-start | bytes 737288 | tf_op jit(solution)/shard_map/ppermute | solution.py:26
  58.4 1.1 %collective-permute-start = (s32[1,192]{1,0:T(1,128)S(1)}, s32[1,192]{1,0:T(1,128)S(1)}, u32[]{:S(2)}, u32[]{:S(2)}) collective-permute-start(s32[1,192]{1,0:T(1,128)S(1)} %bitcast.28), channel_id=1, source_target_pairs={{0,8},{4,12},{8,0},{12,4},{1,9},{5,13},{9,1},{13,5},{2,10},{6,14},... | collective-permute-start | bytes 2312 | tf_op jit(solution)/shard_map/ppermute | solution.py:26
  60.0 3.6 %collective-permute-done.26.refs_9_ = bf16[96,1280]{1,0:T(8,128)(2,1)S(1)} collective-permute-done((bf16[96,1280]{1,0:T(8,128)(2,1)S(1)}, bf16[96,1280]{1,0:T(8,128)(2,1)S(1)}, u32[]{:S(2)}, u32[]{:S(2)}) %collective-permute-start.26) | collective-permute-done | bytes 245792 | tf_op jit(solution)/shard_map/ppermute | solution.py:26
  63.7 0.5 collective-permute-start.1
  64.2 0.9 %collective-permute-done.1 = s32[2,1,192]{2,1,0:T(1,128)S(1)} collective-permute-done((s32[2,1,192]{2,1,0:T(1,128)S(1)}, s32[2,1,192]{2,1,0:T(1,128)S(1)}, u32[]{:S(2)}, u32[]{:S(2)}) %collective-permute-start.1) | collective-permute-done | bytes 1568 | tf_op jit(solution)/shard_map/ppermute | solution.py:26
  65.2 1.9 %placement.1 = bf16[192,1280]{1,0:T(8,128)(2,1)} custom-call(s32[3]{0:T(128)S(1)} %pad_add_fusion.1.index_ref, s32[1,192]{1,0:T(1,128)S(1)} %bitcast.30, s32[1,192]{1,0:T(1,128)S(1)} %get-tuple-element.102.refs_1_, s32[1,192]{1,0:T(1,128)S(1)} %collective-permute-done.refs_2_, s32[1,192]{1,0:T(1,128)S(1)} %get-tuple-element.101.refs_3_, ...), custom_call_target="tpu_custom_call" | custom-call | tf_op jit(solution)/shard_map/placement/pallas_call | solution.py:381
  (54 shorter events, 4.2 us)
Async XLA Ops:
  0.0 18.1 %copy-start = (bf16[768,1280]{1,0:T(8,128)(2,1)S(1)}, bf16[768,1280]{1,0:T(8,128)(2,1)}, u32[]{:S(2)}) copy-start(bf16[768,1280]{1,0:T(8,128)(2,1)} %patches_ref) | copy-start | bytes 5898244
  2.0 8.9 %collective-permute-start.3 = (bf16[3,800,128]{2,1,0:T(8,128)(2,1)S(1)}, bf16[3,800,128]{2,1,0:T(8,128)(2,1)S(1)}, u32[]{:S(2)}, u32[]{:S(2)}) collective-permute-start(bf16[3,800,128]{2,1,0:T(8,128)(2,1)S(1)} %get-tuple-element.54.refs_0_), channel_id=1, source_target_pairs={{0,4},{4,0},{8,12},{12,8},{1,5},{5,1},{9,13},{13,9},{2,6},{6,2},{1... | collective-permute-start | bytes 1843208 | tf_op jit(solution)/shard_map/ppermute | solution.py:26
  2.5 8.3 %collective-permute-start.2 = (bf16[800,128]{1,0:T(8,128)(2,1)S(1)}, bf16[800,128]{1,0:T(8,128)(2,1)S(1)}, u32[]{:S(2)}, u32[]{:S(2)}) collective-permute-start(bf16[800,128]{1,0:T(8,128)(2,1)S(1)} %get-tuple-element.53), channel_id=1, source_target_pairs={{0,8},{4,12},{8,0},{12,4},{1,9},{5,13},{9,1},{13,5},{2,10},{6,14},... | collective-permute-start | bytes 614408 | tf_op jit(solution)/shard_map/ppermute | solution.py:26
  6.1 16.1 %copy-start.4 = (s32[768]{0:T(1024)S(1)}, s32[768]{0:T(1024)}, u32[]{:S(2)}) copy-start(s32[768]{0:T(1024)} %param.8) | copy-start | bytes 9220
  6.1 11.5 %collective-permute-start.11 = (bf16[800,128]{1,0:T(8,128)(2,1)S(1)}, bf16[800,128]{1,0:T(8,128)(2,1)S(1)}, u32[]{:S(2)}, u32[]{:S(2)}) collective-permute-start(bf16[800,128]{1,0:T(8,128)(2,1)S(1)} %pack_proj.1.refs_4_), channel_id=1, source_target_pairs={{0,1},{1,0},{2,3},{3,2},{4,5},{5,4},{6,7},{7,6},{8,9},{9,8},{10,11... | collective-permute-start | bytes 614408 | tf_op jit(solution)/shard_map/ppermute | solution.py:26
  7.8 13.1 %collective-permute-start.9 = (bf16[800,128]{1,0:T(8,128)(2,1)S(1)}, bf16[800,128]{1,0:T(8,128)(2,1)S(1)}, u32[]{:S(2)}, u32[]{:S(2)}) collective-permute-start(bf16[800,128]{1,0:T(8,128)(2,1)S(1)} %pack_proj.1.refs_4_), channel_id=1, source_target_pairs={{0,2},{1,3},{2,0},{3,1},{16,19},{17,18},{18,17},{19,16},{4,6},{5,7... | collective-permute-start | bytes 614408 | tf_op jit(solution)/shard_map/ppermute | solution.py:281
  10.4 9.9 %collective-permute-start.5 = (bf16[800,128]{1,0:T(8,128)(2,1)S(1)}, bf16[800,128]{1,0:T(8,128)(2,1)S(1)}, u32[]{:S(2)}, u32[]{:S(2)}) collective-permute-start(bf16[800,128]{1,0:T(8,128)(2,1)S(1)} %get-tuple-element.56), channel_id=1, source_target_pairs={{0,8},{4,12},{8,0},{12,4},{1,9},{5,13},{9,1},{13,5},{2,10},{6,14},... | collective-permute-start | bytes 614408 | tf_op jit(solution)/shard_map/ppermute | solution.py:26
  10.9 9.4 %collective-permute-start.4 = (bf16[800,128]{1,0:T(8,128)(2,1)S(1)}, bf16[800,128]{1,0:T(8,128)(2,1)S(1)}, u32[]{:S(2)}, u32[]{:S(2)}) collective-permute-start(bf16[800,128]{1,0:T(8,128)(2,1)S(1)} %collective-permute-done.2.refs_2_), channel_id=1, source_target_pairs={{0,16},{16,0},{1,17},{17,1},{2,18},{18,2},{3,19},{19,3},{4,20},{20... | collective-permute-start | bytes 614408 | tf_op jit(solution)/shard_map/ppermute | solution.py:26
  12.5 7.8 %collective-permute-start.6 = (bf16[800,128]{1,0:T(8,128)(2,1)S(1)}, bf16[800,128]{1,0:T(8,128)(2,1)S(1)}, u32[]{:S(2)}, u32[]{:S(2)}) collective-permute-start(bf16[800,128]{1,0:T(8,128)(2,1)S(1)} %collective-permute-done.2.refs_2_), channel_id=1, source_target_pairs={{0,4},{4,0},{8,12},{12,8},{1,5},{5,1},{9,13},{13,9},{2,6},{6,2},{1... | collective-permute-start | bytes 614408 | tf_op jit(solution)/shard_map/ppermute | solution.py:26
  17.7 10.8 %collective-permute-start.12 = (bf16[2,800,128]{2,1,0:T(8,128)(2,1)S(1)}, bf16[2,800,128]{2,1,0:T(8,128)(2,1)S(1)}, u32[]{:S(2)}, u32[]{:S(2)}) collective-permute-start(bf16[2,800,128]{2,1,0:T(8,128)(2,1)S(1)} %pad_maximum_fusion.1), channel_id=1, source_target_pairs={{0,8},{4,12},{8,0},{12,4},{1,9},{5,13},{9,1},{13,5},{2,10},{6,14},... | collective-permute-start | bytes 1228808 | tf_op jit(solution)/shard_map/ppermute | solution.py:26
  20.3 1.5 %collective-permute-start.7 = (bf16[800,128]{1,0:T(8,128)(2,1)S(1)}, bf16[800,128]{1,0:T(8,128)(2,1)S(1)}, u32[]{:S(2)}, u32[]{:S(2)}) collective-permute-start(bf16[800,128]{1,0:T(8,128)(2,1)S(1)} %collective-permute-done.4.refs_3_), channel_id=1, source_target_pairs={{0,4},{4,0},{8,12},{12,8},{1,5},{5,1},{9,13},{13,9},{2,6},{6,2},{1... | collective-permute-start | bytes 614408 | tf_op jit(solution)/shard_map/ppermute | solution.py:26
  20.4 1.7 %collective-permute-start.8 = (bf16[800,128]{1,0:T(8,128)(2,1)S(1)}, bf16[800,128]{1,0:T(8,128)(2,1)S(1)}, u32[]{:S(2)}, u32[]{:S(2)}) collective-permute-start(bf16[800,128]{1,0:T(8,128)(2,1)S(1)} %collective-permute-done.5.refs_4_), channel_id=1, source_target_pairs={{0,4},{4,0},{8,12},{12,8},{1,5},{5,1},{9,13},{13,9},{2,6},{6,2},{1... | collective-permute-start | bytes 614408 | tf_op jit(solution)/shard_map/ppermute | solution.py:26
  20.9 7.1 %collective-permute-start.10 = (bf16[800,128]{1,0:T(8,128)(2,1)S(1)}, bf16[800,128]{1,0:T(8,128)(2,1)S(1)}, u32[]{:S(2)}, u32[]{:S(2)}) collective-permute-start(bf16[800,128]{1,0:T(8,128)(2,1)S(1)} %collective-permute-done.9.refs_6_), channel_id=1, source_target_pairs={{0,16},{16,0},{1,17},{17,1},{2,18},{18,2},{3,19},{19,3},{4,20},{20... | collective-permute-start | bytes 614408 | tf_op jit(solution)/shard_map/ppermute | solution.py:26
  28.4 5.7 %collective-permute-start.13 = (bf16[240,128]{1,0:T(8,128)(2,1)S(1)}, bf16[240,128]{1,0:T(8,128)(2,1)S(1)}, u32[]{:S(2)}, u32[]{:S(2)}) collective-permute-start(bf16[240,128]{1,0:T(8,128)(2,1)S(1)} %get-tuple-element.68), channel_id=1, source_target_pairs={{0,1},{1,0},{2,3},{3,2},{4,5},{5,4},{6,7},{7,6},{8,9},{9,8},{10,11... | collective-permute-start | bytes 184328 | tf_op jit(solution)/shard_map/ppermute | solution.py:26
  28.4 9.7 %collective-permute-start.14 = (bf16[240,128]{1,0:T(8,128)(2,1)S(1)}, bf16[240,128]{1,0:T(8,128)(2,1)S(1)}, u32[]{:S(2)}, u32[]{:S(2)}) collective-permute-start(bf16[240,128]{1,0:T(8,128)(2,1)S(1)} %get-tuple-element.77), channel_id=1, source_target_pairs={{0,2},{1,3},{2,0},{3,1},{4,6},{5,7},{6,4},{7,5},{8,10},{9,11},{10,... | collective-permute-start | bytes 184328 | tf_op jit(solution)/shard_map/ppermute | solution.py:26
  32.2 6.0 %collective-permute-start.15 = (bf16[240,128]{1,0:T(8,128)(2,1)S(1)}, bf16[240,128]{1,0:T(8,128)(2,1)S(1)}, u32[]{:S(2)}, u32[]{:S(2)}) collective-permute-start(bf16[240,128]{1,0:T(8,128)(2,1)S(1)} %get-tuple-element.78), channel_id=1, source_target_pairs={{0,3},{1,2},{2,1},{3,0},{4,7},{5,6},{6,5},{7,4},{8,11},{9,10},{10,... | collective-permute-start | bytes 184328 | tf_op jit(solution)/shard_map/ppermute | solution.py:26
  32.9 9.9 %collective-permute-start.17 = (bf16[2,800,128]{2,1,0:T(8,128)(2,1)S(1)}, bf16[2,800,128]{2,1,0:T(8,128)(2,1)S(1)}, u32[]{:S(2)}, u32[]{:S(2)}) collective-permute-start(bf16[2,800,128]{2,1,0:T(8,128)(2,1)S(1)} %pad_maximum_fusion.2), channel_id=1, source_target_pairs={{0,8},{4,12},{8,0},{12,4},{1,9},{5,13},{9,1},{13,5},{2,10},{6,14},... | collective-permute-start | bytes 1228808 | tf_op jit(solution)/shard_map/ppermute | solution.py:26
  38.3 6.3 %collective-permute-start.16 = (bf16[4,800,128]{2,1,0:T(8,128)(2,1)S(1)}, bf16[4,800,128]{2,1,0:T(8,128)(2,1)S(1)}, u32[]{:S(2)}, u32[]{:S(2)}) collective-permute-start(bf16[4,800,128]{2,1,0:T(8,128)(2,1)S(1)} %pad_maximum_fusion), channel_id=1, source_target_pairs={{0,4},{4,0},{8,12},{12,8},{1,5},{5,1},{9,13},{13,9},{2,6},{6,2},{1... | collective-permute-start | bytes 2457608 | tf_op jit(solution)/shard_map/ppermute | solution.py:26
  38.4 4.4 %collective-permute-start.18 = (bf16[240,128]{1,0:T(8,128)(2,1)S(1)}, bf16[240,128]{1,0:T(8,128)(2,1)S(1)}, u32[]{:S(2)}, u32[]{:S(2)}) collective-permute-start(bf16[240,128]{1,0:T(8,128)(2,1)S(1)} %get-tuple-element.88), channel_id=1, source_target_pairs={{0,1},{1,0},{2,3},{3,2},{4,5},{5,4},{6,7},{7,6},{8,9},{9,8},{10,11... | collective-permute-start | bytes 184328 | tf_op jit(solution)/shard_map/ppermute | solution.py:26
  38.6 4.2 %collective-permute-start.19 = (bf16[2,800,128]{2,1,0:T(8,128)(2,1)S(1)}, bf16[2,800,128]{2,1,0:T(8,128)(2,1)S(1)}, u32[]{:S(2)}, u32[]{:S(2)}) collective-permute-start(bf16[2,800,128]{2,1,0:T(8,128)(2,1)S(1)} %collective-permute-done.12.refs_9_), channel_id=1, source_target_pairs={{0,4},{4,0},{8,12},{12,8},{1,5},{5,1},{9,13},{13,9},{2,6},{6,2},{1... | collective-permute-start | bytes 1228808 | tf_op jit(solution)/shard_map/ppermute | solution.py:26
  42.8 1.7 %collective-permute-start.20 = (bf16[2,800,128]{2,1,0:T(8,128)(2,1)S(1)}, bf16[2,800,128]{2,1,0:T(8,128)(2,1)S(1)}, u32[]{:S(2)}, u32[]{:S(2)}) collective-permute-start(bf16[2,800,128]{2,1,0:T(8,128)(2,1)S(1)} %collective-permute-done.17.refs_10_), channel_id=1, source_target_pairs={{0,4},{4,0},{8,12},{12,8},{1,5},{5,1},{9,13},{13,9},{2,6},{6,2},{1... | collective-permute-start | bytes 1228808 | tf_op jit(solution)/shard_map/ppermute | solution.py:26
  46.2 12.2 %copy-start.6 = (s32[192]{0:T(256)S(1)}, s32[192]{0:T(256)}, u32[]{:S(2)}) copy-start(s32[192]{0:T(256)} %param.9) | copy-start | bytes 2308
  46.2 12.2 %collective-permute-start.25 = (bf16[96,1280]{1,0:T(8,128)(2,1)S(1)}, bf16[96,1280]{1,0:T(8,128)(2,1)S(1)}, u32[]{:S(2)}, u32[]{:S(2)}) collective-permute-start(bf16[96,1280]{1,0:T(8,128)(2,1)S(1)} %project0.1.refs_4_), channel_id=1, source_target_pairs={{0,8},{4,12},{8,0},{12,4},{1,9},{5,13},{9,1},{13,5},{2,10},{6,14},... | collective-permute-start | bytes 737288 | tf_op jit(solution)/shard_map/ppermute | solution.py:26
  47.8 7.8 %collective-permute-start.21 = (bf16[240,128]{1,0:T(8,128)(2,1)S(1)}, bf16[240,128]{1,0:T(8,128)(2,1)S(1)}, u32[]{:S(2)}, u32[]{:S(2)}) collective-permute-start(bf16[240,128]{1,0:T(8,128)(2,1)S(1)} %get-tuple-element.93), channel_id=1, source_target_pairs={{0,2},{1,3},{2,0},{3,1},{4,6},{5,7},{6,4},{7,5},{8,10},{9,11},{10,... | collective-permute-start | bytes 184328 | tf_op jit(solution)/shard_map/ppermute | solution.py:26
  49.1 6.5 %collective-permute-start.22 = (bf16[240,128]{1,0:T(8,128)(2,1)S(1)}, bf16[240,128]{1,0:T(8,128)(2,1)S(1)}, u32[]{:S(2)}, u32[]{:S(2)}) collective-permute-start(bf16[240,128]{1,0:T(8,128)(2,1)S(1)} %get-tuple-element.94), channel_id=1, source_target_pairs={{0,3},{1,2},{2,1},{3,0},{4,7},{5,6},{6,5},{7,4},{8,11},{9,10},{10,... | collective-permute-start | bytes 184328 | tf_op jit(solution)/shard_map/ppermute | solution.py:26
  57.3 6.3 %collective-permute-start.26 = (bf16[96,1280]{1,0:T(8,128)(2,1)S(1)}, bf16[96,1280]{1,0:T(8,128)(2,1)S(1)}, u32[]{:S(2)}, u32[]{:S(2)}) collective-permute-start(bf16[96,1280]{1,0:T(8,128)(2,1)S(1)} %project1.1.refs_5_), channel_id=1, source_target_pairs={{0,8},{4,12},{8,0},{12,4},{1,9},{5,13},{9,1},{13,5},{2,10},{6,14},... | collective-permute-start | bytes 737288 | tf_op jit(solution)/shard_map/ppermute | solution.py:26
  58.4 5.2 %collective-permute-start.27 = (bf16[96,1280]{1,0:T(8,128)(2,1)S(1)}, bf16[96,1280]{1,0:T(8,128)(2,1)S(1)}, u32[]{:S(2)}, u32[]{:S(2)}) collective-permute-start(bf16[96,1280]{1,0:T(8,128)(2,1)S(1)} %collective-permute-done.25.refs_8_), channel_id=1, source_target_pairs={{0,4},{4,0},{8,12},{12,8},{1,5},{5,1},{9,13},{13,9},{2,6},{6,2},{1... | collective-permute-start | bytes 737288 | tf_op jit(solution)/shard_map/ppermute | solution.py:26
  58.4 5.2 %collective-permute-start = (s32[1,192]{1,0:T(1,128)S(1)}, s32[1,192]{1,0:T(1,128)S(1)}, u32[]{:S(2)}, u32[]{:S(2)}) collective-permute-start(s32[1,192]{1,0:T(1,128)S(1)} %bitcast.28), channel_id=1, source_target_pairs={{0,8},{4,12},{8,0},{12,4},{1,9},{5,13},{9,1},{13,5},{2,10},{6,14},... | collective-permute-start | bytes 2312 | tf_op jit(solution)/shard_map/ppermute | solution.py:26
  59.5 5.6 %collective-permute-start.24 = (bf16[96,1280]{1,0:T(8,128)(2,1)S(1)}, bf16[96,1280]{1,0:T(8,128)(2,1)S(1)}, u32[]{:S(2)}, u32[]{:S(2)}) collective-permute-start(bf16[96,1280]{1,0:T(8,128)(2,1)S(1)} %project1.1.refs_5_), channel_id=1, source_target_pairs={{0,4},{4,0},{8,12},{12,8},{1,5},{5,1},{9,13},{13,9},{2,6},{6,2},{1... | collective-permute-start | bytes 737288 | tf_op jit(solution)/shard_map/ppermute | solution.py:26
  59.7 5.5 %collective-permute-start.23 = (bf16[96,1280]{1,0:T(8,128)(2,1)S(1)}, bf16[96,1280]{1,0:T(8,128)(2,1)S(1)}, u32[]{:S(2)}, u32[]{:S(2)}) collective-permute-start(bf16[96,1280]{1,0:T(8,128)(2,1)S(1)} %project0.1.refs_4_), channel_id=1, source_target_pairs={{0,4},{4,0},{8,12},{12,8},{1,5},{5,1},{9,13},{13,9},{2,6},{6,2},{1... | collective-permute-start | bytes 737288 | tf_op jit(solution)/shard_map/ppermute | solution.py:26
  63.6 1.5 %collective-permute-start.28 = (bf16[96,1280]{1,0:T(8,128)(2,1)S(1)}, bf16[96,1280]{1,0:T(8,128)(2,1)S(1)}, u32[]{:S(2)}, u32[]{:S(2)}) collective-permute-start(bf16[96,1280]{1,0:T(8,128)(2,1)S(1)} %collective-permute-done.26.refs_9_), channel_id=1, source_target_pairs={{0,4},{4,0},{8,12},{12,8},{1,5},{5,1},{9,13},{13,9},{2,6},{6,2},{1... | collective-permute-start | bytes 737288 | tf_op jit(solution)/shard_map/ppermute | solution.py:26
  63.7 1.5 %collective-permute-start.1 = (s32[2,1,192]{2,1,0:T(1,128)S(1)}, s32[2,1,192]{2,1,0:T(1,128)S(1)}, u32[]{:S(2)}, u32[]{:S(2)}) collective-permute-start(s32[2,1,192]{2,1,0:T(1,128)S(1)} %pad_add_fusion), channel_id=1, source_target_pairs={{0,4},{4,0},{8,12},{12,8},{1,5},{5,1},{9,13},{13,9},{2,6},{6,2},{1... | collective-permute-start | bytes 4616 | tf_op jit(solution)/shard_map/ppermute | solution.py:26
  (4 other events, 13.3 us)

commit v8 on v7

--- a/solution.py
+++ b/solution.py
@@ -11,7 +11,7 @@
 WIN = 64
 PAIR = 2 * WIN
 LANES = 128
-CHUNKS = 2
+HALVES = 2
 F32 = jnp.float32
 BF16 = jnp.bfloat16
 VMEM = pl.BlockSpec(memory_space=pltpu.VMEM)
@@ -113,12 +113,12 @@
         ).astype(BF16)
 
 
-def attend(row0, index_ref, hidden_ref, valid_ref, w_ref, out_refs, q_ref, k_ref, v_ref, mix_ref):
+def attend(index_ref, hidden_ref, valid_ref, w_ref, out_refs, q_ref, k_ref, v_ref, mix_ref):
     rows, width = q_ref.shape
     heads = width // HD
     main = 2 * LANES
     rest = width - main
-    qkv = jnp.dot(hidden_ref[row0 : row0 + rows, :], w_ref[...], preferred_element_type=F32)
+    qkv = jnp.dot(hidden_ref[...], w_ref[...], preferred_element_type=F32)
     for j, ref in enumerate((q_ref, k_ref, v_ref)):
         ref[:, :main] = qkv[:, j * main : (j + 1) * main].astype(BF16)
         at = 3 * main + j * rest
@@ -141,7 +141,7 @@
         k_all = jnp.concatenate([k * m for m in head_masks], axis=0)
         v_all = jnp.concatenate([v * m for m in head_masks], axis=0)
         scores = lax.dot_general(q, k_all, (((1,), (1,)), ((), ())), preferred_element_type=F32)
-        live = valid_ref[row0 // PAIR + p : row0 // PAIR + p + 1, :] > 0
+        live = valid_ref[p : p + 1, :] > 0
         weights = []
         for h in range(heads):
             s = scores[:, h * PAIR : (h + 1) * PAIR] * F32(HD ** (-0.5))
@@ -157,7 +157,7 @@
         out_ref[...] = pack(mix_ref[index_ref[1] ^ s])
 
 
-def first_attention_kernel(n_ctx, width, index_ref, hidden_ref, valid_ref, *refs):
+def attention_kernel(n_ctx, width, index_ref, hidden_ref, valid_ref, *refs):
     shards = list(refs[: 2 + 3 * (n_ctx - 2)])
     *out_refs, w_ref, q_ref, k_ref, v_ref, mix_ref = refs[len(shards) :]
     depth = w_ref.shape[0] // n_ctx
@@ -177,23 +177,19 @@
             w_ref[rows, j * main : (j + 1) * main], tail = unpack(third, depth, width)
             tails.append(tail)
         w_ref[rows, 3 * main :] = jnp.concatenate(tails, axis=1)
-    attend(0, index_ref, hidden_ref, valid_ref, w_ref, out_refs, q_ref, k_ref, v_ref, mix_ref)
-
-
-def next_attention_kernel(row0, index_ref, hidden_ref, valid_ref, w_ref, *refs):
-    *out_refs, q_ref, k_ref, v_ref, mix_ref = refs
-    attend(row0, index_ref, hidden_ref, valid_ref, w_ref, out_refs, q_ref, k_ref, v_ref, mix_ref)
-
-
-def project_kernel(n_ctx, row0, width, col, index_ref, *refs):
-    mixes = [unpack(m[...], refs[-2].shape[0], width) for m in refs[:4]]
+    attend(index_ref, hidden_ref, valid_ref, w_ref, out_refs, q_ref, k_ref, v_ref, mix_ref)
+
+
+def project_kernel(n_ctx, width, col, index_ref, *refs):
+    *blocks, own_ref, gain_ref = refs[4 : -HALVES - 1]
+    *out_refs, part_ref = refs[-HALVES - 1 :]
+    rows = own_ref.shape[0]
+    mixes = [unpack(m[...], rows, width) for m in refs[:4]]
     flip = index_ref[2] > 0
     mixes[2:] = [
         [jnp.where(flip, b, a) for a, b in zip(mixes[2], mixes[3])],
         [jnp.where(flip, a, b) for a, b in zip(mixes[2], mixes[3])],
     ]
-    *blocks, own_ref, gain_ref, out_ref, part_ref = refs[4:]
-    rows = out_ref.shape[0]
     me = index_ref[0]
     main = 2 * LANES
     mixed = jnp.concatenate([m for m, _ in mixes] + [r for _, r in mixes], axis=1)
@@ -219,9 +215,12 @@
     for key in range(n_ctx):
         part_ref[me ^ key] = mains[key]
     total = jnp.concatenate([part_ref[i] for i in range(n_ctx)], axis=1)
-    total = total + own_ref[row0 : row0 + rows, :].astype(F32)
+    total = total + own_ref[...].astype(F32)
     mean_sq = jnp.mean(total * total, axis=-1, keepdims=True)
-    out_ref[...] = (total * lax.rsqrt(mean_sq + 1e-06) * gain_ref[...].reshape(1, -1)).astype(BF16)
+    normed = (total * lax.rsqrt(mean_sq + 1e-06) * gain_ref[...].reshape(1, -1)).astype(BF16)
+    count = rows // HALVES
+    for i, out_ref in enumerate(out_refs):
+        out_ref[...] = normed[i * count : (i + 1) * count]
 
 
 def place_kernel(n_ctx, index_ref, *refs):
@@ -300,92 +299,76 @@
         compiler_params=params(16),
         name="norm",
     )(index, patches, gain_attn)
+    by_one, hidden = together(by_one, hidden)
     low = gather_cross(jnp.stack([w_proj, by_one]), n_ctx)
     second, value, first_twin, hidden = together(second, value, first_twin, hidden)
 
     second_twin = {k: over_core(second[k]) for k in cross}
     value_twin = {k: over_core(value[k]) for k in cross}
+    far, *_ = together(far, *second.values())
     far2 = over_dp(far)
 
     shard_list = [own, twin]
     for k in cross:
         shard_list += [first[k], second[k], value[k], first_twin[k], second_twin[k], value_twin[k]]
 
-    valid_pairs = valid.reshape(rows // PAIR, PAIR)
-    part = rows // CHUNKS
-    mix_shapes = (shape(*packed_shape(part // 4, width)),) * n_ten
-    scratch = [pltpu.VMEM((part, width), BF16)] * 3 + [pltpu.VMEM((4, part // 4, width), BF16)]
-    *mixed, w_full = pl.pallas_call(
-        functools.partial(first_attention_kernel, n_ctx, width),
-        out_shape=mix_shapes + (shape(feat, 3 * width),),
+    mix_shapes = (shape(*packed_shape(groups, width)),) * n_ten
+    mixed = pl.pallas_call(
+        functools.partial(attention_kernel, n_ctx, width),
+        out_shape=mix_shapes,
         in_specs=[SMEM] + [VMEM] * (2 + len(shard_list)),
-        out_specs=(VMEM,) * (n_ten + 1),
-        scratch_shapes=scratch,
-        compiler_params=params(16),
-        name="attention0",
-    )(index, hidden, valid_pairs, *shard_list)
-
-    def exchange(pieces):
-        return [pieces[0]] + [swap(pieces[s], "tensor", n_ten, s) for s in range(1, n_ten)]
+        out_specs=(VMEM,) * n_ten,
+        scratch_shapes=[pltpu.VMEM((feat, 3 * width), BF16)]
+        + [pltpu.VMEM((rows, width), BF16)] * 3
+        + [pltpu.VMEM((4, groups, width), BF16)],
+        compiler_params=params(20),
+        name="attention",
+    )(index, hidden, valid.reshape(rows // PAIR, PAIR), *shard_list)
 
     mixed, far, far2, low = together(mixed, far, far2, low)
-    received = [exchange(mixed)]
+    mixed = [mixed[0]] + [swap(mixed[s], "tensor", n_ten, s) for s in range(1, n_ten)]
     high = gather_cross(jnp.stack([far, far2]), n_ctx)
-    own_twin = None
-    for r in range(1, CHUNKS):
-        received[r - 1][1], hidden = together(received[r - 1][1], hidden)
-        mixed = pl.pallas_call(
-            functools.partial(next_attention_kernel, r * part),
-            out_shape=mix_shapes,
-            in_specs=[SMEM, VMEM, VMEM, VMEM],
-            out_specs=(VMEM,) * n_ten,
-            scratch_shapes=scratch,
-            compiler_params=params(12),
-            name="attention" + str(r),
-        )(index, hidden, valid_pairs, w_full)
-        mixed, received[r - 1], low, w_proj = together(mixed, received[r - 1], low, w_proj)
-        received.append(exchange(mixed))
-        if own_twin is None:
-            own_twin = over_core(jnp.stack([w_proj, by_one, far, far2]))
-
-    high, received[-1][1] = together(high, received[-1][1])
-
-    blocks = [w_proj, by_one, far, far2, own_twin]
+    blocks = [w_proj, by_one, far, far2, over_core(jnp.stack([w_proj, by_one, far, far2]))]
+    low_twin = {k: over_core(low[k]) for k in cross}
+    mixed, high = together(mixed, high)
     for k in cross:
-        blocks += [low[k], high[k], over_core(low[k]), over_core(high[k])]
+        blocks += [low[k], high[k], low_twin[k], over_core(high[k])]
+    done = pl.pallas_call(
+        functools.partial(project_kernel, n_ctx, width, col),
+        out_shape=(shape(groups // HALVES, feat),) * HALVES,
+        in_specs=[SMEM] + [VMEM] * (n_ten + len(blocks) + 2),
+        out_specs=(VMEM,) * HALVES,
+        scratch_shapes=[pltpu.VMEM((n_ctx, groups, col), F32)],
+        compiler_params=params(24),
+        name="project",
+    )(index, *mixed, *blocks, own_patches, gain_merge)
+
     gathered = []
-    for r in range(CHUNKS):
-        if r > 0:
-            received[r], done = together(received[r], done)
-        done = pl.pallas_call(
-            functools.partial(project_kernel, n_ctx, r * (part // 4), width, col),
-            out_shape=shape(part // 4, feat),
-            in_specs=[SMEM] + [VMEM] * (n_ten + len(blocks) + 2),
-            out_specs=VMEM,
-            scratch_shapes=[pltpu.VMEM((n_ctx, part // 4, col), F32)],
-            compiler_params=params(20),
-            name="project" + str(r),
-        )(index, *received[r], *blocks, own_patches, gain_merge)
-        crossed = gather_cross(done, n_ctx)
-        if r > 0:
+    for r in range(HALVES):
+        crossed = gather_cross(done[r], n_ctx)
+        if r == 0:
+            place, crossed[0] = together(place, crossed[0])
+            places = gather_cross(place.reshape(1, groups), n_ctx)
+            place_twin = over_core(jnp.stack([places[k] for k in (0, *cross)]))
+        else:
             for k in cross:
-                crossed[k], gathered[r - 1][k ^ 1] = together(crossed[k], gathered[r - 1][k ^ 1])
+                crossed[k], gathered[r - 1][k ^ 1], place_twin = together(
+                    crossed[k], gathered[r - 1][k ^ 1], place_twin
+                )
         for k in list(crossed):
             crossed[k ^ 1] = over_core(crossed[k])
         gathered.append(crossed)
-    places = gather_cross(place.reshape(1, groups), n_ctx)
-    place_twin = over_core(jnp.stack([places[k] for k in (0, *cross)]))
     place_list = []
     for i, k in enumerate((0, *cross)):
         place_list += [places[k], place_twin[i]]
     return pl.pallas_call(
         functools.partial(place_kernel, n_ctx),
         out_shape=shape(groups, feat),
-        in_specs=[SMEM] + [VMEM] * (n_ctx + n_ctx * CHUNKS),
+        in_specs=[SMEM] + [VMEM] * (n_ctx + n_ctx * HALVES),
         out_specs=VMEM,
         compiler_params=params(28),
         name="placement",
-    )(index, *place_list, *[gathered[r][k] for k in range(n_ctx) for r in range(CHUNKS)])
+    )(index, *place_list, *[gathered[r][k] for k in range(n_ctx) for r in range(HALVES)])
 
 
 def solution(mesh):

time: 67.7 us -> 66.5 us (0.982)
  waiting for transfers between devices: 22.4 us -> 27.1 us
  starting transfers between devices: 25.3 us -> 20.8 us
  Pallas kernels: 16 us -> 13.6 us
  local copies, waits for them, and re-layouts: 2.9 us -> 4.32 us
    ppermute x28 -> x25, starting transfers between devices: 22.8 us -> 18.2 us  [swap(): return lax.ppermute(x, axis, [(i, i ^ bit) for i in range(size)])]
    ppermute x28 -> x25, waiting for transfers between devices: 22.4 us -> 25.7 us  [swap(): return lax.ppermute(x, axis, [(i, i ^ bit) for i in range(size)])]
    pallas_call x4 -> x2, Pallas kernels: 11.8 us -> 9.39 us  [the longest x1 7.47 us: local(): pl.pallas_call(functools.partial(attention_kernel, n_ctx, width), out_sha...]
    unnamed x14, local copies, waits for them, and re-layouts: 2.9 us -> 4.32 us
    ppermute x1, waiting for transfers between devices: 0.01 us -> 1.32 us  [local(): lax.ppermute(w_proj, ('dp', 'tensor'), [(d * n_ten + t, d * n_ten + (t ^...]
  transfers between devices with their start and end apart: 29 -> 26, of which waited for: 10 -> 10; matrix products, arithmetic and copies ran while one was open for 0% -> 0% of each run, Pallas kernels for 17% -> 14%
where the time goes in v8:
time: 66.5 us; the launch traced here: 66.2 us
  waiting for transfers between devices  27.1 us (41%)
  starting transfers between devices  20.8 us (31%)
  Pallas kernels  13.6 us (20%)
  local copies, waits for them, and re-layouts  4.32 us (6%)
    ppermute x25, waiting for transfers between devices, swap(): return lax.ppermute(x, axis, [(i, i ^ bit) for i in range(size)])  25.7 us
    ppermute x25, starting transfers between devices, swap(): return lax.ppermute(x, axis, [(i, i ^ bit) for i in range(size)])  18.2 us
    pallas_call x1, Pallas kernels, local(): pl.pallas_call(functools.partial(attention_kernel, n_ctx, width), out_sha...  7.47 us
    unnamed x14, local copies, waits for them, and re-layouts  4.32 us
    ppermute x1, starting transfers between devices, local(): lax.ppermute(w_proj, ('dp', 'tensor'), [(d * n_ten + t, d * n_ten + (t ^...  2.59 us
    pallas_call x1, Pallas kernels, local(): pl.pallas_call(functools.partial(place_kernel, n_ctx), out_shape=shape(gr...  1.93 us
    pallas_call x1, Pallas kernels, local(): pl.pallas_call(functools.partial(project_kernel, n_ctx, width, col), out_...  1.92 us
    pallas_call x1, Pallas kernels, local(): pl.pallas_call(norm_kernel, out_shape=(shape(rows, feat), shape(groups, f...  1.57 us
  transfers between devices with their start and end apart: 26, of which 10 were waited for; matrix products, arithmetic and copies ran while one was open for 0% of the time, Pallas kernels for 14%

profile of v8, /device:TPU:0, one launch (start us, length us, event | category | flops | bytes accessed | tf_op | source)
XLA Modules:
  0.0 66.2 jit_solution(16668006569351786826)
XLA Ops:
  0.1 1.1 %copy-done.1 = bf16[320,3,320]{2,0,1:T(8,128)(2,1)S(1)} copy-done((bf16[320,3,320]{2,0,1:T(8,128)(2,1)S(1)}, bf16[320,3,320]{2,0,1:T(8,128)(2,1)}, u32[]{:S(2)}) %copy-start.1) | copy-done | bytes 614424
  1.2 0.7 %pack.1 = (bf16[800,128]{1,0:T(8,128)(2,1)S(1)}, bf16[800,128]{1,0:T(8,128)(2,1)S(1)}, bf16[3,800,128]{2,1,0:T(8,128)(2,1)S(1)}) custom-call(s32[3]{0:T(128)S(1)} %pad_add_fusion.1.index_ref, bf16[3,320,320]{2,1,0:T(8,128)(2,1)S(1)} %bitcast.24), custom_call_target="tpu_custom_call" | custom-call | tf_op jit(solution)/shard_map/pack/pallas_call | solution.py:261
  1.9 0.5 collective-permute-start.1
  2.4 2.6 %collective-permute-start = (bf16[800,128]{1,0:T(8,128)(2,1)S(1)}, bf16[800,128]{1,0:T(8,128)(2,1)S(1)}, u32[]{:S(2)}, u32[]{:S(2)}) collective-permute-start(bf16[800,128]{1,0:T(8,128)(2,1)S(1)} %get-tuple-element.43), channel_id=1, source_target_pairs={{0,8},{4,12},{8,0},{12,4},{1,9},{5,13},{9,1},{13,5},{2,10},{6,14},... | collective-permute-start | bytes 614408 | tf_op jit(solution)/shard_map/ppermute | solution.py:26
  5.0 0.9 %copy-done.2 = bf16[320,320]{1,0:T(8,128)(2,1)S(1)} copy-done((bf16[320,320]{1,0:T(8,128)(2,1)S(1)}, bf16[320,320]{1,0:T(8,128)(2,1)}, u32[]{:S(2)}) %copy-start.2) | copy-done | bytes 204824
  6.0 1.6 %collective-permute-start.5 = (bf16[800,128]{1,0:T(8,128)(2,1)S(1)}, bf16[800,128]{1,0:T(8,128)(2,1)S(1)}, u32[]{:S(2)}, u32[]{:S(2)}) collective-permute-start(bf16[800,128]{1,0:T(8,128)(2,1)S(1)} %pack_proj.1.refs_4_), channel_id=1, source_target_pairs={{0,1},{1,0},{2,3},{3,2},{4,5},{5,4},{6,7},{7,6},{8,9},{9,8},{10,11... | collective-permute-start | bytes 614408 | tf_op jit(solution)/shard_map/ppermute | solution.py:26
  7.6 2.6 %collective-permute-start.8 = (bf16[800,128]{1,0:T(8,128)(2,1)S(1)}, bf16[800,128]{1,0:T(8,128)(2,1)S(1)}, u32[]{:S(2)}, u32[]{:S(2)}) collective-permute-start(bf16[800,128]{1,0:T(8,128)(2,1)S(1)} %pack_proj.1.refs_4_), channel_id=1, source_target_pairs={{0,2},{1,3},{2,0},{3,1},{16,19},{17,18},{18,17},{19,16},{4,6},{5,7... | collective-permute-start | bytes 614408 | tf_op jit(solution)/shard_map/ppermute | solution.py:280
  10.2 0.5 collective-permute-start.3
  10.7 1.7 %collective-permute-start.2 = (bf16[800,128]{1,0:T(8,128)(2,1)S(1)}, bf16[800,128]{1,0:T(8,128)(2,1)S(1)}, u32[]{:S(2)}, u32[]{:S(2)}) collective-permute-start(bf16[800,128]{1,0:T(8,128)(2,1)S(1)} %collective-permute-done.refs_2_), channel_id=1, source_target_pairs={{0,16},{16,0},{1,17},{17,1},{2,18},{18,2},{3,19},{19,3},{4,20},{20... | collective-permute-start | bytes 614408 | tf_op jit(solution)/shard_map/ppermute | solution.py:26
  12.4 1.5 %copy-done = bf16[768,1280]{1,0:T(8,128)(2,1)S(1)} copy-done((bf16[768,1280]{1,0:T(8,128)(2,1)S(1)}, bf16[768,1280]{1,0:T(8,128)(2,1)}, u32[]{:S(2)}) %copy-start) | copy-done | bytes 1966104
  13.9 0.7 %copy-done.3 = f32[1280]{0:T(1024)S(1)} copy-done((f32[1280]{0:T(1024)S(1)}, f32[1280]{0:T(1024)}, u32[]{:S(2)}) %copy-start.3) | copy-done | bytes 5144
  14.6 1.6 %norm.1 = (bf16[768,1280]{1,0:T(8,128)(2,1)S(1)}, bf16[192,1280]{1,0:T(8,128)(2,1)S(1)}) custom-call(s32[3]{0:T(128)S(1)} %pad_add_fusion.1.index_ref, bf16[768,1280]{1,0:T(8,128)(2,1)S(1)} %copy-done, f32[1280]{0:T(1024)S(1)} %copy-done.3), custom_call_target="tpu_custom_call" | custom-call | tf_op jit(solution)/shard_map/norm/pallas_call | solution.py:294
  16.2 1.3 %collective-permute-done.5.refs_5_ = bf16[800,128]{1,0:T(8,128)(2,1)S(1)} collective-permute-done((bf16[800,128]{1,0:T(8,128)(2,1)S(1)}, bf16[800,128]{1,0:T(8,128)(2,1)S(1)}, u32[]{:S(2)}, u32[]{:S(2)}) %collective-permute-start.5) | collective-permute-done | bytes 204832 | tf_op jit(solution)/shard_map/ppermute | solution.py:26
  17.5 0.4 collective-permute-start.10
  18.5 1.3 %collective-permute-done.8.refs_6_ = bf16[800,128]{1,0:T(8,128)(2,1)S(1)} collective-permute-done((bf16[800,128]{1,0:T(8,128)(2,1)S(1)}, bf16[800,128]{1,0:T(8,128)(2,1)S(1)}, u32[]{:S(2)}, u32[]{:S(2)}) %collective-permute-start.8) | collective-permute-done | bytes 204832 | tf_op jit(solution)/shard_map/ppermute | solution.py:280
  19.8 1.4 %collective-permute-start.9 = (bf16[800,128]{1,0:T(8,128)(2,1)S(1)}, bf16[800,128]{1,0:T(8,128)(2,1)S(1)}, u32[]{:S(2)}, u32[]{:S(2)}) collective-permute-start(bf16[800,128]{1,0:T(8,128)(2,1)S(1)} %collective-permute-done.8.refs_6_), channel_id=1, source_target_pairs={{0,16},{16,0},{1,17},{17,1},{2,18},{18,2},{3,19},{19,3},{4,20},{20... | collective-permute-start | bytes 614408 | tf_op jit(solution)/shard_map/ppermute | solution.py:26
  21.2 7.5 %attention.1 = (bf16[480,128]{1,0:T(8,128)(2,1)S(1)}, bf16[480,128]{1,0:T(8,128)(2,1)S(1)}, bf16[480,128]{1,0:T(8,128)(2,1)S(1)}, bf16[480,128]{1,0:T(8,128)(2,1)S(1)}) custom-call(s32[3]{0:T(128)S(1)} %pad_add_fusion.1.index_ref, bf16[768,1280]{1,0:T(8,128)(2,1)S(1)} %get-tuple-element.50.hidden_ref, s32[6,128]{1,0:T(8,128)S(1)} %bitcast.29, ...), custom_call_target="tpu_custom_call" | custom-call | tf_op jit(solution)/shard_map/attention/pallas_call | solution.py:316
  28.8 1.1 %collective-permute-start.14 = (bf16[2,800,128]{2,1,0:T(8,128)(2,1)S(1)}, bf16[2,800,128]{2,1,0:T(8,128)(2,1)S(1)}, u32[]{:S(2)}, u32[]{:S(2)}) collective-permute-start(bf16[2,800,128]{2,1,0:T(8,128)(2,1)S(1)} %pad_maximum_fusion.2), channel_id=1, source_target_pairs={{0,8},{4,12},{8,0},{12,4},{1,9},{5,13},{9,1},{13,5},{2,10},{6,14},... | collective-permute-start | bytes 1228808 | tf_op jit(solution)/shard_map/ppermute | solution.py:26
  30.0 2.1 %collective-permute-start.11 = (bf16[480,128]{1,0:T(8,128)(2,1)S(1)}, bf16[480,128]{1,0:T(8,128)(2,1)S(1)}, u32[]{:S(2)}, u32[]{:S(2)}) collective-permute-start(bf16[480,128]{1,0:T(8,128)(2,1)S(1)} %get-tuple-element.62), channel_id=1, source_target_pairs={{0,1},{1,0},{2,3},{3,2},{4,5},{5,4},{6,7},{7,6},{8,9},{9,8},{10,11... | collective-permute-start | bytes 368648 | tf_op jit(solution)/shard_map/ppermute | solution.py:26
  32.1 2.6 %collective-permute-start.12 = (bf16[480,128]{1,0:T(8,128)(2,1)S(1)}, bf16[480,128]{1,0:T(8,128)(2,1)S(1)}, u32[]{:S(2)}, u32[]{:S(2)}) collective-permute-start(bf16[480,128]{1,0:T(8,128)(2,1)S(1)} %get-tuple-element.63), channel_id=1, source_target_pairs={{0,2},{1,3},{2,0},{3,1},{4,6},{5,7},{6,4},{7,5},{8,10},{9,11},{10,... | collective-permute-start | bytes 368648 | tf_op jit(solution)/shard_map/ppermute | solution.py:26
  34.7 3.3 %collective-permute-done.11.refs_1_ = bf16[480,128]{1,0:T(8,128)(2,1)S(1)} collective-permute-done((bf16[480,128]{1,0:T(8,128)(2,1)S(1)}, bf16[480,128]{1,0:T(8,128)(2,1)S(1)}, u32[]{:S(2)}, u32[]{:S(2)}) %collective-permute-start.11) | collective-permute-done | bytes 122912 | tf_op jit(solution)/shard_map/ppermute | solution.py:26
  38.0 6.5 %collective-permute-done.12.refs_2_ = bf16[480,128]{1,0:T(8,128)(2,1)S(1)} collective-permute-done((bf16[480,128]{1,0:T(8,128)(2,1)S(1)}, bf16[480,128]{1,0:T(8,128)(2,1)S(1)}, u32[]{:S(2)}, u32[]{:S(2)}) %collective-permute-start.12) | collective-permute-done | bytes 122912 | tf_op jit(solution)/shard_map/ppermute | solution.py:26
  44.5 1.7 %collective-permute-done.17.refs_12_ = bf16[2,800,128]{2,1,0:T(8,128)(2,1)S(1)} collective-permute-done((bf16[2,800,128]{2,1,0:T(8,128)(2,1)S(1)}, bf16[2,800,128]{2,1,0:T(8,128)(2,1)S(1)}, u32[]{:S(2)}, u32[]{:S(2)}) %collective-permute-start.17) | collective-permute-done | bytes 409632 | tf_op jit(solution)/shard_map/ppermute | solution.py:26
  46.3 1.9 %project.1 = (bf16[96,1280]{1,0:T(8,128)(2,1)S(1)}, bf16[96,1280]{1,0:T(8,128)(2,1)S(1)}) custom-call(s32[3]{0:T(128)S(1)} %pad_add_fusion.1.index_ref, bf16[480,128]{1,0:T(8,128)(2,1)S(1)} %get-tuple-element.67.refs_0_, bf16[480,128]{1,0:T(8,128)(2,1)S(1)} %collective-permute-done.11.refs_1_, bf16[480,128]{1,0:T(8,128)(2,1)S(1)} %collective-permute-done.12.refs_2_, ...), custom_call_target="tpu_custom_call" | custom-call | tf_op jit(solution)/shard_map/project/pallas_call | solution.py:336
  48.5 1.8 %collective-permute-start.18 = (bf16[96,1280]{1,0:T(8,128)(2,1)S(1)}, bf16[96,1280]{1,0:T(8,128)(2,1)S(1)}, u32[]{:S(2)}, u32[]{:S(2)}) collective-permute-start(bf16[96,1280]{1,0:T(8,128)(2,1)S(1)} %get-tuple-element.76.refs_5_), channel_id=1, source_target_pairs={{0,8},{4,12},{8,0},{12,4},{1,9},{5,13},{9,1},{13,5},{2,10},{6,14},... | collective-permute-start | bytes 737288 | tf_op jit(solution)/shard_map/ppermute | solution.py:26
  50.3 6.8 %collective-permute-done.19.refs_8_ = bf16[96,1280]{1,0:T(8,128)(2,1)S(1)} collective-permute-done((bf16[96,1280]{1,0:T(8,128)(2,1)S(1)}, bf16[96,1280]{1,0:T(8,128)(2,1)S(1)}, u32[]{:S(2)}, u32[]{:S(2)}) %collective-permute-start.19) | collective-permute-done | bytes 245792 | tf_op jit(solution)/shard_map/ppermute | solution.py:26
  57.3 4.3 %collective-permute-done.21.refs_2_ = s32[1,192]{1,0:T(1,128)S(1)} collective-permute-done((s32[1,192]{1,0:T(1,128)S(1)}, s32[1,192]{1,0:T(1,128)S(1)}, u32[]{:S(2)}, u32[]{:S(2)}) %collective-permute-start.21) | collective-permute-done | bytes 800 | tf_op jit(solution)/shard_map/ppermute | solution.py:26
  61.6 0.5 collective-permute-start.24
  62.2 0.6 collective-permute-done.22
  62.9 0.7 %collective-permute-done.23.refs_6_ = bf16[96,1280]{1,0:T(8,128)(2,1)S(1)} collective-permute-done((bf16[96,1280]{1,0:T(8,128)(2,1)S(1)}, bf16[96,1280]{1,0:T(8,128)(2,1)S(1)}, u32[]{:S(2)}, u32[]{:S(2)}) %collective-permute-start.23) | collective-permute-done | bytes 245792 | tf_op jit(solution)/shard_map/ppermute | solution.py:26
  63.6 0.7 collective-permute-done.25.refs_11_
  64.3 1.9 %placement.1 = bf16[192,1280]{1,0:T(8,128)(2,1)} custom-call(s32[3]{0:T(128)S(1)} %pad_add_fusion.1.index_ref, s32[1,192]{1,0:T(1,128)S(1)} %bitcast.27, s32[1,192]{1,0:T(1,128)S(1)} %get-tuple-element.82.refs_1_, s32[1,192]{1,0:T(1,128)S(1)} %collective-permute-done.21.refs_2_, s32[1,192]{1,0:T(1,128)S(1)} %get-tuple-element.81.refs_3_, ...), custom_call_target="tpu_custom_call" | custom-call | tf_op jit(solution)/shard_map/placement/pallas_call | solution.py:364
  (46 shorter events, 1.9 us)
Async XLA Ops:
  0.1 1.1 %copy-start.1 = (bf16[320,3,320]{2,0,1:T(8,128)(2,1)S(1)}, bf16[320,3,320]{2,0,1:T(8,128)(2,1)}, u32[]{:S(2)}) copy-start(bf16[320,3,320]{2,0,1:T(8,128)(2,1)} %param.11) | copy-start | bytes 1843204
  1.2 20.0 %copy-start.6 = (s32[768]{0:T(1024)S(1)}, s32[768]{0:T(1024)}, u32[]{:S(2)}) copy-start(s32[768]{0:T(1024)} %param.8) | copy-start | bytes 9220
  1.9 8.9 %collective-permute-start.1 = (bf16[3,800,128]{2,1,0:T(8,128)(2,1)S(1)}, bf16[3,800,128]{2,1,0:T(8,128)(2,1)S(1)}, u32[]{:S(2)}, u32[]{:S(2)}) collective-permute-start(bf16[3,800,128]{2,1,0:T(8,128)(2,1)S(1)} %get-tuple-element.44.refs_0_), channel_id=1, source_target_pairs={{0,4},{4,0},{8,12},{12,8},{1,5},{5,1},{9,13},{13,9},{2,6},{6,2},{1... | collective-permute-start | bytes 1843208 | tf_op jit(solution)/shard_map/ppermute | solution.py:26
  2.4 8.3 %collective-permute-start = (bf16[800,128]{1,0:T(8,128)(2,1)S(1)}, bf16[800,128]{1,0:T(8,128)(2,1)S(1)}, u32[]{:S(2)}, u32[]{:S(2)}) collective-permute-start(bf16[800,128]{1,0:T(8,128)(2,1)S(1)} %get-tuple-element.43), channel_id=1, source_target_pairs={{0,8},{4,12},{8,0},{12,4},{1,9},{5,13},{9,1},{13,5},{2,10},{6,14},... | collective-permute-start | bytes 614408 | tf_op jit(solution)/shard_map/ppermute | solution.py:26
  5.0 0.9 %copy-start.2 = (bf16[320,320]{1,0:T(8,128)(2,1)S(1)}, bf16[320,320]{1,0:T(8,128)(2,1)}, u32[]{:S(2)}) copy-start(bf16[320,320]{1,0:T(8,128)(2,1)} %proj_ref.1) | copy-start | bytes 614404
  6.0 11.5 %collective-permute-start.5 = (bf16[800,128]{1,0:T(8,128)(2,1)S(1)}, bf16[800,128]{1,0:T(8,128)(2,1)S(1)}, u32[]{:S(2)}, u32[]{:S(2)}) collective-permute-start(bf16[800,128]{1,0:T(8,128)(2,1)S(1)} %pack_proj.1.refs_4_), channel_id=1, source_target_pairs={{0,1},{1,0},{2,3},{3,2},{4,5},{5,4},{6,7},{7,6},{8,9},{9,8},{10,11... | collective-permute-start | bytes 614408 | tf_op jit(solution)/shard_map/ppermute | solution.py:26
  7.6 12.2 %collective-permute-start.8 = (bf16[800,128]{1,0:T(8,128)(2,1)S(1)}, bf16[800,128]{1,0:T(8,128)(2,1)S(1)}, u32[]{:S(2)}, u32[]{:S(2)}) collective-permute-start(bf16[800,128]{1,0:T(8,128)(2,1)S(1)} %pack_proj.1.refs_4_), channel_id=1, source_target_pairs={{0,2},{1,3},{2,0},{3,1},{16,19},{17,18},{18,17},{19,16},{4,6},{5,7... | collective-permute-start | bytes 614408 | tf_op jit(solution)/shard_map/ppermute | solution.py:280
  10.2 7.7 %collective-permute-start.3 = (bf16[800,128]{1,0:T(8,128)(2,1)S(1)}, bf16[800,128]{1,0:T(8,128)(2,1)S(1)}, u32[]{:S(2)}, u32[]{:S(2)}) collective-permute-start(bf16[800,128]{1,0:T(8,128)(2,1)S(1)} %get-tuple-element.46), channel_id=1, source_target_pairs={{0,8},{4,12},{8,0},{12,4},{1,9},{5,13},{9,1},{13,5},{2,10},{6,14},... | collective-permute-start | bytes 614408 | tf_op jit(solution)/shard_map/ppermute | solution.py:26
  10.7 7.2 %collective-permute-start.2 = (bf16[800,128]{1,0:T(8,128)(2,1)S(1)}, bf16[800,128]{1,0:T(8,128)(2,1)S(1)}, u32[]{:S(2)}, u32[]{:S(2)}) collective-permute-start(bf16[800,128]{1,0:T(8,128)(2,1)S(1)} %collective-permute-done.refs_2_), channel_id=1, source_target_pairs={{0,16},{16,0},{1,17},{17,1},{2,18},{18,2},{3,19},{19,3},{4,20},{20... | collective-permute-start | bytes 614408 | tf_op jit(solution)/shard_map/ppermute | solution.py:26
  12.4 5.6 %collective-permute-start.4 = (bf16[800,128]{1,0:T(8,128)(2,1)S(1)}, bf16[800,128]{1,0:T(8,128)(2,1)S(1)}, u32[]{:S(2)}, u32[]{:S(2)}) collective-permute-start(bf16[800,128]{1,0:T(8,128)(2,1)S(1)} %collective-permute-done.refs_2_), channel_id=1, source_target_pairs={{0,4},{4,0},{8,12},{12,8},{1,5},{5,1},{9,13},{13,9},{2,6},{6,2},{1... | collective-permute-start | bytes 614408 | tf_op jit(solution)/shard_map/ppermute | solution.py:26
  12.4 1.5 %copy-start = (bf16[768,1280]{1,0:T(8,128)(2,1)S(1)}, bf16[768,1280]{1,0:T(8,128)(2,1)}, u32[]{:S(2)}) copy-start(bf16[768,1280]{1,0:T(8,128)(2,1)} %patches_ref) | copy-start | bytes 5898244
  17.5 11.2 %collective-permute-start.10 = (bf16[2,800,128]{2,1,0:T(8,128)(2,1)S(1)}, bf16[2,800,128]{2,1,0:T(8,128)(2,1)S(1)}, u32[]{:S(2)}, u32[]{:S(2)}) collective-permute-start(bf16[2,800,128]{2,1,0:T(8,128)(2,1)S(1)} %pad_maximum_fusion.1), channel_id=1, source_target_pairs={{0,8},{4,12},{8,0},{12,4},{1,9},{5,13},{9,1},{13,5},{2,10},{6,14},... | collective-permute-start | bytes 1228808 | tf_op jit(solution)/shard_map/ppermute | solution.py:26
  18.0 3.3 %collective-permute-start.6 = (bf16[800,128]{1,0:T(8,128)(2,1)S(1)}, bf16[800,128]{1,0:T(8,128)(2,1)S(1)}, u32[]{:S(2)}, u32[]{:S(2)}) collective-permute-start(bf16[800,128]{1,0:T(8,128)(2,1)S(1)} %collective-permute-done.2.refs_3_), channel_id=1, source_target_pairs={{0,4},{4,0},{8,12},{12,8},{1,5},{5,1},{9,13},{13,9},{2,6},{6,2},{1... | collective-permute-start | bytes 614408 | tf_op jit(solution)/shard_map/ppermute | solution.py:26
  18.2 3.1 %collective-permute-start.7 = (bf16[800,128]{1,0:T(8,128)(2,1)S(1)}, bf16[800,128]{1,0:T(8,128)(2,1)S(1)}, u32[]{:S(2)}, u32[]{:S(2)}) collective-permute-start(bf16[800,128]{1,0:T(8,128)(2,1)S(1)} %collective-permute-done.3.refs_4_), channel_id=1, source_target_pairs={{0,4},{4,0},{8,12},{12,8},{1,5},{5,1},{9,13},{13,9},{2,6},{6,2},{1... | collective-permute-start | bytes 614408 | tf_op jit(solution)/shard_map/ppermute | solution.py:26
  19.8 8.9 %collective-permute-start.9 = (bf16[800,128]{1,0:T(8,128)(2,1)S(1)}, bf16[800,128]{1,0:T(8,128)(2,1)S(1)}, u32[]{:S(2)}, u32[]{:S(2)}) collective-permute-start(bf16[800,128]{1,0:T(8,128)(2,1)S(1)} %collective-permute-done.8.refs_6_), channel_id=1, source_target_pairs={{0,16},{16,0},{1,17},{17,1},{2,18},{18,2},{3,19},{19,3},{4,20},{20... | collective-permute-start | bytes 614408 | tf_op jit(solution)/shard_map/ppermute | solution.py:26
  28.7 17.6 %copy-start.4 = (f32[1280]{0:T(1024)S(1)}, f32[1280]{0:T(1024)}, u32[]{:S(2)}) copy-start(f32[1280]{0:T(1024)} %refs_14_.1) | copy-start | bytes 15364
  28.8 15.7 %collective-permute-start.14 = (bf16[2,800,128]{2,1,0:T(8,128)(2,1)S(1)}, bf16[2,800,128]{2,1,0:T(8,128)(2,1)S(1)}, u32[]{:S(2)}, u32[]{:S(2)}) collective-permute-start(bf16[2,800,128]{2,1,0:T(8,128)(2,1)S(1)} %pad_maximum_fusion.2), channel_id=1, source_target_pairs={{0,8},{4,12},{8,0},{12,4},{1,9},{5,13},{9,1},{13,5},{2,10},{6,14},... | collective-permute-start | bytes 1228808 | tf_op jit(solution)/shard_map/ppermute | solution.py:26
  30.0 14.6 %collective-permute-start.15 = (bf16[4,800,128]{2,1,0:T(8,128)(2,1)S(1)}, bf16[4,800,128]{2,1,0:T(8,128)(2,1)S(1)}, u32[]{:S(2)}, u32[]{:S(2)}) collective-permute-start(bf16[4,800,128]{2,1,0:T(8,128)(2,1)S(1)} %pad_maximum_fusion), channel_id=1, source_target_pairs={{0,4},{4,0},{8,12},{12,8},{1,5},{5,1},{9,13},{13,9},{2,6},{6,2},{1... | collective-permute-start | bytes 2457608 | tf_op jit(solution)/shard_map/ppermute | solution.py:26
  30.0 8.0 %collective-permute-start.11 = (bf16[480,128]{1,0:T(8,128)(2,1)S(1)}, bf16[480,128]{1,0:T(8,128)(2,1)S(1)}, u32[]{:S(2)}, u32[]{:S(2)}) collective-permute-start(bf16[480,128]{1,0:T(8,128)(2,1)S(1)} %get-tuple-element.62), channel_id=1, source_target_pairs={{0,1},{1,0},{2,3},{3,2},{4,5},{5,4},{6,7},{7,6},{8,9},{9,8},{10,11... | collective-permute-start | bytes 368648 | tf_op jit(solution)/shard_map/ppermute | solution.py:26
  32.1 12.4 %collective-permute-start.12 = (bf16[480,128]{1,0:T(8,128)(2,1)S(1)}, bf16[480,128]{1,0:T(8,128)(2,1)S(1)}, u32[]{:S(2)}, u32[]{:S(2)}) collective-permute-start(bf16[480,128]{1,0:T(8,128)(2,1)S(1)} %get-tuple-element.63), channel_id=1, source_target_pairs={{0,2},{1,3},{2,0},{3,1},{4,6},{5,7},{6,4},{7,5},{8,10},{9,11},{10,... | collective-permute-start | bytes 368648 | tf_op jit(solution)/shard_map/ppermute | solution.py:26
  34.7 9.8 %collective-permute-start.13 = (bf16[480,128]{1,0:T(8,128)(2,1)S(1)}, bf16[480,128]{1,0:T(8,128)(2,1)S(1)}, u32[]{:S(2)}, u32[]{:S(2)}) collective-permute-start(bf16[480,128]{1,0:T(8,128)(2,1)S(1)} %get-tuple-element.64), channel_id=1, source_target_pairs={{0,3},{1,2},{2,1},{3,0},{4,7},{5,6},{6,5},{7,4},{8,11},{9,10},{10,... | collective-permute-start | bytes 368648 | tf_op jit(solution)/shard_map/ppermute | solution.py:26
  38.0 6.5 %collective-permute-start.16 = (bf16[2,800,128]{2,1,0:T(8,128)(2,1)S(1)}, bf16[2,800,128]{2,1,0:T(8,128)(2,1)S(1)}, u32[]{:S(2)}, u32[]{:S(2)}) collective-permute-start(bf16[2,800,128]{2,1,0:T(8,128)(2,1)S(1)} %collective-permute-done.10.refs_9_), channel_id=1, source_target_pairs={{0,4},{4,0},{8,12},{12,8},{1,5},{5,1},{9,13},{13,9},{2,6},{6,2},{1... | collective-permute-start | bytes 1228808 | tf_op jit(solution)/shard_map/ppermute | solution.py:26
  44.5 1.7 %collective-permute-start.17 = (bf16[2,800,128]{2,1,0:T(8,128)(2,1)S(1)}, bf16[2,800,128]{2,1,0:T(8,128)(2,1)S(1)}, u32[]{:S(2)}, u32[]{:S(2)}) collective-permute-start(bf16[2,800,128]{2,1,0:T(8,128)(2,1)S(1)} %collective-permute-done.14.refs_10_), channel_id=1, source_target_pairs={{0,4},{4,0},{8,12},{12,8},{1,5},{5,1},{9,13},{13,9},{2,6},{6,2},{1... | collective-permute-start | bytes 1228808 | tf_op jit(solution)/shard_map/ppermute | solution.py:26
  46.3 10.8 %copy-start.5 = (s32[192]{0:T(256)S(1)}, s32[192]{0:T(256)}, u32[]{:S(2)}) copy-start(s32[192]{0:T(256)} %param.9) | copy-start | bytes 2308
  48.2 8.9 %collective-permute-start.19 = (bf16[96,1280]{1,0:T(8,128)(2,1)S(1)}, bf16[96,1280]{1,0:T(8,128)(2,1)S(1)}, u32[]{:S(2)}, u32[]{:S(2)}) collective-permute-start(bf16[96,1280]{1,0:T(8,128)(2,1)S(1)} %get-tuple-element.78.refs_4_), channel_id=1, source_target_pairs={{0,8},{4,12},{8,0},{12,4},{1,9},{5,13},{9,1},{13,5},{2,10},{6,14},... | collective-permute-start | bytes 737288 | tf_op jit(solution)/shard_map/ppermute | solution.py:26
  48.5 14.2 %collective-permute-start.18 = (bf16[96,1280]{1,0:T(8,128)(2,1)S(1)}, bf16[96,1280]{1,0:T(8,128)(2,1)S(1)}, u32[]{:S(2)}, u32[]{:S(2)}) collective-permute-start(bf16[96,1280]{1,0:T(8,128)(2,1)S(1)} %get-tuple-element.76.refs_5_), channel_id=1, source_target_pairs={{0,8},{4,12},{8,0},{12,4},{1,9},{5,13},{9,1},{13,5},{2,10},{6,14},... | collective-permute-start | bytes 737288 | tf_op jit(solution)/shard_map/ppermute | solution.py:26
  57.1 5.7 %collective-permute-start.20 = (bf16[96,1280]{1,0:T(8,128)(2,1)S(1)}, bf16[96,1280]{1,0:T(8,128)(2,1)S(1)}, u32[]{:S(2)}, u32[]{:S(2)}) collective-permute-start(bf16[96,1280]{1,0:T(8,128)(2,1)S(1)} %collective-permute-done.19.refs_8_), channel_id=1, source_target_pairs={{0,4},{4,0},{8,12},{12,8},{1,5},{5,1},{9,13},{13,9},{2,6},{6,2},{1... | collective-permute-start | bytes 737288 | tf_op jit(solution)/shard_map/ppermute | solution.py:26
  57.1 4.5 %collective-permute-start.21 = (s32[1,192]{1,0:T(1,128)S(1)}, s32[1,192]{1,0:T(1,128)S(1)}, u32[]{:S(2)}, u32[]{:S(2)}) collective-permute-start(s32[1,192]{1,0:T(1,128)S(1)} %bitcast.25), channel_id=1, source_target_pairs={{0,8},{4,12},{8,0},{12,4},{1,9},{5,13},{9,1},{13,5},{2,10},{6,14},... | collective-permute-start | bytes 2312 | tf_op jit(solution)/shard_map/ppermute | solution.py:26
  61.6 1.2 %collective-permute-start.22 = (s32[2,1,192]{2,1,0:T(1,128)S(1)}, s32[2,1,192]{2,1,0:T(1,128)S(1)}, u32[]{:S(2)}, u32[]{:S(2)}) collective-permute-start(s32[2,1,192]{2,1,0:T(1,128)S(1)} %pad_add_fusion), channel_id=1, source_target_pairs={{0,4},{4,0},{8,12},{12,8},{1,5},{5,1},{9,13},{13,9},{2,6},{6,2},{1... | collective-permute-start | bytes 4616 | tf_op jit(solution)/shard_map/ppermute | solution.py:26
  61.6 2.0 %collective-permute-start.24 = (bf16[96,1280]{1,0:T(8,128)(2,1)S(1)}, bf16[96,1280]{1,0:T(8,128)(2,1)S(1)}, u32[]{:S(2)}, u32[]{:S(2)}) collective-permute-start(bf16[96,1280]{1,0:T(8,128)(2,1)S(1)} %get-tuple-element.76.refs_5_), channel_id=1, source_target_pairs={{0,4},{4,0},{8,12},{12,8},{1,5},{5,1},{9,13},{13,9},{2,6},{6,2},{1... | collective-permute-start | bytes 737288 | tf_op jit(solution)/shard_map/ppermute | solution.py:26
  62.1 1.5 %collective-permute-start.23 = (bf16[96,1280]{1,0:T(8,128)(2,1)S(1)}, bf16[96,1280]{1,0:T(8,128)(2,1)S(1)}, u32[]{:S(2)}, u32[]{:S(2)}) collective-permute-start(bf16[96,1280]{1,0:T(8,128)(2,1)S(1)} %get-tuple-element.78.refs_4_), channel_id=1, source_target_pairs={{0,4},{4,0},{8,12},{12,8},{1,5},{5,1},{9,13},{13,9},{2,6},{6,2},{1... | collective-permute-start | bytes 737288 | tf_op jit(solution)/shard_map/ppermute | solution.py:26
  62.8 1.5 %collective-permute-start.25 = (bf16[96,1280]{1,0:T(8,128)(2,1)S(1)}, bf16[96,1280]{1,0:T(8,128)(2,1)S(1)}, u32[]{:S(2)}, u32[]{:S(2)}) collective-permute-start(bf16[96,1280]{1,0:T(8,128)(2,1)S(1)} %collective-permute-done.18.refs_9_), channel_id=1, source_target_pairs={{0,4},{4,0},{8,12},{12,8},{1,5},{5,1},{9,13},{13,9},{2,6},{6,2},{1... | collective-permute-start | bytes 737288 | tf_op jit(solution)/shard_map/ppermute | solution.py:26
  (1 other events, 0.7 us)

commit v9 on v8

--- a/solution.py
+++ b/solution.py
@@ -1,4 +1,5 @@
 import functools
+import math
 
 import jax
 import jax.numpy as jnp
@@ -84,15 +85,18 @@
     return jnp.concatenate([p[:rows], p[rows : 2 * rows]], axis=1), rest
 
 
-def pack_kernel(index_ref, qkv_ref, first_ref, value_ref, all_ref):
-    for j in range(3):
+def pack_kernel(qkv_ref, all_ref, *third_refs):
+    for j, ref in enumerate(third_refs):
         all_ref[j] = pack(qkv_ref[j])
-    first_ref[...] = all_ref[index_ref[2]]
-    value_ref[...] = all_ref[2]
-
-
-def pack_proj_kernel(proj_ref, out_ref):
-    out_ref[...] = pack(proj_ref[...])
+        ref[...] = all_ref[j]
+
+
+def pack_proj_kernel(proj_ref, all_ref, low_ref, high_ref):
+    half = low_ref.shape[0]
+    for t in range(2 * half):
+        all_ref[t] = pack(proj_ref[t])
+    low_ref[...] = all_ref[:half]
+    high_ref[...] = all_ref[half:]
 
 
 def norm_kernel(index_ref, patches_ref, gain_ref, hidden_ref, own_ref):
@@ -113,43 +117,84 @@
         ).astype(BF16)
 
 
-def attend(index_ref, hidden_ref, valid_ref, w_ref, out_refs, q_ref, k_ref, v_ref, mix_ref):
-    rows, width = q_ref.shape
+def load_weights(me, depth, width, count, blocks, w_ref):
+    main = 2 * LANES
+    for key, thirds in enumerate(blocks):
+        rows = pl.ds(pl.multiple_of((me ^ key) * depth, depth), depth)
+        tails = []
+        for j, third in enumerate(thirds):
+            w_ref[rows, j * main : (j + 1) * main], tail = unpack(third, depth, width)
+            tails.append(tail)
+        w_ref[rows, count * main :] = tails[0] if count == 1 else jnp.concatenate(tails, axis=1)
+
+
+def score_kernel(n_ctx, width, index_ref, hidden_ref, valid_ref, *refs):
+    own_ref, twin_ref = refs[:2]
+    others = refs[2 : 2 + 2 * (n_ctx - 2)]
+    out_ref, w_ref, q_ref, k_ref = refs[2 + len(others) :]
+    rows, feat = hidden_ref.shape
     heads = width // HD
     main = 2 * LANES
     rest = width - main
-    qkv = jnp.dot(hidden_ref[...], w_ref[...], preferred_element_type=F32)
-    for j, ref in enumerate((q_ref, k_ref, v_ref)):
-        ref[:, :main] = qkv[:, j * main : (j + 1) * main].astype(BF16)
-        at = 3 * main + j * rest
-        ref[:, main:] = qkv[:, at : at + rest].astype(BF16)
-    lane = lax.broadcasted_iota(jnp.int32, (1, width), 1)
-    head_masks = [one_hot((lane >= h * HD) & (lane < (h + 1) * HD)) for h in range(heads)]
+    blocks = [[own_ref[0], own_ref[1]], [twin_ref[0], twin_ref[1]]]
+    for key in range(2, n_ctx):
+        blocks.append([others[2 * key - 4][...], others[2 * key - 3][...]])
+    load_weights(index_ref[0], feat // n_ctx, width, 2, blocks, w_ref)
+    qk = jnp.dot(hidden_ref[...], w_ref[...], preferred_element_type=F32)
+    for j, ref in enumerate((q_ref, k_ref)):
+        ref[:, :main] = qk[:, j * main : (j + 1) * main].astype(BF16)
+        at = 2 * main + j * rest
+        ref[:, main:] = qk[:, at : at + rest].astype(BF16)
     q_win = lax.broadcasted_iota(jnp.int32, (PAIR, PAIR), 0) // WIN
     k_win = lax.broadcasted_iota(jnp.int32, (PAIR, PAIR), 1) // WIN
     same = q_win == k_win
     floor = jnp.where(same, F32(-1e30), F32(-3e38))
+    zero = jnp.zeros((HD, PAIR), BF16)
+    factor = F32(HD ** (-0.5) * math.log2(math.e))
+    for p in range(rows // PAIR):
+        at = p * PAIR
+        turned = k_ref[at : at + PAIR, :].T
+        k_all = jnp.concatenate(
+            [
+                jnp.concatenate(
+                    [turned[h * HD : (h + 1) * HD] if i == h else zero for i in range(heads)], axis=1
+                )
+                for h in range(heads)
+            ],
+            axis=0,
+        )
+        scores = jnp.dot(q_ref[at : at + PAIR, :], k_all, preferred_element_type=F32)
+        seen = same & (valid_ref[p : p + 1, :] > 0)
+        for h in range(heads):
+            s = jnp.where(seen, scores[:, h * PAIR : (h + 1) * PAIR], floor)
+            e = jnp.exp2((s - jnp.max(s, axis=-1, keepdims=True)) * factor)
+            out_ref[at : at + PAIR, h * PAIR : (h + 1) * PAIR] = e.astype(BF16)
+
+
+def mix_kernel(n_ctx, width, index_ref, hidden_ref, exps_ref, *refs):
+    own_ref, twin_ref = refs[:2]
+    others = refs[2:n_ctx]
+    *out_refs, w_ref, v_ref, mix_ref = refs[n_ctx:]
+    rows, feat = hidden_ref.shape
+    heads = width // HD
+    blocks = [[own_ref[2]], [twin_ref[2]]] + [[ref[...]] for ref in others]
+    load_weights(index_ref[0], feat // n_ctx, width, 1, blocks, w_ref)
+    v_ref[...] = jnp.dot(hidden_ref[...], w_ref[...], preferred_element_type=F32).astype(BF16)
+    lane = lax.broadcasted_iota(jnp.int32, (1, width), 1)
+    head_masks = [one_hot((lane >= h * HD) & (lane < (h + 1) * HD)) for h in range(heads)]
+    ones = jnp.concatenate([jnp.broadcast_to(m, (PAIR, width)) for m in head_masks], axis=0)
     pick = PAIR // 4
     src = lax.broadcasted_iota(jnp.int32, (PAIR, PAIR), 1)
     dst = lax.broadcasted_iota(jnp.int32, (PAIR, PAIR), 0)
     order = one_hot(src == 4 * (dst % pick) + dst // pick)
     for p in range(rows // PAIR):
         at = p * PAIR
-        q = q_ref[at : at + PAIR, :]
-        k = k_ref[at : at + PAIR, :]
+        exps = exps_ref[at : at + PAIR, :]
         v = v_ref[at : at + PAIR, :]
-        k_all = jnp.concatenate([k * m for m in head_masks], axis=0)
         v_all = jnp.concatenate([v * m for m in head_masks], axis=0)
-        scores = lax.dot_general(q, k_all, (((1,), (1,)), ((), ())), preferred_element_type=F32)
-        live = valid_ref[p : p + 1, :] > 0
-        weights = []
-        for h in range(heads):
-            s = scores[:, h * PAIR : (h + 1) * PAIR] * F32(HD ** (-0.5))
-            s = jnp.where(same & live, s, floor)
-            e = jnp.exp(s - jnp.max(s, axis=-1, keepdims=True))
-            weights.append((e / jnp.sum(e, axis=-1, keepdims=True)).astype(BF16))
-        w_all = jnp.concatenate(weights, axis=1)
-        mixed = jnp.dot(w_all, v_all, preferred_element_type=F32).astype(BF16)
+        mixed = jnp.dot(exps, v_all, preferred_element_type=F32)
+        total = jnp.dot(exps, ones, preferred_element_type=F32)
+        mixed = (mixed / total).astype(BF16)
         mixed = jnp.dot(order, mixed, preferred_element_type=F32).astype(BF16)
         for t in range(4):
             mix_ref[t, p * pick : (p + 1) * pick, :] = mixed[t * pick : (t + 1) * pick]
@@ -157,39 +202,13 @@
         out_ref[...] = pack(mix_ref[index_ref[1] ^ s])
 
 
-def attention_kernel(n_ctx, width, index_ref, hidden_ref, valid_ref, *refs):
-    shards = list(refs[: 2 + 3 * (n_ctx - 2)])
-    *out_refs, w_ref, q_ref, k_ref, v_ref, mix_ref = refs[len(shards) :]
-    depth = w_ref.shape[0] // n_ctx
-    me = index_ref[0]
-    flip = index_ref[2] > 0
-    main = 2 * LANES
-    for key in range(n_ctx):
-        rows = pl.ds(pl.multiple_of((me ^ key) * depth, depth), depth)
-        if key < 2:
-            block = shards.pop(0)
-            thirds = [block[j] for j in range(3)]
-        else:
-            first, second, value = [shards.pop(0)[...] for _ in range(3)]
-            thirds = [jnp.where(flip, second, first), jnp.where(flip, first, second), value]
-        tails = []
-        for j, third in enumerate(thirds):
-            w_ref[rows, j * main : (j + 1) * main], tail = unpack(third, depth, width)
-            tails.append(tail)
-        w_ref[rows, 3 * main :] = jnp.concatenate(tails, axis=1)
-    attend(index_ref, hidden_ref, valid_ref, w_ref, out_refs, q_ref, k_ref, v_ref, mix_ref)
-
-
 def project_kernel(n_ctx, width, col, index_ref, *refs):
-    *blocks, own_ref, gain_ref = refs[4 : -HALVES - 1]
-    *out_refs, part_ref = refs[-HALVES - 1 :]
+    *blocks, own_ref, gain_ref = refs[4 : -HALVES - 2]
+    *out_refs, part_ref, mix_ref = refs[-HALVES - 2 :]
     rows = own_ref.shape[0]
-    mixes = [unpack(m[...], rows, width) for m in refs[:4]]
-    flip = index_ref[2] > 0
-    mixes[2:] = [
-        [jnp.where(flip, b, a) for a, b in zip(mixes[2], mixes[3])],
-        [jnp.where(flip, a, b) for a, b in zip(mixes[2], mixes[3])],
-    ]
+    for s in range(4):
+        mix_ref[index_ref[1] ^ s] = refs[s][...]
+    mixes = [unpack(mix_ref[t], rows, width) for t in range(4)]
     me = index_ref[0]
     main = 2 * LANES
     mixed = jnp.concatenate([m for m, _ in mixes] + [r for _, r in mixes], axis=1)
@@ -197,8 +216,8 @@
     rests = []
     for key in range(n_ctx):
         pieces = []
-        for ref in [blocks.pop(0) for _ in range((4, 1)[key] if key < 2 else 2)]:
-            pieces += [ref[...]] if len(ref.shape) == 2 else [ref[i] for i in range(ref.shape[0])]
+        for ref in [blocks.pop(0) for _ in range(1 if key < 2 else 2)]:
+            pieces += [ref[i] for i in range(ref.shape[0])]
         halves = [unpack(p, width, col) for p in pieces]
         both = []
         for half in ([h[0] for h in halves], [h[1] for h in halves]):
@@ -258,39 +277,20 @@
 
     third = packed_shape(depth, width)
     piece = packed_shape(width, col)
-    first, value, own = pl.pallas_call(
+    own, *thirds = pl.pallas_call(
         pack_kernel,
-        out_shape=(shape(*third), shape(*third), shape(3, *third)),
-        in_specs=[SMEM, VMEM],
-        out_specs=(VMEM,) * 3,
+        out_shape=(shape(3, *third),) + (shape(*third),) * 3,
+        in_specs=[VMEM],
+        out_specs=(VMEM,) * 4,
         compiler_params=params(8),
         name="pack",
-    )(index, jnp.transpose(w_qkv, (1, 0, 2)))
-    w_proj = pl.pallas_call(
-        pack_proj_kernel,
-        out_shape=shape(*piece),
-        in_specs=[VMEM],
-        out_specs=VMEM,
-        compiler_params=params(8),
-        name="pack_proj",
-    )(w_proj)
-    first = gather_cross(first, n_ctx)
-    value = gather_cross(value, n_ctx)
-    twin = over_core(own)
-    far = lax.ppermute(
-        w_proj,
-        ("dp", "tensor"),
-        [
-            (d * n_ten + t, d * n_ten + (t ^ (2 + d % 2)))
-            for d in range(n_dp)
-            for t in range(n_ten)
-        ],
-    )
-    by_one = swap(w_proj, "tensor", n_ten, 1)
-    first, twin, patches = together(first, twin, patches)
-
-    second = {k: over_dp(first[k]) for k in cross}
-    first_twin = {k: over_core(first[k]) for k in cross}
+    )(jnp.transpose(w_qkv, (1, 0, 2)))
+    proj = lax.all_gather(w_proj, "tensor")
+    query = gather_cross(thirds[0], n_ctx)
+    key = gather_cross(thirds[1], n_ctx)
+    value = gather_cross(thirds[2], n_ctx)
+    query, patches = together(query, patches)
+    query_twin = {k: over_core(query[k]) for k in cross}
     hidden, own_patches = pl.pallas_call(
         norm_kernel,
         out_shape=(shape(rows, feat), shape(groups, feat)),
@@ -299,46 +299,67 @@
         compiler_params=params(16),
         name="norm",
     )(index, patches, gain_attn)
-    by_one, hidden = together(by_one, hidden)
-    low = gather_cross(jnp.stack([w_proj, by_one]), n_ctx)
-    second, value, first_twin, hidden = together(second, value, first_twin, hidden)
-
-    second_twin = {k: over_core(second[k]) for k in cross}
-    value_twin = {k: over_core(value[k]) for k in cross}
-    far, *_ = together(far, *second.values())
-    far2 = over_dp(far)
+    key, hidden = together(key, hidden)
+    twin = over_core(own)
+    key_twin = {k: over_core(key[k]) for k in cross}
 
     shard_list = [own, twin]
     for k in cross:
-        shard_list += [first[k], second[k], value[k], first_twin[k], second_twin[k], value_twin[k]]
-
-    mix_shapes = (shape(*packed_shape(groups, width)),) * n_ten
+        shard_list += [query[k], key[k], query_twin[k], key_twin[k]]
+    exps = pl.pallas_call(
+        functools.partial(score_kernel, n_ctx, width),
+        out_shape=shape(rows, width // HD * PAIR),
+        in_specs=[SMEM] + [VMEM] * (2 + len(shard_list)),
+        out_specs=VMEM,
+        scratch_shapes=[pltpu.VMEM((feat, 2 * width), BF16)] + [pltpu.VMEM((rows, width), BF16)] * 2,
+        compiler_params=params(20),
+        name="scores",
+    )(index, hidden, valid.reshape(rows // PAIR, PAIR), *shard_list)
+    exps, value, proj = together(exps, value, proj)
+    value_twin = {k: over_core(value[k]) for k in cross}
+    proj, proj_low, proj_high = pl.pallas_call(
+        pack_proj_kernel,
+        out_shape=(shape(n_ten, *piece), shape(n_ten // 2, *piece), shape(n_ten // 2, *piece)),
+        in_specs=[VMEM],
+        out_specs=(VMEM,) * 3,
+        compiler_params=params(12),
+        name="pack_proj",
+    )(proj)
+    low = gather_cross(proj_low, n_ctx)
+    high = gather_cross(proj_high, n_ctx)
+    value_list = []
+    for k in cross:
+        value_list += [value[k], value_twin[k]]
     mixed = pl.pallas_call(
-        functools.partial(attention_kernel, n_ctx, width),
-        out_shape=mix_shapes,
-        in_specs=[SMEM] + [VMEM] * (2 + len(shard_list)),
+        functools.partial(mix_kernel, n_ctx, width),
+        out_shape=(shape(*packed_shape(groups, width)),) * n_ten,
+        in_specs=[SMEM] + [VMEM] * (2 + n_ctx),
         out_specs=(VMEM,) * n_ten,
-        scratch_shapes=[pltpu.VMEM((feat, 3 * width), BF16)]
-        + [pltpu.VMEM((rows, width), BF16)] * 3
-        + [pltpu.VMEM((4, groups, width), BF16)],
-        compiler_params=params(20),
-        name="attention",
-    )(index, hidden, valid.reshape(rows // PAIR, PAIR), *shard_list)
-
-    mixed, far, far2, low = together(mixed, far, far2, low)
-    mixed = [mixed[0]] + [swap(mixed[s], "tensor", n_ten, s) for s in range(1, n_ten)]
-    high = gather_cross(jnp.stack([far, far2]), n_ctx)
-    blocks = [w_proj, by_one, far, far2, over_core(jnp.stack([w_proj, by_one, far, far2]))]
-    low_twin = {k: over_core(low[k]) for k in cross}
-    mixed, high = together(mixed, high)
+        scratch_shapes=[
+            pltpu.VMEM((feat, width), BF16),
+            pltpu.VMEM((rows, width), BF16),
+            pltpu.VMEM((4, groups, width), BF16),
+        ],
+        compiler_params=params(16),
+        name="mix",
+    )(index, hidden, exps, own, twin, *value_list)
+
+    received = {s: swap(mixed[s], "tensor", n_ten, s) for s in (2, 3, 1)}
+    mixed = [mixed[0]] + [received[s] for s in range(1, n_ten)]
+    proj_twin = over_core(proj)
+    mixed, low, high = together(mixed, low, high)
+    blocks = [proj, proj_twin]
     for k in cross:
-        blocks += [low[k], high[k], low_twin[k], over_core(high[k])]
+        blocks += [low[k], high[k], over_core(low[k]), over_core(high[k])]
     done = pl.pallas_call(
         functools.partial(project_kernel, n_ctx, width, col),
         out_shape=(shape(groups // HALVES, feat),) * HALVES,
         in_specs=[SMEM] + [VMEM] * (n_ten + len(blocks) + 2),
         out_specs=(VMEM,) * HALVES,
-        scratch_shapes=[pltpu.VMEM((n_ctx, groups, col), F32)],
+        scratch_shapes=[
+            pltpu.VMEM((n_ctx, groups, col), F32),
+            pltpu.VMEM((n_ten, *packed_shape(groups, width)), BF16),
+        ],
         compiler_params=params(24),
         name="project",
     )(index, *mixed, *blocks, own_patches, gain_merge)

time: 66.5 us -> 85.3 us (1.28)
  blocking collectives: 0 us -> 22.4 us
  starting transfers between devices: 20.8 us -> 17.2 us
  waiting for transfers between devices: 27.1 us -> 28.3 us
  local copies, waits for them, and re-layouts: 4.32 us -> 3.37 us
    all_gather x0 -> x1, blocking collectives: none -> 22.4 us  [local(): proj = lax.all_gather(w_proj, 'tensor')]
    ppermute x25 -> x23, waiting for transfers between devices: 25.7 us -> 28.3 us  [swap(): return lax.ppermute(x, axis, [(i, i ^ bit) for i in range(size)])]
    ppermute x1 -> x0, starting transfers between devices: 2.59 us -> none  [local(): lax.ppermute(w_proj, ('dp', 'tensor'), [(d * n_ten + t, d * n_ten + (t ^...]
    ppermute x1 -> x0, waiting for transfers between devices: 1.32 us -> none  [local(): lax.ppermute(w_proj, ('dp', 'tensor'), [(d * n_ten + t, d * n_ten + (t ^...]
    ppermute x25 -> x23, starting transfers between devices: 18.2 us -> 17.2 us  [swap(): return lax.ppermute(x, axis, [(i, i ^ bit) for i in range(size)])]
    unnamed x14, local copies, waits for them, and re-layouts: 4.32 us -> 3.37 us
    pallas_call x3 -> x4, Pallas kernels: 8.23 us -> 8.13 us  [the longest x1 3.91 us: local(): pl.pallas_call(functools.partial(score_kernel, n_ctx, width), out_shape=s...]
  transfers between devices with their start and end apart: 26 -> 23, of which waited for: 10 -> 11; matrix products, arithmetic and copies ran while one was open for 0% -> 0% of each run, Pallas kernels for 14% -> 11%
where the time goes in v9:
time: 85.3 us; the launch traced here: 85.1 us
  waiting for transfers between devices  28.3 us (33%)
  blocking collectives  22.4 us (26%)
  starting transfers between devices  17.2 us (20%)
  Pallas kernels  13.6 us (16%)
  local copies, waits for them, and re-layouts  3.37 us (4%)
    ppermute x23, waiting for transfers between devices, swap(): return lax.ppermute(x, axis, [(i, i ^ bit) for i in range(size)])  28.3 us
    all_gather x1, blocking collectives, local(): proj = lax.all_gather(w_proj, 'tensor')  22.4 us
    ppermute x23, starting transfers between devices, swap(): return lax.ppermute(x, axis, [(i, i ^ bit) for i in range(size)])  17.2 us
    pallas_call x1, Pallas kernels, local(): pl.pallas_call(functools.partial(score_kernel, n_ctx, width), out_shape=s...  3.91 us
    pallas_call x1, Pallas kernels, local(): pl.pallas_call(functools.partial(mix_kernel, n_ctx, width), out_shape=(sh...  3.85 us
    unnamed x14, local copies, waits for them, and re-layouts  3.37 us
    pallas_call x1, Pallas kernels, local(): pl.pallas_call(functools.partial(project_kernel, n_ctx, width, col), out_...  1.95 us
    pallas_call x1, Pallas kernels, local(): pl.pallas_call(functools.partial(place_kernel, n_ctx), out_shape=shape(gr...  1.92 us
  transfers between devices with their start and end apart: 23, of which 11 were waited for; matrix products, arithmetic and copies ran while one was open for 0% of the time, Pallas kernels for 11%

profile of v9, /device:TPU:0, one launch (start us, length us, event | category | flops | bytes accessed | tf_op | source)
XLA Modules:
  0.0 85.1 jit_solution(16766784335145251697)
XLA Ops:
  0.0 1.1 %copy-done.1 = bf16[320,3,320]{2,0,1:T(8,128)(2,1)S(1)} copy-done((bf16[320,3,320]{2,0,1:T(8,128)(2,1)S(1)}, bf16[320,3,320]{2,0,1:T(8,128)(2,1)}, u32[]{:S(2)}) %copy-start.1) | copy-done | bytes 614424
  1.3 0.5 collective-permute-start.2
  1.8 2.6 %collective-permute-start.1 = (bf16[800,128]{1,0:T(8,128)(2,1)S(1)}, bf16[800,128]{1,0:T(8,128)(2,1)S(1)}, u32[]{:S(2)}, u32[]{:S(2)}) collective-permute-start(bf16[800,128]{1,0:T(8,128)(2,1)S(1)} %get-tuple-element.39), channel_id=1, source_target_pairs={{0,8},{4,12},{8,0},{12,4},{1,9},{5,13},{9,1},{13,5},{2,10},{6,14},... | collective-permute-start | bytes 614408 | tf_op jit(solution)/shard_map/ppermute | solution.py:27
  4.5 1.9 %collective-permute-start.5 = (bf16[800,128]{1,0:T(8,128)(2,1)S(1)}, bf16[800,128]{1,0:T(8,128)(2,1)S(1)}, u32[]{:S(2)}, u32[]{:S(2)}) collective-permute-start(bf16[800,128]{1,0:T(8,128)(2,1)S(1)} %get-tuple-element.46), channel_id=1, source_target_pairs={{0,8},{4,12},{8,0},{12,4},{1,9},{5,13},{9,1},{13,5},{2,10},{6,14},... | collective-permute-start | bytes 614408 | tf_op jit(solution)/shard_map/ppermute | solution.py:27
  6.5 3.8 %collective-permute-done.1.refs_2_ = bf16[800,128]{1,0:T(8,128)(2,1)S(1)} collective-permute-done((bf16[800,128]{1,0:T(8,128)(2,1)S(1)}, bf16[800,128]{1,0:T(8,128)(2,1)S(1)}, u32[]{:S(2)}, u32[]{:S(2)}) %collective-permute-start.1) | collective-permute-done | bytes 204832 | tf_op jit(solution)/shard_map/ppermute | solution.py:27
  10.3 1.5 %copy-done = bf16[768,1280]{1,0:T(8,128)(2,1)S(1)} copy-done((bf16[768,1280]{1,0:T(8,128)(2,1)S(1)}, bf16[768,1280]{1,0:T(8,128)(2,1)}, u32[]{:S(2)}) %copy-start) | copy-done | bytes 1966104
  11.9 0.7 copy-done.2
  12.6 1.6 %norm.1 = (bf16[768,1280]{1,0:T(8,128)(2,1)S(1)}, bf16[192,1280]{1,0:T(8,128)(2,1)S(1)}) custom-call(s32[3]{0:T(128)S(1)} %pad_add_fusion.1.index_ref, bf16[768,1280]{1,0:T(8,128)(2,1)S(1)} %copy-done, f32[1280]{0:T(1024)S(1)} %copy-done.2), custom_call_target="tpu_custom_call" | custom-call | tf_op jit(solution)/shard_map/norm/pallas_call | solution.py:294
  14.1 0.6 collective-permute-done.refs_3_
  14.7 0.5 collective-permute-start.4
  15.2 22.4 %all-gather = bf16[1280,320]{1,0:T(8,128)(2,1)S(1)} all-gather(bf16[320,320]{1,0:T(8,128)(2,1)S(1)} %copy-done.6), channel_id=2, replica_groups=mesh['dp'=2,'context'=4,'tensor'=4] {'tensor'}, dimensions={0}, use_global_device_ids=true | all-gather | bytes 1024000 | tf_op jit(solution)/shard_map/all_gather | solution.py:288
  37.7 3.9 %scores.1.exps_ref = bf16[768,512]{1,0:T(8,128)(2,1)S(1)} custom-call(s32[3]{0:T(128)S(1)} %pad_add_fusion.1.index_ref, bf16[768,1280]{1,0:T(8,128)(2,1)S(1)} %get-tuple-element.42.hidden_ref, s32[6,128]{1,0:T(8,128)S(1)} %bitcast.19, bf16[3,800,128]{2,1,0:T(8,128)(2,1)S(1)} %get-tuple-element.43.refs_0_, ...), custom_call_target="tpu_custom_call" | custom-call | tf_op jit(solution)/shard_map/scores/pallas_call | solution.py:309
  41.9 1.6 %collective-permute-start.10 = (bf16[2,800,128]{2,1,0:T(8,128)(2,1)S(1)}, bf16[2,800,128]{2,1,0:T(8,128)(2,1)S(1)}, u32[]{:S(2)}, u32[]{:S(2)}) collective-permute-start(bf16[2,800,128]{2,1,0:T(8,128)(2,1)S(1)} %get-tuple-element.54), channel_id=1, source_target_pairs={{0,8},{4,12},{8,0},{12,4},{1,9},{5,13},{9,1},{13,5},{2,10},{6,14},... | collective-permute-start | bytes 1228808 | tf_op jit(solution)/shard_map/ppermute | solution.py:27
  43.5 0.5 collective-permute-start.11
  44.0 3.8 %mix.1 = (bf16[480,128]{1,0:T(8,128)(2,1)S(1)}, bf16[480,128]{1,0:T(8,128)(2,1)S(1)}, bf16[480,128]{1,0:T(8,128)(2,1)S(1)}, bf16[480,128]{1,0:T(8,128)(2,1)S(1)}) custom-call(s32[3]{0:T(128)S(1)} %pad_add_fusion.1.index_ref, bf16[768,1280]{1,0:T(8,128)(2,1)S(1)} %get-tuple-element.42.hidden_ref, bf16[768,512]{1,0:T(8,128)(2,1)S(1)} %scores.1.exps_ref, ...), custom_call_target="tpu_custom_call" | custom-call | tf_op jit(solution)/shard_map/mix/pallas_call | solution.py:333
  48.2 2.7 %collective-permute-start.8 = (bf16[480,128]{1,0:T(8,128)(2,1)S(1)}, bf16[480,128]{1,0:T(8,128)(2,1)S(1)}, u32[]{:S(2)}, u32[]{:S(2)}) collective-permute-start(bf16[480,128]{1,0:T(8,128)(2,1)S(1)} %get-tuple-element.51), channel_id=1, source_target_pairs={{0,2},{1,3},{2,0},{3,1},{4,6},{5,7},{6,4},{7,5},{8,10},{9,11},{10,... | collective-permute-start | bytes 368648 | tf_op jit(solution)/shard_map/ppermute | solution.py:27
  50.9 5.1 %collective-permute-done.7.refs_1_ = bf16[480,128]{1,0:T(8,128)(2,1)S(1)} collective-permute-done((bf16[480,128]{1,0:T(8,128)(2,1)S(1)}, bf16[480,128]{1,0:T(8,128)(2,1)S(1)}, u32[]{:S(2)}, u32[]{:S(2)}) %collective-permute-start.7) | collective-permute-done | bytes 122912 | tf_op jit(solution)/shard_map/ppermute | solution.py:27
  56.0 1.4 %collective-permute-start.9 = (bf16[480,128]{1,0:T(8,128)(2,1)S(1)}, bf16[480,128]{1,0:T(8,128)(2,1)S(1)}, u32[]{:S(2)}, u32[]{:S(2)}) collective-permute-start(bf16[480,128]{1,0:T(8,128)(2,1)S(1)} %get-tuple-element.52), channel_id=1, source_target_pairs={{0,3},{1,2},{2,1},{3,0},{4,7},{5,6},{6,5},{7,4},{8,11},{9,10},{10,... | collective-permute-start | bytes 368648 | tf_op jit(solution)/shard_map/ppermute | solution.py:27
  57.5 5.3 %collective-permute-done.9.refs_3_ = bf16[480,128]{1,0:T(8,128)(2,1)S(1)} collective-permute-done((bf16[480,128]{1,0:T(8,128)(2,1)S(1)}, bf16[480,128]{1,0:T(8,128)(2,1)S(1)}, u32[]{:S(2)}, u32[]{:S(2)}) %collective-permute-start.9) | collective-permute-done | bytes 122912 | tf_op jit(solution)/shard_map/ppermute | solution.py:27
  62.8 0.5 collective-permute-start.14
  63.3 1.2 %collective-permute-done.13.refs_8_ = bf16[2,800,128]{2,1,0:T(8,128)(2,1)S(1)} collective-permute-done((bf16[2,800,128]{2,1,0:T(8,128)(2,1)S(1)}, bf16[2,800,128]{2,1,0:T(8,128)(2,1)S(1)}, u32[]{:S(2)}, u32[]{:S(2)}) %collective-permute-start.13) | collective-permute-done | bytes 409632 | tf_op jit(solution)/shard_map/ppermute | solution.py:27
  64.5 0.6 collective-permute-done.14.refs_9_
  65.1 1.9 %project.1 = (bf16[96,1280]{1,0:T(8,128)(2,1)S(1)}, bf16[96,1280]{1,0:T(8,128)(2,1)S(1)}) custom-call(s32[3]{0:T(128)S(1)} %pad_add_fusion.1.index_ref, bf16[480,128]{1,0:T(8,128)(2,1)S(1)} %get-tuple-element.56.refs_0_, bf16[480,128]{1,0:T(8,128)(2,1)S(1)} %collective-permute-done.7.refs_1_, bf16[480,128]{1,0:T(8,128)(2,1)S(1)} %collective-permute-done.8.refs_2_, ...), custom_call_target="tpu_custom_call" | custom-call | tf_op jit(solution)/shard_map/project/pallas_call | solution.py:354
  67.1 1.6 %collective-permute-start.16 = (bf16[96,1280]{1,0:T(8,128)(2,1)S(1)}, bf16[96,1280]{1,0:T(8,128)(2,1)S(1)}, u32[]{:S(2)}, u32[]{:S(2)}) collective-permute-start(bf16[96,1280]{1,0:T(8,128)(2,1)S(1)} %get-tuple-element.68.refs_4_), channel_id=1, source_target_pairs={{0,8},{4,12},{8,0},{12,4},{1,9},{5,13},{9,1},{13,5},{2,10},{6,14},... | collective-permute-start | bytes 737288 | tf_op jit(solution)/shard_map/ppermute | solution.py:27
  69.2 6.8 %collective-permute-done.16.refs_8_ = bf16[96,1280]{1,0:T(8,128)(2,1)S(1)} collective-permute-done((bf16[96,1280]{1,0:T(8,128)(2,1)S(1)}, bf16[96,1280]{1,0:T(8,128)(2,1)S(1)}, u32[]{:S(2)}, u32[]{:S(2)}) %collective-permute-start.16) | collective-permute-done | bytes 245792 | tf_op jit(solution)/shard_map/ppermute | solution.py:27
  76.0 1.5 %collective-permute-start.18 = (s32[1,192]{1,0:T(1,128)S(1)}, s32[1,192]{1,0:T(1,128)S(1)}, u32[]{:S(2)}, u32[]{:S(2)}) collective-permute-start(s32[1,192]{1,0:T(1,128)S(1)} %bitcast.15), channel_id=1, source_target_pairs={{0,8},{4,12},{8,0},{12,4},{1,9},{5,13},{9,1},{13,5},{2,10},{6,14},... | collective-permute-start | bytes 2312 | tf_op jit(solution)/shard_map/ppermute | solution.py:27
  77.5 3.0 %collective-permute-done.18.refs_2_ = s32[1,192]{1,0:T(1,128)S(1)} collective-permute-done((s32[1,192]{1,0:T(1,128)S(1)}, s32[1,192]{1,0:T(1,128)S(1)}, u32[]{:S(2)}, u32[]{:S(2)}) %collective-permute-start.18) | collective-permute-done | bytes 800 | tf_op jit(solution)/shard_map/ppermute | solution.py:27
  80.5 0.5 collective-permute-start.21
  81.1 0.6 collective-permute-done.19
  81.8 0.7 collective-permute-done.20.refs_6_
  82.5 0.7 collective-permute-done.22.refs_11_
  83.2 1.9 %placement.1 = bf16[192,1280]{1,0:T(8,128)(2,1)} custom-call(s32[3]{0:T(128)S(1)} %pad_add_fusion.1.index_ref, s32[1,192]{1,0:T(1,128)S(1)} %bitcast.17, s32[1,192]{1,0:T(1,128)S(1)} %get-tuple-element.72.refs_1_, s32[1,192]{1,0:T(1,128)S(1)} %collective-permute-done.18.refs_2_, s32[1,192]{1,0:T(1,128)S(1)} %get-tuple-element.71.refs_3_, ...), custom_call_target="tpu_custom_call" | custom-call | tf_op jit(solution)/shard_map/placement/pallas_call | solution.py:385
  (39 shorter events, 1.8 us)
Async XLA Ops:
  0.0 1.1 %copy-start.1 = (bf16[320,3,320]{2,0,1:T(8,128)(2,1)S(1)}, bf16[320,3,320]{2,0,1:T(8,128)(2,1)}, u32[]{:S(2)}) copy-start(bf16[320,3,320]{2,0,1:T(8,128)(2,1)} %param.11) | copy-start | bytes 1843204
  1.1 14.1 %copy-start.6 = (bf16[320,320]{1,0:T(8,128)(2,1)S(1)}, bf16[320,320]{1,0:T(8,128)(2,1)}, u32[]{:S(2)}) copy-start(bf16[320,320]{1,0:T(8,128)(2,1)} %param.12) | copy-start | bytes 614404
  1.1 36.5 %copy-start.5 = (s32[768]{0:T(1024)S(1)}, s32[768]{0:T(1024)}, u32[]{:S(2)}) copy-start(s32[768]{0:T(1024)} %param.8) | copy-start | bytes 9220
  1.3 36.4 %collective-permute-start.2 = (bf16[3,800,128]{2,1,0:T(8,128)(2,1)S(1)}, bf16[3,800,128]{2,1,0:T(8,128)(2,1)S(1)}, u32[]{:S(2)}, u32[]{:S(2)}) collective-permute-start(bf16[3,800,128]{2,1,0:T(8,128)(2,1)S(1)} %get-tuple-element.43.refs_0_), channel_id=1, source_target_pairs={{0,4},{4,0},{8,12},{12,8},{1,5},{5,1},{9,13},{13,9},{2,6},{6,2},{1... | collective-permute-start | bytes 1843208 | tf_op jit(solution)/shard_map/ppermute | solution.py:27
  1.8 8.5 %collective-permute-start.1 = (bf16[800,128]{1,0:T(8,128)(2,1)S(1)}, bf16[800,128]{1,0:T(8,128)(2,1)S(1)}, u32[]{:S(2)}, u32[]{:S(2)}) collective-permute-start(bf16[800,128]{1,0:T(8,128)(2,1)S(1)} %get-tuple-element.39), channel_id=1, source_target_pairs={{0,8},{4,12},{8,0},{12,4},{1,9},{5,13},{9,1},{13,5},{2,10},{6,14},... | collective-permute-start | bytes 614408 | tf_op jit(solution)/shard_map/ppermute | solution.py:27
  4.4 10.3 %collective-permute-start = (bf16[800,128]{1,0:T(8,128)(2,1)S(1)}, bf16[800,128]{1,0:T(8,128)(2,1)S(1)}, u32[]{:S(2)}, u32[]{:S(2)}) collective-permute-start(bf16[800,128]{1,0:T(8,128)(2,1)S(1)} %get-tuple-element.38), channel_id=1, source_target_pairs={{0,8},{4,12},{8,0},{12,4},{1,9},{5,13},{9,1},{13,5},{2,10},{6,14},... | collective-permute-start | bytes 614408 | tf_op jit(solution)/shard_map/ppermute | solution.py:27
  4.5 37.1 %collective-permute-start.5 = (bf16[800,128]{1,0:T(8,128)(2,1)S(1)}, bf16[800,128]{1,0:T(8,128)(2,1)S(1)}, u32[]{:S(2)}, u32[]{:S(2)}) collective-permute-start(bf16[800,128]{1,0:T(8,128)(2,1)S(1)} %get-tuple-element.46), channel_id=1, source_target_pairs={{0,8},{4,12},{8,0},{12,4},{1,9},{5,13},{9,1},{13,5},{2,10},{6,14},... | collective-permute-start | bytes 614408 | tf_op jit(solution)/shard_map/ppermute | solution.py:27
  10.3 1.5 %copy-start = (bf16[768,1280]{1,0:T(8,128)(2,1)S(1)}, bf16[768,1280]{1,0:T(8,128)(2,1)}, u32[]{:S(2)}) copy-start(bf16[768,1280]{1,0:T(8,128)(2,1)} %patches_ref) | copy-start | bytes 5898244
  11.9 0.7 copy-start.2
  14.7 22.9 %collective-permute-start.3 = (bf16[800,128]{1,0:T(8,128)(2,1)S(1)}, bf16[800,128]{1,0:T(8,128)(2,1)S(1)}, u32[]{:S(2)}, u32[]{:S(2)}) collective-permute-start(bf16[800,128]{1,0:T(8,128)(2,1)S(1)} %collective-permute-done.1.refs_2_), channel_id=1, source_target_pairs={{0,4},{4,0},{8,12},{12,8},{1,5},{5,1},{9,13},{13,9},{2,6},{6,2},{1... | collective-permute-start | bytes 614408 | tf_op jit(solution)/shard_map/ppermute | solution.py:27
  14.7 22.9 %collective-permute-start.4 = (bf16[800,128]{1,0:T(8,128)(2,1)S(1)}, bf16[800,128]{1,0:T(8,128)(2,1)S(1)}, u32[]{:S(2)}, u32[]{:S(2)}) collective-permute-start(bf16[800,128]{1,0:T(8,128)(2,1)S(1)} %collective-permute-done.refs_3_), channel_id=1, source_target_pairs={{0,4},{4,0},{8,12},{12,8},{1,5},{5,1},{9,13},{13,9},{2,6},{6,2},{1... | collective-permute-start | bytes 614408 | tf_op jit(solution)/shard_map/ppermute | solution.py:27
  41.6 2.4 %collective-permute-start.6 = (bf16[800,128]{1,0:T(8,128)(2,1)S(1)}, bf16[800,128]{1,0:T(8,128)(2,1)S(1)}, u32[]{:S(2)}, u32[]{:S(2)}) collective-permute-start(bf16[800,128]{1,0:T(8,128)(2,1)S(1)} %collective-permute-done.5.refs_2_), channel_id=1, source_target_pairs={{0,4},{4,0},{8,12},{12,8},{1,5},{5,1},{9,13},{13,9},{2,6},{6,2},{1... | collective-permute-start | bytes 614408 | tf_op jit(solution)/shard_map/ppermute | solution.py:27
  41.9 20.9 %collective-permute-start.10 = (bf16[2,800,128]{2,1,0:T(8,128)(2,1)S(1)}, bf16[2,800,128]{2,1,0:T(8,128)(2,1)S(1)}, u32[]{:S(2)}, u32[]{:S(2)}) collective-permute-start(bf16[2,800,128]{2,1,0:T(8,128)(2,1)S(1)} %get-tuple-element.54), channel_id=1, source_target_pairs={{0,8},{4,12},{8,0},{12,4},{1,9},{5,13},{9,1},{13,5},{2,10},{6,14},... | collective-permute-start | bytes 1228808 | tf_op jit(solution)/shard_map/ppermute | solution.py:27
  43.5 19.3 %collective-permute-start.11 = (bf16[2,800,128]{2,1,0:T(8,128)(2,1)S(1)}, bf16[2,800,128]{2,1,0:T(8,128)(2,1)S(1)}, u32[]{:S(2)}, u32[]{:S(2)}) collective-permute-start(bf16[2,800,128]{2,1,0:T(8,128)(2,1)S(1)} %get-tuple-element.55), channel_id=1, source_target_pairs={{0,8},{4,12},{8,0},{12,4},{1,9},{5,13},{9,1},{13,5},{2,10},{6,14},... | collective-permute-start | bytes 1228808 | tf_op jit(solution)/shard_map/ppermute | solution.py:27
  44.0 21.2 %copy-start.3 = (f32[1280]{0:T(1024)S(1)}, f32[1280]{0:T(1024)}, u32[]{:S(2)}) copy-start(f32[1280]{0:T(1024)} %refs_11_.1) | copy-start | bytes 15364
  44.0 19.3 %collective-permute-start.12 = (bf16[4,800,128]{2,1,0:T(8,128)(2,1)S(1)}, bf16[4,800,128]{2,1,0:T(8,128)(2,1)S(1)}, u32[]{:S(2)}, u32[]{:S(2)}) collective-permute-start(bf16[4,800,128]{2,1,0:T(8,128)(2,1)S(1)} %get-tuple-element.60.refs_4_), channel_id=1, source_target_pairs={{0,4},{4,0},{8,12},{12,8},{1,5},{5,1},{9,13},{13,9},{2,6},{6,2},{1... | collective-permute-start | bytes 2457608 | tf_op jit(solution)/shard_map/ppermute | solution.py:27
  47.8 8.2 %collective-permute-start.7 = (bf16[480,128]{1,0:T(8,128)(2,1)S(1)}, bf16[480,128]{1,0:T(8,128)(2,1)S(1)}, u32[]{:S(2)}, u32[]{:S(2)}) collective-permute-start(bf16[480,128]{1,0:T(8,128)(2,1)S(1)} %get-tuple-element.50), channel_id=1, source_target_pairs={{0,1},{1,0},{2,3},{3,2},{4,5},{5,4},{6,7},{7,6},{8,9},{9,8},{10,11... | collective-permute-start | bytes 368648 | tf_op jit(solution)/shard_map/ppermute | solution.py:27
  48.2 9.2 %collective-permute-start.8 = (bf16[480,128]{1,0:T(8,128)(2,1)S(1)}, bf16[480,128]{1,0:T(8,128)(2,1)S(1)}, u32[]{:S(2)}, u32[]{:S(2)}) collective-permute-start(bf16[480,128]{1,0:T(8,128)(2,1)S(1)} %get-tuple-element.51), channel_id=1, source_target_pairs={{0,2},{1,3},{2,0},{3,1},{4,6},{5,7},{6,4},{7,5},{8,10},{9,11},{10,... | collective-permute-start | bytes 368648 | tf_op jit(solution)/shard_map/ppermute | solution.py:27
  56.0 6.7 %collective-permute-start.9 = (bf16[480,128]{1,0:T(8,128)(2,1)S(1)}, bf16[480,128]{1,0:T(8,128)(2,1)S(1)}, u32[]{:S(2)}, u32[]{:S(2)}) collective-permute-start(bf16[480,128]{1,0:T(8,128)(2,1)S(1)} %get-tuple-element.52), channel_id=1, source_target_pairs={{0,3},{1,2},{2,1},{3,0},{4,7},{5,6},{6,5},{7,4},{8,11},{9,10},{10,... | collective-permute-start | bytes 368648 | tf_op jit(solution)/shard_map/ppermute | solution.py:27
  62.8 1.7 %collective-permute-start.13 = (bf16[2,800,128]{2,1,0:T(8,128)(2,1)S(1)}, bf16[2,800,128]{2,1,0:T(8,128)(2,1)S(1)}, u32[]{:S(2)}, u32[]{:S(2)}) collective-permute-start(bf16[2,800,128]{2,1,0:T(8,128)(2,1)S(1)} %collective-permute-done.10.refs_6_), channel_id=1, source_target_pairs={{0,4},{4,0},{8,12},{12,8},{1,5},{5,1},{9,13},{13,9},{2,6},{6,2},{1... | collective-permute-start | bytes 1228808 | tf_op jit(solution)/shard_map/ppermute | solution.py:27
  62.8 2.3 %collective-permute-start.14 = (bf16[2,800,128]{2,1,0:T(8,128)(2,1)S(1)}, bf16[2,800,128]{2,1,0:T(8,128)(2,1)S(1)}, u32[]{:S(2)}, u32[]{:S(2)}) collective-permute-start(bf16[2,800,128]{2,1,0:T(8,128)(2,1)S(1)} %collective-permute-done.11.refs_7_), channel_id=1, source_target_pairs={{0,4},{4,0},{8,12},{12,8},{1,5},{5,1},{9,13},{13,9},{2,6},{6,2},{1... | collective-permute-start | bytes 1228808 | tf_op jit(solution)/shard_map/ppermute | solution.py:27
  65.1 10.8 %copy-start.4 = (s32[192]{0:T(256)S(1)}, s32[192]{0:T(256)}, u32[]{:S(2)}) copy-start(s32[192]{0:T(256)} %param.9) | copy-start | bytes 2308
  67.1 8.9 %collective-permute-start.16 = (bf16[96,1280]{1,0:T(8,128)(2,1)S(1)}, bf16[96,1280]{1,0:T(8,128)(2,1)S(1)}, u32[]{:S(2)}, u32[]{:S(2)}) collective-permute-start(bf16[96,1280]{1,0:T(8,128)(2,1)S(1)} %get-tuple-element.68.refs_4_), channel_id=1, source_target_pairs={{0,8},{4,12},{8,0},{12,4},{1,9},{5,13},{9,1},{13,5},{2,10},{6,14},... | collective-permute-start | bytes 737288 | tf_op jit(solution)/shard_map/ppermute | solution.py:27
  68.7 13.0 %collective-permute-start.15 = (bf16[96,1280]{1,0:T(8,128)(2,1)S(1)}, bf16[96,1280]{1,0:T(8,128)(2,1)S(1)}, u32[]{:S(2)}, u32[]{:S(2)}) collective-permute-start(bf16[96,1280]{1,0:T(8,128)(2,1)S(1)} %get-tuple-element.66.refs_5_), channel_id=1, source_target_pairs={{0,8},{4,12},{8,0},{12,4},{1,9},{5,13},{9,1},{13,5},{2,10},{6,14},... | collective-permute-start | bytes 737288 | tf_op jit(solution)/shard_map/ppermute | solution.py:27
  76.0 5.7 %collective-permute-start.17 = (bf16[96,1280]{1,0:T(8,128)(2,1)S(1)}, bf16[96,1280]{1,0:T(8,128)(2,1)S(1)}, u32[]{:S(2)}, u32[]{:S(2)}) collective-permute-start(bf16[96,1280]{1,0:T(8,128)(2,1)S(1)} %collective-permute-done.16.refs_8_), channel_id=1, source_target_pairs={{0,4},{4,0},{8,12},{12,8},{1,5},{5,1},{9,13},{13,9},{2,6},{6,2},{1... | collective-permute-start | bytes 737288 | tf_op jit(solution)/shard_map/ppermute | solution.py:27
  76.0 4.5 %collective-permute-start.18 = (s32[1,192]{1,0:T(1,128)S(1)}, s32[1,192]{1,0:T(1,128)S(1)}, u32[]{:S(2)}, u32[]{:S(2)}) collective-permute-start(s32[1,192]{1,0:T(1,128)S(1)} %bitcast.15), channel_id=1, source_target_pairs={{0,8},{4,12},{8,0},{12,4},{1,9},{5,13},{9,1},{13,5},{2,10},{6,14},... | collective-permute-start | bytes 2312 | tf_op jit(solution)/shard_map/ppermute | solution.py:27
  80.5 1.2 %collective-permute-start.19 = (s32[2,1,192]{2,1,0:T(1,128)S(1)}, s32[2,1,192]{2,1,0:T(1,128)S(1)}, u32[]{:S(2)}, u32[]{:S(2)}) collective-permute-start(s32[2,1,192]{2,1,0:T(1,128)S(1)} %pad_add_fusion), channel_id=1, source_target_pairs={{0,4},{4,0},{8,12},{12,8},{1,5},{5,1},{9,13},{13,9},{2,6},{6,2},{1... | collective-permute-start | bytes 4616 | tf_op jit(solution)/shard_map/ppermute | solution.py:27
  80.5 2.0 %collective-permute-start.21 = (bf16[96,1280]{1,0:T(8,128)(2,1)S(1)}, bf16[96,1280]{1,0:T(8,128)(2,1)S(1)}, u32[]{:S(2)}, u32[]{:S(2)}) collective-permute-start(bf16[96,1280]{1,0:T(8,128)(2,1)S(1)} %get-tuple-element.66.refs_5_), channel_id=1, source_target_pairs={{0,4},{4,0},{8,12},{12,8},{1,5},{5,1},{9,13},{13,9},{2,6},{6,2},{1... | collective-permute-start | bytes 737288 | tf_op jit(solution)/shard_map/ppermute | solution.py:27
  81.0 1.5 %collective-permute-start.20 = (bf16[96,1280]{1,0:T(8,128)(2,1)S(1)}, bf16[96,1280]{1,0:T(8,128)(2,1)S(1)}, u32[]{:S(2)}, u32[]{:S(2)}) collective-permute-start(bf16[96,1280]{1,0:T(8,128)(2,1)S(1)} %get-tuple-element.68.refs_4_), channel_id=1, source_target_pairs={{0,4},{4,0},{8,12},{12,8},{1,5},{5,1},{9,13},{13,9},{2,6},{6,2},{1... | collective-permute-start | bytes 737288 | tf_op jit(solution)/shard_map/ppermute | solution.py:27
  81.7 1.5 %collective-permute-start.22 = (bf16[96,1280]{1,0:T(8,128)(2,1)S(1)}, bf16[96,1280]{1,0:T(8,128)(2,1)S(1)}, u32[]{:S(2)}, u32[]{:S(2)}) collective-permute-start(bf16[96,1280]{1,0:T(8,128)(2,1)S(1)} %collective-permute-done.15.refs_9_), channel_id=1, source_target_pairs={{0,4},{4,0},{8,12},{12,8},{1,5},{5,1},{9,13},{13,9},{2,6},{6,2},{1... | collective-permute-start | bytes 737288 | tf_op jit(solution)/shard_map/ppermute | solution.py:27

commit v10 on v9

--- a/solution.py
+++ b/solution.py
@@ -23,6 +23,10 @@
     return pltpu.CompilerParams(vmem_limit_bytes=mib * 1024 * 1024)
 
 
+def cost(us):
+    return pl.CostEstimate(flops=0, bytes_accessed=int(us * 3.3e6), transcendentals=0)
+
+
 def swap(x, axis, size, bit):
     return lax.ppermute(x, axis, [(i, i ^ bit) for i in range(size)])
 
@@ -91,12 +95,10 @@
         ref[...] = all_ref[j]
 
 
-def pack_proj_kernel(proj_ref, all_ref, low_ref, high_ref):
-    half = low_ref.shape[0]
-    for t in range(2 * half):
-        all_ref[t] = pack(proj_ref[t])
-    low_ref[...] = all_ref[:half]
-    high_ref[...] = all_ref[half:]
+def pack_proj_kernel(own_ref, next_ref, far_ref, all_ref, far_out_ref):
+    for i, ref in enumerate((own_ref, next_ref, far_ref)):
+        all_ref[i] = pack(ref[...])
+    far_out_ref[...] = all_ref[2]
 
 
 def norm_kernel(index_ref, patches_ref, gain_ref, hidden_ref, own_ref):
@@ -203,12 +205,15 @@
 
 
 def project_kernel(n_ctx, width, col, index_ref, *refs):
-    *blocks, own_ref, gain_ref = refs[4 : -HALVES - 2]
-    *out_refs, part_ref, mix_ref = refs[-HALVES - 2 :]
+    *blocks, own_ref, gain_ref = refs[4 : -HALVES - 1]
+    *out_refs, part_ref = refs[-HALVES - 1 :]
     rows = own_ref.shape[0]
-    for s in range(4):
-        mix_ref[index_ref[1] ^ s] = refs[s][...]
-    mixes = [unpack(mix_ref[t], rows, width) for t in range(4)]
+    mixes = [unpack(m[...], rows, width) for m in refs[:4]]
+    flip = index_ref[2] > 0
+    mixes[2:] = [
+        [jnp.where(flip, b, a) for a, b in zip(mixes[2], mixes[3])],
+        [jnp.where(flip, a, b) for a, b in zip(mixes[2], mixes[3])],
+    ]
     me = index_ref[0]
     main = 2 * LANES
     mixed = jnp.concatenate([m for m, _ in mixes] + [r for _, r in mixes], axis=1)
@@ -216,8 +221,8 @@
     rests = []
     for key in range(n_ctx):
         pieces = []
-        for ref in [blocks.pop(0) for _ in range(1 if key < 2 else 2)]:
-            pieces += [ref[i] for i in range(ref.shape[0])]
+        for ref in [blocks.pop(0) for _ in range(2)]:
+            pieces += [ref[...]] if len(ref.shape) == 2 else [ref[i] for i in range(ref.shape[0])]
         halves = [unpack(p, width, col) for p in pieces]
         both = []
         for half in ([h[0] for h in halves], [h[1] for h in halves]):
@@ -285,12 +290,28 @@
         compiler_params=params(8),
         name="pack",
     )(jnp.transpose(w_qkv, (1, 0, 2)))
-    proj = lax.all_gather(w_proj, "tensor")
     query = gather_cross(thirds[0], n_ctx)
     key = gather_cross(thirds[1], n_ctx)
     value = gather_cross(thirds[2], n_ctx)
-    query, patches = together(query, patches)
-    query_twin = {k: over_core(query[k]) for k in cross}
+    by_one = swap(w_proj, "tensor", n_ten, 1)
+    far = lax.ppermute(
+        w_proj,
+        ("dp", "tensor"),
+        [
+            (d * n_ten + t, d * n_ten + (t ^ (2 + d % 2)))
+            for d in range(n_dp)
+            for t in range(n_ten)
+        ],
+    )
+    near, far = pl.pallas_call(
+        pack_proj_kernel,
+        out_shape=(shape(3, *piece), shape(*piece)),
+        in_specs=[VMEM] * 3,
+        out_specs=(VMEM, VMEM),
+        compiler_params=params(8),
+        cost_estimate=cost(5),
+        name="pack_proj",
+    )(w_proj, by_one, far)
     hidden, own_patches = pl.pallas_call(
         norm_kernel,
         out_shape=(shape(rows, feat), shape(groups, feat)),
@@ -299,9 +320,12 @@
         compiler_params=params(16),
         name="norm",
     )(index, patches, gain_attn)
-    key, hidden = together(key, hidden)
     twin = over_core(own)
+    query, key, hidden, near, far = together(query, key, hidden, near, far)
+
+    query_twin = {k: over_core(query[k]) for k in cross}
     key_twin = {k: over_core(key[k]) for k in cross}
+    far2 = over_dp(far)
 
     shard_list = [own, twin]
     for k in cross:
@@ -315,18 +339,13 @@
         compiler_params=params(20),
         name="scores",
     )(index, hidden, valid.reshape(rows // PAIR, PAIR), *shard_list)
-    exps, value, proj = together(exps, value, proj)
+    exps, value = together(exps, value)
     value_twin = {k: over_core(value[k]) for k in cross}
-    proj, proj_low, proj_high = pl.pallas_call(
-        pack_proj_kernel,
-        out_shape=(shape(n_ten, *piece), shape(n_ten // 2, *piece), shape(n_ten // 2, *piece)),
-        in_specs=[VMEM],
-        out_specs=(VMEM,) * 3,
-        compiler_params=params(12),
-        name="pack_proj",
-    )(proj)
-    low = gather_cross(proj_low, n_ctx)
-    high = gather_cross(proj_high, n_ctx)
+    near, far2 = together(near, far2, exps)[:2]
+    low = gather_cross(near, n_ctx)
+    high = gather_cross(far2, n_ctx)
+    near_twin = over_core(near)
+    far2_twin = over_core(far2)
     value_list = []
     for k in cross:
         value_list += [value[k], value_twin[k]]
@@ -346,9 +365,8 @@
 
     received = {s: swap(mixed[s], "tensor", n_ten, s) for s in (2, 3, 1)}
     mixed = [mixed[0]] + [received[s] for s in range(1, n_ten)]
-    proj_twin = over_core(proj)
+    blocks = [near, far2, near_twin, far2_twin]
     mixed, low, high = together(mixed, low, high)
-    blocks = [proj, proj_twin]
     for k in cross:
         blocks += [low[k], high[k], over_core(low[k]), over_core(high[k])]
     done = pl.pallas_call(
@@ -356,10 +374,7 @@
         out_shape=(shape(groups // HALVES, feat),) * HALVES,
         in_specs=[SMEM] + [VMEM] * (n_ten + len(blocks) + 2),
         out_specs=(VMEM,) * HALVES,
-        scratch_shapes=[
-            pltpu.VMEM((n_ctx, groups, col), F32),
-            pltpu.VMEM((n_ten, *packed_shape(groups, width)), BF16),
-        ],
+        scratch_shapes=[pltpu.VMEM((n_ctx, groups, col), F32)],
         compiler_params=params(24),
         name="project",
     )(index, *mixed, *blocks, own_patches, gain_merge)

time: 85.3 us -> 70.7 us (0.83)
  blocking collectives: 22.4 us -> 0 us
  starting transfers between devices: 17.2 us -> 22.2 us
  waiting for transfers between devices: 28.3 us -> 31.2 us
    all_gather x1 -> x0, blocking collectives: 22.4 us -> none  [local(): proj = lax.all_gather(w_proj, 'tensor')]
    ppermute x0 -> x1, starting transfers between devices: none -> 2.59 us  [local(): lax.ppermute(w_proj, ('dp', 'tensor'), [(d * n_ten + t, d * n_ten + (t ^...]
    ppermute x0 -> x1, waiting for transfers between devices: none -> 2.57 us  [local(): lax.ppermute(w_proj, ('dp', 'tensor'), [(d * n_ten + t, d * n_ten + (t ^...]
    ppermute x23 -> x26, starting transfers between devices: 17.2 us -> 19.7 us  [swap(): return lax.ppermute(x, axis, [(i, i ^ bit) for i in range(size)])]
    ppermute x23 -> x26, waiting for transfers between devices: 28.3 us -> 28.6 us  [swap(): return lax.ppermute(x, axis, [(i, i ^ bit) for i in range(size)])]
  transfers between devices with their start and end apart: 23 -> 27, of which waited for: 11 -> 12; matrix products, arithmetic and copies ran while one was open for 0% -> 0% of each run, Pallas kernels for 11% -> 13%
where the time goes in v10:
time: 70.7 us; the launch traced here: 70.4 us
  waiting for transfers between devices  31.2 us (44%)
  starting transfers between devices  22.2 us (31%)
  Pallas kernels  13.5 us (19%)
  local copies, waits for them, and re-layouts  3.38 us (5%)
    ppermute x26, waiting for transfers between devices, swap(): return lax.ppermute(x, axis, [(i, i ^ bit) for i in range(size)])  28.6 us
    ppermute x26, starting transfers between devices, swap(): return lax.ppermute(x, axis, [(i, i ^ bit) for i in range(size)])  19.7 us
    pallas_call x1, Pallas kernels, local(): pl.pallas_call(functools.partial(score_kernel, n_ctx, width), out_shape=s...  3.91 us
    pallas_call x1, Pallas kernels, local(): pl.pallas_call(functools.partial(mix_kernel, n_ctx, width), out_shape=(sh...  3.85 us
    unnamed x14, local copies, waits for them, and re-layouts  3.38 us
    ppermute x1, starting transfers between devices, local(): lax.ppermute(w_proj, ('dp', 'tensor'), [(d * n_ten + t, d * n_ten + (t ^...  2.59 us
    ppermute x1, waiting for transfers between devices, local(): lax.ppermute(w_proj, ('dp', 'tensor'), [(d * n_ten + t, d * n_ten + (t ^...  2.57 us
    pallas_call x1, Pallas kernels, local(): pl.pallas_call(functools.partial(project_kernel, n_ctx, width, col), out_...  1.94 us
  transfers between devices with their start and end apart: 27, of which 12 were waited for; matrix products, arithmetic and copies ran while one was open for 0% of the time, Pallas kernels for 13%

profile of v10, /device:TPU:0, one launch (start us, length us, event | category | flops | bytes accessed | tf_op | source)
XLA Modules:
  0.0 70.4 jit_solution(2419912382500367862)
XLA Ops:
  0.0 1.1 %copy-done.1 = bf16[320,3,320]{2,0,1:T(8,128)(2,1)S(1)} copy-done((bf16[320,3,320]{2,0,1:T(8,128)(2,1)S(1)}, bf16[320,3,320]{2,0,1:T(8,128)(2,1)}, u32[]{:S(2)}) %copy-start.1) | copy-done | bytes 614424
  1.3 0.5 collective-permute-start.4
  1.8 2.6 %collective-permute-start.2 = (bf16[320,320]{1,0:T(8,128)(2,1)}, bf16[320,320]{1,0:T(8,128)(2,1)S(1)}, u32[]{:S(2)}, u32[]{:S(2)}) collective-permute-start(bf16[320,320]{1,0:T(8,128)(2,1)} %own_ref.1), channel_id=1, source_target_pairs={{0,1},{1,0},{2,3},{3,2},{4,5},{5,4},{6,7},{7,6},{8,9},{9,8},{10,11... | collective-permute-start | bytes 614408 | tf_op jit(solution)/shard_map/ppermute | solution.py:31
  4.5 2.6 %collective-permute-start.3 = (bf16[320,320]{1,0:T(8,128)(2,1)}, bf16[320,320]{1,0:T(8,128)(2,1)S(1)}, u32[]{:S(2)}, u32[]{:S(2)}) collective-permute-start(bf16[320,320]{1,0:T(8,128)(2,1)} %own_ref.1), channel_id=1, source_target_pairs={{0,2},{1,3},{2,0},{3,1},{16,19},{17,18},{18,17},{19,16},{4,6},{5,7... | collective-permute-start | bytes 614408 | tf_op jit(solution)/shard_map/ppermute | solution.py:297
  7.0 1.5 %collective-permute-start = (bf16[800,128]{1,0:T(8,128)(2,1)S(1)}, bf16[800,128]{1,0:T(8,128)(2,1)S(1)}, u32[]{:S(2)}, u32[]{:S(2)}) collective-permute-start(bf16[800,128]{1,0:T(8,128)(2,1)S(1)} %get-tuple-element.39), channel_id=1, source_target_pairs={{0,8},{4,12},{8,0},{12,4},{1,9},{5,13},{9,1},{13,5},{2,10},{6,14},... | collective-permute-start | bytes 614408 | tf_op jit(solution)/shard_map/ppermute | solution.py:31
  8.6 0.5 collective-permute-start.1
  9.2 1.5 %copy-done = bf16[768,1280]{1,0:T(8,128)(2,1)S(1)} copy-done((bf16[768,1280]{1,0:T(8,128)(2,1)S(1)}, bf16[768,1280]{1,0:T(8,128)(2,1)}, u32[]{:S(2)}) %copy-start) | copy-done | bytes 1966104
  10.7 0.7 copy-done.3
  11.4 1.6 %norm.1 = (bf16[768,1280]{1,0:T(8,128)(2,1)S(1)}, bf16[192,1280]{1,0:T(8,128)(2,1)S(1)}) custom-call(s32[3]{0:T(128)S(1)} %pad_add_fusion.1.index_ref, bf16[768,1280]{1,0:T(8,128)(2,1)S(1)} %copy-done, f32[1280]{0:T(1024)S(1)} %copy-done.3), custom_call_target="tpu_custom_call" | custom-call | tf_op jit(solution)/shard_map/norm/pallas_call | solution.py:315
  13.0 3.4 %collective-permute-done.2.next_ref = bf16[320,320]{1,0:T(8,128)(2,1)S(1)} collective-permute-done((bf16[320,320]{1,0:T(8,128)(2,1)}, bf16[320,320]{1,0:T(8,128)(2,1)S(1)}, u32[]{:S(2)}, u32[]{:S(2)}) %collective-permute-start.2) | collective-permute-done | bytes 204832 | tf_op jit(solution)/shard_map/ppermute | solution.py:31
  16.4 2.6 %collective-permute-done.3.far_ref = bf16[320,320]{1,0:T(8,128)(2,1)S(1)} collective-permute-done((bf16[320,320]{1,0:T(8,128)(2,1)}, bf16[320,320]{1,0:T(8,128)(2,1)S(1)}, u32[]{:S(2)}, u32[]{:S(2)}) %collective-permute-start.3) | collective-permute-done | bytes 204832 | tf_op jit(solution)/shard_map/ppermute | solution.py:297
  19.6 1.5 %collective-permute-start.7 = (bf16[800,128]{1,0:T(8,128)(2,1)S(1)}, bf16[800,128]{1,0:T(8,128)(2,1)S(1)}, u32[]{:S(2)}, u32[]{:S(2)}) collective-permute-start(bf16[800,128]{1,0:T(8,128)(2,1)S(1)} %get-tuple-element.48), channel_id=1, source_target_pairs={{0,8},{4,12},{8,0},{12,4},{1,9},{5,13},{9,1},{13,5},{2,10},{6,14},... | collective-permute-start | bytes 614408 | tf_op jit(solution)/shard_map/ppermute | solution.py:31
  21.2 1.4 %collective-permute-start.12 = (bf16[800,128]{1,0:T(8,128)(2,1)S(1)}, bf16[800,128]{1,0:T(8,128)(2,1)S(1)}, u32[]{:S(2)}, u32[]{:S(2)}) collective-permute-start(bf16[800,128]{1,0:T(8,128)(2,1)S(1)} %get-tuple-element.56), channel_id=1, source_target_pairs={{0,16},{16,0},{1,17},{17,1},{2,18},{18,2},{3,19},{19,3},{4,20},{20... | collective-permute-start | bytes 614408 | tf_op jit(solution)/shard_map/ppermute | solution.py:31
  22.5 3.9 %scores.1.exps_ref = bf16[768,512]{1,0:T(8,128)(2,1)S(1)} custom-call(s32[3]{0:T(128)S(1)} %pad_add_fusion.1.index_ref, bf16[768,1280]{1,0:T(8,128)(2,1)S(1)} %get-tuple-element.44.hidden_ref, s32[6,128]{1,0:T(8,128)S(1)} %bitcast.17, bf16[3,800,128]{2,1,0:T(8,128)(2,1)S(1)} %get-tuple-element.45.refs_0_, ...), custom_call_target="tpu_custom_call" | custom-call | tf_op jit(solution)/shard_map/scores/pallas_call | solution.py:333
  26.7 1.2 %collective-permute-done.12.refs_5_ = bf16[800,128]{1,0:T(8,128)(2,1)S(1)} collective-permute-done((bf16[800,128]{1,0:T(8,128)(2,1)S(1)}, bf16[800,128]{1,0:T(8,128)(2,1)S(1)}, u32[]{:S(2)}, u32[]{:S(2)}) %collective-permute-start.12) | collective-permute-done | bytes 204832 | tf_op jit(solution)/shard_map/ppermute | solution.py:31
  28.5 1.5 %collective-permute-start.14 = (bf16[800,128]{1,0:T(8,128)(2,1)S(1)}, bf16[800,128]{1,0:T(8,128)(2,1)S(1)}, u32[]{:S(2)}, u32[]{:S(2)}) collective-permute-start(bf16[800,128]{1,0:T(8,128)(2,1)S(1)} %collective-permute-done.12.refs_5_), channel_id=1, source_target_pairs={{0,8},{4,12},{8,0},{12,4},{1,9},{5,13},{9,1},{13,5},{2,10},{6,14},... | collective-permute-start | bytes 614408 | tf_op jit(solution)/shard_map/ppermute | solution.py:31
  30.0 3.9 %mix.1 = (bf16[480,128]{1,0:T(8,128)(2,1)S(1)}, bf16[480,128]{1,0:T(8,128)(2,1)S(1)}, bf16[480,128]{1,0:T(8,128)(2,1)S(1)}, bf16[480,128]{1,0:T(8,128)(2,1)S(1)}) custom-call(s32[3]{0:T(128)S(1)} %pad_add_fusion.1.index_ref, bf16[768,1280]{1,0:T(8,128)(2,1)S(1)} %get-tuple-element.44.hidden_ref, bf16[768,512]{1,0:T(8,128)(2,1)S(1)} %scores.1.exps_ref, ...), custom_call_target="tpu_custom_call" | custom-call | tf_op jit(solution)/shard_map/mix/pallas_call | solution.py:352
  34.3 2.6 %collective-permute-start.10 = (bf16[480,128]{1,0:T(8,128)(2,1)S(1)}, bf16[480,128]{1,0:T(8,128)(2,1)S(1)}, u32[]{:S(2)}, u32[]{:S(2)}) collective-permute-start(bf16[480,128]{1,0:T(8,128)(2,1)S(1)} %get-tuple-element.53), channel_id=1, source_target_pairs={{0,2},{1,3},{2,0},{3,1},{4,6},{5,7},{6,4},{7,5},{8,10},{9,11},{10,... | collective-permute-start | bytes 368648 | tf_op jit(solution)/shard_map/ppermute | solution.py:31
  36.9 1.4 %collective-permute-start.11 = (bf16[480,128]{1,0:T(8,128)(2,1)S(1)}, bf16[480,128]{1,0:T(8,128)(2,1)S(1)}, u32[]{:S(2)}, u32[]{:S(2)}) collective-permute-start(bf16[480,128]{1,0:T(8,128)(2,1)S(1)} %get-tuple-element.54), channel_id=1, source_target_pairs={{0,3},{1,2},{2,1},{3,0},{4,7},{5,6},{6,5},{7,4},{8,11},{9,10},{10,... | collective-permute-start | bytes 368648 | tf_op jit(solution)/shard_map/ppermute | solution.py:31
  38.3 8.7 %collective-permute-done.14.refs_9_ = bf16[800,128]{1,0:T(8,128)(2,1)S(1)} collective-permute-done((bf16[800,128]{1,0:T(8,128)(2,1)S(1)}, bf16[800,128]{1,0:T(8,128)(2,1)S(1)}, u32[]{:S(2)}, u32[]{:S(2)}) %collective-permute-start.14) | collective-permute-done | bytes 204832 | tf_op jit(solution)/shard_map/ppermute | solution.py:31
  47.0 0.6 collective-permute-start.17
  48.1 2.1 %collective-permute-done.16.refs_7_ = bf16[800,128]{1,0:T(8,128)(2,1)S(1)} collective-permute-done((bf16[800,128]{1,0:T(8,128)(2,1)S(1)}, bf16[800,128]{1,0:T(8,128)(2,1)S(1)}, u32[]{:S(2)}, u32[]{:S(2)}) %collective-permute-start.16) | collective-permute-done | bytes 204832 | tf_op jit(solution)/shard_map/ppermute | solution.py:31
  50.5 1.9 %project.1 = (bf16[96,1280]{1,0:T(8,128)(2,1)S(1)}, bf16[96,1280]{1,0:T(8,128)(2,1)S(1)}) custom-call(s32[3]{0:T(128)S(1)} %pad_add_fusion.1.index_ref, bf16[480,128]{1,0:T(8,128)(2,1)S(1)} %get-tuple-element.59.refs_0_, bf16[480,128]{1,0:T(8,128)(2,1)S(1)} %collective-permute-done.9.refs_1_, bf16[480,128]{1,0:T(8,128)(2,1)S(1)} %collective-permute-done.10.refs_2_, ...), custom_call_target="tpu_custom_call" | custom-call | tf_op jit(solution)/shard_map/project/pallas_call | solution.py:372
  52.5 0.7 collective-permute-start.20
  53.1 1.4 %collective-permute-start.19 = (bf16[96,1280]{1,0:T(8,128)(2,1)S(1)}, bf16[96,1280]{1,0:T(8,128)(2,1)S(1)}, u32[]{:S(2)}, u32[]{:S(2)}) collective-permute-start(bf16[96,1280]{1,0:T(8,128)(2,1)S(1)} %get-tuple-element.68.refs_5_), channel_id=1, source_target_pairs={{0,8},{4,12},{8,0},{12,4},{1,9},{5,13},{9,1},{13,5},{2,10},{6,14},... | collective-permute-start | bytes 737288 | tf_op jit(solution)/shard_map/ppermute | solution.py:31
  54.6 6.8 %collective-permute-done.20.refs_8_ = bf16[96,1280]{1,0:T(8,128)(2,1)S(1)} collective-permute-done((bf16[96,1280]{1,0:T(8,128)(2,1)S(1)}, bf16[96,1280]{1,0:T(8,128)(2,1)S(1)}, u32[]{:S(2)}, u32[]{:S(2)}) %collective-permute-start.20) | collective-permute-done | bytes 245792 | tf_op jit(solution)/shard_map/ppermute | solution.py:31
  61.3 0.6 collective-permute-start.22
  61.9 3.9 %collective-permute-done.22.refs_2_ = s32[1,192]{1,0:T(1,128)S(1)} collective-permute-done((s32[1,192]{1,0:T(1,128)S(1)}, s32[1,192]{1,0:T(1,128)S(1)}, u32[]{:S(2)}, u32[]{:S(2)}) %collective-permute-start.22) | collective-permute-done | bytes 800 | tf_op jit(solution)/shard_map/ppermute | solution.py:31
  66.4 0.6 collective-permute-done.23
  67.2 0.7 collective-permute-done.24.refs_6_
  67.9 0.7 collective-permute-done.26.refs_11_
  68.5 1.9 %placement.1 = bf16[192,1280]{1,0:T(8,128)(2,1)} custom-call(s32[3]{0:T(128)S(1)} %pad_add_fusion.1.index_ref, s32[1,192]{1,0:T(1,128)S(1)} %bitcast.15, s32[1,192]{1,0:T(1,128)S(1)} %get-tuple-element.74.refs_1_, s32[1,192]{1,0:T(1,128)S(1)} %collective-permute-done.22.refs_2_, s32[1,192]{1,0:T(1,128)S(1)} %get-tuple-element.73.refs_3_, ...), custom_call_target="tpu_custom_call" | custom-call | tf_op jit(solution)/shard_map/placement/pallas_call | solution.py:400
  (46 shorter events, 3.8 us)
Async XLA Ops:
  1.1 17.8 %copy-start.2 = (bf16[320,320]{1,0:T(8,128)(2,1)S(1)}, bf16[320,320]{1,0:T(8,128)(2,1)}, u32[]{:S(2)}) copy-start(bf16[320,320]{1,0:T(8,128)(2,1)} %own_ref.1) | copy-start | bytes 614404
  1.1 21.4 %copy-start.6 = (s32[768]{0:T(1024)S(1)}, s32[768]{0:T(1024)}, u32[]{:S(2)}) copy-start(s32[768]{0:T(1024)} %param.8) | copy-start | bytes 9220
  1.3 21.2 %collective-permute-start.4 = (bf16[3,800,128]{2,1,0:T(8,128)(2,1)S(1)}, bf16[3,800,128]{2,1,0:T(8,128)(2,1)S(1)}, u32[]{:S(2)}, u32[]{:S(2)}) collective-permute-start(bf16[3,800,128]{2,1,0:T(8,128)(2,1)S(1)} %get-tuple-element.45.refs_0_), channel_id=1, source_target_pairs={{0,4},{4,0},{8,12},{12,8},{1,5},{5,1},{9,13},{13,9},{2,6},{6,2},{1... | collective-permute-start | bytes 1843208 | tf_op jit(solution)/shard_map/ppermute | solution.py:31
  1.8 14.5 %collective-permute-start.2 = (bf16[320,320]{1,0:T(8,128)(2,1)}, bf16[320,320]{1,0:T(8,128)(2,1)S(1)}, u32[]{:S(2)}, u32[]{:S(2)}) collective-permute-start(bf16[320,320]{1,0:T(8,128)(2,1)} %own_ref.1), channel_id=1, source_target_pairs={{0,1},{1,0},{2,3},{3,2},{4,5},{5,4},{6,7},{7,6},{8,9},{9,8},{10,11... | collective-permute-start | bytes 614408 | tf_op jit(solution)/shard_map/ppermute | solution.py:31
  4.5 14.5 %collective-permute-start.3 = (bf16[320,320]{1,0:T(8,128)(2,1)}, bf16[320,320]{1,0:T(8,128)(2,1)S(1)}, u32[]{:S(2)}, u32[]{:S(2)}) collective-permute-start(bf16[320,320]{1,0:T(8,128)(2,1)} %own_ref.1), channel_id=1, source_target_pairs={{0,2},{1,3},{2,0},{3,1},{16,19},{17,18},{18,17},{19,16},{4,6},{5,7... | collective-permute-start | bytes 614408 | tf_op jit(solution)/shard_map/ppermute | solution.py:297
  7.0 12.0 %collective-permute-start = (bf16[800,128]{1,0:T(8,128)(2,1)S(1)}, bf16[800,128]{1,0:T(8,128)(2,1)S(1)}, u32[]{:S(2)}, u32[]{:S(2)}) collective-permute-start(bf16[800,128]{1,0:T(8,128)(2,1)S(1)} %get-tuple-element.39), channel_id=1, source_target_pairs={{0,8},{4,12},{8,0},{12,4},{1,9},{5,13},{9,1},{13,5},{2,10},{6,14},... | collective-permute-start | bytes 614408 | tf_op jit(solution)/shard_map/ppermute | solution.py:31
  8.6 10.5 %collective-permute-start.1 = (bf16[800,128]{1,0:T(8,128)(2,1)S(1)}, bf16[800,128]{1,0:T(8,128)(2,1)S(1)}, u32[]{:S(2)}, u32[]{:S(2)}) collective-permute-start(bf16[800,128]{1,0:T(8,128)(2,1)S(1)} %get-tuple-element.40), channel_id=1, source_target_pairs={{0,8},{4,12},{8,0},{12,4},{1,9},{5,13},{9,1},{13,5},{2,10},{6,14},... | collective-permute-start | bytes 614408 | tf_op jit(solution)/shard_map/ppermute | solution.py:31
  9.1 1.5 %copy-start = (bf16[768,1280]{1,0:T(8,128)(2,1)S(1)}, bf16[768,1280]{1,0:T(8,128)(2,1)}, u32[]{:S(2)}) copy-start(bf16[768,1280]{1,0:T(8,128)(2,1)} %patches_ref.1) | copy-start | bytes 5898244
  19.1 3.5 %collective-permute-start.5 = (bf16[800,128]{1,0:T(8,128)(2,1)S(1)}, bf16[800,128]{1,0:T(8,128)(2,1)S(1)}, u32[]{:S(2)}, u32[]{:S(2)}) collective-permute-start(bf16[800,128]{1,0:T(8,128)(2,1)S(1)} %collective-permute-done.refs_2_), channel_id=1, source_target_pairs={{0,4},{4,0},{8,12},{12,8},{1,5},{5,1},{9,13},{13,9},{2,6},{6,2},{1... | collective-permute-start | bytes 614408 | tf_op jit(solution)/shard_map/ppermute | solution.py:31
  19.1 3.4 %collective-permute-start.6 = (bf16[800,128]{1,0:T(8,128)(2,1)S(1)}, bf16[800,128]{1,0:T(8,128)(2,1)S(1)}, u32[]{:S(2)}, u32[]{:S(2)}) collective-permute-start(bf16[800,128]{1,0:T(8,128)(2,1)S(1)} %collective-permute-done.1.refs_3_), channel_id=1, source_target_pairs={{0,4},{4,0},{8,12},{12,8},{1,5},{5,1},{9,13},{13,9},{2,6},{6,2},{1... | collective-permute-start | bytes 614408 | tf_op jit(solution)/shard_map/ppermute | solution.py:31
  19.6 7.1 %collective-permute-start.7 = (bf16[800,128]{1,0:T(8,128)(2,1)S(1)}, bf16[800,128]{1,0:T(8,128)(2,1)S(1)}, u32[]{:S(2)}, u32[]{:S(2)}) collective-permute-start(bf16[800,128]{1,0:T(8,128)(2,1)S(1)} %get-tuple-element.48), channel_id=1, source_target_pairs={{0,8},{4,12},{8,0},{12,4},{1,9},{5,13},{9,1},{13,5},{2,10},{6,14},... | collective-permute-start | bytes 614408 | tf_op jit(solution)/shard_map/ppermute | solution.py:31
  21.2 6.8 %collective-permute-start.12 = (bf16[800,128]{1,0:T(8,128)(2,1)S(1)}, bf16[800,128]{1,0:T(8,128)(2,1)S(1)}, u32[]{:S(2)}, u32[]{:S(2)}) collective-permute-start(bf16[800,128]{1,0:T(8,128)(2,1)S(1)} %get-tuple-element.56), channel_id=1, source_target_pairs={{0,16},{16,0},{1,17},{17,1},{2,18},{18,2},{3,19},{19,3},{4,20},{20... | collective-permute-start | bytes 614408 | tf_op jit(solution)/shard_map/ppermute | solution.py:31
  26.5 24.1 %copy-start.4 = (f32[1280]{0:T(1024)S(1)}, f32[1280]{0:T(1024)}, u32[]{:S(2)}) copy-start(f32[1280]{0:T(1024)} %refs_13_.1) | copy-start | bytes 15364
  27.9 19.1 %collective-permute-start.13 = (bf16[3,800,128]{2,1,0:T(8,128)(2,1)S(1)}, bf16[3,800,128]{2,1,0:T(8,128)(2,1)S(1)}, u32[]{:S(2)}, u32[]{:S(2)}) collective-permute-start(bf16[3,800,128]{2,1,0:T(8,128)(2,1)S(1)} %get-tuple-element.57.refs_4_), channel_id=1, source_target_pairs={{0,8},{4,12},{8,0},{12,4},{1,9},{5,13},{9,1},{13,5},{2,10},{6,14},... | collective-permute-start | bytes 1843208 | tf_op jit(solution)/shard_map/ppermute | solution.py:31
  28.4 1.5 %collective-permute-start.8 = (bf16[800,128]{1,0:T(8,128)(2,1)S(1)}, bf16[800,128]{1,0:T(8,128)(2,1)S(1)}, u32[]{:S(2)}, u32[]{:S(2)}) collective-permute-start(bf16[800,128]{1,0:T(8,128)(2,1)S(1)} %collective-permute-done.7.refs_2_), channel_id=1, source_target_pairs={{0,4},{4,0},{8,12},{12,8},{1,5},{5,1},{9,13},{13,9},{2,6},{6,2},{1... | collective-permute-start | bytes 614408 | tf_op jit(solution)/shard_map/ppermute | solution.py:31
  28.5 18.6 %collective-permute-start.14 = (bf16[800,128]{1,0:T(8,128)(2,1)S(1)}, bf16[800,128]{1,0:T(8,128)(2,1)S(1)}, u32[]{:S(2)}, u32[]{:S(2)}) collective-permute-start(bf16[800,128]{1,0:T(8,128)(2,1)S(1)} %collective-permute-done.12.refs_5_), channel_id=1, source_target_pairs={{0,8},{4,12},{8,0},{12,4},{1,9},{5,13},{9,1},{13,5},{2,10},{6,14},... | collective-permute-start | bytes 614408 | tf_op jit(solution)/shard_map/ppermute | solution.py:31
  33.8 13.2 %collective-permute-start.9 = (bf16[480,128]{1,0:T(8,128)(2,1)S(1)}, bf16[480,128]{1,0:T(8,128)(2,1)S(1)}, u32[]{:S(2)}, u32[]{:S(2)}) collective-permute-start(bf16[480,128]{1,0:T(8,128)(2,1)S(1)} %get-tuple-element.52), channel_id=1, source_target_pairs={{0,1},{1,0},{2,3},{3,2},{4,5},{5,4},{6,7},{7,6},{8,9},{9,8},{10,11... | collective-permute-start | bytes 368648 | tf_op jit(solution)/shard_map/ppermute | solution.py:31
  34.3 12.7 %collective-permute-start.10 = (bf16[480,128]{1,0:T(8,128)(2,1)S(1)}, bf16[480,128]{1,0:T(8,128)(2,1)S(1)}, u32[]{:S(2)}, u32[]{:S(2)}) collective-permute-start(bf16[480,128]{1,0:T(8,128)(2,1)S(1)} %get-tuple-element.53), channel_id=1, source_target_pairs={{0,2},{1,3},{2,0},{3,1},{4,6},{5,7},{6,4},{7,5},{8,10},{9,11},{10,... | collective-permute-start | bytes 368648 | tf_op jit(solution)/shard_map/ppermute | solution.py:31
  36.9 10.1 %collective-permute-start.11 = (bf16[480,128]{1,0:T(8,128)(2,1)S(1)}, bf16[480,128]{1,0:T(8,128)(2,1)S(1)}, u32[]{:S(2)}, u32[]{:S(2)}) collective-permute-start(bf16[480,128]{1,0:T(8,128)(2,1)S(1)} %get-tuple-element.54), channel_id=1, source_target_pairs={{0,3},{1,2},{2,1},{3,0},{4,7},{5,6},{6,5},{7,4},{8,11},{9,10},{10,... | collective-permute-start | bytes 368648 | tf_op jit(solution)/shard_map/ppermute | solution.py:31
  47.0 3.2 %collective-permute-start.15 = (bf16[3,800,128]{2,1,0:T(8,128)(2,1)S(1)}, bf16[3,800,128]{2,1,0:T(8,128)(2,1)S(1)}, u32[]{:S(2)}, u32[]{:S(2)}) collective-permute-start(bf16[3,800,128]{2,1,0:T(8,128)(2,1)S(1)} %get-tuple-element.57.refs_4_), channel_id=1, source_target_pairs={{0,4},{4,0},{8,12},{12,8},{1,5},{5,1},{9,13},{13,9},{2,6},{6,2},{1... | collective-permute-start | bytes 1843208 | tf_op jit(solution)/shard_map/ppermute | solution.py:31
  47.0 3.5 %collective-permute-start.17 = (bf16[3,800,128]{2,1,0:T(8,128)(2,1)S(1)}, bf16[3,800,128]{2,1,0:T(8,128)(2,1)S(1)}, u32[]{:S(2)}, u32[]{:S(2)}) collective-permute-start(bf16[3,800,128]{2,1,0:T(8,128)(2,1)S(1)} %collective-permute-done.13.refs_8_), channel_id=1, source_target_pairs={{0,4},{4,0},{8,12},{12,8},{1,5},{5,1},{9,13},{13,9},{2,6},{6,2},{1... | collective-permute-start | bytes 1843208 | tf_op jit(solution)/shard_map/ppermute | solution.py:31
  47.6 2.6 %collective-permute-start.16 = (bf16[800,128]{1,0:T(8,128)(2,1)S(1)}, bf16[800,128]{1,0:T(8,128)(2,1)S(1)}, u32[]{:S(2)}, u32[]{:S(2)}) collective-permute-start(bf16[800,128]{1,0:T(8,128)(2,1)S(1)} %collective-permute-done.12.refs_5_), channel_id=1, source_target_pairs={{0,4},{4,0},{8,12},{12,8},{1,5},{5,1},{9,13},{13,9},{2,6},{6,2},{1... | collective-permute-start | bytes 614408 | tf_op jit(solution)/shard_map/ppermute | solution.py:31
  47.7 2.8 %collective-permute-start.18 = (bf16[800,128]{1,0:T(8,128)(2,1)S(1)}, bf16[800,128]{1,0:T(8,128)(2,1)S(1)}, u32[]{:S(2)}, u32[]{:S(2)}) collective-permute-start(bf16[800,128]{1,0:T(8,128)(2,1)S(1)} %collective-permute-done.14.refs_9_), channel_id=1, source_target_pairs={{0,4},{4,0},{8,12},{12,8},{1,5},{5,1},{9,13},{13,9},{2,6},{6,2},{1... | collective-permute-start | bytes 614408 | tf_op jit(solution)/shard_map/ppermute | solution.py:31
  50.5 10.8 %copy-start.5 = (s32[192]{0:T(256)S(1)}, s32[192]{0:T(256)}, u32[]{:S(2)}) copy-start(s32[192]{0:T(256)} %param.9) | copy-start | bytes 2308
  52.5 8.9 %collective-permute-start.20 = (bf16[96,1280]{1,0:T(8,128)(2,1)S(1)}, bf16[96,1280]{1,0:T(8,128)(2,1)S(1)}, u32[]{:S(2)}, u32[]{:S(2)}) collective-permute-start(bf16[96,1280]{1,0:T(8,128)(2,1)S(1)} %get-tuple-element.70.refs_4_), channel_id=1, source_target_pairs={{0,8},{4,12},{8,0},{12,4},{1,9},{5,13},{9,1},{13,5},{2,10},{6,14},... | collective-permute-start | bytes 737288 | tf_op jit(solution)/shard_map/ppermute | solution.py:31
  53.1 13.9 %collective-permute-start.19 = (bf16[96,1280]{1,0:T(8,128)(2,1)S(1)}, bf16[96,1280]{1,0:T(8,128)(2,1)S(1)}, u32[]{:S(2)}, u32[]{:S(2)}) collective-permute-start(bf16[96,1280]{1,0:T(8,128)(2,1)S(1)} %get-tuple-element.68.refs_5_), channel_id=1, source_target_pairs={{0,8},{4,12},{8,0},{12,4},{1,9},{5,13},{9,1},{13,5},{2,10},{6,14},... | collective-permute-start | bytes 737288 | tf_op jit(solution)/shard_map/ppermute | solution.py:31
  61.3 5.7 %collective-permute-start.21 = (bf16[96,1280]{1,0:T(8,128)(2,1)S(1)}, bf16[96,1280]{1,0:T(8,128)(2,1)S(1)}, u32[]{:S(2)}, u32[]{:S(2)}) collective-permute-start(bf16[96,1280]{1,0:T(8,128)(2,1)S(1)} %collective-permute-done.20.refs_8_), channel_id=1, source_target_pairs={{0,4},{4,0},{8,12},{12,8},{1,5},{5,1},{9,13},{13,9},{2,6},{6,2},{1... | collective-permute-start | bytes 737288 | tf_op jit(solution)/shard_map/ppermute | solution.py:31
  61.3 4.5 %collective-permute-start.22 = (s32[1,192]{1,0:T(1,128)S(1)}, s32[1,192]{1,0:T(1,128)S(1)}, u32[]{:S(2)}, u32[]{:S(2)}) collective-permute-start(s32[1,192]{1,0:T(1,128)S(1)} %bitcast.13), channel_id=1, source_target_pairs={{0,8},{4,12},{8,0},{12,4},{1,9},{5,13},{9,1},{13,5},{2,10},{6,14},... | collective-permute-start | bytes 2312 | tf_op jit(solution)/shard_map/ppermute | solution.py:31
  65.9 1.2 %collective-permute-start.23 = (s32[2,1,192]{2,1,0:T(1,128)S(1)}, s32[2,1,192]{2,1,0:T(1,128)S(1)}, u32[]{:S(2)}, u32[]{:S(2)}) collective-permute-start(s32[2,1,192]{2,1,0:T(1,128)S(1)} %pad_add_fusion), channel_id=1, source_target_pairs={{0,4},{4,0},{8,12},{12,8},{1,5},{5,1},{9,13},{13,9},{2,6},{6,2},{1... | collective-permute-start | bytes 4616 | tf_op jit(solution)/shard_map/ppermute | solution.py:31
  65.9 2.0 %collective-permute-start.25 = (bf16[96,1280]{1,0:T(8,128)(2,1)S(1)}, bf16[96,1280]{1,0:T(8,128)(2,1)S(1)}, u32[]{:S(2)}, u32[]{:S(2)}) collective-permute-start(bf16[96,1280]{1,0:T(8,128)(2,1)S(1)} %get-tuple-element.68.refs_5_), channel_id=1, source_target_pairs={{0,4},{4,0},{8,12},{12,8},{1,5},{5,1},{9,13},{13,9},{2,6},{6,2},{1... | collective-permute-start | bytes 737288 | tf_op jit(solution)/shard_map/ppermute | solution.py:31
  66.4 1.5 %collective-permute-start.24 = (bf16[96,1280]{1,0:T(8,128)(2,1)S(1)}, bf16[96,1280]{1,0:T(8,128)(2,1)S(1)}, u32[]{:S(2)}, u32[]{:S(2)}) collective-permute-start(bf16[96,1280]{1,0:T(8,128)(2,1)S(1)} %get-tuple-element.70.refs_4_), channel_id=1, source_target_pairs={{0,4},{4,0},{8,12},{12,8},{1,5},{5,1},{9,13},{13,9},{2,6},{6,2},{1... | collective-permute-start | bytes 737288 | tf_op jit(solution)/shard_map/ppermute | solution.py:31
  67.0 1.5 %collective-permute-start.26 = (bf16[96,1280]{1,0:T(8,128)(2,1)S(1)}, bf16[96,1280]{1,0:T(8,128)(2,1)S(1)}, u32[]{:S(2)}, u32[]{:S(2)}) collective-permute-start(bf16[96,1280]{1,0:T(8,128)(2,1)S(1)} %collective-permute-done.19.refs_9_), channel_id=1, source_target_pairs={{0,4},{4,0},{8,12},{12,8},{1,5},{5,1},{9,13},{13,9},{2,6},{6,2},{1... | collective-permute-start | bytes 737288 | tf_op jit(solution)/shard_map/ppermute | solution.py:31
  (2 other events, 1.8 us)

commit v11 on v10

--- a/solution.py
+++ b/solution.py
@@ -89,10 +89,9 @@
     return jnp.concatenate([p[:rows], p[rows : 2 * rows]], axis=1), rest
 
 
-def pack_kernel(qkv_ref, all_ref, *third_refs):
-    for j, ref in enumerate(third_refs):
-        all_ref[j] = pack(qkv_ref[j])
-        ref[...] = all_ref[j]
+def pack_kernel(qkv_ref, *out_refs):
+    for j, out_ref in enumerate(out_refs):
+        out_ref[...] = pack(qkv_ref[j])
 
 
 def pack_proj_kernel(own_ref, next_ref, far_ref, all_ref, far_out_ref):
@@ -130,27 +129,34 @@
         w_ref[rows, count * main :] = tails[0] if count == 1 else jnp.concatenate(tails, axis=1)
 
 
-def score_kernel(n_ctx, width, index_ref, hidden_ref, valid_ref, *refs):
-    own_ref, twin_ref = refs[:2]
-    others = refs[2 : 2 + 2 * (n_ctx - 2)]
-    out_ref, w_ref, q_ref, k_ref = refs[2 + len(others) :]
+def bias_kernel(valid_ref, out_ref):
+    q_win = lax.broadcasted_iota(jnp.int32, (PAIR, PAIR), 0) // WIN
+    k_win = lax.broadcasted_iota(jnp.int32, (PAIR, PAIR), 1) // WIN
+    same = q_win == k_win
+    floor = jnp.where(same, F32(-1e30), F32(-3e38))
+    for p in range(valid_ref.shape[0]):
+        seen = same & (valid_ref[p : p + 1, :] > 0)
+        out_ref[p * PAIR : (p + 1) * PAIR, :] = jnp.where(seen, F32(0), floor)
+
+
+def score_kernel(n_ctx, width, index_ref, hidden_ref, bias_ref, *refs):
+    count = n_ctx // 2
+    *shards, query_ref, key_ref = refs[: n_ctx + 2]
+    out_ref, w_ref, q_ref, k_ref = refs[n_ctx + 2 :]
     rows, feat = hidden_ref.shape
     heads = width // HD
     main = 2 * LANES
     rest = width - main
-    blocks = [[own_ref[0], own_ref[1]], [twin_ref[0], twin_ref[1]]]
-    for key in range(2, n_ctx):
-        blocks.append([others[2 * key - 4][...], others[2 * key - 3][...]])
+    blocks = []
+    for i in range(count):
+        blocks.append([shards[i][...], shards[count + i][...]])
+        blocks.append([query_ref[i], key_ref[i]])
     load_weights(index_ref[0], feat // n_ctx, width, 2, blocks, w_ref)
     qk = jnp.dot(hidden_ref[...], w_ref[...], preferred_element_type=F32)
     for j, ref in enumerate((q_ref, k_ref)):
         ref[:, :main] = qk[:, j * main : (j + 1) * main].astype(BF16)
         at = 2 * main + j * rest
         ref[:, main:] = qk[:, at : at + rest].astype(BF16)
-    q_win = lax.broadcasted_iota(jnp.int32, (PAIR, PAIR), 0) // WIN
-    k_win = lax.broadcasted_iota(jnp.int32, (PAIR, PAIR), 1) // WIN
-    same = q_win == k_win
-    floor = jnp.where(same, F32(-1e30), F32(-3e38))
     zero = jnp.zeros((HD, PAIR), BF16)
     factor = F32(HD ** (-0.5) * math.log2(math.e))
     for p in range(rows // PAIR):
@@ -166,20 +172,21 @@
             axis=0,
         )
         scores = jnp.dot(q_ref[at : at + PAIR, :], k_all, preferred_element_type=F32)
-        seen = same & (valid_ref[p : p + 1, :] > 0)
+        bias = bias_ref[at : at + PAIR, :]
         for h in range(heads):
-            s = jnp.where(seen, scores[:, h * PAIR : (h + 1) * PAIR], floor)
+            s = scores[:, h * PAIR : (h + 1) * PAIR] + bias
             e = jnp.exp2((s - jnp.max(s, axis=-1, keepdims=True)) * factor)
             out_ref[at : at + PAIR, h * PAIR : (h + 1) * PAIR] = e.astype(BF16)
 
 
 def mix_kernel(n_ctx, width, index_ref, hidden_ref, exps_ref, *refs):
-    own_ref, twin_ref = refs[:2]
-    others = refs[2:n_ctx]
-    *out_refs, w_ref, v_ref, mix_ref = refs[n_ctx:]
+    twin_ref, *own_refs = refs[: n_ctx // 2 + 1]
+    *out_refs, w_ref, v_ref, mix_ref = refs[n_ctx // 2 + 1 :]
     rows, feat = hidden_ref.shape
     heads = width // HD
-    blocks = [[own_ref[2]], [twin_ref[2]]] + [[ref[...]] for ref in others]
+    blocks = []
+    for i, ref in enumerate(own_refs):
+        blocks += [[ref[...]], [twin_ref[i]]]
     load_weights(index_ref[0], feat // n_ctx, width, 1, blocks, w_ref)
     v_ref[...] = jnp.dot(hidden_ref[...], w_ref[...], preferred_element_type=F32).astype(BF16)
     lane = lax.broadcasted_iota(jnp.int32, (1, width), 1)
@@ -220,9 +227,8 @@
     mains = []
     rests = []
     for key in range(n_ctx):
-        pieces = []
-        for ref in [blocks.pop(0) for _ in range(2)]:
-            pieces += [ref[...]] if len(ref.shape) == 2 else [ref[i] for i in range(ref.shape[0])]
+        three, one = blocks.pop(0), blocks.pop(0)
+        pieces = [three[0], three[1], three[2], one[...]]
         halves = [unpack(p, width, col) for p in pieces]
         both = []
         for half in ([h[0] for h in halves], [h[1] for h in halves]):
@@ -282,17 +288,17 @@
 
     third = packed_shape(depth, width)
     piece = packed_shape(width, col)
-    own, *thirds = pl.pallas_call(
+    query, key, value = pl.pallas_call(
         pack_kernel,
-        out_shape=(shape(3, *third),) + (shape(*third),) * 3,
+        out_shape=(shape(*third),) * 3,
         in_specs=[VMEM],
-        out_specs=(VMEM,) * 4,
+        out_specs=(VMEM,) * 3,
         compiler_params=params(8),
         name="pack",
     )(jnp.transpose(w_qkv, (1, 0, 2)))
-    query = gather_cross(thirds[0], n_ctx)
-    key = gather_cross(thirds[1], n_ctx)
-    value = gather_cross(thirds[2], n_ctx)
+    query = gather_cross(query, n_ctx)
+    key = gather_cross(key, n_ctx)
+    value = gather_cross(value, n_ctx)
     by_one = swap(w_proj, "tensor", n_ten, 1)
     far = lax.ppermute(
         w_proj,
@@ -303,15 +309,6 @@
             for t in range(n_ten)
         ],
     )
-    near, far = pl.pallas_call(
-        pack_proj_kernel,
-        out_shape=(shape(3, *piece), shape(*piece)),
-        in_specs=[VMEM] * 3,
-        out_specs=(VMEM, VMEM),
-        compiler_params=params(8),
-        cost_estimate=cost(5),
-        name="pack_proj",
-    )(w_proj, by_one, far)
     hidden, own_patches = pl.pallas_call(
         norm_kernel,
         out_shape=(shape(rows, feat), shape(groups, feat)),
@@ -320,16 +317,31 @@
         compiler_params=params(16),
         name="norm",
     )(index, patches, gain_attn)
-    twin = over_core(own)
+    by_one, far, hidden = together(by_one, far, hidden)
+    near, far = pl.pallas_call(
+        pack_proj_kernel,
+        out_shape=(shape(3, *piece), shape(*piece)),
+        in_specs=[VMEM] * 3,
+        out_specs=(VMEM, VMEM),
+        compiler_params=params(8),
+        cost_estimate=cost(1000),
+        name="pack_proj",
+    )(w_proj, by_one, far)
     query, key, hidden, near, far = together(query, key, hidden, near, far)
 
-    query_twin = {k: over_core(query[k]) for k in cross}
-    key_twin = {k: over_core(key[k]) for k in cross}
-    far2 = over_dp(far)
-
-    shard_list = [own, twin]
-    for k in cross:
-        shard_list += [query[k], key[k], query_twin[k], key_twin[k]]
+    low = gather_cross(near[0], n_ctx)
+    shard_list = [x[k] for x in (query, key) for k in (0, *cross)]
+    count = len(shard_list) // 2
+    shard_list += [over_core(jnp.stack(shard_list[:count])), over_core(jnp.stack(shard_list[count:]))]
+    bias = pl.pallas_call(
+        bias_kernel,
+        out_shape=jax.ShapeDtypeStruct((rows, PAIR), F32),
+        in_specs=[VMEM],
+        out_specs=VMEM,
+        compiler_params=params(8),
+        name="bias",
+    )(valid.reshape(rows // PAIR, PAIR))
+
     exps = pl.pallas_call(
         functools.partial(score_kernel, n_ctx, width),
         out_shape=shape(rows, width // HD * PAIR),
@@ -338,21 +350,17 @@
         scratch_shapes=[pltpu.VMEM((feat, 2 * width), BF16)] + [pltpu.VMEM((rows, width), BF16)] * 2,
         compiler_params=params(20),
         name="scores",
-    )(index, hidden, valid.reshape(rows // PAIR, PAIR), *shard_list)
-    exps, value = together(exps, value)
-    value_twin = {k: over_core(value[k]) for k in cross}
-    near, far2 = together(near, far2, exps)[:2]
-    low = gather_cross(near, n_ctx)
-    high = gather_cross(far2, n_ctx)
+    )(index, hidden, bias, *shard_list)
+    exps, value, far = together(exps, value, far)
+    values = [value[k] for k in (0, *cross)]
+    value_twin = over_core(jnp.stack(values))
+    far2 = over_dp(far)
+    middle = gather_cross(near[1:], n_ctx)
     near_twin = over_core(near)
-    far2_twin = over_core(far2)
-    value_list = []
-    for k in cross:
-        value_list += [value[k], value_twin[k]]
     mixed = pl.pallas_call(
         functools.partial(mix_kernel, n_ctx, width),
         out_shape=(shape(*packed_shape(groups, width)),) * n_ten,
-        in_specs=[SMEM] + [VMEM] * (2 + n_ctx),
+        in_specs=[SMEM] + [VMEM] * (3 + len(values)),
         out_specs=(VMEM,) * n_ten,
         scratch_shapes=[
             pltpu.VMEM((feat, width), BF16),
@@ -361,14 +369,18 @@
         ],
         compiler_params=params(16),
         name="mix",
-    )(index, hidden, exps, own, twin, *value_list)
-
+    )(index, hidden, exps, value_twin, *values)
+
+    mixed, far2, near_twin = together(mixed, far2, near_twin)
     received = {s: swap(mixed[s], "tensor", n_ten, s) for s in (2, 3, 1)}
     mixed = [mixed[0]] + [received[s] for s in range(1, n_ten)]
-    blocks = [near, far2, near_twin, far2_twin]
-    mixed, low, high = together(mixed, low, high)
-    for k in cross:
-        blocks += [low[k], high[k], over_core(low[k]), over_core(high[k])]
+    high = gather_cross(far2, n_ctx)
+    mixed, low, middle, high = together(mixed, low, middle, high)
+    high_twin = over_core(jnp.stack([far2] + [high[k] for k in cross]))
+    blocks = [near, far2, near_twin, high_twin[0]]
+    for i, k in enumerate(cross):
+        three = jnp.concatenate([low[k][None], middle[k]], axis=0)
+        blocks += [three, high[k], over_core(three), high_twin[1 + i]]
     done = pl.pallas_call(
         functools.partial(project_kernel, n_ctx, width, col),
         out_shape=(shape(groups // HALVES, feat),) * HALVES,

time: 70.7 us -> 71.8 us (1.016)
  starting transfers between devices: 22.2 us -> 23.4 us
    ppermute x26 -> x25, starting transfers between devices: 19.7 us -> 20.8 us  [swap(): return lax.ppermute(x, axis, [(i, i ^ bit) for i in range(size)])]
    ppermute x26 -> x25, waiting for transfers between devices: 28.6 us -> 28.3 us  [swap(): return lax.ppermute(x, axis, [(i, i ^ bit) for i in range(size)])]
  transfers between devices with their start and end apart: 27 -> 26, of which waited for: 12 -> 15; matrix products, arithmetic and copies ran while one was open for 0% -> 0% of each run, Pallas kernels for 13% -> 13%
where the time goes in v11:
time: 71.8 us; the launch traced here: 71.6 us
  waiting for transfers between devices  30.8 us (43%)
  starting transfers between devices  23.4 us (33%)
  Pallas kernels  13.4 us (19%)
  local copies, waits for them, and re-layouts  3.45 us (5%)
    ppermute x25, waiting for transfers between devices, swap(): return lax.ppermute(x, axis, [(i, i ^ bit) for i in range(size)])  28.3 us
    ppermute x25, starting transfers between devices, swap(): return lax.ppermute(x, axis, [(i, i ^ bit) for i in range(size)])  20.8 us
    pallas_call x1, Pallas kernels, local(): pl.pallas_call(functools.partial(score_kernel, n_ctx, width), out_shape=s...  3.9 us
    pallas_call x1, Pallas kernels, local(): pl.pallas_call(functools.partial(mix_kernel, n_ctx, width), out_shape=(sh...  3.87 us
    unnamed x14, local copies, waits for them, and re-layouts  3.38 us
    ppermute x1, starting transfers between devices, local(): lax.ppermute(w_proj, ('dp', 'tensor'), [(d * n_ten + t, d * n_ten + (t ^...  2.59 us
    ppermute x1, waiting for transfers between devices, local(): lax.ppermute(w_proj, ('dp', 'tensor'), [(d * n_ten + t, d * n_ten + (t ^...  2.56 us
    pallas_call x1, Pallas kernels, local(): pl.pallas_call(functools.partial(project_kernel, n_ctx, width, col), out_...  1.92 us
  transfers between devices with their start and end apart: 26, of which 15 were waited for; matrix products, arithmetic and copies ran while one was open for 0% of the time, Pallas kernels for 13%

profile of v11, /device:TPU:0, one launch (start us, length us, event | category | flops | bytes accessed | tf_op | source)
XLA Modules:
  0.0 71.6 jit_solution(16007675000638841233)
XLA Ops:
  0.0 3.0 %collective-permute-start.2 = (bf16[320,320]{1,0:T(8,128)(2,1)}, bf16[320,320]{1,0:T(8,128)(2,1)S(1)}, u32[]{:S(2)}, u32[]{:S(2)}) collective-permute-start(bf16[320,320]{1,0:T(8,128)(2,1)} %own_ref.1), channel_id=1, source_target_pairs={{0,1},{1,0},{2,3},{3,2},{4,5},{5,4},{6,7},{7,6},{8,9},{9,8},{10,11... | collective-permute-start | bytes 614408 | tf_op jit(solution)/shard_map/ppermute | solution.py:31
  3.0 2.6 %collective-permute-start.3 = (bf16[320,320]{1,0:T(8,128)(2,1)}, bf16[320,320]{1,0:T(8,128)(2,1)S(1)}, u32[]{:S(2)}, u32[]{:S(2)}) collective-permute-start(bf16[320,320]{1,0:T(8,128)(2,1)} %own_ref.1), channel_id=1, source_target_pairs={{0,2},{1,3},{2,0},{3,1},{16,19},{17,18},{18,17},{19,16},{4,6},{5,7... | collective-permute-start | bytes 614408 | tf_op jit(solution)/shard_map/ppermute | solution.py:303
  5.6 1.1 %copy-done.1 = bf16[320,3,320]{2,0,1:T(8,128)(2,1)S(1)} copy-done((bf16[320,3,320]{2,0,1:T(8,128)(2,1)S(1)}, bf16[320,3,320]{2,0,1:T(8,128)(2,1)}, u32[]{:S(2)}) %copy-start.1) | copy-done | bytes 614424
  6.8 1.6 %collective-permute-start = (bf16[800,128]{1,0:T(8,128)(2,1)S(1)}, bf16[800,128]{1,0:T(8,128)(2,1)S(1)}, u32[]{:S(2)}, u32[]{:S(2)}) collective-permute-start(bf16[800,128]{1,0:T(8,128)(2,1)S(1)} %get-tuple-element.59.refs_0_), channel_id=1, source_target_pairs={{0,8},{4,12},{8,0},{12,4},{1,9},{5,13},{9,1},{13,5},{2,10},{6,14},... | collective-permute-start | bytes 614408 | tf_op jit(solution)/shard_map/ppermute | solution.py:31
  9.0 1.5 %copy-done = bf16[768,1280]{1,0:T(8,128)(2,1)S(1)} copy-done((bf16[768,1280]{1,0:T(8,128)(2,1)S(1)}, bf16[768,1280]{1,0:T(8,128)(2,1)}, u32[]{:S(2)}) %copy-start) | copy-done | bytes 1966104
  10.6 0.7 copy-done.3
  11.2 1.6 %norm.1 = (bf16[768,1280]{1,0:T(8,128)(2,1)S(1)}, bf16[192,1280]{1,0:T(8,128)(2,1)S(1)}) custom-call(s32[3]{0:T(128)S(1)} %pad_add_fusion.1.index_ref, bf16[768,1280]{1,0:T(8,128)(2,1)S(1)} %copy-done, f32[1280]{0:T(1024)S(1)} %copy-done.3), custom_call_target="tpu_custom_call" | custom-call | tf_op jit(solution)/shard_map/norm/pallas_call | solution.py:312
  12.8 1.5 %collective-permute-done.2.next_ref = bf16[320,320]{1,0:T(8,128)(2,1)S(1)} collective-permute-done((bf16[320,320]{1,0:T(8,128)(2,1)}, bf16[320,320]{1,0:T(8,128)(2,1)S(1)}, u32[]{:S(2)}, u32[]{:S(2)}) %collective-permute-start.2) | collective-permute-done | bytes 204832 | tf_op jit(solution)/shard_map/ppermute | solution.py:31
  14.3 2.6 %collective-permute-done.3.far_ref = bf16[320,320]{1,0:T(8,128)(2,1)S(1)} collective-permute-done((bf16[320,320]{1,0:T(8,128)(2,1)}, bf16[320,320]{1,0:T(8,128)(2,1)S(1)}, u32[]{:S(2)}, u32[]{:S(2)}) %collective-permute-start.3) | collective-permute-done | bytes 204832 | tf_op jit(solution)/shard_map/ppermute | solution.py:303
  18.3 1.5 %collective-permute-start.6 = (bf16[800,128]{1,0:T(8,128)(2,1)S(1)}, bf16[800,128]{1,0:T(8,128)(2,1)S(1)}, u32[]{:S(2)}, u32[]{:S(2)}) collective-permute-start(bf16[800,128]{1,0:T(8,128)(2,1)S(1)} %get-tuple-element.66.refs_1_), channel_id=1, source_target_pairs={{0,8},{4,12},{8,0},{12,4},{1,9},{5,13},{9,1},{13,5},{2,10},{6,14},... | collective-permute-start | bytes 614408 | tf_op jit(solution)/shard_map/ppermute | solution.py:31
  20.0 3.9 %scores.1.exps_ref = bf16[768,512]{1,0:T(8,128)(2,1)S(1)} custom-call(s32[3]{0:T(128)S(1)} %pad_add_fusion.1.index_ref, bf16[768,1280]{1,0:T(8,128)(2,1)S(1)} %get-tuple-element.58.hidden_ref, f32[768,128]{1,0:T(8,128)S(1)} %bias.1.bias_ref, bf16[800,128]{1,0:T(8,128)(2,1)S(1)} %get-tuple-element.59.refs_0_, ...), custom_call_target="tpu_custom_call" | custom-call | tf_op jit(solution)/shard_map/scores/pallas_call | solution.py:345
  23.9 1.4 %collective-permute-done.6.refs_2_ = bf16[800,128]{1,0:T(8,128)(2,1)S(1)} collective-permute-done((bf16[800,128]{1,0:T(8,128)(2,1)S(1)}, bf16[800,128]{1,0:T(8,128)(2,1)S(1)}, u32[]{:S(2)}, u32[]{:S(2)}) %collective-permute-start.6) | collective-permute-done | bytes 204832 | tf_op jit(solution)/shard_map/ppermute | solution.py:31
  25.5 1.6 %collective-permute-start.14 = (bf16[2,800,128]{2,1,0:T(8,128)(2,1)S(1)}, bf16[2,800,128]{2,1,0:T(8,128)(2,1)S(1)}, u32[]{:S(2)}, u32[]{:S(2)}) collective-permute-start(bf16[2,800,128]{2,1,0:T(8,128)(2,1)S(1)} %slice.19), channel_id=1, source_target_pairs={{0,8},{4,12},{8,0},{12,4},{1,9},{5,13},{9,1},{13,5},{2,10},{6,14},... | collective-permute-start | bytes 1228808 | tf_op jit(solution)/shard_map/ppermute | solution.py:31
  27.1 1.4 %collective-permute-start.8 = (bf16[800,128]{1,0:T(8,128)(2,1)S(1)}, bf16[800,128]{1,0:T(8,128)(2,1)S(1)}, u32[]{:S(2)}, u32[]{:S(2)}) collective-permute-start(bf16[800,128]{1,0:T(8,128)(2,1)S(1)} %get-tuple-element.72), channel_id=1, source_target_pairs={{0,16},{16,0},{1,17},{17,1},{2,18},{18,2},{3,19},{19,3},{4,20},{20... | collective-permute-start | bytes 614408 | tf_op jit(solution)/shard_map/ppermute | solution.py:31
  28.5 0.6 collective-permute-start.13
  29.0 3.9 %mix.1 = (bf16[480,128]{1,0:T(8,128)(2,1)S(1)}, bf16[480,128]{1,0:T(8,128)(2,1)S(1)}, bf16[480,128]{1,0:T(8,128)(2,1)S(1)}, bf16[480,128]{1,0:T(8,128)(2,1)S(1)}) custom-call(s32[3]{0:T(128)S(1)} %pad_add_fusion.1.index_ref, bf16[768,1280]{1,0:T(8,128)(2,1)S(1)} %get-tuple-element.58.hidden_ref, bf16[768,512]{1,0:T(8,128)(2,1)S(1)} %scores.1.exps_ref, ...), custom_call_target="tpu_custom_call" | custom-call | tf_op jit(solution)/shard_map/mix/pallas_call | solution.py:360
  32.9 1.3 %collective-permute-done.8.refs_5_ = bf16[800,128]{1,0:T(8,128)(2,1)S(1)} collective-permute-done((bf16[800,128]{1,0:T(8,128)(2,1)S(1)}, bf16[800,128]{1,0:T(8,128)(2,1)S(1)}, u32[]{:S(2)}, u32[]{:S(2)}) %collective-permute-start.8) | collective-permute-done | bytes 204832 | tf_op jit(solution)/shard_map/ppermute | solution.py:31
  35.2 2.1 %collective-permute-start.11 = (bf16[480,128]{1,0:T(8,128)(2,1)S(1)}, bf16[480,128]{1,0:T(8,128)(2,1)S(1)}, u32[]{:S(2)}, u32[]{:S(2)}) collective-permute-start(bf16[480,128]{1,0:T(8,128)(2,1)S(1)} %get-tuple-element.76), channel_id=1, source_target_pairs={{0,2},{1,3},{2,0},{3,1},{4,6},{5,7},{6,4},{7,5},{8,10},{9,11},{10,... | collective-permute-start | bytes 368648 | tf_op jit(solution)/shard_map/ppermute | solution.py:31
  37.3 4.9 %collective-permute-done.13 = bf16[800,128]{1,0:T(8,128)(2,1)S(1)} collective-permute-done((bf16[800,128]{1,0:T(8,128)(2,1)S(1)}, bf16[800,128]{1,0:T(8,128)(2,1)S(1)}, u32[]{:S(2)}, u32[]{:S(2)}) %collective-permute-start.13) | collective-permute-done | bytes 204832 | tf_op jit(solution)/shard_map/ppermute | solution.py:31
  42.2 1.9 %collective-permute-start.12 = (bf16[480,128]{1,0:T(8,128)(2,1)S(1)}, bf16[480,128]{1,0:T(8,128)(2,1)S(1)}, u32[]{:S(2)}, u32[]{:S(2)}) collective-permute-start(bf16[480,128]{1,0:T(8,128)(2,1)S(1)} %get-tuple-element.77), channel_id=1, source_target_pairs={{0,3},{1,2},{2,1},{3,0},{4,7},{5,6},{6,5},{7,4},{8,11},{9,10},{10,... | collective-permute-start | bytes 368648 | tf_op jit(solution)/shard_map/ppermute | solution.py:31
  44.2 4.8 %collective-permute-done.12.refs_3_ = bf16[480,128]{1,0:T(8,128)(2,1)S(1)} collective-permute-done((bf16[480,128]{1,0:T(8,128)(2,1)S(1)}, bf16[480,128]{1,0:T(8,128)(2,1)S(1)}, u32[]{:S(2)}, u32[]{:S(2)}) %collective-permute-start.12) | collective-permute-done | bytes 122912 | tf_op jit(solution)/shard_map/ppermute | solution.py:31
  49.7 1.1 %collective-permute-done.16 = bf16[2,800,128]{2,1,0:T(8,128)(2,1)S(1)} collective-permute-done((bf16[2,800,128]{2,1,0:T(8,128)(2,1)S(1)}, bf16[2,800,128]{2,1,0:T(8,128)(2,1)S(1)}, u32[]{:S(2)}, u32[]{:S(2)}) %collective-permute-start.16) | collective-permute-done | bytes 409632 | tf_op jit(solution)/shard_map/ppermute | solution.py:31
  50.8 0.8 %collective-permute-done.17.refs_10_ = bf16[3,800,128]{2,1,0:T(8,128)(2,1)S(1)} collective-permute-done((bf16[3,800,128]{2,1,0:T(8,128)(2,1)S(1)}, bf16[3,800,128]{2,1,0:T(8,128)(2,1)S(1)}, u32[]{:S(2)}, u32[]{:S(2)}) %collective-permute-start.17) | collective-permute-done | bytes 614432 | tf_op jit(solution)/shard_map/ppermute | solution.py:31
  51.7 1.9 %project.1 = (bf16[96,1280]{1,0:T(8,128)(2,1)S(1)}, bf16[96,1280]{1,0:T(8,128)(2,1)S(1)}) custom-call(s32[3]{0:T(128)S(1)} %pad_add_fusion.1.index_ref, bf16[480,128]{1,0:T(8,128)(2,1)S(1)} %get-tuple-element.79.refs_0_, bf16[480,128]{1,0:T(8,128)(2,1)S(1)} %collective-permute-done.10.refs_1_, bf16[480,128]{1,0:T(8,128)(2,1)S(1)} %collective-permute-done.11.refs_2_, ...), custom_call_target="tpu_custom_call" | custom-call | tf_op jit(solution)/shard_map/project/pallas_call | solution.py:384
  53.6 1.6 %collective-permute-start.19 = (bf16[96,1280]{1,0:T(8,128)(2,1)S(1)}, bf16[96,1280]{1,0:T(8,128)(2,1)S(1)}, u32[]{:S(2)}, u32[]{:S(2)}) collective-permute-start(bf16[96,1280]{1,0:T(8,128)(2,1)S(1)} %get-tuple-element.92.refs_4_), channel_id=1, source_target_pairs={{0,8},{4,12},{8,0},{12,4},{1,9},{5,13},{9,1},{13,5},{2,10},{6,14},... | collective-permute-start | bytes 737288 | tf_op jit(solution)/shard_map/ppermute | solution.py:31
  55.7 6.8 %collective-permute-done.19.refs_8_ = bf16[96,1280]{1,0:T(8,128)(2,1)S(1)} collective-permute-done((bf16[96,1280]{1,0:T(8,128)(2,1)S(1)}, bf16[96,1280]{1,0:T(8,128)(2,1)S(1)}, u32[]{:S(2)}, u32[]{:S(2)}) %collective-permute-start.19) | collective-permute-done | bytes 245792 | tf_op jit(solution)/shard_map/ppermute | solution.py:31
  62.5 1.5 %collective-permute-start.21 = (s32[1,192]{1,0:T(1,128)S(1)}, s32[1,192]{1,0:T(1,128)S(1)}, u32[]{:S(2)}, u32[]{:S(2)}) collective-permute-start(s32[1,192]{1,0:T(1,128)S(1)} %bitcast.37), channel_id=1, source_target_pairs={{0,8},{4,12},{8,0},{12,4},{1,9},{5,13},{9,1},{13,5},{2,10},{6,14},... | collective-permute-start | bytes 2312 | tf_op jit(solution)/shard_map/ppermute | solution.py:31
  64.0 3.0 %collective-permute-done.21.refs_2_ = s32[1,192]{1,0:T(1,128)S(1)} collective-permute-done((s32[1,192]{1,0:T(1,128)S(1)}, s32[1,192]{1,0:T(1,128)S(1)}, u32[]{:S(2)}, u32[]{:S(2)}) %collective-permute-start.21) | collective-permute-done | bytes 800 | tf_op jit(solution)/shard_map/ppermute | solution.py:31
  67.6 0.6 collective-permute-done.22
  68.4 0.7 collective-permute-done.23.refs_6_
  69.0 0.7 collective-permute-done.25.refs_11_
  69.7 1.9 %placement.1 = bf16[192,1280]{1,0:T(8,128)(2,1)} custom-call(s32[3]{0:T(128)S(1)} %pad_add_fusion.1.index_ref, s32[1,192]{1,0:T(1,128)S(1)} %bitcast.39, s32[1,192]{1,0:T(1,128)S(1)} %get-tuple-element.98.refs_1_, s32[1,192]{1,0:T(1,128)S(1)} %collective-permute-done.21.refs_2_, s32[1,192]{1,0:T(1,128)S(1)} %get-tuple-element.97.refs_3_, ...), custom_call_target="tpu_custom_call" | custom-call | tf_op jit(solution)/shard_map/placement/pallas_call | solution.py:412
  (53 shorter events, 5.4 us)
Async XLA Ops:
  0.0 14.3 %collective-permute-start.2 = (bf16[320,320]{1,0:T(8,128)(2,1)}, bf16[320,320]{1,0:T(8,128)(2,1)S(1)}, u32[]{:S(2)}, u32[]{:S(2)}) collective-permute-start(bf16[320,320]{1,0:T(8,128)(2,1)} %own_ref.1), channel_id=1, source_target_pairs={{0,1},{1,0},{2,3},{3,2},{4,5},{5,4},{6,7},{7,6},{8,9},{9,8},{10,11... | collective-permute-start | bytes 614408 | tf_op jit(solution)/shard_map/ppermute | solution.py:31
  3.0 13.9 %collective-permute-start.3 = (bf16[320,320]{1,0:T(8,128)(2,1)}, bf16[320,320]{1,0:T(8,128)(2,1)S(1)}, u32[]{:S(2)}, u32[]{:S(2)}) collective-permute-start(bf16[320,320]{1,0:T(8,128)(2,1)} %own_ref.1), channel_id=1, source_target_pairs={{0,2},{1,3},{2,0},{3,1},{16,19},{17,18},{18,17},{19,16},{4,6},{5,7... | collective-permute-start | bytes 614408 | tf_op jit(solution)/shard_map/ppermute | solution.py:303
  5.6 1.1 %copy-start.1 = (bf16[320,3,320]{2,0,1:T(8,128)(2,1)S(1)}, bf16[320,3,320]{2,0,1:T(8,128)(2,1)}, u32[]{:S(2)}) copy-start(bf16[320,3,320]{2,0,1:T(8,128)(2,1)} %param.11) | copy-start | bytes 1843204
  6.7 10.1 %copy-start.2 = (bf16[320,320]{1,0:T(8,128)(2,1)S(1)}, bf16[320,320]{1,0:T(8,128)(2,1)}, u32[]{:S(2)}) copy-start(bf16[320,320]{1,0:T(8,128)(2,1)} %own_ref.1) | copy-start | bytes 614404
  6.8 10.2 %collective-permute-start = (bf16[800,128]{1,0:T(8,128)(2,1)S(1)}, bf16[800,128]{1,0:T(8,128)(2,1)S(1)}, u32[]{:S(2)}, u32[]{:S(2)}) collective-permute-start(bf16[800,128]{1,0:T(8,128)(2,1)S(1)} %get-tuple-element.59.refs_0_), channel_id=1, source_target_pairs={{0,8},{4,12},{8,0},{12,4},{1,9},{5,13},{9,1},{13,5},{2,10},{6,14},... | collective-permute-start | bytes 614408 | tf_op jit(solution)/shard_map/ppermute | solution.py:31
  8.4 9.1 %collective-permute-start.1 = (bf16[800,128]{1,0:T(8,128)(2,1)S(1)}, bf16[800,128]{1,0:T(8,128)(2,1)S(1)}, u32[]{:S(2)}, u32[]{:S(2)}) collective-permute-start(bf16[800,128]{1,0:T(8,128)(2,1)S(1)} %get-tuple-element.61.refs_2_), channel_id=1, source_target_pairs={{0,8},{4,12},{8,0},{12,4},{1,9},{5,13},{9,1},{13,5},{2,10},{6,14},... | collective-permute-start | bytes 614408 | tf_op jit(solution)/shard_map/ppermute | solution.py:31
  9.0 1.5 %copy-start = (bf16[768,1280]{1,0:T(8,128)(2,1)S(1)}, bf16[768,1280]{1,0:T(8,128)(2,1)}, u32[]{:S(2)}) copy-start(bf16[768,1280]{1,0:T(8,128)(2,1)} %patches_ref.1) | copy-start | bytes 5898244
  11.2 8.6 %copy-start.5 = (s32[768]{0:T(1024)S(1)}, s32[768]{0:T(1024)}, u32[]{:S(2)}) copy-start(s32[768]{0:T(1024)} %param.8) | copy-start | bytes 9220
  17.6 2.3 %collective-permute-start.5 = (bf16[2,800,128]{2,1,0:T(8,128)(2,1)S(1)}, bf16[2,800,128]{2,1,0:T(8,128)(2,1)S(1)}, u32[]{:S(2)}, u32[]{:S(2)}) collective-permute-start(bf16[2,800,128]{2,1,0:T(8,128)(2,1)S(1)} %pad_maximum_fusion.2), channel_id=1, source_target_pairs={{0,4},{4,0},{8,12},{12,8},{1,5},{5,1},{9,13},{13,9},{2,6},{6,2},{1... | collective-permute-start | bytes 1228808 | tf_op jit(solution)/shard_map/ppermute | solution.py:31
  17.7 2.3 %collective-permute-start.4 = (bf16[2,800,128]{2,1,0:T(8,128)(2,1)S(1)}, bf16[2,800,128]{2,1,0:T(8,128)(2,1)S(1)}, u32[]{:S(2)}, u32[]{:S(2)}) collective-permute-start(bf16[2,800,128]{2,1,0:T(8,128)(2,1)S(1)} %pad_maximum_fusion.1), channel_id=1, source_target_pairs={{0,4},{4,0},{8,12},{12,8},{1,5},{5,1},{9,13},{13,9},{2,6},{6,2},{1... | collective-permute-start | bytes 1228808 | tf_op jit(solution)/shard_map/ppermute | solution.py:31
  18.3 7.1 %collective-permute-start.6 = (bf16[800,128]{1,0:T(8,128)(2,1)S(1)}, bf16[800,128]{1,0:T(8,128)(2,1)S(1)}, u32[]{:S(2)}, u32[]{:S(2)}) collective-permute-start(bf16[800,128]{1,0:T(8,128)(2,1)S(1)} %get-tuple-element.66.refs_1_), channel_id=1, source_target_pairs={{0,8},{4,12},{8,0},{12,4},{1,9},{5,13},{9,1},{13,5},{2,10},{6,14},... | collective-permute-start | bytes 614408 | tf_op jit(solution)/shard_map/ppermute | solution.py:31
  19.8 14.5 %collective-permute-start.9 = (bf16[3,800,128]{2,1,0:T(8,128)(2,1)S(1)}, bf16[3,800,128]{2,1,0:T(8,128)(2,1)S(1)}, u32[]{:S(2)}, u32[]{:S(2)}) collective-permute-start(bf16[3,800,128]{2,1,0:T(8,128)(2,1)S(1)} %get-tuple-element.73.refs_4_), channel_id=1, source_target_pairs={{0,4},{4,0},{8,12},{12,8},{1,5},{5,1},{9,13},{13,9},{2,6},{6,2},{1... | collective-permute-start | bytes 1843208 | tf_op jit(solution)/shard_map/ppermute | solution.py:31
  25.4 3.7 %collective-permute-start.7 = (bf16[2,800,128]{2,1,0:T(8,128)(2,1)S(1)}, bf16[2,800,128]{2,1,0:T(8,128)(2,1)S(1)}, u32[]{:S(2)}, u32[]{:S(2)}) collective-permute-start(bf16[2,800,128]{2,1,0:T(8,128)(2,1)S(1)} %pad_maximum_fusion.3), channel_id=1, source_target_pairs={{0,4},{4,0},{8,12},{12,8},{1,5},{5,1},{9,13},{13,9},{2,6},{6,2},{1... | collective-permute-start | bytes 1228808 | tf_op jit(solution)/shard_map/ppermute | solution.py:31
  25.5 18.7 %collective-permute-start.14 = (bf16[2,800,128]{2,1,0:T(8,128)(2,1)S(1)}, bf16[2,800,128]{2,1,0:T(8,128)(2,1)S(1)}, u32[]{:S(2)}, u32[]{:S(2)}) collective-permute-start(bf16[2,800,128]{2,1,0:T(8,128)(2,1)S(1)} %slice.19), channel_id=1, source_target_pairs={{0,8},{4,12},{8,0},{12,4},{1,9},{5,13},{9,1},{13,5},{2,10},{6,14},... | collective-permute-start | bytes 1228808 | tf_op jit(solution)/shard_map/ppermute | solution.py:31
  27.1 7.2 %collective-permute-start.8 = (bf16[800,128]{1,0:T(8,128)(2,1)S(1)}, bf16[800,128]{1,0:T(8,128)(2,1)S(1)}, u32[]{:S(2)}, u32[]{:S(2)}) collective-permute-start(bf16[800,128]{1,0:T(8,128)(2,1)S(1)} %get-tuple-element.72), channel_id=1, source_target_pairs={{0,16},{16,0},{1,17},{17,1},{2,18},{18,2},{3,19},{19,3},{4,20},{20... | collective-permute-start | bytes 614408 | tf_op jit(solution)/shard_map/ppermute | solution.py:31
  28.5 13.7 %collective-permute-start.13 = (bf16[800,128]{1,0:T(8,128)(2,1)S(1)}, bf16[800,128]{1,0:T(8,128)(2,1)S(1)}, u32[]{:S(2)}, u32[]{:S(2)}) collective-permute-start(bf16[800,128]{1,0:T(8,128)(2,1)S(1)} %slice_bitcast_fusion.2), channel_id=1, source_target_pairs={{0,8},{4,12},{8,0},{12,4},{1,9},{5,13},{9,1},{13,5},{2,10},{6,14},... | collective-permute-start | bytes 614408 | tf_op jit(solution)/shard_map/ppermute | solution.py:31
  32.9 18.8 %copy-start.4 = (f32[1280]{0:T(1024)S(1)}, f32[1280]{0:T(1024)}, u32[]{:S(2)}) copy-start(f32[1280]{0:T(1024)} %refs_13_.1) | copy-start | bytes 15364
  34.3 14.7 %collective-permute-start.15 = (bf16[800,128]{1,0:T(8,128)(2,1)S(1)}, bf16[800,128]{1,0:T(8,128)(2,1)S(1)}, u32[]{:S(2)}, u32[]{:S(2)}) collective-permute-start(bf16[800,128]{1,0:T(8,128)(2,1)S(1)} %collective-permute-done.8.refs_5_), channel_id=1, source_target_pairs={{0,8},{4,12},{8,0},{12,4},{1,9},{5,13},{9,1},{13,5},{2,10},{6,14},... | collective-permute-start | bytes 614408 | tf_op jit(solution)/shard_map/ppermute | solution.py:31
  34.8 9.4 %collective-permute-start.10 = (bf16[480,128]{1,0:T(8,128)(2,1)S(1)}, bf16[480,128]{1,0:T(8,128)(2,1)S(1)}, u32[]{:S(2)}, u32[]{:S(2)}) collective-permute-start(bf16[480,128]{1,0:T(8,128)(2,1)S(1)} %get-tuple-element.75), channel_id=1, source_target_pairs={{0,1},{1,0},{2,3},{3,2},{4,5},{5,4},{6,7},{7,6},{8,9},{9,8},{10,11... | collective-permute-start | bytes 368648 | tf_op jit(solution)/shard_map/ppermute | solution.py:31
  35.2 8.9 %collective-permute-start.11 = (bf16[480,128]{1,0:T(8,128)(2,1)S(1)}, bf16[480,128]{1,0:T(8,128)(2,1)S(1)}, u32[]{:S(2)}, u32[]{:S(2)}) collective-permute-start(bf16[480,128]{1,0:T(8,128)(2,1)S(1)} %get-tuple-element.76), channel_id=1, source_target_pairs={{0,2},{1,3},{2,0},{3,1},{4,6},{5,7},{6,4},{7,5},{8,10},{9,11},{10,... | collective-permute-start | bytes 368648 | tf_op jit(solution)/shard_map/ppermute | solution.py:31
  42.2 6.7 %collective-permute-start.12 = (bf16[480,128]{1,0:T(8,128)(2,1)S(1)}, bf16[480,128]{1,0:T(8,128)(2,1)S(1)}, u32[]{:S(2)}, u32[]{:S(2)}) collective-permute-start(bf16[480,128]{1,0:T(8,128)(2,1)S(1)} %get-tuple-element.77), channel_id=1, source_target_pairs={{0,3},{1,2},{2,1},{3,0},{4,7},{5,6},{6,5},{7,4},{8,11},{9,10},{10,... | collective-permute-start | bytes 368648 | tf_op jit(solution)/shard_map/ppermute | solution.py:31
  49.0 1.8 %collective-permute-start.16 = (bf16[2,800,128]{2,1,0:T(8,128)(2,1)S(1)}, bf16[2,800,128]{2,1,0:T(8,128)(2,1)S(1)}, u32[]{:S(2)}, u32[]{:S(2)}) collective-permute-start(bf16[2,800,128]{2,1,0:T(8,128)(2,1)S(1)} %pad_maximum_fusion.4), channel_id=1, source_target_pairs={{0,4},{4,0},{8,12},{12,8},{1,5},{5,1},{9,13},{13,9},{2,6},{6,2},{1... | collective-permute-start | bytes 1228808 | tf_op jit(solution)/shard_map/ppermute | solution.py:31
  49.1 2.5 %collective-permute-start.17 = (bf16[3,800,128]{2,1,0:T(8,128)(2,1)S(1)}, bf16[3,800,128]{2,1,0:T(8,128)(2,1)S(1)}, u32[]{:S(2)}, u32[]{:S(2)}) collective-permute-start(bf16[3,800,128]{2,1,0:T(8,128)(2,1)S(1)} %pad_maximum_fusion.refs_8_), channel_id=1, source_target_pairs={{0,4},{4,0},{8,12},{12,8},{1,5},{5,1},{9,13},{13,9},{2,6},{6,2},{1... | collective-permute-start | bytes 1843208 | tf_op jit(solution)/shard_map/ppermute | solution.py:31
  51.7 10.8 %copy-start.6 = (s32[192]{0:T(256)S(1)}, s32[192]{0:T(256)}, u32[]{:S(2)}) copy-start(s32[192]{0:T(256)} %param.9) | copy-start | bytes 2308
  53.6 8.9 %collective-permute-start.19 = (bf16[96,1280]{1,0:T(8,128)(2,1)S(1)}, bf16[96,1280]{1,0:T(8,128)(2,1)S(1)}, u32[]{:S(2)}, u32[]{:S(2)}) collective-permute-start(bf16[96,1280]{1,0:T(8,128)(2,1)S(1)} %get-tuple-element.92.refs_4_), channel_id=1, source_target_pairs={{0,8},{4,12},{8,0},{12,4},{1,9},{5,13},{9,1},{13,5},{2,10},{6,14},... | collective-permute-start | bytes 737288 | tf_op jit(solution)/shard_map/ppermute | solution.py:31
  55.2 13.0 %collective-permute-start.18 = (bf16[96,1280]{1,0:T(8,128)(2,1)S(1)}, bf16[96,1280]{1,0:T(8,128)(2,1)S(1)}, u32[]{:S(2)}, u32[]{:S(2)}) collective-permute-start(bf16[96,1280]{1,0:T(8,128)(2,1)S(1)} %get-tuple-element.90.refs_5_), channel_id=1, source_target_pairs={{0,8},{4,12},{8,0},{12,4},{1,9},{5,13},{9,1},{13,5},{2,10},{6,14},... | collective-permute-start | bytes 737288 | tf_op jit(solution)/shard_map/ppermute | solution.py:31
  62.5 5.7 %collective-permute-start.20 = (bf16[96,1280]{1,0:T(8,128)(2,1)S(1)}, bf16[96,1280]{1,0:T(8,128)(2,1)S(1)}, u32[]{:S(2)}, u32[]{:S(2)}) collective-permute-start(bf16[96,1280]{1,0:T(8,128)(2,1)S(1)} %collective-permute-done.19.refs_8_), channel_id=1, source_target_pairs={{0,4},{4,0},{8,12},{12,8},{1,5},{5,1},{9,13},{13,9},{2,6},{6,2},{1... | collective-permute-start | bytes 737288 | tf_op jit(solution)/shard_map/ppermute | solution.py:31
  62.5 4.5 %collective-permute-start.21 = (s32[1,192]{1,0:T(1,128)S(1)}, s32[1,192]{1,0:T(1,128)S(1)}, u32[]{:S(2)}, u32[]{:S(2)}) collective-permute-start(s32[1,192]{1,0:T(1,128)S(1)} %bitcast.37), channel_id=1, source_target_pairs={{0,8},{4,12},{8,0},{12,4},{1,9},{5,13},{9,1},{13,5},{2,10},{6,14},... | collective-permute-start | bytes 2312 | tf_op jit(solution)/shard_map/ppermute | solution.py:31
  67.0 1.2 %collective-permute-start.22 = (s32[2,1,192]{2,1,0:T(1,128)S(1)}, s32[2,1,192]{2,1,0:T(1,128)S(1)}, u32[]{:S(2)}, u32[]{:S(2)}) collective-permute-start(s32[2,1,192]{2,1,0:T(1,128)S(1)} %pad_add_fusion), channel_id=1, source_target_pairs={{0,4},{4,0},{8,12},{12,8},{1,5},{5,1},{9,13},{13,9},{2,6},{6,2},{1... | collective-permute-start | bytes 4616 | tf_op jit(solution)/shard_map/ppermute | solution.py:31
  67.0 2.0 %collective-permute-start.24 = (bf16[96,1280]{1,0:T(8,128)(2,1)S(1)}, bf16[96,1280]{1,0:T(8,128)(2,1)S(1)}, u32[]{:S(2)}, u32[]{:S(2)}) collective-permute-start(bf16[96,1280]{1,0:T(8,128)(2,1)S(1)} %get-tuple-element.90.refs_5_), channel_id=1, source_target_pairs={{0,4},{4,0},{8,12},{12,8},{1,5},{5,1},{9,13},{13,9},{2,6},{6,2},{1... | collective-permute-start | bytes 737288 | tf_op jit(solution)/shard_map/ppermute | solution.py:31
  67.5 1.5 %collective-permute-start.23 = (bf16[96,1280]{1,0:T(8,128)(2,1)S(1)}, bf16[96,1280]{1,0:T(8,128)(2,1)S(1)}, u32[]{:S(2)}, u32[]{:S(2)}) collective-permute-start(bf16[96,1280]{1,0:T(8,128)(2,1)S(1)} %get-tuple-element.92.refs_4_), channel_id=1, source_target_pairs={{0,4},{4,0},{8,12},{12,8},{1,5},{5,1},{9,13},{13,9},{2,6},{6,2},{1... | collective-permute-start | bytes 737288 | tf_op jit(solution)/shard_map/ppermute | solution.py:31
  68.2 1.5 %collective-permute-start.25 = (bf16[96,1280]{1,0:T(8,128)(2,1)S(1)}, bf16[96,1280]{1,0:T(8,128)(2,1)S(1)}, u32[]{:S(2)}, u32[]{:S(2)}) collective-permute-start(bf16[96,1280]{1,0:T(8,128)(2,1)S(1)} %collective-permute-done.18.refs_9_), channel_id=1, source_target_pairs={{0,4},{4,0},{8,12},{12,8},{1,5},{5,1},{9,13},{13,9},{2,6},{6,2},{1... | collective-permute-start | bytes 737288 | tf_op jit(solution)/shard_map/ppermute | solution.py:31
  (1 other events, 0.7 us)

commit v12 on v9

--- a/solution.py
+++ b/solution.py
@@ -91,10 +91,17 @@
         ref[...] = all_ref[j]
 
 
-def pack_proj_kernel(proj_ref, all_ref, low_ref, high_ref):
-    half = low_ref.shape[0]
-    for t in range(2 * half):
-        all_ref[t] = pack(proj_ref[t])
+def pack_proj_kernel(proj_ref, out_ref):
+    block = pack(proj_ref[...])
+    rows = block.shape[0]
+    out_ref[:rows, :] = block
+    if out_ref.shape[0] > rows:
+        out_ref[rows:, :] = jnp.zeros((out_ref.shape[0] - rows, block.shape[1]), BF16)
+
+
+def split_proj_kernel(proj_ref, all_ref, low_ref, high_ref):
+    half, rows = low_ref.shape[:2]
+    all_ref[...] = proj_ref[:, :rows, :]
     low_ref[...] = all_ref[:half]
     high_ref[...] = all_ref[half:]
 
@@ -285,7 +292,17 @@
         compiler_params=params(8),
         name="pack",
     )(jnp.transpose(w_qkv, (1, 0, 2)))
-    proj = lax.all_gather(w_proj, "tensor")
+    w_proj, own = together(w_proj, own)
+    spare = 256 if packs(width, col) else 0
+    proj = pl.pallas_call(
+        pack_proj_kernel,
+        out_shape=shape(piece[0] + spare, piece[1]),
+        in_specs=[VMEM],
+        out_specs=VMEM,
+        compiler_params=params(8),
+        name="pack_proj",
+    )(w_proj)
+    proj = lax.all_gather(proj, "tensor")
     query = gather_cross(thirds[0], n_ctx)
     key = gather_cross(thirds[1], n_ctx)
     value = gather_cross(thirds[2], n_ctx)
@@ -318,12 +335,12 @@
     exps, value, proj = together(exps, value, proj)
     value_twin = {k: over_core(value[k]) for k in cross}
     proj, proj_low, proj_high = pl.pallas_call(
-        pack_proj_kernel,
+        split_proj_kernel,
         out_shape=(shape(n_ten, *piece), shape(n_ten // 2, *piece), shape(n_ten // 2, *piece)),
         in_specs=[VMEM],
         out_specs=(VMEM,) * 3,
         compiler_params=params(12),
-        name="pack_proj",
+        name="split_proj",
     )(proj)
     low = gather_cross(proj_low, n_ctx)
     high = gather_cross(proj_high, n_ctx)
@@ -344,10 +361,12 @@
         name="mix",
     )(index, hidden, exps, own, twin, *value_list)
 
+    proj_twin = over_core(proj)
+    mixed, proj_twin = together(mixed, proj_twin)
     received = {s: swap(mixed[s], "tensor", n_ten, s) for s in (2, 3, 1)}
     mixed = [mixed[0]] + [received[s] for s in range(1, n_ten)]
-    proj_twin = over_core(proj)
-    mixed, low, high = together(mixed, low, high)
+    mixed, low, high, place = together(mixed, low, high, place)
+    places = gather_cross(place.reshape(1, groups), n_ctx)
     blocks = [proj, proj_twin]
     for k in cross:
         blocks += [low[k], high[k], over_core(low[k]), over_core(high[k])]
@@ -364,13 +383,12 @@
         name="project",
     )(index, *mixed, *blocks, own_patches, gain_merge)
 
+    done, place_group = together(done, jnp.stack([places[k] for k in (0, *cross)]))
     gathered = []
     for r in range(HALVES):
         crossed = gather_cross(done[r], n_ctx)
         if r == 0:
-            place, crossed[0] = together(place, crossed[0])
-            places = gather_cross(place.reshape(1, groups), n_ctx)
-            place_twin = over_core(jnp.stack([places[k] for k in (0, *cross)]))
+            place_twin = over_core(place_group)
         else:
             for k in cross:
                 crossed[k], gathered[r - 1][k ^ 1], place_twin = together(

time: 85.3 us -> 95.6 us (1.12)
  blocking collectives: 22.4 us -> 0 us
  between operations: 0.1 us -> 13.5 us
  waiting for transfers between devices: 28.3 us -> 38.2 us
  local copies, waits for them, and re-layouts: 3.37 us -> 10.1 us
  Pallas kernels: 13.6 us -> 15.9 us
    all_gather x1 -> x0, blocking collectives: 22.4 us -> none  [local(): proj = lax.all_gather(w_proj, 'tensor')]
    all_gather x0 -> x1, waiting for transfers between devices: none -> 8.68 us  [local(): proj = lax.all_gather(proj, 'tensor')]
    unnamed x14 -> x30, local copies, waits for them, and re-layouts: 3.37 us -> 10.1 us
    ppermute x23, waiting for transfers between devices: 28.3 us -> 29.5 us  [swap(): return lax.ppermute(x, axis, [(i, i ^ bit) for i in range(size)])]
  transfers between devices with their start and end apart: 23 -> 24, of which waited for: 11 -> 10; matrix products, arithmetic and copies ran while one was open for 0% -> 0% of each run, Pallas kernels for 11% -> 11%
where the time goes in v12:
time: 95.6 us; the launch traced here: 95.2 us
  waiting for transfers between devices  38.2 us (40%)
  starting transfers between devices  17.4 us (18%)
  Pallas kernels  15.9 us (17%)
  between operations  13.5 us (14%)
  local copies, waits for them, and re-layouts  10.1 us (11%)
    ppermute x23, waiting for transfers between devices, swap(): return lax.ppermute(x, axis, [(i, i ^ bit) for i in range(size)])  29.5 us
    ppermute x23, starting transfers between devices, swap(): return lax.ppermute(x, axis, [(i, i ^ bit) for i in range(size)])  17.4 us
    unnamed x30, local copies, waits for them, and re-layouts  10.1 us
    all_gather x1, waiting for transfers between devices, local(): proj = lax.all_gather(proj, 'tensor')  8.68 us
    pallas_call x1, Pallas kernels, local(): pl.pallas_call(functools.partial(score_kernel, n_ctx, width), out_shape=s...  4.4 us
    pallas_call x1, Pallas kernels, local(): pl.pallas_call(functools.partial(mix_kernel, n_ctx, width), out_shape=(sh...  4.3 us
    pallas_call x1, Pallas kernels, local(): pl.pallas_call(functools.partial(project_kernel, n_ctx, width, col), out_...  1.96 us
    pallas_call x1, Pallas kernels, local(): pl.pallas_call(functools.partial(place_kernel, n_ctx), out_shape=shape(gr...  1.92 us
  transfers between devices with their start and end apart: 24, of which 10 were waited for; matrix products, arithmetic and copies ran while one was open for 0% of the time, Pallas kernels for 11%

profile of v12, /device:TPU:0, one launch (start us, length us, event | category | flops | bytes accessed | tf_op | source)
XLA Modules:
  0.0 95.2 jit_solution(15754565617791954281)
XLA Ops:
  6.5 1.1 %copy-done.5 = bf16[320,3,320]{2,0,1:T(8,128)(2,1)S(1)} copy-done((bf16[320,3,320]{2,0,1:T(8,128)(2,1)S(1)}, bf16[320,3,320]{2,0,1:T(8,128)(2,1)}, u32[]{:S(2)}) %copy-start.5) | copy-done | bytes 614424
  7.7 0.9 pack.1
  9.2 0.9 copy-done.8
  10.1 0.8 pack_proj.1
  11.5 2.6 %collective-permute-start.1 = (bf16[800,128]{1,0:T(8,128)(2,1)S(1)}, bf16[800,128]{1,0:T(8,128)(2,1)}, u32[]{:S(2)}, u32[]{:S(2)}) collective-permute-start(bf16[800,128]{1,0:T(8,128)(2,1)S(1)} %get-tuple-element.48), channel_id=1, source_target_pairs={{0,8},{4,12},{8,0},{12,4},{1,9},{5,13},{9,1},{13,5},{2,10},{6,14},... | collective-permute-start | bytes 614408 | tf_op jit(solution)/shard_map/ppermute | solution.py:27
  14.2 5.9 %collective-permute-done.1.refs_2_ = bf16[800,128]{1,0:T(8,128)(2,1)} collective-permute-done((bf16[800,128]{1,0:T(8,128)(2,1)S(1)}, bf16[800,128]{1,0:T(8,128)(2,1)}, u32[]{:S(2)}, u32[]{:S(2)}) %collective-permute-start.1) | collective-permute-done | bytes 204832 | tf_op jit(solution)/shard_map/ppermute | solution.py:27
  20.1 1.6 %copy-done.3 = bf16[768,1280]{1,0:T(8,128)(2,1)S(1)} copy-done((bf16[768,1280]{1,0:T(8,128)(2,1)S(1)}, bf16[768,1280]{1,0:T(8,128)(2,1)}, u32[]{:S(2)}) %copy-start.3) | copy-done | bytes 1966104
  22.4 1.6 %norm.1 = (bf16[768,1280]{1,0:T(8,128)(2,1)S(1)}, bf16[192,1280]{1,0:T(8,128)(2,1)S(1)}) custom-call(s32[3]{0:T(128)S(1)} %pad_add_fusion.1.index_ref, bf16[768,1280]{1,0:T(8,128)(2,1)S(1)} %copy-done.3, f32[1280]{0:T(1024)S(1)} %copy-done.9), custom_call_target="tpu_custom_call" | custom-call | tf_op jit(solution)/shard_map/norm/pallas_call | solution.py:311
  24.0 0.8 copy-done.6
  25.3 1.9 %collective-permute-start.5 = (bf16[800,128]{1,0:T(8,128)(2,1)S(1)}, bf16[800,128]{1,0:T(8,128)(2,1)}, u32[]{:S(2)}, u32[]{:S(2)}) collective-permute-start(bf16[800,128]{1,0:T(8,128)(2,1)S(1)} %copy-done.14), channel_id=1, source_target_pairs={{0,8},{4,12},{8,0},{12,4},{1,9},{5,13},{9,1},{13,5},{2,10},{6,14},... | collective-permute-start | bytes 614408 | tf_op jit(solution)/shard_map/ppermute | solution.py:27
  27.3 0.8 copy-done
  28.1 1.1 %copy-done.1 = bf16[3,800,128]{2,1,0:T(8,128)(2,1)S(1)} copy-done((bf16[3,800,128]{2,1,0:T(8,128)(2,1)S(1)}, bf16[3,800,128]{2,1,0:T(8,128)(2,1)}, u32[]{:S(2)}) %copy-start.1) | copy-done | bytes 614424
  29.2 4.4 %scores.1.exps_ref = bf16[768,512]{1,0:T(8,128)(2,1)S(1)} custom-call(s32[3]{0:T(128)S(1)} %pad_add_fusion.1.index_ref, bf16[768,1280]{1,0:T(8,128)(2,1)S(1)} %get-tuple-element.51.hidden_ref, s32[6,128]{1,0:T(8,128)S(1)} %bitcast.19, bf16[3,800,128]{2,1,0:T(8,128)(2,1)S(1)} %get-tuple-element.53.refs_0_, bf16[3,800,128]{2,1,0:T(8,128)(2,1)S(1)} %copy-done.1, ...), custom_call_target="tpu_custom_call" | custom-call | tf_op jit(solution)/shard_map/scores/pallas_call | solution.py:326
  33.6 8.7 %all-gather.3.cloned.1.call-done = bf16[4224,128]{1,0:T(8,128)(2,1)} async-done(((bf16[1056,128]{1,0:T(8,128)(2,1)}), bf16[4224,128]{1,0:T(8,128)(2,1)}) %all-gather.3.cloned.1.call-update) | async-done | bytes 1081360 | tf_op jit(solution)/shard_map/all_gather | solution.py:305
  42.3 1.2 %copy-done.4 = bf16[4224,128]{1,0:T(8,128)(2,1)S(1)} copy-done((bf16[4224,128]{1,0:T(8,128)(2,1)S(1)}, bf16[4224,128]{1,0:T(8,128)(2,1)}, u32[]{:S(2)}) %copy-start.4) | copy-done | bytes 1081368
  43.7 1.5 %collective-permute-start.11 = (bf16[2,800,128]{2,1,0:T(8,128)(2,1)S(1)}, bf16[2,800,128]{2,1,0:T(8,128)(2,1)S(1)}, u32[]{:S(2)}, u32[]{:S(2)}) collective-permute-start(bf16[2,800,128]{2,1,0:T(8,128)(2,1)S(1)} %get-tuple-element.70), channel_id=1, source_target_pairs={{0,8},{4,12},{8,0},{12,4},{1,9},{5,13},{9,1},{13,5},{2,10},{6,14},... | collective-permute-start | bytes 1228808 | tf_op jit(solution)/shard_map/ppermute | solution.py:27
  45.8 1.7 %collective-permute-done.6.refs_3_ = bf16[800,128]{1,0:T(8,128)(2,1)S(1)} collective-permute-done((bf16[800,128]{1,0:T(8,128)(2,1)}, bf16[800,128]{1,0:T(8,128)(2,1)S(1)}, u32[]{:S(2)}, u32[]{:S(2)}) %collective-permute-start.6) | collective-permute-done | bytes 204832 | tf_op jit(solution)/shard_map/ppermute | solution.py:27
  47.5 1.1 %copy-done.2 = bf16[3,800,128]{2,1,0:T(8,128)(2,1)S(1)} copy-done((bf16[3,800,128]{2,1,0:T(8,128)(2,1)S(1)}, bf16[3,800,128]{2,1,0:T(8,128)(2,1)}, u32[]{:S(2)}) %copy-start.2) | copy-done | bytes 614424
  48.5 4.3 %mix.1 = (bf16[480,128]{1,0:T(8,128)(2,1)S(1)}, bf16[480,128]{1,0:T(8,128)(2,1)S(1)}, bf16[480,128]{1,0:T(8,128)(2,1)S(1)}, bf16[480,128]{1,0:T(8,128)(2,1)S(1)}) custom-call(s32[3]{0:T(128)S(1)} %pad_add_fusion.1.index_ref, bf16[768,1280]{1,0:T(8,128)(2,1)S(1)} %get-tuple-element.51.hidden_ref, bf16[768,512]{1,0:T(8,128)(2,1)S(1)} %scores.1.exps_ref, ...), custom_call_target="tpu_custom_call" | custom-call | tf_op jit(solution)/shard_map/mix/pallas_call | solution.py:350
  52.9 1.5 %collective-permute-start.8 = (bf16[480,128]{1,0:T(8,128)(2,1)S(1)}, bf16[480,128]{1,0:T(8,128)(2,1)S(1)}, u32[]{:S(2)}, u32[]{:S(2)}) collective-permute-start(bf16[480,128]{1,0:T(8,128)(2,1)S(1)} %get-tuple-element.67), channel_id=1, source_target_pairs={{0,1},{1,0},{2,3},{3,2},{4,5},{5,4},{6,7},{7,6},{8,9},{9,8},{10,11... | collective-permute-start | bytes 368648 | tf_op jit(solution)/shard_map/ppermute | solution.py:27
  54.4 1.0 %collective-permute-start.9 = (bf16[480,128]{1,0:T(8,128)(2,1)S(1)}, bf16[480,128]{1,0:T(8,128)(2,1)S(1)}, u32[]{:S(2)}, u32[]{:S(2)}) collective-permute-start(bf16[480,128]{1,0:T(8,128)(2,1)S(1)} %get-tuple-element.68), channel_id=1, source_target_pairs={{0,2},{1,3},{2,0},{3,1},{4,6},{5,7},{6,4},{7,5},{8,10},{9,11},{10,... | collective-permute-start | bytes 368648 | tf_op jit(solution)/shard_map/ppermute | solution.py:27
  55.4 1.9 %collective-permute-start.10 = (bf16[480,128]{1,0:T(8,128)(2,1)S(1)}, bf16[480,128]{1,0:T(8,128)(2,1)S(1)}, u32[]{:S(2)}, u32[]{:S(2)}) collective-permute-start(bf16[480,128]{1,0:T(8,128)(2,1)S(1)} %get-tuple-element.69), channel_id=1, source_target_pairs={{0,3},{1,2},{2,1},{3,0},{4,7},{5,6},{6,5},{7,4},{8,11},{9,10},{10,... | collective-permute-start | bytes 368648 | tf_op jit(solution)/shard_map/ppermute | solution.py:27
  57.3 7.0 %collective-permute-done.12.refs_7_ = bf16[2,800,128]{2,1,0:T(8,128)(2,1)S(1)} collective-permute-done((bf16[2,800,128]{2,1,0:T(8,128)(2,1)S(1)}, bf16[2,800,128]{2,1,0:T(8,128)(2,1)S(1)}, u32[]{:S(2)}, u32[]{:S(2)}) %collective-permute-start.12) | collective-permute-done | bytes 409632 | tf_op jit(solution)/shard_map/ppermute | solution.py:27
  64.4 2.4 %collective-permute-done.9.refs_2_ = bf16[480,128]{1,0:T(8,128)(2,1)S(1)} collective-permute-done((bf16[480,128]{1,0:T(8,128)(2,1)S(1)}, bf16[480,128]{1,0:T(8,128)(2,1)S(1)}, u32[]{:S(2)}, u32[]{:S(2)}) %collective-permute-start.9) | collective-permute-done | bytes 122912 | tf_op jit(solution)/shard_map/ppermute | solution.py:27
  67.2 1.5 %collective-permute-start.15 = (s32[1,192]{1,0:T(1,128)S(1)}, s32[1,192]{1,0:T(1,128)S(1)}, u32[]{:S(2)}, u32[]{:S(2)}) collective-permute-start(s32[1,192]{1,0:T(1,128)S(1)} %bitcast.15), channel_id=1, source_target_pairs={{0,8},{4,12},{8,0},{12,4},{1,9},{5,13},{9,1},{13,5},{2,10},{6,14},... | collective-permute-start | bytes 2312 | tf_op jit(solution)/shard_map/ppermute | solution.py:27
  68.7 2.1 %collective-permute-done.15.refs_2_ = s32[1,192]{1,0:T(1,128)S(1)} collective-permute-done((s32[1,192]{1,0:T(1,128)S(1)}, s32[1,192]{1,0:T(1,128)S(1)}, u32[]{:S(2)}, u32[]{:S(2)}) %collective-permute-start.15) | collective-permute-done | bytes 800 | tf_op jit(solution)/shard_map/ppermute | solution.py:27
  70.9 2.0 %project.1 = (bf16[96,1280]{1,0:T(8,128)(2,1)S(1)}, bf16[96,1280]{1,0:T(8,128)(2,1)S(1)}) custom-call(s32[3]{0:T(128)S(1)} %pad_add_fusion.1.index_ref, bf16[480,128]{1,0:T(8,128)(2,1)S(1)} %get-tuple-element.73.refs_0_, bf16[480,128]{1,0:T(8,128)(2,1)S(1)} %collective-permute-done.8.refs_1_, bf16[480,128]{1,0:T(8,128)(2,1)S(1)} %collective-permute-done.9.refs_2_, ...), custom_call_target="tpu_custom_call" | custom-call | tf_op jit(solution)/shard_map/project/pallas_call | solution.py:373
  72.8 1.6 %collective-permute-start.17 = (bf16[96,1280]{1,0:T(8,128)(2,1)S(1)}, bf16[96,1280]{1,0:T(8,128)(2,1)S(1)}, u32[]{:S(2)}, u32[]{:S(2)}) collective-permute-start(bf16[96,1280]{1,0:T(8,128)(2,1)S(1)} %get-tuple-element.84.refs_4_), channel_id=1, source_target_pairs={{0,8},{4,12},{8,0},{12,4},{1,9},{5,13},{9,1},{13,5},{2,10},{6,14},... | collective-permute-start | bytes 737288 | tf_op jit(solution)/shard_map/ppermute | solution.py:27
  74.9 6.9 %collective-permute-done.17.refs_8_ = bf16[96,1280]{1,0:T(8,128)(2,1)S(1)} collective-permute-done((bf16[96,1280]{1,0:T(8,128)(2,1)S(1)}, bf16[96,1280]{1,0:T(8,128)(2,1)S(1)}, u32[]{:S(2)}, u32[]{:S(2)}) %collective-permute-start.17) | collective-permute-done | bytes 245792 | tf_op jit(solution)/shard_map/ppermute | solution.py:27
  83.3 1.6 %collective-permute-done.16.refs_9_ = bf16[96,1280]{1,0:T(8,128)(2,1)S(1)} collective-permute-done((bf16[96,1280]{1,0:T(8,128)(2,1)S(1)}, bf16[96,1280]{1,0:T(8,128)(2,1)S(1)}, u32[]{:S(2)}, u32[]{:S(2)}) %collective-permute-start.16) | collective-permute-done | bytes 245792 | tf_op jit(solution)/shard_map/ppermute | solution.py:27
  84.9 1.5 %collective-permute-done.22.refs_11_ = bf16[96,1280]{1,0:T(8,128)(2,1)S(1)} collective-permute-done((bf16[96,1280]{1,0:T(8,128)(2,1)S(1)}, bf16[96,1280]{1,0:T(8,128)(2,1)S(1)}, u32[]{:S(2)}, u32[]{:S(2)}) %collective-permute-start.22) | collective-permute-done | bytes 245792 | tf_op jit(solution)/shard_map/ppermute | solution.py:27
  86.4 1.9 %placement.1 = bf16[192,1280]{1,0:T(8,128)(2,1)} custom-call(s32[3]{0:T(128)S(1)} %pad_add_fusion.1.index_ref, s32[1,192]{1,0:T(1,128)S(1)} %bitcast.17, s32[1,192]{1,0:T(1,128)S(1)} %get-tuple-element.90.refs_1_, s32[1,192]{1,0:T(1,128)S(1)} %collective-permute-done.15.refs_2_, s32[1,192]{1,0:T(1,128)S(1)} %get-tuple-element.89.refs_3_, ...), custom_call_target="tpu_custom_call" | custom-call | tf_op jit(solution)/shard_map/placement/pallas_call | solution.py:403
  (58 shorter events, 6.0 us)
Async XLA Ops:
  6.5 35.8 %all-gather.3.cloned.1.call-start = ((), (), s32[]{:S(2)}) async-start(), calls=%async_computation | async-start | bytes 1351680 | tf_op jit(solution)/shard_map/all_gather | solution.py:305
  6.5 1.1 %copy-start.5 = (bf16[320,3,320]{2,0,1:T(8,128)(2,1)S(1)}, bf16[320,3,320]{2,0,1:T(8,128)(2,1)}, u32[]{:S(2)}) copy-start(bf16[320,3,320]{2,0,1:T(8,128)(2,1)} %param.11) | copy-start | bytes 1843204
  7.7 20.5 %copy-start.12 = (s32[768]{0:T(1024)S(1)}, s32[768]{0:T(1024)}, u32[]{:S(2)}) copy-start(s32[768]{0:T(1024)} %param.8) | copy-start | bytes 9220
  11.0 16.3 %collective-permute-start.2 = (bf16[3,800,128]{2,1,0:T(8,128)(2,1)S(1)}, bf16[3,800,128]{2,1,0:T(8,128)(2,1)S(1)}, u32[]{:S(2)}, u32[]{:S(2)}) collective-permute-start(bf16[3,800,128]{2,1,0:T(8,128)(2,1)S(1)} %get-tuple-element.53.refs_0_), channel_id=1, source_target_pairs={{0,4},{4,0},{8,12},{12,8},{1,5},{5,1},{9,13},{13,9},{2,6},{6,2},{1... | collective-permute-start | bytes 1843208 | tf_op jit(solution)/shard_map/ppermute | solution.py:27
  11.5 8.6 %collective-permute-start.1 = (bf16[800,128]{1,0:T(8,128)(2,1)S(1)}, bf16[800,128]{1,0:T(8,128)(2,1)}, u32[]{:S(2)}, u32[]{:S(2)}) collective-permute-start(bf16[800,128]{1,0:T(8,128)(2,1)S(1)} %get-tuple-element.48), channel_id=1, source_target_pairs={{0,8},{4,12},{8,0},{12,4},{1,9},{5,13},{9,1},{13,5},{2,10},{6,14},... | collective-permute-start | bytes 614408 | tf_op jit(solution)/shard_map/ppermute | solution.py:27
  14.1 10.7 %collective-permute-start = (bf16[800,128]{1,0:T(8,128)(2,1)}, bf16[800,128]{1,0:T(8,128)(2,1)}, u32[]{:S(2)}, u32[]{:S(2)}) collective-permute-start(bf16[800,128]{1,0:T(8,128)(2,1)} %get-tuple-element.47), channel_id=1, source_target_pairs={{0,8},{4,12},{8,0},{12,4},{1,9},{5,13},{9,1},{13,5},{2,10},{6,14},... | collective-permute-start | bytes 614408 | tf_op jit(solution)/shard_map/ppermute | solution.py:27
  20.1 1.6 %copy-start.3 = (bf16[768,1280]{1,0:T(8,128)(2,1)S(1)}, bf16[768,1280]{1,0:T(8,128)(2,1)}, u32[]{:S(2)}) copy-start(bf16[768,1280]{1,0:T(8,128)(2,1)} %patches_ref) | copy-start | bytes 5898244
  22.4 2.9 %copy-start.14 = (bf16[800,128]{1,0:T(8,128)(2,1)S(1)}, bf16[800,128]{1,0:T(8,128)(2,1)}, u32[]{:S(2)}) copy-start(bf16[800,128]{1,0:T(8,128)(2,1)} %copy-done.13) | copy-start | bytes 614404
  24.8 2.5 %collective-permute-start.3 = (bf16[800,128]{1,0:T(8,128)(2,1)}, bf16[800,128]{1,0:T(8,128)(2,1)S(1)}, u32[]{:S(2)}, u32[]{:S(2)}) collective-permute-start(bf16[800,128]{1,0:T(8,128)(2,1)} %collective-permute-done.1.refs_2_), channel_id=1, source_target_pairs={{0,4},{4,0},{8,12},{12,8},{1,5},{5,1},{9,13},{13,9},{2,6},{6,2},{1... | collective-permute-start | bytes 614408 | tf_op jit(solution)/shard_map/ppermute | solution.py:27
  24.8 2.5 %collective-permute-start.4 = (bf16[800,128]{1,0:T(8,128)(2,1)}, bf16[800,128]{1,0:T(8,128)(2,1)S(1)}, u32[]{:S(2)}, u32[]{:S(2)}) collective-permute-start(bf16[800,128]{1,0:T(8,128)(2,1)} %collective-permute-done.refs_3_), channel_id=1, source_target_pairs={{0,4},{4,0},{8,12},{12,8},{1,5},{5,1},{9,13},{13,9},{2,6},{6,2},{1... | collective-permute-start | bytes 614408 | tf_op jit(solution)/shard_map/ppermute | solution.py:27
  25.3 8.3 %collective-permute-start.5 = (bf16[800,128]{1,0:T(8,128)(2,1)S(1)}, bf16[800,128]{1,0:T(8,128)(2,1)}, u32[]{:S(2)}, u32[]{:S(2)}) collective-permute-start(bf16[800,128]{1,0:T(8,128)(2,1)S(1)} %copy-done.14), channel_id=1, source_target_pairs={{0,8},{4,12},{8,0},{12,4},{1,9},{5,13},{9,1},{13,5},{2,10},{6,14},... | collective-permute-start | bytes 614408 | tf_op jit(solution)/shard_map/ppermute | solution.py:27
  42.3 1.2 %copy-start.4 = (bf16[4224,128]{1,0:T(8,128)(2,1)S(1)}, bf16[4224,128]{1,0:T(8,128)(2,1)}, u32[]{:S(2)}) copy-start(bf16[4224,128]{1,0:T(8,128)(2,1)} %all-gather.3.cloned.1.call-done) | copy-start | bytes 3244036
  43.6 9.2 %collective-permute-start.7 = (bf16[4,800,128]{2,1,0:T(8,128)(2,1)S(1)}, bf16[4,800,128]{2,1,0:T(8,128)(2,1)S(1)}, u32[]{:S(2)}, u32[]{:S(2)}) collective-permute-start(bf16[4,800,128]{2,1,0:T(8,128)(2,1)S(1)} %get-tuple-element.65.refs_4_), channel_id=1, source_target_pairs={{0,4},{4,0},{8,12},{12,8},{1,5},{5,1},{9,13},{13,9},{2,6},{6,2},{1... | collective-permute-start | bytes 2457608 | tf_op jit(solution)/shard_map/ppermute | solution.py:27
  43.7 13.6 %collective-permute-start.11 = (bf16[2,800,128]{2,1,0:T(8,128)(2,1)S(1)}, bf16[2,800,128]{2,1,0:T(8,128)(2,1)S(1)}, u32[]{:S(2)}, u32[]{:S(2)}) collective-permute-start(bf16[2,800,128]{2,1,0:T(8,128)(2,1)S(1)} %get-tuple-element.70), channel_id=1, source_target_pairs={{0,8},{4,12},{8,0},{12,4},{1,9},{5,13},{9,1},{13,5},{2,10},{6,14},... | collective-permute-start | bytes 1228808 | tf_op jit(solution)/shard_map/ppermute | solution.py:27
  45.3 22.0 %copy-start.11 = (s32[192]{0:T(256)S(1)}, s32[192]{0:T(256)}, u32[]{:S(2)}) copy-start(s32[192]{0:T(256)} %param.9) | copy-start | bytes 2308
  45.3 19.1 %collective-permute-start.12 = (bf16[2,800,128]{2,1,0:T(8,128)(2,1)S(1)}, bf16[2,800,128]{2,1,0:T(8,128)(2,1)S(1)}, u32[]{:S(2)}, u32[]{:S(2)}) collective-permute-start(bf16[2,800,128]{2,1,0:T(8,128)(2,1)S(1)} %get-tuple-element.71), channel_id=1, source_target_pairs={{0,8},{4,12},{8,0},{12,4},{1,9},{5,13},{9,1},{13,5},{2,10},{6,14},... | collective-permute-start | bytes 1228808 | tf_op jit(solution)/shard_map/ppermute | solution.py:27
  45.8 1.7 %collective-permute-start.6 = (bf16[800,128]{1,0:T(8,128)(2,1)}, bf16[800,128]{1,0:T(8,128)(2,1)S(1)}, u32[]{:S(2)}, u32[]{:S(2)}) collective-permute-start(bf16[800,128]{1,0:T(8,128)(2,1)} %collective-permute-done.5.refs_2_), channel_id=1, source_target_pairs={{0,4},{4,0},{8,12},{12,8},{1,5},{5,1},{9,13},{13,9},{2,6},{6,2},{1... | collective-permute-start | bytes 614408 | tf_op jit(solution)/shard_map/ppermute | solution.py:27
  48.5 22.3 %copy-start.7 = (bf16[192,1280]{1,0:T(8,128)(2,1)S(1)}, bf16[192,1280]{1,0:T(8,128)(2,1)}, u32[]{:S(2)}) copy-start(bf16[192,1280]{1,0:T(8,128)(2,1)} %copy-done.6) | copy-start | bytes 1474564
  48.5 22.3 %copy-start.10 = (f32[1280]{0:T(1024)S(1)}, f32[1280]{0:T(1024)}, u32[]{:S(2)}) copy-start(f32[1280]{0:T(1024)} %refs_11_.1) | copy-start | bytes 15364
  52.9 11.5 %collective-permute-start.8 = (bf16[480,128]{1,0:T(8,128)(2,1)S(1)}, bf16[480,128]{1,0:T(8,128)(2,1)S(1)}, u32[]{:S(2)}, u32[]{:S(2)}) collective-permute-start(bf16[480,128]{1,0:T(8,128)(2,1)S(1)} %get-tuple-element.67), channel_id=1, source_target_pairs={{0,1},{1,0},{2,3},{3,2},{4,5},{5,4},{6,7},{7,6},{8,9},{9,8},{10,11... | collective-permute-start | bytes 368648 | tf_op jit(solution)/shard_map/ppermute | solution.py:27
  54.4 12.4 %collective-permute-start.9 = (bf16[480,128]{1,0:T(8,128)(2,1)S(1)}, bf16[480,128]{1,0:T(8,128)(2,1)S(1)}, u32[]{:S(2)}, u32[]{:S(2)}) collective-permute-start(bf16[480,128]{1,0:T(8,128)(2,1)S(1)} %get-tuple-element.68), channel_id=1, source_target_pairs={{0,2},{1,3},{2,0},{3,1},{4,6},{5,7},{6,4},{7,5},{8,10},{9,11},{10,... | collective-permute-start | bytes 368648 | tf_op jit(solution)/shard_map/ppermute | solution.py:27
  55.4 11.3 %collective-permute-start.10 = (bf16[480,128]{1,0:T(8,128)(2,1)S(1)}, bf16[480,128]{1,0:T(8,128)(2,1)S(1)}, u32[]{:S(2)}, u32[]{:S(2)}) collective-permute-start(bf16[480,128]{1,0:T(8,128)(2,1)S(1)} %get-tuple-element.69), channel_id=1, source_target_pairs={{0,3},{1,2},{2,1},{3,0},{4,7},{5,6},{6,5},{7,4},{8,11},{9,10},{10,... | collective-permute-start | bytes 368648 | tf_op jit(solution)/shard_map/ppermute | solution.py:27
  66.7 4.1 %collective-permute-start.13 = (bf16[2,800,128]{2,1,0:T(8,128)(2,1)S(1)}, bf16[2,800,128]{2,1,0:T(8,128)(2,1)S(1)}, u32[]{:S(2)}, u32[]{:S(2)}) collective-permute-start(bf16[2,800,128]{2,1,0:T(8,128)(2,1)S(1)} %collective-permute-done.11.refs_6_), channel_id=1, source_target_pairs={{0,4},{4,0},{8,12},{12,8},{1,5},{5,1},{9,13},{13,9},{2,6},{6,2},{1... | collective-permute-start | bytes 1228808 | tf_op jit(solution)/shard_map/ppermute | solution.py:27
  66.7 4.1 %collective-permute-start.14 = (bf16[2,800,128]{2,1,0:T(8,128)(2,1)S(1)}, bf16[2,800,128]{2,1,0:T(8,128)(2,1)S(1)}, u32[]{:S(2)}, u32[]{:S(2)}) collective-permute-start(bf16[2,800,128]{2,1,0:T(8,128)(2,1)S(1)} %collective-permute-done.12.refs_7_), channel_id=1, source_target_pairs={{0,4},{4,0},{8,12},{12,8},{1,5},{5,1},{9,13},{13,9},{2,6},{6,2},{1... | collective-permute-start | bytes 1228808 | tf_op jit(solution)/shard_map/ppermute | solution.py:27
  67.2 3.6 %collective-permute-start.15 = (s32[1,192]{1,0:T(1,128)S(1)}, s32[1,192]{1,0:T(1,128)S(1)}, u32[]{:S(2)}, u32[]{:S(2)}) collective-permute-start(s32[1,192]{1,0:T(1,128)S(1)} %bitcast.15), channel_id=1, source_target_pairs={{0,8},{4,12},{8,0},{12,4},{1,9},{5,13},{9,1},{13,5},{2,10},{6,14},... | collective-permute-start | bytes 2312 | tf_op jit(solution)/shard_map/ppermute | solution.py:27
  72.8 9.0 %collective-permute-start.17 = (bf16[96,1280]{1,0:T(8,128)(2,1)S(1)}, bf16[96,1280]{1,0:T(8,128)(2,1)S(1)}, u32[]{:S(2)}, u32[]{:S(2)}) collective-permute-start(bf16[96,1280]{1,0:T(8,128)(2,1)S(1)} %get-tuple-element.84.refs_4_), channel_id=1, source_target_pairs={{0,8},{4,12},{8,0},{12,4},{1,9},{5,13},{9,1},{13,5},{2,10},{6,14},... | collective-permute-start | bytes 737288 | tf_op jit(solution)/shard_map/ppermute | solution.py:27
  74.4 10.5 %collective-permute-start.16 = (bf16[96,1280]{1,0:T(8,128)(2,1)S(1)}, bf16[96,1280]{1,0:T(8,128)(2,1)S(1)}, u32[]{:S(2)}, u32[]{:S(2)}) collective-permute-start(bf16[96,1280]{1,0:T(8,128)(2,1)S(1)} %get-tuple-element.83.refs_5_), channel_id=1, source_target_pairs={{0,8},{4,12},{8,0},{12,4},{1,9},{5,13},{9,1},{13,5},{2,10},{6,14},... | collective-permute-start | bytes 737288 | tf_op jit(solution)/shard_map/ppermute | solution.py:27
  81.8 3.1 %collective-permute-start.18 = (bf16[96,1280]{1,0:T(8,128)(2,1)S(1)}, bf16[96,1280]{1,0:T(8,128)(2,1)S(1)}, u32[]{:S(2)}, u32[]{:S(2)}) collective-permute-start(bf16[96,1280]{1,0:T(8,128)(2,1)S(1)} %collective-permute-done.17.refs_8_), channel_id=1, source_target_pairs={{0,4},{4,0},{8,12},{12,8},{1,5},{5,1},{9,13},{13,9},{2,6},{6,2},{1... | collective-permute-start | bytes 737288 | tf_op jit(solution)/shard_map/ppermute | solution.py:27
  81.8 1.5 %collective-permute-start.19 = (s32[2,1,192]{2,1,0:T(1,128)S(1)}, s32[2,1,192]{2,1,0:T(1,128)S(1)}, u32[]{:S(2)}, u32[]{:S(2)}) collective-permute-start(s32[2,1,192]{2,1,0:T(1,128)S(1)} %pad_add_fusion), channel_id=1, source_target_pairs={{0,4},{4,0},{8,12},{12,8},{1,5},{5,1},{9,13},{13,9},{2,6},{6,2},{1... | collective-permute-start | bytes 4616 | tf_op jit(solution)/shard_map/ppermute | solution.py:27
  82.3 2.6 %collective-permute-start.20 = (bf16[96,1280]{1,0:T(8,128)(2,1)S(1)}, bf16[96,1280]{1,0:T(8,128)(2,1)S(1)}, u32[]{:S(2)}, u32[]{:S(2)}) collective-permute-start(bf16[96,1280]{1,0:T(8,128)(2,1)S(1)} %get-tuple-element.84.refs_4_), channel_id=1, source_target_pairs={{0,4},{4,0},{8,12},{12,8},{1,5},{5,1},{9,13},{13,9},{2,6},{6,2},{1... | collective-permute-start | bytes 737288 | tf_op jit(solution)/shard_map/ppermute | solution.py:27
  82.3 2.6 %collective-permute-start.21 = (bf16[96,1280]{1,0:T(8,128)(2,1)S(1)}, bf16[96,1280]{1,0:T(8,128)(2,1)S(1)}, u32[]{:S(2)}, u32[]{:S(2)}) collective-permute-start(bf16[96,1280]{1,0:T(8,128)(2,1)S(1)} %get-tuple-element.83.refs_5_), channel_id=1, source_target_pairs={{0,4},{4,0},{8,12},{12,8},{1,5},{5,1},{9,13},{13,9},{2,6},{6,2},{1... | collective-permute-start | bytes 737288 | tf_op jit(solution)/shard_map/ppermute | solution.py:27
  84.9 1.5 %collective-permute-start.22 = (bf16[96,1280]{1,0:T(8,128)(2,1)S(1)}, bf16[96,1280]{1,0:T(8,128)(2,1)S(1)}, u32[]{:S(2)}, u32[]{:S(2)}) collective-permute-start(bf16[96,1280]{1,0:T(8,128)(2,1)S(1)} %collective-permute-done.16.refs_9_), channel_id=1, source_target_pairs={{0,4},{4,0},{8,12},{12,8},{1,5},{5,1},{9,13},{13,9},{2,6},{6,2},{1... | collective-permute-start | bytes 737288 | tf_op jit(solution)/shard_map/ppermute | solution.py:27
  (7 other events, 6.1 us)
Sparse Core Ops, SparseCore 0:
  11.1 31.1 all-gather.2

commit v13 on v8

--- a/solution.py
+++ b/solution.py
@@ -326,11 +326,13 @@
     )(index, hidden, valid.reshape(rows // PAIR, PAIR), *shard_list)
 
     mixed, far, far2, low = together(mixed, far, far2, low)
-    mixed = [mixed[0]] + [swap(mixed[s], "tensor", n_ten, s) for s in range(1, n_ten)]
+    received = {s: swap(mixed[s], "tensor", n_ten, s) for s in (2, 3, 1)}
+    mixed = [mixed[0]] + [received[s] for s in range(1, n_ten)]
     high = gather_cross(jnp.stack([far, far2]), n_ctx)
     blocks = [w_proj, by_one, far, far2, over_core(jnp.stack([w_proj, by_one, far, far2]))]
     low_twin = {k: over_core(low[k]) for k in cross}
-    mixed, high = together(mixed, high)
+    mixed, high, place = together(mixed, high, place)
+    places = gather_cross(place.reshape(1, groups), n_ctx)
     for k in cross:
         blocks += [low[k], high[k], low_twin[k], over_core(high[k])]
     done = pl.pallas_call(
@@ -343,13 +345,12 @@
         name="project",
     )(index, *mixed, *blocks, own_patches, gain_merge)
 
+    done, place_group = together(done, jnp.stack([places[k] for k in (0, *cross)]))
     gathered = []
     for r in range(HALVES):
         crossed = gather_cross(done[r], n_ctx)
         if r == 0:
-            place, crossed[0] = together(place, crossed[0])
-            places = gather_cross(place.reshape(1, groups), n_ctx)
-            place_twin = over_core(jnp.stack([places[k] for k in (0, *cross)]))
+            place_twin = over_core(place_group)
         else:
             for k in cross:
                 crossed[k], gathered[r - 1][k ^ 1], place_twin = together(

time: 66.5 us -> 66.3 us (level)
  transfers between devices with their start and end apart: 26 -> 26, of which waited for: 10 -> 9; matrix products, arithmetic and copies ran while one was open for 0% -> 0% of each run, Pallas kernels for 14% -> 14%
where the time goes in v13:
time: 66.3 us; the launch traced here: 66.1 us
  waiting for transfers between devices  26.6 us (40%)
  starting transfers between devices  21.1 us (32%)
  Pallas kernels  13.7 us (21%)
  local copies, waits for them, and re-layouts  4.32 us (7%)
    ppermute x25, waiting for transfers between devices, swap(): return lax.ppermute(x, axis, [(i, i ^ bit) for i in range(size)])  25.3 us
    ppermute x25, starting transfers between devices, swap(): return lax.ppermute(x, axis, [(i, i ^ bit) for i in range(size)])  18.5 us
    pallas_call x1, Pallas kernels, local(): pl.pallas_call(functools.partial(attention_kernel, n_ctx, width), out_sha...  7.47 us
    unnamed x14, local copies, waits for them, and re-layouts  4.32 us
    ppermute x1, starting transfers between devices, local(): lax.ppermute(w_proj, ('dp', 'tensor'), [(d * n_ten + t, d * n_ten + (t ^...  2.59 us
    pallas_call x1, Pallas kernels, local(): pl.pallas_call(functools.partial(project_kernel, n_ctx, width, col), out_...  1.93 us
    pallas_call x1, Pallas kernels, local(): pl.pallas_call(functools.partial(place_kernel, n_ctx), out_shape=shape(gr...  1.93 us
    pallas_call x1, Pallas kernels, local(): pl.pallas_call(norm_kernel, out_shape=(shape(rows, feat), shape(groups, f...  1.57 us
  transfers between devices with their start and end apart: 26, of which 9 were waited for; matrix products, arithmetic and copies ran while one was open for 0% of the time, Pallas kernels for 14%

profile of v13, /device:TPU:0, one launch (start us, length us, event | category | flops | bytes accessed | tf_op | source)
XLA Modules:
  0.0 66.1 jit_solution(10105109253273269565)
XLA Ops:
  0.1 1.1 %copy-done.1 = bf16[320,3,320]{2,0,1:T(8,128)(2,1)S(1)} copy-done((bf16[320,3,320]{2,0,1:T(8,128)(2,1)S(1)}, bf16[320,3,320]{2,0,1:T(8,128)(2,1)}, u32[]{:S(2)}) %copy-start.1) | copy-done | bytes 614424
  1.2 0.7 %pack.1 = (bf16[800,128]{1,0:T(8,128)(2,1)S(1)}, bf16[800,128]{1,0:T(8,128)(2,1)S(1)}, bf16[3,800,128]{2,1,0:T(8,128)(2,1)S(1)}) custom-call(s32[3]{0:T(128)S(1)} %pad_add_fusion.1.index_ref, bf16[3,320,320]{2,1,0:T(8,128)(2,1)S(1)} %bitcast.24), custom_call_target="tpu_custom_call" | custom-call | tf_op jit(solution)/shard_map/pack/pallas_call | solution.py:261
  1.9 0.5 collective-permute-start.1
  2.4 2.6 %collective-permute-start = (bf16[800,128]{1,0:T(8,128)(2,1)S(1)}, bf16[800,128]{1,0:T(8,128)(2,1)S(1)}, u32[]{:S(2)}, u32[]{:S(2)}) collective-permute-start(bf16[800,128]{1,0:T(8,128)(2,1)S(1)} %get-tuple-element.45), channel_id=1, source_target_pairs={{0,8},{4,12},{8,0},{12,4},{1,9},{5,13},{9,1},{13,5},{2,10},{6,14},... | collective-permute-start | bytes 614408 | tf_op jit(solution)/shard_map/ppermute | solution.py:26
  5.0 0.9 %copy-done.2 = bf16[320,320]{1,0:T(8,128)(2,1)S(1)} copy-done((bf16[320,320]{1,0:T(8,128)(2,1)S(1)}, bf16[320,320]{1,0:T(8,128)(2,1)}, u32[]{:S(2)}) %copy-start.2) | copy-done | bytes 204824
  6.0 1.6 %collective-permute-start.5 = (bf16[800,128]{1,0:T(8,128)(2,1)S(1)}, bf16[800,128]{1,0:T(8,128)(2,1)S(1)}, u32[]{:S(2)}, u32[]{:S(2)}) collective-permute-start(bf16[800,128]{1,0:T(8,128)(2,1)S(1)} %pack_proj.1.refs_4_), channel_id=1, source_target_pairs={{0,1},{1,0},{2,3},{3,2},{4,5},{5,4},{6,7},{7,6},{8,9},{9,8},{10,11... | collective-permute-start | bytes 614408 | tf_op jit(solution)/shard_map/ppermute | solution.py:26
  7.6 2.6 %collective-permute-start.8 = (bf16[800,128]{1,0:T(8,128)(2,1)S(1)}, bf16[800,128]{1,0:T(8,128)(2,1)S(1)}, u32[]{:S(2)}, u32[]{:S(2)}) collective-permute-start(bf16[800,128]{1,0:T(8,128)(2,1)S(1)} %pack_proj.1.refs_4_), channel_id=1, source_target_pairs={{0,2},{1,3},{2,0},{3,1},{16,19},{17,18},{18,17},{19,16},{4,6},{5,7... | collective-permute-start | bytes 614408 | tf_op jit(solution)/shard_map/ppermute | solution.py:280
  10.2 0.5 collective-permute-start.3
  10.7 1.7 %collective-permute-start.2 = (bf16[800,128]{1,0:T(8,128)(2,1)S(1)}, bf16[800,128]{1,0:T(8,128)(2,1)S(1)}, u32[]{:S(2)}, u32[]{:S(2)}) collective-permute-start(bf16[800,128]{1,0:T(8,128)(2,1)S(1)} %collective-permute-done.refs_2_), channel_id=1, source_target_pairs={{0,16},{16,0},{1,17},{17,1},{2,18},{18,2},{3,19},{19,3},{4,20},{20... | collective-permute-start | bytes 614408 | tf_op jit(solution)/shard_map/ppermute | solution.py:26
  12.4 1.5 %copy-done = bf16[768,1280]{1,0:T(8,128)(2,1)S(1)} copy-done((bf16[768,1280]{1,0:T(8,128)(2,1)S(1)}, bf16[768,1280]{1,0:T(8,128)(2,1)}, u32[]{:S(2)}) %copy-start) | copy-done | bytes 1966104
  13.9 0.7 %copy-done.3 = f32[1280]{0:T(1024)S(1)} copy-done((f32[1280]{0:T(1024)S(1)}, f32[1280]{0:T(1024)}, u32[]{:S(2)}) %copy-start.3) | copy-done | bytes 5144
  14.6 1.6 %norm.1 = (bf16[768,1280]{1,0:T(8,128)(2,1)S(1)}, bf16[192,1280]{1,0:T(8,128)(2,1)S(1)}) custom-call(s32[3]{0:T(128)S(1)} %pad_add_fusion.1.index_ref, bf16[768,1280]{1,0:T(8,128)(2,1)S(1)} %copy-done, f32[1280]{0:T(1024)S(1)} %copy-done.3), custom_call_target="tpu_custom_call" | custom-call | tf_op jit(solution)/shard_map/norm/pallas_call | solution.py:294
  16.2 1.3 %collective-permute-done.5.refs_5_ = bf16[800,128]{1,0:T(8,128)(2,1)S(1)} collective-permute-done((bf16[800,128]{1,0:T(8,128)(2,1)S(1)}, bf16[800,128]{1,0:T(8,128)(2,1)S(1)}, u32[]{:S(2)}, u32[]{:S(2)}) %collective-permute-start.5) | collective-permute-done | bytes 204832 | tf_op jit(solution)/shard_map/ppermute | solution.py:26
  17.5 0.4 collective-permute-start.10
  18.5 1.3 %collective-permute-done.8.refs_6_ = bf16[800,128]{1,0:T(8,128)(2,1)S(1)} collective-permute-done((bf16[800,128]{1,0:T(8,128)(2,1)S(1)}, bf16[800,128]{1,0:T(8,128)(2,1)S(1)}, u32[]{:S(2)}, u32[]{:S(2)}) %collective-permute-start.8) | collective-permute-done | bytes 204832 | tf_op jit(solution)/shard_map/ppermute | solution.py:280
  19.8 1.4 %collective-permute-start.9 = (bf16[800,128]{1,0:T(8,128)(2,1)S(1)}, bf16[800,128]{1,0:T(8,128)(2,1)S(1)}, u32[]{:S(2)}, u32[]{:S(2)}) collective-permute-start(bf16[800,128]{1,0:T(8,128)(2,1)S(1)} %collective-permute-done.8.refs_6_), channel_id=1, source_target_pairs={{0,16},{16,0},{1,17},{17,1},{2,18},{18,2},{3,19},{19,3},{4,20},{20... | collective-permute-start | bytes 614408 | tf_op jit(solution)/shard_map/ppermute | solution.py:26
  21.2 7.5 %attention.1 = (bf16[480,128]{1,0:T(8,128)(2,1)S(1)}, bf16[480,128]{1,0:T(8,128)(2,1)S(1)}, bf16[480,128]{1,0:T(8,128)(2,1)S(1)}, bf16[480,128]{1,0:T(8,128)(2,1)S(1)}) custom-call(s32[3]{0:T(128)S(1)} %pad_add_fusion.1.index_ref, bf16[768,1280]{1,0:T(8,128)(2,1)S(1)} %get-tuple-element.52.hidden_ref, s32[6,128]{1,0:T(8,128)S(1)} %bitcast.29, ...), custom_call_target="tpu_custom_call" | custom-call | tf_op jit(solution)/shard_map/attention/pallas_call | solution.py:316
  28.8 1.1 %collective-permute-start.14 = (bf16[2,800,128]{2,1,0:T(8,128)(2,1)S(1)}, bf16[2,800,128]{2,1,0:T(8,128)(2,1)S(1)}, u32[]{:S(2)}, u32[]{:S(2)}) collective-permute-start(bf16[2,800,128]{2,1,0:T(8,128)(2,1)S(1)} %pad_maximum_fusion.2), channel_id=1, source_target_pairs={{0,8},{4,12},{8,0},{12,4},{1,9},{5,13},{9,1},{13,5},{2,10},{6,14},... | collective-permute-start | bytes 1228808 | tf_op jit(solution)/shard_map/ppermute | solution.py:26
  30.0 2.1 %collective-permute-start.11 = (bf16[480,128]{1,0:T(8,128)(2,1)S(1)}, bf16[480,128]{1,0:T(8,128)(2,1)S(1)}, u32[]{:S(2)}, u32[]{:S(2)}) collective-permute-start(bf16[480,128]{1,0:T(8,128)(2,1)S(1)} %get-tuple-element.64), channel_id=1, source_target_pairs={{0,1},{1,0},{2,3},{3,2},{4,5},{5,4},{6,7},{7,6},{8,9},{9,8},{10,11... | collective-permute-start | bytes 368648 | tf_op jit(solution)/shard_map/ppermute | solution.py:26
  32.1 2.6 %collective-permute-start.12 = (bf16[480,128]{1,0:T(8,128)(2,1)S(1)}, bf16[480,128]{1,0:T(8,128)(2,1)S(1)}, u32[]{:S(2)}, u32[]{:S(2)}) collective-permute-start(bf16[480,128]{1,0:T(8,128)(2,1)S(1)} %get-tuple-element.65), channel_id=1, source_target_pairs={{0,2},{1,3},{2,0},{3,1},{4,6},{5,7},{6,4},{7,5},{8,10},{9,11},{10,... | collective-permute-start | bytes 368648 | tf_op jit(solution)/shard_map/ppermute | solution.py:26
  34.7 3.3 %collective-permute-done.11.refs_1_ = bf16[480,128]{1,0:T(8,128)(2,1)S(1)} collective-permute-done((bf16[480,128]{1,0:T(8,128)(2,1)S(1)}, bf16[480,128]{1,0:T(8,128)(2,1)S(1)}, u32[]{:S(2)}, u32[]{:S(2)}) %collective-permute-start.11) | collective-permute-done | bytes 122912 | tf_op jit(solution)/shard_map/ppermute | solution.py:26
  38.0 6.5 %collective-permute-done.12.refs_2_ = bf16[480,128]{1,0:T(8,128)(2,1)S(1)} collective-permute-done((bf16[480,128]{1,0:T(8,128)(2,1)S(1)}, bf16[480,128]{1,0:T(8,128)(2,1)S(1)}, u32[]{:S(2)}, u32[]{:S(2)}) %collective-permute-start.12) | collective-permute-done | bytes 122912 | tf_op jit(solution)/shard_map/ppermute | solution.py:26
  44.9 3.3 %collective-permute-done.18.refs_2_ = s32[1,192]{1,0:T(1,128)S(1)} collective-permute-done((s32[1,192]{1,0:T(1,128)S(1)}, s32[1,192]{1,0:T(1,128)S(1)}, u32[]{:S(2)}, u32[]{:S(2)}) %collective-permute-start.18) | collective-permute-done | bytes 800 | tf_op jit(solution)/shard_map/ppermute | solution.py:26
  48.2 1.9 %project.1 = (bf16[96,1280]{1,0:T(8,128)(2,1)S(1)}, bf16[96,1280]{1,0:T(8,128)(2,1)S(1)}) custom-call(s32[3]{0:T(128)S(1)} %pad_add_fusion.1.index_ref, bf16[480,128]{1,0:T(8,128)(2,1)S(1)} %get-tuple-element.70.refs_0_, bf16[480,128]{1,0:T(8,128)(2,1)S(1)} %collective-permute-done.11.refs_1_, bf16[480,128]{1,0:T(8,128)(2,1)S(1)} %collective-permute-done.12.refs_2_, ...), custom_call_target="tpu_custom_call" | custom-call | tf_op jit(solution)/shard_map/project/pallas_call | solution.py:338
  50.5 1.8 %collective-permute-start.19 = (bf16[96,1280]{1,0:T(8,128)(2,1)S(1)}, bf16[96,1280]{1,0:T(8,128)(2,1)S(1)}, u32[]{:S(2)}, u32[]{:S(2)}) collective-permute-start(bf16[96,1280]{1,0:T(8,128)(2,1)S(1)} %get-tuple-element.79.refs_5_), channel_id=1, source_target_pairs={{0,8},{4,12},{8,0},{12,4},{1,9},{5,13},{9,1},{13,5},{2,10},{6,14},... | collective-permute-start | bytes 737288 | tf_op jit(solution)/shard_map/ppermute | solution.py:26
  52.2 6.9 %collective-permute-done.20.refs_8_ = bf16[96,1280]{1,0:T(8,128)(2,1)S(1)} collective-permute-done((bf16[96,1280]{1,0:T(8,128)(2,1)S(1)}, bf16[96,1280]{1,0:T(8,128)(2,1)S(1)}, u32[]{:S(2)}, u32[]{:S(2)}) %collective-permute-start.20) | collective-permute-done | bytes 245792 | tf_op jit(solution)/shard_map/ppermute | solution.py:26
  59.1 0.5 collective-permute-start.22
  59.6 0.5 collective-permute-start.24
  60.1 0.5 collective-permute-done.22
  60.6 2.0 %collective-permute-done.19.refs_9_ = bf16[96,1280]{1,0:T(8,128)(2,1)S(1)} collective-permute-done((bf16[96,1280]{1,0:T(8,128)(2,1)S(1)}, bf16[96,1280]{1,0:T(8,128)(2,1)S(1)}, u32[]{:S(2)}, u32[]{:S(2)}) %collective-permute-start.19) | collective-permute-done | bytes 245792 | tf_op jit(solution)/shard_map/ppermute | solution.py:26
  62.7 1.5 %collective-permute-done.25.refs_11_ = bf16[96,1280]{1,0:T(8,128)(2,1)S(1)} collective-permute-done((bf16[96,1280]{1,0:T(8,128)(2,1)S(1)}, bf16[96,1280]{1,0:T(8,128)(2,1)S(1)}, u32[]{:S(2)}, u32[]{:S(2)}) %collective-permute-start.25) | collective-permute-done | bytes 245792 | tf_op jit(solution)/shard_map/ppermute | solution.py:26
  64.2 1.9 %placement.1 = bf16[192,1280]{1,0:T(8,128)(2,1)} custom-call(s32[3]{0:T(128)S(1)} %pad_add_fusion.1.index_ref, s32[1,192]{1,0:T(1,128)S(1)} %bitcast.27, s32[1,192]{1,0:T(1,128)S(1)} %get-tuple-element.86.refs_1_, s32[1,192]{1,0:T(1,128)S(1)} %collective-permute-done.18.refs_2_, s32[1,192]{1,0:T(1,128)S(1)} %get-tuple-element.85.refs_3_, ...), custom_call_target="tpu_custom_call" | custom-call | tf_op jit(solution)/shard_map/placement/pallas_call | solution.py:365
  (46 shorter events, 1.7 us)
Async XLA Ops:
  0.1 1.1 %copy-start.1 = (bf16[320,3,320]{2,0,1:T(8,128)(2,1)S(1)}, bf16[320,3,320]{2,0,1:T(8,128)(2,1)}, u32[]{:S(2)}) copy-start(bf16[320,3,320]{2,0,1:T(8,128)(2,1)} %param.11) | copy-start | bytes 1843204
  1.2 20.0 %copy-start.6 = (s32[768]{0:T(1024)S(1)}, s32[768]{0:T(1024)}, u32[]{:S(2)}) copy-start(s32[768]{0:T(1024)} %param.8) | copy-start | bytes 9220
  1.9 8.9 %collective-permute-start.1 = (bf16[3,800,128]{2,1,0:T(8,128)(2,1)S(1)}, bf16[3,800,128]{2,1,0:T(8,128)(2,1)S(1)}, u32[]{:S(2)}, u32[]{:S(2)}) collective-permute-start(bf16[3,800,128]{2,1,0:T(8,128)(2,1)S(1)} %get-tuple-element.46.refs_0_), channel_id=1, source_target_pairs={{0,4},{4,0},{8,12},{12,8},{1,5},{5,1},{9,13},{13,9},{2,6},{6,2},{1... | collective-permute-start | bytes 1843208 | tf_op jit(solution)/shard_map/ppermute | solution.py:26
  2.4 8.3 %collective-permute-start = (bf16[800,128]{1,0:T(8,128)(2,1)S(1)}, bf16[800,128]{1,0:T(8,128)(2,1)S(1)}, u32[]{:S(2)}, u32[]{:S(2)}) collective-permute-start(bf16[800,128]{1,0:T(8,128)(2,1)S(1)} %get-tuple-element.45), channel_id=1, source_target_pairs={{0,8},{4,12},{8,0},{12,4},{1,9},{5,13},{9,1},{13,5},{2,10},{6,14},... | collective-permute-start | bytes 614408 | tf_op jit(solution)/shard_map/ppermute | solution.py:26
  5.0 0.9 %copy-start.2 = (bf16[320,320]{1,0:T(8,128)(2,1)S(1)}, bf16[320,320]{1,0:T(8,128)(2,1)}, u32[]{:S(2)}) copy-start(bf16[320,320]{1,0:T(8,128)(2,1)} %proj_ref.1) | copy-start | bytes 614404
  6.0 11.5 %collective-permute-start.5 = (bf16[800,128]{1,0:T(8,128)(2,1)S(1)}, bf16[800,128]{1,0:T(8,128)(2,1)S(1)}, u32[]{:S(2)}, u32[]{:S(2)}) collective-permute-start(bf16[800,128]{1,0:T(8,128)(2,1)S(1)} %pack_proj.1.refs_4_), channel_id=1, source_target_pairs={{0,1},{1,0},{2,3},{3,2},{4,5},{5,4},{6,7},{7,6},{8,9},{9,8},{10,11... | collective-permute-start | bytes 614408 | tf_op jit(solution)/shard_map/ppermute | solution.py:26
  7.6 12.2 %collective-permute-start.8 = (bf16[800,128]{1,0:T(8,128)(2,1)S(1)}, bf16[800,128]{1,0:T(8,128)(2,1)S(1)}, u32[]{:S(2)}, u32[]{:S(2)}) collective-permute-start(bf16[800,128]{1,0:T(8,128)(2,1)S(1)} %pack_proj.1.refs_4_), channel_id=1, source_target_pairs={{0,2},{1,3},{2,0},{3,1},{16,19},{17,18},{18,17},{19,16},{4,6},{5,7... | collective-permute-start | bytes 614408 | tf_op jit(solution)/shard_map/ppermute | solution.py:280
  10.2 7.7 %collective-permute-start.3 = (bf16[800,128]{1,0:T(8,128)(2,1)S(1)}, bf16[800,128]{1,0:T(8,128)(2,1)S(1)}, u32[]{:S(2)}, u32[]{:S(2)}) collective-permute-start(bf16[800,128]{1,0:T(8,128)(2,1)S(1)} %get-tuple-element.48), channel_id=1, source_target_pairs={{0,8},{4,12},{8,0},{12,4},{1,9},{5,13},{9,1},{13,5},{2,10},{6,14},... | collective-permute-start | bytes 614408 | tf_op jit(solution)/shard_map/ppermute | solution.py:26
  10.7 7.2 %collective-permute-start.2 = (bf16[800,128]{1,0:T(8,128)(2,1)S(1)}, bf16[800,128]{1,0:T(8,128)(2,1)S(1)}, u32[]{:S(2)}, u32[]{:S(2)}) collective-permute-start(bf16[800,128]{1,0:T(8,128)(2,1)S(1)} %collective-permute-done.refs_2_), channel_id=1, source_target_pairs={{0,16},{16,0},{1,17},{17,1},{2,18},{18,2},{3,19},{19,3},{4,20},{20... | collective-permute-start | bytes 614408 | tf_op jit(solution)/shard_map/ppermute | solution.py:26
  12.4 5.6 %collective-permute-start.4 = (bf16[800,128]{1,0:T(8,128)(2,1)S(1)}, bf16[800,128]{1,0:T(8,128)(2,1)S(1)}, u32[]{:S(2)}, u32[]{:S(2)}) collective-permute-start(bf16[800,128]{1,0:T(8,128)(2,1)S(1)} %collective-permute-done.refs_2_), channel_id=1, source_target_pairs={{0,4},{4,0},{8,12},{12,8},{1,5},{5,1},{9,13},{13,9},{2,6},{6,2},{1... | collective-permute-start | bytes 614408 | tf_op jit(solution)/shard_map/ppermute | solution.py:26
  12.4 1.5 %copy-start = (bf16[768,1280]{1,0:T(8,128)(2,1)S(1)}, bf16[768,1280]{1,0:T(8,128)(2,1)}, u32[]{:S(2)}) copy-start(bf16[768,1280]{1,0:T(8,128)(2,1)} %patches_ref) | copy-start | bytes 5898244
  17.5 11.2 %collective-permute-start.10 = (bf16[2,800,128]{2,1,0:T(8,128)(2,1)S(1)}, bf16[2,800,128]{2,1,0:T(8,128)(2,1)S(1)}, u32[]{:S(2)}, u32[]{:S(2)}) collective-permute-start(bf16[2,800,128]{2,1,0:T(8,128)(2,1)S(1)} %pad_maximum_fusion.1), channel_id=1, source_target_pairs={{0,8},{4,12},{8,0},{12,4},{1,9},{5,13},{9,1},{13,5},{2,10},{6,14},... | collective-permute-start | bytes 1228808 | tf_op jit(solution)/shard_map/ppermute | solution.py:26
  18.0 3.3 %collective-permute-start.6 = (bf16[800,128]{1,0:T(8,128)(2,1)S(1)}, bf16[800,128]{1,0:T(8,128)(2,1)S(1)}, u32[]{:S(2)}, u32[]{:S(2)}) collective-permute-start(bf16[800,128]{1,0:T(8,128)(2,1)S(1)} %collective-permute-done.2.refs_3_), channel_id=1, source_target_pairs={{0,4},{4,0},{8,12},{12,8},{1,5},{5,1},{9,13},{13,9},{2,6},{6,2},{1... | collective-permute-start | bytes 614408 | tf_op jit(solution)/shard_map/ppermute | solution.py:26
  18.2 3.1 %collective-permute-start.7 = (bf16[800,128]{1,0:T(8,128)(2,1)S(1)}, bf16[800,128]{1,0:T(8,128)(2,1)S(1)}, u32[]{:S(2)}, u32[]{:S(2)}) collective-permute-start(bf16[800,128]{1,0:T(8,128)(2,1)S(1)} %collective-permute-done.3.refs_4_), channel_id=1, source_target_pairs={{0,4},{4,0},{8,12},{12,8},{1,5},{5,1},{9,13},{13,9},{2,6},{6,2},{1... | collective-permute-start | bytes 614408 | tf_op jit(solution)/shard_map/ppermute | solution.py:26
  19.8 8.9 %collective-permute-start.9 = (bf16[800,128]{1,0:T(8,128)(2,1)S(1)}, bf16[800,128]{1,0:T(8,128)(2,1)S(1)}, u32[]{:S(2)}, u32[]{:S(2)}) collective-permute-start(bf16[800,128]{1,0:T(8,128)(2,1)S(1)} %collective-permute-done.8.refs_6_), channel_id=1, source_target_pairs={{0,16},{16,0},{1,17},{17,1},{2,18},{18,2},{3,19},{19,3},{4,20},{20... | collective-permute-start | bytes 614408 | tf_op jit(solution)/shard_map/ppermute | solution.py:26
  28.7 15.8 %copy-start.5 = (s32[192]{0:T(256)S(1)}, s32[192]{0:T(256)}, u32[]{:S(2)}) copy-start(s32[192]{0:T(256)} %param.9) | copy-start | bytes 2308
  28.7 19.5 %copy-start.4 = (f32[1280]{0:T(1024)S(1)}, f32[1280]{0:T(1024)}, u32[]{:S(2)}) copy-start(f32[1280]{0:T(1024)} %refs_14_.1) | copy-start | bytes 15364
  28.8 15.7 %collective-permute-start.14 = (bf16[2,800,128]{2,1,0:T(8,128)(2,1)S(1)}, bf16[2,800,128]{2,1,0:T(8,128)(2,1)S(1)}, u32[]{:S(2)}, u32[]{:S(2)}) collective-permute-start(bf16[2,800,128]{2,1,0:T(8,128)(2,1)S(1)} %pad_maximum_fusion.2), channel_id=1, source_target_pairs={{0,8},{4,12},{8,0},{12,4},{1,9},{5,13},{9,1},{13,5},{2,10},{6,14},... | collective-permute-start | bytes 1228808 | tf_op jit(solution)/shard_map/ppermute | solution.py:26
  30.0 18.2 %collective-permute-start.15 = (bf16[4,800,128]{2,1,0:T(8,128)(2,1)S(1)}, bf16[4,800,128]{2,1,0:T(8,128)(2,1)S(1)}, u32[]{:S(2)}, u32[]{:S(2)}) collective-permute-start(bf16[4,800,128]{2,1,0:T(8,128)(2,1)S(1)} %pad_maximum_fusion), channel_id=1, source_target_pairs={{0,4},{4,0},{8,12},{12,8},{1,5},{5,1},{9,13},{13,9},{2,6},{6,2},{1... | collective-permute-start | bytes 2457608 | tf_op jit(solution)/shard_map/ppermute | solution.py:26
  30.0 8.0 %collective-permute-start.11 = (bf16[480,128]{1,0:T(8,128)(2,1)S(1)}, bf16[480,128]{1,0:T(8,128)(2,1)S(1)}, u32[]{:S(2)}, u32[]{:S(2)}) collective-permute-start(bf16[480,128]{1,0:T(8,128)(2,1)S(1)} %get-tuple-element.64), channel_id=1, source_target_pairs={{0,1},{1,0},{2,3},{3,2},{4,5},{5,4},{6,7},{7,6},{8,9},{9,8},{10,11... | collective-permute-start | bytes 368648 | tf_op jit(solution)/shard_map/ppermute | solution.py:26
  32.1 12.4 %collective-permute-start.12 = (bf16[480,128]{1,0:T(8,128)(2,1)S(1)}, bf16[480,128]{1,0:T(8,128)(2,1)S(1)}, u32[]{:S(2)}, u32[]{:S(2)}) collective-permute-start(bf16[480,128]{1,0:T(8,128)(2,1)S(1)} %get-tuple-element.65), channel_id=1, source_target_pairs={{0,2},{1,3},{2,0},{3,1},{4,6},{5,7},{6,4},{7,5},{8,10},{9,11},{10,... | collective-permute-start | bytes 368648 | tf_op jit(solution)/shard_map/ppermute | solution.py:26
  34.7 9.8 %collective-permute-start.13 = (bf16[480,128]{1,0:T(8,128)(2,1)S(1)}, bf16[480,128]{1,0:T(8,128)(2,1)S(1)}, u32[]{:S(2)}, u32[]{:S(2)}) collective-permute-start(bf16[480,128]{1,0:T(8,128)(2,1)S(1)} %get-tuple-element.66), channel_id=1, source_target_pairs={{0,3},{1,2},{2,1},{3,0},{4,7},{5,6},{6,5},{7,4},{8,11},{9,10},{10,... | collective-permute-start | bytes 368648 | tf_op jit(solution)/shard_map/ppermute | solution.py:26
  38.0 10.2 %collective-permute-start.16 = (bf16[2,800,128]{2,1,0:T(8,128)(2,1)S(1)}, bf16[2,800,128]{2,1,0:T(8,128)(2,1)S(1)}, u32[]{:S(2)}, u32[]{:S(2)}) collective-permute-start(bf16[2,800,128]{2,1,0:T(8,128)(2,1)S(1)} %collective-permute-done.10.refs_9_), channel_id=1, source_target_pairs={{0,4},{4,0},{8,12},{12,8},{1,5},{5,1},{9,13},{13,9},{2,6},{6,2},{1... | collective-permute-start | bytes 1228808 | tf_op jit(solution)/shard_map/ppermute | solution.py:26
  44.5 3.7 %collective-permute-start.17 = (bf16[2,800,128]{2,1,0:T(8,128)(2,1)S(1)}, bf16[2,800,128]{2,1,0:T(8,128)(2,1)S(1)}, u32[]{:S(2)}, u32[]{:S(2)}) collective-permute-start(bf16[2,800,128]{2,1,0:T(8,128)(2,1)S(1)} %collective-permute-done.14.refs_10_), channel_id=1, source_target_pairs={{0,4},{4,0},{8,12},{12,8},{1,5},{5,1},{9,13},{13,9},{2,6},{6,2},{1... | collective-permute-start | bytes 1228808 | tf_op jit(solution)/shard_map/ppermute | solution.py:26
  44.5 3.6 %collective-permute-start.18 = (s32[1,192]{1,0:T(1,128)S(1)}, s32[1,192]{1,0:T(1,128)S(1)}, u32[]{:S(2)}, u32[]{:S(2)}) collective-permute-start(s32[1,192]{1,0:T(1,128)S(1)} %bitcast.25), channel_id=1, source_target_pairs={{0,8},{4,12},{8,0},{12,4},{1,9},{5,13},{9,1},{13,5},{2,10},{6,14},... | collective-permute-start | bytes 2312 | tf_op jit(solution)/shard_map/ppermute | solution.py:26
  50.1 9.0 %collective-permute-start.20 = (bf16[96,1280]{1,0:T(8,128)(2,1)S(1)}, bf16[96,1280]{1,0:T(8,128)(2,1)S(1)}, u32[]{:S(2)}, u32[]{:S(2)}) collective-permute-start(bf16[96,1280]{1,0:T(8,128)(2,1)S(1)} %get-tuple-element.80.refs_4_), channel_id=1, source_target_pairs={{0,8},{4,12},{8,0},{12,4},{1,9},{5,13},{9,1},{13,5},{2,10},{6,14},... | collective-permute-start | bytes 737288 | tf_op jit(solution)/shard_map/ppermute | solution.py:26
  50.5 12.2 %collective-permute-start.19 = (bf16[96,1280]{1,0:T(8,128)(2,1)S(1)}, bf16[96,1280]{1,0:T(8,128)(2,1)S(1)}, u32[]{:S(2)}, u32[]{:S(2)}) collective-permute-start(bf16[96,1280]{1,0:T(8,128)(2,1)S(1)} %get-tuple-element.79.refs_5_), channel_id=1, source_target_pairs={{0,8},{4,12},{8,0},{12,4},{1,9},{5,13},{9,1},{13,5},{2,10},{6,14},... | collective-permute-start | bytes 737288 | tf_op jit(solution)/shard_map/ppermute | solution.py:26
  59.1 3.5 %collective-permute-start.21 = (bf16[96,1280]{1,0:T(8,128)(2,1)S(1)}, bf16[96,1280]{1,0:T(8,128)(2,1)S(1)}, u32[]{:S(2)}, u32[]{:S(2)}) collective-permute-start(bf16[96,1280]{1,0:T(8,128)(2,1)S(1)} %collective-permute-done.20.refs_8_), channel_id=1, source_target_pairs={{0,4},{4,0},{8,12},{12,8},{1,5},{5,1},{9,13},{13,9},{2,6},{6,2},{1... | collective-permute-start | bytes 737288 | tf_op jit(solution)/shard_map/ppermute | solution.py:26
  59.1 1.5 %collective-permute-start.22 = (s32[2,1,192]{2,1,0:T(1,128)S(1)}, s32[2,1,192]{2,1,0:T(1,128)S(1)}, u32[]{:S(2)}, u32[]{:S(2)}) collective-permute-start(s32[2,1,192]{2,1,0:T(1,128)S(1)} %pad_add_fusion), channel_id=1, source_target_pairs={{0,4},{4,0},{8,12},{12,8},{1,5},{5,1},{9,13},{13,9},{2,6},{6,2},{1... | collective-permute-start | bytes 4616 | tf_op jit(solution)/shard_map/ppermute | solution.py:26
  59.6 3.0 %collective-permute-start.23 = (bf16[96,1280]{1,0:T(8,128)(2,1)S(1)}, bf16[96,1280]{1,0:T(8,128)(2,1)S(1)}, u32[]{:S(2)}, u32[]{:S(2)}) collective-permute-start(bf16[96,1280]{1,0:T(8,128)(2,1)S(1)} %get-tuple-element.80.refs_4_), channel_id=1, source_target_pairs={{0,4},{4,0},{8,12},{12,8},{1,5},{5,1},{9,13},{13,9},{2,6},{6,2},{1... | collective-permute-start | bytes 737288 | tf_op jit(solution)/shard_map/ppermute | solution.py:26
  59.6 3.0 %collective-permute-start.24 = (bf16[96,1280]{1,0:T(8,128)(2,1)S(1)}, bf16[96,1280]{1,0:T(8,128)(2,1)S(1)}, u32[]{:S(2)}, u32[]{:S(2)}) collective-permute-start(bf16[96,1280]{1,0:T(8,128)(2,1)S(1)} %get-tuple-element.79.refs_5_), channel_id=1, source_target_pairs={{0,4},{4,0},{8,12},{12,8},{1,5},{5,1},{9,13},{13,9},{2,6},{6,2},{1... | collective-permute-start | bytes 737288 | tf_op jit(solution)/shard_map/ppermute | solution.py:26
  62.6 1.5 %collective-permute-start.25 = (bf16[96,1280]{1,0:T(8,128)(2,1)S(1)}, bf16[96,1280]{1,0:T(8,128)(2,1)S(1)}, u32[]{:S(2)}, u32[]{:S(2)}) collective-permute-start(bf16[96,1280]{1,0:T(8,128)(2,1)S(1)} %collective-permute-done.19.refs_9_), channel_id=1, source_target_pairs={{0,4},{4,0},{8,12},{12,8},{1,5},{5,1},{9,13},{13,9},{2,6},{6,2},{1... | collective-permute-start | bytes 737288 | tf_op jit(solution)/shard_map/ppermute | solution.py:26
  (1 other events, 0.7 us)

commit v14 on v13

--- a/solution.py
+++ b/solution.py
@@ -20,6 +20,10 @@
 
 def params(mib):
     return pltpu.CompilerParams(vmem_limit_bytes=mib * 1024 * 1024)
+
+
+def cost(us):
+    return pl.CostEstimate(flops=0, bytes_accessed=int(us * 3.3e6), transcendentals=0)
 
 
 def swap(x, axis, size, bit):
@@ -113,12 +117,12 @@
         ).astype(BF16)
 
 
-def attend(index_ref, hidden_ref, valid_ref, w_ref, out_refs, q_ref, k_ref, v_ref, mix_ref):
+def attend(row0, index_ref, hidden_ref, valid_ref, w_ref, out_refs, q_ref, k_ref, v_ref, mix_ref):
     rows, width = q_ref.shape
     heads = width // HD
     main = 2 * LANES
     rest = width - main
-    qkv = jnp.dot(hidden_ref[...], w_ref[...], preferred_element_type=F32)
+    qkv = jnp.dot(hidden_ref[row0 : row0 + rows, :], w_ref[...], preferred_element_type=F32)
     for j, ref in enumerate((q_ref, k_ref, v_ref)):
         ref[:, :main] = qkv[:, j * main : (j + 1) * main].astype(BF16)
         at = 3 * main + j * rest
@@ -141,7 +145,7 @@
         k_all = jnp.concatenate([k * m for m in head_masks], axis=0)
         v_all = jnp.concatenate([v * m for m in head_masks], axis=0)
         scores = lax.dot_general(q, k_all, (((1,), (1,)), ((), ())), preferred_element_type=F32)
-        live = valid_ref[p : p + 1, :] > 0
+        live = valid_ref[row0 // PAIR + p : row0 // PAIR + p + 1, :] > 0
         weights = []
         for h in range(heads):
             s = scores[:, h * PAIR : (h + 1) * PAIR] * F32(HD ** (-0.5))
@@ -157,7 +161,7 @@
         out_ref[...] = pack(mix_ref[index_ref[1] ^ s])
 
 
-def attention_kernel(n_ctx, width, index_ref, hidden_ref, valid_ref, *refs):
+def first_attention_kernel(n_ctx, width, index_ref, hidden_ref, valid_ref, *refs):
     shards = list(refs[: 2 + 3 * (n_ctx - 2)])
     *out_refs, w_ref, q_ref, k_ref, v_ref, mix_ref = refs[len(shards) :]
     depth = w_ref.shape[0] // n_ctx
@@ -177,14 +181,26 @@
             w_ref[rows, j * main : (j + 1) * main], tail = unpack(third, depth, width)
             tails.append(tail)
         w_ref[rows, 3 * main :] = jnp.concatenate(tails, axis=1)
-    attend(index_ref, hidden_ref, valid_ref, w_ref, out_refs, q_ref, k_ref, v_ref, mix_ref)
+    attend(0, index_ref, hidden_ref, valid_ref, w_ref, out_refs, q_ref, k_ref, v_ref, mix_ref)
+
+
+def next_attention_kernel(row0, index_ref, hidden_ref, valid_ref, w_ref, before_ref, *refs):
+    *out_refs, q_ref, k_ref, v_ref, mix_ref = refs
+    out_refs[1][0] = before_ref[...]
+    out_refs[1] = out_refs[1].at[1]
+    attend(row0, index_ref, hidden_ref, valid_ref, w_ref, out_refs, q_ref, k_ref, v_ref, mix_ref)
 
 
 def project_kernel(n_ctx, width, col, index_ref, *refs):
-    *blocks, own_ref, gain_ref = refs[4 : -HALVES - 1]
+    *blocks, own_ref, gain_ref = refs[7 : -HALVES - 1]
     *out_refs, part_ref = refs[-HALVES - 1 :]
     rows = own_ref.shape[0]
-    mixes = [unpack(m[...], rows, width) for m in refs[:4]]
+    halves = [refs[0][...], refs[1][...], refs[2][0], refs[2][1]] + [ref[...] for ref in refs[3:7]]
+    halves = [unpack(half, rows // 2, width) for half in halves]
+    mixes = [
+        [jnp.concatenate([a, b], axis=0) for a, b in zip(halves[2 * s], halves[2 * s + 1])]
+        for s in range(4)
+    ]
     flip = index_ref[2] > 0
     mixes[2:] = [
         [jnp.where(flip, b, a) for a, b in zip(mixes[2], mixes[3])],
@@ -312,24 +328,39 @@
     for k in cross:
         shard_list += [first[k], second[k], value[k], first_twin[k], second_twin[k], value_twin[k]]
 
-    mix_shapes = (shape(*packed_shape(groups, width)),) * n_ten
-    mixed = pl.pallas_call(
-        functools.partial(attention_kernel, n_ctx, width),
-        out_shape=mix_shapes,
+    valid_pairs = valid.reshape(rows // PAIR, PAIR)
+    part = rows // HALVES
+    mix_shape = shape(*packed_shape(part // 4, width))
+    scratch = [pltpu.VMEM((part, width), BF16)] * 3 + [pltpu.VMEM((4, part // 4, width), BF16)]
+    *mixed, w_full = pl.pallas_call(
+        functools.partial(first_attention_kernel, n_ctx, width),
+        out_shape=(mix_shape,) * n_ten + (shape(feat, 3 * width),),
         in_specs=[SMEM] + [VMEM] * (2 + len(shard_list)),
+        out_specs=(VMEM,) * (n_ten + 1),
+        scratch_shapes=scratch,
+        compiler_params=params(16),
+        name="attention0",
+    )(index, hidden, valid_pairs, *shard_list)
+
+    mixed, far, far2, low = together(mixed, far, far2, low)
+    early = [swap(mixed[s], "tensor", n_ten, s) for s in (2, 3)]
+    later = pl.pallas_call(
+        functools.partial(next_attention_kernel, part),
+        out_shape=(mix_shape, shape(2, *mix_shape.shape), mix_shape, mix_shape),
+        in_specs=[SMEM] + [VMEM] * 4,
         out_specs=(VMEM,) * n_ten,
-        scratch_shapes=[pltpu.VMEM((feat, 3 * width), BF16)]
-        + [pltpu.VMEM((rows, width), BF16)] * 3
-        + [pltpu.VMEM((4, groups, width), BF16)],
-        compiler_params=params(20),
-        name="attention",
-    )(index, hidden, valid.reshape(rows // PAIR, PAIR), *shard_list)
-
-    mixed, far, far2, low = together(mixed, far, far2, low)
-    received = {s: swap(mixed[s], "tensor", n_ten, s) for s in (2, 3, 1)}
-    mixed = [mixed[0]] + [received[s] for s in range(1, n_ten)]
+        scratch_shapes=scratch,
+        compiler_params=params(16),
+        cost_estimate=cost(1000),
+        name="attention1",
+    )(index, hidden, valid_pairs, w_full, mixed[1])
     high = gather_cross(jnp.stack([far, far2]), n_ctx)
-    blocks = [w_proj, by_one, far, far2, over_core(jnp.stack([w_proj, by_one, far, far2]))]
+    own_twin = over_core(jnp.stack([w_proj, by_one, far, far2]))
+    later, early, own_twin = together(later, early, own_twin)
+    late = [swap(later[s], "tensor", n_ten, s) for s in (2, 3)]
+    mixed = [mixed[0], later[0], swap(later[1], "tensor", n_ten, 1)]
+    mixed += [early[0], late[0], early[1], late[1]]
+    blocks = [w_proj, by_one, far, far2, own_twin]
     low_twin = {k: over_core(low[k]) for k in cross}
     mixed, high, place = together(mixed, high, place)
     places = gather_cross(place.reshape(1, groups), n_ctx)
@@ -338,7 +369,7 @@
     done = pl.pallas_call(
         functools.partial(project_kernel, n_ctx, width, col),
         out_shape=(shape(groups // HALVES, feat),) * HALVES,
-        in_specs=[SMEM] + [VMEM] * (n_ten + len(blocks) + 2),
+        in_specs=[SMEM] + [VMEM] * (len(mixed) + len(blocks) + 2),
         out_specs=(VMEM,) * HALVES,
         scratch_shapes=[pltpu.VMEM((n_ctx, groups, col), F32)],
         compiler_params=params(24),

time: 66.3 us -> 71.2 us (1.074)
  starting transfers between devices: 21.1 us -> 25.9 us
  waiting for transfers between devices: 26.6 us -> 25.7 us
  Pallas kernels: 13.7 us -> 14.6 us
    ppermute x25 -> x27, starting transfers between devices: 18.5 us -> 23.3 us  [swap(): return lax.ppermute(x, axis, [(i, i ^ bit) for i in range(size)])]
    pallas_call x1 -> x2, Pallas kernels: 7.47 us -> 8.47 us  [the longest x1 4.52 us: local(): pl.pallas_call(functools.partial(first_attention_kernel, n_ctx, width), o...]
    ppermute x25 -> x27, waiting for transfers between devices: 25.3 us -> 24.4 us  [swap(): return lax.ppermute(x, axis, [(i, i ^ bit) for i in range(size)])]
  transfers between devices with their start and end apart: 26 -> 28, of which waited for: 9 -> 11; matrix products, arithmetic and copies ran while one was open for 0% -> 0% of each run, Pallas kernels for 14% -> 14%
where the time goes in v14:
time: 71.2 us; the launch traced here: 71 us
  starting transfers between devices  25.9 us (36%)
  waiting for transfers between devices  25.7 us (36%)
  Pallas kernels  14.6 us (21%)
  local copies, waits for them, and re-layouts  4.31 us (6%)
    ppermute x27, waiting for transfers between devices, swap(): return lax.ppermute(x, axis, [(i, i ^ bit) for i in range(size)])  24.4 us
    ppermute x27, starting transfers between devices, swap(): return lax.ppermute(x, axis, [(i, i ^ bit) for i in range(size)])  23.3 us
    pallas_call x1, Pallas kernels, local(): pl.pallas_call(functools.partial(first_attention_kernel, n_ctx, width), o...  4.52 us
    unnamed x14, local copies, waits for them, and re-layouts  4.31 us
    pallas_call x1, Pallas kernels, local(): pl.pallas_call(functools.partial(next_attention_kernel, part), out_shape=...  3.96 us
    ppermute x1, starting transfers between devices, local(): lax.ppermute(w_proj, ('dp', 'tensor'), [(d * n_ten + t, d * n_ten + (t ^...  2.59 us
    pallas_call x1, Pallas kernels, local(): pl.pallas_call(functools.partial(place_kernel, n_ctx), out_shape=shape(gr...  1.93 us
    pallas_call x1, Pallas kernels, local(): pl.pallas_call(functools.partial(project_kernel, n_ctx, width, col), out_...  1.92 us
  transfers between devices with their start and end apart: 28, of which 11 were waited for; matrix products, arithmetic and copies ran while one was open for 0% of the time, Pallas kernels for 14%

profile of v14, /device:TPU:0, one launch (start us, length us, event | category | flops | bytes accessed | tf_op | source)
XLA Modules:
  0.0 71.0 jit_solution(9741888816346425961)
XLA Ops:
  0.1 1.1 %copy-done.1 = bf16[320,3,320]{2,0,1:T(8,128)(2,1)S(1)} copy-done((bf16[320,3,320]{2,0,1:T(8,128)(2,1)S(1)}, bf16[320,3,320]{2,0,1:T(8,128)(2,1)}, u32[]{:S(2)}) %copy-start.1) | copy-done | bytes 614424
  1.2 0.7 pack.1
  2.4 2.6 %collective-permute-start = (bf16[800,128]{1,0:T(8,128)(2,1)S(1)}, bf16[800,128]{1,0:T(8,128)(2,1)S(1)}, u32[]{:S(2)}, u32[]{:S(2)}) collective-permute-start(bf16[800,128]{1,0:T(8,128)(2,1)S(1)} %get-tuple-element.60), channel_id=1, source_target_pairs={{0,8},{4,12},{8,0},{12,4},{1,9},{5,13},{9,1},{13,5},{2,10},{6,14},... | collective-permute-start | bytes 614408 | tf_op jit(solution)/shard_map/ppermute | solution.py:30
  5.0 0.9 %copy-done.2 = bf16[320,320]{1,0:T(8,128)(2,1)S(1)} copy-done((bf16[320,320]{1,0:T(8,128)(2,1)S(1)}, bf16[320,320]{1,0:T(8,128)(2,1)}, u32[]{:S(2)}) %copy-start.2) | copy-done | bytes 204824
  6.0 1.6 %collective-permute-start.5 = (bf16[800,128]{1,0:T(8,128)(2,1)S(1)}, bf16[800,128]{1,0:T(8,128)(2,1)S(1)}, u32[]{:S(2)}, u32[]{:S(2)}) collective-permute-start(bf16[800,128]{1,0:T(8,128)(2,1)S(1)} %pack_proj.1.refs_7_), channel_id=1, source_target_pairs={{0,1},{1,0},{2,3},{3,2},{4,5},{5,4},{6,7},{7,6},{8,9},{9,8},{10,11... | collective-permute-start | bytes 614408 | tf_op jit(solution)/shard_map/ppermute | solution.py:30
  7.6 2.6 %collective-permute-start.8 = (bf16[800,128]{1,0:T(8,128)(2,1)S(1)}, bf16[800,128]{1,0:T(8,128)(2,1)S(1)}, u32[]{:S(2)}, u32[]{:S(2)}) collective-permute-start(bf16[800,128]{1,0:T(8,128)(2,1)S(1)} %pack_proj.1.refs_7_), channel_id=1, source_target_pairs={{0,2},{1,3},{2,0},{3,1},{16,19},{17,18},{18,17},{19,16},{4,6},{5,7... | collective-permute-start | bytes 614408 | tf_op jit(solution)/shard_map/ppermute | solution.py:296
  10.7 1.7 %collective-permute-start.2 = (bf16[800,128]{1,0:T(8,128)(2,1)S(1)}, bf16[800,128]{1,0:T(8,128)(2,1)S(1)}, u32[]{:S(2)}, u32[]{:S(2)}) collective-permute-start(bf16[800,128]{1,0:T(8,128)(2,1)S(1)} %collective-permute-done.refs_2_), channel_id=1, source_target_pairs={{0,16},{16,0},{1,17},{17,1},{2,18},{18,2},{3,19},{19,3},{4,20},{20... | collective-permute-start | bytes 614408 | tf_op jit(solution)/shard_map/ppermute | solution.py:30
  12.4 1.5 %copy-done = bf16[768,1280]{1,0:T(8,128)(2,1)S(1)} copy-done((bf16[768,1280]{1,0:T(8,128)(2,1)S(1)}, bf16[768,1280]{1,0:T(8,128)(2,1)}, u32[]{:S(2)}) %copy-start) | copy-done | bytes 1966104
  13.9 0.7 copy-done.4
  14.6 1.6 %norm.1 = (bf16[768,1280]{1,0:T(8,128)(2,1)S(1)}, bf16[192,1280]{1,0:T(8,128)(2,1)S(1)}) custom-call(s32[3]{0:T(128)S(1)} %pad_add_fusion.1.index_ref, bf16[768,1280]{1,0:T(8,128)(2,1)S(1)} %copy-done, f32[1280]{0:T(1024)S(1)} %copy-done.4), custom_call_target="tpu_custom_call" | custom-call | tf_op jit(solution)/shard_map/norm/pallas_call | solution.py:310
  16.2 1.3 %collective-permute-done.5.refs_8_ = bf16[800,128]{1,0:T(8,128)(2,1)S(1)} collective-permute-done((bf16[800,128]{1,0:T(8,128)(2,1)S(1)}, bf16[800,128]{1,0:T(8,128)(2,1)S(1)}, u32[]{:S(2)}, u32[]{:S(2)}) %collective-permute-start.5) | collective-permute-done | bytes 204832 | tf_op jit(solution)/shard_map/ppermute | solution.py:30
  18.5 1.3 %collective-permute-done.8.refs_9_ = bf16[800,128]{1,0:T(8,128)(2,1)S(1)} collective-permute-done((bf16[800,128]{1,0:T(8,128)(2,1)S(1)}, bf16[800,128]{1,0:T(8,128)(2,1)S(1)}, u32[]{:S(2)}, u32[]{:S(2)}) %collective-permute-start.8) | collective-permute-done | bytes 204832 | tf_op jit(solution)/shard_map/ppermute | solution.py:296
  19.8 1.4 %collective-permute-start.9 = (bf16[800,128]{1,0:T(8,128)(2,1)S(1)}, bf16[800,128]{1,0:T(8,128)(2,1)S(1)}, u32[]{:S(2)}, u32[]{:S(2)}) collective-permute-start(bf16[800,128]{1,0:T(8,128)(2,1)S(1)} %collective-permute-done.8.refs_9_), channel_id=1, source_target_pairs={{0,16},{16,0},{1,17},{17,1},{2,18},{18,2},{3,19},{19,3},{4,20},{20... | collective-permute-start | bytes 614408 | tf_op jit(solution)/shard_map/ppermute | solution.py:30
  21.2 4.5 %attention0.1 = (bf16[240,128]{1,0:T(8,128)(2,1)S(1)}, bf16[240,128]{1,0:T(8,128)(2,1)S(1)}, bf16[240,128]{1,0:T(8,128)(2,1)S(1)}, bf16[240,128]{1,0:T(8,128)(2,1)S(1)}, bf16[1280,960]{1,0:T(8,128)(2,1)S(1)}) custom-call(s32[3]{0:T(128)S(1)} %pad_add_fusion.1.index_ref, bf16[768,1280]{1,0:T(8,128)(2,1)S(1)} %get-tuple-element.67.hidden_ref, ...), custom_call_target="tpu_custom_call" | custom-call | tf_op jit(solution)/shard_map/attention0/pallas_call | solution.py:335
  25.8 2.5 %collective-permute-done.10.refs_12_ = bf16[2,800,128]{2,1,0:T(8,128)(2,1)S(1)} collective-permute-done((bf16[2,800,128]{2,1,0:T(8,128)(2,1)S(1)}, bf16[2,800,128]{2,1,0:T(8,128)(2,1)S(1)}, u32[]{:S(2)}, u32[]{:S(2)}) %collective-permute-start.10) | collective-permute-done | bytes 409632 | tf_op jit(solution)/shard_map/ppermute | solution.py:30
  28.5 1.5 %collective-permute-start.17 = (bf16[2,800,128]{2,1,0:T(8,128)(2,1)S(1)}, bf16[2,800,128]{2,1,0:T(8,128)(2,1)S(1)}, u32[]{:S(2)}, u32[]{:S(2)}) collective-permute-start(bf16[2,800,128]{2,1,0:T(8,128)(2,1)S(1)} %pad_maximum_fusion.2), channel_id=1, source_target_pairs={{0,8},{4,12},{8,0},{12,4},{1,9},{5,13},{9,1},{13,5},{2,10},{6,14},... | collective-permute-start | bytes 1228808 | tf_op jit(solution)/shard_map/ppermute | solution.py:30
  30.1 3.0 %collective-permute-start.11 = (bf16[240,128]{1,0:T(8,128)(2,1)S(1)}, bf16[240,128]{1,0:T(8,128)(2,1)S(1)}, u32[]{:S(2)}, u32[]{:S(2)}) collective-permute-start(bf16[240,128]{1,0:T(8,128)(2,1)S(1)} %get-tuple-element.85), channel_id=1, source_target_pairs={{0,2},{1,3},{2,0},{3,1},{4,6},{5,7},{6,4},{7,5},{8,10},{9,11},{10,... | collective-permute-start | bytes 184328 | tf_op jit(solution)/shard_map/ppermute | solution.py:30
  33.1 1.3 %collective-permute-start.12 = (bf16[240,128]{1,0:T(8,128)(2,1)S(1)}, bf16[240,128]{1,0:T(8,128)(2,1)S(1)}, u32[]{:S(2)}, u32[]{:S(2)}) collective-permute-start(bf16[240,128]{1,0:T(8,128)(2,1)S(1)} %get-tuple-element.86), channel_id=1, source_target_pairs={{0,3},{1,2},{2,1},{3,0},{4,7},{5,6},{6,5},{7,4},{8,11},{9,10},{10,... | collective-permute-start | bytes 184328 | tf_op jit(solution)/shard_map/ppermute | solution.py:30
  34.4 4.0 %attention1.1 = (bf16[240,128]{1,0:T(8,128)(2,1)S(1)}, bf16[2,240,128]{2,1,0:T(8,128)(2,1)S(1)}, bf16[240,128]{1,0:T(8,128)(2,1)S(1)}, bf16[240,128]{1,0:T(8,128)(2,1)S(1)}) custom-call(s32[3]{0:T(128)S(1)} %pad_add_fusion.1.index_ref, bf16[768,1280]{1,0:T(8,128)(2,1)S(1)} %get-tuple-element.67.hidden_ref, s32[6,128]{1,0:T(8,128)S(1)} %bitcast.26, ...), custom_call_target="tpu_custom_call" | custom-call | bytes 3300000000 | tf_op jit(solution)/shard_map/attention1/pallas_call | solution.py:347
  38.4 0.8 %collective-permute-done.12.refs_5_ = bf16[240,128]{1,0:T(8,128)(2,1)S(1)} collective-permute-done((bf16[240,128]{1,0:T(8,128)(2,1)S(1)}, bf16[240,128]{1,0:T(8,128)(2,1)S(1)}, u32[]{:S(2)}, u32[]{:S(2)}) %collective-permute-start.12) | collective-permute-done | bytes 61472 | tf_op jit(solution)/shard_map/ppermute | solution.py:30
  39.2 1.0 %collective-permute-start.14 = (bf16[2,240,128]{2,1,0:T(8,128)(2,1)S(1)}, bf16[2,240,128]{2,1,0:T(8,128)(2,1)S(1)}, u32[]{:S(2)}, u32[]{:S(2)}) collective-permute-start(bf16[2,240,128]{2,1,0:T(8,128)(2,1)S(1)} %get-tuple-element.90), channel_id=1, source_target_pairs={{0,1},{1,0},{2,3},{3,2},{4,5},{5,4},{6,7},{7,6},{8,9},{9,8},{10,11... | collective-permute-start | bytes 368648 | tf_op jit(solution)/shard_map/ppermute | solution.py:30
  40.1 2.2 %collective-permute-start.15 = (bf16[240,128]{1,0:T(8,128)(2,1)S(1)}, bf16[240,128]{1,0:T(8,128)(2,1)S(1)}, u32[]{:S(2)}, u32[]{:S(2)}) collective-permute-start(bf16[240,128]{1,0:T(8,128)(2,1)S(1)} %get-tuple-element.92), channel_id=1, source_target_pairs={{0,2},{1,3},{2,0},{3,1},{4,6},{5,7},{6,4},{7,5},{8,10},{9,11},{10,... | collective-permute-start | bytes 184328 | tf_op jit(solution)/shard_map/ppermute | solution.py:30
  42.3 1.2 %collective-permute-start.16 = (bf16[240,128]{1,0:T(8,128)(2,1)S(1)}, bf16[240,128]{1,0:T(8,128)(2,1)S(1)}, u32[]{:S(2)}, u32[]{:S(2)}) collective-permute-start(bf16[240,128]{1,0:T(8,128)(2,1)S(1)} %get-tuple-element.94), channel_id=1, source_target_pairs={{0,3},{1,2},{2,1},{3,0},{4,7},{5,6},{6,5},{7,4},{8,11},{9,10},{10,... | collective-permute-start | bytes 184328 | tf_op jit(solution)/shard_map/ppermute | solution.py:30
  43.6 1.8 %collective-permute-done.15.refs_4_ = bf16[240,128]{1,0:T(8,128)(2,1)S(1)} collective-permute-done((bf16[240,128]{1,0:T(8,128)(2,1)S(1)}, bf16[240,128]{1,0:T(8,128)(2,1)S(1)}, u32[]{:S(2)}, u32[]{:S(2)}) %collective-permute-start.15) | collective-permute-done | bytes 61472 | tf_op jit(solution)/shard_map/ppermute | solution.py:30
  45.4 4.1 %collective-permute-done.16.refs_6_ = bf16[240,128]{1,0:T(8,128)(2,1)S(1)} collective-permute-done((bf16[240,128]{1,0:T(8,128)(2,1)S(1)}, bf16[240,128]{1,0:T(8,128)(2,1)S(1)}, u32[]{:S(2)}, u32[]{:S(2)}) %collective-permute-start.16) | collective-permute-done | bytes 61472 | tf_op jit(solution)/shard_map/ppermute | solution.py:30
  50.0 3.1 %collective-permute-done.20.refs_2_ = s32[1,192]{1,0:T(1,128)S(1)} collective-permute-done((s32[1,192]{1,0:T(1,128)S(1)}, s32[1,192]{1,0:T(1,128)S(1)}, u32[]{:S(2)}, u32[]{:S(2)}) %collective-permute-start.20) | collective-permute-done | bytes 800 | tf_op jit(solution)/shard_map/ppermute | solution.py:30
  53.1 1.9 %project.1 = (bf16[96,1280]{1,0:T(8,128)(2,1)S(1)}, bf16[96,1280]{1,0:T(8,128)(2,1)S(1)}) custom-call(s32[3]{0:T(128)S(1)} %pad_add_fusion.1.index_ref, bf16[240,128]{1,0:T(8,128)(2,1)S(1)} %get-tuple-element.96.refs_0_, bf16[240,128]{1,0:T(8,128)(2,1)S(1)} %get-tuple-element.97.refs_1_, bf16[2,240,128]{2,1,0:T(8,128)(2,1)S(1)} %collective-permute-done.14.refs_2_, ...), custom_call_target="tpu_custom_call" | custom-call | tf_op jit(solution)/shard_map/project/pallas_call | solution.py:369
  55.6 1.5 %collective-permute-start.21 = (bf16[96,1280]{1,0:T(8,128)(2,1)S(1)}, bf16[96,1280]{1,0:T(8,128)(2,1)S(1)}, u32[]{:S(2)}, u32[]{:S(2)}) collective-permute-start(bf16[96,1280]{1,0:T(8,128)(2,1)S(1)} %get-tuple-element.109.refs_5_), channel_id=1, source_target_pairs={{0,8},{4,12},{8,0},{12,4},{1,9},{5,13},{9,1},{13,5},{2,10},{6,14},... | collective-permute-start | bytes 737288 | tf_op jit(solution)/shard_map/ppermute | solution.py:30
  57.2 6.9 %collective-permute-done.22.refs_8_ = bf16[96,1280]{1,0:T(8,128)(2,1)S(1)} collective-permute-done((bf16[96,1280]{1,0:T(8,128)(2,1)S(1)}, bf16[96,1280]{1,0:T(8,128)(2,1)S(1)}, u32[]{:S(2)}, u32[]{:S(2)}) %collective-permute-start.22) | collective-permute-done | bytes 245792 | tf_op jit(solution)/shard_map/ppermute | solution.py:30
  65.5 2.0 %collective-permute-done.21.refs_9_ = bf16[96,1280]{1,0:T(8,128)(2,1)S(1)} collective-permute-done((bf16[96,1280]{1,0:T(8,128)(2,1)S(1)}, bf16[96,1280]{1,0:T(8,128)(2,1)S(1)}, u32[]{:S(2)}, u32[]{:S(2)}) %collective-permute-start.21) | collective-permute-done | bytes 245792 | tf_op jit(solution)/shard_map/ppermute | solution.py:30
  67.6 1.5 %collective-permute-done.27.refs_11_ = bf16[96,1280]{1,0:T(8,128)(2,1)S(1)} collective-permute-done((bf16[96,1280]{1,0:T(8,128)(2,1)S(1)}, bf16[96,1280]{1,0:T(8,128)(2,1)S(1)}, u32[]{:S(2)}, u32[]{:S(2)}) %collective-permute-start.27) | collective-permute-done | bytes 245792 | tf_op jit(solution)/shard_map/ppermute | solution.py:30
  69.1 1.9 %placement.1 = bf16[192,1280]{1,0:T(8,128)(2,1)} custom-call(s32[3]{0:T(128)S(1)} %pad_add_fusion.1.index_ref, s32[1,192]{1,0:T(1,128)S(1)} %bitcast.29, s32[1,192]{1,0:T(1,128)S(1)} %get-tuple-element.116.refs_1_, s32[1,192]{1,0:T(1,128)S(1)} %collective-permute-done.20.refs_2_, s32[1,192]{1,0:T(1,128)S(1)} %get-tuple-element.115.refs_3_, ...), custom_call_target="tpu_custom_call" | custom-call | tf_op jit(solution)/shard_map/placement/pallas_call | solution.py:396
  (51 shorter events, 5.1 us)
Async XLA Ops:
  1.2 20.0 %copy-start.3 = (s32[768]{0:T(1024)S(1)}, s32[768]{0:T(1024)}, u32[]{:S(2)}) copy-start(s32[768]{0:T(1024)} %param.8) | copy-start | bytes 9220
  1.9 8.9 %collective-permute-start.1 = (bf16[3,800,128]{2,1,0:T(8,128)(2,1)S(1)}, bf16[3,800,128]{2,1,0:T(8,128)(2,1)S(1)}, u32[]{:S(2)}, u32[]{:S(2)}) collective-permute-start(bf16[3,800,128]{2,1,0:T(8,128)(2,1)S(1)} %get-tuple-element.61.refs_0_), channel_id=1, source_target_pairs={{0,4},{4,0},{8,12},{12,8},{1,5},{5,1},{9,13},{13,9},{2,6},{6,2},{1... | collective-permute-start | bytes 1843208 | tf_op jit(solution)/shard_map/ppermute | solution.py:30
  2.4 8.3 %collective-permute-start = (bf16[800,128]{1,0:T(8,128)(2,1)S(1)}, bf16[800,128]{1,0:T(8,128)(2,1)S(1)}, u32[]{:S(2)}, u32[]{:S(2)}) collective-permute-start(bf16[800,128]{1,0:T(8,128)(2,1)S(1)} %get-tuple-element.60), channel_id=1, source_target_pairs={{0,8},{4,12},{8,0},{12,4},{1,9},{5,13},{9,1},{13,5},{2,10},{6,14},... | collective-permute-start | bytes 614408 | tf_op jit(solution)/shard_map/ppermute | solution.py:30
  6.0 11.5 %collective-permute-start.5 = (bf16[800,128]{1,0:T(8,128)(2,1)S(1)}, bf16[800,128]{1,0:T(8,128)(2,1)S(1)}, u32[]{:S(2)}, u32[]{:S(2)}) collective-permute-start(bf16[800,128]{1,0:T(8,128)(2,1)S(1)} %pack_proj.1.refs_7_), channel_id=1, source_target_pairs={{0,1},{1,0},{2,3},{3,2},{4,5},{5,4},{6,7},{7,6},{8,9},{9,8},{10,11... | collective-permute-start | bytes 614408 | tf_op jit(solution)/shard_map/ppermute | solution.py:30
  7.6 12.2 %collective-permute-start.8 = (bf16[800,128]{1,0:T(8,128)(2,1)S(1)}, bf16[800,128]{1,0:T(8,128)(2,1)S(1)}, u32[]{:S(2)}, u32[]{:S(2)}) collective-permute-start(bf16[800,128]{1,0:T(8,128)(2,1)S(1)} %pack_proj.1.refs_7_), channel_id=1, source_target_pairs={{0,2},{1,3},{2,0},{3,1},{16,19},{17,18},{18,17},{19,16},{4,6},{5,7... | collective-permute-start | bytes 614408 | tf_op jit(solution)/shard_map/ppermute | solution.py:296
  10.2 7.7 %collective-permute-start.3 = (bf16[800,128]{1,0:T(8,128)(2,1)S(1)}, bf16[800,128]{1,0:T(8,128)(2,1)S(1)}, u32[]{:S(2)}, u32[]{:S(2)}) collective-permute-start(bf16[800,128]{1,0:T(8,128)(2,1)S(1)} %get-tuple-element.63), channel_id=1, source_target_pairs={{0,8},{4,12},{8,0},{12,4},{1,9},{5,13},{9,1},{13,5},{2,10},{6,14},... | collective-permute-start | bytes 614408 | tf_op jit(solution)/shard_map/ppermute | solution.py:30
  10.7 7.2 %collective-permute-start.2 = (bf16[800,128]{1,0:T(8,128)(2,1)S(1)}, bf16[800,128]{1,0:T(8,128)(2,1)S(1)}, u32[]{:S(2)}, u32[]{:S(2)}) collective-permute-start(bf16[800,128]{1,0:T(8,128)(2,1)S(1)} %collective-permute-done.refs_2_), channel_id=1, source_target_pairs={{0,16},{16,0},{1,17},{17,1},{2,18},{18,2},{3,19},{19,3},{4,20},{20... | collective-permute-start | bytes 614408 | tf_op jit(solution)/shard_map/ppermute | solution.py:30
  12.4 5.6 %collective-permute-start.4 = (bf16[800,128]{1,0:T(8,128)(2,1)S(1)}, bf16[800,128]{1,0:T(8,128)(2,1)S(1)}, u32[]{:S(2)}, u32[]{:S(2)}) collective-permute-start(bf16[800,128]{1,0:T(8,128)(2,1)S(1)} %collective-permute-done.refs_2_), channel_id=1, source_target_pairs={{0,4},{4,0},{8,12},{12,8},{1,5},{5,1},{9,13},{13,9},{2,6},{6,2},{1... | collective-permute-start | bytes 614408 | tf_op jit(solution)/shard_map/ppermute | solution.py:30
  12.4 1.5 %copy-start = (bf16[768,1280]{1,0:T(8,128)(2,1)S(1)}, bf16[768,1280]{1,0:T(8,128)(2,1)}, u32[]{:S(2)}) copy-start(bf16[768,1280]{1,0:T(8,128)(2,1)} %patches_ref) | copy-start | bytes 5898244
  17.5 10.8 %collective-permute-start.10 = (bf16[2,800,128]{2,1,0:T(8,128)(2,1)S(1)}, bf16[2,800,128]{2,1,0:T(8,128)(2,1)S(1)}, u32[]{:S(2)}, u32[]{:S(2)}) collective-permute-start(bf16[2,800,128]{2,1,0:T(8,128)(2,1)S(1)} %pad_maximum_fusion.1), channel_id=1, source_target_pairs={{0,8},{4,12},{8,0},{12,4},{1,9},{5,13},{9,1},{13,5},{2,10},{6,14},... | collective-permute-start | bytes 1228808 | tf_op jit(solution)/shard_map/ppermute | solution.py:30
  17.9 3.3 %collective-permute-start.6 = (bf16[800,128]{1,0:T(8,128)(2,1)S(1)}, bf16[800,128]{1,0:T(8,128)(2,1)S(1)}, u32[]{:S(2)}, u32[]{:S(2)}) collective-permute-start(bf16[800,128]{1,0:T(8,128)(2,1)S(1)} %collective-permute-done.2.refs_3_), channel_id=1, source_target_pairs={{0,4},{4,0},{8,12},{12,8},{1,5},{5,1},{9,13},{13,9},{2,6},{6,2},{1... | collective-permute-start | bytes 614408 | tf_op jit(solution)/shard_map/ppermute | solution.py:30
  18.2 3.1 %collective-permute-start.7 = (bf16[800,128]{1,0:T(8,128)(2,1)S(1)}, bf16[800,128]{1,0:T(8,128)(2,1)S(1)}, u32[]{:S(2)}, u32[]{:S(2)}) collective-permute-start(bf16[800,128]{1,0:T(8,128)(2,1)S(1)} %collective-permute-done.3.refs_4_), channel_id=1, source_target_pairs={{0,4},{4,0},{8,12},{12,8},{1,5},{5,1},{9,13},{13,9},{2,6},{6,2},{1... | collective-permute-start | bytes 614408 | tf_op jit(solution)/shard_map/ppermute | solution.py:30
  19.8 5.9 %collective-permute-start.9 = (bf16[800,128]{1,0:T(8,128)(2,1)S(1)}, bf16[800,128]{1,0:T(8,128)(2,1)S(1)}, u32[]{:S(2)}, u32[]{:S(2)}) collective-permute-start(bf16[800,128]{1,0:T(8,128)(2,1)S(1)} %collective-permute-done.8.refs_9_), channel_id=1, source_target_pairs={{0,16},{16,0},{1,17},{17,1},{2,18},{18,2},{3,19},{19,3},{4,20},{20... | collective-permute-start | bytes 614408 | tf_op jit(solution)/shard_map/ppermute | solution.py:30
  28.4 10.8 %collective-permute-start.13 = (bf16[4,800,128]{2,1,0:T(8,128)(2,1)S(1)}, bf16[4,800,128]{2,1,0:T(8,128)(2,1)S(1)}, u32[]{:S(2)}, u32[]{:S(2)}) collective-permute-start(bf16[4,800,128]{2,1,0:T(8,128)(2,1)S(1)} %pad_maximum_fusion), channel_id=1, source_target_pairs={{0,4},{4,0},{8,12},{12,8},{1,5},{5,1},{9,13},{13,9},{2,6},{6,2},{1... | collective-permute-start | bytes 2457608 | tf_op jit(solution)/shard_map/ppermute | solution.py:30
  28.5 15.0 %collective-permute-start.17 = (bf16[2,800,128]{2,1,0:T(8,128)(2,1)S(1)}, bf16[2,800,128]{2,1,0:T(8,128)(2,1)S(1)}, u32[]{:S(2)}, u32[]{:S(2)}) collective-permute-start(bf16[2,800,128]{2,1,0:T(8,128)(2,1)S(1)} %pad_maximum_fusion.2), channel_id=1, source_target_pairs={{0,8},{4,12},{8,0},{12,4},{1,9},{5,13},{9,1},{13,5},{2,10},{6,14},... | collective-permute-start | bytes 1228808 | tf_op jit(solution)/shard_map/ppermute | solution.py:30
  30.1 8.3 %collective-permute-start.11 = (bf16[240,128]{1,0:T(8,128)(2,1)S(1)}, bf16[240,128]{1,0:T(8,128)(2,1)S(1)}, u32[]{:S(2)}, u32[]{:S(2)}) collective-permute-start(bf16[240,128]{1,0:T(8,128)(2,1)S(1)} %get-tuple-element.85), channel_id=1, source_target_pairs={{0,2},{1,3},{2,0},{3,1},{4,6},{5,7},{6,4},{7,5},{8,10},{9,11},{10,... | collective-permute-start | bytes 184328 | tf_op jit(solution)/shard_map/ppermute | solution.py:30
  33.1 6.1 %collective-permute-start.12 = (bf16[240,128]{1,0:T(8,128)(2,1)S(1)}, bf16[240,128]{1,0:T(8,128)(2,1)S(1)}, u32[]{:S(2)}, u32[]{:S(2)}) collective-permute-start(bf16[240,128]{1,0:T(8,128)(2,1)S(1)} %get-tuple-element.86), channel_id=1, source_target_pairs={{0,3},{1,2},{2,1},{3,0},{4,7},{5,6},{6,5},{7,4},{8,11},{9,10},{10,... | collective-permute-start | bytes 184328 | tf_op jit(solution)/shard_map/ppermute | solution.py:30
  34.4 15.0 %copy-start.6 = (s32[192]{0:T(256)S(1)}, s32[192]{0:T(256)}, u32[]{:S(2)}) copy-start(s32[192]{0:T(256)} %param.9) | copy-start | bytes 2308
  34.4 18.7 %copy-start.5 = (f32[1280]{0:T(1024)S(1)}, f32[1280]{0:T(1024)}, u32[]{:S(2)}) copy-start(f32[1280]{0:T(1024)} %refs_17_.1) | copy-start | bytes 15364
  39.2 10.3 %collective-permute-start.14 = (bf16[2,240,128]{2,1,0:T(8,128)(2,1)S(1)}, bf16[2,240,128]{2,1,0:T(8,128)(2,1)S(1)}, u32[]{:S(2)}, u32[]{:S(2)}) collective-permute-start(bf16[2,240,128]{2,1,0:T(8,128)(2,1)S(1)} %get-tuple-element.90), channel_id=1, source_target_pairs={{0,1},{1,0},{2,3},{3,2},{4,5},{5,4},{6,7},{7,6},{8,9},{9,8},{10,11... | collective-permute-start | bytes 368648 | tf_op jit(solution)/shard_map/ppermute | solution.py:30
  40.1 5.2 %collective-permute-start.15 = (bf16[240,128]{1,0:T(8,128)(2,1)S(1)}, bf16[240,128]{1,0:T(8,128)(2,1)S(1)}, u32[]{:S(2)}, u32[]{:S(2)}) collective-permute-start(bf16[240,128]{1,0:T(8,128)(2,1)S(1)} %get-tuple-element.92), channel_id=1, source_target_pairs={{0,2},{1,3},{2,0},{3,1},{4,6},{5,7},{6,4},{7,5},{8,10},{9,11},{10,... | collective-permute-start | bytes 184328 | tf_op jit(solution)/shard_map/ppermute | solution.py:30
  42.3 7.2 %collective-permute-start.16 = (bf16[240,128]{1,0:T(8,128)(2,1)S(1)}, bf16[240,128]{1,0:T(8,128)(2,1)S(1)}, u32[]{:S(2)}, u32[]{:S(2)}) collective-permute-start(bf16[240,128]{1,0:T(8,128)(2,1)S(1)} %get-tuple-element.94), channel_id=1, source_target_pairs={{0,3},{1,2},{2,1},{3,0},{4,7},{5,6},{6,5},{7,4},{8,11},{9,10},{10,... | collective-permute-start | bytes 184328 | tf_op jit(solution)/shard_map/ppermute | solution.py:30
  43.6 9.6 %collective-permute-start.18 = (bf16[2,800,128]{2,1,0:T(8,128)(2,1)S(1)}, bf16[2,800,128]{2,1,0:T(8,128)(2,1)S(1)}, u32[]{:S(2)}, u32[]{:S(2)}) collective-permute-start(bf16[2,800,128]{2,1,0:T(8,128)(2,1)S(1)} %collective-permute-done.10.refs_12_), channel_id=1, source_target_pairs={{0,4},{4,0},{8,12},{12,8},{1,5},{5,1},{9,13},{13,9},{2,6},{6,2},{1... | collective-permute-start | bytes 1228808 | tf_op jit(solution)/shard_map/ppermute | solution.py:30
  49.5 3.7 %collective-permute-start.19 = (bf16[2,800,128]{2,1,0:T(8,128)(2,1)S(1)}, bf16[2,800,128]{2,1,0:T(8,128)(2,1)S(1)}, u32[]{:S(2)}, u32[]{:S(2)}) collective-permute-start(bf16[2,800,128]{2,1,0:T(8,128)(2,1)S(1)} %collective-permute-done.17.refs_13_), channel_id=1, source_target_pairs={{0,4},{4,0},{8,12},{12,8},{1,5},{5,1},{9,13},{13,9},{2,6},{6,2},{1... | collective-permute-start | bytes 1228808 | tf_op jit(solution)/shard_map/ppermute | solution.py:30
  49.5 3.6 %collective-permute-start.20 = (s32[1,192]{1,0:T(1,128)S(1)}, s32[1,192]{1,0:T(1,128)S(1)}, u32[]{:S(2)}, u32[]{:S(2)}) collective-permute-start(s32[1,192]{1,0:T(1,128)S(1)} %bitcast.27), channel_id=1, source_target_pairs={{0,8},{4,12},{8,0},{12,4},{1,9},{5,13},{9,1},{13,5},{2,10},{6,14},... | collective-permute-start | bytes 2312 | tf_op jit(solution)/shard_map/ppermute | solution.py:30
  55.1 9.0 %collective-permute-start.22 = (bf16[96,1280]{1,0:T(8,128)(2,1)S(1)}, bf16[96,1280]{1,0:T(8,128)(2,1)S(1)}, u32[]{:S(2)}, u32[]{:S(2)}) collective-permute-start(bf16[96,1280]{1,0:T(8,128)(2,1)S(1)} %get-tuple-element.110.refs_4_), channel_id=1, source_target_pairs={{0,8},{4,12},{8,0},{12,4},{1,9},{5,13},{9,1},{13,5},{2,10},{6,14},... | collective-permute-start | bytes 737288 | tf_op jit(solution)/shard_map/ppermute | solution.py:30
  55.6 11.9 %collective-permute-start.21 = (bf16[96,1280]{1,0:T(8,128)(2,1)S(1)}, bf16[96,1280]{1,0:T(8,128)(2,1)S(1)}, u32[]{:S(2)}, u32[]{:S(2)}) collective-permute-start(bf16[96,1280]{1,0:T(8,128)(2,1)S(1)} %get-tuple-element.109.refs_5_), channel_id=1, source_target_pairs={{0,8},{4,12},{8,0},{12,4},{1,9},{5,13},{9,1},{13,5},{2,10},{6,14},... | collective-permute-start | bytes 737288 | tf_op jit(solution)/shard_map/ppermute | solution.py:30
  64.0 3.5 %collective-permute-start.23 = (bf16[96,1280]{1,0:T(8,128)(2,1)S(1)}, bf16[96,1280]{1,0:T(8,128)(2,1)S(1)}, u32[]{:S(2)}, u32[]{:S(2)}) collective-permute-start(bf16[96,1280]{1,0:T(8,128)(2,1)S(1)} %collective-permute-done.22.refs_8_), channel_id=1, source_target_pairs={{0,4},{4,0},{8,12},{12,8},{1,5},{5,1},{9,13},{13,9},{2,6},{6,2},{1... | collective-permute-start | bytes 737288 | tf_op jit(solution)/shard_map/ppermute | solution.py:30
  64.0 1.5 %collective-permute-start.24 = (s32[2,1,192]{2,1,0:T(1,128)S(1)}, s32[2,1,192]{2,1,0:T(1,128)S(1)}, u32[]{:S(2)}, u32[]{:S(2)}) collective-permute-start(s32[2,1,192]{2,1,0:T(1,128)S(1)} %pad_add_fusion), channel_id=1, source_target_pairs={{0,4},{4,0},{8,12},{12,8},{1,5},{5,1},{9,13},{13,9},{2,6},{6,2},{1... | collective-permute-start | bytes 4616 | tf_op jit(solution)/shard_map/ppermute | solution.py:30
  64.5 3.0 %collective-permute-start.25 = (bf16[96,1280]{1,0:T(8,128)(2,1)S(1)}, bf16[96,1280]{1,0:T(8,128)(2,1)S(1)}, u32[]{:S(2)}, u32[]{:S(2)}) collective-permute-start(bf16[96,1280]{1,0:T(8,128)(2,1)S(1)} %get-tuple-element.110.refs_4_), channel_id=1, source_target_pairs={{0,4},{4,0},{8,12},{12,8},{1,5},{5,1},{9,13},{13,9},{2,6},{6,2},{1... | collective-permute-start | bytes 737288 | tf_op jit(solution)/shard_map/ppermute | solution.py:30
  64.5 3.0 %collective-permute-start.26 = (bf16[96,1280]{1,0:T(8,128)(2,1)S(1)}, bf16[96,1280]{1,0:T(8,128)(2,1)S(1)}, u32[]{:S(2)}, u32[]{:S(2)}) collective-permute-start(bf16[96,1280]{1,0:T(8,128)(2,1)S(1)} %get-tuple-element.109.refs_5_), channel_id=1, source_target_pairs={{0,4},{4,0},{8,12},{12,8},{1,5},{5,1},{9,13},{13,9},{2,6},{6,2},{1... | collective-permute-start | bytes 737288 | tf_op jit(solution)/shard_map/ppermute | solution.py:30
  67.6 1.5 %collective-permute-start.27 = (bf16[96,1280]{1,0:T(8,128)(2,1)S(1)}, bf16[96,1280]{1,0:T(8,128)(2,1)S(1)}, u32[]{:S(2)}, u32[]{:S(2)}) collective-permute-start(bf16[96,1280]{1,0:T(8,128)(2,1)S(1)} %collective-permute-done.21.refs_9_), channel_id=1, source_target_pairs={{0,4},{4,0},{8,12},{12,8},{1,5},{5,1},{9,13},{13,9},{2,6},{6,2},{1... | collective-permute-start | bytes 737288 | tf_op jit(solution)/shard_map/ppermute | solution.py:30
  (3 other events, 2.8 us)

commit v15 on v13

--- a/solution.py
+++ b/solution.py
@@ -1,4 +1,5 @@
 import functools
+import math
 
 import jax
 import jax.numpy as jnp
@@ -11,7 +12,6 @@
 WIN = 64
 PAIR = 2 * WIN
 LANES = 128
-HALVES = 2
 F32 = jnp.float32
 BF16 = jnp.bfloat16
 VMEM = pl.BlockSpec(memory_space=pltpu.VMEM)
@@ -123,34 +123,44 @@
         ref[:, :main] = qkv[:, j * main : (j + 1) * main].astype(BF16)
         at = 3 * main + j * rest
         ref[:, main:] = qkv[:, at : at + rest].astype(BF16)
-    lane = lax.broadcasted_iota(jnp.int32, (1, width), 1)
-    head_masks = [one_hot((lane >= h * HD) & (lane < (h + 1) * HD)) for h in range(heads)]
-    q_win = lax.broadcasted_iota(jnp.int32, (PAIR, PAIR), 0) // WIN
-    k_win = lax.broadcasted_iota(jnp.int32, (PAIR, PAIR), 1) // WIN
+    q_win = lax.broadcasted_iota(jnp.int32, (PAIR, PAIR), 1) // WIN
+    k_win = lax.broadcasted_iota(jnp.int32, (PAIR, PAIR), 0) // WIN
     same = q_win == k_win
     floor = jnp.where(same, F32(-1e30), F32(-3e38))
     pick = PAIR // 4
     src = lax.broadcasted_iota(jnp.int32, (PAIR, PAIR), 1)
     dst = lax.broadcasted_iota(jnp.int32, (PAIR, PAIR), 0)
     order = one_hot(src == 4 * (dst % pick) + dst // pick)
+    zero = jnp.zeros((HD, PAIR), BF16)
+    factor = F32(HD ** (-0.5) * math.log2(math.e))
     for p in range(rows // PAIR):
         at = p * PAIR
-        q = q_ref[at : at + PAIR, :]
-        k = k_ref[at : at + PAIR, :]
-        v = v_ref[at : at + PAIR, :]
-        k_all = jnp.concatenate([k * m for m in head_masks], axis=0)
-        v_all = jnp.concatenate([v * m for m in head_masks], axis=0)
-        scores = lax.dot_general(q, k_all, (((1,), (1,)), ((), ())), preferred_element_type=F32)
-        live = valid_ref[p : p + 1, :] > 0
-        weights = []
+        q_turned = q_ref[at : at + PAIR, :].T
+        v_turned = v_ref[at : at + PAIR, :].T
+        q_all = jnp.concatenate(
+            [
+                jnp.concatenate(
+                    [q_turned[h * HD : (h + 1) * HD] if i == h else zero for i in range(heads)], axis=1
+                )
+                for h in range(heads)
+            ],
+            axis=0,
+        )
+        scores = jnp.dot(k_ref[at : at + PAIR, :], q_all, preferred_element_type=F32)
+        live = jnp.broadcast_to(valid_ref[p : p + 1, :].astype(F32), (PAIR, PAIR)).T > 0
+        bias = jnp.where(same & live, F32(0), floor)
+        mixed = []
         for h in range(heads):
-            s = scores[:, h * PAIR : (h + 1) * PAIR] * F32(HD ** (-0.5))
-            s = jnp.where(same & live, s, floor)
-            e = jnp.exp(s - jnp.max(s, axis=-1, keepdims=True))
-            weights.append((e / jnp.sum(e, axis=-1, keepdims=True)).astype(BF16))
-        w_all = jnp.concatenate(weights, axis=1)
-        mixed = jnp.dot(w_all, v_all, preferred_element_type=F32).astype(BF16)
-        mixed = jnp.dot(order, mixed, preferred_element_type=F32).astype(BF16)
+            s = scores[:, h * PAIR : (h + 1) * PAIR] + bias
+            e = jnp.exp2((s - jnp.max(s, axis=0, keepdims=True)) * factor)
+            weights = (e * (1.0 / jnp.sum(e, axis=0, keepdims=True))).astype(BF16)
+            mixed.append(
+                jnp.dot(v_turned[h * HD : (h + 1) * HD], weights, preferred_element_type=F32)
+            )
+        mixed = jnp.concatenate(mixed, axis=0).astype(BF16)
+        mixed = lax.dot_general(
+            order, mixed, (((1,), (1,)), ((), ())), preferred_element_type=F32
+        ).astype(BF16)
         for t in range(4):
             mix_ref[t, p * pick : (p + 1) * pick, :] = mixed[t * pick : (t + 1) * pick]
     for s, out_ref in enumerate(out_refs):
@@ -181,8 +191,7 @@
 
 
 def project_kernel(n_ctx, width, col, index_ref, *refs):
-    *blocks, own_ref, gain_ref = refs[4 : -HALVES - 1]
-    *out_refs, part_ref = refs[-HALVES - 1 :]
+    *blocks, own_ref, gain_ref, out_ref, part_ref = refs[4:]
     rows = own_ref.shape[0]
     mixes = [unpack(m[...], rows, width) for m in refs[:4]]
     flip = index_ref[2] > 0
@@ -217,15 +226,14 @@
     total = jnp.concatenate([part_ref[i] for i in range(n_ctx)], axis=1)
     total = total + own_ref[...].astype(F32)
     mean_sq = jnp.mean(total * total, axis=-1, keepdims=True)
-    normed = (total * lax.rsqrt(mean_sq + 1e-06) * gain_ref[...].reshape(1, -1)).astype(BF16)
-    count = rows // HALVES
-    for i, out_ref in enumerate(out_refs):
-        out_ref[...] = normed[i * count : (i + 1) * count]
-
-
-def place_kernel(n_ctx, index_ref, *refs):
-    place_refs = refs[:n_ctx]
-    row_refs = refs[n_ctx:-1]
+    gain = gain_ref[...].reshape(1, -1)
+    out_ref[...] = (total * lax.rsqrt(mean_sq + 1e-06) * gain).astype(BF16)
+
+
+def place_kernel(count, index_ref, *refs):
+    place_refs = refs[:count]
+    row_refs = refs[count : 2 * count]
+    before = refs[2 * count : -1]
     out_ref = refs[-1]
     spots = out_ref.shape[0]
     chosen = []
@@ -233,11 +241,14 @@
         target = place_ref[...] - index_ref[0] * spots
         grid = lax.broadcasted_iota(jnp.int32, (spots, target.shape[1]), 0)
         chosen.append(one_hot(grid == target))
-    out_ref[...] = jnp.dot(
+    total = jnp.dot(
         jnp.concatenate(chosen, axis=1),
         jnp.concatenate([ref[...] for ref in row_refs], axis=0),
         preferred_element_type=F32,
-    ).astype(BF16)
+    )
+    for ref in before:
+        total = total + ref[...]
+    out_ref[...] = total.astype(out_ref.dtype)
 
 
 def local(n_dp, n_ctx, n_ten, patches, valid, place, gain_attn, w_qkv, w_proj, gain_merge):
@@ -331,45 +342,42 @@
     high = gather_cross(jnp.stack([far, far2]), n_ctx)
     blocks = [w_proj, by_one, far, far2, over_core(jnp.stack([w_proj, by_one, far, far2]))]
     low_twin = {k: over_core(low[k]) for k in cross}
-    mixed, high, place = together(mixed, high, place)
-    places = gather_cross(place.reshape(1, groups), n_ctx)
+    mixed, high = together(mixed, high)
     for k in cross:
         blocks += [low[k], high[k], low_twin[k], over_core(high[k])]
     done = pl.pallas_call(
         functools.partial(project_kernel, n_ctx, width, col),
-        out_shape=(shape(groups // HALVES, feat),) * HALVES,
+        out_shape=shape(groups, feat),
         in_specs=[SMEM] + [VMEM] * (n_ten + len(blocks) + 2),
-        out_specs=(VMEM,) * HALVES,
+        out_specs=VMEM,
         scratch_shapes=[pltpu.VMEM((n_ctx, groups, col), F32)],
         compiler_params=params(24),
         name="project",
     )(index, *mixed, *blocks, own_patches, gain_merge)
 
-    done, place_group = together(done, jnp.stack([places[k] for k in (0, *cross)]))
-    gathered = []
-    for r in range(HALVES):
-        crossed = gather_cross(done[r], n_ctx)
-        if r == 0:
-            place_twin = over_core(place_group)
-        else:
-            for k in cross:
-                crossed[k], gathered[r - 1][k ^ 1], place_twin = together(
-                    crossed[k], gathered[r - 1][k ^ 1], place_twin
-                )
-        for k in list(crossed):
-            crossed[k ^ 1] = over_core(crossed[k])
-        gathered.append(crossed)
-    place_list = []
-    for i, k in enumerate((0, *cross)):
-        place_list += [places[k], place_twin[i]]
-    return pl.pallas_call(
-        functools.partial(place_kernel, n_ctx),
-        out_shape=shape(groups, feat),
-        in_specs=[SMEM] + [VMEM] * (n_ctx + n_ctx * HALVES),
-        out_specs=VMEM,
-        compiler_params=params(28),
-        name="placement",
-    )(index, *place_list, *[gathered[r][k] for k in range(n_ctx) for r in range(HALVES)])
+    crossed = gather_cross(done, n_ctx)
+    near_rows = over_core(done)
+    places = gather_cross(place.reshape(1, groups), n_ctx)
+    place_twin = over_core(jnp.stack([places[k] for k in (0, *cross)]))
+
+    def put(ids, rows_in, before, dtype, name):
+        return pl.pallas_call(
+            functools.partial(place_kernel, len(ids)),
+            out_shape=jax.ShapeDtypeStruct((groups, feat), dtype),
+            in_specs=[SMEM] + [VMEM] * (2 * len(ids) + len(before)),
+            out_specs=VMEM,
+            compiler_params=params(24),
+            name=name,
+        )(index, *ids, *rows_in, *before)
+
+    total = put([places[0], place_twin[0]], [done, near_rows], [], F32, "placement0")
+    for k in cross:
+        crossed[k], total = together(crossed[k], total)
+        crossed[k ^ 1] = over_core(crossed[k])
+    ids = []
+    for i, k in enumerate(cross):
+        ids += [places[k], place_twin[1 + i]]
+    return put(ids, [crossed[k] for k in range(2, n_ctx)], [total], BF16, "placement1")
 
 
 def solution(mesh):

time: 66.3 us -> 68.1 us (1.027)
  waiting for transfers between devices: 26.6 us -> 29.2 us
    ppermute x25 -> x22, waiting for transfers between devices: 25.3 us -> 27.9 us  [swap(): return lax.ppermute(x, axis, [(i, i ^ bit) for i in range(size)])]
    pallas_call x1, Pallas kernels: 7.47 us -> 6.33 us  [local(): pl.pallas_call(functools.partial(attention_kernel, n_ctx, width), out_sha...]
    pallas_call x1 -> x2, Pallas kernels: 1.93 us -> 2.79 us  [put(): pl.pallas_call(functools.partial(place_kernel, len(ids)), out_shape=jax.S...]
    ppermute x25 -> x22, starting transfers between devices: 18.5 us -> 18 us  [swap(): return lax.ppermute(x, axis, [(i, i ^ bit) for i in range(size)])]
  transfers between devices with their start and end apart: 26 -> 23, of which waited for: 9 -> 9; matrix products, arithmetic and copies ran while one was open for 0% -> 0% of each run, Pallas kernels for 14% -> 13%
where the time goes in v15:
time: 68.1 us; the launch traced here: 67.9 us
  waiting for transfers between devices  29.2 us (43%)
  starting transfers between devices  20.6 us (30%)
  Pallas kernels  13.4 us (20%)
  local copies, waits for them, and re-layouts  4.32 us (6%)
    ppermute x22, waiting for transfers between devices, swap(): return lax.ppermute(x, axis, [(i, i ^ bit) for i in range(size)])  27.9 us
    ppermute x22, starting transfers between devices, swap(): return lax.ppermute(x, axis, [(i, i ^ bit) for i in range(size)])  18 us
    pallas_call x1, Pallas kernels, local(): pl.pallas_call(functools.partial(attention_kernel, n_ctx, width), out_sha...  6.33 us
    unnamed x14, local copies, waits for them, and re-layouts  4.32 us
    pallas_call x2, Pallas kernels, put(): pl.pallas_call(functools.partial(place_kernel, len(ids)), out_shape=jax.S...  2.79 us
    ppermute x1, starting transfers between devices, local(): lax.ppermute(w_proj, ('dp', 'tensor'), [(d * n_ten + t, d * n_ten + (t ^...  2.59 us
    pallas_call x1, Pallas kernels, local(): pl.pallas_call(functools.partial(project_kernel, n_ctx, width, col), out_...  1.92 us
    pallas_call x1, Pallas kernels, local(): pl.pallas_call(norm_kernel, out_shape=(shape(rows, feat), shape(groups, f...  1.57 us
  transfers between devices with their start and end apart: 23, of which 9 were waited for; matrix products, arithmetic and copies ran while one was open for 0% of the time, Pallas kernels for 13%

profile of v15, /device:TPU:0, one launch (start us, length us, event | category | flops | bytes accessed | tf_op | source)
XLA Modules:
  0.0 67.9 jit_solution(16560783533411139513)
XLA Ops:
  0.1 1.1 %copy-done.1 = bf16[320,3,320]{2,0,1:T(8,128)(2,1)S(1)} copy-done((bf16[320,3,320]{2,0,1:T(8,128)(2,1)S(1)}, bf16[320,3,320]{2,0,1:T(8,128)(2,1)}, u32[]{:S(2)}) %copy-start.1) | copy-done | bytes 614424
  1.2 0.7 %pack.1 = (bf16[800,128]{1,0:T(8,128)(2,1)S(1)}, bf16[800,128]{1,0:T(8,128)(2,1)S(1)}, bf16[3,800,128]{2,1,0:T(8,128)(2,1)S(1)}) custom-call(s32[3]{0:T(128)S(1)} %pad_add_fusion.1.index_ref, bf16[3,320,320]{2,1,0:T(8,128)(2,1)S(1)} %bitcast.24), custom_call_target="tpu_custom_call" | custom-call | tf_op jit(solution)/shard_map/pack/pallas_call | solution.py:272
  1.9 0.5 collective-permute-start.3
  2.4 2.6 %collective-permute-start.2 = (bf16[800,128]{1,0:T(8,128)(2,1)S(1)}, bf16[800,128]{1,0:T(8,128)(2,1)S(1)}, u32[]{:S(2)}, u32[]{:S(2)}) collective-permute-start(bf16[800,128]{1,0:T(8,128)(2,1)S(1)} %get-tuple-element.38), channel_id=1, source_target_pairs={{0,8},{4,12},{8,0},{12,4},{1,9},{5,13},{9,1},{13,5},{2,10},{6,14},... | collective-permute-start | bytes 614408 | tf_op jit(solution)/shard_map/ppermute | solution.py:26
  5.0 0.9 %copy-done.2 = bf16[320,320]{1,0:T(8,128)(2,1)S(1)} copy-done((bf16[320,320]{1,0:T(8,128)(2,1)S(1)}, bf16[320,320]{1,0:T(8,128)(2,1)}, u32[]{:S(2)}) %copy-start.2) | copy-done | bytes 204824
  6.0 1.6 %collective-permute-start.7 = (bf16[800,128]{1,0:T(8,128)(2,1)S(1)}, bf16[800,128]{1,0:T(8,128)(2,1)S(1)}, u32[]{:S(2)}, u32[]{:S(2)}) collective-permute-start(bf16[800,128]{1,0:T(8,128)(2,1)S(1)} %pack_proj.1.refs_4_), channel_id=1, source_target_pairs={{0,1},{1,0},{2,3},{3,2},{4,5},{5,4},{6,7},{7,6},{8,9},{9,8},{10,11... | collective-permute-start | bytes 614408 | tf_op jit(solution)/shard_map/ppermute | solution.py:26
  7.6 2.6 %collective-permute-start.10 = (bf16[800,128]{1,0:T(8,128)(2,1)S(1)}, bf16[800,128]{1,0:T(8,128)(2,1)S(1)}, u32[]{:S(2)}, u32[]{:S(2)}) collective-permute-start(bf16[800,128]{1,0:T(8,128)(2,1)S(1)} %pack_proj.1.refs_4_), channel_id=1, source_target_pairs={{0,2},{1,3},{2,0},{3,1},{16,19},{17,18},{18,17},{19,16},{4,6},{5,7... | collective-permute-start | bytes 614408 | tf_op jit(solution)/shard_map/ppermute | solution.py:291
  10.2 0.5 collective-permute-start.5
  10.7 1.7 %collective-permute-start.4 = (bf16[800,128]{1,0:T(8,128)(2,1)S(1)}, bf16[800,128]{1,0:T(8,128)(2,1)S(1)}, u32[]{:S(2)}, u32[]{:S(2)}) collective-permute-start(bf16[800,128]{1,0:T(8,128)(2,1)S(1)} %collective-permute-done.2.refs_2_), channel_id=1, source_target_pairs={{0,16},{16,0},{1,17},{17,1},{2,18},{18,2},{3,19},{19,3},{4,20},{20... | collective-permute-start | bytes 614408 | tf_op jit(solution)/shard_map/ppermute | solution.py:26
  12.4 1.5 %copy-done = bf16[768,1280]{1,0:T(8,128)(2,1)S(1)} copy-done((bf16[768,1280]{1,0:T(8,128)(2,1)S(1)}, bf16[768,1280]{1,0:T(8,128)(2,1)}, u32[]{:S(2)}) %copy-start) | copy-done | bytes 1966104
  13.9 0.7 %copy-done.3 = f32[1280]{0:T(1024)S(1)} copy-done((f32[1280]{0:T(1024)S(1)}, f32[1280]{0:T(1024)}, u32[]{:S(2)}) %copy-start.3) | copy-done | bytes 5144
  14.6 1.6 %norm.1 = (bf16[768,1280]{1,0:T(8,128)(2,1)S(1)}, bf16[192,1280]{1,0:T(8,128)(2,1)S(1)}) custom-call(s32[3]{0:T(128)S(1)} %pad_add_fusion.1.index_ref, bf16[768,1280]{1,0:T(8,128)(2,1)S(1)} %copy-done, f32[1280]{0:T(1024)S(1)} %copy-done.3), custom_call_target="tpu_custom_call" | custom-call | tf_op jit(solution)/shard_map/norm/pallas_call | solution.py:305
  16.2 1.3 %collective-permute-done.7.refs_5_ = bf16[800,128]{1,0:T(8,128)(2,1)S(1)} collective-permute-done((bf16[800,128]{1,0:T(8,128)(2,1)S(1)}, bf16[800,128]{1,0:T(8,128)(2,1)S(1)}, u32[]{:S(2)}, u32[]{:S(2)}) %collective-permute-start.7) | collective-permute-done | bytes 204832 | tf_op jit(solution)/shard_map/ppermute | solution.py:26
  17.5 0.4 collective-permute-start.12
  18.2 0.3 collective-permute-start.9
  18.5 1.3 %collective-permute-done.10.refs_6_ = bf16[800,128]{1,0:T(8,128)(2,1)S(1)} collective-permute-done((bf16[800,128]{1,0:T(8,128)(2,1)S(1)}, bf16[800,128]{1,0:T(8,128)(2,1)S(1)}, u32[]{:S(2)}, u32[]{:S(2)}) %collective-permute-start.10) | collective-permute-done | bytes 204832 | tf_op jit(solution)/shard_map/ppermute | solution.py:291
  19.8 1.4 %collective-permute-start.11 = (bf16[800,128]{1,0:T(8,128)(2,1)S(1)}, bf16[800,128]{1,0:T(8,128)(2,1)S(1)}, u32[]{:S(2)}, u32[]{:S(2)}) collective-permute-start(bf16[800,128]{1,0:T(8,128)(2,1)S(1)} %collective-permute-done.10.refs_6_), channel_id=1, source_target_pairs={{0,16},{16,0},{1,17},{17,1},{2,18},{18,2},{3,19},{19,3},{4,20},{20... | collective-permute-start | bytes 614408 | tf_op jit(solution)/shard_map/ppermute | solution.py:26
  21.2 6.3 %attention.1 = (bf16[480,128]{1,0:T(8,128)(2,1)S(1)}, bf16[480,128]{1,0:T(8,128)(2,1)S(1)}, bf16[480,128]{1,0:T(8,128)(2,1)S(1)}, bf16[480,128]{1,0:T(8,128)(2,1)S(1)}) custom-call(s32[3]{0:T(128)S(1)} %pad_add_fusion.1.index_ref, bf16[768,1280]{1,0:T(8,128)(2,1)S(1)} %get-tuple-element.45.hidden_ref, s32[6,128]{1,0:T(8,128)S(1)} %bitcast.29, ...), custom_call_target="tpu_custom_call" | custom-call | tf_op jit(solution)/shard_map/attention/pallas_call | solution.py:327
  27.6 0.7 %collective-permute-done.12.refs_9_ = bf16[2,800,128]{2,1,0:T(8,128)(2,1)S(1)} collective-permute-done((bf16[2,800,128]{2,1,0:T(8,128)(2,1)S(1)}, bf16[2,800,128]{2,1,0:T(8,128)(2,1)S(1)}, u32[]{:S(2)}, u32[]{:S(2)}) %collective-permute-start.12) | collective-permute-done | bytes 409632 | tf_op jit(solution)/shard_map/ppermute | solution.py:26
  28.3 1.5 %collective-permute-start.16 = (bf16[2,800,128]{2,1,0:T(8,128)(2,1)S(1)}, bf16[2,800,128]{2,1,0:T(8,128)(2,1)S(1)}, u32[]{:S(2)}, u32[]{:S(2)}) collective-permute-start(bf16[2,800,128]{2,1,0:T(8,128)(2,1)S(1)} %pad_maximum_fusion.2), channel_id=1, source_target_pairs={{0,8},{4,12},{8,0},{12,4},{1,9},{5,13},{9,1},{13,5},{2,10},{6,14},... | collective-permute-start | bytes 1228808 | tf_op jit(solution)/shard_map/ppermute | solution.py:26
  30.0 2.1 %collective-permute-start.13 = (bf16[480,128]{1,0:T(8,128)(2,1)S(1)}, bf16[480,128]{1,0:T(8,128)(2,1)S(1)}, u32[]{:S(2)}, u32[]{:S(2)}) collective-permute-start(bf16[480,128]{1,0:T(8,128)(2,1)S(1)} %get-tuple-element.57), channel_id=1, source_target_pairs={{0,1},{1,0},{2,3},{3,2},{4,5},{5,4},{6,7},{7,6},{8,9},{9,8},{10,11... | collective-permute-start | bytes 368648 | tf_op jit(solution)/shard_map/ppermute | solution.py:26
  32.1 2.6 %collective-permute-start.14 = (bf16[480,128]{1,0:T(8,128)(2,1)S(1)}, bf16[480,128]{1,0:T(8,128)(2,1)S(1)}, u32[]{:S(2)}, u32[]{:S(2)}) collective-permute-start(bf16[480,128]{1,0:T(8,128)(2,1)S(1)} %get-tuple-element.58), channel_id=1, source_target_pairs={{0,2},{1,3},{2,0},{3,1},{4,6},{5,7},{6,4},{7,5},{8,10},{9,11},{10,... | collective-permute-start | bytes 368648 | tf_op jit(solution)/shard_map/ppermute | solution.py:26
  34.7 3.3 %collective-permute-done.13.refs_1_ = bf16[480,128]{1,0:T(8,128)(2,1)S(1)} collective-permute-done((bf16[480,128]{1,0:T(8,128)(2,1)S(1)}, bf16[480,128]{1,0:T(8,128)(2,1)S(1)}, u32[]{:S(2)}, u32[]{:S(2)}) %collective-permute-start.13) | collective-permute-done | bytes 122912 | tf_op jit(solution)/shard_map/ppermute | solution.py:26
  38.0 6.5 %collective-permute-done.14.refs_2_ = bf16[480,128]{1,0:T(8,128)(2,1)S(1)} collective-permute-done((bf16[480,128]{1,0:T(8,128)(2,1)S(1)}, bf16[480,128]{1,0:T(8,128)(2,1)S(1)}, u32[]{:S(2)}, u32[]{:S(2)}) %collective-permute-start.14) | collective-permute-done | bytes 122912 | tf_op jit(solution)/shard_map/ppermute | solution.py:26
  44.5 1.7 %collective-permute-done.19.refs_12_ = bf16[2,800,128]{2,1,0:T(8,128)(2,1)S(1)} collective-permute-done((bf16[2,800,128]{2,1,0:T(8,128)(2,1)S(1)}, bf16[2,800,128]{2,1,0:T(8,128)(2,1)S(1)}, u32[]{:S(2)}, u32[]{:S(2)}) %collective-permute-start.19) | collective-permute-done | bytes 409632 | tf_op jit(solution)/shard_map/ppermute | solution.py:26
  46.3 1.9 %project.1.refs_2_ = bf16[192,1280]{1,0:T(8,128)(2,1)S(1)} custom-call(s32[3]{0:T(128)S(1)} %pad_add_fusion.1.index_ref, bf16[480,128]{1,0:T(8,128)(2,1)S(1)} %get-tuple-element.62.refs_0_, bf16[480,128]{1,0:T(8,128)(2,1)S(1)} %collective-permute-done.13.refs_1_, bf16[480,128]{1,0:T(8,128)(2,1)S(1)} %collective-permute-done.14.refs_2_, ...), custom_call_target="tpu_custom_call" | custom-call | tf_op jit(solution)/shard_map/project/pallas_call | solution.py:348
  48.7 1.8 %collective-permute-start = (s32[1,192]{1,0:T(1,128)S(1)}, s32[1,192]{1,0:T(1,128)S(1)}, u32[]{:S(2)}, u32[]{:S(2)}) collective-permute-start(s32[1,192]{1,0:T(1,128)S(1)} %bitcast.25), channel_id=1, source_target_pairs={{0,8},{4,12},{8,0},{12,4},{1,9},{5,13},{9,1},{13,5},{2,10},{6,14},... | collective-permute-start | bytes 2312 | tf_op jit(solution)/shard_map/ppermute | solution.py:26
  50.5 11.5 %collective-permute-done.refs_0_ = s32[1,192]{1,0:T(1,128)S(1)} collective-permute-done((s32[1,192]{1,0:T(1,128)S(1)}, s32[1,192]{1,0:T(1,128)S(1)}, u32[]{:S(2)}, u32[]{:S(2)}) %collective-permute-start) | collective-permute-done | bytes 800 | tf_op jit(solution)/shard_map/ppermute | solution.py:26
  62.0 1.2 %collective-permute-done.1 = s32[2,1,192]{2,1,0:T(1,128)S(1)} collective-permute-done((s32[2,1,192]{2,1,0:T(1,128)S(1)}, s32[2,1,192]{2,1,0:T(1,128)S(1)}, u32[]{:S(2)}, u32[]{:S(2)}) %collective-permute-start.1) | collective-permute-done | bytes 1568 | tf_op jit(solution)/shard_map/ppermute | solution.py:26
  63.1 1.0 %placement0.1.refs_4_ = f32[192,1280]{1,0:T(8,128)S(1)} custom-call(s32[3]{0:T(128)S(1)} %pad_add_fusion.1.index_ref, s32[1,192]{1,0:T(1,128)S(1)} %bitcast.27, s32[1,192]{1,0:T(1,128)S(1)} %get-tuple-element.71.refs_1_, bf16[192,1280]{1,0:T(8,128)(2,1)S(1)} %project.1.refs_2_, bf16[192,1280]{1,0:T(8,128)(2,1)S(1)} %collective-permute-done.21.refs_3_), custom_call_target="tpu_custom_call" | custom-call | tf_op jit(solution)/shard_map/placement0/pallas_call | solution.py:364
  64.4 1.7 %collective-permute-done.22.refs_3_ = bf16[192,1280]{1,0:T(8,128)(2,1)S(1)} collective-permute-done((bf16[192,1280]{1,0:T(8,128)(2,1)S(1)}, bf16[192,1280]{1,0:T(8,128)(2,1)S(1)}, u32[]{:S(2)}, u32[]{:S(2)}) %collective-permute-start.22) | collective-permute-done | bytes 491552 | tf_op jit(solution)/shard_map/ppermute | solution.py:26
  66.1 1.8 %placement1.1 = bf16[192,1280]{1,0:T(8,128)(2,1)} custom-call(s32[3]{0:T(128)S(1)} %pad_add_fusion.1.index_ref, s32[1,192]{1,0:T(1,128)S(1)} %collective-permute-done.refs_0_, s32[1,192]{1,0:T(1,128)S(1)} %get-tuple-element.72.refs_1_, bf16[192,1280]{1,0:T(8,128)(2,1)S(1)} %collective-permute-done.20.refs_2_, ...), custom_call_target="tpu_custom_call" | custom-call | tf_op jit(solution)/shard_map/placement1/pallas_call | solution.py:364
  (41 shorter events, 1.4 us)
Async XLA Ops:
  0.1 1.1 %copy-start.1 = (bf16[320,3,320]{2,0,1:T(8,128)(2,1)S(1)}, bf16[320,3,320]{2,0,1:T(8,128)(2,1)}, u32[]{:S(2)}) copy-start(bf16[320,3,320]{2,0,1:T(8,128)(2,1)} %param.11) | copy-start | bytes 1843204
  1.2 20.0 %copy-start.6 = (s32[768]{0:T(1024)S(1)}, s32[768]{0:T(1024)}, u32[]{:S(2)}) copy-start(s32[768]{0:T(1024)} %param.8) | copy-start | bytes 9220
  1.9 8.9 %collective-permute-start.3 = (bf16[3,800,128]{2,1,0:T(8,128)(2,1)S(1)}, bf16[3,800,128]{2,1,0:T(8,128)(2,1)S(1)}, u32[]{:S(2)}, u32[]{:S(2)}) collective-permute-start(bf16[3,800,128]{2,1,0:T(8,128)(2,1)S(1)} %get-tuple-element.39.refs_0_), channel_id=1, source_target_pairs={{0,4},{4,0},{8,12},{12,8},{1,5},{5,1},{9,13},{13,9},{2,6},{6,2},{1... | collective-permute-start | bytes 1843208 | tf_op jit(solution)/shard_map/ppermute | solution.py:26
  2.4 8.3 %collective-permute-start.2 = (bf16[800,128]{1,0:T(8,128)(2,1)S(1)}, bf16[800,128]{1,0:T(8,128)(2,1)S(1)}, u32[]{:S(2)}, u32[]{:S(2)}) collective-permute-start(bf16[800,128]{1,0:T(8,128)(2,1)S(1)} %get-tuple-element.38), channel_id=1, source_target_pairs={{0,8},{4,12},{8,0},{12,4},{1,9},{5,13},{9,1},{13,5},{2,10},{6,14},... | collective-permute-start | bytes 614408 | tf_op jit(solution)/shard_map/ppermute | solution.py:26
  5.0 0.9 %copy-start.2 = (bf16[320,320]{1,0:T(8,128)(2,1)S(1)}, bf16[320,320]{1,0:T(8,128)(2,1)}, u32[]{:S(2)}) copy-start(bf16[320,320]{1,0:T(8,128)(2,1)} %proj_ref.1) | copy-start | bytes 614404
  6.0 11.5 %collective-permute-start.7 = (bf16[800,128]{1,0:T(8,128)(2,1)S(1)}, bf16[800,128]{1,0:T(8,128)(2,1)S(1)}, u32[]{:S(2)}, u32[]{:S(2)}) collective-permute-start(bf16[800,128]{1,0:T(8,128)(2,1)S(1)} %pack_proj.1.refs_4_), channel_id=1, source_target_pairs={{0,1},{1,0},{2,3},{3,2},{4,5},{5,4},{6,7},{7,6},{8,9},{9,8},{10,11... | collective-permute-start | bytes 614408 | tf_op jit(solution)/shard_map/ppermute | solution.py:26
  7.6 12.2 %collective-permute-start.10 = (bf16[800,128]{1,0:T(8,128)(2,1)S(1)}, bf16[800,128]{1,0:T(8,128)(2,1)S(1)}, u32[]{:S(2)}, u32[]{:S(2)}) collective-permute-start(bf16[800,128]{1,0:T(8,128)(2,1)S(1)} %pack_proj.1.refs_4_), channel_id=1, source_target_pairs={{0,2},{1,3},{2,0},{3,1},{16,19},{17,18},{18,17},{19,16},{4,6},{5,7... | collective-permute-start | bytes 614408 | tf_op jit(solution)/shard_map/ppermute | solution.py:291
  10.2 7.7 %collective-permute-start.5 = (bf16[800,128]{1,0:T(8,128)(2,1)S(1)}, bf16[800,128]{1,0:T(8,128)(2,1)S(1)}, u32[]{:S(2)}, u32[]{:S(2)}) collective-permute-start(bf16[800,128]{1,0:T(8,128)(2,1)S(1)} %get-tuple-element.41), channel_id=1, source_target_pairs={{0,8},{4,12},{8,0},{12,4},{1,9},{5,13},{9,1},{13,5},{2,10},{6,14},... | collective-permute-start | bytes 614408 | tf_op jit(solution)/shard_map/ppermute | solution.py:26
  10.7 7.2 %collective-permute-start.4 = (bf16[800,128]{1,0:T(8,128)(2,1)S(1)}, bf16[800,128]{1,0:T(8,128)(2,1)S(1)}, u32[]{:S(2)}, u32[]{:S(2)}) collective-permute-start(bf16[800,128]{1,0:T(8,128)(2,1)S(1)} %collective-permute-done.2.refs_2_), channel_id=1, source_target_pairs={{0,16},{16,0},{1,17},{17,1},{2,18},{18,2},{3,19},{19,3},{4,20},{20... | collective-permute-start | bytes 614408 | tf_op jit(solution)/shard_map/ppermute | solution.py:26
  12.4 5.6 %collective-permute-start.6 = (bf16[800,128]{1,0:T(8,128)(2,1)S(1)}, bf16[800,128]{1,0:T(8,128)(2,1)S(1)}, u32[]{:S(2)}, u32[]{:S(2)}) collective-permute-start(bf16[800,128]{1,0:T(8,128)(2,1)S(1)} %collective-permute-done.2.refs_2_), channel_id=1, source_target_pairs={{0,4},{4,0},{8,12},{12,8},{1,5},{5,1},{9,13},{13,9},{2,6},{6,2},{1... | collective-permute-start | bytes 614408 | tf_op jit(solution)/shard_map/ppermute | solution.py:26
  12.4 1.5 %copy-start = (bf16[768,1280]{1,0:T(8,128)(2,1)S(1)}, bf16[768,1280]{1,0:T(8,128)(2,1)}, u32[]{:S(2)}) copy-start(bf16[768,1280]{1,0:T(8,128)(2,1)} %patches_ref) | copy-start | bytes 5898244
  13.9 0.7 %copy-start.3 = (f32[1280]{0:T(1024)S(1)}, f32[1280]{0:T(1024)}, u32[]{:S(2)}) copy-start(f32[1280]{0:T(1024)} %gain_ref.1) | copy-start | bytes 15364
  17.5 10.8 %collective-permute-start.12 = (bf16[2,800,128]{2,1,0:T(8,128)(2,1)S(1)}, bf16[2,800,128]{2,1,0:T(8,128)(2,1)S(1)}, u32[]{:S(2)}, u32[]{:S(2)}) collective-permute-start(bf16[2,800,128]{2,1,0:T(8,128)(2,1)S(1)} %pad_maximum_fusion.1), channel_id=1, source_target_pairs={{0,8},{4,12},{8,0},{12,4},{1,9},{5,13},{9,1},{13,5},{2,10},{6,14},... | collective-permute-start | bytes 1228808 | tf_op jit(solution)/shard_map/ppermute | solution.py:26
  18.0 3.3 %collective-permute-start.8 = (bf16[800,128]{1,0:T(8,128)(2,1)S(1)}, bf16[800,128]{1,0:T(8,128)(2,1)S(1)}, u32[]{:S(2)}, u32[]{:S(2)}) collective-permute-start(bf16[800,128]{1,0:T(8,128)(2,1)S(1)} %collective-permute-done.4.refs_3_), channel_id=1, source_target_pairs={{0,4},{4,0},{8,12},{12,8},{1,5},{5,1},{9,13},{13,9},{2,6},{6,2},{1... | collective-permute-start | bytes 614408 | tf_op jit(solution)/shard_map/ppermute | solution.py:26
  18.2 3.1 %collective-permute-start.9 = (bf16[800,128]{1,0:T(8,128)(2,1)S(1)}, bf16[800,128]{1,0:T(8,128)(2,1)S(1)}, u32[]{:S(2)}, u32[]{:S(2)}) collective-permute-start(bf16[800,128]{1,0:T(8,128)(2,1)S(1)} %collective-permute-done.5.refs_4_), channel_id=1, source_target_pairs={{0,4},{4,0},{8,12},{12,8},{1,5},{5,1},{9,13},{13,9},{2,6},{6,2},{1... | collective-permute-start | bytes 614408 | tf_op jit(solution)/shard_map/ppermute | solution.py:26
  19.8 7.7 %collective-permute-start.11 = (bf16[800,128]{1,0:T(8,128)(2,1)S(1)}, bf16[800,128]{1,0:T(8,128)(2,1)S(1)}, u32[]{:S(2)}, u32[]{:S(2)}) collective-permute-start(bf16[800,128]{1,0:T(8,128)(2,1)S(1)} %collective-permute-done.10.refs_6_), channel_id=1, source_target_pairs={{0,16},{16,0},{1,17},{17,1},{2,18},{18,2},{3,19},{19,3},{4,20},{20... | collective-permute-start | bytes 614408 | tf_op jit(solution)/shard_map/ppermute | solution.py:26
  27.6 18.7 %copy-start.4 = (f32[1280]{0:T(1024)S(1)}, f32[1280]{0:T(1024)}, u32[]{:S(2)}) copy-start(f32[1280]{0:T(1024)} %refs_14_.1) | copy-start | bytes 15364
  28.3 16.2 %collective-permute-start.16 = (bf16[2,800,128]{2,1,0:T(8,128)(2,1)S(1)}, bf16[2,800,128]{2,1,0:T(8,128)(2,1)S(1)}, u32[]{:S(2)}, u32[]{:S(2)}) collective-permute-start(bf16[2,800,128]{2,1,0:T(8,128)(2,1)S(1)} %pad_maximum_fusion.2), channel_id=1, source_target_pairs={{0,8},{4,12},{8,0},{12,4},{1,9},{5,13},{9,1},{13,5},{2,10},{6,14},... | collective-permute-start | bytes 1228808 | tf_op jit(solution)/shard_map/ppermute | solution.py:26
  30.0 14.6 %collective-permute-start.17 = (bf16[4,800,128]{2,1,0:T(8,128)(2,1)S(1)}, bf16[4,800,128]{2,1,0:T(8,128)(2,1)S(1)}, u32[]{:S(2)}, u32[]{:S(2)}) collective-permute-start(bf16[4,800,128]{2,1,0:T(8,128)(2,1)S(1)} %pad_maximum_fusion), channel_id=1, source_target_pairs={{0,4},{4,0},{8,12},{12,8},{1,5},{5,1},{9,13},{13,9},{2,6},{6,2},{1... | collective-permute-start | bytes 2457608 | tf_op jit(solution)/shard_map/ppermute | solution.py:26
  30.0 8.0 %collective-permute-start.13 = (bf16[480,128]{1,0:T(8,128)(2,1)S(1)}, bf16[480,128]{1,0:T(8,128)(2,1)S(1)}, u32[]{:S(2)}, u32[]{:S(2)}) collective-permute-start(bf16[480,128]{1,0:T(8,128)(2,1)S(1)} %get-tuple-element.57), channel_id=1, source_target_pairs={{0,1},{1,0},{2,3},{3,2},{4,5},{5,4},{6,7},{7,6},{8,9},{9,8},{10,11... | collective-permute-start | bytes 368648 | tf_op jit(solution)/shard_map/ppermute | solution.py:26
  32.1 12.4 %collective-permute-start.14 = (bf16[480,128]{1,0:T(8,128)(2,1)S(1)}, bf16[480,128]{1,0:T(8,128)(2,1)S(1)}, u32[]{:S(2)}, u32[]{:S(2)}) collective-permute-start(bf16[480,128]{1,0:T(8,128)(2,1)S(1)} %get-tuple-element.58), channel_id=1, source_target_pairs={{0,2},{1,3},{2,0},{3,1},{4,6},{5,7},{6,4},{7,5},{8,10},{9,11},{10,... | collective-permute-start | bytes 368648 | tf_op jit(solution)/shard_map/ppermute | solution.py:26
  34.7 9.8 %collective-permute-start.15 = (bf16[480,128]{1,0:T(8,128)(2,1)S(1)}, bf16[480,128]{1,0:T(8,128)(2,1)S(1)}, u32[]{:S(2)}, u32[]{:S(2)}) collective-permute-start(bf16[480,128]{1,0:T(8,128)(2,1)S(1)} %get-tuple-element.59), channel_id=1, source_target_pairs={{0,3},{1,2},{2,1},{3,0},{4,7},{5,6},{6,5},{7,4},{8,11},{9,10},{10,... | collective-permute-start | bytes 368648 | tf_op jit(solution)/shard_map/ppermute | solution.py:26
  38.0 6.5 %collective-permute-start.18 = (bf16[2,800,128]{2,1,0:T(8,128)(2,1)S(1)}, bf16[2,800,128]{2,1,0:T(8,128)(2,1)S(1)}, u32[]{:S(2)}, u32[]{:S(2)}) collective-permute-start(bf16[2,800,128]{2,1,0:T(8,128)(2,1)S(1)} %collective-permute-done.12.refs_9_), channel_id=1, source_target_pairs={{0,4},{4,0},{8,12},{12,8},{1,5},{5,1},{9,13},{13,9},{2,6},{6,2},{1... | collective-permute-start | bytes 1228808 | tf_op jit(solution)/shard_map/ppermute | solution.py:26
  44.5 1.7 %collective-permute-start.19 = (bf16[2,800,128]{2,1,0:T(8,128)(2,1)S(1)}, bf16[2,800,128]{2,1,0:T(8,128)(2,1)S(1)}, u32[]{:S(2)}, u32[]{:S(2)}) collective-permute-start(bf16[2,800,128]{2,1,0:T(8,128)(2,1)S(1)} %collective-permute-done.16.refs_10_), channel_id=1, source_target_pairs={{0,4},{4,0},{8,12},{12,8},{1,5},{5,1},{9,13},{13,9},{2,6},{6,2},{1... | collective-permute-start | bytes 1228808 | tf_op jit(solution)/shard_map/ppermute | solution.py:26
  46.3 2.4 %copy-start.5 = (s32[192]{0:T(256)S(1)}, s32[192]{0:T(256)}, u32[]{:S(2)}) copy-start(s32[192]{0:T(256)} %param.9) | copy-start | bytes 2308
  48.2 14.9 %collective-permute-start.21 = (bf16[192,1280]{1,0:T(8,128)(2,1)S(1)}, bf16[192,1280]{1,0:T(8,128)(2,1)S(1)}, u32[]{:S(2)}, u32[]{:S(2)}) collective-permute-start(bf16[192,1280]{1,0:T(8,128)(2,1)S(1)} %project.1.refs_2_), channel_id=1, source_target_pairs={{0,4},{4,0},{8,12},{12,8},{1,5},{5,1},{9,13},{13,9},{2,6},{6,2},{1... | collective-permute-start | bytes 1474568 | tf_op jit(solution)/shard_map/ppermute | solution.py:26
  48.4 15.7 %collective-permute-start.20 = (bf16[192,1280]{1,0:T(8,128)(2,1)S(1)}, bf16[192,1280]{1,0:T(8,128)(2,1)S(1)}, u32[]{:S(2)}, u32[]{:S(2)}) collective-permute-start(bf16[192,1280]{1,0:T(8,128)(2,1)S(1)} %project.1.refs_2_), channel_id=1, source_target_pairs={{0,8},{4,12},{8,0},{12,4},{1,9},{5,13},{9,1},{13,5},{2,10},{6,14},... | collective-permute-start | bytes 1474568 | tf_op jit(solution)/shard_map/ppermute | solution.py:26
  48.7 13.3 %collective-permute-start = (s32[1,192]{1,0:T(1,128)S(1)}, s32[1,192]{1,0:T(1,128)S(1)}, u32[]{:S(2)}, u32[]{:S(2)}) collective-permute-start(s32[1,192]{1,0:T(1,128)S(1)} %bitcast.25), channel_id=1, source_target_pairs={{0,8},{4,12},{8,0},{12,4},{1,9},{5,13},{9,1},{13,5},{2,10},{6,14},... | collective-permute-start | bytes 2312 | tf_op jit(solution)/shard_map/ppermute | solution.py:26
  62.0 1.2 %collective-permute-start.1 = (s32[2,1,192]{2,1,0:T(1,128)S(1)}, s32[2,1,192]{2,1,0:T(1,128)S(1)}, u32[]{:S(2)}, u32[]{:S(2)}) collective-permute-start(s32[2,1,192]{2,1,0:T(1,128)S(1)} %pad_add_fusion), channel_id=1, source_target_pairs={{0,4},{4,0},{8,12},{12,8},{1,5},{5,1},{9,13},{13,9},{2,6},{6,2},{1... | collective-permute-start | bytes 4616 | tf_op jit(solution)/shard_map/ppermute | solution.py:26
  64.2 1.9 %collective-permute-start.22 = (bf16[192,1280]{1,0:T(8,128)(2,1)S(1)}, bf16[192,1280]{1,0:T(8,128)(2,1)S(1)}, u32[]{:S(2)}, u32[]{:S(2)}) collective-permute-start(bf16[192,1280]{1,0:T(8,128)(2,1)S(1)} %collective-permute-done.20.refs_2_), channel_id=1, source_target_pairs={{0,4},{4,0},{8,12},{12,8},{1,5},{5,1},{9,13},{13,9},{2,6},{6,2},{1... | collective-permute-start | bytes 1474568 | tf_op jit(solution)/shard_map/ppermute | solution.py:26

commit v16 on v15

--- a/solution.py
+++ b/solution.py
@@ -78,15 +78,47 @@
 
 def unpack(p, rows, cols):
     if not packs(rows, cols):
-        return p[:, : 2 * LANES], p[:, 2 * LANES :]
-    tail = p[2 * rows :]
+        return p[:rows, : 2 * LANES], p[:rows, 2 * LANES :]
+    tail = p[2 * rows : 5 * rows // 2]
     rest = jnp.concatenate([tail[:, : LANES // 2], tail[:, LANES // 2 :]], axis=0)
     return jnp.concatenate([p[:rows], p[rows : 2 * rows]], axis=1), rest
 
 
-def pack_kernel(index_ref, qkv_ref, first_ref, value_ref, all_ref):
+NOTE = 16
+
+
+def write_note(place, lanes):
+    count = place.shape[1]
+    filled = []
+    for digit in (place >> 6, place & 63):
+        for at in range(0, count, lanes):
+            part = digit[:, at : at + lanes].astype(F32)
+            spare = lanes - part.shape[1]
+            filled.append(jnp.concatenate([part, jnp.zeros((1, spare), F32)], axis=1) if spare else part)
+    filled.append(jnp.zeros((NOTE - len(filled), lanes), F32))
+    return jnp.concatenate(filled, axis=0).astype(BF16)
+
+
+def read_note(ref, count):
+    note = ref[ref.shape[0] - NOTE :, :].astype(F32)
+    lanes = note.shape[1]
+    lines = -(-count // lanes)
+    digits = []
+    for d in range(2):
+        parts = [
+            note[d * lines + i : d * lines + i + 1, : min(lanes, count - i * lanes)]
+            for i in range(lines)
+        ]
+        digits.append(parts[0] if lines == 1 else jnp.concatenate(parts, axis=1))
+    return digits[0] * 64 + digits[1]
+
+
+def pack_kernel(index_ref, qkv_ref, place_ref, first_ref, value_ref, all_ref):
+    note = write_note(place_ref[...], all_ref.shape[2])
+    count = all_ref.shape[1] - NOTE
     for j in range(3):
-        all_ref[j] = pack(qkv_ref[j])
+        all_ref[j, :count, :] = pack(qkv_ref[j])
+        all_ref[j, count:, :] = note
     first_ref[...] = all_ref[index_ref[2]]
     value_ref[...] = all_ref[2]
 
@@ -191,7 +223,7 @@
 
 
 def project_kernel(n_ctx, width, col, index_ref, *refs):
-    *blocks, own_ref, gain_ref, out_ref, part_ref = refs[4:]
+    *blocks, own_ref, gain_ref, low_ref, high_ref, part_ref = refs[4:]
     rows = own_ref.shape[0]
     mixes = [unpack(m[...], rows, width) for m in refs[:4]]
     flip = index_ref[2] > 0
@@ -227,19 +259,24 @@
     total = total + own_ref[...].astype(F32)
     mean_sq = jnp.mean(total * total, axis=-1, keepdims=True)
     gain = gain_ref[...].reshape(1, -1)
-    out_ref[...] = (total * lax.rsqrt(mean_sq + 1e-06) * gain).astype(BF16)
+    normed = (total * lax.rsqrt(mean_sq + 1e-06) * gain).astype(BF16)
+    half = low_ref.shape[0]
+    low_ref[...] = normed[:half]
+    high_ref[...] = normed[half:]
 
 
 def place_kernel(count, index_ref, *refs):
     place_refs = refs[:count]
-    row_refs = refs[count : 2 * count]
-    before = refs[2 * count : -1]
+    row_refs = refs[count : 3 * count]
+    before = refs[3 * count : -1]
     out_ref = refs[-1]
     spots = out_ref.shape[0]
     chosen = []
+    base = (index_ref[0] * spots).astype(F32)
     for place_ref in place_refs:
-        target = place_ref[...] - index_ref[0] * spots
-        grid = lax.broadcasted_iota(jnp.int32, (spots, target.shape[1]), 0)
+        note_ref = place_ref.at[0] if len(place_ref.shape) == 3 else place_ref
+        target = read_note(note_ref, spots) - base
+        grid = lax.broadcasted_iota(jnp.int32, (spots, spots), 0).astype(F32)
         chosen.append(one_hot(grid == target))
     total = jnp.dot(
         jnp.concatenate(chosen, axis=1),
@@ -247,7 +284,7 @@
         preferred_element_type=F32,
     )
     for ref in before:
-        total = total + ref[...]
+        total = total + ref[...].astype(F32)
     out_ref[...] = total.astype(out_ref.dtype)
 
 
@@ -268,15 +305,16 @@
         return swap(x, "context", n_ctx, 1)
 
     third = packed_shape(depth, width)
+    third = (third[0] + NOTE, third[1])
     piece = packed_shape(width, col)
     first, value, own = pl.pallas_call(
         pack_kernel,
         out_shape=(shape(*third), shape(*third), shape(3, *third)),
-        in_specs=[SMEM, VMEM],
+        in_specs=[SMEM, VMEM, VMEM],
         out_specs=(VMEM,) * 3,
         compiler_params=params(8),
         name="pack",
-    )(index, jnp.transpose(w_qkv, (1, 0, 2)))
+    )(index, jnp.transpose(w_qkv, (1, 0, 2)), place.reshape(1, groups))
     w_proj = pl.pallas_call(
         pack_proj_kernel,
         out_shape=shape(*piece),
@@ -336,48 +374,47 @@
         name="attention",
     )(index, hidden, valid.reshape(rows // PAIR, PAIR), *shard_list)
 
-    mixed, far, far2, low = together(mixed, far, far2, low)
-    received = {s: swap(mixed[s], "tensor", n_ten, s) for s in (2, 3, 1)}
-    mixed = [mixed[0]] + [received[s] for s in range(1, n_ten)]
+    mixed, far, far2, low = together(list(mixed), far, far2, low)
+    received = [mixed[0]] + [swap(mixed[s], "tensor", n_ten, s) for s in range(1, n_ten)]
     high = gather_cross(jnp.stack([far, far2]), n_ctx)
     blocks = [w_proj, by_one, far, far2, over_core(jnp.stack([w_proj, by_one, far, far2]))]
     low_twin = {k: over_core(low[k]) for k in cross}
-    mixed, high = together(mixed, high)
+    received, high = together(received, high)
     for k in cross:
         blocks += [low[k], high[k], low_twin[k], over_core(high[k])]
     done = pl.pallas_call(
         functools.partial(project_kernel, n_ctx, width, col),
-        out_shape=shape(groups, feat),
+        out_shape=(shape(groups // 2, feat),) * 2,
         in_specs=[SMEM] + [VMEM] * (n_ten + len(blocks) + 2),
-        out_specs=VMEM,
+        out_specs=(VMEM,) * 2,
         scratch_shapes=[pltpu.VMEM((n_ctx, groups, col), F32)],
         compiler_params=params(24),
         name="project",
-    )(index, *mixed, *blocks, own_patches, gain_merge)
-
-    crossed = gather_cross(done, n_ctx)
-    near_rows = over_core(done)
-    places = gather_cross(place.reshape(1, groups), n_ctx)
-    place_twin = over_core(jnp.stack([places[k] for k in (0, *cross)]))
-
-    def put(ids, rows_in, before, dtype, name):
+    )(index, *received, *blocks, own_patches, gain_merge)
+
+    crossed = [gather_cross(x, n_ctx) for x in done]
+    near_rows = [over_core(x) for x in done]
+
+    def put(ids, rows_in, before, name):
         return pl.pallas_call(
             functools.partial(place_kernel, len(ids)),
-            out_shape=jax.ShapeDtypeStruct((groups, feat), dtype),
-            in_specs=[SMEM] + [VMEM] * (2 * len(ids) + len(before)),
+            out_shape=shape(groups, feat),
+            in_specs=[SMEM] + [VMEM] * (3 * len(ids) + len(before)),
             out_specs=VMEM,
             compiler_params=params(24),
             name=name,
         )(index, *ids, *rows_in, *before)
 
-    total = put([places[0], place_twin[0]], [done, near_rows], [], F32, "placement0")
+    total = put([own, twin], [*done, *near_rows], [], "placement0")
+    last = []
     for k in cross:
-        crossed[k], total = together(crossed[k], total)
-        crossed[k ^ 1] = over_core(crossed[k])
+        crossed[0][k], crossed[1][k], total = together(crossed[0][k], crossed[1][k], total)
+        twins = [over_core(x[k]) for x in crossed]
+        last += [crossed[0][k], crossed[1][k], *twins]
     ids = []
-    for i, k in enumerate(cross):
-        ids += [places[k], place_twin[1 + i]]
-    return put(ids, [crossed[k] for k in range(2, n_ctx)], [total], BF16, "placement1")
+    for k in cross:
+        ids += [first[k], first_twin[k]]
+    return put(ids, last, [total], "placement1")
 
 
 def solution(mesh):

time: 68.1 us -> 66.7 us (0.979)
  waiting for transfers between devices: 29.2 us -> 26.3 us
  starting transfers between devices: 20.6 us -> 21.4 us
    ppermute x22 -> x23, waiting for transfers between devices: 27.9 us -> 25 us  [swap(): return lax.ppermute(x, axis, [(i, i ^ bit) for i in range(size)])]
    ppermute x22 -> x23, starting transfers between devices: 18 us -> 18.8 us  [swap(): return lax.ppermute(x, axis, [(i, i ^ bit) for i in range(size)])]
  transfers between devices with their start and end apart: 23 -> 24, of which waited for: 9 -> 10; matrix products, arithmetic and copies ran while one was open for 0% -> 0% of each run, Pallas kernels for 13% -> 13%
where the time goes in v16:
time: 66.7 us; the launch traced here: 66.5 us
  waiting for transfers between devices  26.3 us (39%)
  starting transfers between devices  21.4 us (32%)
  Pallas kernels  13.4 us (20%)
  local copies, waits for them, and re-layouts  4.99 us (7%)
    ppermute x23, waiting for transfers between devices, swap(): return lax.ppermute(x, axis, [(i, i ^ bit) for i in range(size)])  25 us
    ppermute x23, starting transfers between devices, swap(): return lax.ppermute(x, axis, [(i, i ^ bit) for i in range(size)])  18.8 us
    pallas_call x1, Pallas kernels, local(): pl.pallas_call(functools.partial(attention_kernel, n_ctx, width), out_sha...  6.32 us
    unnamed x14, local copies, waits for them, and re-layouts  4.99 us
    pallas_call x2, Pallas kernels, put(): pl.pallas_call(functools.partial(place_kernel, len(ids)), out_shape=shape...  2.79 us
    ppermute x1, starting transfers between devices, local(): lax.ppermute(w_proj, ('dp', 'tensor'), [(d * n_ten + t, d * n_ten + (t ^...  2.59 us
    pallas_call x1, Pallas kernels, local(): pl.pallas_call(functools.partial(project_kernel, n_ctx, width, col), out_...  1.92 us
    pallas_call x1, Pallas kernels, local(): pl.pallas_call(norm_kernel, out_shape=(shape(rows, feat), shape(groups, f...  1.56 us
  transfers between devices with their start and end apart: 24, of which 10 were waited for; matrix products, arithmetic and copies ran while one was open for 0% of the time, Pallas kernels for 13%

profile of v16, /device:TPU:0, one launch (start us, length us, event | category | flops | bytes accessed | tf_op | source)
XLA Modules:
  0.0 66.5 jit_solution(3031896010120960662)
XLA Ops:
  0.1 1.1 %copy-done.1 = bf16[320,3,320]{2,0,1:T(8,128)(2,1)S(1)} copy-done((bf16[320,3,320]{2,0,1:T(8,128)(2,1)S(1)}, bf16[320,3,320]{2,0,1:T(8,128)(2,1)}, u32[]{:S(2)}) %copy-start.1) | copy-done | bytes 614424
  1.2 0.7 %copy-done.6 = s32[192]{0:T(256)S(1)} copy-done((s32[192]{0:T(256)S(1)}, s32[192]{0:T(256)}, u32[]{:S(2)}) %copy-start.6) | copy-done | bytes 792
  1.9 0.7 %pack.1 = (bf16[816,128]{1,0:T(8,128)(2,1)S(1)}, bf16[816,128]{1,0:T(8,128)(2,1)S(1)}, bf16[3,816,128]{2,1,0:T(8,128)(2,1)S(1)}) custom-call(s32[3]{0:T(128)S(1)} %pad_add_fusion.index_ref, bf16[3,320,320]{2,1,0:T(8,128)(2,1)S(1)} %bitcast.18, s32[1,192]{1,0:T(1,128)S(1)} %bitcast.20), custom_call_target="tpu_custom_call" | custom-call | tf_op jit(solution)/shard_map/pack/pallas_call | solution.py:310
  2.6 0.5 collective-permute-start.1
  3.1 2.6 %collective-permute-start = (bf16[816,128]{1,0:T(8,128)(2,1)S(1)}, bf16[816,128]{1,0:T(8,128)(2,1)S(1)}, u32[]{:S(2)}, u32[]{:S(2)}) collective-permute-start(bf16[816,128]{1,0:T(8,128)(2,1)S(1)} %get-tuple-element.41), channel_id=1, source_target_pairs={{0,8},{4,12},{8,0},{12,4},{1,9},{5,13},{9,1},{13,5},{2,10},{6,14},... | collective-permute-start | bytes 626696 | tf_op jit(solution)/shard_map/ppermute | solution.py:26
  5.7 0.9 %copy-done.2 = bf16[320,320]{1,0:T(8,128)(2,1)S(1)} copy-done((bf16[320,320]{1,0:T(8,128)(2,1)S(1)}, bf16[320,320]{1,0:T(8,128)(2,1)}, u32[]{:S(2)}) %copy-start.2) | copy-done | bytes 204824
  6.7 1.6 %collective-permute-start.5 = (bf16[800,128]{1,0:T(8,128)(2,1)S(1)}, bf16[800,128]{1,0:T(8,128)(2,1)S(1)}, u32[]{:S(2)}, u32[]{:S(2)}) collective-permute-start(bf16[800,128]{1,0:T(8,128)(2,1)S(1)} %pack_proj.1.refs_4_), channel_id=1, source_target_pairs={{0,1},{1,0},{2,3},{3,2},{4,5},{5,4},{6,7},{7,6},{8,9},{9,8},{10,11... | collective-permute-start | bytes 614408 | tf_op jit(solution)/shard_map/ppermute | solution.py:26
  8.3 2.6 %collective-permute-start.8 = (bf16[800,128]{1,0:T(8,128)(2,1)S(1)}, bf16[800,128]{1,0:T(8,128)(2,1)S(1)}, u32[]{:S(2)}, u32[]{:S(2)}) collective-permute-start(bf16[800,128]{1,0:T(8,128)(2,1)S(1)} %pack_proj.1.refs_4_), channel_id=1, source_target_pairs={{0,2},{1,3},{2,0},{3,1},{16,19},{17,18},{18,17},{19,16},{4,6},{5,7... | collective-permute-start | bytes 614408 | tf_op jit(solution)/shard_map/ppermute | solution.py:329
  10.9 0.5 collective-permute-start.3
  11.4 1.7 %collective-permute-start.2 = (bf16[816,128]{1,0:T(8,128)(2,1)S(1)}, bf16[816,128]{1,0:T(8,128)(2,1)S(1)}, u32[]{:S(2)}, u32[]{:S(2)}) collective-permute-start(bf16[816,128]{1,0:T(8,128)(2,1)S(1)} %collective-permute-done.refs_2_.refs_0_), channel_id=1, source_target_pairs={{0,16},{16,0},{1,17},{17,1},{2,18},{18,2},{3,19},{19,3},{4,20},{20... | collective-permute-start | bytes 626696 | tf_op jit(solution)/shard_map/ppermute | solution.py:26
  13.2 1.5 %copy-done = bf16[768,1280]{1,0:T(8,128)(2,1)S(1)} copy-done((bf16[768,1280]{1,0:T(8,128)(2,1)S(1)}, bf16[768,1280]{1,0:T(8,128)(2,1)}, u32[]{:S(2)}) %copy-start) | copy-done | bytes 1966104
  14.7 0.7 %copy-done.3 = f32[1280]{0:T(1024)S(1)} copy-done((f32[1280]{0:T(1024)S(1)}, f32[1280]{0:T(1024)}, u32[]{:S(2)}) %copy-start.3) | copy-done | bytes 5144
  15.4 1.6 %norm.1 = (bf16[768,1280]{1,0:T(8,128)(2,1)S(1)}, bf16[192,1280]{1,0:T(8,128)(2,1)S(1)}) custom-call(s32[3]{0:T(128)S(1)} %pad_add_fusion.index_ref, bf16[768,1280]{1,0:T(8,128)(2,1)S(1)} %copy-done, f32[1280]{0:T(1024)S(1)} %copy-done.3), custom_call_target="tpu_custom_call" | custom-call | tf_op jit(solution)/shard_map/norm/pallas_call | solution.py:343
  17.0 1.2 %collective-permute-done.5.refs_5_ = bf16[800,128]{1,0:T(8,128)(2,1)S(1)} collective-permute-done((bf16[800,128]{1,0:T(8,128)(2,1)S(1)}, bf16[800,128]{1,0:T(8,128)(2,1)S(1)}, u32[]{:S(2)}, u32[]{:S(2)}) %collective-permute-start.5) | collective-permute-done | bytes 204832 | tf_op jit(solution)/shard_map/ppermute | solution.py:26
  19.2 1.3 %collective-permute-done.8.refs_6_ = bf16[800,128]{1,0:T(8,128)(2,1)S(1)} collective-permute-done((bf16[800,128]{1,0:T(8,128)(2,1)S(1)}, bf16[800,128]{1,0:T(8,128)(2,1)S(1)}, u32[]{:S(2)}, u32[]{:S(2)}) %collective-permute-start.8) | collective-permute-done | bytes 204832 | tf_op jit(solution)/shard_map/ppermute | solution.py:329
  20.5 1.4 %collective-permute-start.9 = (bf16[800,128]{1,0:T(8,128)(2,1)S(1)}, bf16[800,128]{1,0:T(8,128)(2,1)S(1)}, u32[]{:S(2)}, u32[]{:S(2)}) collective-permute-start(bf16[800,128]{1,0:T(8,128)(2,1)S(1)} %collective-permute-done.8.refs_6_), channel_id=1, source_target_pairs={{0,16},{16,0},{1,17},{17,1},{2,18},{18,2},{3,19},{19,3},{4,20},{20... | collective-permute-start | bytes 614408 | tf_op jit(solution)/shard_map/ppermute | solution.py:26
  21.9 6.3 %attention.1 = (bf16[480,128]{1,0:T(8,128)(2,1)S(1)}, bf16[480,128]{1,0:T(8,128)(2,1)S(1)}, bf16[480,128]{1,0:T(8,128)(2,1)S(1)}, bf16[480,128]{1,0:T(8,128)(2,1)S(1)}) custom-call(s32[3]{0:T(128)S(1)} %pad_add_fusion.index_ref, bf16[768,1280]{1,0:T(8,128)(2,1)S(1)} %get-tuple-element.49.hidden_ref, s32[6,128]{1,0:T(8,128)S(1)} %bitcast.19, ...), custom_call_target="tpu_custom_call" | custom-call | tf_op jit(solution)/shard_map/attention/pallas_call | solution.py:365
  28.3 0.7 %collective-permute-done.10.refs_9_ = bf16[2,800,128]{2,1,0:T(8,128)(2,1)S(1)} collective-permute-done((bf16[2,800,128]{2,1,0:T(8,128)(2,1)S(1)}, bf16[2,800,128]{2,1,0:T(8,128)(2,1)S(1)}, u32[]{:S(2)}, u32[]{:S(2)}) %collective-permute-start.10) | collective-permute-done | bytes 409632 | tf_op jit(solution)/shard_map/ppermute | solution.py:26
  29.0 1.6 %collective-permute-start.14 = (bf16[2,800,128]{2,1,0:T(8,128)(2,1)S(1)}, bf16[2,800,128]{2,1,0:T(8,128)(2,1)S(1)}, u32[]{:S(2)}, u32[]{:S(2)}) collective-permute-start(bf16[2,800,128]{2,1,0:T(8,128)(2,1)S(1)} %pad_maximum_fusion.2), channel_id=1, source_target_pairs={{0,8},{4,12},{8,0},{12,4},{1,9},{5,13},{9,1},{13,5},{2,10},{6,14},... | collective-permute-start | bytes 1228808 | tf_op jit(solution)/shard_map/ppermute | solution.py:26
  30.8 2.1 %collective-permute-start.11 = (bf16[480,128]{1,0:T(8,128)(2,1)S(1)}, bf16[480,128]{1,0:T(8,128)(2,1)S(1)}, u32[]{:S(2)}, u32[]{:S(2)}) collective-permute-start(bf16[480,128]{1,0:T(8,128)(2,1)S(1)} %get-tuple-element.60), channel_id=1, source_target_pairs={{0,1},{1,0},{2,3},{3,2},{4,5},{5,4},{6,7},{7,6},{8,9},{9,8},{10,11... | collective-permute-start | bytes 368648 | tf_op jit(solution)/shard_map/ppermute | solution.py:26
  32.9 2.6 %collective-permute-start.12 = (bf16[480,128]{1,0:T(8,128)(2,1)S(1)}, bf16[480,128]{1,0:T(8,128)(2,1)S(1)}, u32[]{:S(2)}, u32[]{:S(2)}) collective-permute-start(bf16[480,128]{1,0:T(8,128)(2,1)S(1)} %get-tuple-element.61), channel_id=1, source_target_pairs={{0,2},{1,3},{2,0},{3,1},{4,6},{5,7},{6,4},{7,5},{8,10},{9,11},{10,... | collective-permute-start | bytes 368648 | tf_op jit(solution)/shard_map/ppermute | solution.py:26
  35.5 3.3 %collective-permute-done.11.refs_1_ = bf16[480,128]{1,0:T(8,128)(2,1)S(1)} collective-permute-done((bf16[480,128]{1,0:T(8,128)(2,1)S(1)}, bf16[480,128]{1,0:T(8,128)(2,1)S(1)}, u32[]{:S(2)}, u32[]{:S(2)}) %collective-permute-start.11) | collective-permute-done | bytes 122912 | tf_op jit(solution)/shard_map/ppermute | solution.py:26
  38.8 6.5 %collective-permute-done.12.refs_2_ = bf16[480,128]{1,0:T(8,128)(2,1)S(1)} collective-permute-done((bf16[480,128]{1,0:T(8,128)(2,1)S(1)}, bf16[480,128]{1,0:T(8,128)(2,1)S(1)}, u32[]{:S(2)}, u32[]{:S(2)}) %collective-permute-start.12) | collective-permute-done | bytes 122912 | tf_op jit(solution)/shard_map/ppermute | solution.py:26
  45.3 1.7 %collective-permute-done.17.refs_12_ = bf16[2,800,128]{2,1,0:T(8,128)(2,1)S(1)} collective-permute-done((bf16[2,800,128]{2,1,0:T(8,128)(2,1)S(1)}, bf16[2,800,128]{2,1,0:T(8,128)(2,1)S(1)}, u32[]{:S(2)}, u32[]{:S(2)}) %collective-permute-start.17) | collective-permute-done | bytes 409632 | tf_op jit(solution)/shard_map/ppermute | solution.py:26
  47.0 1.9 %project.1 = (bf16[96,1280]{1,0:T(8,128)(2,1)S(1)}, bf16[96,1280]{1,0:T(8,128)(2,1)S(1)}) custom-call(s32[3]{0:T(128)S(1)} %pad_add_fusion.index_ref, bf16[480,128]{1,0:T(8,128)(2,1)S(1)} %get-tuple-element.65.refs_0_, bf16[480,128]{1,0:T(8,128)(2,1)S(1)} %collective-permute-done.11.refs_1_, bf16[480,128]{1,0:T(8,128)(2,1)S(1)} %collective-permute-done.12.refs_2_, ...), custom_call_target="tpu_custom_call" | custom-call | tf_op jit(solution)/shard_map/project/pallas_call | solution.py:385
  49.8 1.8 %collective-permute-start.19 = (bf16[96,1280]{1,0:T(8,128)(2,1)S(1)}, bf16[96,1280]{1,0:T(8,128)(2,1)S(1)}, u32[]{:S(2)}, u32[]{:S(2)}) collective-permute-start(bf16[96,1280]{1,0:T(8,128)(2,1)S(1)} %get-tuple-element.73.refs_3_), channel_id=1, source_target_pairs={{0,8},{4,12},{8,0},{12,4},{1,9},{5,13},{9,1},{13,5},{2,10},{6,14},... | collective-permute-start | bytes 737288 | tf_op jit(solution)/shard_map/ppermute | solution.py:26
  51.6 1.0 %placement0.1.refs_6_ = bf16[192,1280]{1,0:T(8,128)(2,1)S(1)} custom-call(s32[3]{0:T(128)S(1)} %pad_add_fusion.index_ref, bf16[3,816,128]{2,1,0:T(8,128)(2,1)S(1)} %get-tuple-element.42.refs_0_, bf16[3,816,128]{2,1,0:T(8,128)(2,1)S(1)} %collective-permute-done.1.refs_1_, bf16[96,1280]{1,0:T(8,128)(2,1)S(1)} %get-tuple-element.72.refs_2_, ...), custom_call_target="tpu_custom_call" | custom-call | tf_op jit(solution)/shard_map/placement0/pallas_call | solution.py:399
  52.6 5.8 %collective-permute-done.18.refs_2_ = bf16[96,1280]{1,0:T(8,128)(2,1)S(1)} collective-permute-done((bf16[96,1280]{1,0:T(8,128)(2,1)S(1)}, bf16[96,1280]{1,0:T(8,128)(2,1)S(1)}, u32[]{:S(2)}, u32[]{:S(2)}) %collective-permute-start.18) | collective-permute-done | bytes 245792 | tf_op jit(solution)/shard_map/ppermute | solution.py:26
  58.3 4.5 %collective-permute-done.19.refs_3_ = bf16[96,1280]{1,0:T(8,128)(2,1)S(1)} collective-permute-done((bf16[96,1280]{1,0:T(8,128)(2,1)S(1)}, bf16[96,1280]{1,0:T(8,128)(2,1)S(1)}, u32[]{:S(2)}, u32[]{:S(2)}) %collective-permute-start.19) | collective-permute-done | bytes 245792 | tf_op jit(solution)/shard_map/ppermute | solution.py:26
  62.8 0.5 collective-permute-start.23
  63.3 1.0 %collective-permute-done.22.refs_4_ = bf16[96,1280]{1,0:T(8,128)(2,1)S(1)} collective-permute-done((bf16[96,1280]{1,0:T(8,128)(2,1)S(1)}, bf16[96,1280]{1,0:T(8,128)(2,1)S(1)}, u32[]{:S(2)}, u32[]{:S(2)}) %collective-permute-start.22) | collective-permute-done | bytes 245792 | tf_op jit(solution)/shard_map/ppermute | solution.py:26
  64.7 1.8 %placement1.1 = bf16[192,1280]{1,0:T(8,128)(2,1)} custom-call(s32[3]{0:T(128)S(1)} %pad_add_fusion.index_ref, bf16[816,128]{1,0:T(8,128)(2,1)S(1)} %collective-permute-done.refs_2_.refs_0_, bf16[816,128]{1,0:T(8,128)(2,1)S(1)} %collective-permute-done.4.refs_5_.refs_1_, bf16[96,1280]{1,0:T(8,128)(2,1)S(1)} %collective-permute-done.18.refs_2_, ...), custom_call_target="tpu_custom_call" | custom-call | tf_op jit(solution)/shard_map/placement1/pallas_call | solution.py:399
  (41 shorter events, 2.6 us)
Async XLA Ops:
  0.1 1.1 %copy-start.1 = (bf16[320,3,320]{2,0,1:T(8,128)(2,1)S(1)}, bf16[320,3,320]{2,0,1:T(8,128)(2,1)}, u32[]{:S(2)}) copy-start(bf16[320,3,320]{2,0,1:T(8,128)(2,1)} %param.11) | copy-start | bytes 1843204
  1.2 0.7 %copy-start.6 = (s32[192]{0:T(256)S(1)}, s32[192]{0:T(256)}, u32[]{:S(2)}) copy-start(s32[192]{0:T(256)} %param.9) | copy-start | bytes 2308
  1.9 20.0 %copy-start.5 = (s32[768]{0:T(1024)S(1)}, s32[768]{0:T(1024)}, u32[]{:S(2)}) copy-start(s32[768]{0:T(1024)} %param.8) | copy-start | bytes 9220
  2.6 8.9 %collective-permute-start.1 = (bf16[3,816,128]{2,1,0:T(8,128)(2,1)S(1)}, bf16[3,816,128]{2,1,0:T(8,128)(2,1)S(1)}, u32[]{:S(2)}, u32[]{:S(2)}) collective-permute-start(bf16[3,816,128]{2,1,0:T(8,128)(2,1)S(1)} %get-tuple-element.42.refs_0_), channel_id=1, source_target_pairs={{0,4},{4,0},{8,12},{12,8},{1,5},{5,1},{9,13},{13,9},{2,6},{6,2},{1... | collective-permute-start | bytes 1880072 | tf_op jit(solution)/shard_map/ppermute | solution.py:26
  3.1 8.4 %collective-permute-start = (bf16[816,128]{1,0:T(8,128)(2,1)S(1)}, bf16[816,128]{1,0:T(8,128)(2,1)S(1)}, u32[]{:S(2)}, u32[]{:S(2)}) collective-permute-start(bf16[816,128]{1,0:T(8,128)(2,1)S(1)} %get-tuple-element.41), channel_id=1, source_target_pairs={{0,8},{4,12},{8,0},{12,4},{1,9},{5,13},{9,1},{13,5},{2,10},{6,14},... | collective-permute-start | bytes 626696 | tf_op jit(solution)/shard_map/ppermute | solution.py:26
  5.7 0.9 %copy-start.2 = (bf16[320,320]{1,0:T(8,128)(2,1)S(1)}, bf16[320,320]{1,0:T(8,128)(2,1)}, u32[]{:S(2)}) copy-start(bf16[320,320]{1,0:T(8,128)(2,1)} %proj_ref.1) | copy-start | bytes 614404
  6.7 11.5 %collective-permute-start.5 = (bf16[800,128]{1,0:T(8,128)(2,1)S(1)}, bf16[800,128]{1,0:T(8,128)(2,1)S(1)}, u32[]{:S(2)}, u32[]{:S(2)}) collective-permute-start(bf16[800,128]{1,0:T(8,128)(2,1)S(1)} %pack_proj.1.refs_4_), channel_id=1, source_target_pairs={{0,1},{1,0},{2,3},{3,2},{4,5},{5,4},{6,7},{7,6},{8,9},{9,8},{10,11... | collective-permute-start | bytes 614408 | tf_op jit(solution)/shard_map/ppermute | solution.py:26
  8.3 12.2 %collective-permute-start.8 = (bf16[800,128]{1,0:T(8,128)(2,1)S(1)}, bf16[800,128]{1,0:T(8,128)(2,1)S(1)}, u32[]{:S(2)}, u32[]{:S(2)}) collective-permute-start(bf16[800,128]{1,0:T(8,128)(2,1)S(1)} %pack_proj.1.refs_4_), channel_id=1, source_target_pairs={{0,2},{1,3},{2,0},{3,1},{16,19},{17,18},{18,17},{19,16},{4,6},{5,7... | collective-permute-start | bytes 614408 | tf_op jit(solution)/shard_map/ppermute | solution.py:329
  10.9 7.7 %collective-permute-start.3 = (bf16[816,128]{1,0:T(8,128)(2,1)S(1)}, bf16[816,128]{1,0:T(8,128)(2,1)S(1)}, u32[]{:S(2)}, u32[]{:S(2)}) collective-permute-start(bf16[816,128]{1,0:T(8,128)(2,1)S(1)} %get-tuple-element.44), channel_id=1, source_target_pairs={{0,8},{4,12},{8,0},{12,4},{1,9},{5,13},{9,1},{13,5},{2,10},{6,14},... | collective-permute-start | bytes 626696 | tf_op jit(solution)/shard_map/ppermute | solution.py:26
  11.4 7.2 %collective-permute-start.2 = (bf16[816,128]{1,0:T(8,128)(2,1)S(1)}, bf16[816,128]{1,0:T(8,128)(2,1)S(1)}, u32[]{:S(2)}, u32[]{:S(2)}) collective-permute-start(bf16[816,128]{1,0:T(8,128)(2,1)S(1)} %collective-permute-done.refs_2_.refs_0_), channel_id=1, source_target_pairs={{0,16},{16,0},{1,17},{17,1},{2,18},{18,2},{3,19},{19,3},{4,20},{20... | collective-permute-start | bytes 626696 | tf_op jit(solution)/shard_map/ppermute | solution.py:26
  13.2 5.5 %collective-permute-start.4 = (bf16[816,128]{1,0:T(8,128)(2,1)S(1)}, bf16[816,128]{1,0:T(8,128)(2,1)S(1)}, u32[]{:S(2)}, u32[]{:S(2)}) collective-permute-start(bf16[816,128]{1,0:T(8,128)(2,1)S(1)} %collective-permute-done.refs_2_.refs_0_), channel_id=1, source_target_pairs={{0,4},{4,0},{8,12},{12,8},{1,5},{5,1},{9,13},{13,9},{2,6},{6,2},{1... | collective-permute-start | bytes 626696 | tf_op jit(solution)/shard_map/ppermute | solution.py:26
  13.2 1.5 %copy-start = (bf16[768,1280]{1,0:T(8,128)(2,1)S(1)}, bf16[768,1280]{1,0:T(8,128)(2,1)}, u32[]{:S(2)}) copy-start(bf16[768,1280]{1,0:T(8,128)(2,1)} %patches_ref) | copy-start | bytes 5898244
  14.7 0.7 %copy-start.3 = (f32[1280]{0:T(1024)S(1)}, f32[1280]{0:T(1024)}, u32[]{:S(2)}) copy-start(f32[1280]{0:T(1024)} %gain_ref.1) | copy-start | bytes 15364
  18.2 10.8 %collective-permute-start.10 = (bf16[2,800,128]{2,1,0:T(8,128)(2,1)S(1)}, bf16[2,800,128]{2,1,0:T(8,128)(2,1)S(1)}, u32[]{:S(2)}, u32[]{:S(2)}) collective-permute-start(bf16[2,800,128]{2,1,0:T(8,128)(2,1)S(1)} %pad_maximum_fusion.1), channel_id=1, source_target_pairs={{0,8},{4,12},{8,0},{12,4},{1,9},{5,13},{9,1},{13,5},{2,10},{6,14},... | collective-permute-start | bytes 1228808 | tf_op jit(solution)/shard_map/ppermute | solution.py:26
  18.6 3.3 %collective-permute-start.6 = (bf16[816,128]{1,0:T(8,128)(2,1)S(1)}, bf16[816,128]{1,0:T(8,128)(2,1)S(1)}, u32[]{:S(2)}, u32[]{:S(2)}) collective-permute-start(bf16[816,128]{1,0:T(8,128)(2,1)S(1)} %collective-permute-done.2.refs_3_), channel_id=1, source_target_pairs={{0,4},{4,0},{8,12},{12,8},{1,5},{5,1},{9,13},{13,9},{2,6},{6,2},{1... | collective-permute-start | bytes 626696 | tf_op jit(solution)/shard_map/ppermute | solution.py:26
  18.9 3.0 %collective-permute-start.7 = (bf16[816,128]{1,0:T(8,128)(2,1)S(1)}, bf16[816,128]{1,0:T(8,128)(2,1)S(1)}, u32[]{:S(2)}, u32[]{:S(2)}) collective-permute-start(bf16[816,128]{1,0:T(8,128)(2,1)S(1)} %collective-permute-done.3.refs_4_), channel_id=1, source_target_pairs={{0,4},{4,0},{8,12},{12,8},{1,5},{5,1},{9,13},{13,9},{2,6},{6,2},{1... | collective-permute-start | bytes 626696 | tf_op jit(solution)/shard_map/ppermute | solution.py:26
  20.5 8.5 %collective-permute-start.9 = (bf16[800,128]{1,0:T(8,128)(2,1)S(1)}, bf16[800,128]{1,0:T(8,128)(2,1)S(1)}, u32[]{:S(2)}, u32[]{:S(2)}) collective-permute-start(bf16[800,128]{1,0:T(8,128)(2,1)S(1)} %collective-permute-done.8.refs_6_), channel_id=1, source_target_pairs={{0,16},{16,0},{1,17},{17,1},{2,18},{18,2},{3,19},{19,3},{4,20},{20... | collective-permute-start | bytes 614408 | tf_op jit(solution)/shard_map/ppermute | solution.py:26
  28.2 18.8 %copy-start.4 = (f32[1280]{0:T(1024)S(1)}, f32[1280]{0:T(1024)}, u32[]{:S(2)}) copy-start(f32[1280]{0:T(1024)} %refs_14_.1) | copy-start | bytes 15364
  29.0 16.2 %collective-permute-start.14 = (bf16[2,800,128]{2,1,0:T(8,128)(2,1)S(1)}, bf16[2,800,128]{2,1,0:T(8,128)(2,1)S(1)}, u32[]{:S(2)}, u32[]{:S(2)}) collective-permute-start(bf16[2,800,128]{2,1,0:T(8,128)(2,1)S(1)} %pad_maximum_fusion.2), channel_id=1, source_target_pairs={{0,8},{4,12},{8,0},{12,4},{1,9},{5,13},{9,1},{13,5},{2,10},{6,14},... | collective-permute-start | bytes 1228808 | tf_op jit(solution)/shard_map/ppermute | solution.py:26
  30.7 14.6 %collective-permute-start.15 = (bf16[4,800,128]{2,1,0:T(8,128)(2,1)S(1)}, bf16[4,800,128]{2,1,0:T(8,128)(2,1)S(1)}, u32[]{:S(2)}, u32[]{:S(2)}) collective-permute-start(bf16[4,800,128]{2,1,0:T(8,128)(2,1)S(1)} %pad_maximum_fusion), channel_id=1, source_target_pairs={{0,4},{4,0},{8,12},{12,8},{1,5},{5,1},{9,13},{13,9},{2,6},{6,2},{1... | collective-permute-start | bytes 2457608 | tf_op jit(solution)/shard_map/ppermute | solution.py:26
  30.8 8.0 %collective-permute-start.11 = (bf16[480,128]{1,0:T(8,128)(2,1)S(1)}, bf16[480,128]{1,0:T(8,128)(2,1)S(1)}, u32[]{:S(2)}, u32[]{:S(2)}) collective-permute-start(bf16[480,128]{1,0:T(8,128)(2,1)S(1)} %get-tuple-element.60), channel_id=1, source_target_pairs={{0,1},{1,0},{2,3},{3,2},{4,5},{5,4},{6,7},{7,6},{8,9},{9,8},{10,11... | collective-permute-start | bytes 368648 | tf_op jit(solution)/shard_map/ppermute | solution.py:26
  32.9 12.4 %collective-permute-start.12 = (bf16[480,128]{1,0:T(8,128)(2,1)S(1)}, bf16[480,128]{1,0:T(8,128)(2,1)S(1)}, u32[]{:S(2)}, u32[]{:S(2)}) collective-permute-start(bf16[480,128]{1,0:T(8,128)(2,1)S(1)} %get-tuple-element.61), channel_id=1, source_target_pairs={{0,2},{1,3},{2,0},{3,1},{4,6},{5,7},{6,4},{7,5},{8,10},{9,11},{10,... | collective-permute-start | bytes 368648 | tf_op jit(solution)/shard_map/ppermute | solution.py:26
  35.5 9.8 %collective-permute-start.13 = (bf16[480,128]{1,0:T(8,128)(2,1)S(1)}, bf16[480,128]{1,0:T(8,128)(2,1)S(1)}, u32[]{:S(2)}, u32[]{:S(2)}) collective-permute-start(bf16[480,128]{1,0:T(8,128)(2,1)S(1)} %get-tuple-element.62), channel_id=1, source_target_pairs={{0,3},{1,2},{2,1},{3,0},{4,7},{5,6},{6,5},{7,4},{8,11},{9,10},{10,... | collective-permute-start | bytes 368648 | tf_op jit(solution)/shard_map/ppermute | solution.py:26
  38.8 6.5 %collective-permute-start.16 = (bf16[2,800,128]{2,1,0:T(8,128)(2,1)S(1)}, bf16[2,800,128]{2,1,0:T(8,128)(2,1)S(1)}, u32[]{:S(2)}, u32[]{:S(2)}) collective-permute-start(bf16[2,800,128]{2,1,0:T(8,128)(2,1)S(1)} %collective-permute-done.10.refs_9_), channel_id=1, source_target_pairs={{0,4},{4,0},{8,12},{12,8},{1,5},{5,1},{9,13},{13,9},{2,6},{6,2},{1... | collective-permute-start | bytes 1228808 | tf_op jit(solution)/shard_map/ppermute | solution.py:26
  45.3 1.7 %collective-permute-start.17 = (bf16[2,800,128]{2,1,0:T(8,128)(2,1)S(1)}, bf16[2,800,128]{2,1,0:T(8,128)(2,1)S(1)}, u32[]{:S(2)}, u32[]{:S(2)}) collective-permute-start(bf16[2,800,128]{2,1,0:T(8,128)(2,1)S(1)} %collective-permute-done.14.refs_10_), channel_id=1, source_target_pairs={{0,4},{4,0},{8,12},{12,8},{1,5},{5,1},{9,13},{13,9},{2,6},{6,2},{1... | collective-permute-start | bytes 1228808 | tf_op jit(solution)/shard_map/ppermute | solution.py:26
  49.0 2.6 %collective-permute-start.20 = (bf16[96,1280]{1,0:T(8,128)(2,1)S(1)}, bf16[96,1280]{1,0:T(8,128)(2,1)S(1)}, u32[]{:S(2)}, u32[]{:S(2)}) collective-permute-start(bf16[96,1280]{1,0:T(8,128)(2,1)S(1)} %get-tuple-element.72.refs_2_), channel_id=1, source_target_pairs={{0,4},{4,0},{8,12},{12,8},{1,5},{5,1},{9,13},{13,9},{2,6},{6,2},{1... | collective-permute-start | bytes 737288 | tf_op jit(solution)/shard_map/ppermute | solution.py:26
  49.2 2.4 %collective-permute-start.21 = (bf16[96,1280]{1,0:T(8,128)(2,1)S(1)}, bf16[96,1280]{1,0:T(8,128)(2,1)S(1)}, u32[]{:S(2)}, u32[]{:S(2)}) collective-permute-start(bf16[96,1280]{1,0:T(8,128)(2,1)S(1)} %get-tuple-element.73.refs_3_), channel_id=1, source_target_pairs={{0,4},{4,0},{8,12},{12,8},{1,5},{5,1},{9,13},{13,9},{2,6},{6,2},{1... | collective-permute-start | bytes 737288 | tf_op jit(solution)/shard_map/ppermute | solution.py:26
  49.5 8.8 %collective-permute-start.18 = (bf16[96,1280]{1,0:T(8,128)(2,1)S(1)}, bf16[96,1280]{1,0:T(8,128)(2,1)S(1)}, u32[]{:S(2)}, u32[]{:S(2)}) collective-permute-start(bf16[96,1280]{1,0:T(8,128)(2,1)S(1)} %get-tuple-element.72.refs_2_), channel_id=1, source_target_pairs={{0,8},{4,12},{8,0},{12,4},{1,9},{5,13},{9,1},{13,5},{2,10},{6,14},... | collective-permute-start | bytes 737288 | tf_op jit(solution)/shard_map/ppermute | solution.py:26
  49.8 13.0 %collective-permute-start.19 = (bf16[96,1280]{1,0:T(8,128)(2,1)S(1)}, bf16[96,1280]{1,0:T(8,128)(2,1)S(1)}, u32[]{:S(2)}, u32[]{:S(2)}) collective-permute-start(bf16[96,1280]{1,0:T(8,128)(2,1)S(1)} %get-tuple-element.73.refs_3_), channel_id=1, source_target_pairs={{0,8},{4,12},{8,0},{12,4},{1,9},{5,13},{9,1},{13,5},{2,10},{6,14},... | collective-permute-start | bytes 737288 | tf_op jit(solution)/shard_map/ppermute | solution.py:26
  62.8 1.5 %collective-permute-start.22 = (bf16[96,1280]{1,0:T(8,128)(2,1)S(1)}, bf16[96,1280]{1,0:T(8,128)(2,1)S(1)}, u32[]{:S(2)}, u32[]{:S(2)}) collective-permute-start(bf16[96,1280]{1,0:T(8,128)(2,1)S(1)} %collective-permute-done.18.refs_2_), channel_id=1, source_target_pairs={{0,4},{4,0},{8,12},{12,8},{1,5},{5,1},{9,13},{13,9},{2,6},{6,2},{1... | collective-permute-start | bytes 737288 | tf_op jit(solution)/shard_map/ppermute | solution.py:26
  62.8 1.9 %collective-permute-start.23 = (bf16[96,1280]{1,0:T(8,128)(2,1)S(1)}, bf16[96,1280]{1,0:T(8,128)(2,1)S(1)}, u32[]{:S(2)}, u32[]{:S(2)}) collective-permute-start(bf16[96,1280]{1,0:T(8,128)(2,1)S(1)} %collective-permute-done.19.refs_3_), channel_id=1, source_target_pairs={{0,4},{4,0},{8,12},{12,8},{1,5},{5,1},{9,13},{13,9},{2,6},{6,2},{1... | collective-permute-start | bytes 737288 | tf_op jit(solution)/shard_map/ppermute | solution.py:26

commit v17 on v16

--- a/solution.py
+++ b/solution.py
@@ -85,6 +85,7 @@
 
 
 NOTE = 16
+SPARE = 32
 
 
 def write_note(place, lanes):
@@ -113,18 +114,19 @@
     return digits[0] * 64 + digits[1]
 
 
-def pack_kernel(index_ref, qkv_ref, place_ref, first_ref, value_ref, all_ref):
-    note = write_note(place_ref[...], all_ref.shape[2])
-    count = all_ref.shape[1] - NOTE
+def pack_kernel(index_ref, qkv_ref, first_ref, value_ref, all_ref):
+    count = all_ref.shape[1] - SPARE
     for j in range(3):
         all_ref[j, :count, :] = pack(qkv_ref[j])
-        all_ref[j, count:, :] = note
+        all_ref[j, count:, :] = jnp.zeros((SPARE, all_ref.shape[2]), BF16)
     first_ref[...] = all_ref[index_ref[2]]
     value_ref[...] = all_ref[2]
 
 
-def pack_proj_kernel(proj_ref, out_ref):
-    out_ref[...] = pack(proj_ref[...])
+def pack_proj_kernel(proj_ref, place_ref, out_ref):
+    count = out_ref.shape[0] - NOTE
+    out_ref[:count, :] = pack(proj_ref[...])
+    out_ref[count:, :] = write_note(place_ref[...], out_ref.shape[1])
 
 
 def norm_kernel(index_ref, patches_ref, gain_ref, hidden_ref, own_ref):
@@ -267,8 +269,7 @@
 
 def place_kernel(count, index_ref, *refs):
     place_refs = refs[:count]
-    row_refs = refs[count : 3 * count]
-    before = refs[3 * count : -1]
+    row_refs = refs[count:-1]
     out_ref = refs[-1]
     spots = out_ref.shape[0]
     chosen = []
@@ -278,14 +279,11 @@
         target = read_note(note_ref, spots) - base
         grid = lax.broadcasted_iota(jnp.int32, (spots, spots), 0).astype(F32)
         chosen.append(one_hot(grid == target))
-    total = jnp.dot(
+    out_ref[...] = jnp.dot(
         jnp.concatenate(chosen, axis=1),
         jnp.concatenate([ref[...] for ref in row_refs], axis=0),
         preferred_element_type=F32,
-    )
-    for ref in before:
-        total = total + ref[...].astype(F32)
-    out_ref[...] = total.astype(out_ref.dtype)
+    ).astype(BF16)
 
 
 def local(n_dp, n_ctx, n_ten, patches, valid, place, gain_attn, w_qkv, w_proj, gain_merge):
@@ -305,24 +303,24 @@
         return swap(x, "context", n_ctx, 1)
 
     third = packed_shape(depth, width)
-    third = (third[0] + NOTE, third[1])
+    third = (third[0] + SPARE, third[1])
     piece = packed_shape(width, col)
     first, value, own = pl.pallas_call(
         pack_kernel,
         out_shape=(shape(*third), shape(*third), shape(3, *third)),
-        in_specs=[SMEM, VMEM, VMEM],
+        in_specs=[SMEM, VMEM],
         out_specs=(VMEM,) * 3,
         compiler_params=params(8),
         name="pack",
-    )(index, jnp.transpose(w_qkv, (1, 0, 2)), place.reshape(1, groups))
+    )(index, jnp.transpose(w_qkv, (1, 0, 2)))
     w_proj = pl.pallas_call(
         pack_proj_kernel,
-        out_shape=shape(*piece),
-        in_specs=[VMEM],
+        out_shape=shape(piece[0] + NOTE, piece[1]),
+        in_specs=[VMEM, VMEM],
         out_specs=VMEM,
         compiler_params=params(8),
         name="pack_proj",
-    )(w_proj)
+    )(w_proj, place.reshape(1, groups))
     first = gather_cross(first, n_ctx)
     value = gather_cross(value, n_ctx)
     twin = over_core(own)
@@ -392,29 +390,26 @@
         name="project",
     )(index, *received, *blocks, own_patches, gain_merge)
 
-    crossed = [gather_cross(x, n_ctx) for x in done]
-    near_rows = [over_core(x) for x in done]
-
-    def put(ids, rows_in, before, name):
-        return pl.pallas_call(
-            functools.partial(place_kernel, len(ids)),
-            out_shape=shape(groups, feat),
-            in_specs=[SMEM] + [VMEM] * (3 * len(ids) + len(before)),
-            out_specs=VMEM,
-            compiler_params=params(24),
-            name=name,
-        )(index, *ids, *rows_in, *before)
-
-    total = put([own, twin], [*done, *near_rows], [], "placement0")
-    last = []
+    gathered = []
+    for rows_out in done:
+        crossed = gather_cross(rows_out, n_ctx)
+        if gathered:
+            for k in cross:
+                crossed[k], gathered[0][k ^ 1] = together(crossed[k], gathered[0][k ^ 1])
+        for k in list(crossed):
+            crossed[k ^ 1] = over_core(crossed[k])
+        gathered.append(crossed)
+    notes = [w_proj, blocks[4]]
     for k in cross:
-        crossed[0][k], crossed[1][k], total = together(crossed[0][k], crossed[1][k], total)
-        twins = [over_core(x[k]) for x in crossed]
-        last += [crossed[0][k], crossed[1][k], *twins]
-    ids = []
-    for k in cross:
-        ids += [first[k], first_twin[k]]
-    return put(ids, last, [total], "placement1")
+        notes += [low[k], low_twin[k]]
+    return pl.pallas_call(
+        functools.partial(place_kernel, n_ctx),
+        out_shape=shape(groups, feat),
+        in_specs=[SMEM] + [VMEM] * (3 * n_ctx),
+        out_specs=VMEM,
+        compiler_params=params(28),
+        name="placement",
+    )(index, *notes, *[half[k] for k in range(n_ctx) for half in gathered])
 
 
 def solution(mesh):

time: 66.7 us -> 65.3 us (0.979)
  starting transfers between devices: 21.4 us -> 19.8 us
  waiting for transfers between devices: 26.3 us -> 27.3 us
  Pallas kernels: 13.4 us -> 12.5 us
    ppermute x23, starting transfers between devices: 18.8 us -> 17.2 us  [swap(): return lax.ppermute(x, axis, [(i, i ^ bit) for i in range(size)])]
    ppermute x23, waiting for transfers between devices: 25 us -> 26 us  [swap(): return lax.ppermute(x, axis, [(i, i ^ bit) for i in range(size)])]
    pallas_call x3 -> x2, Pallas kernels: 2.87 us -> 2 us  [the longest x1 1.92 us: local(): pl.pallas_call(functools.partial(place_kernel, n_ctx), out_shape=shape(gr...]
  transfers between devices with their start and end apart: 24 -> 24, of which waited for: 10 -> 9; matrix products, arithmetic and copies ran while one was open for 0% -> 0% of each run, Pallas kernels for 13% -> 12%
where the time goes in v17:
time: 65.3 us; the launch traced here: 65 us
  waiting for transfers between devices  27.3 us (42%)
  starting transfers between devices  19.8 us (30%)
  Pallas kernels  12.5 us (19%)
  local copies, waits for them, and re-layouts  4.99 us (8%)
    ppermute x23, waiting for transfers between devices, swap(): return lax.ppermute(x, axis, [(i, i ^ bit) for i in range(size)])  26 us
    ppermute x23, starting transfers between devices, swap(): return lax.ppermute(x, axis, [(i, i ^ bit) for i in range(size)])  17.2 us
    pallas_call x1, Pallas kernels, local(): pl.pallas_call(functools.partial(attention_kernel, n_ctx, width), out_sha...  6.33 us
    unnamed x14, local copies, waits for them, and re-layouts  4.99 us
    ppermute x1, starting transfers between devices, local(): lax.ppermute(w_proj, ('dp', 'tensor'), [(d * n_ten + t, d * n_ten + (t ^...  2.59 us
    pallas_call x1, Pallas kernels, local(): pl.pallas_call(functools.partial(place_kernel, n_ctx), out_shape=shape(gr...  1.92 us
    pallas_call x1, Pallas kernels, local(): pl.pallas_call(functools.partial(project_kernel, n_ctx, width, col), out_...  1.92 us
    pallas_call x1, Pallas kernels, local(): pl.pallas_call(norm_kernel, out_shape=(shape(rows, feat), shape(groups, f...  1.57 us
  transfers between devices with their start and end apart: 24, of which 9 were waited for; matrix products, arithmetic and copies ran while one was open for 0% of the time, Pallas kernels for 12%

profile of v17, /device:TPU:0, one launch (start us, length us, event | category | flops | bytes accessed | tf_op | source)
XLA Modules:
  0.0 65.0 jit_solution(516867954280136479)
XLA Ops:
  0.1 1.1 %copy-done.1 = bf16[320,3,320]{2,0,1:T(8,128)(2,1)S(1)} copy-done((bf16[320,3,320]{2,0,1:T(8,128)(2,1)S(1)}, bf16[320,3,320]{2,0,1:T(8,128)(2,1)}, u32[]{:S(2)}) %copy-start.1) | copy-done | bytes 614424
  1.2 0.7 %pack.1 = (bf16[832,128]{1,0:T(8,128)(2,1)S(1)}, bf16[832,128]{1,0:T(8,128)(2,1)S(1)}, bf16[3,832,128]{2,1,0:T(8,128)(2,1)S(1)}) custom-call(s32[3]{0:T(128)S(1)} %pad_add_fusion.index_ref, bf16[3,320,320]{2,1,0:T(8,128)(2,1)S(1)} %bitcast.18), custom_call_target="tpu_custom_call" | custom-call | tf_op jit(solution)/shard_map/pack/pallas_call | solution.py:308
  1.9 0.5 collective-permute-start.2
  2.4 2.6 %collective-permute-start.1 = (bf16[832,128]{1,0:T(8,128)(2,1)S(1)}, bf16[832,128]{1,0:T(8,128)(2,1)S(1)}, u32[]{:S(2)}, u32[]{:S(2)}) collective-permute-start(bf16[832,128]{1,0:T(8,128)(2,1)S(1)} %get-tuple-element.40), channel_id=1, source_target_pairs={{0,8},{4,12},{8,0},{12,4},{1,9},{5,13},{9,1},{13,5},{2,10},{6,14},... | collective-permute-start | bytes 638984 | tf_op jit(solution)/shard_map/ppermute | solution.py:26
  5.0 0.9 %copy-done.2 = bf16[320,320]{1,0:T(8,128)(2,1)S(1)} copy-done((bf16[320,320]{1,0:T(8,128)(2,1)S(1)}, bf16[320,320]{1,0:T(8,128)(2,1)}, u32[]{:S(2)}) %copy-start.2) | copy-done | bytes 204824
  5.9 0.7 %copy-done.6 = s32[192]{0:T(256)S(1)} copy-done((s32[192]{0:T(256)S(1)}, s32[192]{0:T(256)}, u32[]{:S(2)}) %copy-start.6) | copy-done | bytes 792
  6.7 1.6 %collective-permute-start = (bf16[816,128]{1,0:T(8,128)(2,1)S(1)}, bf16[816,128]{1,0:T(8,128)(2,1)S(1)}, u32[]{:S(2)}, u32[]{:S(2)}) collective-permute-start(bf16[816,128]{1,0:T(8,128)(2,1)S(1)} %pack_proj.1.refs_4_.refs_0_), channel_id=1, source_target_pairs={{0,1},{1,0},{2,3},{3,2},{4,5},{5,4},{6,7},{7,6},{8,9},{9,8},{10,11... | collective-permute-start | bytes 626696 | tf_op jit(solution)/shard_map/ppermute | solution.py:26
  8.3 2.6 %collective-permute-start.8 = (bf16[816,128]{1,0:T(8,128)(2,1)S(1)}, bf16[816,128]{1,0:T(8,128)(2,1)S(1)}, u32[]{:S(2)}, u32[]{:S(2)}) collective-permute-start(bf16[816,128]{1,0:T(8,128)(2,1)S(1)} %pack_proj.1.refs_4_.refs_0_), channel_id=1, source_target_pairs={{0,2},{1,3},{2,0},{3,1},{16,19},{17,18},{18,17},{19,16},{4,6},{5,7... | collective-permute-start | bytes 626696 | tf_op jit(solution)/shard_map/ppermute | solution.py:327
  10.9 0.5 collective-permute-start.4
  11.4 1.4 %collective-permute-start.3 = (bf16[832,128]{1,0:T(8,128)(2,1)S(1)}, bf16[832,128]{1,0:T(8,128)(2,1)S(1)}, u32[]{:S(2)}, u32[]{:S(2)}) collective-permute-start(bf16[832,128]{1,0:T(8,128)(2,1)S(1)} %collective-permute-done.1.refs_2_), channel_id=1, source_target_pairs={{0,16},{16,0},{1,17},{17,1},{2,18},{18,2},{3,19},{19,3},{4,20},{20... | collective-permute-start | bytes 638984 | tf_op jit(solution)/shard_map/ppermute | solution.py:26
  12.8 1.5 %copy-done = bf16[768,1280]{1,0:T(8,128)(2,1)S(1)} copy-done((bf16[768,1280]{1,0:T(8,128)(2,1)S(1)}, bf16[768,1280]{1,0:T(8,128)(2,1)}, u32[]{:S(2)}) %copy-start) | copy-done | bytes 1966104
  14.4 0.7 %copy-done.3 = f32[1280]{0:T(1024)S(1)} copy-done((f32[1280]{0:T(1024)S(1)}, f32[1280]{0:T(1024)}, u32[]{:S(2)}) %copy-start.3) | copy-done | bytes 5144
  15.1 1.6 %norm.1 = (bf16[768,1280]{1,0:T(8,128)(2,1)S(1)}, bf16[192,1280]{1,0:T(8,128)(2,1)S(1)}) custom-call(s32[3]{0:T(128)S(1)} %pad_add_fusion.index_ref, bf16[768,1280]{1,0:T(8,128)(2,1)S(1)} %copy-done, f32[1280]{0:T(1024)S(1)} %copy-done.3), custom_call_target="tpu_custom_call" | custom-call | tf_op jit(solution)/shard_map/norm/pallas_call | solution.py:341
  16.6 1.7 %collective-permute-done.refs_5_ = bf16[816,128]{1,0:T(8,128)(2,1)S(1)} collective-permute-done((bf16[816,128]{1,0:T(8,128)(2,1)S(1)}, bf16[816,128]{1,0:T(8,128)(2,1)S(1)}, u32[]{:S(2)}, u32[]{:S(2)}) %collective-permute-start) | collective-permute-done | bytes 208928 | tf_op jit(solution)/shard_map/ppermute | solution.py:26
  18.9 0.5 collective-permute-start.7
  19.4 1.3 %collective-permute-done.8.refs_6_ = bf16[816,128]{1,0:T(8,128)(2,1)S(1)} collective-permute-done((bf16[816,128]{1,0:T(8,128)(2,1)S(1)}, bf16[816,128]{1,0:T(8,128)(2,1)S(1)}, u32[]{:S(2)}, u32[]{:S(2)}) %collective-permute-start.8) | collective-permute-done | bytes 208928 | tf_op jit(solution)/shard_map/ppermute | solution.py:327
  20.7 1.4 %collective-permute-start.9 = (bf16[816,128]{1,0:T(8,128)(2,1)S(1)}, bf16[816,128]{1,0:T(8,128)(2,1)S(1)}, u32[]{:S(2)}, u32[]{:S(2)}) collective-permute-start(bf16[816,128]{1,0:T(8,128)(2,1)S(1)} %collective-permute-done.8.refs_6_), channel_id=1, source_target_pairs={{0,16},{16,0},{1,17},{17,1},{2,18},{18,2},{3,19},{19,3},{4,20},{20... | collective-permute-start | bytes 626696 | tf_op jit(solution)/shard_map/ppermute | solution.py:26
  22.1 6.3 %attention.1 = (bf16[480,128]{1,0:T(8,128)(2,1)S(1)}, bf16[480,128]{1,0:T(8,128)(2,1)S(1)}, bf16[480,128]{1,0:T(8,128)(2,1)S(1)}, bf16[480,128]{1,0:T(8,128)(2,1)S(1)}) custom-call(s32[3]{0:T(128)S(1)} %pad_add_fusion.index_ref, bf16[768,1280]{1,0:T(8,128)(2,1)S(1)} %get-tuple-element.48.hidden_ref, s32[6,128]{1,0:T(8,128)S(1)} %bitcast.19, ...), custom_call_target="tpu_custom_call" | custom-call | tf_op jit(solution)/shard_map/attention/pallas_call | solution.py:363
  28.4 0.9 %collective-permute-done.10.refs_9_.refs_2_ = bf16[2,816,128]{2,1,0:T(8,128)(2,1)S(1)} collective-permute-done((bf16[2,816,128]{2,1,0:T(8,128)(2,1)S(1)}, bf16[2,816,128]{2,1,0:T(8,128)(2,1)S(1)}, u32[]{:S(2)}, u32[]{:S(2)}) %collective-permute-start.10) | collective-permute-done | bytes 417824 | tf_op jit(solution)/shard_map/ppermute | solution.py:26
  29.4 1.1 %collective-permute-start.16 = (bf16[2,816,128]{2,1,0:T(8,128)(2,1)S(1)}, bf16[2,816,128]{2,1,0:T(8,128)(2,1)S(1)}, u32[]{:S(2)}, u32[]{:S(2)}) collective-permute-start(bf16[2,816,128]{2,1,0:T(8,128)(2,1)S(1)} %pad_maximum_fusion.2), channel_id=1, source_target_pairs={{0,8},{4,12},{8,0},{12,4},{1,9},{5,13},{9,1},{13,5},{2,10},{6,14},... | collective-permute-start | bytes 1253384 | tf_op jit(solution)/shard_map/ppermute | solution.py:26
  30.6 1.4 %collective-permute-start.13 = (bf16[480,128]{1,0:T(8,128)(2,1)S(1)}, bf16[480,128]{1,0:T(8,128)(2,1)S(1)}, u32[]{:S(2)}, u32[]{:S(2)}) collective-permute-start(bf16[480,128]{1,0:T(8,128)(2,1)S(1)} %get-tuple-element.62), channel_id=1, source_target_pairs={{0,1},{1,0},{2,3},{3,2},{4,5},{5,4},{6,7},{7,6},{8,9},{9,8},{10,11... | collective-permute-start | bytes 368648 | tf_op jit(solution)/shard_map/ppermute | solution.py:26
  32.0 3.0 %collective-permute-start.14 = (bf16[480,128]{1,0:T(8,128)(2,1)S(1)}, bf16[480,128]{1,0:T(8,128)(2,1)S(1)}, u32[]{:S(2)}, u32[]{:S(2)}) collective-permute-start(bf16[480,128]{1,0:T(8,128)(2,1)S(1)} %get-tuple-element.63), channel_id=1, source_target_pairs={{0,2},{1,3},{2,0},{3,1},{4,6},{5,7},{6,4},{7,5},{8,10},{9,11},{10,... | collective-permute-start | bytes 368648 | tf_op jit(solution)/shard_map/ppermute | solution.py:26
  35.1 3.5 %collective-permute-done.13.refs_1_ = bf16[480,128]{1,0:T(8,128)(2,1)S(1)} collective-permute-done((bf16[480,128]{1,0:T(8,128)(2,1)S(1)}, bf16[480,128]{1,0:T(8,128)(2,1)S(1)}, u32[]{:S(2)}, u32[]{:S(2)}) %collective-permute-start.13) | collective-permute-done | bytes 122912 | tf_op jit(solution)/shard_map/ppermute | solution.py:26
  38.6 5.9 %collective-permute-done.14.refs_2_ = bf16[480,128]{1,0:T(8,128)(2,1)S(1)} collective-permute-done((bf16[480,128]{1,0:T(8,128)(2,1)S(1)}, bf16[480,128]{1,0:T(8,128)(2,1)S(1)}, u32[]{:S(2)}, u32[]{:S(2)}) %collective-permute-start.14) | collective-permute-done | bytes 122912 | tf_op jit(solution)/shard_map/ppermute | solution.py:26
  44.5 1.7 %collective-permute-done.17.refs_12_ = bf16[2,816,128]{2,1,0:T(8,128)(2,1)S(1)} collective-permute-done((bf16[2,816,128]{2,1,0:T(8,128)(2,1)S(1)}, bf16[2,816,128]{2,1,0:T(8,128)(2,1)S(1)}, u32[]{:S(2)}, u32[]{:S(2)}) %collective-permute-start.17) | collective-permute-done | bytes 417824 | tf_op jit(solution)/shard_map/ppermute | solution.py:26
  46.3 1.9 %project.1 = (bf16[96,1280]{1,0:T(8,128)(2,1)S(1)}, bf16[96,1280]{1,0:T(8,128)(2,1)S(1)}) custom-call(s32[3]{0:T(128)S(1)} %pad_add_fusion.index_ref, bf16[480,128]{1,0:T(8,128)(2,1)S(1)} %get-tuple-element.65.refs_0_, bf16[480,128]{1,0:T(8,128)(2,1)S(1)} %collective-permute-done.13.refs_1_, bf16[480,128]{1,0:T(8,128)(2,1)S(1)} %collective-permute-done.14.refs_2_, ...), custom_call_target="tpu_custom_call" | custom-call | tf_op jit(solution)/shard_map/project/pallas_call | solution.py:383
  48.7 1.6 %collective-permute-start.21 = (bf16[96,1280]{1,0:T(8,128)(2,1)S(1)}, bf16[96,1280]{1,0:T(8,128)(2,1)S(1)}, u32[]{:S(2)}, u32[]{:S(2)}) collective-permute-start(bf16[96,1280]{1,0:T(8,128)(2,1)S(1)} %get-tuple-element.72.refs_5_), channel_id=1, source_target_pairs={{0,8},{4,12},{8,0},{12,4},{1,9},{5,13},{9,1},{13,5},{2,10},{6,14},... | collective-permute-start | bytes 737288 | tf_op jit(solution)/shard_map/ppermute | solution.py:26
  50.3 6.8 %collective-permute-done.20.refs_8_ = bf16[96,1280]{1,0:T(8,128)(2,1)S(1)} collective-permute-done((bf16[96,1280]{1,0:T(8,128)(2,1)S(1)}, bf16[96,1280]{1,0:T(8,128)(2,1)S(1)}, u32[]{:S(2)}, u32[]{:S(2)}) %collective-permute-start.20) | collective-permute-done | bytes 245792 | tf_op jit(solution)/shard_map/ppermute | solution.py:26
  57.1 0.5 collective-permute-start.18
  57.6 4.0 %collective-permute-done.21.refs_9_ = bf16[96,1280]{1,0:T(8,128)(2,1)S(1)} collective-permute-done((bf16[96,1280]{1,0:T(8,128)(2,1)S(1)}, bf16[96,1280]{1,0:T(8,128)(2,1)S(1)}, u32[]{:S(2)}, u32[]{:S(2)}) %collective-permute-start.21) | collective-permute-done | bytes 245792 | tf_op jit(solution)/shard_map/ppermute | solution.py:26
  61.5 1.5 %collective-permute-done.23.refs_11_ = bf16[96,1280]{1,0:T(8,128)(2,1)S(1)} collective-permute-done((bf16[96,1280]{1,0:T(8,128)(2,1)S(1)}, bf16[96,1280]{1,0:T(8,128)(2,1)S(1)}, u32[]{:S(2)}, u32[]{:S(2)}) %collective-permute-start.23) | collective-permute-done | bytes 245792 | tf_op jit(solution)/shard_map/ppermute | solution.py:26
  63.0 1.9 %placement.1 = bf16[192,1280]{1,0:T(8,128)(2,1)} custom-call(s32[3]{0:T(128)S(1)} %pad_add_fusion.index_ref, bf16[816,128]{1,0:T(8,128)(2,1)S(1)} %pack_proj.1.refs_4_.refs_0_, bf16[4,816,128]{2,1,0:T(8,128)(2,1)S(1)} %collective-permute-done.11.refs_8_.refs_1_, bf16[2,816,128]{2,1,0:T(8,128)(2,1)S(1)} %collective-permute-done.10.refs_9_.refs_2_, ...), custom_call_target="tpu_custom_call" | custom-call | tf_op jit(solution)/shard_map/placement/pallas_call | solution.py:405
  (40 shorter events, 1.4 us)
Async XLA Ops:
  0.1 1.1 %copy-start.1 = (bf16[320,3,320]{2,0,1:T(8,128)(2,1)S(1)}, bf16[320,3,320]{2,0,1:T(8,128)(2,1)}, u32[]{:S(2)}) copy-start(bf16[320,3,320]{2,0,1:T(8,128)(2,1)} %param.11) | copy-start | bytes 1843204
  1.2 20.9 %copy-start.5 = (s32[768]{0:T(1024)S(1)}, s32[768]{0:T(1024)}, u32[]{:S(2)}) copy-start(s32[768]{0:T(1024)} %param.8) | copy-start | bytes 9220
  1.9 9.5 %collective-permute-start.2 = (bf16[3,832,128]{2,1,0:T(8,128)(2,1)S(1)}, bf16[3,832,128]{2,1,0:T(8,128)(2,1)S(1)}, u32[]{:S(2)}, u32[]{:S(2)}) collective-permute-start(bf16[3,832,128]{2,1,0:T(8,128)(2,1)S(1)} %get-tuple-element.41.refs_0_), channel_id=1, source_target_pairs={{0,4},{4,0},{8,12},{12,8},{1,5},{5,1},{9,13},{13,9},{2,6},{6,2},{1... | collective-permute-start | bytes 1916936 | tf_op jit(solution)/shard_map/ppermute | solution.py:26
  2.4 9.0 %collective-permute-start.1 = (bf16[832,128]{1,0:T(8,128)(2,1)S(1)}, bf16[832,128]{1,0:T(8,128)(2,1)S(1)}, u32[]{:S(2)}, u32[]{:S(2)}) collective-permute-start(bf16[832,128]{1,0:T(8,128)(2,1)S(1)} %get-tuple-element.40), channel_id=1, source_target_pairs={{0,8},{4,12},{8,0},{12,4},{1,9},{5,13},{9,1},{13,5},{2,10},{6,14},... | collective-permute-start | bytes 638984 | tf_op jit(solution)/shard_map/ppermute | solution.py:26
  5.0 0.9 %copy-start.2 = (bf16[320,320]{1,0:T(8,128)(2,1)S(1)}, bf16[320,320]{1,0:T(8,128)(2,1)}, u32[]{:S(2)}) copy-start(bf16[320,320]{1,0:T(8,128)(2,1)} %proj_ref.1) | copy-start | bytes 614404
  5.9 0.7 %copy-start.6 = (s32[192]{0:T(256)S(1)}, s32[192]{0:T(256)}, u32[]{:S(2)}) copy-start(s32[192]{0:T(256)} %param.9) | copy-start | bytes 2308
  6.7 11.6 %collective-permute-start = (bf16[816,128]{1,0:T(8,128)(2,1)S(1)}, bf16[816,128]{1,0:T(8,128)(2,1)S(1)}, u32[]{:S(2)}, u32[]{:S(2)}) collective-permute-start(bf16[816,128]{1,0:T(8,128)(2,1)S(1)} %pack_proj.1.refs_4_.refs_0_), channel_id=1, source_target_pairs={{0,1},{1,0},{2,3},{3,2},{4,5},{5,4},{6,7},{7,6},{8,9},{9,8},{10,11... | collective-permute-start | bytes 626696 | tf_op jit(solution)/shard_map/ppermute | solution.py:26
  8.3 12.4 %collective-permute-start.8 = (bf16[816,128]{1,0:T(8,128)(2,1)S(1)}, bf16[816,128]{1,0:T(8,128)(2,1)S(1)}, u32[]{:S(2)}, u32[]{:S(2)}) collective-permute-start(bf16[816,128]{1,0:T(8,128)(2,1)S(1)} %pack_proj.1.refs_4_.refs_0_), channel_id=1, source_target_pairs={{0,2},{1,3},{2,0},{3,1},{16,19},{17,18},{18,17},{19,16},{4,6},{5,7... | collective-permute-start | bytes 626696 | tf_op jit(solution)/shard_map/ppermute | solution.py:327
  10.9 7.9 %collective-permute-start.4 = (bf16[832,128]{1,0:T(8,128)(2,1)S(1)}, bf16[832,128]{1,0:T(8,128)(2,1)S(1)}, u32[]{:S(2)}, u32[]{:S(2)}) collective-permute-start(bf16[832,128]{1,0:T(8,128)(2,1)S(1)} %get-tuple-element.46), channel_id=1, source_target_pairs={{0,8},{4,12},{8,0},{12,4},{1,9},{5,13},{9,1},{13,5},{2,10},{6,14},... | collective-permute-start | bytes 638984 | tf_op jit(solution)/shard_map/ppermute | solution.py:26
  11.4 7.4 %collective-permute-start.3 = (bf16[832,128]{1,0:T(8,128)(2,1)S(1)}, bf16[832,128]{1,0:T(8,128)(2,1)S(1)}, u32[]{:S(2)}, u32[]{:S(2)}) collective-permute-start(bf16[832,128]{1,0:T(8,128)(2,1)S(1)} %collective-permute-done.1.refs_2_), channel_id=1, source_target_pairs={{0,16},{16,0},{1,17},{17,1},{2,18},{18,2},{3,19},{19,3},{4,20},{20... | collective-permute-start | bytes 638984 | tf_op jit(solution)/shard_map/ppermute | solution.py:26
  12.8 6.0 %collective-permute-start.5 = (bf16[832,128]{1,0:T(8,128)(2,1)S(1)}, bf16[832,128]{1,0:T(8,128)(2,1)S(1)}, u32[]{:S(2)}, u32[]{:S(2)}) collective-permute-start(bf16[832,128]{1,0:T(8,128)(2,1)S(1)} %collective-permute-done.1.refs_2_), channel_id=1, source_target_pairs={{0,4},{4,0},{8,12},{12,8},{1,5},{5,1},{9,13},{13,9},{2,6},{6,2},{1... | collective-permute-start | bytes 638984 | tf_op jit(solution)/shard_map/ppermute | solution.py:26
  12.8 1.5 %copy-start = (bf16[768,1280]{1,0:T(8,128)(2,1)S(1)}, bf16[768,1280]{1,0:T(8,128)(2,1)}, u32[]{:S(2)}) copy-start(bf16[768,1280]{1,0:T(8,128)(2,1)} %patches_ref) | copy-start | bytes 5898244
  14.4 0.7 %copy-start.3 = (f32[1280]{0:T(1024)S(1)}, f32[1280]{0:T(1024)}, u32[]{:S(2)}) copy-start(f32[1280]{0:T(1024)} %gain_ref.1) | copy-start | bytes 15364
  18.4 10.9 %collective-permute-start.10 = (bf16[2,816,128]{2,1,0:T(8,128)(2,1)S(1)}, bf16[2,816,128]{2,1,0:T(8,128)(2,1)S(1)}, u32[]{:S(2)}, u32[]{:S(2)}) collective-permute-start(bf16[2,816,128]{2,1,0:T(8,128)(2,1)S(1)} %pad_maximum_fusion.1), channel_id=1, source_target_pairs={{0,8},{4,12},{8,0},{12,4},{1,9},{5,13},{9,1},{13,5},{2,10},{6,14},... | collective-permute-start | bytes 1253384 | tf_op jit(solution)/shard_map/ppermute | solution.py:26
  18.8 3.3 %collective-permute-start.6 = (bf16[832,128]{1,0:T(8,128)(2,1)S(1)}, bf16[832,128]{1,0:T(8,128)(2,1)S(1)}, u32[]{:S(2)}, u32[]{:S(2)}) collective-permute-start(bf16[832,128]{1,0:T(8,128)(2,1)S(1)} %collective-permute-done.3.refs_3_), channel_id=1, source_target_pairs={{0,4},{4,0},{8,12},{12,8},{1,5},{5,1},{9,13},{13,9},{2,6},{6,2},{1... | collective-permute-start | bytes 638984 | tf_op jit(solution)/shard_map/ppermute | solution.py:26
  18.9 3.2 %collective-permute-start.7 = (bf16[832,128]{1,0:T(8,128)(2,1)S(1)}, bf16[832,128]{1,0:T(8,128)(2,1)S(1)}, u32[]{:S(2)}, u32[]{:S(2)}) collective-permute-start(bf16[832,128]{1,0:T(8,128)(2,1)S(1)} %collective-permute-done.4.refs_4_), channel_id=1, source_target_pairs={{0,4},{4,0},{8,12},{12,8},{1,5},{5,1},{9,13},{13,9},{2,6},{6,2},{1... | collective-permute-start | bytes 638984 | tf_op jit(solution)/shard_map/ppermute | solution.py:26
  20.7 8.6 %collective-permute-start.9 = (bf16[816,128]{1,0:T(8,128)(2,1)S(1)}, bf16[816,128]{1,0:T(8,128)(2,1)S(1)}, u32[]{:S(2)}, u32[]{:S(2)}) collective-permute-start(bf16[816,128]{1,0:T(8,128)(2,1)S(1)} %collective-permute-done.8.refs_6_), channel_id=1, source_target_pairs={{0,16},{16,0},{1,17},{17,1},{2,18},{18,2},{3,19},{19,3},{4,20},{20... | collective-permute-start | bytes 626696 | tf_op jit(solution)/shard_map/ppermute | solution.py:26
  28.4 17.8 %copy-start.4 = (f32[1280]{0:T(1024)S(1)}, f32[1280]{0:T(1024)}, u32[]{:S(2)}) copy-start(f32[1280]{0:T(1024)} %refs_14_.1) | copy-start | bytes 15364
  29.4 15.1 %collective-permute-start.16 = (bf16[2,816,128]{2,1,0:T(8,128)(2,1)S(1)}, bf16[2,816,128]{2,1,0:T(8,128)(2,1)S(1)}, u32[]{:S(2)}, u32[]{:S(2)}) collective-permute-start(bf16[2,816,128]{2,1,0:T(8,128)(2,1)S(1)} %pad_maximum_fusion.2), channel_id=1, source_target_pairs={{0,8},{4,12},{8,0},{12,4},{1,9},{5,13},{9,1},{13,5},{2,10},{6,14},... | collective-permute-start | bytes 1253384 | tf_op jit(solution)/shard_map/ppermute | solution.py:26
  30.5 15.7 %collective-permute-start.11 = (bf16[4,816,128]{2,1,0:T(8,128)(2,1)S(1)}, bf16[4,816,128]{2,1,0:T(8,128)(2,1)S(1)}, u32[]{:S(2)}, u32[]{:S(2)}) collective-permute-start(bf16[4,816,128]{2,1,0:T(8,128)(2,1)S(1)} %pad_maximum_fusion), channel_id=1, source_target_pairs={{0,4},{4,0},{8,12},{12,8},{1,5},{5,1},{9,13},{13,9},{2,6},{6,2},{1... | collective-permute-start | bytes 2506760 | tf_op jit(solution)/shard_map/ppermute | solution.py:26
  30.6 7.9 %collective-permute-start.13 = (bf16[480,128]{1,0:T(8,128)(2,1)S(1)}, bf16[480,128]{1,0:T(8,128)(2,1)S(1)}, u32[]{:S(2)}, u32[]{:S(2)}) collective-permute-start(bf16[480,128]{1,0:T(8,128)(2,1)S(1)} %get-tuple-element.62), channel_id=1, source_target_pairs={{0,1},{1,0},{2,3},{3,2},{4,5},{5,4},{6,7},{7,6},{8,9},{9,8},{10,11... | collective-permute-start | bytes 368648 | tf_op jit(solution)/shard_map/ppermute | solution.py:26
  32.0 12.5 %collective-permute-start.14 = (bf16[480,128]{1,0:T(8,128)(2,1)S(1)}, bf16[480,128]{1,0:T(8,128)(2,1)S(1)}, u32[]{:S(2)}, u32[]{:S(2)}) collective-permute-start(bf16[480,128]{1,0:T(8,128)(2,1)S(1)} %get-tuple-element.63), channel_id=1, source_target_pairs={{0,2},{1,3},{2,0},{3,1},{4,6},{5,7},{6,4},{7,5},{8,10},{9,11},{10,... | collective-permute-start | bytes 368648 | tf_op jit(solution)/shard_map/ppermute | solution.py:26
  35.1 9.4 %collective-permute-start.15 = (bf16[480,128]{1,0:T(8,128)(2,1)S(1)}, bf16[480,128]{1,0:T(8,128)(2,1)S(1)}, u32[]{:S(2)}, u32[]{:S(2)}) collective-permute-start(bf16[480,128]{1,0:T(8,128)(2,1)S(1)} %get-tuple-element.64), channel_id=1, source_target_pairs={{0,3},{1,2},{2,1},{3,0},{4,7},{5,6},{6,5},{7,4},{8,11},{9,10},{10,... | collective-permute-start | bytes 368648 | tf_op jit(solution)/shard_map/ppermute | solution.py:26
  38.6 5.9 %collective-permute-start.12 = (bf16[2,816,128]{2,1,0:T(8,128)(2,1)S(1)}, bf16[2,816,128]{2,1,0:T(8,128)(2,1)S(1)}, u32[]{:S(2)}, u32[]{:S(2)}) collective-permute-start(bf16[2,816,128]{2,1,0:T(8,128)(2,1)S(1)} %collective-permute-done.10.refs_9_.refs_2_), channel_id=1, source_target_pairs={{0,4},{4,0},{8,12},{12,8},{1,5},{5,1},{9,13},{13,9},{2,6},{6,2},{1... | collective-permute-start | bytes 1253384 | tf_op jit(solution)/shard_map/ppermute | solution.py:26
  44.5 1.8 %collective-permute-start.17 = (bf16[2,816,128]{2,1,0:T(8,128)(2,1)S(1)}, bf16[2,816,128]{2,1,0:T(8,128)(2,1)S(1)}, u32[]{:S(2)}, u32[]{:S(2)}) collective-permute-start(bf16[2,816,128]{2,1,0:T(8,128)(2,1)S(1)} %collective-permute-done.16.refs_10_), channel_id=1, source_target_pairs={{0,4},{4,0},{8,12},{12,8},{1,5},{5,1},{9,13},{13,9},{2,6},{6,2},{1... | collective-permute-start | bytes 1253384 | tf_op jit(solution)/shard_map/ppermute | solution.py:26
  48.2 8.9 %collective-permute-start.20 = (bf16[96,1280]{1,0:T(8,128)(2,1)S(1)}, bf16[96,1280]{1,0:T(8,128)(2,1)S(1)}, u32[]{:S(2)}, u32[]{:S(2)}) collective-permute-start(bf16[96,1280]{1,0:T(8,128)(2,1)S(1)} %get-tuple-element.71.refs_4_), channel_id=1, source_target_pairs={{0,8},{4,12},{8,0},{12,4},{1,9},{5,13},{9,1},{13,5},{2,10},{6,14},... | collective-permute-start | bytes 737288 | tf_op jit(solution)/shard_map/ppermute | solution.py:26
  48.7 12.9 %collective-permute-start.21 = (bf16[96,1280]{1,0:T(8,128)(2,1)S(1)}, bf16[96,1280]{1,0:T(8,128)(2,1)S(1)}, u32[]{:S(2)}, u32[]{:S(2)}) collective-permute-start(bf16[96,1280]{1,0:T(8,128)(2,1)S(1)} %get-tuple-element.72.refs_5_), channel_id=1, source_target_pairs={{0,8},{4,12},{8,0},{12,4},{1,9},{5,13},{9,1},{13,5},{2,10},{6,14},... | collective-permute-start | bytes 737288 | tf_op jit(solution)/shard_map/ppermute | solution.py:26
  57.1 4.5 %collective-permute-start.22 = (bf16[96,1280]{1,0:T(8,128)(2,1)S(1)}, bf16[96,1280]{1,0:T(8,128)(2,1)S(1)}, u32[]{:S(2)}, u32[]{:S(2)}) collective-permute-start(bf16[96,1280]{1,0:T(8,128)(2,1)S(1)} %collective-permute-done.20.refs_8_), channel_id=1, source_target_pairs={{0,4},{4,0},{8,12},{12,8},{1,5},{5,1},{9,13},{13,9},{2,6},{6,2},{1... | collective-permute-start | bytes 737288 | tf_op jit(solution)/shard_map/ppermute | solution.py:26
  57.1 4.5 %collective-permute-start.18 = (bf16[96,1280]{1,0:T(8,128)(2,1)S(1)}, bf16[96,1280]{1,0:T(8,128)(2,1)S(1)}, u32[]{:S(2)}, u32[]{:S(2)}) collective-permute-start(bf16[96,1280]{1,0:T(8,128)(2,1)S(1)} %get-tuple-element.71.refs_4_), channel_id=1, source_target_pairs={{0,4},{4,0},{8,12},{12,8},{1,5},{5,1},{9,13},{13,9},{2,6},{6,2},{1... | collective-permute-start | bytes 737288 | tf_op jit(solution)/shard_map/ppermute | solution.py:26
  57.6 4.0 %collective-permute-start.19 = (bf16[96,1280]{1,0:T(8,128)(2,1)S(1)}, bf16[96,1280]{1,0:T(8,128)(2,1)S(1)}, u32[]{:S(2)}, u32[]{:S(2)}) collective-permute-start(bf16[96,1280]{1,0:T(8,128)(2,1)S(1)} %get-tuple-element.72.refs_5_), channel_id=1, source_target_pairs={{0,4},{4,0},{8,12},{12,8},{1,5},{5,1},{9,13},{13,9},{2,6},{6,2},{1... | collective-permute-start | bytes 737288 | tf_op jit(solution)/shard_map/ppermute | solution.py:26
  61.5 1.5 %collective-permute-start.23 = (bf16[96,1280]{1,0:T(8,128)(2,1)S(1)}, bf16[96,1280]{1,0:T(8,128)(2,1)S(1)}, u32[]{:S(2)}, u32[]{:S(2)}) collective-permute-start(bf16[96,1280]{1,0:T(8,128)(2,1)S(1)} %collective-permute-done.21.refs_9_), channel_id=1, source_target_pairs={{0,4},{4,0},{8,12},{12,8},{1,5},{5,1},{9,13},{13,9},{2,6},{6,2},{1... | collective-permute-start | bytes 737288 | tf_op jit(solution)/shard_map/ppermute | solution.py:26

commit v18 on v17

--- a/solution.py
+++ b/solution.py
@@ -269,8 +269,7 @@
 
 def place_kernel(count, index_ref, *refs):
     place_refs = refs[:count]
-    row_refs = refs[count:-1]
-    out_ref = refs[-1]
+    *row_refs, out_ref, stage_ref, sem = refs[count:]
     spots = out_ref.shape[0]
     chosen = []
     base = (index_ref[0] * spots).astype(F32)
@@ -279,11 +278,21 @@
         target = read_note(note_ref, spots) - base
         grid = lax.broadcasted_iota(jnp.int32, (spots, spots), 0).astype(F32)
         chosen.append(one_hot(grid == target))
-    out_ref[...] = jnp.dot(
-        jnp.concatenate(chosen, axis=1),
-        jnp.concatenate([ref[...] for ref in row_refs], axis=0),
-        preferred_element_type=F32,
-    ).astype(BF16)
+    chosen = jnp.concatenate(chosen, axis=1)
+    step = stage_ref.shape[2]
+    copies = []
+    for i in range(out_ref.shape[1] // step):
+        cols = slice(i * step, (i + 1) * step)
+        slot = stage_ref.at[i]
+        slot[...] = jnp.dot(
+            chosen,
+            jnp.concatenate([ref[:, cols] for ref in row_refs], axis=0),
+            preferred_element_type=F32,
+        ).astype(BF16)
+        copies.append(pltpu.make_async_copy(slot, out_ref.at[:, cols], sem.at[i]))
+        copies[i].start()
+    for copy in copies:
+        copy.wait()
 
 
 def local(n_dp, n_ctx, n_ten, patches, valid, place, gain_attn, w_qkv, w_proj, gain_merge):
@@ -406,7 +415,11 @@
         functools.partial(place_kernel, n_ctx),
         out_shape=shape(groups, feat),
         in_specs=[SMEM] + [VMEM] * (3 * n_ctx),
-        out_specs=VMEM,
+        out_specs=pl.BlockSpec(memory_space=pl.ANY),
+        scratch_shapes=[
+            pltpu.VMEM((feat // 256, groups, 256), BF16),
+            pltpu.SemaphoreType.DMA((feat // 256,)),
+        ],
         compiler_params=params(28),
         name="placement",
     )(index, *notes, *[half[k] for k in range(n_ctx) for half in gathered])

time: 65.3 us -> 65.2 us (level)
  no operation moved by 1% of the time
where the time goes in v18:
time: 65.2 us; the launch traced here: 64.9 us
  waiting for transfers between devices  27.3 us (42%)
  starting transfers between devices  19.8 us (30%)
  Pallas kernels  12.4 us (19%)
  local copies, waits for them, and re-layouts  4.99 us (8%)
    ppermute x23, waiting for transfers between devices, swap(): return lax.ppermute(x, axis, [(i, i ^ bit) for i in range(size)])  26 us
    ppermute x23, starting transfers between devices, swap(): return lax.ppermute(x, axis, [(i, i ^ bit) for i in range(size)])  17.2 us
    pallas_call x1, Pallas kernels, local(): pl.pallas_call(functools.partial(attention_kernel, n_ctx, width), out_sha...  6.33 us
    unnamed x14, local copies, waits for them, and re-layouts  4.99 us
    ppermute x1, starting transfers between devices, local(): lax.ppermute(w_proj, ('dp', 'tensor'), [(d * n_ten + t, d * n_ten + (t ^...  2.59 us
    pallas_call x1, Pallas kernels, local(): pl.pallas_call(functools.partial(project_kernel, n_ctx, width, col), out_...  1.92 us
    pallas_call x1, Pallas kernels, local(): pl.pallas_call(functools.partial(place_kernel, n_ctx), out_shape=shape(gr...  1.83 us
    pallas_call x1, Pallas kernels, local(): pl.pallas_call(norm_kernel, out_shape=(shape(rows, feat), shape(groups, f...  1.57 us
  transfers between devices with their start and end apart: 24, of which 9 were waited for; matrix products, arithmetic and copies ran while one was open for 0% of the time, Pallas kernels for 12%

profile of v18, /device:TPU:0, one launch (start us, length us, event | category | flops | bytes accessed | tf_op | source)
XLA Modules:
  0.0 64.9 jit_solution(14228049983449731570)
XLA Ops:
  0.1 1.1 %copy-done.1 = bf16[320,3,320]{2,0,1:T(8,128)(2,1)S(1)} copy-done((bf16[320,3,320]{2,0,1:T(8,128)(2,1)S(1)}, bf16[320,3,320]{2,0,1:T(8,128)(2,1)}, u32[]{:S(2)}) %copy-start.1) | copy-done | bytes 614424
  1.2 0.7 %pack.1 = (bf16[832,128]{1,0:T(8,128)(2,1)S(1)}, bf16[832,128]{1,0:T(8,128)(2,1)S(1)}, bf16[3,832,128]{2,1,0:T(8,128)(2,1)S(1)}) custom-call(s32[3]{0:T(128)S(1)} %pad_add_fusion.index_ref, bf16[3,320,320]{2,1,0:T(8,128)(2,1)S(1)} %bitcast.18), custom_call_target="tpu_custom_call" | custom-call | tf_op jit(solution)/shard_map/pack/pallas_call | solution.py:317
  1.9 0.5 collective-permute-start.2
  2.4 2.6 %collective-permute-start.1 = (bf16[832,128]{1,0:T(8,128)(2,1)S(1)}, bf16[832,128]{1,0:T(8,128)(2,1)S(1)}, u32[]{:S(2)}, u32[]{:S(2)}) collective-permute-start(bf16[832,128]{1,0:T(8,128)(2,1)S(1)} %get-tuple-element.40), channel_id=1, source_target_pairs={{0,8},{4,12},{8,0},{12,4},{1,9},{5,13},{9,1},{13,5},{2,10},{6,14},... | collective-permute-start | bytes 638984 | tf_op jit(solution)/shard_map/ppermute | solution.py:26
  5.0 0.9 %copy-done.2 = bf16[320,320]{1,0:T(8,128)(2,1)S(1)} copy-done((bf16[320,320]{1,0:T(8,128)(2,1)S(1)}, bf16[320,320]{1,0:T(8,128)(2,1)}, u32[]{:S(2)}) %copy-start.2) | copy-done | bytes 204824
  5.9 0.7 %copy-done.6 = s32[192]{0:T(256)S(1)} copy-done((s32[192]{0:T(256)S(1)}, s32[192]{0:T(256)}, u32[]{:S(2)}) %copy-start.6) | copy-done | bytes 792
  6.7 1.6 %collective-permute-start = (bf16[816,128]{1,0:T(8,128)(2,1)S(1)}, bf16[816,128]{1,0:T(8,128)(2,1)S(1)}, u32[]{:S(2)}, u32[]{:S(2)}) collective-permute-start(bf16[816,128]{1,0:T(8,128)(2,1)S(1)} %pack_proj.1.refs_4_.refs_0_), channel_id=1, source_target_pairs={{0,1},{1,0},{2,3},{3,2},{4,5},{5,4},{6,7},{7,6},{8,9},{9,8},{10,11... | collective-permute-start | bytes 626696 | tf_op jit(solution)/shard_map/ppermute | solution.py:26
  8.3 2.6 %collective-permute-start.8 = (bf16[816,128]{1,0:T(8,128)(2,1)S(1)}, bf16[816,128]{1,0:T(8,128)(2,1)S(1)}, u32[]{:S(2)}, u32[]{:S(2)}) collective-permute-start(bf16[816,128]{1,0:T(8,128)(2,1)S(1)} %pack_proj.1.refs_4_.refs_0_), channel_id=1, source_target_pairs={{0,2},{1,3},{2,0},{3,1},{16,19},{17,18},{18,17},{19,16},{4,6},{5,7... | collective-permute-start | bytes 626696 | tf_op jit(solution)/shard_map/ppermute | solution.py:336
  10.9 0.5 collective-permute-start.4
  11.4 1.4 %collective-permute-start.3 = (bf16[832,128]{1,0:T(8,128)(2,1)S(1)}, bf16[832,128]{1,0:T(8,128)(2,1)S(1)}, u32[]{:S(2)}, u32[]{:S(2)}) collective-permute-start(bf16[832,128]{1,0:T(8,128)(2,1)S(1)} %collective-permute-done.1.refs_2_), channel_id=1, source_target_pairs={{0,16},{16,0},{1,17},{17,1},{2,18},{18,2},{3,19},{19,3},{4,20},{20... | collective-permute-start | bytes 638984 | tf_op jit(solution)/shard_map/ppermute | solution.py:26
  12.8 1.5 %copy-done = bf16[768,1280]{1,0:T(8,128)(2,1)S(1)} copy-done((bf16[768,1280]{1,0:T(8,128)(2,1)S(1)}, bf16[768,1280]{1,0:T(8,128)(2,1)}, u32[]{:S(2)}) %copy-start) | copy-done | bytes 1966104
  14.4 0.7 %copy-done.3 = f32[1280]{0:T(1024)S(1)} copy-done((f32[1280]{0:T(1024)S(1)}, f32[1280]{0:T(1024)}, u32[]{:S(2)}) %copy-start.3) | copy-done | bytes 5144
  15.1 1.6 %norm.1 = (bf16[768,1280]{1,0:T(8,128)(2,1)S(1)}, bf16[192,1280]{1,0:T(8,128)(2,1)S(1)}) custom-call(s32[3]{0:T(128)S(1)} %pad_add_fusion.index_ref, bf16[768,1280]{1,0:T(8,128)(2,1)S(1)} %copy-done, f32[1280]{0:T(1024)S(1)} %copy-done.3), custom_call_target="tpu_custom_call" | custom-call | tf_op jit(solution)/shard_map/norm/pallas_call | solution.py:350
  16.6 1.7 %collective-permute-done.refs_5_ = bf16[816,128]{1,0:T(8,128)(2,1)S(1)} collective-permute-done((bf16[816,128]{1,0:T(8,128)(2,1)S(1)}, bf16[816,128]{1,0:T(8,128)(2,1)S(1)}, u32[]{:S(2)}, u32[]{:S(2)}) %collective-permute-start) | collective-permute-done | bytes 208928 | tf_op jit(solution)/shard_map/ppermute | solution.py:26
  18.9 0.5 collective-permute-start.7
  19.4 1.3 %collective-permute-done.8.refs_6_ = bf16[816,128]{1,0:T(8,128)(2,1)S(1)} collective-permute-done((bf16[816,128]{1,0:T(8,128)(2,1)S(1)}, bf16[816,128]{1,0:T(8,128)(2,1)S(1)}, u32[]{:S(2)}, u32[]{:S(2)}) %collective-permute-start.8) | collective-permute-done | bytes 208928 | tf_op jit(solution)/shard_map/ppermute | solution.py:336
  20.7 1.4 %collective-permute-start.9 = (bf16[816,128]{1,0:T(8,128)(2,1)S(1)}, bf16[816,128]{1,0:T(8,128)(2,1)S(1)}, u32[]{:S(2)}, u32[]{:S(2)}) collective-permute-start(bf16[816,128]{1,0:T(8,128)(2,1)S(1)} %collective-permute-done.8.refs_6_), channel_id=1, source_target_pairs={{0,16},{16,0},{1,17},{17,1},{2,18},{18,2},{3,19},{19,3},{4,20},{20... | collective-permute-start | bytes 626696 | tf_op jit(solution)/shard_map/ppermute | solution.py:26
  22.1 6.3 %attention.1 = (bf16[480,128]{1,0:T(8,128)(2,1)S(1)}, bf16[480,128]{1,0:T(8,128)(2,1)S(1)}, bf16[480,128]{1,0:T(8,128)(2,1)S(1)}, bf16[480,128]{1,0:T(8,128)(2,1)S(1)}) custom-call(s32[3]{0:T(128)S(1)} %pad_add_fusion.index_ref, bf16[768,1280]{1,0:T(8,128)(2,1)S(1)} %get-tuple-element.48.hidden_ref, s32[6,128]{1,0:T(8,128)S(1)} %bitcast.19, ...), custom_call_target="tpu_custom_call" | custom-call | tf_op jit(solution)/shard_map/attention/pallas_call | solution.py:372
  28.4 0.9 %collective-permute-done.10.refs_9_.refs_2_ = bf16[2,816,128]{2,1,0:T(8,128)(2,1)S(1)} collective-permute-done((bf16[2,816,128]{2,1,0:T(8,128)(2,1)S(1)}, bf16[2,816,128]{2,1,0:T(8,128)(2,1)S(1)}, u32[]{:S(2)}, u32[]{:S(2)}) %collective-permute-start.10) | collective-permute-done | bytes 417824 | tf_op jit(solution)/shard_map/ppermute | solution.py:26
  29.4 1.1 %collective-permute-start.16 = (bf16[2,816,128]{2,1,0:T(8,128)(2,1)S(1)}, bf16[2,816,128]{2,1,0:T(8,128)(2,1)S(1)}, u32[]{:S(2)}, u32[]{:S(2)}) collective-permute-start(bf16[2,816,128]{2,1,0:T(8,128)(2,1)S(1)} %pad_maximum_fusion.2), channel_id=1, source_target_pairs={{0,8},{4,12},{8,0},{12,4},{1,9},{5,13},{9,1},{13,5},{2,10},{6,14},... | collective-permute-start | bytes 1253384 | tf_op jit(solution)/shard_map/ppermute | solution.py:26
  30.6 1.4 %collective-permute-start.13 = (bf16[480,128]{1,0:T(8,128)(2,1)S(1)}, bf16[480,128]{1,0:T(8,128)(2,1)S(1)}, u32[]{:S(2)}, u32[]{:S(2)}) collective-permute-start(bf16[480,128]{1,0:T(8,128)(2,1)S(1)} %get-tuple-element.62), channel_id=1, source_target_pairs={{0,1},{1,0},{2,3},{3,2},{4,5},{5,4},{6,7},{7,6},{8,9},{9,8},{10,11... | collective-permute-start | bytes 368648 | tf_op jit(solution)/shard_map/ppermute | solution.py:26
  32.0 3.0 %collective-permute-start.14 = (bf16[480,128]{1,0:T(8,128)(2,1)S(1)}, bf16[480,128]{1,0:T(8,128)(2,1)S(1)}, u32[]{:S(2)}, u32[]{:S(2)}) collective-permute-start(bf16[480,128]{1,0:T(8,128)(2,1)S(1)} %get-tuple-element.63), channel_id=1, source_target_pairs={{0,2},{1,3},{2,0},{3,1},{4,6},{5,7},{6,4},{7,5},{8,10},{9,11},{10,... | collective-permute-start | bytes 368648 | tf_op jit(solution)/shard_map/ppermute | solution.py:26
  35.1 3.5 %collective-permute-done.13.refs_1_ = bf16[480,128]{1,0:T(8,128)(2,1)S(1)} collective-permute-done((bf16[480,128]{1,0:T(8,128)(2,1)S(1)}, bf16[480,128]{1,0:T(8,128)(2,1)S(1)}, u32[]{:S(2)}, u32[]{:S(2)}) %collective-permute-start.13) | collective-permute-done | bytes 122912 | tf_op jit(solution)/shard_map/ppermute | solution.py:26
  38.6 5.9 %collective-permute-done.14.refs_2_ = bf16[480,128]{1,0:T(8,128)(2,1)S(1)} collective-permute-done((bf16[480,128]{1,0:T(8,128)(2,1)S(1)}, bf16[480,128]{1,0:T(8,128)(2,1)S(1)}, u32[]{:S(2)}, u32[]{:S(2)}) %collective-permute-start.14) | collective-permute-done | bytes 122912 | tf_op jit(solution)/shard_map/ppermute | solution.py:26
  44.5 1.7 %collective-permute-done.17.refs_12_ = bf16[2,816,128]{2,1,0:T(8,128)(2,1)S(1)} collective-permute-done((bf16[2,816,128]{2,1,0:T(8,128)(2,1)S(1)}, bf16[2,816,128]{2,1,0:T(8,128)(2,1)S(1)}, u32[]{:S(2)}, u32[]{:S(2)}) %collective-permute-start.17) | collective-permute-done | bytes 417824 | tf_op jit(solution)/shard_map/ppermute | solution.py:26
  46.3 1.9 %project.1 = (bf16[96,1280]{1,0:T(8,128)(2,1)S(1)}, bf16[96,1280]{1,0:T(8,128)(2,1)S(1)}) custom-call(s32[3]{0:T(128)S(1)} %pad_add_fusion.index_ref, bf16[480,128]{1,0:T(8,128)(2,1)S(1)} %get-tuple-element.65.refs_0_, bf16[480,128]{1,0:T(8,128)(2,1)S(1)} %collective-permute-done.13.refs_1_, bf16[480,128]{1,0:T(8,128)(2,1)S(1)} %collective-permute-done.14.refs_2_, ...), custom_call_target="tpu_custom_call" | custom-call | tf_op jit(solution)/shard_map/project/pallas_call | solution.py:392
  48.7 1.6 %collective-permute-start.21 = (bf16[96,1280]{1,0:T(8,128)(2,1)S(1)}, bf16[96,1280]{1,0:T(8,128)(2,1)S(1)}, u32[]{:S(2)}, u32[]{:S(2)}) collective-permute-start(bf16[96,1280]{1,0:T(8,128)(2,1)S(1)} %get-tuple-element.72.refs_5_), channel_id=1, source_target_pairs={{0,8},{4,12},{8,0},{12,4},{1,9},{5,13},{9,1},{13,5},{2,10},{6,14},... | collective-permute-start | bytes 737288 | tf_op jit(solution)/shard_map/ppermute | solution.py:26
  50.3 6.8 %collective-permute-done.20.refs_8_ = bf16[96,1280]{1,0:T(8,128)(2,1)S(1)} collective-permute-done((bf16[96,1280]{1,0:T(8,128)(2,1)S(1)}, bf16[96,1280]{1,0:T(8,128)(2,1)S(1)}, u32[]{:S(2)}, u32[]{:S(2)}) %collective-permute-start.20) | collective-permute-done | bytes 245792 | tf_op jit(solution)/shard_map/ppermute | solution.py:26
  57.1 0.5 collective-permute-start.18
  57.6 4.0 %collective-permute-done.21.refs_9_ = bf16[96,1280]{1,0:T(8,128)(2,1)S(1)} collective-permute-done((bf16[96,1280]{1,0:T(8,128)(2,1)S(1)}, bf16[96,1280]{1,0:T(8,128)(2,1)S(1)}, u32[]{:S(2)}, u32[]{:S(2)}) %collective-permute-start.21) | collective-permute-done | bytes 245792 | tf_op jit(solution)/shard_map/ppermute | solution.py:26
  61.5 1.5 %collective-permute-done.23.refs_11_ = bf16[96,1280]{1,0:T(8,128)(2,1)S(1)} collective-permute-done((bf16[96,1280]{1,0:T(8,128)(2,1)S(1)}, bf16[96,1280]{1,0:T(8,128)(2,1)S(1)}, u32[]{:S(2)}, u32[]{:S(2)}) %collective-permute-start.23) | collective-permute-done | bytes 245792 | tf_op jit(solution)/shard_map/ppermute | solution.py:26
  63.0 1.8 %placement.1 = bf16[192,1280]{1,0:T(8,128)(2,1)} custom-call(s32[3]{0:T(128)S(1)} %pad_add_fusion.index_ref, bf16[816,128]{1,0:T(8,128)(2,1)S(1)} %pack_proj.1.refs_4_.refs_0_, bf16[4,816,128]{2,1,0:T(8,128)(2,1)S(1)} %collective-permute-done.11.refs_8_.refs_1_, bf16[2,816,128]{2,1,0:T(8,128)(2,1)S(1)} %collective-permute-done.10.refs_9_.refs_2_, ...), custom_call_target="tpu_custom_call" | custom-call | tf_op jit(solution)/shard_map/placement/pallas_call | solution.py:414
  (40 shorter events, 1.4 us)
Async XLA Ops:
  0.1 1.1 %copy-start.1 = (bf16[320,3,320]{2,0,1:T(8,128)(2,1)S(1)}, bf16[320,3,320]{2,0,1:T(8,128)(2,1)}, u32[]{:S(2)}) copy-start(bf16[320,3,320]{2,0,1:T(8,128)(2,1)} %param.11) | copy-start | bytes 1843204
  1.2 20.9 %copy-start.5 = (s32[768]{0:T(1024)S(1)}, s32[768]{0:T(1024)}, u32[]{:S(2)}) copy-start(s32[768]{0:T(1024)} %param.8) | copy-start | bytes 9220
  1.9 9.5 %collective-permute-start.2 = (bf16[3,832,128]{2,1,0:T(8,128)(2,1)S(1)}, bf16[3,832,128]{2,1,0:T(8,128)(2,1)S(1)}, u32[]{:S(2)}, u32[]{:S(2)}) collective-permute-start(bf16[3,832,128]{2,1,0:T(8,128)(2,1)S(1)} %get-tuple-element.41.refs_0_), channel_id=1, source_target_pairs={{0,4},{4,0},{8,12},{12,8},{1,5},{5,1},{9,13},{13,9},{2,6},{6,2},{1... | collective-permute-start | bytes 1916936 | tf_op jit(solution)/shard_map/ppermute | solution.py:26
  2.4 9.0 %collective-permute-start.1 = (bf16[832,128]{1,0:T(8,128)(2,1)S(1)}, bf16[832,128]{1,0:T(8,128)(2,1)S(1)}, u32[]{:S(2)}, u32[]{:S(2)}) collective-permute-start(bf16[832,128]{1,0:T(8,128)(2,1)S(1)} %get-tuple-element.40), channel_id=1, source_target_pairs={{0,8},{4,12},{8,0},{12,4},{1,9},{5,13},{9,1},{13,5},{2,10},{6,14},... | collective-permute-start | bytes 638984 | tf_op jit(solution)/shard_map/ppermute | solution.py:26
  5.0 0.9 %copy-start.2 = (bf16[320,320]{1,0:T(8,128)(2,1)S(1)}, bf16[320,320]{1,0:T(8,128)(2,1)}, u32[]{:S(2)}) copy-start(bf16[320,320]{1,0:T(8,128)(2,1)} %proj_ref.1) | copy-start | bytes 614404
  5.9 0.7 %copy-start.6 = (s32[192]{0:T(256)S(1)}, s32[192]{0:T(256)}, u32[]{:S(2)}) copy-start(s32[192]{0:T(256)} %param.9) | copy-start | bytes 2308
  6.7 11.6 %collective-permute-start = (bf16[816,128]{1,0:T(8,128)(2,1)S(1)}, bf16[816,128]{1,0:T(8,128)(2,1)S(1)}, u32[]{:S(2)}, u32[]{:S(2)}) collective-permute-start(bf16[816,128]{1,0:T(8,128)(2,1)S(1)} %pack_proj.1.refs_4_.refs_0_), channel_id=1, source_target_pairs={{0,1},{1,0},{2,3},{3,2},{4,5},{5,4},{6,7},{7,6},{8,9},{9,8},{10,11... | collective-permute-start | bytes 626696 | tf_op jit(solution)/shard_map/ppermute | solution.py:26
  8.3 12.4 %collective-permute-start.8 = (bf16[816,128]{1,0:T(8,128)(2,1)S(1)}, bf16[816,128]{1,0:T(8,128)(2,1)S(1)}, u32[]{:S(2)}, u32[]{:S(2)}) collective-permute-start(bf16[816,128]{1,0:T(8,128)(2,1)S(1)} %pack_proj.1.refs_4_.refs_0_), channel_id=1, source_target_pairs={{0,2},{1,3},{2,0},{3,1},{16,19},{17,18},{18,17},{19,16},{4,6},{5,7... | collective-permute-start | bytes 626696 | tf_op jit(solution)/shard_map/ppermute | solution.py:336
  10.9 7.9 %collective-permute-start.4 = (bf16[832,128]{1,0:T(8,128)(2,1)S(1)}, bf16[832,128]{1,0:T(8,128)(2,1)S(1)}, u32[]{:S(2)}, u32[]{:S(2)}) collective-permute-start(bf16[832,128]{1,0:T(8,128)(2,1)S(1)} %get-tuple-element.46), channel_id=1, source_target_pairs={{0,8},{4,12},{8,0},{12,4},{1,9},{5,13},{9,1},{13,5},{2,10},{6,14},... | collective-permute-start | bytes 638984 | tf_op jit(solution)/shard_map/ppermute | solution.py:26
  11.4 7.4 %collective-permute-start.3 = (bf16[832,128]{1,0:T(8,128)(2,1)S(1)}, bf16[832,128]{1,0:T(8,128)(2,1)S(1)}, u32[]{:S(2)}, u32[]{:S(2)}) collective-permute-start(bf16[832,128]{1,0:T(8,128)(2,1)S(1)} %collective-permute-done.1.refs_2_), channel_id=1, source_target_pairs={{0,16},{16,0},{1,17},{17,1},{2,18},{18,2},{3,19},{19,3},{4,20},{20... | collective-permute-start | bytes 638984 | tf_op jit(solution)/shard_map/ppermute | solution.py:26
  12.8 6.0 %collective-permute-start.5 = (bf16[832,128]{1,0:T(8,128)(2,1)S(1)}, bf16[832,128]{1,0:T(8,128)(2,1)S(1)}, u32[]{:S(2)}, u32[]{:S(2)}) collective-permute-start(bf16[832,128]{1,0:T(8,128)(2,1)S(1)} %collective-permute-done.1.refs_2_), channel_id=1, source_target_pairs={{0,4},{4,0},{8,12},{12,8},{1,5},{5,1},{9,13},{13,9},{2,6},{6,2},{1... | collective-permute-start | bytes 638984 | tf_op jit(solution)/shard_map/ppermute | solution.py:26
  12.8 1.5 %copy-start = (bf16[768,1280]{1,0:T(8,128)(2,1)S(1)}, bf16[768,1280]{1,0:T(8,128)(2,1)}, u32[]{:S(2)}) copy-start(bf16[768,1280]{1,0:T(8,128)(2,1)} %patches_ref) | copy-start | bytes 5898244
  14.4 0.7 %copy-start.3 = (f32[1280]{0:T(1024)S(1)}, f32[1280]{0:T(1024)}, u32[]{:S(2)}) copy-start(f32[1280]{0:T(1024)} %gain_ref.1) | copy-start | bytes 15364
  18.4 10.9 %collective-permute-start.10 = (bf16[2,816,128]{2,1,0:T(8,128)(2,1)S(1)}, bf16[2,816,128]{2,1,0:T(8,128)(2,1)S(1)}, u32[]{:S(2)}, u32[]{:S(2)}) collective-permute-start(bf16[2,816,128]{2,1,0:T(8,128)(2,1)S(1)} %pad_maximum_fusion.1), channel_id=1, source_target_pairs={{0,8},{4,12},{8,0},{12,4},{1,9},{5,13},{9,1},{13,5},{2,10},{6,14},... | collective-permute-start | bytes 1253384 | tf_op jit(solution)/shard_map/ppermute | solution.py:26
  18.8 3.3 %collective-permute-start.6 = (bf16[832,128]{1,0:T(8,128)(2,1)S(1)}, bf16[832,128]{1,0:T(8,128)(2,1)S(1)}, u32[]{:S(2)}, u32[]{:S(2)}) collective-permute-start(bf16[832,128]{1,0:T(8,128)(2,1)S(1)} %collective-permute-done.3.refs_3_), channel_id=1, source_target_pairs={{0,4},{4,0},{8,12},{12,8},{1,5},{5,1},{9,13},{13,9},{2,6},{6,2},{1... | collective-permute-start | bytes 638984 | tf_op jit(solution)/shard_map/ppermute | solution.py:26
  18.9 3.2 %collective-permute-start.7 = (bf16[832,128]{1,0:T(8,128)(2,1)S(1)}, bf16[832,128]{1,0:T(8,128)(2,1)S(1)}, u32[]{:S(2)}, u32[]{:S(2)}) collective-permute-start(bf16[832,128]{1,0:T(8,128)(2,1)S(1)} %collective-permute-done.4.refs_4_), channel_id=1, source_target_pairs={{0,4},{4,0},{8,12},{12,8},{1,5},{5,1},{9,13},{13,9},{2,6},{6,2},{1... | collective-permute-start | bytes 638984 | tf_op jit(solution)/shard_map/ppermute | solution.py:26
  20.7 8.6 %collective-permute-start.9 = (bf16[816,128]{1,0:T(8,128)(2,1)S(1)}, bf16[816,128]{1,0:T(8,128)(2,1)S(1)}, u32[]{:S(2)}, u32[]{:S(2)}) collective-permute-start(bf16[816,128]{1,0:T(8,128)(2,1)S(1)} %collective-permute-done.8.refs_6_), channel_id=1, source_target_pairs={{0,16},{16,0},{1,17},{17,1},{2,18},{18,2},{3,19},{19,3},{4,20},{20... | collective-permute-start | bytes 626696 | tf_op jit(solution)/shard_map/ppermute | solution.py:26
  28.4 17.8 %copy-start.4 = (f32[1280]{0:T(1024)S(1)}, f32[1280]{0:T(1024)}, u32[]{:S(2)}) copy-start(f32[1280]{0:T(1024)} %refs_14_.1) | copy-start | bytes 15364
  29.4 15.1 %collective-permute-start.16 = (bf16[2,816,128]{2,1,0:T(8,128)(2,1)S(1)}, bf16[2,816,128]{2,1,0:T(8,128)(2,1)S(1)}, u32[]{:S(2)}, u32[]{:S(2)}) collective-permute-start(bf16[2,816,128]{2,1,0:T(8,128)(2,1)S(1)} %pad_maximum_fusion.2), channel_id=1, source_target_pairs={{0,8},{4,12},{8,0},{12,4},{1,9},{5,13},{9,1},{13,5},{2,10},{6,14},... | collective-permute-start | bytes 1253384 | tf_op jit(solution)/shard_map/ppermute | solution.py:26
  30.5 15.7 %collective-permute-start.11 = (bf16[4,816,128]{2,1,0:T(8,128)(2,1)S(1)}, bf16[4,816,128]{2,1,0:T(8,128)(2,1)S(1)}, u32[]{:S(2)}, u32[]{:S(2)}) collective-permute-start(bf16[4,816,128]{2,1,0:T(8,128)(2,1)S(1)} %pad_maximum_fusion), channel_id=1, source_target_pairs={{0,4},{4,0},{8,12},{12,8},{1,5},{5,1},{9,13},{13,9},{2,6},{6,2},{1... | collective-permute-start | bytes 2506760 | tf_op jit(solution)/shard_map/ppermute | solution.py:26
  30.6 7.9 %collective-permute-start.13 = (bf16[480,128]{1,0:T(8,128)(2,1)S(1)}, bf16[480,128]{1,0:T(8,128)(2,1)S(1)}, u32[]{:S(2)}, u32[]{:S(2)}) collective-permute-start(bf16[480,128]{1,0:T(8,128)(2,1)S(1)} %get-tuple-element.62), channel_id=1, source_target_pairs={{0,1},{1,0},{2,3},{3,2},{4,5},{5,4},{6,7},{7,6},{8,9},{9,8},{10,11... | collective-permute-start | bytes 368648 | tf_op jit(solution)/shard_map/ppermute | solution.py:26
  32.0 12.5 %collective-permute-start.14 = (bf16[480,128]{1,0:T(8,128)(2,1)S(1)}, bf16[480,128]{1,0:T(8,128)(2,1)S(1)}, u32[]{:S(2)}, u32[]{:S(2)}) collective-permute-start(bf16[480,128]{1,0:T(8,128)(2,1)S(1)} %get-tuple-element.63), channel_id=1, source_target_pairs={{0,2},{1,3},{2,0},{3,1},{4,6},{5,7},{6,4},{7,5},{8,10},{9,11},{10,... | collective-permute-start | bytes 368648 | tf_op jit(solution)/shard_map/ppermute | solution.py:26
  35.1 9.4 %collective-permute-start.15 = (bf16[480,128]{1,0:T(8,128)(2,1)S(1)}, bf16[480,128]{1,0:T(8,128)(2,1)S(1)}, u32[]{:S(2)}, u32[]{:S(2)}) collective-permute-start(bf16[480,128]{1,0:T(8,128)(2,1)S(1)} %get-tuple-element.64), channel_id=1, source_target_pairs={{0,3},{1,2},{2,1},{3,0},{4,7},{5,6},{6,5},{7,4},{8,11},{9,10},{10,... | collective-permute-start | bytes 368648 | tf_op jit(solution)/shard_map/ppermute | solution.py:26
  38.6 5.9 %collective-permute-start.12 = (bf16[2,816,128]{2,1,0:T(8,128)(2,1)S(1)}, bf16[2,816,128]{2,1,0:T(8,128)(2,1)S(1)}, u32[]{:S(2)}, u32[]{:S(2)}) collective-permute-start(bf16[2,816,128]{2,1,0:T(8,128)(2,1)S(1)} %collective-permute-done.10.refs_9_.refs_2_), channel_id=1, source_target_pairs={{0,4},{4,0},{8,12},{12,8},{1,5},{5,1},{9,13},{13,9},{2,6},{6,2},{1... | collective-permute-start | bytes 1253384 | tf_op jit(solution)/shard_map/ppermute | solution.py:26
  44.5 1.8 %collective-permute-start.17 = (bf16[2,816,128]{2,1,0:T(8,128)(2,1)S(1)}, bf16[2,816,128]{2,1,0:T(8,128)(2,1)S(1)}, u32[]{:S(2)}, u32[]{:S(2)}) collective-permute-start(bf16[2,816,128]{2,1,0:T(8,128)(2,1)S(1)} %collective-permute-done.16.refs_10_), channel_id=1, source_target_pairs={{0,4},{4,0},{8,12},{12,8},{1,5},{5,1},{9,13},{13,9},{2,6},{6,2},{1... | collective-permute-start | bytes 1253384 | tf_op jit(solution)/shard_map/ppermute | solution.py:26
  48.2 8.9 %collective-permute-start.20 = (bf16[96,1280]{1,0:T(8,128)(2,1)S(1)}, bf16[96,1280]{1,0:T(8,128)(2,1)S(1)}, u32[]{:S(2)}, u32[]{:S(2)}) collective-permute-start(bf16[96,1280]{1,0:T(8,128)(2,1)S(1)} %get-tuple-element.71.refs_4_), channel_id=1, source_target_pairs={{0,8},{4,12},{8,0},{12,4},{1,9},{5,13},{9,1},{13,5},{2,10},{6,14},... | collective-permute-start | bytes 737288 | tf_op jit(solution)/shard_map/ppermute | solution.py:26
  48.7 12.9 %collective-permute-start.21 = (bf16[96,1280]{1,0:T(8,128)(2,1)S(1)}, bf16[96,1280]{1,0:T(8,128)(2,1)S(1)}, u32[]{:S(2)}, u32[]{:S(2)}) collective-permute-start(bf16[96,1280]{1,0:T(8,128)(2,1)S(1)} %get-tuple-element.72.refs_5_), channel_id=1, source_target_pairs={{0,8},{4,12},{8,0},{12,4},{1,9},{5,13},{9,1},{13,5},{2,10},{6,14},... | collective-permute-start | bytes 737288 | tf_op jit(solution)/shard_map/ppermute | solution.py:26
  57.1 4.5 %collective-permute-start.22 = (bf16[96,1280]{1,0:T(8,128)(2,1)S(1)}, bf16[96,1280]{1,0:T(8,128)(2,1)S(1)}, u32[]{:S(2)}, u32[]{:S(2)}) collective-permute-start(bf16[96,1280]{1,0:T(8,128)(2,1)S(1)} %collective-permute-done.20.refs_8_), channel_id=1, source_target_pairs={{0,4},{4,0},{8,12},{12,8},{1,5},{5,1},{9,13},{13,9},{2,6},{6,2},{1... | collective-permute-start | bytes 737288 | tf_op jit(solution)/shard_map/ppermute | solution.py:26
  57.1 4.5 %collective-permute-start.18 = (bf16[96,1280]{1,0:T(8,128)(2,1)S(1)}, bf16[96,1280]{1,0:T(8,128)(2,1)S(1)}, u32[]{:S(2)}, u32[]{:S(2)}) collective-permute-start(bf16[96,1280]{1,0:T(8,128)(2,1)S(1)} %get-tuple-element.71.refs_4_), channel_id=1, source_target_pairs={{0,4},{4,0},{8,12},{12,8},{1,5},{5,1},{9,13},{13,9},{2,6},{6,2},{1... | collective-permute-start | bytes 737288 | tf_op jit(solution)/shard_map/ppermute | solution.py:26
  57.6 4.0 %collective-permute-start.19 = (bf16[96,1280]{1,0:T(8,128)(2,1)S(1)}, bf16[96,1280]{1,0:T(8,128)(2,1)S(1)}, u32[]{:S(2)}, u32[]{:S(2)}) collective-permute-start(bf16[96,1280]{1,0:T(8,128)(2,1)S(1)} %get-tuple-element.72.refs_5_), channel_id=1, source_target_pairs={{0,4},{4,0},{8,12},{12,8},{1,5},{5,1},{9,13},{13,9},{2,6},{6,2},{1... | collective-permute-start | bytes 737288 | tf_op jit(solution)/shard_map/ppermute | solution.py:26
  61.5 1.5 %collective-permute-start.23 = (bf16[96,1280]{1,0:T(8,128)(2,1)S(1)}, bf16[96,1280]{1,0:T(8,128)(2,1)S(1)}, u32[]{:S(2)}, u32[]{:S(2)}) collective-permute-start(bf16[96,1280]{1,0:T(8,128)(2,1)S(1)} %collective-permute-done.21.refs_9_), channel_id=1, source_target_pairs={{0,4},{4,0},{8,12},{12,8},{1,5},{5,1},{9,13},{13,9},{2,6},{6,2},{1... | collective-permute-start | bytes 737288 | tf_op jit(solution)/shard_map/ppermute | solution.py:26

commit v19 on v18

--- a/solution.py
+++ b/solution.py
@@ -85,7 +85,8 @@
 
 
 NOTE = 16
-SPARE = 32
+SPARE = 16
+FAR_SPARE = 48
 
 
 def write_note(place, lanes):
@@ -123,10 +124,18 @@
     value_ref[...] = all_ref[2]
 
 
-def pack_proj_kernel(proj_ref, place_ref, out_ref):
-    count = out_ref.shape[0] - NOTE
-    out_ref[:count, :] = pack(proj_ref[...])
-    out_ref[count:, :] = write_note(place_ref[...], out_ref.shape[1])
+def pack_proj_kernel(proj_ref, out_ref, far_ref):
+    count = out_ref.shape[0]
+    out_ref[...] = pack(proj_ref[...])
+    far_ref[:count, :] = out_ref[...]
+    far_ref[count:, :] = jnp.zeros((far_ref.shape[0] - count, far_ref.shape[1]), BF16)
+
+
+def near_kernel(own_ref, next_ref, place_ref, out_ref):
+    count = own_ref.shape[0]
+    for i, ref in enumerate((own_ref, next_ref)):
+        out_ref[i, :count, :] = ref[...]
+        out_ref[i, count:, :] = write_note(place_ref[...], out_ref.shape[2])
 
 
 def norm_kernel(index_ref, patches_ref, gain_ref, hidden_ref, own_ref):
@@ -239,9 +248,7 @@
     mains = []
     rests = []
     for key in range(n_ctx):
-        pieces = []
-        for ref in [blocks.pop(0) for _ in range((4, 1)[key] if key < 2 else 2)]:
-            pieces += [ref[...]] if len(ref.shape) == 2 else [ref[i] for i in range(ref.shape[0])]
+        pieces = [ref[i] for ref in (blocks.pop(0), blocks.pop(0)) for i in range(2)]
         halves = [unpack(p, width, col) for p in pieces]
         both = []
         for half in ([h[0] for h in halves], [h[1] for h in halves]):
@@ -322,19 +329,19 @@
         compiler_params=params(8),
         name="pack",
     )(index, jnp.transpose(w_qkv, (1, 0, 2)))
-    w_proj = pl.pallas_call(
+    w_proj, far = pl.pallas_call(
         pack_proj_kernel,
-        out_shape=shape(piece[0] + NOTE, piece[1]),
-        in_specs=[VMEM, VMEM],
-        out_specs=VMEM,
+        out_shape=(shape(*piece), shape(piece[0] + FAR_SPARE, piece[1])),
+        in_specs=[VMEM],
+        out_specs=(VMEM, VMEM),
         compiler_params=params(8),
         name="pack_proj",
-    )(w_proj, place.reshape(1, groups))
+    )(w_proj)
     first = gather_cross(first, n_ctx)
     value = gather_cross(value, n_ctx)
     twin = over_core(own)
     far = lax.ppermute(
-        w_proj,
+        far,
         ("dp", "tensor"),
         [
             (d * n_ten + t, d * n_ten + (t ^ (2 + d % 2)))
@@ -356,12 +363,21 @@
         name="norm",
     )(index, patches, gain_attn)
     by_one, hidden = together(by_one, hidden)
-    low = gather_cross(jnp.stack([w_proj, by_one]), n_ctx)
+    near = pl.pallas_call(
+        near_kernel,
+        out_shape=shape(2, piece[0] + NOTE, piece[1]),
+        in_specs=[VMEM] * 3,
+        out_specs=VMEM,
+        compiler_params=params(8),
+        name="near",
+    )(w_proj, by_one, place.reshape(1, groups))
+    low = gather_cross(near, n_ctx)
     second, value, first_twin, hidden = together(second, value, first_twin, hidden)
 
     second_twin = {k: over_core(second[k]) for k in cross}
     value_twin = {k: over_core(value[k]) for k in cross}
     far, *_ = together(far, *second.values())
+    far = far[: piece[0]]
     far2 = over_dp(far)
 
     shard_list = [own, twin]
@@ -384,7 +400,8 @@
     mixed, far, far2, low = together(list(mixed), far, far2, low)
     received = [mixed[0]] + [swap(mixed[s], "tensor", n_ten, s) for s in range(1, n_ten)]
     high = gather_cross(jnp.stack([far, far2]), n_ctx)
-    blocks = [w_proj, by_one, far, far2, over_core(jnp.stack([w_proj, by_one, far, far2]))]
+    far_pair = jnp.stack([far, far2])
+    blocks = [near, far_pair, over_core(near), over_core(far_pair)]
     low_twin = {k: over_core(low[k]) for k in cross}
     received, high = together(received, high)
     for k in cross:
@@ -408,7 +425,7 @@
         for k in list(crossed):
             crossed[k ^ 1] = over_core(crossed[k])
         gathered.append(crossed)
-    notes = [w_proj, blocks[4]]
+    notes = [near, blocks[2]]
     for k in cross:
         notes += [low[k], low_twin[k]]
     return pl.pallas_call(

time: 65.2 us -> 65.2 us (level)
  starting transfers between devices: 19.8 us -> 21 us
  local copies, waits for them, and re-layouts: 4.99 us -> 4.33 us
    ppermute x23 -> x24, starting transfers between devices: 17.2 us -> 18.4 us  [swap(): return lax.ppermute(x, axis, [(i, i ^ bit) for i in range(size)])]
    ppermute x23 -> x24, waiting for transfers between devices: 26 us -> 25.1 us  [swap(): return lax.ppermute(x, axis, [(i, i ^ bit) for i in range(size)])]
    unnamed x14, local copies, waits for them, and re-layouts: 4.99 us -> 4.32 us
  transfers between devices with their start and end apart: 24 -> 25, of which waited for: 9 -> 10; matrix products, arithmetic and copies ran while one was open for 0% -> 0% of each run, Pallas kernels for 12% -> 12%
where the time goes in v19:
time: 65.2 us; the launch traced here: 65 us
  waiting for transfers between devices  27 us (41%)
  starting transfers between devices  21 us (32%)
  Pallas kernels  12.4 us (19%)
  local copies, waits for them, and re-layouts  4.33 us (7%)
    ppermute x24, waiting for transfers between devices, swap(): return lax.ppermute(x, axis, [(i, i ^ bit) for i in range(size)])  25.1 us
    ppermute x24, starting transfers between devices, swap(): return lax.ppermute(x, axis, [(i, i ^ bit) for i in range(size)])  18.4 us
    pallas_call x1, Pallas kernels, local(): pl.pallas_call(functools.partial(attention_kernel, n_ctx, width), out_sha...  6.32 us
    unnamed x14, local copies, waits for them, and re-layouts  4.32 us
    ppermute x1, starting transfers between devices, local(): lax.ppermute(far, ('dp', 'tensor'), [(d * n_ten + t, d * n_ten + (t ^ 2 +...  2.59 us
    pallas_call x1, Pallas kernels, local(): pl.pallas_call(functools.partial(project_kernel, n_ctx, width, col), out_...  1.93 us
    ppermute x1, waiting for transfers between devices, local(): lax.ppermute(far, ('dp', 'tensor'), [(d * n_ten + t, d * n_ten + (t ^ 2 +...  1.85 us
    pallas_call x1, Pallas kernels, local(): pl.pallas_call(functools.partial(place_kernel, n_ctx), out_shape=shape(gr...  1.84 us
  transfers between devices with their start and end apart: 25, of which 10 were waited for; matrix products, arithmetic and copies ran while one was open for 0% of the time, Pallas kernels for 12%

profile of v19, /device:TPU:0, one launch (start us, length us, event | category | flops | bytes accessed | tf_op | source)
XLA Modules:
  0.0 65.0 jit_solution(10140831902339130268)
XLA Ops:
  0.1 1.1 %copy-done.1 = bf16[320,3,320]{2,0,1:T(8,128)(2,1)S(1)} copy-done((bf16[320,3,320]{2,0,1:T(8,128)(2,1)S(1)}, bf16[320,3,320]{2,0,1:T(8,128)(2,1)}, u32[]{:S(2)}) %copy-start.1) | copy-done | bytes 614424
  1.2 0.7 %pack.1 = (bf16[816,128]{1,0:T(8,128)(2,1)S(1)}, bf16[816,128]{1,0:T(8,128)(2,1)S(1)}, bf16[3,816,128]{2,1,0:T(8,128)(2,1)S(1)}) custom-call(s32[3]{0:T(128)S(1)} %pad_add_fusion.index_ref, bf16[3,320,320]{2,1,0:T(8,128)(2,1)S(1)} %bitcast.8), custom_call_target="tpu_custom_call" | custom-call | tf_op jit(solution)/shard_map/pack/pallas_call | solution.py:324
  1.9 0.5 collective-permute-start.2
  2.4 2.6 %collective-permute-start.1 = (bf16[816,128]{1,0:T(8,128)(2,1)S(1)}, bf16[816,128]{1,0:T(8,128)(2,1)S(1)}, u32[]{:S(2)}, u32[]{:S(2)}) collective-permute-start(bf16[816,128]{1,0:T(8,128)(2,1)S(1)} %get-tuple-element.43), channel_id=1, source_target_pairs={{0,8},{4,12},{8,0},{12,4},{1,9},{5,13},{9,1},{13,5},{2,10},{6,14},... | collective-permute-start | bytes 626696 | tf_op jit(solution)/shard_map/ppermute | solution.py:26
  5.0 0.9 %copy-done.2 = bf16[320,320]{1,0:T(8,128)(2,1)S(1)} copy-done((bf16[320,320]{1,0:T(8,128)(2,1)S(1)}, bf16[320,320]{1,0:T(8,128)(2,1)}, u32[]{:S(2)}) %copy-start.2) | copy-done | bytes 204824
  6.0 1.6 %collective-permute-start = (bf16[800,128]{1,0:T(8,128)(2,1)S(1)}, bf16[800,128]{1,0:T(8,128)(2,1)S(1)}, u32[]{:S(2)}, u32[]{:S(2)}) collective-permute-start(bf16[800,128]{1,0:T(8,128)(2,1)S(1)} %get-tuple-element.42.own_ref), channel_id=1, source_target_pairs={{0,1},{1,0},{2,3},{3,2},{4,5},{5,4},{6,7},{7,6},{8,9},{9,8},{10,11... | collective-permute-start | bytes 614408 | tf_op jit(solution)/shard_map/ppermute | solution.py:26
  7.7 2.6 %collective-permute-start.9 = (bf16[848,128]{1,0:T(8,128)(2,1)S(1)}, bf16[848,128]{1,0:T(8,128)(2,1)S(1)}, u32[]{:S(2)}, u32[]{:S(2)}) collective-permute-start(bf16[848,128]{1,0:T(8,128)(2,1)S(1)} %get-tuple-element.60), channel_id=1, source_target_pairs={{0,2},{1,3},{2,0},{3,1},{16,19},{17,18},{18,17},{19,16},{4,6},{5,7... | collective-permute-start | bytes 651272 | tf_op jit(solution)/shard_map/ppermute | solution.py:343
  10.3 0.5 collective-permute-start.5
  10.8 1.7 %collective-permute-start.4 = (bf16[816,128]{1,0:T(8,128)(2,1)S(1)}, bf16[816,128]{1,0:T(8,128)(2,1)S(1)}, u32[]{:S(2)}, u32[]{:S(2)}) collective-permute-start(bf16[816,128]{1,0:T(8,128)(2,1)S(1)} %collective-permute-done.1.refs_2_), channel_id=1, source_target_pairs={{0,16},{16,0},{1,17},{17,1},{2,18},{18,2},{3,19},{19,3},{4,20},{20... | collective-permute-start | bytes 626696 | tf_op jit(solution)/shard_map/ppermute | solution.py:26
  12.5 1.5 %copy-done = bf16[768,1280]{1,0:T(8,128)(2,1)S(1)} copy-done((bf16[768,1280]{1,0:T(8,128)(2,1)S(1)}, bf16[768,1280]{1,0:T(8,128)(2,1)}, u32[]{:S(2)}) %copy-start) | copy-done | bytes 1966104
  14.0 0.7 %copy-done.3 = f32[1280]{0:T(1024)S(1)} copy-done((f32[1280]{0:T(1024)S(1)}, f32[1280]{0:T(1024)}, u32[]{:S(2)}) %copy-start.3) | copy-done | bytes 5144
  14.7 1.6 %norm.1 = (bf16[768,1280]{1,0:T(8,128)(2,1)S(1)}, bf16[192,1280]{1,0:T(8,128)(2,1)S(1)}) custom-call(s32[3]{0:T(128)S(1)} %pad_add_fusion.index_ref, bf16[768,1280]{1,0:T(8,128)(2,1)S(1)} %copy-done, f32[1280]{0:T(1024)S(1)} %copy-done.3), custom_call_target="tpu_custom_call" | custom-call | tf_op jit(solution)/shard_map/norm/pallas_call | solution.py:357
  16.3 1.2 %collective-permute-done.next_ref = bf16[800,128]{1,0:T(8,128)(2,1)S(1)} collective-permute-done((bf16[800,128]{1,0:T(8,128)(2,1)S(1)}, bf16[800,128]{1,0:T(8,128)(2,1)S(1)}, u32[]{:S(2)}, u32[]{:S(2)}) %collective-permute-start) | collective-permute-done | bytes 204832 | tf_op jit(solution)/shard_map/ppermute | solution.py:26
  18.5 1.9 %collective-permute-done.9 = bf16[848,128]{1,0:T(8,128)(2,1)S(1)} collective-permute-done((bf16[848,128]{1,0:T(8,128)(2,1)S(1)}, bf16[848,128]{1,0:T(8,128)(2,1)S(1)}, u32[]{:S(2)}, u32[]{:S(2)}) %collective-permute-start.9) | collective-permute-done | bytes 217120 | tf_op jit(solution)/shard_map/ppermute | solution.py:343
  20.4 1.2 %collective-permute-start.10 = (bf16[800,128]{1,0:T(8,128)(2,1)S(1)}, bf16[800,128]{1,0:T(8,128)(2,1)S(1)}, u32[]{:S(2)}, u32[]{:S(2)}) collective-permute-start(bf16[800,128]{1,0:T(8,128)(2,1)S(1)} %slice.3), channel_id=1, source_target_pairs={{0,16},{16,0},{1,17},{17,1},{2,18},{18,2},{3,19},{19,3},{4,20},{20... | collective-permute-start | bytes 614408 | tf_op jit(solution)/shard_map/ppermute | solution.py:26
  21.6 6.3 %attention.1 = (bf16[480,128]{1,0:T(8,128)(2,1)S(1)}, bf16[480,128]{1,0:T(8,128)(2,1)S(1)}, bf16[480,128]{1,0:T(8,128)(2,1)S(1)}, bf16[480,128]{1,0:T(8,128)(2,1)S(1)}) custom-call(s32[3]{0:T(128)S(1)} %pad_add_fusion.index_ref, bf16[768,1280]{1,0:T(8,128)(2,1)S(1)} %get-tuple-element.51.hidden_ref, s32[6,128]{1,0:T(8,128)S(1)} %bitcast.9, ...), custom_call_target="tpu_custom_call" | custom-call | tf_op jit(solution)/shard_map/attention/pallas_call | solution.py:388
  28.0 0.5 collective-permute-done.11.refs_8_.refs_2_
  28.5 1.6 %collective-permute-start.16 = (bf16[2,800,128]{2,1,0:T(8,128)(2,1)S(1)}, bf16[2,800,128]{2,1,0:T(8,128)(2,1)S(1)}, u32[]{:S(2)}, u32[]{:S(2)}) collective-permute-start(bf16[2,800,128]{2,1,0:T(8,128)(2,1)S(1)} %pad_maximum_fusion.refs_5_), channel_id=1, source_target_pairs={{0,8},{4,12},{8,0},{12,4},{1,9},{5,13},{9,1},{13,5},{2,10},{6,14},... | collective-permute-start | bytes 1228808 | tf_op jit(solution)/shard_map/ppermute | solution.py:26
  30.1 2.0 %collective-permute-start.13 = (bf16[480,128]{1,0:T(8,128)(2,1)S(1)}, bf16[480,128]{1,0:T(8,128)(2,1)S(1)}, u32[]{:S(2)}, u32[]{:S(2)}) collective-permute-start(bf16[480,128]{1,0:T(8,128)(2,1)S(1)} %get-tuple-element.64), channel_id=1, source_target_pairs={{0,1},{1,0},{2,3},{3,2},{4,5},{5,4},{6,7},{7,6},{8,9},{9,8},{10,11... | collective-permute-start | bytes 368648 | tf_op jit(solution)/shard_map/ppermute | solution.py:26
  32.1 2.6 %collective-permute-start.14 = (bf16[480,128]{1,0:T(8,128)(2,1)S(1)}, bf16[480,128]{1,0:T(8,128)(2,1)S(1)}, u32[]{:S(2)}, u32[]{:S(2)}) collective-permute-start(bf16[480,128]{1,0:T(8,128)(2,1)S(1)} %get-tuple-element.65), channel_id=1, source_target_pairs={{0,2},{1,3},{2,0},{3,1},{4,6},{5,7},{6,4},{7,5},{8,10},{9,11},{10,... | collective-permute-start | bytes 368648 | tf_op jit(solution)/shard_map/ppermute | solution.py:26
  34.7 1.5 %collective-permute-done.13.refs_1_ = bf16[480,128]{1,0:T(8,128)(2,1)S(1)} collective-permute-done((bf16[480,128]{1,0:T(8,128)(2,1)S(1)}, bf16[480,128]{1,0:T(8,128)(2,1)S(1)}, u32[]{:S(2)}, u32[]{:S(2)}) %collective-permute-start.13) | collective-permute-done | bytes 122912 | tf_op jit(solution)/shard_map/ppermute | solution.py:26
  36.3 7.8 %collective-permute-done.14.refs_2_ = bf16[480,128]{1,0:T(8,128)(2,1)S(1)} collective-permute-done((bf16[480,128]{1,0:T(8,128)(2,1)S(1)}, bf16[480,128]{1,0:T(8,128)(2,1)S(1)}, u32[]{:S(2)}, u32[]{:S(2)}) %collective-permute-start.14) | collective-permute-done | bytes 122912 | tf_op jit(solution)/shard_map/ppermute | solution.py:26
  44.6 1.2 %collective-permute-done.17.refs_7_ = bf16[2,800,128]{2,1,0:T(8,128)(2,1)S(1)} collective-permute-done((bf16[2,800,128]{2,1,0:T(8,128)(2,1)S(1)}, bf16[2,800,128]{2,1,0:T(8,128)(2,1)S(1)}, u32[]{:S(2)}, u32[]{:S(2)}) %collective-permute-start.17) | collective-permute-done | bytes 409632 | tf_op jit(solution)/shard_map/ppermute | solution.py:26
  45.8 0.6 collective-permute-done.18.refs_11_
  46.4 1.9 %project.1 = (bf16[96,1280]{1,0:T(8,128)(2,1)S(1)}, bf16[96,1280]{1,0:T(8,128)(2,1)S(1)}) custom-call(s32[3]{0:T(128)S(1)} %pad_add_fusion.index_ref, bf16[480,128]{1,0:T(8,128)(2,1)S(1)} %get-tuple-element.69.refs_0_, bf16[480,128]{1,0:T(8,128)(2,1)S(1)} %collective-permute-done.13.refs_1_, bf16[480,128]{1,0:T(8,128)(2,1)S(1)} %collective-permute-done.14.refs_2_, ...), custom_call_target="tpu_custom_call" | custom-call | tf_op jit(solution)/shard_map/project/pallas_call | solution.py:409
  48.3 0.5 collective-permute-start.21
  48.9 1.6 %collective-permute-start.22 = (bf16[96,1280]{1,0:T(8,128)(2,1)S(1)}, bf16[96,1280]{1,0:T(8,128)(2,1)S(1)}, u32[]{:S(2)}, u32[]{:S(2)}) collective-permute-start(bf16[96,1280]{1,0:T(8,128)(2,1)S(1)} %get-tuple-element.76.refs_5_), channel_id=1, source_target_pairs={{0,8},{4,12},{8,0},{12,4},{1,9},{5,13},{9,1},{13,5},{2,10},{6,14},... | collective-permute-start | bytes 737288 | tf_op jit(solution)/shard_map/ppermute | solution.py:26
  50.4 6.8 %collective-permute-done.21.refs_8_ = bf16[96,1280]{1,0:T(8,128)(2,1)S(1)} collective-permute-done((bf16[96,1280]{1,0:T(8,128)(2,1)S(1)}, bf16[96,1280]{1,0:T(8,128)(2,1)S(1)}, u32[]{:S(2)}, u32[]{:S(2)}) %collective-permute-start.21) | collective-permute-done | bytes 245792 | tf_op jit(solution)/shard_map/ppermute | solution.py:26
  57.2 0.5 collective-permute-start.19
  57.7 4.0 %collective-permute-done.22.refs_9_ = bf16[96,1280]{1,0:T(8,128)(2,1)S(1)} collective-permute-done((bf16[96,1280]{1,0:T(8,128)(2,1)S(1)}, bf16[96,1280]{1,0:T(8,128)(2,1)S(1)}, u32[]{:S(2)}, u32[]{:S(2)}) %collective-permute-start.22) | collective-permute-done | bytes 245792 | tf_op jit(solution)/shard_map/ppermute | solution.py:26
  61.7 1.5 %collective-permute-done.24.refs_11_ = bf16[96,1280]{1,0:T(8,128)(2,1)S(1)} collective-permute-done((bf16[96,1280]{1,0:T(8,128)(2,1)S(1)}, bf16[96,1280]{1,0:T(8,128)(2,1)S(1)}, u32[]{:S(2)}, u32[]{:S(2)}) %collective-permute-start.24) | collective-permute-done | bytes 245792 | tf_op jit(solution)/shard_map/ppermute | solution.py:26
  63.2 1.8 %placement.1 = bf16[192,1280]{1,0:T(8,128)(2,1)} custom-call(s32[3]{0:T(128)S(1)} %pad_add_fusion.index_ref, bf16[2,816,128]{2,1,0:T(8,128)(2,1)S(1)} %near.1.refs_4_.refs_0_, bf16[2,816,128]{2,1,0:T(8,128)(2,1)S(1)} %collective-permute-done.3.refs_6_.refs_1_, bf16[2,816,128]{2,1,0:T(8,128)(2,1)S(1)} %collective-permute-done.11.refs_8_.refs_2_, ...), custom_call_target="tpu_custom_call" | custom-call | tf_op jit(solution)/shard_map/placement/pallas_call | solution.py:431
  (42 shorter events, 1.8 us)
Async XLA Ops:
  0.0 17.5 %copy-start.6 = (s32[192]{0:T(256)S(1)}, s32[192]{0:T(256)}, u32[]{:S(2)}) copy-start(s32[192]{0:T(256)} %param.9) | copy-start | bytes 2308
  0.1 1.1 %copy-start.1 = (bf16[320,3,320]{2,0,1:T(8,128)(2,1)S(1)}, bf16[320,3,320]{2,0,1:T(8,128)(2,1)}, u32[]{:S(2)}) copy-start(bf16[320,3,320]{2,0,1:T(8,128)(2,1)} %param.11) | copy-start | bytes 1843204
  1.2 20.4 %copy-start.5 = (s32[768]{0:T(1024)S(1)}, s32[768]{0:T(1024)}, u32[]{:S(2)}) copy-start(s32[768]{0:T(1024)} %param.8) | copy-start | bytes 9220
  1.9 8.9 %collective-permute-start.2 = (bf16[3,816,128]{2,1,0:T(8,128)(2,1)S(1)}, bf16[3,816,128]{2,1,0:T(8,128)(2,1)S(1)}, u32[]{:S(2)}, u32[]{:S(2)}) collective-permute-start(bf16[3,816,128]{2,1,0:T(8,128)(2,1)S(1)} %get-tuple-element.44.refs_0_), channel_id=1, source_target_pairs={{0,4},{4,0},{8,12},{12,8},{1,5},{5,1},{9,13},{13,9},{2,6},{6,2},{1... | collective-permute-start | bytes 1880072 | tf_op jit(solution)/shard_map/ppermute | solution.py:26
  2.4 8.4 %collective-permute-start.1 = (bf16[816,128]{1,0:T(8,128)(2,1)S(1)}, bf16[816,128]{1,0:T(8,128)(2,1)S(1)}, u32[]{:S(2)}, u32[]{:S(2)}) collective-permute-start(bf16[816,128]{1,0:T(8,128)(2,1)S(1)} %get-tuple-element.43), channel_id=1, source_target_pairs={{0,8},{4,12},{8,0},{12,4},{1,9},{5,13},{9,1},{13,5},{2,10},{6,14},... | collective-permute-start | bytes 626696 | tf_op jit(solution)/shard_map/ppermute | solution.py:26
  5.0 0.9 %copy-start.2 = (bf16[320,320]{1,0:T(8,128)(2,1)S(1)}, bf16[320,320]{1,0:T(8,128)(2,1)}, u32[]{:S(2)}) copy-start(bf16[320,320]{1,0:T(8,128)(2,1)} %proj_ref.1) | copy-start | bytes 614404
  6.0 11.5 %collective-permute-start = (bf16[800,128]{1,0:T(8,128)(2,1)S(1)}, bf16[800,128]{1,0:T(8,128)(2,1)S(1)}, u32[]{:S(2)}, u32[]{:S(2)}) collective-permute-start(bf16[800,128]{1,0:T(8,128)(2,1)S(1)} %get-tuple-element.42.own_ref), channel_id=1, source_target_pairs={{0,1},{1,0},{2,3},{3,2},{4,5},{5,4},{6,7},{7,6},{8,9},{9,8},{10,11... | collective-permute-start | bytes 614408 | tf_op jit(solution)/shard_map/ppermute | solution.py:26
  7.7 12.7 %collective-permute-start.9 = (bf16[848,128]{1,0:T(8,128)(2,1)S(1)}, bf16[848,128]{1,0:T(8,128)(2,1)S(1)}, u32[]{:S(2)}, u32[]{:S(2)}) collective-permute-start(bf16[848,128]{1,0:T(8,128)(2,1)S(1)} %get-tuple-element.60), channel_id=1, source_target_pairs={{0,2},{1,3},{2,0},{3,1},{16,19},{17,18},{18,17},{19,16},{4,6},{5,7... | collective-permute-start | bytes 651272 | tf_op jit(solution)/shard_map/ppermute | solution.py:343
  10.3 7.7 %collective-permute-start.5 = (bf16[816,128]{1,0:T(8,128)(2,1)S(1)}, bf16[816,128]{1,0:T(8,128)(2,1)S(1)}, u32[]{:S(2)}, u32[]{:S(2)}) collective-permute-start(bf16[816,128]{1,0:T(8,128)(2,1)S(1)} %get-tuple-element.49), channel_id=1, source_target_pairs={{0,8},{4,12},{8,0},{12,4},{1,9},{5,13},{9,1},{13,5},{2,10},{6,14},... | collective-permute-start | bytes 626696 | tf_op jit(solution)/shard_map/ppermute | solution.py:26
  10.8 7.2 %collective-permute-start.4 = (bf16[816,128]{1,0:T(8,128)(2,1)S(1)}, bf16[816,128]{1,0:T(8,128)(2,1)S(1)}, u32[]{:S(2)}, u32[]{:S(2)}) collective-permute-start(bf16[816,128]{1,0:T(8,128)(2,1)S(1)} %collective-permute-done.1.refs_2_), channel_id=1, source_target_pairs={{0,16},{16,0},{1,17},{17,1},{2,18},{18,2},{3,19},{19,3},{4,20},{20... | collective-permute-start | bytes 626696 | tf_op jit(solution)/shard_map/ppermute | solution.py:26
  12.5 5.5 %collective-permute-start.6 = (bf16[816,128]{1,0:T(8,128)(2,1)S(1)}, bf16[816,128]{1,0:T(8,128)(2,1)S(1)}, u32[]{:S(2)}, u32[]{:S(2)}) collective-permute-start(bf16[816,128]{1,0:T(8,128)(2,1)S(1)} %collective-permute-done.1.refs_2_), channel_id=1, source_target_pairs={{0,4},{4,0},{8,12},{12,8},{1,5},{5,1},{9,13},{13,9},{2,6},{6,2},{1... | collective-permute-start | bytes 626696 | tf_op jit(solution)/shard_map/ppermute | solution.py:26
  12.5 1.5 %copy-start = (bf16[768,1280]{1,0:T(8,128)(2,1)S(1)}, bf16[768,1280]{1,0:T(8,128)(2,1)}, u32[]{:S(2)}) copy-start(bf16[768,1280]{1,0:T(8,128)(2,1)} %patches_ref) | copy-start | bytes 5898244
  14.0 0.7 %copy-start.3 = (f32[1280]{0:T(1024)S(1)}, f32[1280]{0:T(1024)}, u32[]{:S(2)}) copy-start(f32[1280]{0:T(1024)} %gain_ref.1) | copy-start | bytes 15364
  17.6 10.9 %collective-permute-start.11 = (bf16[2,816,128]{2,1,0:T(8,128)(2,1)S(1)}, bf16[2,816,128]{2,1,0:T(8,128)(2,1)S(1)}, u32[]{:S(2)}, u32[]{:S(2)}) collective-permute-start(bf16[2,816,128]{2,1,0:T(8,128)(2,1)S(1)} %near.1.refs_4_.refs_0_), channel_id=1, source_target_pairs={{0,8},{4,12},{8,0},{12,4},{1,9},{5,13},{9,1},{13,5},{2,10},{6,14},... | collective-permute-start | bytes 1253384 | tf_op jit(solution)/shard_map/ppermute | solution.py:26
  18.0 3.6 %collective-permute-start.7 = (bf16[816,128]{1,0:T(8,128)(2,1)S(1)}, bf16[816,128]{1,0:T(8,128)(2,1)S(1)}, u32[]{:S(2)}, u32[]{:S(2)}) collective-permute-start(bf16[816,128]{1,0:T(8,128)(2,1)S(1)} %collective-permute-done.4.refs_3_), channel_id=1, source_target_pairs={{0,4},{4,0},{8,12},{12,8},{1,5},{5,1},{9,13},{13,9},{2,6},{6,2},{1... | collective-permute-start | bytes 626696 | tf_op jit(solution)/shard_map/ppermute | solution.py:26
  18.3 3.4 %collective-permute-start.8 = (bf16[816,128]{1,0:T(8,128)(2,1)S(1)}, bf16[816,128]{1,0:T(8,128)(2,1)S(1)}, u32[]{:S(2)}, u32[]{:S(2)}) collective-permute-start(bf16[816,128]{1,0:T(8,128)(2,1)S(1)} %collective-permute-done.5.refs_4_), channel_id=1, source_target_pairs={{0,4},{4,0},{8,12},{12,8},{1,5},{5,1},{9,13},{13,9},{2,6},{6,2},{1... | collective-permute-start | bytes 626696 | tf_op jit(solution)/shard_map/ppermute | solution.py:26
  20.4 7.5 %collective-permute-start.10 = (bf16[800,128]{1,0:T(8,128)(2,1)S(1)}, bf16[800,128]{1,0:T(8,128)(2,1)S(1)}, u32[]{:S(2)}, u32[]{:S(2)}) collective-permute-start(bf16[800,128]{1,0:T(8,128)(2,1)S(1)} %slice.3), channel_id=1, source_target_pairs={{0,16},{16,0},{1,17},{17,1},{2,18},{18,2},{3,19},{19,3},{4,20},{20... | collective-permute-start | bytes 614408 | tf_op jit(solution)/shard_map/ppermute | solution.py:26
  21.6 24.8 %copy-start.4 = (f32[1280]{0:T(1024)S(1)}, f32[1280]{0:T(1024)}, u32[]{:S(2)}) copy-start(f32[1280]{0:T(1024)} %refs_13_.1) | copy-start | bytes 15364
  28.5 15.5 %collective-permute-start.16 = (bf16[2,800,128]{2,1,0:T(8,128)(2,1)S(1)}, bf16[2,800,128]{2,1,0:T(8,128)(2,1)S(1)}, u32[]{:S(2)}, u32[]{:S(2)}) collective-permute-start(bf16[2,800,128]{2,1,0:T(8,128)(2,1)S(1)} %pad_maximum_fusion.refs_5_), channel_id=1, source_target_pairs={{0,8},{4,12},{8,0},{12,4},{1,9},{5,13},{9,1},{13,5},{2,10},{6,14},... | collective-permute-start | bytes 1228808 | tf_op jit(solution)/shard_map/ppermute | solution.py:26
  30.1 6.2 %collective-permute-start.13 = (bf16[480,128]{1,0:T(8,128)(2,1)S(1)}, bf16[480,128]{1,0:T(8,128)(2,1)S(1)}, u32[]{:S(2)}, u32[]{:S(2)}) collective-permute-start(bf16[480,128]{1,0:T(8,128)(2,1)S(1)} %get-tuple-element.64), channel_id=1, source_target_pairs={{0,1},{1,0},{2,3},{3,2},{4,5},{5,4},{6,7},{7,6},{8,9},{9,8},{10,11... | collective-permute-start | bytes 368648 | tf_op jit(solution)/shard_map/ppermute | solution.py:26
  32.1 11.9 %collective-permute-start.14 = (bf16[480,128]{1,0:T(8,128)(2,1)S(1)}, bf16[480,128]{1,0:T(8,128)(2,1)S(1)}, u32[]{:S(2)}, u32[]{:S(2)}) collective-permute-start(bf16[480,128]{1,0:T(8,128)(2,1)S(1)} %get-tuple-element.65), channel_id=1, source_target_pairs={{0,2},{1,3},{2,0},{3,1},{4,6},{5,7},{6,4},{7,5},{8,10},{9,11},{10,... | collective-permute-start | bytes 368648 | tf_op jit(solution)/shard_map/ppermute | solution.py:26
  34.7 9.3 %collective-permute-start.15 = (bf16[480,128]{1,0:T(8,128)(2,1)S(1)}, bf16[480,128]{1,0:T(8,128)(2,1)S(1)}, u32[]{:S(2)}, u32[]{:S(2)}) collective-permute-start(bf16[480,128]{1,0:T(8,128)(2,1)S(1)} %get-tuple-element.66), channel_id=1, source_target_pairs={{0,3},{1,2},{2,1},{3,0},{4,7},{5,6},{6,5},{7,4},{8,11},{9,10},{10,... | collective-permute-start | bytes 368648 | tf_op jit(solution)/shard_map/ppermute | solution.py:26
  34.7 9.8 %collective-permute-start.3 = (bf16[2,816,128]{2,1,0:T(8,128)(2,1)S(1)}, bf16[2,816,128]{2,1,0:T(8,128)(2,1)S(1)}, u32[]{:S(2)}, u32[]{:S(2)}) collective-permute-start(bf16[2,816,128]{2,1,0:T(8,128)(2,1)S(1)} %near.1.refs_4_.refs_0_), channel_id=1, source_target_pairs={{0,4},{4,0},{8,12},{12,8},{1,5},{5,1},{9,13},{13,9},{2,6},{6,2},{1... | collective-permute-start | bytes 1253384 | tf_op jit(solution)/shard_map/ppermute | solution.py:26
  36.3 9.5 %collective-permute-start.12 = (bf16[2,816,128]{2,1,0:T(8,128)(2,1)S(1)}, bf16[2,816,128]{2,1,0:T(8,128)(2,1)S(1)}, u32[]{:S(2)}, u32[]{:S(2)}) collective-permute-start(bf16[2,816,128]{2,1,0:T(8,128)(2,1)S(1)} %collective-permute-done.11.refs_8_.refs_2_), channel_id=1, source_target_pairs={{0,4},{4,0},{8,12},{12,8},{1,5},{5,1},{9,13},{13,9},{2,6},{6,2},{1... | collective-permute-start | bytes 1253384 | tf_op jit(solution)/shard_map/ppermute | solution.py:26
  44.1 1.7 %collective-permute-start.17 = (bf16[2,800,128]{2,1,0:T(8,128)(2,1)S(1)}, bf16[2,800,128]{2,1,0:T(8,128)(2,1)S(1)}, u32[]{:S(2)}, u32[]{:S(2)}) collective-permute-start(bf16[2,800,128]{2,1,0:T(8,128)(2,1)S(1)} %pad_maximum_fusion.refs_5_), channel_id=1, source_target_pairs={{0,4},{4,0},{8,12},{12,8},{1,5},{5,1},{9,13},{13,9},{2,6},{6,2},{1... | collective-permute-start | bytes 1228808 | tf_op jit(solution)/shard_map/ppermute | solution.py:26
  44.1 2.3 %collective-permute-start.18 = (bf16[2,800,128]{2,1,0:T(8,128)(2,1)S(1)}, bf16[2,800,128]{2,1,0:T(8,128)(2,1)S(1)}, u32[]{:S(2)}, u32[]{:S(2)}) collective-permute-start(bf16[2,800,128]{2,1,0:T(8,128)(2,1)S(1)} %collective-permute-done.16.refs_9_), channel_id=1, source_target_pairs={{0,4},{4,0},{8,12},{12,8},{1,5},{5,1},{9,13},{13,9},{2,6},{6,2},{1... | collective-permute-start | bytes 1228808 | tf_op jit(solution)/shard_map/ppermute | solution.py:26
  48.3 8.9 %collective-permute-start.21 = (bf16[96,1280]{1,0:T(8,128)(2,1)S(1)}, bf16[96,1280]{1,0:T(8,128)(2,1)S(1)}, u32[]{:S(2)}, u32[]{:S(2)}) collective-permute-start(bf16[96,1280]{1,0:T(8,128)(2,1)S(1)} %get-tuple-element.75.refs_4_), channel_id=1, source_target_pairs={{0,8},{4,12},{8,0},{12,4},{1,9},{5,13},{9,1},{13,5},{2,10},{6,14},... | collective-permute-start | bytes 737288 | tf_op jit(solution)/shard_map/ppermute | solution.py:26
  48.9 12.8 %collective-permute-start.22 = (bf16[96,1280]{1,0:T(8,128)(2,1)S(1)}, bf16[96,1280]{1,0:T(8,128)(2,1)S(1)}, u32[]{:S(2)}, u32[]{:S(2)}) collective-permute-start(bf16[96,1280]{1,0:T(8,128)(2,1)S(1)} %get-tuple-element.76.refs_5_), channel_id=1, source_target_pairs={{0,8},{4,12},{8,0},{12,4},{1,9},{5,13},{9,1},{13,5},{2,10},{6,14},... | collective-permute-start | bytes 737288 | tf_op jit(solution)/shard_map/ppermute | solution.py:26
  57.2 4.5 %collective-permute-start.23 = (bf16[96,1280]{1,0:T(8,128)(2,1)S(1)}, bf16[96,1280]{1,0:T(8,128)(2,1)S(1)}, u32[]{:S(2)}, u32[]{:S(2)}) collective-permute-start(bf16[96,1280]{1,0:T(8,128)(2,1)S(1)} %collective-permute-done.21.refs_8_), channel_id=1, source_target_pairs={{0,4},{4,0},{8,12},{12,8},{1,5},{5,1},{9,13},{13,9},{2,6},{6,2},{1... | collective-permute-start | bytes 737288 | tf_op jit(solution)/shard_map/ppermute | solution.py:26
  57.2 4.5 %collective-permute-start.19 = (bf16[96,1280]{1,0:T(8,128)(2,1)S(1)}, bf16[96,1280]{1,0:T(8,128)(2,1)S(1)}, u32[]{:S(2)}, u32[]{:S(2)}) collective-permute-start(bf16[96,1280]{1,0:T(8,128)(2,1)S(1)} %get-tuple-element.75.refs_4_), channel_id=1, source_target_pairs={{0,4},{4,0},{8,12},{12,8},{1,5},{5,1},{9,13},{13,9},{2,6},{6,2},{1... | collective-permute-start | bytes 737288 | tf_op jit(solution)/shard_map/ppermute | solution.py:26
  57.7 4.0 %collective-permute-start.20 = (bf16[96,1280]{1,0:T(8,128)(2,1)S(1)}, bf16[96,1280]{1,0:T(8,128)(2,1)S(1)}, u32[]{:S(2)}, u32[]{:S(2)}) collective-permute-start(bf16[96,1280]{1,0:T(8,128)(2,1)S(1)} %get-tuple-element.76.refs_5_), channel_id=1, source_target_pairs={{0,4},{4,0},{8,12},{12,8},{1,5},{5,1},{9,13},{13,9},{2,6},{6,2},{1... | collective-permute-start | bytes 737288 | tf_op jit(solution)/shard_map/ppermute | solution.py:26
  61.7 1.5 %collective-permute-start.24 = (bf16[96,1280]{1,0:T(8,128)(2,1)S(1)}, bf16[96,1280]{1,0:T(8,128)(2,1)S(1)}, u32[]{:S(2)}, u32[]{:S(2)}) collective-permute-start(bf16[96,1280]{1,0:T(8,128)(2,1)S(1)} %collective-permute-done.22.refs_9_), channel_id=1, source_target_pairs={{0,4},{4,0},{8,12},{12,8},{1,5},{5,1},{9,13},{13,9},{2,6},{6,2},{1... | collective-permute-start | bytes 737288 | tf_op jit(solution)/shard_map/ppermute | solution.py:26

commit v20 on v19

--- a/solution.py
+++ b/solution.py
@@ -397,7 +397,9 @@
         name="attention",
     )(index, hidden, valid.reshape(rows // PAIR, PAIR), *shard_list)
 
-    mixed, far, far2, low = together(list(mixed), far, far2, low)
+    mixed, far, far2 = together(list(mixed), far, far2)
+    for k in cross:
+        low[k] = together(low[k], mixed[0])[0]
     received = [mixed[0]] + [swap(mixed[s], "tensor", n_ten, s) for s in range(1, n_ten)]
     high = gather_cross(jnp.stack([far, far2]), n_ctx)
     far_pair = jnp.stack([far, far2])

time: 65.2 us -> 67.3 us (1.032)
  waiting for transfers between devices: 27 us -> 30.3 us
  starting transfers between devices: 21 us -> 19.8 us
    ppermute x24, waiting for transfers between devices: 25.1 us -> 30.3 us  [swap(): return lax.ppermute(x, axis, [(i, i ^ bit) for i in range(size)])]
    ppermute x1, waiting for transfers between devices: 1.85 us -> 0.01 us  [local(): lax.ppermute(far, ('dp', 'tensor'), [(d * n_ten + t, d * n_ten + (t ^ 2 +...]
    ppermute x24, starting transfers between devices: 18.4 us -> 17.1 us  [swap(): return lax.ppermute(x, axis, [(i, i ^ bit) for i in range(size)])]
  transfers between devices with their start and end apart: 25 -> 25, of which waited for: 10 -> 11; matrix products, arithmetic and copies ran while one was open for 0% -> 0% of each run, Pallas kernels for 12% -> 12%
where the time goes in v20:
time: 67.3 us; the launch traced here: 67.1 us
  waiting for transfers between devices  30.3 us (45%)
  starting transfers between devices  19.8 us (29%)
  Pallas kernels  12.5 us (19%)
  local copies, waits for them, and re-layouts  4.33 us (6%)
    ppermute x24, waiting for transfers between devices, swap(): return lax.ppermute(x, axis, [(i, i ^ bit) for i in range(size)])  30.3 us
    ppermute x24, starting transfers between devices, swap(): return lax.ppermute(x, axis, [(i, i ^ bit) for i in range(size)])  17.1 us
    pallas_call x1, Pallas kernels, local(): pl.pallas_call(functools.partial(attention_kernel, n_ctx, width), out_sha...  6.32 us
    unnamed x14, local copies, waits for them, and re-layouts  4.31 us
    ppermute x1, starting transfers between devices, local(): lax.ppermute(far, ('dp', 'tensor'), [(d * n_ten + t, d * n_ten + (t ^ 2 +...  2.65 us
    pallas_call x1, Pallas kernels, local(): pl.pallas_call(functools.partial(project_kernel, n_ctx, width, col), out_...  1.93 us
    pallas_call x1, Pallas kernels, local(): pl.pallas_call(functools.partial(place_kernel, n_ctx), out_shape=shape(gr...  1.84 us
    pallas_call x1, Pallas kernels, local(): pl.pallas_call(norm_kernel, out_shape=(shape(rows, feat), shape(groups, f...  1.56 us
  transfers between devices with their start and end apart: 25, of which 11 were waited for; matrix products, arithmetic and copies ran while one was open for 0% of the time, Pallas kernels for 12%

profile of v20, /device:TPU:0, one launch (start us, length us, event | category | flops | bytes accessed | tf_op | source)
XLA Modules:
  0.0 67.1 jit_solution(5187394809364371420)
XLA Ops:
  0.1 1.1 %copy-done.1 = bf16[320,3,320]{2,0,1:T(8,128)(2,1)S(1)} copy-done((bf16[320,3,320]{2,0,1:T(8,128)(2,1)S(1)}, bf16[320,3,320]{2,0,1:T(8,128)(2,1)}, u32[]{:S(2)}) %copy-start.1) | copy-done | bytes 614424
  1.2 0.7 %pack.1 = (bf16[816,128]{1,0:T(8,128)(2,1)S(1)}, bf16[816,128]{1,0:T(8,128)(2,1)S(1)}, bf16[3,816,128]{2,1,0:T(8,128)(2,1)S(1)}) custom-call(s32[3]{0:T(128)S(1)} %pad_add_fusion.index_ref, bf16[3,320,320]{2,1,0:T(8,128)(2,1)S(1)} %bitcast.8), custom_call_target="tpu_custom_call" | custom-call | tf_op jit(solution)/shard_map/pack/pallas_call | solution.py:324
  1.9 0.5 collective-permute-start.2
  2.4 2.6 %collective-permute-start.1 = (bf16[816,128]{1,0:T(8,128)(2,1)S(1)}, bf16[816,128]{1,0:T(8,128)(2,1)S(1)}, u32[]{:S(2)}, u32[]{:S(2)}) collective-permute-start(bf16[816,128]{1,0:T(8,128)(2,1)S(1)} %get-tuple-element.43), channel_id=1, source_target_pairs={{0,8},{4,12},{8,0},{12,4},{1,9},{5,13},{9,1},{13,5},{2,10},{6,14},... | collective-permute-start | bytes 626696 | tf_op jit(solution)/shard_map/ppermute | solution.py:26
  5.0 0.9 %copy-done.2 = bf16[320,320]{1,0:T(8,128)(2,1)S(1)} copy-done((bf16[320,320]{1,0:T(8,128)(2,1)S(1)}, bf16[320,320]{1,0:T(8,128)(2,1)}, u32[]{:S(2)}) %copy-start.2) | copy-done | bytes 204824
  6.0 2.7 %collective-permute-start.10 = (bf16[848,128]{1,0:T(8,128)(2,1)S(1)}, bf16[848,128]{1,0:T(8,128)(2,1)S(1)}, u32[]{:S(2)}, u32[]{:S(2)}) collective-permute-start(bf16[848,128]{1,0:T(8,128)(2,1)S(1)} %get-tuple-element.60), channel_id=1, source_target_pairs={{0,2},{1,3},{2,0},{3,1},{16,19},{17,18},{18,17},{19,16},{4,6},{5,7... | collective-permute-start | bytes 651272 | tf_op jit(solution)/shard_map/ppermute | solution.py:343
  8.7 0.5 collective-permute-start.6
  9.2 1.6 %collective-permute-done.1.refs_2_ = bf16[816,128]{1,0:T(8,128)(2,1)S(1)} collective-permute-done((bf16[816,128]{1,0:T(8,128)(2,1)S(1)}, bf16[816,128]{1,0:T(8,128)(2,1)S(1)}, u32[]{:S(2)}, u32[]{:S(2)}) %collective-permute-start.1) | collective-permute-done | bytes 208928 | tf_op jit(solution)/shard_map/ppermute | solution.py:26
  10.8 1.7 %collective-permute-start.5 = (bf16[816,128]{1,0:T(8,128)(2,1)S(1)}, bf16[816,128]{1,0:T(8,128)(2,1)S(1)}, u32[]{:S(2)}, u32[]{:S(2)}) collective-permute-start(bf16[816,128]{1,0:T(8,128)(2,1)S(1)} %collective-permute-done.1.refs_2_), channel_id=1, source_target_pairs={{0,16},{16,0},{1,17},{17,1},{2,18},{18,2},{3,19},{19,3},{4,20},{20... | collective-permute-start | bytes 626696 | tf_op jit(solution)/shard_map/ppermute | solution.py:26
  12.5 2.0 %collective-permute-start = (bf16[800,128]{1,0:T(8,128)(2,1)S(1)}, bf16[800,128]{1,0:T(8,128)(2,1)S(1)}, u32[]{:S(2)}, u32[]{:S(2)}) collective-permute-start(bf16[800,128]{1,0:T(8,128)(2,1)S(1)} %get-tuple-element.42.own_ref), channel_id=1, source_target_pairs={{0,1},{1,0},{2,3},{3,2},{4,5},{5,4},{6,7},{7,6},{8,9},{9,8},{10,11... | collective-permute-start | bytes 614408 | tf_op jit(solution)/shard_map/ppermute | solution.py:26
  14.5 1.5 %copy-done = bf16[768,1280]{1,0:T(8,128)(2,1)S(1)} copy-done((bf16[768,1280]{1,0:T(8,128)(2,1)S(1)}, bf16[768,1280]{1,0:T(8,128)(2,1)}, u32[]{:S(2)}) %copy-start) | copy-done | bytes 1966104
  16.1 0.7 %copy-done.3 = f32[1280]{0:T(1024)S(1)} copy-done((f32[1280]{0:T(1024)S(1)}, f32[1280]{0:T(1024)}, u32[]{:S(2)}) %copy-start.3) | copy-done | bytes 5144
  16.8 1.6 %norm.1 = (bf16[768,1280]{1,0:T(8,128)(2,1)S(1)}, bf16[192,1280]{1,0:T(8,128)(2,1)S(1)}) custom-call(s32[3]{0:T(128)S(1)} %pad_add_fusion.index_ref, bf16[768,1280]{1,0:T(8,128)(2,1)S(1)} %copy-done, f32[1280]{0:T(1024)S(1)} %copy-done.3), custom_call_target="tpu_custom_call" | custom-call | tf_op jit(solution)/shard_map/norm/pallas_call | solution.py:357
  18.3 5.1 %collective-permute-done.next_ref = bf16[800,128]{1,0:T(8,128)(2,1)S(1)} collective-permute-done((bf16[800,128]{1,0:T(8,128)(2,1)S(1)}, bf16[800,128]{1,0:T(8,128)(2,1)S(1)}, u32[]{:S(2)}, u32[]{:S(2)}) %collective-permute-start) | collective-permute-done | bytes 204832 | tf_op jit(solution)/shard_map/ppermute | solution.py:26
  23.6 0.4 collective-permute-start.9
  24.2 0.5 collective-permute-start.4
  25.3 6.3 %attention.1 = (bf16[480,128]{1,0:T(8,128)(2,1)S(1)}, bf16[480,128]{1,0:T(8,128)(2,1)S(1)}, bf16[480,128]{1,0:T(8,128)(2,1)S(1)}, bf16[480,128]{1,0:T(8,128)(2,1)S(1)}) custom-call(s32[3]{0:T(128)S(1)} %pad_add_fusion.index_ref, bf16[768,1280]{1,0:T(8,128)(2,1)S(1)} %get-tuple-element.51.hidden_ref, s32[6,128]{1,0:T(8,128)S(1)} %bitcast.9, ...), custom_call_target="tpu_custom_call" | custom-call | tf_op jit(solution)/shard_map/attention/pallas_call | solution.py:388
  31.7 1.1 %collective-permute-start.16 = (bf16[2,800,128]{2,1,0:T(8,128)(2,1)S(1)}, bf16[2,800,128]{2,1,0:T(8,128)(2,1)S(1)}, u32[]{:S(2)}, u32[]{:S(2)}) collective-permute-start(bf16[2,800,128]{2,1,0:T(8,128)(2,1)S(1)} %pad_maximum_fusion.refs_5_), channel_id=1, source_target_pairs={{0,8},{4,12},{8,0},{12,4},{1,9},{5,13},{9,1},{13,5},{2,10},{6,14},... | collective-permute-start | bytes 1228808 | tf_op jit(solution)/shard_map/ppermute | solution.py:26
  32.8 4.0 %collective-permute-start.14 = (bf16[480,128]{1,0:T(8,128)(2,1)S(1)}, bf16[480,128]{1,0:T(8,128)(2,1)S(1)}, u32[]{:S(2)}, u32[]{:S(2)}) collective-permute-start(bf16[480,128]{1,0:T(8,128)(2,1)S(1)} %get-tuple-element.65), channel_id=1, source_target_pairs={{0,2},{1,3},{2,0},{3,1},{4,6},{5,7},{6,4},{7,5},{8,10},{9,11},{10,... | collective-permute-start | bytes 368648 | tf_op jit(solution)/shard_map/ppermute | solution.py:26
  37.1 2.0 %collective-permute-done.13.refs_1_ = bf16[480,128]{1,0:T(8,128)(2,1)S(1)} collective-permute-done((bf16[480,128]{1,0:T(8,128)(2,1)S(1)}, bf16[480,128]{1,0:T(8,128)(2,1)S(1)}, u32[]{:S(2)}, u32[]{:S(2)}) %collective-permute-start.13) | collective-permute-done | bytes 122912 | tf_op jit(solution)/shard_map/ppermute | solution.py:26
  39.1 7.0 %collective-permute-done.14.refs_2_ = bf16[480,128]{1,0:T(8,128)(2,1)S(1)} collective-permute-done((bf16[480,128]{1,0:T(8,128)(2,1)S(1)}, bf16[480,128]{1,0:T(8,128)(2,1)S(1)}, u32[]{:S(2)}, u32[]{:S(2)}) %collective-permute-start.14) | collective-permute-done | bytes 122912 | tf_op jit(solution)/shard_map/ppermute | solution.py:26
  46.2 0.5 collective-permute-start.18
  46.7 1.2 %collective-permute-done.17.refs_7_ = bf16[2,800,128]{2,1,0:T(8,128)(2,1)S(1)} collective-permute-done((bf16[2,800,128]{2,1,0:T(8,128)(2,1)S(1)}, bf16[2,800,128]{2,1,0:T(8,128)(2,1)S(1)}, u32[]{:S(2)}, u32[]{:S(2)}) %collective-permute-start.17) | collective-permute-done | bytes 409632 | tf_op jit(solution)/shard_map/ppermute | solution.py:26
  47.9 0.6 collective-permute-done.18.refs_11_
  48.5 1.9 %project.1 = (bf16[96,1280]{1,0:T(8,128)(2,1)S(1)}, bf16[96,1280]{1,0:T(8,128)(2,1)S(1)}) custom-call(s32[3]{0:T(128)S(1)} %pad_add_fusion.index_ref, bf16[480,128]{1,0:T(8,128)(2,1)S(1)} %get-tuple-element.69.refs_0_, bf16[480,128]{1,0:T(8,128)(2,1)S(1)} %collective-permute-done.13.refs_1_, bf16[480,128]{1,0:T(8,128)(2,1)S(1)} %collective-permute-done.14.refs_2_, ...), custom_call_target="tpu_custom_call" | custom-call | tf_op jit(solution)/shard_map/project/pallas_call | solution.py:411
  50.4 1.2 %collective-permute-start.21 = (bf16[96,1280]{1,0:T(8,128)(2,1)S(1)}, bf16[96,1280]{1,0:T(8,128)(2,1)S(1)}, u32[]{:S(2)}, u32[]{:S(2)}) collective-permute-start(bf16[96,1280]{1,0:T(8,128)(2,1)S(1)} %get-tuple-element.75.refs_4_), channel_id=1, source_target_pairs={{0,8},{4,12},{8,0},{12,4},{1,9},{5,13},{9,1},{13,5},{2,10},{6,14},... | collective-permute-start | bytes 737288 | tf_op jit(solution)/shard_map/ppermute | solution.py:26
  51.6 0.9 %collective-permute-start.22 = (bf16[96,1280]{1,0:T(8,128)(2,1)S(1)}, bf16[96,1280]{1,0:T(8,128)(2,1)S(1)}, u32[]{:S(2)}, u32[]{:S(2)}) collective-permute-start(bf16[96,1280]{1,0:T(8,128)(2,1)S(1)} %get-tuple-element.76.refs_5_), channel_id=1, source_target_pairs={{0,8},{4,12},{8,0},{12,4},{1,9},{5,13},{9,1},{13,5},{2,10},{6,14},... | collective-permute-start | bytes 737288 | tf_op jit(solution)/shard_map/ppermute | solution.py:26
  52.5 6.8 %collective-permute-done.21.refs_8_ = bf16[96,1280]{1,0:T(8,128)(2,1)S(1)} collective-permute-done((bf16[96,1280]{1,0:T(8,128)(2,1)S(1)}, bf16[96,1280]{1,0:T(8,128)(2,1)S(1)}, u32[]{:S(2)}, u32[]{:S(2)}) %collective-permute-start.21) | collective-permute-done | bytes 245792 | tf_op jit(solution)/shard_map/ppermute | solution.py:26
  59.3 0.5 collective-permute-start.19
  59.8 3.9 %collective-permute-done.22.refs_9_ = bf16[96,1280]{1,0:T(8,128)(2,1)S(1)} collective-permute-done((bf16[96,1280]{1,0:T(8,128)(2,1)S(1)}, bf16[96,1280]{1,0:T(8,128)(2,1)S(1)}, u32[]{:S(2)}, u32[]{:S(2)}) %collective-permute-start.22) | collective-permute-done | bytes 245792 | tf_op jit(solution)/shard_map/ppermute | solution.py:26
  63.8 1.5 %collective-permute-done.24.refs_11_ = bf16[96,1280]{1,0:T(8,128)(2,1)S(1)} collective-permute-done((bf16[96,1280]{1,0:T(8,128)(2,1)S(1)}, bf16[96,1280]{1,0:T(8,128)(2,1)S(1)}, u32[]{:S(2)}, u32[]{:S(2)}) %collective-permute-start.24) | collective-permute-done | bytes 245792 | tf_op jit(solution)/shard_map/ppermute | solution.py:26
  65.3 1.8 %placement.1 = bf16[192,1280]{1,0:T(8,128)(2,1)} custom-call(s32[3]{0:T(128)S(1)} %pad_add_fusion.index_ref, bf16[2,816,128]{2,1,0:T(8,128)(2,1)S(1)} %near.1.refs_4_.refs_0_, bf16[2,816,128]{2,1,0:T(8,128)(2,1)S(1)} %collective-permute-done.3.refs_6_.refs_1_, bf16[2,816,128]{2,1,0:T(8,128)(2,1)S(1)} %collective-permute-done.4.refs_8_.refs_2_, ...), custom_call_target="tpu_custom_call" | custom-call | tf_op jit(solution)/shard_map/placement/pallas_call | solution.py:433
  (42 shorter events, 1.5 us)
Async XLA Ops:
  0.0 24.1 %copy-start.6 = (s32[192]{0:T(256)S(1)}, s32[192]{0:T(256)}, u32[]{:S(2)}) copy-start(s32[192]{0:T(256)} %param.9) | copy-start | bytes 2308
  0.1 1.1 %copy-start.1 = (bf16[320,3,320]{2,0,1:T(8,128)(2,1)S(1)}, bf16[320,3,320]{2,0,1:T(8,128)(2,1)}, u32[]{:S(2)}) copy-start(bf16[320,3,320]{2,0,1:T(8,128)(2,1)} %param.11) | copy-start | bytes 1843204
  1.2 24.1 %copy-start.5 = (s32[768]{0:T(1024)S(1)}, s32[768]{0:T(1024)}, u32[]{:S(2)}) copy-start(s32[768]{0:T(1024)} %param.8) | copy-start | bytes 9220
  1.9 8.9 %collective-permute-start.2 = (bf16[3,816,128]{2,1,0:T(8,128)(2,1)S(1)}, bf16[3,816,128]{2,1,0:T(8,128)(2,1)S(1)}, u32[]{:S(2)}, u32[]{:S(2)}) collective-permute-start(bf16[3,816,128]{2,1,0:T(8,128)(2,1)S(1)} %get-tuple-element.44.refs_0_), channel_id=1, source_target_pairs={{0,4},{4,0},{8,12},{12,8},{1,5},{5,1},{9,13},{13,9},{2,6},{6,2},{1... | collective-permute-start | bytes 1880072 | tf_op jit(solution)/shard_map/ppermute | solution.py:26
  2.4 8.4 %collective-permute-start.1 = (bf16[816,128]{1,0:T(8,128)(2,1)S(1)}, bf16[816,128]{1,0:T(8,128)(2,1)S(1)}, u32[]{:S(2)}, u32[]{:S(2)}) collective-permute-start(bf16[816,128]{1,0:T(8,128)(2,1)S(1)} %get-tuple-element.43), channel_id=1, source_target_pairs={{0,8},{4,12},{8,0},{12,4},{1,9},{5,13},{9,1},{13,5},{2,10},{6,14},... | collective-permute-start | bytes 626696 | tf_op jit(solution)/shard_map/ppermute | solution.py:26
  5.0 0.9 %copy-start.2 = (bf16[320,320]{1,0:T(8,128)(2,1)S(1)}, bf16[320,320]{1,0:T(8,128)(2,1)}, u32[]{:S(2)}) copy-start(bf16[320,320]{1,0:T(8,128)(2,1)} %proj_ref.1) | copy-start | bytes 614404
  6.0 18.0 %collective-permute-start.10 = (bf16[848,128]{1,0:T(8,128)(2,1)S(1)}, bf16[848,128]{1,0:T(8,128)(2,1)S(1)}, u32[]{:S(2)}, u32[]{:S(2)}) collective-permute-start(bf16[848,128]{1,0:T(8,128)(2,1)S(1)} %get-tuple-element.60), channel_id=1, source_target_pairs={{0,2},{1,3},{2,0},{3,1},{16,19},{17,18},{18,17},{19,16},{4,6},{5,7... | collective-permute-start | bytes 651272 | tf_op jit(solution)/shard_map/ppermute | solution.py:343
  8.7 14.8 %collective-permute-start.6 = (bf16[816,128]{1,0:T(8,128)(2,1)S(1)}, bf16[816,128]{1,0:T(8,128)(2,1)S(1)}, u32[]{:S(2)}, u32[]{:S(2)}) collective-permute-start(bf16[816,128]{1,0:T(8,128)(2,1)S(1)} %get-tuple-element.49), channel_id=1, source_target_pairs={{0,8},{4,12},{8,0},{12,4},{1,9},{5,13},{9,1},{13,5},{2,10},{6,14},... | collective-permute-start | bytes 626696 | tf_op jit(solution)/shard_map/ppermute | solution.py:26
  10.8 12.7 %collective-permute-start.5 = (bf16[816,128]{1,0:T(8,128)(2,1)S(1)}, bf16[816,128]{1,0:T(8,128)(2,1)S(1)}, u32[]{:S(2)}, u32[]{:S(2)}) collective-permute-start(bf16[816,128]{1,0:T(8,128)(2,1)S(1)} %collective-permute-done.1.refs_2_), channel_id=1, source_target_pairs={{0,16},{16,0},{1,17},{17,1},{2,18},{18,2},{3,19},{19,3},{4,20},{20... | collective-permute-start | bytes 626696 | tf_op jit(solution)/shard_map/ppermute | solution.py:26
  12.5 11.0 %collective-permute-start.7 = (bf16[816,128]{1,0:T(8,128)(2,1)S(1)}, bf16[816,128]{1,0:T(8,128)(2,1)S(1)}, u32[]{:S(2)}, u32[]{:S(2)}) collective-permute-start(bf16[816,128]{1,0:T(8,128)(2,1)S(1)} %collective-permute-done.1.refs_2_), channel_id=1, source_target_pairs={{0,4},{4,0},{8,12},{12,8},{1,5},{5,1},{9,13},{13,9},{2,6},{6,2},{1... | collective-permute-start | bytes 626696 | tf_op jit(solution)/shard_map/ppermute | solution.py:26
  12.5 11.0 %collective-permute-start = (bf16[800,128]{1,0:T(8,128)(2,1)S(1)}, bf16[800,128]{1,0:T(8,128)(2,1)S(1)}, u32[]{:S(2)}, u32[]{:S(2)}) collective-permute-start(bf16[800,128]{1,0:T(8,128)(2,1)S(1)} %get-tuple-element.42.own_ref), channel_id=1, source_target_pairs={{0,1},{1,0},{2,3},{3,2},{4,5},{5,4},{6,7},{7,6},{8,9},{9,8},{10,11... | collective-permute-start | bytes 614408 | tf_op jit(solution)/shard_map/ppermute | solution.py:26
  14.5 1.5 %copy-start = (bf16[768,1280]{1,0:T(8,128)(2,1)S(1)}, bf16[768,1280]{1,0:T(8,128)(2,1)}, u32[]{:S(2)}) copy-start(bf16[768,1280]{1,0:T(8,128)(2,1)} %patches_ref) | copy-start | bytes 5898244
  16.1 0.7 %copy-start.3 = (f32[1280]{0:T(1024)S(1)}, f32[1280]{0:T(1024)}, u32[]{:S(2)}) copy-start(f32[1280]{0:T(1024)} %gain_ref.1) | copy-start | bytes 15364
  23.5 1.5 %collective-permute-start.8 = (bf16[816,128]{1,0:T(8,128)(2,1)S(1)}, bf16[816,128]{1,0:T(8,128)(2,1)S(1)}, u32[]{:S(2)}, u32[]{:S(2)}) collective-permute-start(bf16[816,128]{1,0:T(8,128)(2,1)S(1)} %collective-permute-done.5.refs_3_), channel_id=1, source_target_pairs={{0,4},{4,0},{8,12},{12,8},{1,5},{5,1},{9,13},{13,9},{2,6},{6,2},{1... | collective-permute-start | bytes 626696 | tf_op jit(solution)/shard_map/ppermute | solution.py:26
  23.6 1.7 %collective-permute-start.9 = (bf16[816,128]{1,0:T(8,128)(2,1)S(1)}, bf16[816,128]{1,0:T(8,128)(2,1)S(1)}, u32[]{:S(2)}, u32[]{:S(2)}) collective-permute-start(bf16[816,128]{1,0:T(8,128)(2,1)S(1)} %collective-permute-done.6.refs_4_), channel_id=1, source_target_pairs={{0,4},{4,0},{8,12},{12,8},{1,5},{5,1},{9,13},{13,9},{2,6},{6,2},{1... | collective-permute-start | bytes 626696 | tf_op jit(solution)/shard_map/ppermute | solution.py:26
  24.1 7.6 %collective-permute-start.11 = (bf16[800,128]{1,0:T(8,128)(2,1)S(1)}, bf16[800,128]{1,0:T(8,128)(2,1)S(1)}, u32[]{:S(2)}, u32[]{:S(2)}) collective-permute-start(bf16[800,128]{1,0:T(8,128)(2,1)S(1)} %slice.3), channel_id=1, source_target_pairs={{0,16},{16,0},{1,17},{17,1},{2,18},{18,2},{3,19},{19,3},{4,20},{20... | collective-permute-start | bytes 614408 | tf_op jit(solution)/shard_map/ppermute | solution.py:26
  24.2 13.0 %collective-permute-start.4 = (bf16[2,816,128]{2,1,0:T(8,128)(2,1)S(1)}, bf16[2,816,128]{2,1,0:T(8,128)(2,1)S(1)}, u32[]{:S(2)}, u32[]{:S(2)}) collective-permute-start(bf16[2,816,128]{2,1,0:T(8,128)(2,1)S(1)} %near.1.refs_4_.refs_0_), channel_id=1, source_target_pairs={{0,8},{4,12},{8,0},{12,4},{1,9},{5,13},{9,1},{13,5},{2,10},{6,14},... | collective-permute-start | bytes 1253384 | tf_op jit(solution)/shard_map/ppermute | solution.py:26
  25.3 23.2 %copy-start.4 = (f32[1280]{0:T(1024)S(1)}, f32[1280]{0:T(1024)}, u32[]{:S(2)}) copy-start(f32[1280]{0:T(1024)} %refs_13_.1) | copy-start | bytes 15364
  31.7 14.5 %collective-permute-start.16 = (bf16[2,800,128]{2,1,0:T(8,128)(2,1)S(1)}, bf16[2,800,128]{2,1,0:T(8,128)(2,1)S(1)}, u32[]{:S(2)}, u32[]{:S(2)}) collective-permute-start(bf16[2,800,128]{2,1,0:T(8,128)(2,1)S(1)} %pad_maximum_fusion.refs_5_), channel_id=1, source_target_pairs={{0,8},{4,12},{8,0},{12,4},{1,9},{5,13},{9,1},{13,5},{2,10},{6,14},... | collective-permute-start | bytes 1228808 | tf_op jit(solution)/shard_map/ppermute | solution.py:26
  32.8 6.4 %collective-permute-start.13 = (bf16[480,128]{1,0:T(8,128)(2,1)S(1)}, bf16[480,128]{1,0:T(8,128)(2,1)S(1)}, u32[]{:S(2)}, u32[]{:S(2)}) collective-permute-start(bf16[480,128]{1,0:T(8,128)(2,1)S(1)} %get-tuple-element.64), channel_id=1, source_target_pairs={{0,1},{1,0},{2,3},{3,2},{4,5},{5,4},{6,7},{7,6},{8,9},{9,8},{10,11... | collective-permute-start | bytes 368648 | tf_op jit(solution)/shard_map/ppermute | solution.py:26
  32.8 13.4 %collective-permute-start.14 = (bf16[480,128]{1,0:T(8,128)(2,1)S(1)}, bf16[480,128]{1,0:T(8,128)(2,1)S(1)}, u32[]{:S(2)}, u32[]{:S(2)}) collective-permute-start(bf16[480,128]{1,0:T(8,128)(2,1)S(1)} %get-tuple-element.65), channel_id=1, source_target_pairs={{0,2},{1,3},{2,0},{3,1},{4,6},{5,7},{6,4},{7,5},{8,10},{9,11},{10,... | collective-permute-start | bytes 368648 | tf_op jit(solution)/shard_map/ppermute | solution.py:26
  36.8 9.3 %collective-permute-start.15 = (bf16[480,128]{1,0:T(8,128)(2,1)S(1)}, bf16[480,128]{1,0:T(8,128)(2,1)S(1)}, u32[]{:S(2)}, u32[]{:S(2)}) collective-permute-start(bf16[480,128]{1,0:T(8,128)(2,1)S(1)} %get-tuple-element.66), channel_id=1, source_target_pairs={{0,3},{1,2},{2,1},{3,0},{4,7},{5,6},{6,5},{7,4},{8,11},{9,10},{10,... | collective-permute-start | bytes 368648 | tf_op jit(solution)/shard_map/ppermute | solution.py:26
  37.1 9.5 %collective-permute-start.3 = (bf16[2,816,128]{2,1,0:T(8,128)(2,1)S(1)}, bf16[2,816,128]{2,1,0:T(8,128)(2,1)S(1)}, u32[]{:S(2)}, u32[]{:S(2)}) collective-permute-start(bf16[2,816,128]{2,1,0:T(8,128)(2,1)S(1)} %near.1.refs_4_.refs_0_), channel_id=1, source_target_pairs={{0,4},{4,0},{8,12},{12,8},{1,5},{5,1},{9,13},{13,9},{2,6},{6,2},{1... | collective-permute-start | bytes 1253384 | tf_op jit(solution)/shard_map/ppermute | solution.py:26
  39.1 8.8 %collective-permute-start.12 = (bf16[2,816,128]{2,1,0:T(8,128)(2,1)S(1)}, bf16[2,816,128]{2,1,0:T(8,128)(2,1)S(1)}, u32[]{:S(2)}, u32[]{:S(2)}) collective-permute-start(bf16[2,816,128]{2,1,0:T(8,128)(2,1)S(1)} %collective-permute-done.4.refs_8_.refs_2_), channel_id=1, source_target_pairs={{0,4},{4,0},{8,12},{12,8},{1,5},{5,1},{9,13},{13,9},{2,6},{6,2},{1... | collective-permute-start | bytes 1253384 | tf_op jit(solution)/shard_map/ppermute | solution.py:26
  46.1 1.7 %collective-permute-start.17 = (bf16[2,800,128]{2,1,0:T(8,128)(2,1)S(1)}, bf16[2,800,128]{2,1,0:T(8,128)(2,1)S(1)}, u32[]{:S(2)}, u32[]{:S(2)}) collective-permute-start(bf16[2,800,128]{2,1,0:T(8,128)(2,1)S(1)} %pad_maximum_fusion.refs_5_), channel_id=1, source_target_pairs={{0,4},{4,0},{8,12},{12,8},{1,5},{5,1},{9,13},{13,9},{2,6},{6,2},{1... | collective-permute-start | bytes 1228808 | tf_op jit(solution)/shard_map/ppermute | solution.py:26
  46.2 2.3 %collective-permute-start.18 = (bf16[2,800,128]{2,1,0:T(8,128)(2,1)S(1)}, bf16[2,800,128]{2,1,0:T(8,128)(2,1)S(1)}, u32[]{:S(2)}, u32[]{:S(2)}) collective-permute-start(bf16[2,800,128]{2,1,0:T(8,128)(2,1)S(1)} %collective-permute-done.16.refs_9_), channel_id=1, source_target_pairs={{0,4},{4,0},{8,12},{12,8},{1,5},{5,1},{9,13},{13,9},{2,6},{6,2},{1... | collective-permute-start | bytes 1228808 | tf_op jit(solution)/shard_map/ppermute | solution.py:26
  50.4 8.9 %collective-permute-start.21 = (bf16[96,1280]{1,0:T(8,128)(2,1)S(1)}, bf16[96,1280]{1,0:T(8,128)(2,1)S(1)}, u32[]{:S(2)}, u32[]{:S(2)}) collective-permute-start(bf16[96,1280]{1,0:T(8,128)(2,1)S(1)} %get-tuple-element.75.refs_4_), channel_id=1, source_target_pairs={{0,8},{4,12},{8,0},{12,4},{1,9},{5,13},{9,1},{13,5},{2,10},{6,14},... | collective-permute-start | bytes 737288 | tf_op jit(solution)/shard_map/ppermute | solution.py:26
  51.6 12.2 %collective-permute-start.22 = (bf16[96,1280]{1,0:T(8,128)(2,1)S(1)}, bf16[96,1280]{1,0:T(8,128)(2,1)S(1)}, u32[]{:S(2)}, u32[]{:S(2)}) collective-permute-start(bf16[96,1280]{1,0:T(8,128)(2,1)S(1)} %get-tuple-element.76.refs_5_), channel_id=1, source_target_pairs={{0,8},{4,12},{8,0},{12,4},{1,9},{5,13},{9,1},{13,5},{2,10},{6,14},... | collective-permute-start | bytes 737288 | tf_op jit(solution)/shard_map/ppermute | solution.py:26
  59.3 4.5 %collective-permute-start.23 = (bf16[96,1280]{1,0:T(8,128)(2,1)S(1)}, bf16[96,1280]{1,0:T(8,128)(2,1)S(1)}, u32[]{:S(2)}, u32[]{:S(2)}) collective-permute-start(bf16[96,1280]{1,0:T(8,128)(2,1)S(1)} %collective-permute-done.21.refs_8_), channel_id=1, source_target_pairs={{0,4},{4,0},{8,12},{12,8},{1,5},{5,1},{9,13},{13,9},{2,6},{6,2},{1... | collective-permute-start | bytes 737288 | tf_op jit(solution)/shard_map/ppermute | solution.py:26
  59.3 4.5 %collective-permute-start.19 = (bf16[96,1280]{1,0:T(8,128)(2,1)S(1)}, bf16[96,1280]{1,0:T(8,128)(2,1)S(1)}, u32[]{:S(2)}, u32[]{:S(2)}) collective-permute-start(bf16[96,1280]{1,0:T(8,128)(2,1)S(1)} %get-tuple-element.75.refs_4_), channel_id=1, source_target_pairs={{0,4},{4,0},{8,12},{12,8},{1,5},{5,1},{9,13},{13,9},{2,6},{6,2},{1... | collective-permute-start | bytes 737288 | tf_op jit(solution)/shard_map/ppermute | solution.py:26
  59.8 4.0 %collective-permute-start.20 = (bf16[96,1280]{1,0:T(8,128)(2,1)S(1)}, bf16[96,1280]{1,0:T(8,128)(2,1)S(1)}, u32[]{:S(2)}, u32[]{:S(2)}) collective-permute-start(bf16[96,1280]{1,0:T(8,128)(2,1)S(1)} %get-tuple-element.76.refs_5_), channel_id=1, source_target_pairs={{0,4},{4,0},{8,12},{12,8},{1,5},{5,1},{9,13},{13,9},{2,6},{6,2},{1... | collective-permute-start | bytes 737288 | tf_op jit(solution)/shard_map/ppermute | solution.py:26
  63.8 1.5 %collective-permute-start.24 = (bf16[96,1280]{1,0:T(8,128)(2,1)S(1)}, bf16[96,1280]{1,0:T(8,128)(2,1)S(1)}, u32[]{:S(2)}, u32[]{:S(2)}) collective-permute-start(bf16[96,1280]{1,0:T(8,128)(2,1)S(1)} %collective-permute-done.22.refs_9_), channel_id=1, source_target_pairs={{0,4},{4,0},{8,12},{12,8},{1,5},{5,1},{9,13},{13,9},{2,6},{6,2},{1... | collective-permute-start | bytes 737288 | tf_op jit(solution)/shard_map/ppermute | solution.py:26

commit v21 on v19

--- a/solution.py
+++ b/solution.py
@@ -196,10 +196,10 @@
         for h in range(heads):
             s = scores[:, h * PAIR : (h + 1) * PAIR] + bias
             e = jnp.exp2((s - jnp.max(s, axis=0, keepdims=True)) * factor)
-            weights = (e * (1.0 / jnp.sum(e, axis=0, keepdims=True))).astype(BF16)
-            mixed.append(
-                jnp.dot(v_turned[h * HD : (h + 1) * HD], weights, preferred_element_type=F32)
+            part = jnp.dot(
+                v_turned[h * HD : (h + 1) * HD], e.astype(BF16), preferred_element_type=F32
             )
+            mixed.append(part * (1.0 / jnp.sum(e, axis=0, keepdims=True)))
         mixed = jnp.concatenate(mixed, axis=0).astype(BF16)
         mixed = lax.dot_general(
             order, mixed, (((1,), (1,)), ((), ())), preferred_element_type=F32

time: 65.2 us -> 65.2 us (level)
  no operation moved by 1% of the time
where the time goes in v21:
time: 65.2 us; the launch traced here: 65 us
  waiting for transfers between devices  27.1 us (42%)
  starting transfers between devices  21 us (32%)
  Pallas kernels  12.3 us (19%)
  local copies, waits for them, and re-layouts  4.33 us (7%)
    ppermute x24, waiting for transfers between devices, swap(): return lax.ppermute(x, axis, [(i, i ^ bit) for i in range(size)])  25.3 us
    ppermute x24, starting transfers between devices, swap(): return lax.ppermute(x, axis, [(i, i ^ bit) for i in range(size)])  18.4 us
    pallas_call x1, Pallas kernels, local(): pl.pallas_call(functools.partial(attention_kernel, n_ctx, width), out_sha...  6.16 us
    unnamed x14, local copies, waits for them, and re-layouts  4.32 us
    ppermute x1, starting transfers between devices, local(): lax.ppermute(far, ('dp', 'tensor'), [(d * n_ten + t, d * n_ten + (t ^ 2 +...  2.59 us
    pallas_call x1, Pallas kernels, local(): pl.pallas_call(functools.partial(project_kernel, n_ctx, width, col), out_...  1.93 us
    ppermute x1, waiting for transfers between devices, local(): lax.ppermute(far, ('dp', 'tensor'), [(d * n_ten + t, d * n_ten + (t ^ 2 +...  1.85 us
    pallas_call x1, Pallas kernels, local(): pl.pallas_call(functools.partial(place_kernel, n_ctx), out_shape=shape(gr...  1.84 us
  transfers between devices with their start and end apart: 25, of which 10 were waited for; matrix products, arithmetic and copies ran while one was open for 0% of the time, Pallas kernels for 12%

profile of v21, /device:TPU:0, one launch (start us, length us, event | category | flops | bytes accessed | tf_op | source)
XLA Modules:
  0.0 65.0 jit_solution(14639244948506673507)
XLA Ops:
  0.1 1.1 %copy-done.1 = bf16[320,3,320]{2,0,1:T(8,128)(2,1)S(1)} copy-done((bf16[320,3,320]{2,0,1:T(8,128)(2,1)S(1)}, bf16[320,3,320]{2,0,1:T(8,128)(2,1)}, u32[]{:S(2)}) %copy-start.1) | copy-done | bytes 614424
  1.2 0.7 %pack.1 = (bf16[816,128]{1,0:T(8,128)(2,1)S(1)}, bf16[816,128]{1,0:T(8,128)(2,1)S(1)}, bf16[3,816,128]{2,1,0:T(8,128)(2,1)S(1)}) custom-call(s32[3]{0:T(128)S(1)} %pad_add_fusion.index_ref, bf16[3,320,320]{2,1,0:T(8,128)(2,1)S(1)} %bitcast.8), custom_call_target="tpu_custom_call" | custom-call | tf_op jit(solution)/shard_map/pack/pallas_call | solution.py:324
  1.9 0.5 collective-permute-start.2
  2.4 2.6 %collective-permute-start.1 = (bf16[816,128]{1,0:T(8,128)(2,1)S(1)}, bf16[816,128]{1,0:T(8,128)(2,1)S(1)}, u32[]{:S(2)}, u32[]{:S(2)}) collective-permute-start(bf16[816,128]{1,0:T(8,128)(2,1)S(1)} %get-tuple-element.43), channel_id=1, source_target_pairs={{0,8},{4,12},{8,0},{12,4},{1,9},{5,13},{9,1},{13,5},{2,10},{6,14},... | collective-permute-start | bytes 626696 | tf_op jit(solution)/shard_map/ppermute | solution.py:26
  5.0 0.9 %copy-done.2 = bf16[320,320]{1,0:T(8,128)(2,1)S(1)} copy-done((bf16[320,320]{1,0:T(8,128)(2,1)S(1)}, bf16[320,320]{1,0:T(8,128)(2,1)}, u32[]{:S(2)}) %copy-start.2) | copy-done | bytes 204824
  6.0 1.6 %collective-permute-start = (bf16[800,128]{1,0:T(8,128)(2,1)S(1)}, bf16[800,128]{1,0:T(8,128)(2,1)S(1)}, u32[]{:S(2)}, u32[]{:S(2)}) collective-permute-start(bf16[800,128]{1,0:T(8,128)(2,1)S(1)} %get-tuple-element.42.own_ref), channel_id=1, source_target_pairs={{0,1},{1,0},{2,3},{3,2},{4,5},{5,4},{6,7},{7,6},{8,9},{9,8},{10,11... | collective-permute-start | bytes 614408 | tf_op jit(solution)/shard_map/ppermute | solution.py:26
  7.7 2.6 %collective-permute-start.9 = (bf16[848,128]{1,0:T(8,128)(2,1)S(1)}, bf16[848,128]{1,0:T(8,128)(2,1)S(1)}, u32[]{:S(2)}, u32[]{:S(2)}) collective-permute-start(bf16[848,128]{1,0:T(8,128)(2,1)S(1)} %get-tuple-element.60), channel_id=1, source_target_pairs={{0,2},{1,3},{2,0},{3,1},{16,19},{17,18},{18,17},{19,16},{4,6},{5,7... | collective-permute-start | bytes 651272 | tf_op jit(solution)/shard_map/ppermute | solution.py:343
  10.3 0.5 collective-permute-start.5
  10.8 1.7 %collective-permute-start.4 = (bf16[816,128]{1,0:T(8,128)(2,1)S(1)}, bf16[816,128]{1,0:T(8,128)(2,1)S(1)}, u32[]{:S(2)}, u32[]{:S(2)}) collective-permute-start(bf16[816,128]{1,0:T(8,128)(2,1)S(1)} %collective-permute-done.1.refs_2_), channel_id=1, source_target_pairs={{0,16},{16,0},{1,17},{17,1},{2,18},{18,2},{3,19},{19,3},{4,20},{20... | collective-permute-start | bytes 626696 | tf_op jit(solution)/shard_map/ppermute | solution.py:26
  12.5 1.5 %copy-done = bf16[768,1280]{1,0:T(8,128)(2,1)S(1)} copy-done((bf16[768,1280]{1,0:T(8,128)(2,1)S(1)}, bf16[768,1280]{1,0:T(8,128)(2,1)}, u32[]{:S(2)}) %copy-start) | copy-done | bytes 1966104
  14.0 0.7 %copy-done.3 = f32[1280]{0:T(1024)S(1)} copy-done((f32[1280]{0:T(1024)S(1)}, f32[1280]{0:T(1024)}, u32[]{:S(2)}) %copy-start.3) | copy-done | bytes 5144
  14.7 1.6 %norm.1 = (bf16[768,1280]{1,0:T(8,128)(2,1)S(1)}, bf16[192,1280]{1,0:T(8,128)(2,1)S(1)}) custom-call(s32[3]{0:T(128)S(1)} %pad_add_fusion.index_ref, bf16[768,1280]{1,0:T(8,128)(2,1)S(1)} %copy-done, f32[1280]{0:T(1024)S(1)} %copy-done.3), custom_call_target="tpu_custom_call" | custom-call | tf_op jit(solution)/shard_map/norm/pallas_call | solution.py:357
  16.3 1.2 %collective-permute-done.next_ref = bf16[800,128]{1,0:T(8,128)(2,1)S(1)} collective-permute-done((bf16[800,128]{1,0:T(8,128)(2,1)S(1)}, bf16[800,128]{1,0:T(8,128)(2,1)S(1)}, u32[]{:S(2)}, u32[]{:S(2)}) %collective-permute-start) | collective-permute-done | bytes 204832 | tf_op jit(solution)/shard_map/ppermute | solution.py:26
  18.5 1.9 %collective-permute-done.9 = bf16[848,128]{1,0:T(8,128)(2,1)S(1)} collective-permute-done((bf16[848,128]{1,0:T(8,128)(2,1)S(1)}, bf16[848,128]{1,0:T(8,128)(2,1)S(1)}, u32[]{:S(2)}, u32[]{:S(2)}) %collective-permute-start.9) | collective-permute-done | bytes 217120 | tf_op jit(solution)/shard_map/ppermute | solution.py:343
  20.4 1.2 %collective-permute-start.10 = (bf16[800,128]{1,0:T(8,128)(2,1)S(1)}, bf16[800,128]{1,0:T(8,128)(2,1)S(1)}, u32[]{:S(2)}, u32[]{:S(2)}) collective-permute-start(bf16[800,128]{1,0:T(8,128)(2,1)S(1)} %slice.3), channel_id=1, source_target_pairs={{0,16},{16,0},{1,17},{17,1},{2,18},{18,2},{3,19},{19,3},{4,20},{20... | collective-permute-start | bytes 614408 | tf_op jit(solution)/shard_map/ppermute | solution.py:26
  21.6 6.2 %attention.1 = (bf16[480,128]{1,0:T(8,128)(2,1)S(1)}, bf16[480,128]{1,0:T(8,128)(2,1)S(1)}, bf16[480,128]{1,0:T(8,128)(2,1)S(1)}, bf16[480,128]{1,0:T(8,128)(2,1)S(1)}) custom-call(s32[3]{0:T(128)S(1)} %pad_add_fusion.index_ref, bf16[768,1280]{1,0:T(8,128)(2,1)S(1)} %get-tuple-element.51.hidden_ref, s32[6,128]{1,0:T(8,128)S(1)} %bitcast.9, ...), custom_call_target="tpu_custom_call" | custom-call | tf_op jit(solution)/shard_map/attention/pallas_call | solution.py:388
  27.8 0.7 %collective-permute-done.11.refs_8_.refs_2_ = bf16[2,816,128]{2,1,0:T(8,128)(2,1)S(1)} collective-permute-done((bf16[2,816,128]{2,1,0:T(8,128)(2,1)S(1)}, bf16[2,816,128]{2,1,0:T(8,128)(2,1)S(1)}, u32[]{:S(2)}, u32[]{:S(2)}) %collective-permute-start.11) | collective-permute-done | bytes 417824 | tf_op jit(solution)/shard_map/ppermute | solution.py:26
  28.5 1.6 %collective-permute-start.16 = (bf16[2,800,128]{2,1,0:T(8,128)(2,1)S(1)}, bf16[2,800,128]{2,1,0:T(8,128)(2,1)S(1)}, u32[]{:S(2)}, u32[]{:S(2)}) collective-permute-start(bf16[2,800,128]{2,1,0:T(8,128)(2,1)S(1)} %pad_maximum_fusion.refs_5_), channel_id=1, source_target_pairs={{0,8},{4,12},{8,0},{12,4},{1,9},{5,13},{9,1},{13,5},{2,10},{6,14},... | collective-permute-start | bytes 1228808 | tf_op jit(solution)/shard_map/ppermute | solution.py:26
  30.1 2.0 %collective-permute-start.13 = (bf16[480,128]{1,0:T(8,128)(2,1)S(1)}, bf16[480,128]{1,0:T(8,128)(2,1)S(1)}, u32[]{:S(2)}, u32[]{:S(2)}) collective-permute-start(bf16[480,128]{1,0:T(8,128)(2,1)S(1)} %get-tuple-element.64), channel_id=1, source_target_pairs={{0,1},{1,0},{2,3},{3,2},{4,5},{5,4},{6,7},{7,6},{8,9},{9,8},{10,11... | collective-permute-start | bytes 368648 | tf_op jit(solution)/shard_map/ppermute | solution.py:26
  32.1 2.6 %collective-permute-start.14 = (bf16[480,128]{1,0:T(8,128)(2,1)S(1)}, bf16[480,128]{1,0:T(8,128)(2,1)S(1)}, u32[]{:S(2)}, u32[]{:S(2)}) collective-permute-start(bf16[480,128]{1,0:T(8,128)(2,1)S(1)} %get-tuple-element.65), channel_id=1, source_target_pairs={{0,2},{1,3},{2,0},{3,1},{4,6},{5,7},{6,4},{7,5},{8,10},{9,11},{10,... | collective-permute-start | bytes 368648 | tf_op jit(solution)/shard_map/ppermute | solution.py:26
  34.7 1.5 %collective-permute-done.13.refs_1_ = bf16[480,128]{1,0:T(8,128)(2,1)S(1)} collective-permute-done((bf16[480,128]{1,0:T(8,128)(2,1)S(1)}, bf16[480,128]{1,0:T(8,128)(2,1)S(1)}, u32[]{:S(2)}, u32[]{:S(2)}) %collective-permute-start.13) | collective-permute-done | bytes 122912 | tf_op jit(solution)/shard_map/ppermute | solution.py:26
  36.3 7.8 %collective-permute-done.14.refs_2_ = bf16[480,128]{1,0:T(8,128)(2,1)S(1)} collective-permute-done((bf16[480,128]{1,0:T(8,128)(2,1)S(1)}, bf16[480,128]{1,0:T(8,128)(2,1)S(1)}, u32[]{:S(2)}, u32[]{:S(2)}) %collective-permute-start.14) | collective-permute-done | bytes 122912 | tf_op jit(solution)/shard_map/ppermute | solution.py:26
  44.6 1.2 %collective-permute-done.17.refs_7_ = bf16[2,800,128]{2,1,0:T(8,128)(2,1)S(1)} collective-permute-done((bf16[2,800,128]{2,1,0:T(8,128)(2,1)S(1)}, bf16[2,800,128]{2,1,0:T(8,128)(2,1)S(1)}, u32[]{:S(2)}, u32[]{:S(2)}) %collective-permute-start.17) | collective-permute-done | bytes 409632 | tf_op jit(solution)/shard_map/ppermute | solution.py:26
  45.8 0.6 collective-permute-done.18.refs_11_
  46.4 1.9 %project.1 = (bf16[96,1280]{1,0:T(8,128)(2,1)S(1)}, bf16[96,1280]{1,0:T(8,128)(2,1)S(1)}) custom-call(s32[3]{0:T(128)S(1)} %pad_add_fusion.index_ref, bf16[480,128]{1,0:T(8,128)(2,1)S(1)} %get-tuple-element.69.refs_0_, bf16[480,128]{1,0:T(8,128)(2,1)S(1)} %collective-permute-done.13.refs_1_, bf16[480,128]{1,0:T(8,128)(2,1)S(1)} %collective-permute-done.14.refs_2_, ...), custom_call_target="tpu_custom_call" | custom-call | tf_op jit(solution)/shard_map/project/pallas_call | solution.py:409
  48.3 0.5 collective-permute-start.21
  48.9 1.6 %collective-permute-start.22 = (bf16[96,1280]{1,0:T(8,128)(2,1)S(1)}, bf16[96,1280]{1,0:T(8,128)(2,1)S(1)}, u32[]{:S(2)}, u32[]{:S(2)}) collective-permute-start(bf16[96,1280]{1,0:T(8,128)(2,1)S(1)} %get-tuple-element.76.refs_5_), channel_id=1, source_target_pairs={{0,8},{4,12},{8,0},{12,4},{1,9},{5,13},{9,1},{13,5},{2,10},{6,14},... | collective-permute-start | bytes 737288 | tf_op jit(solution)/shard_map/ppermute | solution.py:26
  50.4 6.8 %collective-permute-done.21.refs_8_ = bf16[96,1280]{1,0:T(8,128)(2,1)S(1)} collective-permute-done((bf16[96,1280]{1,0:T(8,128)(2,1)S(1)}, bf16[96,1280]{1,0:T(8,128)(2,1)S(1)}, u32[]{:S(2)}, u32[]{:S(2)}) %collective-permute-start.21) | collective-permute-done | bytes 245792 | tf_op jit(solution)/shard_map/ppermute | solution.py:26
  57.2 0.5 collective-permute-start.19
  57.7 4.0 %collective-permute-done.22.refs_9_ = bf16[96,1280]{1,0:T(8,128)(2,1)S(1)} collective-permute-done((bf16[96,1280]{1,0:T(8,128)(2,1)S(1)}, bf16[96,1280]{1,0:T(8,128)(2,1)S(1)}, u32[]{:S(2)}, u32[]{:S(2)}) %collective-permute-start.22) | collective-permute-done | bytes 245792 | tf_op jit(solution)/shard_map/ppermute | solution.py:26
  61.7 1.5 %collective-permute-done.24.refs_11_ = bf16[96,1280]{1,0:T(8,128)(2,1)S(1)} collective-permute-done((bf16[96,1280]{1,0:T(8,128)(2,1)S(1)}, bf16[96,1280]{1,0:T(8,128)(2,1)S(1)}, u32[]{:S(2)}, u32[]{:S(2)}) %collective-permute-start.24) | collective-permute-done | bytes 245792 | tf_op jit(solution)/shard_map/ppermute | solution.py:26
  63.2 1.8 %placement.1 = bf16[192,1280]{1,0:T(8,128)(2,1)} custom-call(s32[3]{0:T(128)S(1)} %pad_add_fusion.index_ref, bf16[2,816,128]{2,1,0:T(8,128)(2,1)S(1)} %near.1.refs_4_.refs_0_, bf16[2,816,128]{2,1,0:T(8,128)(2,1)S(1)} %collective-permute-done.3.refs_6_.refs_1_, bf16[2,816,128]{2,1,0:T(8,128)(2,1)S(1)} %collective-permute-done.11.refs_8_.refs_2_, ...), custom_call_target="tpu_custom_call" | custom-call | tf_op jit(solution)/shard_map/placement/pallas_call | solution.py:431
  (42 shorter events, 1.8 us)
Async XLA Ops:
  0.0 17.5 %copy-start.6 = (s32[192]{0:T(256)S(1)}, s32[192]{0:T(256)}, u32[]{:S(2)}) copy-start(s32[192]{0:T(256)} %param.9) | copy-start | bytes 2308
  0.1 1.1 %copy-start.1 = (bf16[320,3,320]{2,0,1:T(8,128)(2,1)S(1)}, bf16[320,3,320]{2,0,1:T(8,128)(2,1)}, u32[]{:S(2)}) copy-start(bf16[320,3,320]{2,0,1:T(8,128)(2,1)} %param.11) | copy-start | bytes 1843204
  1.2 20.4 %copy-start.5 = (s32[768]{0:T(1024)S(1)}, s32[768]{0:T(1024)}, u32[]{:S(2)}) copy-start(s32[768]{0:T(1024)} %param.8) | copy-start | bytes 9220
  1.9 8.9 %collective-permute-start.2 = (bf16[3,816,128]{2,1,0:T(8,128)(2,1)S(1)}, bf16[3,816,128]{2,1,0:T(8,128)(2,1)S(1)}, u32[]{:S(2)}, u32[]{:S(2)}) collective-permute-start(bf16[3,816,128]{2,1,0:T(8,128)(2,1)S(1)} %get-tuple-element.44.refs_0_), channel_id=1, source_target_pairs={{0,4},{4,0},{8,12},{12,8},{1,5},{5,1},{9,13},{13,9},{2,6},{6,2},{1... | collective-permute-start | bytes 1880072 | tf_op jit(solution)/shard_map/ppermute | solution.py:26
  2.4 8.4 %collective-permute-start.1 = (bf16[816,128]{1,0:T(8,128)(2,1)S(1)}, bf16[816,128]{1,0:T(8,128)(2,1)S(1)}, u32[]{:S(2)}, u32[]{:S(2)}) collective-permute-start(bf16[816,128]{1,0:T(8,128)(2,1)S(1)} %get-tuple-element.43), channel_id=1, source_target_pairs={{0,8},{4,12},{8,0},{12,4},{1,9},{5,13},{9,1},{13,5},{2,10},{6,14},... | collective-permute-start | bytes 626696 | tf_op jit(solution)/shard_map/ppermute | solution.py:26
  5.0 0.9 %copy-start.2 = (bf16[320,320]{1,0:T(8,128)(2,1)S(1)}, bf16[320,320]{1,0:T(8,128)(2,1)}, u32[]{:S(2)}) copy-start(bf16[320,320]{1,0:T(8,128)(2,1)} %proj_ref.1) | copy-start | bytes 614404
  6.0 11.5 %collective-permute-start = (bf16[800,128]{1,0:T(8,128)(2,1)S(1)}, bf16[800,128]{1,0:T(8,128)(2,1)S(1)}, u32[]{:S(2)}, u32[]{:S(2)}) collective-permute-start(bf16[800,128]{1,0:T(8,128)(2,1)S(1)} %get-tuple-element.42.own_ref), channel_id=1, source_target_pairs={{0,1},{1,0},{2,3},{3,2},{4,5},{5,4},{6,7},{7,6},{8,9},{9,8},{10,11... | collective-permute-start | bytes 614408 | tf_op jit(solution)/shard_map/ppermute | solution.py:26
  7.7 12.7 %collective-permute-start.9 = (bf16[848,128]{1,0:T(8,128)(2,1)S(1)}, bf16[848,128]{1,0:T(8,128)(2,1)S(1)}, u32[]{:S(2)}, u32[]{:S(2)}) collective-permute-start(bf16[848,128]{1,0:T(8,128)(2,1)S(1)} %get-tuple-element.60), channel_id=1, source_target_pairs={{0,2},{1,3},{2,0},{3,1},{16,19},{17,18},{18,17},{19,16},{4,6},{5,7... | collective-permute-start | bytes 651272 | tf_op jit(solution)/shard_map/ppermute | solution.py:343
  10.3 7.7 %collective-permute-start.5 = (bf16[816,128]{1,0:T(8,128)(2,1)S(1)}, bf16[816,128]{1,0:T(8,128)(2,1)S(1)}, u32[]{:S(2)}, u32[]{:S(2)}) collective-permute-start(bf16[816,128]{1,0:T(8,128)(2,1)S(1)} %get-tuple-element.49), channel_id=1, source_target_pairs={{0,8},{4,12},{8,0},{12,4},{1,9},{5,13},{9,1},{13,5},{2,10},{6,14},... | collective-permute-start | bytes 626696 | tf_op jit(solution)/shard_map/ppermute | solution.py:26
  10.8 7.2 %collective-permute-start.4 = (bf16[816,128]{1,0:T(8,128)(2,1)S(1)}, bf16[816,128]{1,0:T(8,128)(2,1)S(1)}, u32[]{:S(2)}, u32[]{:S(2)}) collective-permute-start(bf16[816,128]{1,0:T(8,128)(2,1)S(1)} %collective-permute-done.1.refs_2_), channel_id=1, source_target_pairs={{0,16},{16,0},{1,17},{17,1},{2,18},{18,2},{3,19},{19,3},{4,20},{20... | collective-permute-start | bytes 626696 | tf_op jit(solution)/shard_map/ppermute | solution.py:26
  12.5 5.5 %collective-permute-start.6 = (bf16[816,128]{1,0:T(8,128)(2,1)S(1)}, bf16[816,128]{1,0:T(8,128)(2,1)S(1)}, u32[]{:S(2)}, u32[]{:S(2)}) collective-permute-start(bf16[816,128]{1,0:T(8,128)(2,1)S(1)} %collective-permute-done.1.refs_2_), channel_id=1, source_target_pairs={{0,4},{4,0},{8,12},{12,8},{1,5},{5,1},{9,13},{13,9},{2,6},{6,2},{1... | collective-permute-start | bytes 626696 | tf_op jit(solution)/shard_map/ppermute | solution.py:26
  12.5 1.5 %copy-start = (bf16[768,1280]{1,0:T(8,128)(2,1)S(1)}, bf16[768,1280]{1,0:T(8,128)(2,1)}, u32[]{:S(2)}) copy-start(bf16[768,1280]{1,0:T(8,128)(2,1)} %patches_ref) | copy-start | bytes 5898244
  14.0 0.7 %copy-start.3 = (f32[1280]{0:T(1024)S(1)}, f32[1280]{0:T(1024)}, u32[]{:S(2)}) copy-start(f32[1280]{0:T(1024)} %gain_ref.1) | copy-start | bytes 15364
  17.6 10.9 %collective-permute-start.11 = (bf16[2,816,128]{2,1,0:T(8,128)(2,1)S(1)}, bf16[2,816,128]{2,1,0:T(8,128)(2,1)S(1)}, u32[]{:S(2)}, u32[]{:S(2)}) collective-permute-start(bf16[2,816,128]{2,1,0:T(8,128)(2,1)S(1)} %near.1.refs_4_.refs_0_), channel_id=1, source_target_pairs={{0,8},{4,12},{8,0},{12,4},{1,9},{5,13},{9,1},{13,5},{2,10},{6,14},... | collective-permute-start | bytes 1253384 | tf_op jit(solution)/shard_map/ppermute | solution.py:26
  18.0 3.6 %collective-permute-start.7 = (bf16[816,128]{1,0:T(8,128)(2,1)S(1)}, bf16[816,128]{1,0:T(8,128)(2,1)S(1)}, u32[]{:S(2)}, u32[]{:S(2)}) collective-permute-start(bf16[816,128]{1,0:T(8,128)(2,1)S(1)} %collective-permute-done.4.refs_3_), channel_id=1, source_target_pairs={{0,4},{4,0},{8,12},{12,8},{1,5},{5,1},{9,13},{13,9},{2,6},{6,2},{1... | collective-permute-start | bytes 626696 | tf_op jit(solution)/shard_map/ppermute | solution.py:26
  18.3 3.4 %collective-permute-start.8 = (bf16[816,128]{1,0:T(8,128)(2,1)S(1)}, bf16[816,128]{1,0:T(8,128)(2,1)S(1)}, u32[]{:S(2)}, u32[]{:S(2)}) collective-permute-start(bf16[816,128]{1,0:T(8,128)(2,1)S(1)} %collective-permute-done.5.refs_4_), channel_id=1, source_target_pairs={{0,4},{4,0},{8,12},{12,8},{1,5},{5,1},{9,13},{13,9},{2,6},{6,2},{1... | collective-permute-start | bytes 626696 | tf_op jit(solution)/shard_map/ppermute | solution.py:26
  20.4 7.4 %collective-permute-start.10 = (bf16[800,128]{1,0:T(8,128)(2,1)S(1)}, bf16[800,128]{1,0:T(8,128)(2,1)S(1)}, u32[]{:S(2)}, u32[]{:S(2)}) collective-permute-start(bf16[800,128]{1,0:T(8,128)(2,1)S(1)} %slice.3), channel_id=1, source_target_pairs={{0,16},{16,0},{1,17},{17,1},{2,18},{18,2},{3,19},{19,3},{4,20},{20... | collective-permute-start | bytes 614408 | tf_op jit(solution)/shard_map/ppermute | solution.py:26
  21.6 24.8 %copy-start.4 = (f32[1280]{0:T(1024)S(1)}, f32[1280]{0:T(1024)}, u32[]{:S(2)}) copy-start(f32[1280]{0:T(1024)} %refs_13_.1) | copy-start | bytes 15364
  28.5 15.5 %collective-permute-start.16 = (bf16[2,800,128]{2,1,0:T(8,128)(2,1)S(1)}, bf16[2,800,128]{2,1,0:T(8,128)(2,1)S(1)}, u32[]{:S(2)}, u32[]{:S(2)}) collective-permute-start(bf16[2,800,128]{2,1,0:T(8,128)(2,1)S(1)} %pad_maximum_fusion.refs_5_), channel_id=1, source_target_pairs={{0,8},{4,12},{8,0},{12,4},{1,9},{5,13},{9,1},{13,5},{2,10},{6,14},... | collective-permute-start | bytes 1228808 | tf_op jit(solution)/shard_map/ppermute | solution.py:26
  30.1 6.2 %collective-permute-start.13 = (bf16[480,128]{1,0:T(8,128)(2,1)S(1)}, bf16[480,128]{1,0:T(8,128)(2,1)S(1)}, u32[]{:S(2)}, u32[]{:S(2)}) collective-permute-start(bf16[480,128]{1,0:T(8,128)(2,1)S(1)} %get-tuple-element.64), channel_id=1, source_target_pairs={{0,1},{1,0},{2,3},{3,2},{4,5},{5,4},{6,7},{7,6},{8,9},{9,8},{10,11... | collective-permute-start | bytes 368648 | tf_op jit(solution)/shard_map/ppermute | solution.py:26
  32.1 11.9 %collective-permute-start.14 = (bf16[480,128]{1,0:T(8,128)(2,1)S(1)}, bf16[480,128]{1,0:T(8,128)(2,1)S(1)}, u32[]{:S(2)}, u32[]{:S(2)}) collective-permute-start(bf16[480,128]{1,0:T(8,128)(2,1)S(1)} %get-tuple-element.65), channel_id=1, source_target_pairs={{0,2},{1,3},{2,0},{3,1},{4,6},{5,7},{6,4},{7,5},{8,10},{9,11},{10,... | collective-permute-start | bytes 368648 | tf_op jit(solution)/shard_map/ppermute | solution.py:26
  34.7 9.3 %collective-permute-start.15 = (bf16[480,128]{1,0:T(8,128)(2,1)S(1)}, bf16[480,128]{1,0:T(8,128)(2,1)S(1)}, u32[]{:S(2)}, u32[]{:S(2)}) collective-permute-start(bf16[480,128]{1,0:T(8,128)(2,1)S(1)} %get-tuple-element.66), channel_id=1, source_target_pairs={{0,3},{1,2},{2,1},{3,0},{4,7},{5,6},{6,5},{7,4},{8,11},{9,10},{10,... | collective-permute-start | bytes 368648 | tf_op jit(solution)/shard_map/ppermute | solution.py:26
  34.7 9.8 %collective-permute-start.3 = (bf16[2,816,128]{2,1,0:T(8,128)(2,1)S(1)}, bf16[2,816,128]{2,1,0:T(8,128)(2,1)S(1)}, u32[]{:S(2)}, u32[]{:S(2)}) collective-permute-start(bf16[2,816,128]{2,1,0:T(8,128)(2,1)S(1)} %near.1.refs_4_.refs_0_), channel_id=1, source_target_pairs={{0,4},{4,0},{8,12},{12,8},{1,5},{5,1},{9,13},{13,9},{2,6},{6,2},{1... | collective-permute-start | bytes 1253384 | tf_op jit(solution)/shard_map/ppermute | solution.py:26
  36.3 9.5 %collective-permute-start.12 = (bf16[2,816,128]{2,1,0:T(8,128)(2,1)S(1)}, bf16[2,816,128]{2,1,0:T(8,128)(2,1)S(1)}, u32[]{:S(2)}, u32[]{:S(2)}) collective-permute-start(bf16[2,816,128]{2,1,0:T(8,128)(2,1)S(1)} %collective-permute-done.11.refs_8_.refs_2_), channel_id=1, source_target_pairs={{0,4},{4,0},{8,12},{12,8},{1,5},{5,1},{9,13},{13,9},{2,6},{6,2},{1... | collective-permute-start | bytes 1253384 | tf_op jit(solution)/shard_map/ppermute | solution.py:26
  44.1 1.7 %collective-permute-start.17 = (bf16[2,800,128]{2,1,0:T(8,128)(2,1)S(1)}, bf16[2,800,128]{2,1,0:T(8,128)(2,1)S(1)}, u32[]{:S(2)}, u32[]{:S(2)}) collective-permute-start(bf16[2,800,128]{2,1,0:T(8,128)(2,1)S(1)} %pad_maximum_fusion.refs_5_), channel_id=1, source_target_pairs={{0,4},{4,0},{8,12},{12,8},{1,5},{5,1},{9,13},{13,9},{2,6},{6,2},{1... | collective-permute-start | bytes 1228808 | tf_op jit(solution)/shard_map/ppermute | solution.py:26
  44.1 2.3 %collective-permute-start.18 = (bf16[2,800,128]{2,1,0:T(8,128)(2,1)S(1)}, bf16[2,800,128]{2,1,0:T(8,128)(2,1)S(1)}, u32[]{:S(2)}, u32[]{:S(2)}) collective-permute-start(bf16[2,800,128]{2,1,0:T(8,128)(2,1)S(1)} %collective-permute-done.16.refs_9_), channel_id=1, source_target_pairs={{0,4},{4,0},{8,12},{12,8},{1,5},{5,1},{9,13},{13,9},{2,6},{6,2},{1... | collective-permute-start | bytes 1228808 | tf_op jit(solution)/shard_map/ppermute | solution.py:26
  48.3 8.9 %collective-permute-start.21 = (bf16[96,1280]{1,0:T(8,128)(2,1)S(1)}, bf16[96,1280]{1,0:T(8,128)(2,1)S(1)}, u32[]{:S(2)}, u32[]{:S(2)}) collective-permute-start(bf16[96,1280]{1,0:T(8,128)(2,1)S(1)} %get-tuple-element.75.refs_4_), channel_id=1, source_target_pairs={{0,8},{4,12},{8,0},{12,4},{1,9},{5,13},{9,1},{13,5},{2,10},{6,14},... | collective-permute-start | bytes 737288 | tf_op jit(solution)/shard_map/ppermute | solution.py:26
  48.9 12.8 %collective-permute-start.22 = (bf16[96,1280]{1,0:T(8,128)(2,1)S(1)}, bf16[96,1280]{1,0:T(8,128)(2,1)S(1)}, u32[]{:S(2)}, u32[]{:S(2)}) collective-permute-start(bf16[96,1280]{1,0:T(8,128)(2,1)S(1)} %get-tuple-element.76.refs_5_), channel_id=1, source_target_pairs={{0,8},{4,12},{8,0},{12,4},{1,9},{5,13},{9,1},{13,5},{2,10},{6,14},... | collective-permute-start | bytes 737288 | tf_op jit(solution)/shard_map/ppermute | solution.py:26
  57.2 4.5 %collective-permute-start.23 = (bf16[96,1280]{1,0:T(8,128)(2,1)S(1)}, bf16[96,1280]{1,0:T(8,128)(2,1)S(1)}, u32[]{:S(2)}, u32[]{:S(2)}) collective-permute-start(bf16[96,1280]{1,0:T(8,128)(2,1)S(1)} %collective-permute-done.21.refs_8_), channel_id=1, source_target_pairs={{0,4},{4,0},{8,12},{12,8},{1,5},{5,1},{9,13},{13,9},{2,6},{6,2},{1... | collective-permute-start | bytes 737288 | tf_op jit(solution)/shard_map/ppermute | solution.py:26
  57.2 4.5 %collective-permute-start.19 = (bf16[96,1280]{1,0:T(8,128)(2,1)S(1)}, bf16[96,1280]{1,0:T(8,128)(2,1)S(1)}, u32[]{:S(2)}, u32[]{:S(2)}) collective-permute-start(bf16[96,1280]{1,0:T(8,128)(2,1)S(1)} %get-tuple-element.75.refs_4_), channel_id=1, source_target_pairs={{0,4},{4,0},{8,12},{12,8},{1,5},{5,1},{9,13},{13,9},{2,6},{6,2},{1... | collective-permute-start | bytes 737288 | tf_op jit(solution)/shard_map/ppermute | solution.py:26
  57.7 4.0 %collective-permute-start.20 = (bf16[96,1280]{1,0:T(8,128)(2,1)S(1)}, bf16[96,1280]{1,0:T(8,128)(2,1)S(1)}, u32[]{:S(2)}, u32[]{:S(2)}) collective-permute-start(bf16[96,1280]{1,0:T(8,128)(2,1)S(1)} %get-tuple-element.76.refs_5_), channel_id=1, source_target_pairs={{0,4},{4,0},{8,12},{12,8},{1,5},{5,1},{9,13},{13,9},{2,6},{6,2},{1... | collective-permute-start | bytes 737288 | tf_op jit(solution)/shard_map/ppermute | solution.py:26
  61.7 1.5 %collective-permute-start.24 = (bf16[96,1280]{1,0:T(8,128)(2,1)S(1)}, bf16[96,1280]{1,0:T(8,128)(2,1)S(1)}, u32[]{:S(2)}, u32[]{:S(2)}) collective-permute-start(bf16[96,1280]{1,0:T(8,128)(2,1)S(1)} %collective-permute-done.22.refs_9_), channel_id=1, source_target_pairs={{0,4},{4,0},{8,12},{12,8},{1,5},{5,1},{9,13},{13,9},{2,6},{6,2},{1... | collective-permute-start | bytes 737288 | tf_op jit(solution)/shard_map/ppermute | solution.py:26
